TPU v7x, 32 devices: a whole 2x2x4 slice. The times are simulated.
32 devices in a mesh: replica: 2 (over y), expert: 4 (over z), fsdp: 4 (over x, core).
Axes of the slice: x: 2, y: 2, z: 4, core: 2. Of those that a mesh axis runs over, the one named last changes fastest.
Arguments:
- tokens: bfloat16 [8192, 2048], P(('replica', 'expert', 'fsdp')), parts along dimension 0, may hold values from -6 to 6
- cotangent: bfloat16 [8192, 2048], P(('replica', 'expert', 'fsdp')), parts along dimension 0, may hold values from -6 to 6
- route_ids: int32 [8192, 8], P(('replica', 'expert', 'fsdp')), parts along dimension 0, may hold values from 0 to 127, all different within a row
- route_gates: float32 [8192, 8], P(('replica', 'expert', 'fsdp')), parts along dimension 0, may hold values from 0.2 to 2
- served_order: int32 [32, 256], P(('replica', 'expert', 'fsdp')), parts along dimension 0, may hold values from 0 to 255, each once within a row
- w_in: bfloat16 [4, 2048, 1536], P('expert', 'fsdp'), may hold values from -0.125 to 0.125
- w_out: bfloat16 [4, 2048, 768], P('expert', 'fsdp'), may hold values from -0.21875 to 0.21875
Outputs:
- combined: bfloat16 [8192, 2048], P(('replica', 'expert', 'fsdp')), parts along dimension 0
- d_tokens: bfloat16 [8192, 2048], P(('replica', 'expert', 'fsdp')), parts along dimension 0
- d_w_out: float32 [8, 2048, 768], P(('replica', 'expert'), 'fsdp'), parts along dimension 0
There are 2 independent parts, one for each index of `replica`. A program takes and returns all parts, laid end to end along the dimension named above; an argument that names none is the same for every part. Nothing has to cross between parts.
All inputs are finite; a program needn't handle non-finite values.
Results may differ from a plain program's by a relative error of at most 0.008.
Values may be sent and summed in bfloat16 or wider, within the bound.
No kernel may reach another device: no remote copies, remote signals or barrier semaphores. Data moves between devices by JAX's collectives and lax.ppermute only.
A program may use at most 64 MiB of HBM per device.

v0:
```python
import jax
import jax.numpy as jnp
from jax import lax
from jax.sharding import PartitionSpec as P

EXPERTS = 128


def slot_table(expert_ids, order_row, group_count, capacity):
    tok_count = expert_ids.shape[0]
    choices = expert_ids.shape[1]
    local_count = EXPERTS // group_count
    served = jnp.take(expert_ids, order_row, axis=0)
    inside = (served % local_count == 0).reshape(-1)
    target = (served // local_count).reshape(-1)
    onehot = (
        (target[:, None] == jnp.arange(group_count, dtype=jnp.int32)[None, :]) & inside[:, None]
    ).astype(jnp.int32)
    before = jnp.cumsum(onehot, axis=0, dtype=jnp.int32) - onehot
    position = jnp.sum(before * onehot, axis=1, dtype=jnp.int32)
    retained = inside & (position < capacity)
    slot_total = group_count * capacity
    destination = jnp.where(retained, target * capacity + position, slot_total)
    route_token = jnp.repeat(order_row, choices)
    route_choice = jnp.tile(jnp.arange(choices, dtype=jnp.int32), tok_count)
    slot_token = (
        jnp.full((slot_total + 1,), tok_count, jnp.int32)
        .at[destination]
        .set(route_token)[:slot_total]
    )
    slot_choice = (
        jnp.zeros((slot_total + 1,), jnp.int32).at[destination].set(route_choice)[:slot_total]
    )
    return (slot_token, slot_choice)


def silu_parts(pre_act, feed):
    gate_act = pre_act[:, :feed]
    up_act = pre_act[:, feed:]
    silu_gate = gate_act * jax.nn.sigmoid(gate_act)
    return (silu_gate * up_act).astype(jnp.bfloat16)


def backward_parts(pre_act, back_hidden, feed):
    gate_act = pre_act[:, :feed]
    up_act = pre_act[:, feed:]
    sigmoid_gate = jax.nn.sigmoid(gate_act)
    silu_gate = gate_act * sigmoid_gate
    d_gate = back_hidden * up_act * (sigmoid_gate * (1.0 + gate_act * (1.0 - sigmoid_gate)))
    d_up = back_hidden * silu_gate
    return jnp.concatenate([d_gate, d_up], axis=1).astype(jnp.bfloat16)


def right_product(left, right_rows):
    return lax.dot_general(
        left, right_rows, (((1,), (1,)), ((), ())), preferred_element_type=jnp.float32
    )


def per_device(tokens, cotangent, route_ids, route_gates, served_order, w_in, w_out):
    group_count = lax.axis_size("expert")
    tok_count = tokens.shape[0]
    width = tokens.shape[1]
    choices = route_ids.shape[1]
    feed = w_out.shape[2]
    capacity = tok_count * choices // EXPERTS
    slot_token, slot_choice = slot_table(route_ids, served_order[0], group_count, capacity)
    filled = slot_token < tok_count
    safe_token = jnp.where(filled, slot_token, 0)
    slot_gate = jnp.where(
        filled,
        jnp.take(route_gates.reshape(-1), safe_token * choices + slot_choice),
        jnp.zeros((), jnp.float32),
    )
    slot_rows = jnp.where(
        filled[:, None], jnp.take(tokens, safe_token, axis=0), jnp.zeros((), jnp.bfloat16)
    )
    slot_rows = slot_rows.reshape(group_count, capacity, width)
    slot_grads = (
        slot_gate[:, None] * jnp.take(cotangent, safe_token, axis=0).astype(jnp.float32)
    ).astype(jnp.bfloat16)
    slot_grads = slot_grads.reshape(group_count, capacity, width)
    recv_rows = lax.all_to_all(slot_rows, "expert", split_axis=0, concat_axis=0, tiled=True)
    recv_rows = recv_rows.reshape(-1, width)
    full_in, full_out = (
        lax.all_gather(w_in, "fsdp", axis=1, tiled=True),
        lax.all_gather(w_out, "fsdp", axis=1, tiled=True),
    )
    full_in = full_in[0]
    full_out = full_out[0]
    pre_act = jnp.dot(recv_rows, full_in, preferred_element_type=jnp.float32)
    hidden = silu_parts(pre_act, feed)
    expert_out = right_product(hidden, full_out).astype(jnp.bfloat16)
    returned_out = lax.all_to_all(
        expert_out.reshape(group_count, capacity, width),
        "expert",
        split_axis=0,
        concat_axis=0,
        tiled=True,
    )
    recv_grads = lax.all_to_all(
        slot_grads, "expert", split_axis=0, concat_axis=0, tiled=True
    ).reshape(-1, width)
    back_hidden = jnp.dot(recv_grads, full_out, preferred_element_type=jnp.float32)
    d_pre = backward_parts(pre_act, back_hidden, feed)
    d_rows = right_product(d_pre, full_in).astype(jnp.bfloat16)
    d_w_out = lax.psum_scatter(
        lax.dot_general(
            recv_grads, hidden, (((0,), (0,)), ((), ())), preferred_element_type=jnp.float32
        ).astype(jnp.bfloat16),
        "fsdp",
        scatter_dimension=0,
        tiled=True,
    ).astype(jnp.float32)[None]
    returned_rows = lax.all_to_all(
        d_rows.reshape(group_count, capacity, width),
        "expert",
        split_axis=0,
        concat_axis=0,
        tiled=True,
    )
    weighted = returned_out.reshape(-1, width).astype(jnp.float32) * slot_gate[:, None]
    combined = (
        jnp.zeros((tok_count + 1, width), jnp.float32).at[slot_token].add(weighted)[:tok_count]
    )
    d_tokens = (
        jnp.zeros((tok_count + 1, width), jnp.float32)
        .at[slot_token]
        .add(returned_rows.reshape(-1, width).astype(jnp.float32))[:tok_count]
    )
    return (combined.astype(jnp.bfloat16), d_tokens.astype(jnp.bfloat16), d_w_out)


def solution(mesh):
    in_specs = (
        P(("replica", "expert", "fsdp"), None),
        P(("replica", "expert", "fsdp"), None),
        P(("replica", "expert", "fsdp"), None),
        P(("replica", "expert", "fsdp"), None),
        P(("replica", "expert", "fsdp"), None),
        P("expert", "fsdp", None),
        P("expert", "fsdp", None),
    )
    out_specs = (
        P(("replica", "expert", "fsdp"), None),
        P(("replica", "expert", "fsdp"), None),
        P(("replica", "expert"), "fsdp", None),
    )
    return jax.shard_map(
        per_device, mesh=mesh, in_specs=in_specs, out_specs=out_specs, check_vma=False
    )
```

profile of v0, /device:TPU:0, one launch (start us, length us, event | category | flops | bytes accessed | tf_op | source)
XLA Modules:
  0.0 141.1 jit_solution(15292176370901383479)
XLA Ops:
  7.2 0.7 all-gather.3.cloned.1.call-update
  8.0 0.7 all-gather.5.cloned.1.call-update
  8.7 0.7 compare_select_fusion.5
  9.4 0.7 compare_and_fusion.2
  10.1 0.8 copy.17
  10.9 0.7 gather_fusion
  11.6 0.1 gather.14
  11.7 0.1 broadcast_select_fusion
  11.9 0.1 select_n.151
  12.0 0.1 select_n.149
  12.1 0.5 broadcast.332
  12.6 0.7 reduce.5
  13.4 0.1 copy.18
  13.5 0.1 copy.19
  13.6 1.2 reduce-window.6
  14.8 0.2 slice_reduce_fusion
  15.0 0.2 reduce-window.9
  15.2 0.1 broadcast_in_dim.87
  15.3 0.1 reshape.300
  15.6 8.0 %scatter_custom_fusion = s32[65]{0:T(128)S(1)} fusion(s32[2048]{0:T(1024)S(1)} %bitcast.70, s32[2048]{0:T(1024)S(1)} %reshape.300, s32[]{:T(128)} %constant.54.clone.1), kind=kCustom, calls=%fused_computation.95 | custom fusion | bytes 264 | tf_op jit(solution)/shard_map/scatter | solution.py:29
  23.7 0.7 gather_fusion.2
  24.5 0.8 select_select_fusion
  25.3 6.3 %all-to-all-start = ((bf16[4,16,2048]{2,1,0:T(8,128)(2,1)}), bf16[4,16,2048]{2,1,0:T(8,128)(2,1)S(1)}, u32[]{:S(2)}, u32[]{:S(2)}) async-start(bf16[4,16,2048]{2,1,0:T(8,128)(2,1)} %bitcast.7), calls=%async_computation | async-start | bytes 524288 | tf_op jit(solution)/shard_map/all_to_all | solution.py:83
  31.6 0.1 copy.20
  31.7 0.1 reshape.257
  31.9 0.1 reshape.308
  32.0 8.0 %scatter_custom_fusion.1 = s32[65]{0:T(128)S(1)} fusion(s32[2048]{0:T(1024)S(1)} %bitcast.71, s32[2048]{0:T(1024)S(1)} %reshape.308, s32[]{:T(128)} %constant.55.clone.1), kind=kCustom, calls=%fused_computation.91 | custom fusion | bytes 264 | tf_op jit(solution)/shard_map/scatter | solution.py:32
  40.0 0.7 gather_fusion.3
  40.8 0.8 gather_fusion.1
  41.6 0.9 multiply_convert_fusion
  42.4 5.1 %all-to-all-start.2 = ((bf16[4,16,2048]{2,1,0:T(8,128)(2,1)}), bf16[4,16,2048]{2,1,0:T(8,128)(2,1)S(1)}, u32[]{:S(2)}, u32[]{:S(2)}) async-start(bf16[4,16,2048]{2,1,0:T(8,128)(2,1)} %bitcast.13), calls=%async_computation.2 | async-start | bytes 524288 | tf_op jit(solution)/shard_map/all_to_all | solution.py:101
  47.5 11.2 %all-gather.3.cloned.1.call-done = bf16[1,2048,1536]{2,1,0:T(8,128)(2,1)} async-done(((bf16[1,512,1536]{2,1,0:T(8,128)(2,1)}), bf16[1,2048,1536]{2,1,0:T(8,128)(2,1)}) %all-gather.3.cloned.1.call-update) | async-done | bytes 6291472 | tf_op jit(solution)/shard_map/all_gather | solution.py:86
  58.7 4.0 %fusion.2 = f32[64,1536]{1,0:T(8,128)S(1)} fusion(bf16[64,2048]{1,0:T(8,128)(2,1)S(1)} %bitcast.66, bf16[1,2048,1536]{2,1,0:T(8,128)(2,1)} %all-gather.3.cloned.1.call-done), kind=kOutput, calls=%fused_computation.10 | convolution fusion | flops 402653184 | bytes 6946816 | tf_op jit(solution)/shard_map/dot_general | solution.py:91
  62.7 26.2 %all-gather.5.cloned.1.call-done = bf16[1,2048,768]{2,1,0:T(8,128)(2,1)} async-done(((bf16[1,512,768]{2,1,0:T(8,128)(2,1)}), bf16[1,2048,768]{2,1,0:T(8,128)(2,1)}) %all-gather.5.cloned.1.call-update) | async-done | bytes 3145744 | tf_op jit(solution)/shard_map/all_gather | solution.py:87
  88.8 2.5 %multiply_convert_fusion.2 = (bf16[64,768]{1,0:T(8,128)(2,1)S(1)}, bf16[64,768]{1,0:T(8,128)(2,1)S(1)}, bf16[64,768]{1,0:T(8,128)(2,1)S(1)}) fusion(f32[64,1536]{1,0:T(8,128)S(1)} %fusion.2, bf16[64,2048]{1,0:T(8,128)(2,1)S(1)} %bitcast.63, bf16[1,2048,768]{2,1,0:T(8,128)(2,1)} %all-gather.5.cloned.1.call-done), kind=kOutput, calls=%fused_computation.35 | convolution fusion | flops 202063872 | bytes 4096000 | tf_op jit(solution)/shard_map/dot_general | solution.py:104
  91.4 2.7 %convolution_convert_fusion = bf16[2048,768]{1,0:T(8,128)(2,1)} fusion(bf16[64,2048]{1,0:T(8,128)(2,1)S(1)} %bitcast.64, bf16[64,768]{1,0:T(8,128)(2,1)S(1)} %get-tuple-element.8), kind=kOutput, calls=%fused_computation.12 | convolution fusion | flops 202899456 | bytes 3506176 | tf_op jit(solution)/shard_map/dot_general | solution.py:108
  94.1 3.7 %fusion.8 = bf16[64,2048]{1,0:T(8,128)(2,1)} fusion(bf16[64,768]{1,0:T(8,128)(2,1)S(1)} %get-tuple-element.8, bf16[1,2048,768]{2,1,0:T(8,128)(2,1)} %all-gather.5.cloned.1.call-done), kind=kOutput, calls=%fused_computation.17 | convolution fusion | flops 201457664 | bytes 3506176 | tf_op jit(solution)/shard_map/dot_general | solution.py:55
  97.8 4.6 %all-to-all-start.1 = ((bf16[4,16,2048]{2,1,0:T(8,128)(2,1)}), bf16[4,16,2048]{2,1,0:T(8,128)(2,1)S(1)}, u32[]{:S(2)}, u32[]{:S(2)}) async-start(bf16[4,16,2048]{2,1,0:T(8,128)(2,1)} %bitcast.11), calls=%async_computation.1 | async-start | bytes 524288 | tf_op jit(solution)/shard_map/all_to_all | solution.py:94
  102.4 5.9 %fusion.11 = bf16[64,2048]{1,0:T(8,128)(2,1)} fusion(bf16[1,2048,1536]{2,1,0:T(8,128)(2,1)} %all-gather.3.cloned.1.call-done, bf16[64,768]{1,0:T(8,128)(2,1)S(1)} %get-tuple-element.7, bf16[64,768]{1,0:T(8,128)(2,1)S(1)} %get-tuple-element.6), kind=kOutput, calls=%fused_computation.18 | convolution fusion | flops 403177472 | bytes 6750208 | tf_op jit(solution)/shard_map/dot_general | solution.py:55
  108.3 3.4 %all-to-all-done.1 = bf16[4,16,2048]{2,1,0:T(8,128)(2,1)S(1)} async-done(((bf16[4,16,2048]{2,1,0:T(8,128)(2,1)}), bf16[4,16,2048]{2,1,0:T(8,128)(2,1)S(1)}, u32[]{:S(2)}, u32[]{:S(2)}) %all-to-all-start.1) | async-done | bytes 262176 | tf_op jit(solution)/shard_map/all_to_all | solution.py:94
  111.7 4.0 %all-to-all-start.3 = ((bf16[4,16,2048]{2,1,0:T(8,128)(2,1)}), bf16[4,16,2048]{2,1,0:T(8,128)(2,1)}, u32[]{:S(2)}, u32[]{:S(2)}) async-start(bf16[4,16,2048]{2,1,0:T(8,128)(2,1)} %bitcast.15), calls=%async_computation.3 | async-start | bytes 524288 | tf_op jit(solution)/shard_map/all_to_all | solution.py:115
  115.7 2.0 %scatter_custom_fusion.2 = f32[257,2048]{1,0:T(8,128)S(1)} fusion(s32[64]{0:T(128)S(1)} %get-tuple-element.10, f32[]{:T(128)} %constant.53.clone.1, bf16[64,2048]{1,0:T(8,128)(2,1)S(1)} %bitcast.65, f32[64]{0:T(128)S(1)} %fusion.35), kind=kCustom, calls=%fused_computation.23 | custom fusion | flops 393216 | bytes 2368004 | tf_op jit(solution)/shard_map/scatter-add | solution.py:124
  117.7 1.1 slice.75
  118.9 3.7 %all-to-all-done.3 = bf16[4,16,2048]{2,1,0:T(8,128)(2,1)} async-done(((bf16[4,16,2048]{2,1,0:T(8,128)(2,1)}), bf16[4,16,2048]{2,1,0:T(8,128)(2,1)}, u32[]{:S(2)}, u32[]{:S(2)}) %all-to-all-start.3) | async-done | bytes 262176 | tf_op jit(solution)/shard_map/all_to_all | solution.py:115
  122.6 2.3 %scatter_custom_fusion.3 = f32[257,2048]{1,0:T(8,128)S(1)} fusion(s32[64]{0:T(128)S(1)} %get-tuple-element.10, f32[]{:T(128)} %constant.53.clone.1, bf16[64,2048]{1,0:T(8,128)(2,1)} %bitcast.19), kind=kCustom, calls=%fused_computation.21 | custom fusion | flops 262144 | bytes 2367492 | tf_op jit(solution)/shard_map/scatter-add | solution.py:129
  125.0 1.1 slice.74
  126.1 6.2 %reduce-scatter.2.cloned.1.call-done = bf16[512,768]{1,0:T(8,128)(2,1)} async-done(((bf16[2048,768]{1,0:T(8,128)(2,1)}), bf16[512,768]{1,0:T(8,128)(2,1)}) %reduce-scatter.2.cloned.1.call-update) | async-done | bytes 786448 | tf_op jit(solution)/shard_map/reduce_scatter | solution.py:107
  132.2 2.4 %bitcast_convert_fusion = f32[1,512,768]{2,1,0:T(8,128)} fusion(bf16[512,768]{1,0:T(8,128)(2,1)} %reduce-scatter.2.cloned.1.call-done), kind=kLoop, calls=%fused_computation.25 | loop fusion | flops 393216 | bytes 2359296 | tf_op jit(solution)/shard_map/broadcast_in_dim | solution.py:107
  (32 shorter events, 0.5 us)
Async XLA Ops:
  7.2 16.5 %copy-start = (bf16[256,2048]{1,0:T(8,128)(2,1)S(1)}, bf16[256,2048]{1,0:T(8,128)(2,1)}, u32[]{:S(2)}) copy-start(bf16[256,2048]{1,0:T(8,128)(2,1)} %param.9) | copy-start | bytes 3145732
  7.2 5.4 %copy-start.2 = (s32[1,256]{1,0:T(1,128)S(1)}, s32[1,256]{1,0:T(1,128)}, u32[]{:S(2)}) copy-start(s32[1,256]{1,0:T(1,128)} %param.13) | copy-start | bytes 3076
  7.2 51.5 %all-gather.3.cloned.1.call-start = ((), (), s32[]{:S(2)}) async-start(), calls=%async_computation.5 | async-start | bytes 7864320 | tf_op jit(solution)/shard_map/all_gather | solution.py:86
  7.9 80.9 %all-gather.5.cloned.1.call-start = ((), (), s32[]{:S(2)}) async-start(), calls=%async_computation.6 | async-start | bytes 3932160 | tf_op jit(solution)/shard_map/all_gather | solution.py:87
  8.7 22.9 %copy-start.3 = (f32[256,8]{0,1:T(8,128)S(1)}, f32[256,8]{0,1:T(8,128)}, u32[]{:S(2)}) copy-start(f32[256,8]{0,1:T(8,128)} %param.12) | copy-start | bytes 24580
  10.9 29.1 %copy-start.1 = (bf16[256,2048]{1,0:T(8,128)(2,1)S(1)}, bf16[256,2048]{1,0:T(8,128)(2,1)}, u32[]{:S(2)}) copy-start(bf16[256,2048]{1,0:T(8,128)(2,1)} %param.10) | copy-start | bytes 3145732
  25.3 17.2 %all-to-all-start = ((bf16[4,16,2048]{2,1,0:T(8,128)(2,1)}), bf16[4,16,2048]{2,1,0:T(8,128)(2,1)S(1)}, u32[]{:S(2)}, u32[]{:S(2)}) async-start(bf16[4,16,2048]{2,1,0:T(8,128)(2,1)} %bitcast.7), calls=%async_computation | async-start | bytes 524288 | tf_op jit(solution)/shard_map/all_to_all | solution.py:83
  42.4 20.2 %all-to-all-start.2 = ((bf16[4,16,2048]{2,1,0:T(8,128)(2,1)}), bf16[4,16,2048]{2,1,0:T(8,128)(2,1)S(1)}, u32[]{:S(2)}, u32[]{:S(2)}) async-start(bf16[4,16,2048]{2,1,0:T(8,128)(2,1)} %bitcast.13), calls=%async_computation.2 | async-start | bytes 524288 | tf_op jit(solution)/shard_map/all_to_all | solution.py:101
  47.5 84.7 %reduce-scatter.2.cloned.1.call-start = ((), (), s32[]{:S(2)}) async-start(), calls=%async_computation.7 | async-start | bytes 3932160 | tf_op jit(solution)/shard_map/reduce_scatter | solution.py:107
  97.8 13.9 %all-to-all-start.1 = ((bf16[4,16,2048]{2,1,0:T(8,128)(2,1)}), bf16[4,16,2048]{2,1,0:T(8,128)(2,1)S(1)}, u32[]{:S(2)}, u32[]{:S(2)}) async-start(bf16[4,16,2048]{2,1,0:T(8,128)(2,1)} %bitcast.11), calls=%async_computation.1 | async-start | bytes 524288 | tf_op jit(solution)/shard_map/all_to_all | solution.py:94
  111.7 10.9 %all-to-all-start.3 = ((bf16[4,16,2048]{2,1,0:T(8,128)(2,1)}), bf16[4,16,2048]{2,1,0:T(8,128)(2,1)}, u32[]{:S(2)}, u32[]{:S(2)}) async-start(bf16[4,16,2048]{2,1,0:T(8,128)(2,1)} %bitcast.15), calls=%async_computation.3 | async-start | bytes 524288 | tf_op jit(solution)/shard_map/all_to_all | solution.py:115
Sparse Core Ops, SparseCore 0:
  9.6 49.0 all-gather.2
  60.3 28.5 all-gather.4
  94.2 37.9 reduce-scatter.1
where the time goes:
time: 142 us; the launch traced here: 141 us
  waiting for transfers between devices  52.1 us (37%)
  local copies, waits for them, and re-layouts  24 us (17%)
  starting transfers between devices  20.1 us (14%)
  matrix products  18.8 us (13%)
  between operations  14 us (10%)
  other arithmetic  12.2 us (9%)
    all_gather x1, waiting for transfers between devices, per_device(): lax.all_gather(w_out, 'fsdp', axis=1, tiled=True)  26.2 us
    all_gather x1, waiting for transfers between devices, per_device(): lax.all_gather(w_in, 'fsdp', axis=1, tiled=True)  11.2 us
    dot_general x2, matrix products, right_product(): lax.dot_general(left, right_rows, (((1,), (1,)), ((), ())), preferred_ele...  9.56 us
    scatter x1, local copies, waits for them, and re-layouts, slot_table(): slot_token = jnp.full((slot_total + 1,), tok_count, jnp.int32).at[destina...  8.04 us
    scatter x1, local copies, waits for them, and re-layouts, slot_table(): jnp.zeros((slot_total + 1,), jnp.int32).at[destination].set(route_choice)  8.03 us
    all_to_all x1, starting transfers between devices, per_device(): lax.all_to_all(slot_rows, 'expert', split_axis=0, concat_axis=0, tiled=True)  6.32 us
    reduce_scatter x1, waiting for transfers between devices, per_device(): lax.psum_scatter(lax.dot_general(recv_grads, hidden, (((0,), (0,)), ((),...  6.16 us
    all_to_all x1, starting transfers between devices, per_device(): lax.all_to_all(slot_grads, 'expert', split_axis=0, concat_axis=0, tiled=T...  5.09 us
  transfers between devices with their start and end apart: 7, of which 5 were waited for; matrix products, arithmetic and copies ran while one was open for 34% of the time, Pallas kernels for 0%

commit v1 on v0

v1 whole, which is shorter than its diff:
```python
import jax
import jax.numpy as jnp
from jax import lax
from jax.experimental import pallas as pl
from jax.experimental.pallas import tpu as pltpu
from jax.sharding import PartitionSpec as P

EXPERTS = 128
CORES = 2
VMEM = 40 * 1024 * 1024
F32 = jnp.float32
BF16 = jnp.bfloat16


def product(left, right, left_dim, right_dim, **kw):
    return lax.dot_general(
        left, right, (((left_dim,), (right_dim,)), ((), ())), preferred_element_type=F32, **kw
    )


def call(body, out_shape, args, flops=0, nbytes=0, smem=0):
    specs = [pl.BlockSpec(memory_space=pltpu.SMEM)] * smem
    specs += [pl.BlockSpec(memory_space=pltpu.VMEM)] * (len(args) - smem)
    return pl.pallas_call(
        body,
        out_shape=out_shape,
        in_specs=specs,
        out_specs=jax.tree.map(lambda _: pl.BlockSpec(memory_space=pltpu.VMEM), out_shape),
        compiler_params=pltpu.CompilerParams(vmem_limit_bytes=VMEM),
        cost_estimate=pl.CostEstimate(flops=flops, bytes_accessed=nbytes, transcendentals=0),
    )(*args)


def shape(dims, kind=BF16):
    return jax.ShapeDtypeStruct(dims, kind)


def dispatch_kernel(groups, spread, capacity, where, ids, gates, order, tok, cot, *outs):
    chunks, (pick_out, gate_out) = outs[:-2], outs[-2:]
    count, choices = ids.shape
    slots = groups * capacity
    part = tok.shape[1] // (spread * CORES)
    own_expert, own_part = where[0], where[1]
    slot = lax.broadcasted_iota(jnp.int32, (count, slots), 1)
    wanted = ((slot // capacity) ^ own_expert) * (EXPERTS // groups)
    routed = jnp.zeros((count, slots), F32)
    gate = jnp.zeros((count, slots), F32)
    for k in range(choices):
        hit = ids[:, k : k + 1] == wanted
        routed += jnp.where(hit, 1.0, 0.0)
        gate += jnp.where(hit, gates[:, k : k + 1], 0.0)
    row = lax.broadcasted_iota(jnp.int32, (count, count), 0)
    col = lax.broadcasted_iota(jnp.int32, (count, count), 1)
    served = jnp.where(order[...] == row, 1.0, 0.0).astype(BF16)
    earlier = jnp.where(row < col, 1.0, 0.0).astype(BF16)
    by_rank = product(routed.astype(BF16), served, 0, 0)
    before = product(by_rank.astype(BF16), earlier, 1, 0)
    place = lax.broadcasted_iota(jnp.int32, (slots, count), 0) % capacity
    taken = jnp.where(before.astype(jnp.int32) == place, by_rank, 0.0).astype(BF16)
    pick = product(taken, served, 1, 1)
    pick_out[...] = product(served, taken, 1, 1).astype(BF16)
    crossed = product(pick, gate, 1, 0, precision=lax.Precision.HIGHEST)
    diagonal = lax.broadcasted_iota(jnp.int32, (slots, slots), 0) == lax.broadcasted_iota(
        jnp.int32, (slots, slots), 1
    )
    slot_gate = jnp.sum(jnp.where(diagonal, crossed, 0.0), axis=1, keepdims=True)
    gate_out[...] = jnp.broadcast_to(slot_gate, gate_out.shape)
    pick = pick.astype(BF16)
    for kx in range(spread):
        for kc in range(CORES):
            at = pl.ds(pl.multiple_of((own_part ^ (kx * CORES + kc)) * part, part), part)
            to = pl.ds(kc * part, part)
            rows = product(pick, tok[:, at], 1, 0).astype(BF16)
            grads = (slot_gate * product(pick, cot[:, at], 1, 0)).astype(BF16)
            for ke in range(groups):
                chunk = chunks[ke * spread + kx]
                chunk[:capacity, to] = rows[ke * capacity : (ke + 1) * capacity]
                chunk[capacity:, to] = grads[ke * capacity : (ke + 1) * capacity]


def partial_kernel(groups, spread, capacity, *refs):
    chunks = refs[: groups * spread]
    in_own, in_sib, out_own, out_sib, keep, sib_grads, *sends = refs[groups * spread :]
    part = in_own.shape[0]
    wide = in_own.shape[1]
    block = groups * capacity
    for kx in range(spread):
        mine = [chunks[ke * spread + kx] for ke in range(groups)]
        rows = jnp.concatenate([c[:capacity] for c in mine], axis=0)
        grads = jnp.concatenate([c[capacity:] for c in mine], axis=0)
        pre = product(rows[:, :part], in_own[...], 1, 0) + product(rows[:, part:], in_sib[...], 1, 0)
        back = product(grads[:, :part], out_own[...], 1, 0)
        back += product(grads[:, part:], out_sib[...], 1, 0)
        target = keep if kx == 0 else sends[kx - 1]
        target[:, :wide] = pre.astype(target.dtype)
        target[:, wide:] = back.astype(target.dtype)
        sib_grads[kx * block : (kx + 1) * block] = grads[:, part:]


def act_kernel(keep, *refs):
    others, out = refs[:-1], refs[-1]
    feed = out.shape[1] // 3
    total = keep[...]
    for other in others:
        total += other[...].astype(F32)
    gate_act, up_act, back = (total[:, i * feed : (i + 1) * feed] for i in range(3))
    sig = 1.0 / (1.0 + jnp.exp(-gate_act))
    silu = gate_act * sig
    out[:, :feed] = (silu * up_act).astype(BF16)
    out[:, feed : 2 * feed] = (back * up_act * (sig * (1.0 + gate_act * (1.0 - sig)))).astype(BF16)
    out[:, 2 * feed :] = (back * silu).astype(BF16)


def result_kernel(groups, spread, capacity, *refs):
    acts = refs[:spread]
    in_own, in_sib, out_own, out_sib, hidden_out, *chunks = refs[spread:]
    part = in_own.shape[0]
    feed = out_own.shape[1]
    block = groups * capacity
    for kx in range(spread):
        hidden = acts[kx][:, :feed]
        d_pre = acts[kx][:, feed:]
        hidden_out[kx * block : (kx + 1) * block] = hidden
        for kc, (w_in, w_out) in enumerate(((in_own, out_own), (in_sib, out_sib))):
            expert_out = product(hidden, w_out[...], 1, 1).astype(BF16)
            d_rows = product(d_pre, w_in[...], 1, 1).astype(BF16)
            to = pl.ds(kc * part, part)
            for ke in range(groups):
                chunk = chunks[ke * spread + kx]
                chunk[:capacity, to] = expert_out[ke * capacity : (ke + 1) * capacity]
                chunk[capacity:, to] = d_rows[ke * capacity : (ke + 1) * capacity]


def weight_kernel(groups, spread, capacity, *refs):
    chunks = refs[: groups * spread]
    sib_grads, hidden, sib_hidden, out = refs[groups * spread :]
    part = out.shape[0]
    grads = jnp.concatenate(
        [chunks[ke * spread + kx][capacity:, :part] for kx in range(spread) for ke in range(groups)],
        axis=0,
    )
    out[...] = product(grads, hidden[...], 0, 0) + product(sib_grads[...], sib_hidden[...], 0, 0)


def combine_kernel(groups, spread, capacity, where, pick, gate, *refs):
    chunks, (combined, d_tokens) = refs[:-2], refs[-2:]
    part = combined.shape[1] // (spread * CORES)
    own_part = where[1]
    twice = jnp.concatenate([pick[...], pick[...]], axis=1)
    for kx in range(spread):
        for kc in range(CORES):
            at = pl.ds(pl.multiple_of((own_part ^ (kx * CORES + kc)) * part, part), part)
            mine = [chunks[ke * spread + kx] for ke in range(groups)]
            cols = slice(kc * part, (kc + 1) * part)
            out = jnp.concatenate([c[:capacity, cols] for c in mine], axis=0)
            back = jnp.concatenate([c[capacity:, cols] for c in mine], axis=0)
            weighted = out.astype(F32) * gate[:, :1]
            high = weighted.astype(BF16)
            low = (weighted - high.astype(F32)).astype(BF16)
            both = jnp.concatenate([high, low], axis=0)
            combined[:, at] = product(twice, both, 1, 0).astype(BF16)
            d_tokens[:, at] = product(pick[...], back, 1, 0).astype(BF16)


def per_device(tokens, cotangent, route_ids, route_gates, served_order, w_in, w_out):
    groups = lax.axis_size("expert")
    parts = lax.axis_size("fsdp")
    spread = parts // CORES
    count, width = tokens.shape
    capacity = count * route_ids.shape[1] // EXPERTS
    feed = w_out.shape[2]
    slots = groups * capacity
    half = width // spread
    sizes = (groups, spread, capacity)
    where = jnp.stack([lax.axis_index("expert"), lax.axis_index("fsdp")]).astype(jnp.int32)

    def to_core(value):
        return lax.ppermute(value, "fsdp", [(i, i ^ 1) for i in range(parts)])

    def to_x(value, kx):
        return lax.ppermute(value, "fsdp", [(i, i ^ (kx * CORES)) for i in range(parts)])

    def exchange(chunks):
        got = list(chunks)
        for ke in reversed(range(groups)):
            for kx in reversed(range(spread)):
                if ke or kx:
                    got[ke * spread + kx] = lax.ppermute(
                        chunks[ke * spread + kx],
                        ("expert", "fsdp"),
                        [
                            (e * parts + i, (e ^ ke) * parts + (i ^ (kx * CORES)))
                            for e in range(groups)
                            for i in range(parts)
                        ],
                    )
        return got

    def body(kernel):
        return lambda *refs: kernel(*sizes, *refs)

    in_own, out_own = w_in[0], w_out[0]
    in_sib, out_sib = to_core(in_own), to_core(out_own)
    chunk_shapes = [shape((2 * capacity, half))] * (groups * spread)
    *chunks, pick, gate = call(
        body(dispatch_kernel),
        chunk_shapes + [shape((count, slots)), shape((slots, 128), F32)],
        (where, route_ids, route_gates, served_order, tokens, cotangent),
        flops=4 * slots * count * width,
        nbytes=4 * count * width,
        smem=1,
    )
    chunks = exchange(chunks)
    keep, sib_grads, *sends = call(
        body(partial_kernel),
        [shape((slots, 3 * feed), F32), shape((spread * slots, width // parts))]
        + [shape((slots, 3 * feed))] * (spread - 1),
        (*chunks, in_own, in_sib, out_own, out_sib),
        flops=6 * spread * slots * half * feed,
        nbytes=6 * half * feed,
    )
    others = [to_x(value, kx + 1) for kx, value in enumerate(sends)]
    sib_grads = to_core(sib_grads)
    act = call(
        act_kernel, shape((slots, 3 * feed)), (keep, *others), nbytes=8 * slots * 3 * feed
    )
    acts = [act] + [to_x(act, kx) for kx in range(1, spread)]
    hidden, *results = call(
        body(result_kernel),
        [shape((spread * slots, feed))] + chunk_shapes,
        (*acts, in_own, in_sib, out_own, out_sib),
        flops=6 * spread * slots * half * feed,
        nbytes=6 * half * feed,
    )
    results = exchange(results)
    sib_hidden = to_core(hidden)
    d_w_out = call(
        body(weight_kernel),
        shape((width // parts, feed), F32),
        (*chunks, sib_grads, hidden, sib_hidden),
        flops=4 * spread * slots * (width // parts) * feed,
        nbytes=4 * (width // parts) * feed,
    )
    combined, d_tokens = call(
        body(combine_kernel),
        [shape((count, width))] * 2,
        (where, pick, gate, *results),
        flops=6 * slots * count * width,
        nbytes=4 * count * width,
        smem=1,
    )
    return combined, d_tokens, d_w_out[None]


def solution(mesh):
    rows = P(("replica", "expert", "fsdp"), None)
    weights = P("expert", "fsdp", None)
    return jax.shard_map(
        per_device,
        mesh=mesh,
        in_specs=(rows,) * 5 + (weights,) * 2,
        out_specs=(rows, rows, P(("replica", "expert"), "fsdp", None)),
        check_vma=False,
    )
```

time: 142 us -> 75.3 us (0.53)
  waiting for transfers between devices: 52.1 us -> 17.8 us
  local copies, waits for them, and re-layouts: 24 us -> 4.84 us
  matrix products: 18.8 us -> 0 us
  starting transfers between devices: 20.1 us -> 38.1 us
  Pallas kernels: 0 us -> 13.5 us
  between operations: 14 us -> 0.72 us
  other arithmetic: 12.2 us -> 0.08 us
    ppermute x0 -> x20, starting transfers between devices: none -> 38.1 us  [the longest x14 33.6 us: exchange(): lax.ppermute(chunks[ke * spread + kx], ('expert', 'fsdp'), [(e * parts +...]
    all_gather x2 -> x0, waiting for transfers between devices: 37.3 us -> none  [the longest x1 26.2 us: per_device(): lax.all_gather(w_out, 'fsdp', axis=1, tiled=True)]
    all_to_all x4 -> x0, starting transfers between devices: 20 us -> none  [the longest x1 6.32 us: per_device(): lax.all_to_all(slot_rows, 'expert', split_axis=0, concat_axis=0, tiled=True)]
    dot_general x5 -> x0, matrix products: 18.8 us -> none  [the longest x2 9.56 us: right_product(): lax.dot_general(left, right_rows, (((1,), (1,)), ((), ())), preferred_ele...]
    ppermute x0 -> x20, waiting for transfers between devices: none -> 17.8 us  [the longest x2 11.1 us: to_x(): lax.ppermute(value, 'fsdp', [(i, i ^ kx * CORES) for i in range(parts)])]
    scatter x2 -> x0, local copies, waits for them, and re-layouts: 16.1 us -> none  [the longest x1 8.04 us: slot_table(): slot_token = jnp.full((slot_total + 1,), tok_count, jnp.int32).at[destina...]
    pallas_call x0 -> x6, Pallas kernels: none -> 13.5 us  [call(): pl.pallas_call(body, out_shape=out_shape, in_specs=specs, out_specs=jax.t...]
    all_to_all x4 -> x0, waiting for transfers between devices: 7.16 us -> none  [the longest x1 3.75 us: per_device(): lax.all_to_all(d_rows.reshape(group_count, capacity, width), 'expert', sp...]
  transfers between devices with their start and end apart: 7 -> 20, of which waited for: 5 -> 7; matrix products, arithmetic and copies ran while one was open for 34% -> 2% of each run, Pallas kernels for 0% -> 6%
where the time goes in v1:
time: 75.3 us; the launch traced here: 75 us
  starting transfers between devices  38.1 us (51%)
  waiting for transfers between devices  17.8 us (24%)
  Pallas kernels  13.5 us (18%)
  local copies, waits for them, and re-layouts  4.84 us (6%)
    ppermute x14, starting transfers between devices, exchange(): lax.ppermute(chunks[ke * spread + kx], ('expert', 'fsdp'), [(e * parts +...  33.6 us
    pallas_call x6, Pallas kernels, call(): pl.pallas_call(body, out_shape=out_shape, in_specs=specs, out_specs=jax.t...  13.5 us
    ppermute x2, waiting for transfers between devices, to_x(): lax.ppermute(value, 'fsdp', [(i, i ^ kx * CORES) for i in range(parts)])  11.1 us
    ppermute x14, waiting for transfers between devices, exchange(): lax.ppermute(chunks[ke * spread + kx], ('expert', 'fsdp'), [(e * parts +...  6.72 us
    unnamed x12, local copies, waits for them, and re-layouts  4.84 us
    ppermute x2, starting transfers between devices, to_x(): lax.ppermute(value, 'fsdp', [(i, i ^ kx * CORES) for i in range(parts)])  3.97 us
  transfers between devices with their start and end apart: 20, of which 7 were waited for; matrix products, arithmetic and copies ran while one was open for 2% of the time, Pallas kernels for 6%

profile of v1, /device:TPU:0, one launch (start us, length us, event | category | flops | bytes accessed | tf_op | source)
XLA Modules:
  0.0 75.0 jit_solution(17383778646335023949)
XLA Ops:
  0.6 0.5 collective-permute-start.7
  1.2 0.1 collective-permute-start.8
  1.2 0.8 %copy.10.refs_1_ = s32[256,8]{1,0:T(8,128)S(1)} copy(s32[256,8]{0,1:T(8,128)} %param.9) | data formatting | bytes 16384 | tf_op args[2]
  2.1 0.8 %copy.11.refs_2_ = f32[256,8]{1,0:T(8,128)S(1)} copy(f32[256,8]{0,1:T(8,128)} %param.10) | data formatting | bytes 16384 | tf_op args[3]
  2.9 0.0 copy-start.1
  2.9 0.1 pad_add_fusion.refs_0_
  3.0 1.3 %copy-done.2 = bf16[256,2048]{1,0:T(8,128)(2,1)S(1)} copy-done((bf16[256,2048]{1,0:T(8,128)(2,1)S(1)}, bf16[256,2048]{1,0:T(8,128)(2,1)}, u32[]{:S(2)}) %copy-start.2) | copy-done | bytes 1048600
  4.3 1.2 %copy-done.3 = bf16[256,2048]{1,0:T(8,128)(2,1)S(1)} copy-done((bf16[256,2048]{1,0:T(8,128)(2,1)S(1)}, bf16[256,2048]{1,0:T(8,128)(2,1)}, u32[]{:S(2)}) %copy-start.3) | copy-done | bytes 1048600
  5.5 0.7 copy-done.4
  6.2 2.1 %shard_map.94 = (bf16[32,1024]{1,0:T(8,128)(2,1)S(1)}, bf16[32,1024]{1,0:T(8,128)(2,1)S(1)}, bf16[32,1024]{1,0:T(8,128)(2,1)S(1)}, bf16[32,1024]{1,0:T(8,128)(2,...) custom-call(s32[2]{0:T(128)S(1)} %pad_add_fusion.refs_0_, ...), custom_call_target="tpu_custom_call" | custom-call | flops 134217728 | bytes 2097152 | tf_op jit(solution)/shard_map/pallas_call | solution.py:24
  8.3 3.0 %collective-permute-start = (bf16[32,1024]{1,0:T(8,128)(2,1)S(1)}, bf16[32,1024]{1,0:T(8,128)(2,1)S(1)}, u32[]{:S(2)}, u32[]{:S(2)}) collective-permute-start(bf16[32,1024]{1,0:T(8,128)(2,1)S(1)} %get-tuple-element.30), channel_id=1, source_target_pairs={{0,2},{1,3},{2,0},{3,1},{4,6},{5,7},{6,4},{7,5},{8,10},{9,11},{10,... | collective-permute-start | bytes 196616 | tf_op jit(solution)/shard_map/ppermute | solution.py:188
  11.2 1.6 %collective-permute-start.1 = (bf16[32,1024]{1,0:T(8,128)(2,1)S(1)}, bf16[32,1024]{1,0:T(8,128)(2,1)S(1)}, u32[]{:S(2)}, u32[]{:S(2)}) collective-permute-start(bf16[32,1024]{1,0:T(8,128)(2,1)S(1)} %get-tuple-element.31), channel_id=1, source_target_pairs={{0,4},{1,5},{2,6},{3,7},{4,0},{5,1},{6,2},{7,3},{8,12},{9,13},{10,... | collective-permute-start | bytes 196616 | tf_op jit(solution)/shard_map/ppermute | solution.py:188
  12.8 0.0 collective-permute-start.2
  12.8 0.8 %collective-permute-done.refs_1_ = bf16[32,1024]{1,0:T(8,128)(2,1)S(1)} collective-permute-done((bf16[32,1024]{1,0:T(8,128)(2,1)S(1)}, bf16[32,1024]{1,0:T(8,128)(2,1)S(1)}, u32[]{:S(2)}, u32[]{:S(2)}) %collective-permute-start) | collective-permute-done | bytes 65568 | tf_op jit(solution)/shard_map/ppermute | solution.py:188
  13.6 3.0 %collective-permute-start.3 = (bf16[32,1024]{1,0:T(8,128)(2,1)S(1)}, bf16[32,1024]{1,0:T(8,128)(2,1)S(1)}, u32[]{:S(2)}, u32[]{:S(2)}) collective-permute-start(bf16[32,1024]{1,0:T(8,128)(2,1)S(1)} %get-tuple-element.33), channel_id=1, source_target_pairs={{0,8},{1,9},{2,10},{3,11},{4,12},{5,13},{6,14},{7,15},{8,0},{9,1},... | collective-permute-start | bytes 196616 | tf_op jit(solution)/shard_map/ppermute | solution.py:188
  16.6 0.0 collective-permute-done.1.refs_2_
  16.6 1.5 %collective-permute-start.4 = (bf16[32,1024]{1,0:T(8,128)(2,1)S(1)}, bf16[32,1024]{1,0:T(8,128)(2,1)S(1)}, u32[]{:S(2)}, u32[]{:S(2)}) collective-permute-start(bf16[32,1024]{1,0:T(8,128)(2,1)S(1)} %get-tuple-element.34), channel_id=1, source_target_pairs={{0,10},{1,11},{2,8},{3,9},{4,14},{5,15},{6,12},{7,13},{8,2},{9,3},... | collective-permute-start | bytes 196616 | tf_op jit(solution)/shard_map/ppermute | solution.py:188
  18.1 0.6 collective-permute-done.2.refs_3_
  18.7 2.8 %collective-permute-start.5 = (bf16[32,1024]{1,0:T(8,128)(2,1)S(1)}, bf16[32,1024]{1,0:T(8,128)(2,1)S(1)}, u32[]{:S(2)}, u32[]{:S(2)}) collective-permute-start(bf16[32,1024]{1,0:T(8,128)(2,1)S(1)} %get-tuple-element.35), channel_id=1, source_target_pairs={{0,12},{1,13},{2,14},{3,15},{4,8},{5,9},{6,10},{7,11},{8,4},{9,5},... | collective-permute-start | bytes 196616 | tf_op jit(solution)/shard_map/ppermute | solution.py:188
  21.5 0.0 collective-permute-done.3.refs_4_
  21.5 5.0 %collective-permute-start.6 = (bf16[32,1024]{1,0:T(8,128)(2,1)S(1)}, bf16[32,1024]{1,0:T(8,128)(2,1)S(1)}, u32[]{:S(2)}, u32[]{:S(2)}) collective-permute-start(bf16[32,1024]{1,0:T(8,128)(2,1)S(1)} %get-tuple-element.36), channel_id=1, source_target_pairs={{0,14},{1,15},{2,12},{3,13},{4,10},{5,11},{6,8},{7,9},{8,6},{9,7},... | collective-permute-start | bytes 196616 | tf_op jit(solution)/shard_map/ppermute | solution.py:188
  26.5 0.0 collective-permute-done.4.refs_5_
  26.5 0.0 collective-permute-done.5.refs_6_
  26.5 2.3 %collective-permute-done.6.refs_7_ = bf16[32,1024]{1,0:T(8,128)(2,1)S(1)} collective-permute-done((bf16[32,1024]{1,0:T(8,128)(2,1)S(1)}, bf16[32,1024]{1,0:T(8,128)(2,1)S(1)}, u32[]{:S(2)}, u32[]{:S(2)}) %collective-permute-start.6) | collective-permute-done | bytes 65568 | tf_op jit(solution)/shard_map/ppermute | solution.py:188
  28.8 0.0 collective-permute-done.8.refs_11_.refs_5_
  28.8 0.0 collective-permute-done.7.refs_9_.refs_3_
  28.8 2.9 %shard_map.95 = (f32[64,2304]{1,0:T(8,128)S(1)}, bf16[128,512]{1,0:T(8,128)(2,1)S(1)}, bf16[64,2304]{1,0:T(8,128)(2,1)S(1)}) custom-call(bf16[32,1024]{1,0:T(8,128)(2,1)S(1)} %get-tuple-element.29.refs_0_, bf16[32,1024]{1,0:T(8,128)(2,1)S(1)} %collective-permute-done.refs_1_, bf16[32,1024]{1,0:T(8,128)(2,1)S(1)} %collective-permute-done.1.refs_2_, ...), custom_call_target="tpu_custom_call" | custom-call | flops 603979776 | bytes 4718592 | tf_op jit(solution)/shard_map/pallas_call | solution.py:24
  31.7 1.5 %collective-permute-start.9 = (bf16[64,2304]{1,0:T(8,128)(2,1)S(1)}, bf16[64,2304]{1,0:T(8,128)(2,1)S(1)}, u32[]{:S(2)}, u32[]{:S(2)}) collective-permute-start(bf16[64,2304]{1,0:T(8,128)(2,1)S(1)} %get-tuple-element.38), channel_id=1, source_target_pairs={{0,2},{1,3},{2,0},{3,1},{4,6},{5,7},{6,4},{7,5},{8,10},{9,11},{10,... | collective-permute-start | bytes 884744 | tf_op jit(solution)/shard_map/ppermute | solution.py:181
  33.2 6.3 %collective-permute-done.9.refs_0_ = bf16[64,2304]{1,0:T(8,128)(2,1)S(1)} collective-permute-done((bf16[64,2304]{1,0:T(8,128)(2,1)S(1)}, bf16[64,2304]{1,0:T(8,128)(2,1)S(1)}, u32[]{:S(2)}, u32[]{:S(2)}) %collective-permute-start.9) | collective-permute-done | bytes 294944 | tf_op jit(solution)/shard_map/ppermute | solution.py:181
  39.5 0.1 shard_map.96.refs_0_
  39.7 2.5 %collective-permute-start.10 = (bf16[64,2304]{1,0:T(8,128)(2,1)S(1)}, bf16[64,2304]{1,0:T(8,128)(2,1)S(1)}, u32[]{:S(2)}, u32[]{:S(2)}) collective-permute-start(bf16[64,2304]{1,0:T(8,128)(2,1)S(1)} %shard_map.96.refs_0_), channel_id=1, source_target_pairs={{0,2},{1,3},{2,0},{3,1},{4,6},{5,7},{6,4},{7,5},{8,10},{9,11},{10,... | collective-permute-start | bytes 884744 | tf_op jit(solution)/shard_map/ppermute | solution.py:181
  42.2 4.7 %collective-permute-done.10.refs_1_ = bf16[64,2304]{1,0:T(8,128)(2,1)S(1)} collective-permute-done((bf16[64,2304]{1,0:T(8,128)(2,1)S(1)}, bf16[64,2304]{1,0:T(8,128)(2,1)S(1)}, u32[]{:S(2)}, u32[]{:S(2)}) %collective-permute-start.10) | collective-permute-done | bytes 294944 | tf_op jit(solution)/shard_map/ppermute | solution.py:181
  46.9 4.1 %shard_map.97 = (bf16[128,768]{1,0:T(8,128)(2,1)S(1)}, bf16[32,1024]{1,0:T(8,128)(2,1)S(1)}, bf16[32,1024]{1,0:T(8,128)(2,1)S(1)}, bf16[32,1024]{1,0:T(8,128)(2,...) custom-call(bf16[64,2304]{1,0:T(8,128)(2,1)S(1)} %shard_map.96.refs_, ...), custom_call_target="tpu_custom_call" | custom-call | flops 603979776 | bytes 4718592 | tf_op jit(solution)/shard_map/pallas_call | solution.py:24
  51.0 2.1 %collective-permute-start.11 = (bf16[32,1024]{1,0:T(8,128)(2,1)S(1)}, bf16[32,1024]{1,0:T(8,128)(2,1)S(1)}, u32[]{:S(2)}, u32[]{:S(2)}) collective-permute-start(bf16[32,1024]{1,0:T(8,128)(2,1)S(1)} %get-tuple-element.40), channel_id=1, source_target_pairs={{0,2},{1,3},{2,0},{3,1},{4,6},{5,7},{6,4},{7,5},{8,10},{9,11},{10,... | collective-permute-start | bytes 196616 | tf_op jit(solution)/shard_map/ppermute | solution.py:188
  53.1 0.8 %collective-permute-start.12 = (bf16[32,1024]{1,0:T(8,128)(2,1)S(1)}, bf16[32,1024]{1,0:T(8,128)(2,1)S(1)}, u32[]{:S(2)}, u32[]{:S(2)}) collective-permute-start(bf16[32,1024]{1,0:T(8,128)(2,1)S(1)} %get-tuple-element.41), channel_id=1, source_target_pairs={{0,4},{1,5},{2,6},{3,7},{4,0},{5,1},{6,2},{7,3},{8,12},{9,13},{10,... | collective-permute-start | bytes 196616 | tf_op jit(solution)/shard_map/ppermute | solution.py:188
  53.9 0.8 %collective-permute-start.13 = (bf16[32,1024]{1,0:T(8,128)(2,1)S(1)}, bf16[32,1024]{1,0:T(8,128)(2,1)S(1)}, u32[]{:S(2)}, u32[]{:S(2)}) collective-permute-start(bf16[32,1024]{1,0:T(8,128)(2,1)S(1)} %get-tuple-element.42), channel_id=1, source_target_pairs={{0,6},{1,7},{2,4},{3,5},{4,2},{5,3},{6,0},{7,1},{8,14},{9,15},{10,... | collective-permute-start | bytes 196616 | tf_op jit(solution)/shard_map/ppermute | solution.py:188
  54.7 3.6 %collective-permute-start.14 = (bf16[32,1024]{1,0:T(8,128)(2,1)S(1)}, bf16[32,1024]{1,0:T(8,128)(2,1)S(1)}, u32[]{:S(2)}, u32[]{:S(2)}) collective-permute-start(bf16[32,1024]{1,0:T(8,128)(2,1)S(1)} %get-tuple-element.43), channel_id=1, source_target_pairs={{0,8},{1,9},{2,10},{3,11},{4,12},{5,13},{6,14},{7,15},{8,0},{9,1},... | collective-permute-start | bytes 196616 | tf_op jit(solution)/shard_map/ppermute | solution.py:188
  58.3 0.0 collective-permute-start.18
  58.3 0.0 collective-permute-done.12.refs_5_
  58.3 2.7 %collective-permute-start.15 = (bf16[32,1024]{1,0:T(8,128)(2,1)S(1)}, bf16[32,1024]{1,0:T(8,128)(2,1)S(1)}, u32[]{:S(2)}, u32[]{:S(2)}) collective-permute-start(bf16[32,1024]{1,0:T(8,128)(2,1)S(1)} %get-tuple-element.44), channel_id=1, source_target_pairs={{0,10},{1,11},{2,8},{3,9},{4,14},{5,15},{6,12},{7,13},{8,2},{9,3},... | collective-permute-start | bytes 196616 | tf_op jit(solution)/shard_map/ppermute | solution.py:188
  61.0 2.6 %collective-permute-start.16 = (bf16[32,1024]{1,0:T(8,128)(2,1)S(1)}, bf16[32,1024]{1,0:T(8,128)(2,1)S(1)}, u32[]{:S(2)}, u32[]{:S(2)}) collective-permute-start(bf16[32,1024]{1,0:T(8,128)(2,1)S(1)} %get-tuple-element.45), channel_id=1, source_target_pairs={{0,12},{1,13},{2,14},{3,15},{4,8},{5,9},{6,10},{7,11},{8,4},{9,5},... | collective-permute-start | bytes 196616 | tf_op jit(solution)/shard_map/ppermute | solution.py:188
  63.6 4.1 %collective-permute-start.17 = (bf16[32,1024]{1,0:T(8,128)(2,1)S(1)}, bf16[32,1024]{1,0:T(8,128)(2,1)S(1)}, u32[]{:S(2)}, u32[]{:S(2)}) collective-permute-start(bf16[32,1024]{1,0:T(8,128)(2,1)S(1)} %get-tuple-element.46), channel_id=1, source_target_pairs={{0,14},{1,15},{2,12},{3,13},{4,10},{5,11},{6,8},{7,9},{8,6},{9,7},... | collective-permute-start | bytes 196616 | tf_op jit(solution)/shard_map/ppermute | solution.py:188
  67.7 0.4 collective-permute-done.15.refs_8_
  68.1 0.0 collective-permute-done.16.refs_9_
  68.1 2.6 %collective-permute-done.17.refs_10_ = bf16[32,1024]{1,0:T(8,128)(2,1)S(1)} collective-permute-done((bf16[32,1024]{1,0:T(8,128)(2,1)S(1)}, bf16[32,1024]{1,0:T(8,128)(2,1)S(1)}, u32[]{:S(2)}, u32[]{:S(2)}) %collective-permute-start.17) | collective-permute-done | bytes 65568 | tf_op jit(solution)/shard_map/ppermute | solution.py:188
  70.7 2.6 %shard_map.98 = (bf16[256,2048]{1,0:T(8,128)(2,1)}, bf16[256,2048]{1,0:T(8,128)(2,1)}) custom-call(s32[2]{0:T(128)S(1)} %pad_add_fusion.refs_0_, bf16[256,64]{1,0:T(8,128)(2,1)S(1)} %get-tuple-element.27.refs_1_, f32[64,128]{1,0:T(8,128)S(1)} %get-tuple-element.28.refs_2_, bf16[32,1024]{1,0:T(8,128)(2,1)S(1)} %get-tuple-element.39.refs_3_, ...), custom_call_target="tpu_custom_call" | custom-call | flops 201326592 | bytes 2097152 | tf_op jit(solution)/shard_map/pallas_call | solution.py:24
  73.3 0.0 collective-permute-done.19.refs_10_
  73.3 1.7 %shard_map.99 = f32[512,768]{1,0:T(8,128)} custom-call(bf16[32,1024]{1,0:T(8,128)(2,1)S(1)} %get-tuple-element.29.refs_0_, bf16[32,1024]{1,0:T(8,128)(2,1)S(1)} %collective-permute-done.refs_1_, bf16[32,1024]{1,0:T(8,128)(2,1)S(1)} %collective-permute-done.1.refs_2_, bf16[32,1024]{1,0:T(8,128)(2,1)S(1)} %collective-permute-done.2.refs_3_, ...), custom_call_target="tpu_custom_call" | custom-call | flops 201326592 | bytes 1572864 | tf_op jit(solution)/shard_map/pallas_call | solution.py:24
  (11 shorter events, 0.0 us)
Async XLA Ops:
  0.6 28.2 %copy-start = (bf16[1,512,1536]{2,1,0:T(8,128)(2,1)S(1)}, bf16[1,512,1536]{2,1,0:T(8,128)(2,1)}, u32[]{:S(2)}) copy-start(bf16[1,512,1536]{2,1,0:T(8,128)(2,1)} %param.12) | copy-start | bytes 4718596
  0.6 28.2 %collective-permute-start.7 = (bf16[512,1536]{1,0:T(8,128)(2,1)}, bf16[512,1536]{1,0:T(8,128)(2,1)S(1)}, u32[]{:S(2)}, u32[]{:S(2)}) collective-permute-start(bf16[512,1536]{1,0:T(8,128)(2,1)} %bitcast.5), channel_id=1, source_target_pairs={{0,1},{1,0},{2,3},{3,2},{4,5},{5,4},{6,7},{7,6},{8,9},{9,8},{10,11... | collective-permute-start | bytes 4718600 | tf_op jit(solution)/shard_map/ppermute | solution.py:178
  1.2 27.7 %collective-permute-start.8 = (bf16[512,768]{1,0:T(8,128)(2,1)}, bf16[512,768]{1,0:T(8,128)(2,1)}, u32[]{:S(2)}, u32[]{:S(2)}) collective-permute-start(bf16[512,768]{1,0:T(8,128)(2,1)} %bitcast.8), channel_id=1, source_target_pairs={{0,1},{1,0},{2,3},{3,2},{4,5},{5,4},{6,7},{7,6},{8,9},{9,8},{10,11... | collective-permute-start | bytes 2359304 | tf_op jit(solution)/shard_map/ppermute | solution.py:178
  2.9 25.9 %copy-start.1 = (bf16[1,512,768]{2,1,0:T(8,128)(2,1)S(1)}, bf16[1,512,768]{2,1,0:T(8,128)(2,1)}, u32[]{:S(2)}) copy-start(bf16[1,512,768]{2,1,0:T(8,128)(2,1)} %param.13) | copy-start | bytes 2359300
  3.0 1.3 %copy-start.2 = (bf16[256,2048]{1,0:T(8,128)(2,1)S(1)}, bf16[256,2048]{1,0:T(8,128)(2,1)}, u32[]{:S(2)}) copy-start(bf16[256,2048]{1,0:T(8,128)(2,1)} %refs_4_.1) | copy-start | bytes 3145732
  4.3 1.2 %copy-start.3 = (bf16[256,2048]{1,0:T(8,128)(2,1)S(1)}, bf16[256,2048]{1,0:T(8,128)(2,1)}, u32[]{:S(2)}) copy-start(bf16[256,2048]{1,0:T(8,128)(2,1)} %refs_5_.1) | copy-start | bytes 3145732
  5.5 0.7 copy-start.4
  8.3 5.3 %collective-permute-start = (bf16[32,1024]{1,0:T(8,128)(2,1)S(1)}, bf16[32,1024]{1,0:T(8,128)(2,1)S(1)}, u32[]{:S(2)}, u32[]{:S(2)}) collective-permute-start(bf16[32,1024]{1,0:T(8,128)(2,1)S(1)} %get-tuple-element.30), channel_id=1, source_target_pairs={{0,2},{1,3},{2,0},{3,1},{4,6},{5,7},{6,4},{7,5},{8,10},{9,11},{10,... | collective-permute-start | bytes 196616 | tf_op jit(solution)/shard_map/ppermute | solution.py:188
  11.2 5.4 %collective-permute-start.1 = (bf16[32,1024]{1,0:T(8,128)(2,1)S(1)}, bf16[32,1024]{1,0:T(8,128)(2,1)S(1)}, u32[]{:S(2)}, u32[]{:S(2)}) collective-permute-start(bf16[32,1024]{1,0:T(8,128)(2,1)S(1)} %get-tuple-element.31), channel_id=1, source_target_pairs={{0,4},{1,5},{2,6},{3,7},{4,0},{5,1},{6,2},{7,3},{8,12},{9,13},{10,... | collective-permute-start | bytes 196616 | tf_op jit(solution)/shard_map/ppermute | solution.py:188
  12.8 5.9 %collective-permute-start.2 = (bf16[32,1024]{1,0:T(8,128)(2,1)S(1)}, bf16[32,1024]{1,0:T(8,128)(2,1)S(1)}, u32[]{:S(2)}, u32[]{:S(2)}) collective-permute-start(bf16[32,1024]{1,0:T(8,128)(2,1)S(1)} %get-tuple-element.32), channel_id=1, source_target_pairs={{0,6},{1,7},{2,4},{3,5},{4,2},{5,3},{6,0},{7,1},{8,14},{9,15},{10,... | collective-permute-start | bytes 196616 | tf_op jit(solution)/shard_map/ppermute | solution.py:188
  13.6 7.9 %collective-permute-start.3 = (bf16[32,1024]{1,0:T(8,128)(2,1)S(1)}, bf16[32,1024]{1,0:T(8,128)(2,1)S(1)}, u32[]{:S(2)}, u32[]{:S(2)}) collective-permute-start(bf16[32,1024]{1,0:T(8,128)(2,1)S(1)} %get-tuple-element.33), channel_id=1, source_target_pairs={{0,8},{1,9},{2,10},{3,11},{4,12},{5,13},{6,14},{7,15},{8,0},{9,1},... | collective-permute-start | bytes 196616 | tf_op jit(solution)/shard_map/ppermute | solution.py:188
  16.6 9.9 %collective-permute-start.4 = (bf16[32,1024]{1,0:T(8,128)(2,1)S(1)}, bf16[32,1024]{1,0:T(8,128)(2,1)S(1)}, u32[]{:S(2)}, u32[]{:S(2)}) collective-permute-start(bf16[32,1024]{1,0:T(8,128)(2,1)S(1)} %get-tuple-element.34), channel_id=1, source_target_pairs={{0,10},{1,11},{2,8},{3,9},{4,14},{5,15},{6,12},{7,13},{8,2},{9,3},... | collective-permute-start | bytes 196616 | tf_op jit(solution)/shard_map/ppermute | solution.py:188
  18.7 7.8 %collective-permute-start.5 = (bf16[32,1024]{1,0:T(8,128)(2,1)S(1)}, bf16[32,1024]{1,0:T(8,128)(2,1)S(1)}, u32[]{:S(2)}, u32[]{:S(2)}) collective-permute-start(bf16[32,1024]{1,0:T(8,128)(2,1)S(1)} %get-tuple-element.35), channel_id=1, source_target_pairs={{0,12},{1,13},{2,14},{3,15},{4,8},{5,9},{6,10},{7,11},{8,4},{9,5},... | collective-permute-start | bytes 196616 | tf_op jit(solution)/shard_map/ppermute | solution.py:188
  21.5 7.3 %collective-permute-start.6 = (bf16[32,1024]{1,0:T(8,128)(2,1)S(1)}, bf16[32,1024]{1,0:T(8,128)(2,1)S(1)}, u32[]{:S(2)}, u32[]{:S(2)}) collective-permute-start(bf16[32,1024]{1,0:T(8,128)(2,1)S(1)} %get-tuple-element.36), channel_id=1, source_target_pairs={{0,14},{1,15},{2,12},{3,13},{4,10},{5,11},{6,8},{7,9},{8,6},{9,7},... | collective-permute-start | bytes 196616 | tf_op jit(solution)/shard_map/ppermute | solution.py:188
  31.7 7.8 %collective-permute-start.9 = (bf16[64,2304]{1,0:T(8,128)(2,1)S(1)}, bf16[64,2304]{1,0:T(8,128)(2,1)S(1)}, u32[]{:S(2)}, u32[]{:S(2)}) collective-permute-start(bf16[64,2304]{1,0:T(8,128)(2,1)S(1)} %get-tuple-element.38), channel_id=1, source_target_pairs={{0,2},{1,3},{2,0},{3,1},{4,6},{5,7},{6,4},{7,5},{8,10},{9,11},{10,... | collective-permute-start | bytes 884744 | tf_op jit(solution)/shard_map/ppermute | solution.py:181
  39.7 7.2 %collective-permute-start.10 = (bf16[64,2304]{1,0:T(8,128)(2,1)S(1)}, bf16[64,2304]{1,0:T(8,128)(2,1)S(1)}, u32[]{:S(2)}, u32[]{:S(2)}) collective-permute-start(bf16[64,2304]{1,0:T(8,128)(2,1)S(1)} %shard_map.96.refs_0_), channel_id=1, source_target_pairs={{0,2},{1,3},{2,0},{3,1},{4,6},{5,7},{6,4},{7,5},{8,10},{9,11},{10,... | collective-permute-start | bytes 884744 | tf_op jit(solution)/shard_map/ppermute | solution.py:181
  51.0 7.3 %collective-permute-start.11 = (bf16[32,1024]{1,0:T(8,128)(2,1)S(1)}, bf16[32,1024]{1,0:T(8,128)(2,1)S(1)}, u32[]{:S(2)}, u32[]{:S(2)}) collective-permute-start(bf16[32,1024]{1,0:T(8,128)(2,1)S(1)} %get-tuple-element.40), channel_id=1, source_target_pairs={{0,2},{1,3},{2,0},{3,1},{4,6},{5,7},{6,4},{7,5},{8,10},{9,11},{10,... | collective-permute-start | bytes 196616 | tf_op jit(solution)/shard_map/ppermute | solution.py:188
  53.0 20.2 %collective-permute-start.19 = (bf16[128,768]{1,0:T(8,128)(2,1)S(1)}, bf16[128,768]{1,0:T(8,128)(2,1)S(1)}, u32[]{:S(2)}, u32[]{:S(2)}) collective-permute-start(bf16[128,768]{1,0:T(8,128)(2,1)S(1)} %get-tuple-element.50.refs_9_), channel_id=1, source_target_pairs={{0,1},{1,0},{2,3},{3,2},{4,5},{5,4},{6,7},{7,6},{8,9},{9,8},{10,11... | collective-permute-start | bytes 589832 | tf_op jit(solution)/shard_map/ppermute | solution.py:178
  53.1 5.2 %collective-permute-start.12 = (bf16[32,1024]{1,0:T(8,128)(2,1)S(1)}, bf16[32,1024]{1,0:T(8,128)(2,1)S(1)}, u32[]{:S(2)}, u32[]{:S(2)}) collective-permute-start(bf16[32,1024]{1,0:T(8,128)(2,1)S(1)} %get-tuple-element.41), channel_id=1, source_target_pairs={{0,4},{1,5},{2,6},{3,7},{4,0},{5,1},{6,2},{7,3},{8,12},{9,13},{10,... | collective-permute-start | bytes 196616 | tf_op jit(solution)/shard_map/ppermute | solution.py:188
  53.9 7.2 %collective-permute-start.13 = (bf16[32,1024]{1,0:T(8,128)(2,1)S(1)}, bf16[32,1024]{1,0:T(8,128)(2,1)S(1)}, u32[]{:S(2)}, u32[]{:S(2)}) collective-permute-start(bf16[32,1024]{1,0:T(8,128)(2,1)S(1)} %get-tuple-element.42), channel_id=1, source_target_pairs={{0,6},{1,7},{2,4},{3,5},{4,2},{5,3},{6,0},{7,1},{8,14},{9,15},{10,... | collective-permute-start | bytes 196616 | tf_op jit(solution)/shard_map/ppermute | solution.py:188
  54.7 8.9 %collective-permute-start.14 = (bf16[32,1024]{1,0:T(8,128)(2,1)S(1)}, bf16[32,1024]{1,0:T(8,128)(2,1)S(1)}, u32[]{:S(2)}, u32[]{:S(2)}) collective-permute-start(bf16[32,1024]{1,0:T(8,128)(2,1)S(1)} %get-tuple-element.43), channel_id=1, source_target_pairs={{0,8},{1,9},{2,10},{3,11},{4,12},{5,13},{6,14},{7,15},{8,0},{9,1},... | collective-permute-start | bytes 196616 | tf_op jit(solution)/shard_map/ppermute | solution.py:188
  58.3 15.0 %collective-permute-start.18 = (bf16[128,512]{1,0:T(8,128)(2,1)S(1)}, bf16[128,512]{1,0:T(8,128)(2,1)S(1)}, u32[]{:S(2)}, u32[]{:S(2)}) collective-permute-start(bf16[128,512]{1,0:T(8,128)(2,1)S(1)} %get-tuple-element.49), channel_id=1, source_target_pairs={{0,1},{1,0},{2,3},{3,2},{4,5},{5,4},{6,7},{7,6},{8,9},{9,8},{10,11... | collective-permute-start | bytes 393224 | tf_op jit(solution)/shard_map/ppermute | solution.py:178
  58.3 9.8 %collective-permute-start.15 = (bf16[32,1024]{1,0:T(8,128)(2,1)S(1)}, bf16[32,1024]{1,0:T(8,128)(2,1)S(1)}, u32[]{:S(2)}, u32[]{:S(2)}) collective-permute-start(bf16[32,1024]{1,0:T(8,128)(2,1)S(1)} %get-tuple-element.44), channel_id=1, source_target_pairs={{0,10},{1,11},{2,8},{3,9},{4,14},{5,15},{6,12},{7,13},{8,2},{9,3},... | collective-permute-start | bytes 196616 | tf_op jit(solution)/shard_map/ppermute | solution.py:188
  61.0 7.1 %collective-permute-start.16 = (bf16[32,1024]{1,0:T(8,128)(2,1)S(1)}, bf16[32,1024]{1,0:T(8,128)(2,1)S(1)}, u32[]{:S(2)}, u32[]{:S(2)}) collective-permute-start(bf16[32,1024]{1,0:T(8,128)(2,1)S(1)} %get-tuple-element.45), channel_id=1, source_target_pairs={{0,12},{1,13},{2,14},{3,15},{4,8},{5,9},{6,10},{7,11},{8,4},{9,5},... | collective-permute-start | bytes 196616 | tf_op jit(solution)/shard_map/ppermute | solution.py:188
  63.6 7.1 %collective-permute-start.17 = (bf16[32,1024]{1,0:T(8,128)(2,1)S(1)}, bf16[32,1024]{1,0:T(8,128)(2,1)S(1)}, u32[]{:S(2)}, u32[]{:S(2)}) collective-permute-start(bf16[32,1024]{1,0:T(8,128)(2,1)S(1)} %get-tuple-element.46), channel_id=1, source_target_pairs={{0,14},{1,15},{2,12},{3,13},{4,10},{5,11},{6,8},{7,9},{8,6},{9,7},... | collective-permute-start | bytes 196616 | tf_op jit(solution)/shard_map/ppermute | solution.py:188

commit v2 on v1

v2 whole, which is shorter than its diff:
```python
import jax
import jax.numpy as jnp
from jax import lax
from jax.experimental import pallas as pl
from jax.experimental.pallas import tpu as pltpu
from jax.sharding import PartitionSpec as P

EXPERTS = 128
CORES = 2
VMEM = 40 * 1024 * 1024
F32 = jnp.float32
BF16 = jnp.bfloat16


def product(left, right, left_dim, right_dim, **kw):
    return lax.dot_general(
        left, right, (((left_dim,), (right_dim,)), ((), ())), preferred_element_type=F32, **kw
    )


def call(body, out_shape, args, flops=0, nbytes=0, smem=0, far=0, scratch=()):
    specs = [pl.BlockSpec(memory_space=pltpu.SMEM)] * smem
    specs += [pl.BlockSpec(memory_space=pltpu.VMEM)] * (len(args) - smem - far)
    specs += [pl.BlockSpec(memory_space=pl.ANY)] * far
    return pl.pallas_call(
        body,
        out_shape=out_shape,
        in_specs=specs,
        scratch_shapes=list(scratch),
        out_specs=jax.tree.map(lambda _: pl.BlockSpec(memory_space=pltpu.VMEM), out_shape),
        compiler_params=pltpu.CompilerParams(vmem_limit_bytes=VMEM),
        cost_estimate=pl.CostEstimate(flops=flops, bytes_accessed=nbytes, transcendentals=0),
    )(*args)


def shape(dims, kind=BF16):
    return jax.ShapeDtypeStruct(dims, kind)


def columns(own_part, kx, kc, part):
    return pl.ds(pl.multiple_of((own_part ^ (kx * CORES + kc)) * part, part), part)


def rows_kernel(groups, spread, capacity, where, ids, gates, order, tok_hbm, *refs):
    *outs, pick_out, turned_out, gate_out, tok, sem = refs
    copy = pltpu.make_async_copy(tok_hbm, tok, sem)
    copy.start()
    choices, count = ids.shape
    slots = groups * capacity
    part = tok.shape[1] // (spread * CORES)
    slot = lax.broadcasted_iota(jnp.int32, (slots, count), 0)
    wanted = ((slot // capacity) ^ where[0]) * (EXPERTS // groups)
    routed = jnp.zeros((slots, count), F32)
    gate = jnp.zeros((slots, count), F32)
    for k in range(choices):
        hit = ids[k : k + 1, :] == wanted
        routed = jnp.where(hit, 1.0, routed)
        gate = jnp.where(hit, gates[k : k + 1, :], gate)
    row = lax.broadcasted_iota(jnp.int32, (count, count), 0)
    col = lax.broadcasted_iota(jnp.int32, (count, count), 1)
    served = jnp.where(order[...] == row, 1.0, 0.0).astype(BF16)
    earlier = jnp.where(row < col, 1.0, 0.0).astype(BF16)
    by_rank = product(routed.astype(BF16), served, 1, 0)
    before = product(by_rank.astype(BF16), earlier, 1, 0)
    taken = jnp.where(before.astype(jnp.int32) == slot % capacity, by_rank, 0.0).astype(BF16)
    pick = product(taken, served, 1, 1)
    turned_out[...] = product(served, taken, 1, 1).astype(BF16)
    slot_gate = jnp.sum(pick * gate, axis=1, keepdims=True)
    gate_out[...] = jnp.broadcast_to(slot_gate, gate_out.shape)
    pick = pick.astype(BF16)
    pick_out[...] = pick
    copy.wait()
    for kx in reversed(range(spread)):
        for kc in range(CORES):
            rows = product(pick, tok[:, columns(where[1], kx, kc, part)], 1, 0)
            outs[kx][:, kc * part : (kc + 1) * part] = rows.astype(BF16)


def grads_kernel(groups, spread, capacity, where, pick, gate, cot, *outs):
    part = cot.shape[1] // (spread * CORES)
    for kx in reversed(range(spread)):
        for kc in range(CORES):
            rows = product(pick[...], cot[:, columns(where[1], kx, kc, part)], 1, 0)
            outs[kx][:, kc * part : (kc + 1) * part] = (gate[:, :1] * rows).astype(BF16)


def regroup_kernel(groups, spread, capacity, *refs):
    by_x, by_e = refs[:spread], refs[spread:]
    for ke in range(groups):
        for kx in range(spread):
            by_e[ke][kx * capacity : (kx + 1) * capacity] = by_x[kx][
                ke * capacity : (ke + 1) * capacity
            ]


def far_kernel(groups, spread, capacity, *refs):
    by_e, by_x = refs[:groups], refs[groups:]
    for ke in range(groups):
        for kx in range(1, spread):
            by_x[kx - 1][ke * capacity : (ke + 1) * capacity] = by_e[ke][
                kx * capacity : (kx + 1) * capacity
            ]


def partial(groups, spread, capacity, chunks, own, sib, outs):
    part = own.shape[0]
    left = jnp.concatenate([c[...] for c in chunks], axis=0)
    total = product(left[:, :part], own[...], 1, 0) + product(left[:, part:], sib[...], 1, 0)
    for ke in range(groups):
        for kx in range(spread):
            at = (ke * spread + kx) * capacity
            outs[kx][ke * capacity : (ke + 1) * capacity] = total[at : at + capacity].astype(
                outs[kx].dtype
            )


def pre_kernel(groups, spread, capacity, *refs):
    chunks, (own, sib, *outs) = refs[:groups], refs[groups:]
    partial(groups, spread, capacity, chunks, own, sib, outs)


def back_kernel(groups, spread, capacity, *refs):
    chunks, (own, sib, own_grads, sib_grads, *outs) = refs[:groups], refs[groups:]
    part = own.shape[0]
    partial(groups, spread, capacity, chunks, own, sib, outs)
    for kx in range(spread):
        for ke in range(groups):
            at = (kx * groups + ke) * capacity
            rows = chunks[ke][kx * capacity : (kx + 1) * capacity]
            own_grads[at : at + capacity] = rows[:, :part]
            sib_grads[at : at + capacity] = rows[:, part:]


def summed(refs):
    total = refs[0][...]
    for ref in refs[1:]:
        total += ref[...].astype(F32)
    return total


def hidden_kernel(*refs):
    pre, out = summed(refs[:-1]), refs[-1]
    feed = out.shape[1]
    gate_act, up_act = pre[:, :feed], pre[:, feed:]
    out[...] = (gate_act * (1.0 / (1.0 + jnp.exp(-gate_act))) * up_act).astype(BF16)


def d_pre_kernel(*refs):
    spread = len(refs) // 2
    pre, back, out = summed(refs[:spread]), summed(refs[spread:-1]), refs[-1]
    feed = back.shape[1]
    gate_act, up_act = pre[:, :feed], pre[:, feed:]
    sig = 1.0 / (1.0 + jnp.exp(-gate_act))
    out[:, :feed] = (back * up_act * (sig * (1.0 + gate_act * (1.0 - sig)))).astype(BF16)
    out[:, feed:] = (back * (gate_act * sig)).astype(BF16)


def result_kernel(groups, spread, capacity, *refs):
    left, (own, sib, *chunks) = refs[:spread], refs[spread:]
    part = own.shape[0]
    rows = jnp.concatenate([r[...] for r in left], axis=0)
    for kc, weight in enumerate((own, sib)):
        value = product(rows, weight[...], 1, 1).astype(BF16)
        for ke in range(groups):
            for kx in range(spread):
                at = (kx * groups + ke) * capacity
                chunks[ke][kx * capacity : (kx + 1) * capacity, kc * part : (kc + 1) * part] = value[
                    at : at + capacity
                ]


def weight_kernel(spread, own_grads, sib_grads, *refs):
    hidden, sib_hidden, out = refs[:spread], refs[spread:-1], refs[-1]
    left = jnp.concatenate([own_grads[...], sib_grads[...]], axis=0)
    right = jnp.concatenate([r[...] for r in (*hidden, *sib_hidden)], axis=0)
    out[...] = product(left, right, 0, 0)


def returned(groups, spread, capacity, refs, kx, cols):
    if kx:
        return refs[groups + kx - 1][:, cols]
    return jnp.concatenate([refs[ke][:capacity, cols] for ke in range(groups)], axis=0)


def combine_kernel(groups, spread, capacity, where, turned, gate, *refs):
    out = refs[-1]
    part = out.shape[1] // (spread * CORES)
    twice = jnp.concatenate([turned[...], turned[...]], axis=1)
    for kx in range(spread):
        for kc in range(CORES):
            cols = slice(kc * part, (kc + 1) * part)
            rows = returned(groups, spread, capacity, refs, kx, cols)
            weighted = rows.astype(F32) * gate[:, :1]
            high = weighted.astype(BF16)
            low = (weighted - high.astype(F32)).astype(BF16)
            both = jnp.concatenate([high, low], axis=0)
            out[:, columns(where[1], kx, kc, part)] = product(twice, both, 1, 0).astype(BF16)


def d_tokens_kernel(groups, spread, capacity, where, turned, *refs):
    out = refs[-1]
    part = out.shape[1] // (spread * CORES)
    for kx in range(spread):
        for kc in range(CORES):
            cols = slice(kc * part, (kc + 1) * part)
            rows = returned(groups, spread, capacity, refs, kx, cols)
            out[:, columns(where[1], kx, kc, part)] = product(turned[...], rows, 1, 0).astype(BF16)


def per_device(tokens, cotangent, route_ids, route_gates, served_order, w_in, w_out):
    groups = lax.axis_size("expert")
    parts = lax.axis_size("fsdp")
    spread = parts // CORES
    count, width = tokens.shape
    capacity = count * route_ids.shape[1] // EXPERTS
    feed = w_out.shape[2]
    slots = groups * capacity
    half = width // spread
    part = width // parts
    sizes = (groups, spread, capacity)
    where = jnp.stack([lax.axis_index("expert"), lax.axis_index("fsdp")]).astype(jnp.int32)

    def to_core(value):
        return lax.ppermute(value, "fsdp", [(i, i ^ 1) for i in range(parts)])

    def to_x(values):
        return [
            lax.ppermute(value, "fsdp", [(i, i ^ ((k + 1) * CORES)) for i in range(parts)])
            for k, value in enumerate(values)
        ]

    def to_expert(chunks):
        return [
            lax.ppermute(value, "expert", [(i, i ^ ke) for i in range(groups)]) if ke else value
            for ke, value in enumerate(chunks)
        ]

    def body(kernel):
        return lambda *refs: kernel(*sizes, *refs)

    by_x = [shape((slots, half))] * spread
    by_e = [shape((spread * capacity, half))] * groups

    def inward(near, *far):
        chunks = call(body(regroup_kernel), by_e, (near, *to_x(far)), nbytes=4 * slots * width)
        return to_expert(chunks)

    def outward(left, own, sib):
        chunks = call(
            body(result_kernel),
            by_e,
            (*left, own, sib),
            flops=2 * spread * slots * half * own.shape[1],
            nbytes=2 * half * own.shape[1],
        )
        chunks = to_expert(chunks)
        far = call(body(far_kernel), by_x[1:], chunks, nbytes=4 * slots * width)
        return (*chunks, *to_x(far))

    in_own, out_own = w_in[0], w_out[0]
    *rows, pick, turned, gate = call(
        body(rows_kernel),
        by_x + [shape((slots, count)), shape((count, slots)), shape((slots, 128), F32)],
        (where, route_ids.T, route_gates.T, served_order, tokens),
        flops=2 * slots * count * width,
        nbytes=4 * count * width,
        smem=1,
        far=1,
        scratch=(pltpu.VMEM(tokens.shape, BF16), pltpu.SemaphoreType.DMA),
    )
    in_own, out_own, pick = lax.optimization_barrier((in_own, out_own, pick))
    in_sib, out_sib = to_core(in_own), to_core(out_own)
    grads = call(
        body(grads_kernel),
        by_x,
        (where, pick, gate, cotangent),
        flops=2 * slots * count * width,
        nbytes=4 * count * width,
        smem=1,
    )
    rows = inward(*rows)
    grads = inward(*grads)
    pre, *pre_far = call(
        body(pre_kernel),
        [shape((slots, 2 * feed), F32)] + [shape((slots, 2 * feed))] * (spread - 1),
        (*rows, in_own, in_sib),
        flops=4 * spread * slots * half * feed,
        nbytes=4 * half * feed,
    )
    pre = (pre, *to_x(pre_far))
    own_grads, sib_grads, back, *back_far = call(
        body(back_kernel),
        [shape((spread * slots, part))] * 2
        + [shape((slots, feed), F32)]
        + [shape((slots, feed))] * (spread - 1),
        (*grads, out_own, out_sib),
        flops=2 * spread * slots * half * feed,
        nbytes=2 * half * feed,
    )
    back = (back, *to_x(back_far))
    hidden = call(hidden_kernel, shape((slots, feed)), pre, nbytes=12 * slots * feed)
    hidden = (hidden, *to_x([hidden] * (spread - 1)))
    expert_out = outward(hidden, out_own, out_sib)
    d_pre = call(d_pre_kernel, shape((slots, 2 * feed)), (*pre, *back), nbytes=20 * slots * feed)
    d_pre = (d_pre, *to_x([d_pre] * (spread - 1)))
    d_rows = outward(d_pre, in_own, in_sib)
    d_w_out = call(
        lambda *refs: weight_kernel(spread, *refs),
        shape((part, feed), F32),
        (own_grads, to_core(sib_grads), *hidden, *[to_core(value) for value in hidden]),
        flops=4 * spread * slots * part * feed,
        nbytes=4 * part * feed,
    )
    combined = call(
        body(combine_kernel),
        shape((count, width)),
        (where, turned, gate, *expert_out),
        flops=4 * slots * count * width,
        nbytes=4 * count * width,
        smem=1,
    )
    d_tokens = call(
        body(d_tokens_kernel),
        shape((count, width)),
        (where, turned, *d_rows),
        flops=2 * slots * count * width,
        nbytes=4 * count * width,
        smem=1,
    )
    return combined, d_tokens, d_w_out[None]


def solution(mesh):
    rows = P(("replica", "expert", "fsdp"), None)
    weights = P("expert", "fsdp", None)
    return jax.shard_map(
        per_device,
        mesh=mesh,
        in_specs=(rows,) * 5 + (weights,) * 2,
        out_specs=(rows, rows, P(("replica", "expert"), "fsdp", None)),
        check_vma=False,
    )
```

time: 75.3 us -> 73.6 us (0.977)
  waiting for transfers between devices: 17.8 us -> 26.3 us
  starting transfers between devices: 38.1 us -> 30.7 us
  Pallas kernels: 13.5 us -> 10.7 us
    ppermute x16 -> x20, starting transfers between devices: 37.5 us -> 29.6 us  [the longest x12 18 us: to_expert(): lax.ppermute(value, 'expert', [(i, i ^ ke) for i in range(groups)])]
    ppermute x16 -> x20, waiting for transfers between devices: 17.8 us -> 25.4 us  [the longest x8 12.7 us: to_x(): lax.ppermute(value, 'fsdp', [(i, i ^ (k + 1) * CORES) for i in range(part...]
    pallas_call x6 -> x15, Pallas kernels: 13.5 us -> 10.7 us  [call(): pl.pallas_call(body, out_shape=out_shape, in_specs=specs, scratch_shapes=...]
    ppermute x4 -> x5, waiting for transfers between devices: 0.01 us -> 0.95 us  [to_core(): return lax.ppermute(value, 'fsdp', [(i, i ^ 1) for i in range(parts)])]
    unnamed x12 -> x14, local copies, waits for them, and re-layouts: 4.84 us -> 4.63 us
  transfers between devices with their start and end apart: 20 -> 25, of which waited for: 7 -> 10; matrix products, arithmetic and copies ran while one was open for 2% -> 0% of each run, Pallas kernels for 6% -> 10%
where the time goes in v2:
time: 73.6 us; the launch traced here: 73.3 us
  starting transfers between devices  30.7 us (42%)
  waiting for transfers between devices  26.3 us (36%)
  Pallas kernels  10.7 us (15%)
  local copies, waits for them, and re-layouts  4.63 us (6%)
  between operations  0.77 us (1%)
    ppermute x12, starting transfers between devices, to_expert(): lax.ppermute(value, 'expert', [(i, i ^ ke) for i in range(groups)])  18 us
    ppermute x8, waiting for transfers between devices, to_x(): lax.ppermute(value, 'fsdp', [(i, i ^ (k + 1) * CORES) for i in range(part...  12.7 us
    ppermute x12, waiting for transfers between devices, to_expert(): lax.ppermute(value, 'expert', [(i, i ^ ke) for i in range(groups)])  12.7 us
    ppermute x8, starting transfers between devices, to_x(): lax.ppermute(value, 'fsdp', [(i, i ^ (k + 1) * CORES) for i in range(part...  11.6 us
    pallas_call x15, Pallas kernels, call(): pl.pallas_call(body, out_shape=out_shape, in_specs=specs, scratch_shapes=...  10.7 us
    unnamed x14, local copies, waits for them, and re-layouts  4.63 us
  transfers between devices with their start and end apart: 25, of which 10 were waited for; matrix products, arithmetic and copies ran while one was open for 0% of the time, Pallas kernels for 10%

profile of v2, /device:TPU:0, one launch (start us, length us, event | category | flops | bytes accessed | tf_op | source)
XLA Modules:
  0.0 73.3 jit_solution(16699715957033449404)
XLA Ops:
  0.6 0.1 pad_add_fusion.refs_0_
  0.7 1.3 %copy-done.2 = bf16[256,2048]{1,0:T(8,128)(2,1)S(1)} copy-done((bf16[256,2048]{1,0:T(8,128)(2,1)S(1)}, bf16[256,2048]{1,0:T(8,128)(2,1)}, u32[]{:S(2)}) %copy-start.2) | copy-done | bytes 1048600
  2.1 0.7 copy-done.4
  2.8 0.7 copy-done.5
  3.4 0.7 copy-done.6
  4.1 1.4 %shard_map.94 = (bf16[64,1024]{1,0:T(8,128)(2,1)S(1)}, bf16[64,1024]{1,0:T(8,128)(2,1)S(1)}, bf16[64,256]{1,0:T(8,128)(2,1)S(1)}, bf16[256,64]{1,0:T(8,128)(2,1)S(1)}, f32[64,128]{1,0:T(8,128)S(1)}) custom-call(s32[2]{0:T(128)S(1)} %pad_add_fusion.refs_0_, s32[8,256]{1,0:T(8,128)S(1)} %bitcast.13, f32[8,256]{1,0:T(8,128)S(1)} %bitcast.14, ...), custom_call_target="tpu_custom_call" | custom-call | flops 67108864 | bytes 2097152 | tf_op jit(solution)/shard_map/pallas_call | solution.py:25
  5.6 0.5 collective-permute-start.4
  6.1 0.1 collective-permute-start.7
  6.2 2.9 %collective-permute-start = (bf16[64,1024]{1,0:T(8,128)(2,1)S(1)}, bf16[64,1024]{1,0:T(8,128)(2,1)S(1)}, u32[]{:S(2)}, u32[]{:S(2)}) collective-permute-start(bf16[64,1024]{1,0:T(8,128)(2,1)S(1)} %get-tuple-element.38), channel_id=1, source_target_pairs={{0,2},{1,3},{2,0},{3,1},{4,6},{5,7},{6,4},{7,5},{8,10},{9,11},{10,... | collective-permute-start | bytes 393224 | tf_op jit(solution)/shard_map/ppermute | solution.py:228
  9.1 3.7 %collective-permute-done.refs_1_ = bf16[64,1024]{1,0:T(8,128)(2,1)S(1)} collective-permute-done((bf16[64,1024]{1,0:T(8,128)(2,1)S(1)}, bf16[64,1024]{1,0:T(8,128)(2,1)S(1)}, u32[]{:S(2)}, u32[]{:S(2)}) %collective-permute-start) | collective-permute-done | bytes 131104 | tf_op jit(solution)/shard_map/ppermute | solution.py:228
  12.8 1.9 %collective-permute-start.1 = (bf16[32,1024]{1,0:T(8,128)(2,1)S(1)}, bf16[32,1024]{1,0:T(8,128)(2,1)S(1)}, u32[]{:S(2)}, u32[]{:S(2)}) collective-permute-start(bf16[32,1024]{1,0:T(8,128)(2,1)S(1)} %get-tuple-element.40), channel_id=1, source_target_pairs={{0,4},{4,0},{8,12},{12,8},{1,5},{5,1},{9,13},{13,9},{2,6},{6,2},{1... | collective-permute-start | bytes 196616 | tf_op jit(solution)/shard_map/ppermute | solution.py:234
  14.7 1.2 %copy-done.3 = bf16[256,2048]{1,0:T(8,128)(2,1)S(1)} copy-done((bf16[256,2048]{1,0:T(8,128)(2,1)S(1)}, bf16[256,2048]{1,0:T(8,128)(2,1)}, u32[]{:S(2)}) %copy-start.3) | copy-done | bytes 1048600
  16.0 0.8 %shard_map.101 = (bf16[64,1024]{1,0:T(8,128)(2,1)S(1)}, bf16[64,1024]{1,0:T(8,128)(2,1)S(1)}) custom-call(s32[2]{0:T(128)S(1)} %pad_add_fusion.refs_0_, bf16[64,256]{1,0:T(8,128)(2,1)S(1)} %get-tuple-element.52.refs_1_, f32[64,128]{1,0:T(8,128)S(1)} %get-tuple-element.36.refs_2_, bf16[256,2048]{1,0:T(8,128)(2,1)S(1)} %copy-done.3), custom_call_target="tpu_custom_call" | custom-call | flops 67108864 | bytes 2097152 | tf_op jit(solution)/shard_map/pallas_call | solution.py:25
  16.8 1.6 %collective-permute-start.12 = (bf16[64,1024]{1,0:T(8,128)(2,1)S(1)}, bf16[64,1024]{1,0:T(8,128)(2,1)S(1)}, u32[]{:S(2)}, u32[]{:S(2)}) collective-permute-start(bf16[64,1024]{1,0:T(8,128)(2,1)S(1)} %get-tuple-element.54), channel_id=1, source_target_pairs={{0,2},{1,3},{2,0},{3,1},{4,6},{5,7},{6,4},{7,5},{8,10},{9,11},{10,... | collective-permute-start | bytes 393224 | tf_op jit(solution)/shard_map/ppermute | solution.py:228
  18.4 2.6 %collective-permute-start.2 = (bf16[32,1024]{1,0:T(8,128)(2,1)S(1)}, bf16[32,1024]{1,0:T(8,128)(2,1)S(1)}, u32[]{:S(2)}, u32[]{:S(2)}) collective-permute-start(bf16[32,1024]{1,0:T(8,128)(2,1)S(1)} %get-tuple-element.41), channel_id=1, source_target_pairs={{0,8},{4,12},{8,0},{12,4},{1,9},{5,13},{9,1},{13,5},{2,10},{6,14},... | collective-permute-start | bytes 196616 | tf_op jit(solution)/shard_map/ppermute | solution.py:234
  21.0 0.2 collective-permute-start.3
  21.2 3.6 %collective-permute-done.2.refs_2_ = bf16[32,1024]{1,0:T(8,128)(2,1)S(1)} collective-permute-done((bf16[32,1024]{1,0:T(8,128)(2,1)S(1)}, bf16[32,1024]{1,0:T(8,128)(2,1)S(1)}, u32[]{:S(2)}, u32[]{:S(2)}) %collective-permute-start.2) | collective-permute-done | bytes 65568 | tf_op jit(solution)/shard_map/ppermute | solution.py:234
  24.8 2.2 %collective-permute-done.3.refs_3_ = bf16[32,1024]{1,0:T(8,128)(2,1)S(1)} collective-permute-done((bf16[32,1024]{1,0:T(8,128)(2,1)S(1)}, bf16[32,1024]{1,0:T(8,128)(2,1)S(1)}, u32[]{:S(2)}, u32[]{:S(2)}) %collective-permute-start.3) | collective-permute-done | bytes 65568 | tf_op jit(solution)/shard_map/ppermute | solution.py:234
  27.0 0.6 shard_map.96
  27.6 0.6 collective-permute-start.5
  28.3 1.6 %collective-permute-start.14 = (bf16[32,1024]{1,0:T(8,128)(2,1)S(1)}, bf16[32,1024]{1,0:T(8,128)(2,1)S(1)}, u32[]{:S(2)}, u32[]{:S(2)}) collective-permute-start(bf16[32,1024]{1,0:T(8,128)(2,1)S(1)} %get-tuple-element.57), channel_id=1, source_target_pairs={{0,8},{4,12},{8,0},{12,4},{1,9},{5,13},{9,1},{13,5},{2,10},{6,14},... | collective-permute-start | bytes 196616 | tf_op jit(solution)/shard_map/ppermute | solution.py:234
  29.9 2.8 %collective-permute-start.15 = (bf16[32,1024]{1,0:T(8,128)(2,1)S(1)}, bf16[32,1024]{1,0:T(8,128)(2,1)S(1)}, u32[]{:S(2)}, u32[]{:S(2)}) collective-permute-start(bf16[32,1024]{1,0:T(8,128)(2,1)S(1)} %get-tuple-element.58), channel_id=1, source_target_pairs={{0,12},{4,8},{8,4},{12,0},{1,13},{5,9},{9,5},{13,1},{2,14},{6,10},... | collective-permute-start | bytes 196616 | tf_op jit(solution)/shard_map/ppermute | solution.py:234
  32.7 0.9 %collective-permute-done.14.refs_2_ = bf16[32,1024]{1,0:T(8,128)(2,1)S(1)} collective-permute-done((bf16[32,1024]{1,0:T(8,128)(2,1)S(1)}, bf16[32,1024]{1,0:T(8,128)(2,1)S(1)}, u32[]{:S(2)}, u32[]{:S(2)}) %collective-permute-start.14) | collective-permute-done | bytes 65568 | tf_op jit(solution)/shard_map/ppermute | solution.py:234
  33.5 2.5 %collective-permute-done.15.refs_3_ = bf16[32,1024]{1,0:T(8,128)(2,1)S(1)} collective-permute-done((bf16[32,1024]{1,0:T(8,128)(2,1)S(1)}, bf16[32,1024]{1,0:T(8,128)(2,1)S(1)}, u32[]{:S(2)}, u32[]{:S(2)}) %collective-permute-start.15) | collective-permute-done | bytes 65568 | tf_op jit(solution)/shard_map/ppermute | solution.py:234
  36.1 0.4 shard_map.103
  36.5 1.4 %collective-permute-start.16 = (bf16[64,768]{1,0:T(8,128)(2,1)S(1)}, bf16[64,768]{1,0:T(8,128)(2,1)S(1)}, u32[]{:S(2)}, u32[]{:S(2)}) collective-permute-start(bf16[64,768]{1,0:T(8,128)(2,1)S(1)} %get-tuple-element.60), channel_id=1, source_target_pairs={{0,2},{1,3},{2,0},{3,1},{4,6},{5,7},{6,4},{7,5},{8,10},{9,11},{10,... | collective-permute-start | bytes 294920 | tf_op jit(solution)/shard_map/ppermute | solution.py:228
  37.9 4.4 %collective-permute-done.16.refs_3_ = bf16[64,768]{1,0:T(8,128)(2,1)S(1)} collective-permute-done((bf16[64,768]{1,0:T(8,128)(2,1)S(1)}, bf16[64,768]{1,0:T(8,128)(2,1)S(1)}, u32[]{:S(2)}, u32[]{:S(2)}) %collective-permute-start.16) | collective-permute-done | bytes 98336 | tf_op jit(solution)/shard_map/ppermute | solution.py:228
  42.3 0.1 shard_map.104.refs_0_
  42.4 1.4 %collective-permute-start.17 = (bf16[64,1536]{1,0:T(8,128)(2,1)S(1)}, bf16[64,1536]{1,0:T(8,128)(2,1)S(1)}, u32[]{:S(2)}, u32[]{:S(2)}) collective-permute-start(bf16[64,1536]{1,0:T(8,128)(2,1)S(1)} %shard_map.104.refs_0_), channel_id=1, source_target_pairs={{0,2},{1,3},{2,0},{3,1},{4,6},{5,7},{6,4},{7,5},{8,10},{9,11},{10,... | collective-permute-start | bytes 589832 | tf_op jit(solution)/shard_map/ppermute | solution.py:228
  43.8 0.1 shard_map.97.refs_0_.refs_2_
  43.9 0.8 %collective-permute-start.6 = (bf16[64,768]{1,0:T(8,128)(2,1)S(1)}, bf16[64,768]{1,0:T(8,128)(2,1)S(1)}, u32[]{:S(2)}, u32[]{:S(2)}) collective-permute-start(bf16[64,768]{1,0:T(8,128)(2,1)S(1)} %shard_map.97.refs_0_.refs_2_), channel_id=1, source_target_pairs={{0,2},{1,3},{2,0},{3,1},{4,6},{5,7},{6,4},{7,5},{8,10},{9,11},{10,... | collective-permute-start | bytes 294920 | tf_op jit(solution)/shard_map/ppermute | solution.py:228
  44.6 4.5 %collective-permute-done.6.refs_1_.refs_3_ = bf16[64,768]{1,0:T(8,128)(2,1)S(1)} collective-permute-done((bf16[64,768]{1,0:T(8,128)(2,1)S(1)}, bf16[64,768]{1,0:T(8,128)(2,1)S(1)}, u32[]{:S(2)}, u32[]{:S(2)}) %collective-permute-start.6) | collective-permute-done | bytes 98336 | tf_op jit(solution)/shard_map/ppermute | solution.py:228
  49.2 0.6 shard_map.98
  49.8 0.7 collective-permute-start.8
  50.5 2.6 %collective-permute-start.9 = (bf16[32,1024]{1,0:T(8,128)(2,1)S(1)}, bf16[32,1024]{1,0:T(8,128)(2,1)S(1)}, u32[]{:S(2)}, u32[]{:S(2)}) collective-permute-start(bf16[32,1024]{1,0:T(8,128)(2,1)S(1)} %get-tuple-element.50), channel_id=1, source_target_pairs={{0,8},{4,12},{8,0},{12,4},{1,9},{5,13},{9,1},{13,5},{2,10},{6,14},... | collective-permute-start | bytes 196616 | tf_op jit(solution)/shard_map/ppermute | solution.py:234
  53.1 1.2 %collective-permute-start.10 = (bf16[32,1024]{1,0:T(8,128)(2,1)S(1)}, bf16[32,1024]{1,0:T(8,128)(2,1)S(1)}, u32[]{:S(2)}, u32[]{:S(2)}) collective-permute-start(bf16[32,1024]{1,0:T(8,128)(2,1)S(1)} %get-tuple-element.51), channel_id=1, source_target_pairs={{0,12},{4,8},{8,4},{12,0},{1,13},{5,9},{9,5},{13,1},{2,14},{6,10},... | collective-permute-start | bytes 196616 | tf_op jit(solution)/shard_map/ppermute | solution.py:234
  54.3 1.1 %shard_map.105 = (bf16[32,1024]{1,0:T(8,128)(2,1)S(1)}, bf16[32,1024]{1,0:T(8,128)(2,1)S(1)}, bf16[32,1024]{1,0:T(8,128)(2,1)S(1)}, bf16[32,1024]{1,0:T(8,128)(2,1)S(1)}) custom-call(bf16[64,1536]{1,0:T(8,128)(2,1)S(1)} %shard_map.104.refs_0_, bf16[64,1536]{1,0:T(8,128)(2,1)S(1)} %collective-permute-done.17.refs_1_, bf16[512,1536]{1,0:T(8,128)(2,1)S(1)} %bitcast.9, ...), custom_call_target="tpu_custom_call" | custom-call | flops 402653184 | bytes 3145728 | tf_op jit(solution)/shard_map/pallas_call | solution.py:25
  55.5 3.2 %collective-permute-start.19 = (bf16[32,1024]{1,0:T(8,128)(2,1)S(1)}, bf16[32,1024]{1,0:T(8,128)(2,1)S(1)}, u32[]{:S(2)}, u32[]{:S(2)}) collective-permute-start(bf16[32,1024]{1,0:T(8,128)(2,1)S(1)} %get-tuple-element.63), channel_id=1, source_target_pairs={{0,8},{4,12},{8,0},{12,4},{1,9},{5,13},{9,1},{13,5},{2,10},{6,14},... | collective-permute-start | bytes 196616 | tf_op jit(solution)/shard_map/ppermute | solution.py:234
  58.7 1.2 %collective-permute-start.20 = (bf16[32,1024]{1,0:T(8,128)(2,1)S(1)}, bf16[32,1024]{1,0:T(8,128)(2,1)S(1)}, u32[]{:S(2)}, u32[]{:S(2)}) collective-permute-start(bf16[32,1024]{1,0:T(8,128)(2,1)S(1)} %get-tuple-element.64), channel_id=1, source_target_pairs={{0,12},{4,8},{8,4},{12,0},{1,13},{5,9},{9,5},{13,1},{2,14},{6,10},... | collective-permute-start | bytes 196616 | tf_op jit(solution)/shard_map/ppermute | solution.py:234
  59.9 1.4 %collective-permute-start.11 = (bf16[64,1024]{1,0:T(8,128)(2,1)S(1)}, bf16[64,1024]{1,0:T(8,128)(2,1)S(1)}, u32[]{:S(2)}, u32[]{:S(2)}) collective-permute-start(bf16[64,1024]{1,0:T(8,128)(2,1)S(1)} %shard_map.99), channel_id=1, source_target_pairs={{0,2},{1,3},{2,0},{3,1},{4,6},{5,7},{6,4},{7,5},{8,10},{9,11},{10,... | collective-permute-start | bytes 393224 | tf_op jit(solution)/shard_map/ppermute | solution.py:228
  61.3 3.4 %collective-permute-done.20.refs_3_.refs_5_ = bf16[32,1024]{1,0:T(8,128)(2,1)S(1)} collective-permute-done((bf16[32,1024]{1,0:T(8,128)(2,1)S(1)}, bf16[32,1024]{1,0:T(8,128)(2,1)S(1)}, u32[]{:S(2)}, u32[]{:S(2)}) %collective-permute-start.20) | collective-permute-done | bytes 65568 | tf_op jit(solution)/shard_map/ppermute | solution.py:234
  64.8 1.6 %collective-permute-start.21 = (bf16[64,1024]{1,0:T(8,128)(2,1)S(1)}, bf16[64,1024]{1,0:T(8,128)(2,1)S(1)}, u32[]{:S(2)}, u32[]{:S(2)}) collective-permute-start(bf16[64,1024]{1,0:T(8,128)(2,1)S(1)} %shard_map.106), channel_id=1, source_target_pairs={{0,2},{1,3},{2,0},{3,1},{4,6},{5,7},{6,4},{7,5},{8,10},{9,11},{10,... | collective-permute-start | bytes 393224 | tf_op jit(solution)/shard_map/ppermute | solution.py:228
  66.3 0.5 collective-permute-start.24
  66.8 0.8 %collective-permute-done.23.refs_4_ = bf16[64,768]{1,0:T(8,128)(2,1)S(1)} collective-permute-done((bf16[64,768]{1,0:T(8,128)(2,1)S(1)}, bf16[64,768]{1,0:T(8,128)(2,1)S(1)}, u32[]{:S(2)}, u32[]{:S(2)}) %collective-permute-start.23) | collective-permute-done | bytes 98336 | tf_op jit(solution)/shard_map/ppermute | solution.py:224
  67.6 0.2 collective-permute-done.24.refs_5_
  67.8 1.5 %shard_map.108 = f32[512,768]{1,0:T(8,128)} custom-call(bf16[128,512]{1,0:T(8,128)(2,1)S(1)} %get-tuple-element.65.refs_0_, bf16[128,512]{1,0:T(8,128)(2,1)S(1)} %collective-permute-done.22.refs_1_, bf16[64,768]{1,0:T(8,128)(2,1)S(1)} %shard_map.97.refs_0_.refs_2_, bf16[64,768]{1,0:T(8,128)(2,1)S(1)} %collective-permute-done.6.refs_1_.refs_3_, ...), custom_call_target="tpu_custom_call" | custom-call | flops 201326592 | bytes 1572864 | tf_op jit(solution)/shard_map/pallas_call | solution.py:25
  69.3 2.0 %shard_map.100 = bf16[256,2048]{1,0:T(8,128)(2,1)} custom-call(s32[2]{0:T(128)S(1)} %pad_add_fusion.refs_0_, bf16[256,64]{1,0:T(8,128)(2,1)S(1)} %get-tuple-element.35.refs_1_, f32[64,128]{1,0:T(8,128)S(1)} %get-tuple-element.36.refs_2_, bf16[32,1024]{1,0:T(8,128)(2,1)S(1)} %get-tuple-element.48.refs_0_.refs_3_, ...), custom_call_target="tpu_custom_call" | custom-call | flops 134217728 | bytes 2097152 | tf_op jit(solution)/shard_map/pallas_call | solution.py:25
  71.4 1.9 %shard_map.107 = bf16[256,2048]{1,0:T(8,128)(2,1)} custom-call(s32[2]{0:T(128)S(1)} %pad_add_fusion.refs_0_, bf16[256,64]{1,0:T(8,128)(2,1)S(1)} %get-tuple-element.35.refs_1_, bf16[32,1024]{1,0:T(8,128)(2,1)S(1)} %get-tuple-element.61.refs_0_.refs_2_, bf16[32,1024]{1,0:T(8,128)(2,1)S(1)} %collective-permute-done.18.refs_1_.refs_3_, ...), custom_call_target="tpu_custom_call" | custom-call | flops 67108864 | bytes 2097152 | tf_op jit(solution)/shard_map/pallas_call | solution.py:25
  (32 shorter events, 0.3 us)
Async XLA Ops:
  0.6 26.4 %copy-start = (bf16[1,512,1536]{2,1,0:T(8,128)(2,1)S(1)}, bf16[1,512,1536]{2,1,0:T(8,128)(2,1)}, u32[]{:S(2)}) copy-start(bf16[1,512,1536]{2,1,0:T(8,128)(2,1)} %param.12) | copy-start | bytes 4718596
  0.7 1.3 %copy-start.2 = (bf16[256,2048]{1,0:T(8,128)(2,1)S(1)}, bf16[256,2048]{1,0:T(8,128)(2,1)}, u32[]{:S(2)}) copy-start(bf16[256,2048]{1,0:T(8,128)(2,1)} %refs_4_.1) | copy-start | bytes 3145732
  2.1 0.7 copy-start.4
  2.7 0.7 copy-start.5
  3.4 0.7 copy-start.6
  5.6 21.5 %collective-permute-start.4 = (bf16[512,1536]{1,0:T(8,128)(2,1)}, bf16[512,1536]{1,0:T(8,128)(2,1)S(1)}, u32[]{:S(2)}, u32[]{:S(2)}) collective-permute-start(bf16[512,1536]{1,0:T(8,128)(2,1)} %bitcast.7), channel_id=1, source_target_pairs={{0,1},{1,0},{2,3},{3,2},{4,5},{5,4},{6,7},{7,6},{8,9},{9,8},{10,11... | collective-permute-start | bytes 4718600 | tf_op jit(solution)/shard_map/ppermute | solution.py:224
  6.1 30.0 %collective-permute-start.7 = (bf16[512,768]{1,0:T(8,128)(2,1)}, bf16[512,768]{1,0:T(8,128)(2,1)S(1)}, u32[]{:S(2)}, u32[]{:S(2)}) collective-permute-start(bf16[512,768]{1,0:T(8,128)(2,1)} %bitcast.10), channel_id=1, source_target_pairs={{0,1},{1,0},{2,3},{3,2},{4,5},{5,4},{6,7},{7,6},{8,9},{9,8},{10,11... | collective-permute-start | bytes 2359304 | tf_op jit(solution)/shard_map/ppermute | solution.py:224
  6.2 6.7 %collective-permute-start = (bf16[64,1024]{1,0:T(8,128)(2,1)S(1)}, bf16[64,1024]{1,0:T(8,128)(2,1)S(1)}, u32[]{:S(2)}, u32[]{:S(2)}) collective-permute-start(bf16[64,1024]{1,0:T(8,128)(2,1)S(1)} %get-tuple-element.38), channel_id=1, source_target_pairs={{0,2},{1,3},{2,0},{3,1},{4,6},{5,7},{6,4},{7,5},{8,10},{9,11},{10,... | collective-permute-start | bytes 393224 | tf_op jit(solution)/shard_map/ppermute | solution.py:228
  12.8 8.1 %collective-permute-start.1 = (bf16[32,1024]{1,0:T(8,128)(2,1)S(1)}, bf16[32,1024]{1,0:T(8,128)(2,1)S(1)}, u32[]{:S(2)}, u32[]{:S(2)}) collective-permute-start(bf16[32,1024]{1,0:T(8,128)(2,1)S(1)} %get-tuple-element.40), channel_id=1, source_target_pairs={{0,4},{4,0},{8,12},{12,8},{1,5},{5,1},{9,13},{13,9},{2,6},{6,2},{1... | collective-permute-start | bytes 196616 | tf_op jit(solution)/shard_map/ppermute | solution.py:234
  14.7 1.2 %copy-start.3 = (bf16[256,2048]{1,0:T(8,128)(2,1)S(1)}, bf16[256,2048]{1,0:T(8,128)(2,1)}, u32[]{:S(2)}) copy-start(bf16[256,2048]{1,0:T(8,128)(2,1)} %refs_3_.3) | copy-start | bytes 3145732
  16.8 11.4 %collective-permute-start.12 = (bf16[64,1024]{1,0:T(8,128)(2,1)S(1)}, bf16[64,1024]{1,0:T(8,128)(2,1)S(1)}, u32[]{:S(2)}, u32[]{:S(2)}) collective-permute-start(bf16[64,1024]{1,0:T(8,128)(2,1)S(1)} %get-tuple-element.54), channel_id=1, source_target_pairs={{0,2},{1,3},{2,0},{3,1},{4,6},{5,7},{6,4},{7,5},{8,10},{9,11},{10,... | collective-permute-start | bytes 393224 | tf_op jit(solution)/shard_map/ppermute | solution.py:228
  18.4 6.5 %collective-permute-start.2 = (bf16[32,1024]{1,0:T(8,128)(2,1)S(1)}, bf16[32,1024]{1,0:T(8,128)(2,1)S(1)}, u32[]{:S(2)}, u32[]{:S(2)}) collective-permute-start(bf16[32,1024]{1,0:T(8,128)(2,1)S(1)} %get-tuple-element.41), channel_id=1, source_target_pairs={{0,8},{4,12},{8,0},{12,4},{1,9},{5,13},{9,1},{13,5},{2,10},{6,14},... | collective-permute-start | bytes 196616 | tf_op jit(solution)/shard_map/ppermute | solution.py:234
  21.0 6.1 %collective-permute-start.3 = (bf16[32,1024]{1,0:T(8,128)(2,1)S(1)}, bf16[32,1024]{1,0:T(8,128)(2,1)S(1)}, u32[]{:S(2)}, u32[]{:S(2)}) collective-permute-start(bf16[32,1024]{1,0:T(8,128)(2,1)S(1)} %get-tuple-element.42), channel_id=1, source_target_pairs={{0,12},{4,8},{8,4},{12,0},{1,13},{5,9},{9,5},{13,1},{2,14},{6,10},... | collective-permute-start | bytes 196616 | tf_op jit(solution)/shard_map/ppermute | solution.py:234
  27.0 9.0 %copy-start.1 = (bf16[1,512,768]{2,1,0:T(8,128)(2,1)S(1)}, bf16[1,512,768]{2,1,0:T(8,128)(2,1)}, u32[]{:S(2)}) copy-start(bf16[1,512,768]{2,1,0:T(8,128)(2,1)} %param.13) | copy-start | bytes 2359300
  27.6 14.7 %collective-permute-start.5 = (bf16[64,1536]{1,0:T(8,128)(2,1)S(1)}, bf16[64,1536]{1,0:T(8,128)(2,1)S(1)}, u32[]{:S(2)}, u32[]{:S(2)}) collective-permute-start(bf16[64,1536]{1,0:T(8,128)(2,1)S(1)} %get-tuple-element.46), channel_id=1, source_target_pairs={{0,2},{1,3},{2,0},{3,1},{4,6},{5,7},{6,4},{7,5},{8,10},{9,11},{10,... | collective-permute-start | bytes 589832 | tf_op jit(solution)/shard_map/ppermute | solution.py:228
  28.2 4.5 %collective-permute-start.13 = (bf16[32,1024]{1,0:T(8,128)(2,1)S(1)}, bf16[32,1024]{1,0:T(8,128)(2,1)S(1)}, u32[]{:S(2)}, u32[]{:S(2)}) collective-permute-start(bf16[32,1024]{1,0:T(8,128)(2,1)S(1)} %get-tuple-element.56), channel_id=1, source_target_pairs={{0,4},{4,0},{8,12},{12,8},{1,5},{5,1},{9,13},{13,9},{2,6},{6,2},{1... | collective-permute-start | bytes 196616 | tf_op jit(solution)/shard_map/ppermute | solution.py:234
  28.3 5.2 %collective-permute-start.14 = (bf16[32,1024]{1,0:T(8,128)(2,1)S(1)}, bf16[32,1024]{1,0:T(8,128)(2,1)S(1)}, u32[]{:S(2)}, u32[]{:S(2)}) collective-permute-start(bf16[32,1024]{1,0:T(8,128)(2,1)S(1)} %get-tuple-element.57), channel_id=1, source_target_pairs={{0,8},{4,12},{8,0},{12,4},{1,9},{5,13},{9,1},{13,5},{2,10},{6,14},... | collective-permute-start | bytes 196616 | tf_op jit(solution)/shard_map/ppermute | solution.py:234
  29.9 6.1 %collective-permute-start.15 = (bf16[32,1024]{1,0:T(8,128)(2,1)S(1)}, bf16[32,1024]{1,0:T(8,128)(2,1)S(1)}, u32[]{:S(2)}, u32[]{:S(2)}) collective-permute-start(bf16[32,1024]{1,0:T(8,128)(2,1)S(1)} %get-tuple-element.58), channel_id=1, source_target_pairs={{0,12},{4,8},{8,4},{12,0},{1,13},{5,9},{9,5},{13,1},{2,14},{6,10},... | collective-permute-start | bytes 196616 | tf_op jit(solution)/shard_map/ppermute | solution.py:234
  36.5 5.8 %collective-permute-start.16 = (bf16[64,768]{1,0:T(8,128)(2,1)S(1)}, bf16[64,768]{1,0:T(8,128)(2,1)S(1)}, u32[]{:S(2)}, u32[]{:S(2)}) collective-permute-start(bf16[64,768]{1,0:T(8,128)(2,1)S(1)} %get-tuple-element.60), channel_id=1, source_target_pairs={{0,2},{1,3},{2,0},{3,1},{4,6},{5,7},{6,4},{7,5},{8,10},{9,11},{10,... | collective-permute-start | bytes 294920 | tf_op jit(solution)/shard_map/ppermute | solution.py:228
  42.4 11.9 %collective-permute-start.17 = (bf16[64,1536]{1,0:T(8,128)(2,1)S(1)}, bf16[64,1536]{1,0:T(8,128)(2,1)S(1)}, u32[]{:S(2)}, u32[]{:S(2)}) collective-permute-start(bf16[64,1536]{1,0:T(8,128)(2,1)S(1)} %shard_map.104.refs_0_), channel_id=1, source_target_pairs={{0,2},{1,3},{2,0},{3,1},{4,6},{5,7},{6,4},{7,5},{8,10},{9,11},{10,... | collective-permute-start | bytes 589832 | tf_op jit(solution)/shard_map/ppermute | solution.py:228
  43.9 5.3 %collective-permute-start.6 = (bf16[64,768]{1,0:T(8,128)(2,1)S(1)}, bf16[64,768]{1,0:T(8,128)(2,1)S(1)}, u32[]{:S(2)}, u32[]{:S(2)}) collective-permute-start(bf16[64,768]{1,0:T(8,128)(2,1)S(1)} %shard_map.97.refs_0_.refs_2_), channel_id=1, source_target_pairs={{0,2},{1,3},{2,0},{3,1},{4,6},{5,7},{6,4},{7,5},{8,10},{9,11},{10,... | collective-permute-start | bytes 294920 | tf_op jit(solution)/shard_map/ppermute | solution.py:228
  49.8 8.9 %collective-permute-start.8 = (bf16[32,1024]{1,0:T(8,128)(2,1)S(1)}, bf16[32,1024]{1,0:T(8,128)(2,1)S(1)}, u32[]{:S(2)}, u32[]{:S(2)}) collective-permute-start(bf16[32,1024]{1,0:T(8,128)(2,1)S(1)} %get-tuple-element.49), channel_id=1, source_target_pairs={{0,4},{4,0},{8,12},{12,8},{1,5},{5,1},{9,13},{13,9},{2,6},{6,2},{1... | collective-permute-start | bytes 196616 | tf_op jit(solution)/shard_map/ppermute | solution.py:234
  50.5 9.4 %collective-permute-start.9 = (bf16[32,1024]{1,0:T(8,128)(2,1)S(1)}, bf16[32,1024]{1,0:T(8,128)(2,1)S(1)}, u32[]{:S(2)}, u32[]{:S(2)}) collective-permute-start(bf16[32,1024]{1,0:T(8,128)(2,1)S(1)} %get-tuple-element.50), channel_id=1, source_target_pairs={{0,8},{4,12},{8,0},{12,4},{1,9},{5,13},{9,1},{13,5},{2,10},{6,14},... | collective-permute-start | bytes 196616 | tf_op jit(solution)/shard_map/ppermute | solution.py:234
  53.1 6.8 %collective-permute-start.10 = (bf16[32,1024]{1,0:T(8,128)(2,1)S(1)}, bf16[32,1024]{1,0:T(8,128)(2,1)S(1)}, u32[]{:S(2)}, u32[]{:S(2)}) collective-permute-start(bf16[32,1024]{1,0:T(8,128)(2,1)S(1)} %get-tuple-element.51), channel_id=1, source_target_pairs={{0,12},{4,8},{8,4},{12,0},{1,13},{5,9},{9,5},{13,1},{2,14},{6,10},... | collective-permute-start | bytes 196616 | tf_op jit(solution)/shard_map/ppermute | solution.py:234
  55.4 5.9 %collective-permute-start.18 = (bf16[32,1024]{1,0:T(8,128)(2,1)S(1)}, bf16[32,1024]{1,0:T(8,128)(2,1)S(1)}, u32[]{:S(2)}, u32[]{:S(2)}) collective-permute-start(bf16[32,1024]{1,0:T(8,128)(2,1)S(1)} %get-tuple-element.62), channel_id=1, source_target_pairs={{0,4},{4,0},{8,12},{12,8},{1,5},{5,1},{9,13},{13,9},{2,6},{6,2},{1... | collective-permute-start | bytes 196616 | tf_op jit(solution)/shard_map/ppermute | solution.py:234
  55.5 5.8 %collective-permute-start.19 = (bf16[32,1024]{1,0:T(8,128)(2,1)S(1)}, bf16[32,1024]{1,0:T(8,128)(2,1)S(1)}, u32[]{:S(2)}, u32[]{:S(2)}) collective-permute-start(bf16[32,1024]{1,0:T(8,128)(2,1)S(1)} %get-tuple-element.63), channel_id=1, source_target_pairs={{0,8},{4,12},{8,0},{12,4},{1,9},{5,13},{9,1},{13,5},{2,10},{6,14},... | collective-permute-start | bytes 196616 | tf_op jit(solution)/shard_map/ppermute | solution.py:234
  58.7 6.1 %collective-permute-start.20 = (bf16[32,1024]{1,0:T(8,128)(2,1)S(1)}, bf16[32,1024]{1,0:T(8,128)(2,1)S(1)}, u32[]{:S(2)}, u32[]{:S(2)}) collective-permute-start(bf16[32,1024]{1,0:T(8,128)(2,1)S(1)} %get-tuple-element.64), channel_id=1, source_target_pairs={{0,12},{4,8},{8,4},{12,0},{1,13},{5,9},{9,5},{13,1},{2,14},{6,10},... | collective-permute-start | bytes 196616 | tf_op jit(solution)/shard_map/ppermute | solution.py:234
  59.9 7.0 %collective-permute-start.22 = (bf16[128,512]{1,0:T(8,128)(2,1)S(1)}, bf16[128,512]{1,0:T(8,128)(2,1)S(1)}, u32[]{:S(2)}, u32[]{:S(2)}) collective-permute-start(bf16[128,512]{1,0:T(8,128)(2,1)S(1)} %get-tuple-element.66), channel_id=1, source_target_pairs={{0,1},{1,0},{2,3},{3,2},{4,5},{5,4},{6,7},{7,6},{8,9},{9,8},{10,11... | collective-permute-start | bytes 393224 | tf_op jit(solution)/shard_map/ppermute | solution.py:224
  59.9 9.4 %collective-permute-start.11 = (bf16[64,1024]{1,0:T(8,128)(2,1)S(1)}, bf16[64,1024]{1,0:T(8,128)(2,1)S(1)}, u32[]{:S(2)}, u32[]{:S(2)}) collective-permute-start(bf16[64,1024]{1,0:T(8,128)(2,1)S(1)} %shard_map.99), channel_id=1, source_target_pairs={{0,2},{1,3},{2,0},{3,1},{4,6},{5,7},{6,4},{7,5},{8,10},{9,11},{10,... | collective-permute-start | bytes 393224 | tf_op jit(solution)/shard_map/ppermute | solution.py:228
  64.8 6.6 %collective-permute-start.21 = (bf16[64,1024]{1,0:T(8,128)(2,1)S(1)}, bf16[64,1024]{1,0:T(8,128)(2,1)S(1)}, u32[]{:S(2)}, u32[]{:S(2)}) collective-permute-start(bf16[64,1024]{1,0:T(8,128)(2,1)S(1)} %shard_map.106), channel_id=1, source_target_pairs={{0,2},{1,3},{2,0},{3,1},{4,6},{5,7},{6,4},{7,5},{8,10},{9,11},{10,... | collective-permute-start | bytes 393224 | tf_op jit(solution)/shard_map/ppermute | solution.py:228
  66.3 1.3 %collective-permute-start.23 = (bf16[64,768]{1,0:T(8,128)(2,1)S(1)}, bf16[64,768]{1,0:T(8,128)(2,1)S(1)}, u32[]{:S(2)}, u32[]{:S(2)}) collective-permute-start(bf16[64,768]{1,0:T(8,128)(2,1)S(1)} %shard_map.97.refs_0_.refs_2_), channel_id=1, source_target_pairs={{0,1},{1,0},{2,3},{3,2},{4,5},{5,4},{6,7},{7,6},{8,9},{9,8},{10,11... | collective-permute-start | bytes 294920 | tf_op jit(solution)/shard_map/ppermute | solution.py:224
  66.3 1.5 %collective-permute-start.24 = (bf16[64,768]{1,0:T(8,128)(2,1)S(1)}, bf16[64,768]{1,0:T(8,128)(2,1)S(1)}, u32[]{:S(2)}, u32[]{:S(2)}) collective-permute-start(bf16[64,768]{1,0:T(8,128)(2,1)S(1)} %collective-permute-done.6.refs_1_.refs_3_), channel_id=1, source_target_pairs={{0,1},{1,0},{2,3},{3,2},{4,5},{5,4},{6,7},{7,6},{8,9},{9,8},{10,11... | collective-permute-start | bytes 294920 | tf_op jit(solution)/shard_map/ppermute | solution.py:224

commit v3 on v2

--- a/solution.py
+++ b/solution.py
@@ -18,19 +18,32 @@
     )
 
 
-def call(body, out_shape, args, flops=0, nbytes=0, smem=0, far=0, scratch=()):
+def call(body, out_shape, args, flops=0, nbytes=0, smem=0, far=0, after=(), **kw):
     specs = [pl.BlockSpec(memory_space=pltpu.SMEM)] * smem
     specs += [pl.BlockSpec(memory_space=pltpu.VMEM)] * (len(args) - smem - far)
-    specs += [pl.BlockSpec(memory_space=pl.ANY)] * far
-    return pl.pallas_call(
-        body,
-        out_shape=out_shape,
+    specs += [pl.BlockSpec(memory_space=pltpu.HBM)] * far
+    specs += [pl.BlockSpec(memory_space=pl.ANY)] * len(after)
+    out_specs = kw.pop("out_specs", [pl.BlockSpec(memory_space=pltpu.VMEM)] * len(out_shape))
+    args = [
+        pltpu.with_memory_space_constraint(arg, pltpu.HBM) if i >= len(args) - far else arg
+        for i, arg in enumerate(args)
+    ]
+    count, first, last = len(args), len(args) + len(after), len(args) + len(after) + len(out_shape)
+
+    def kernel(*refs):
+        refs[last][...] = jnp.zeros(refs[last].shape, F32)
+        body(*refs[:count], *refs[first:last], *refs[last + 1 :])
+
+    *out, token = pl.pallas_call(
+        kernel,
+        out_shape=[*out_shape, shape((8, 128), F32)],
         in_specs=specs,
-        scratch_shapes=list(scratch),
-        out_specs=jax.tree.map(lambda _: pl.BlockSpec(memory_space=pltpu.VMEM), out_shape),
+        out_specs=[*out_specs, pl.BlockSpec(memory_space=pltpu.VMEM)],
         compiler_params=pltpu.CompilerParams(vmem_limit_bytes=VMEM),
         cost_estimate=pl.CostEstimate(flops=flops, bytes_accessed=nbytes, transcendentals=0),
-    )(*args)
+        **kw,
+    )(*args, *after)
+    return out, token
 
 
 def shape(dims, kind=BF16):
@@ -41,10 +54,16 @@
     return pl.ds(pl.multiple_of((own_part ^ (kx * CORES + kc)) * part, part), part)
 
 
-def rows_kernel(groups, spread, capacity, where, ids, gates, order, tok_hbm, *refs):
-    *outs, pick_out, turned_out, gate_out, tok, sem = refs
-    copy = pltpu.make_async_copy(tok_hbm, tok, sem)
-    copy.start()
+def rows_kernel(groups, spread, capacity, where, *refs):
+    *outs, pick_out, turned_out, gate_out, cot, ids, gates, order, tok, sems = refs[5:]
+    copies = [
+        pltpu.make_async_copy(source, target, sems.at[i])
+        for i, (source, target) in enumerate(zip(refs[:5], (ids, gates, order, tok, cot)))
+    ]
+    for copy in copies:
+        copy.start()
+    for copy in copies[:3]:
+        copy.wait()
     choices, count = ids.shape
     slots = groups * capacity
     part = tok.shape[1] // (spread * CORES)
@@ -69,11 +88,12 @@
     gate_out[...] = jnp.broadcast_to(slot_gate, gate_out.shape)
     pick = pick.astype(BF16)
     pick_out[...] = pick
-    copy.wait()
+    copies[3].wait()
     for kx in reversed(range(spread)):
         for kc in range(CORES):
             rows = product(pick, tok[:, columns(where[1], kx, kc, part)], 1, 0)
             outs[kx][:, kc * part : (kc + 1) * part] = rows.astype(BF16)
+    copies[4].wait()
 
 
 def grads_kernel(groups, spread, capacity, where, pick, gate, cot, *outs):
@@ -197,14 +217,24 @@
             out[:, columns(where[1], kx, kc, part)] = product(twice, both, 1, 0).astype(BF16)
 
 
-def d_tokens_kernel(groups, spread, capacity, where, turned, *refs):
-    out = refs[-1]
+def d_tokens_kernel(groups, spread, capacity, span, where, turned, *refs):
+    *refs, out, held, sems = refs
     part = out.shape[1] // (spread * CORES)
-    for kx in range(spread):
+    copies = []
+    for kx in span:
         for kc in range(CORES):
             cols = slice(kc * part, (kc + 1) * part)
             rows = returned(groups, spread, capacity, refs, kx, cols)
-            out[:, columns(where[1], kx, kc, part)] = product(turned[...], rows, 1, 0).astype(BF16)
+            n = len(copies)
+            held[n] = product(turned[...], rows, 1, 0).astype(BF16)
+            copies.append(
+                pltpu.make_async_copy(
+                    held.at[n], out.at[:, columns(where[1], kx, kc, part)], sems.at[n]
+                )
+            )
+            copies[-1].start()
+    for copy in copies:
+        copy.wait()
 
 
 def per_device(tokens, cotangent, route_ids, route_gates, served_order, w_in, w_out):
@@ -241,36 +271,49 @@
     by_x = [shape((slots, half))] * spread
     by_e = [shape((spread * capacity, half))] * groups
 
-    def inward(near, *far):
-        chunks = call(body(regroup_kernel), by_e, (near, *to_x(far)), nbytes=4 * slots * width)
+    def inward(near, far, after):
+        chunks, _ = call(
+            body(regroup_kernel), by_e, (near, *far), nbytes=4 * slots * width, after=after
+        )
         return to_expert(chunks)
 
     def outward(left, own, sib):
-        chunks = call(
+        chunks, token = call(
             body(result_kernel),
             by_e,
             (*left, own, sib),
             flops=2 * spread * slots * half * own.shape[1],
             nbytes=2 * half * own.shape[1],
         )
-        chunks = to_expert(chunks)
-        far = call(body(far_kernel), by_x[1:], chunks, nbytes=4 * slots * width)
-        return (*chunks, *to_x(far))
+        return to_expert(chunks), token
+
+    def outward_far(chunks, after):
+        far, _ = call(
+            body(far_kernel), by_x[1:], chunks, nbytes=4 * slots * width, after=after
+        )
+        return to_x(far)
 
     in_own, out_own = w_in[0], w_out[0]
-    *rows, pick, turned, gate = call(
+    (*rows, pick, turned, gate, cotangent), _ = call(
         body(rows_kernel),
-        by_x + [shape((slots, count)), shape((count, slots)), shape((slots, 128), F32)],
-        (where, route_ids.T, route_gates.T, served_order, tokens),
+        by_x
+        + [shape((slots, count)), shape((count, slots)), shape((slots, 128), F32)]
+        + [shape(cotangent.shape)],
+        (where, route_ids.T, route_gates.T, served_order, tokens, cotangent),
         flops=2 * slots * count * width,
         nbytes=4 * count * width,
         smem=1,
-        far=1,
-        scratch=(pltpu.VMEM(tokens.shape, BF16), pltpu.SemaphoreType.DMA),
-    )
-    in_own, out_own, pick = lax.optimization_barrier((in_own, out_own, pick))
-    in_sib, out_sib = to_core(in_own), to_core(out_own)
-    grads = call(
+        far=5,
+        scratch_shapes=[
+            pltpu.VMEM(route_ids.shape[::-1], jnp.int32),
+            pltpu.VMEM(route_gates.shape[::-1], F32),
+            pltpu.VMEM(served_order.shape, jnp.int32),
+            pltpu.VMEM(tokens.shape, BF16),
+            pltpu.SemaphoreType.DMA((5,)),
+        ],
+    )
+    far = to_x(rows[1:])
+    grads, grads_token = call(
         body(grads_kernel),
         by_x,
         (where, pick, gate, cotangent),
@@ -278,9 +321,11 @@
         nbytes=4 * count * width,
         smem=1,
     )
-    rows = inward(*rows)
-    grads = inward(*grads)
-    pre, *pre_far = call(
+    in_own, out_own, rows[0] = lax.optimization_barrier((in_own, out_own, rows[0]))
+    in_sib, out_sib = to_core(in_own), to_core(out_own)
+    rows = inward(rows[0], far, (grads_token,))
+    grads = inward(grads[0], to_x(grads[1:]), ())
+    (pre, *pre_far), _ = call(
         body(pre_kernel),
         [shape((slots, 2 * feed), F32)] + [shape((slots, 2 * feed))] * (spread - 1),
         (*rows, in_own, in_sib),
@@ -288,7 +333,11 @@
         nbytes=4 * half * feed,
     )
     pre = (pre, *to_x(pre_far))
-    own_grads, sib_grads, back, *back_far = call(
+    (hidden,), hidden_token = call(
+        hidden_kernel, [shape((slots, feed))], pre, nbytes=12 * slots * feed
+    )
+    hidden = (hidden, *to_x([hidden] * (spread - 1)))
+    (own_grads, sib_grads, back, *back_far), _ = call(
         body(back_kernel),
         [shape((spread * slots, part))] * 2
         + [shape((slots, feed), F32)]
@@ -296,36 +345,62 @@
         (*grads, out_own, out_sib),
         flops=2 * spread * slots * half * feed,
         nbytes=2 * half * feed,
+        after=(hidden_token,),
     )
     back = (back, *to_x(back_far))
-    hidden = call(hidden_kernel, shape((slots, feed)), pre, nbytes=12 * slots * feed)
-    hidden = (hidden, *to_x([hidden] * (spread - 1)))
-    expert_out = outward(hidden, out_own, out_sib)
-    d_pre = call(d_pre_kernel, shape((slots, 2 * feed)), (*pre, *back), nbytes=20 * slots * feed)
+    expert_out, out_token = outward(hidden, out_own, out_sib)
+    (d_pre,), _ = call(
+        d_pre_kernel,
+        [shape((slots, 2 * feed))],
+        (*pre, *back),
+        nbytes=20 * slots * feed,
+        after=(out_token,),
+    )
     d_pre = (d_pre, *to_x([d_pre] * (spread - 1)))
-    d_rows = outward(d_pre, in_own, in_sib)
-    d_w_out = call(
+    d_rows, _ = outward(d_pre, in_own, in_sib)
+    (d_w_out,), weight_token = call(
         lambda *refs: weight_kernel(spread, *refs),
-        shape((part, feed), F32),
+        [shape((part, feed), F32)],
         (own_grads, to_core(sib_grads), *hidden, *[to_core(value) for value in hidden]),
         flops=4 * spread * slots * part * feed,
         nbytes=4 * part * feed,
     )
-    combined = call(
+    expert_out_far = outward_far(expert_out, ())
+    d_rows_far = outward_far(d_rows, (weight_token,))
+    (combined,), combined_token = call(
         body(combine_kernel),
-        shape((count, width)),
-        (where, turned, gate, *expert_out),
+        [shape((count, width))],
+        (where, turned, gate, *expert_out, *expert_out_far),
         flops=4 * slots * count * width,
         nbytes=4 * count * width,
         smem=1,
     )
-    d_tokens = call(
-        body(d_tokens_kernel),
-        shape((count, width)),
-        (where, turned, *d_rows),
-        flops=2 * slots * count * width,
-        nbytes=4 * count * width,
-        smem=1,
+
+    def d_tokens_columns(span, *operands, **kw):
+        pieces = len(span) * CORES
+        (value,), token = call(
+            lambda *refs: d_tokens_kernel(*sizes, span, *refs),
+            [shape((count, width))],
+            (where, turned, *d_rows, *operands),
+            flops=2 * slots * half * count,
+            nbytes=2 * count * half,
+            smem=1,
+            out_specs=[pl.BlockSpec(memory_space=pltpu.HBM)],
+            scratch_shapes=[
+                pltpu.VMEM((pieces, count, part), BF16),
+                pltpu.SemaphoreType.DMA((pieces,)),
+            ],
+            **kw,
+        )
+        return value
+
+    d_tokens = d_tokens_columns([0], after=(combined_token,))
+    d_tokens = d_tokens_columns(
+        range(1, spread),
+        *d_rows_far,
+        d_tokens,
+        far=1,
+        input_output_aliases={2 + groups + len(d_rows_far): 0},
     )
     return combined, d_tokens, d_w_out[None]
 

time: 73.6 us -> 65.2 us (0.89)
  waiting for transfers between devices: 26.3 us -> 15.1 us
  Pallas kernels: 10.7 us -> 18.7 us
  local copies, waits for them, and re-layouts: 4.63 us -> 0.01 us
    pallas_call x15 -> x16, Pallas kernels: 10.7 us -> 18.7 us  [call(): pl.pallas_call(kernel, out_shape=[*out_shape, shape((8, 128), F32)], in_s...]
    ppermute x8, waiting for transfers between devices: 12.7 us -> 7.07 us  [to_x(): lax.ppermute(value, 'fsdp', [(i, i ^ (k + 1) * CORES) for i in range(part...]
    ppermute x12, waiting for transfers between devices: 12.7 us -> 8.04 us  [to_expert(): lax.ppermute(value, 'expert', [(i, i ^ ke) for i in range(groups)])]
    unnamed x14 -> x4, local copies, waits for them, and re-layouts: 4.63 us -> 0.01 us
    ppermute x12, starting transfers between devices: 18 us -> 16.5 us  [to_expert(): lax.ppermute(value, 'expert', [(i, i ^ ke) for i in range(groups)])]
    ppermute x8, starting transfers between devices: 11.6 us -> 12.7 us  [to_x(): lax.ppermute(value, 'fsdp', [(i, i ^ (k + 1) * CORES) for i in range(part...]
    ppermute x5, waiting for transfers between devices: 0.95 us -> 0.01 us  [to_core(): return lax.ppermute(value, 'fsdp', [(i, i ^ 1) for i in range(parts)])]
  transfers between devices with their start and end apart: 25 -> 25, of which waited for: 10 -> 7; matrix products, arithmetic and copies ran while one was open for 0% -> 0% of each run, Pallas kernels for 10% -> 20%
where the time goes in v3:
time: 65.2 us; the launch traced here: 65 us
  starting transfers between devices  30.3 us (46%)
  Pallas kernels  18.7 us (29%)
  waiting for transfers between devices  15.1 us (23%)
  between operations  0.73 us (1%)
    pallas_call x16, Pallas kernels, call(): pl.pallas_call(kernel, out_shape=[*out_shape, shape((8, 128), F32)], in_s...  18.7 us
    ppermute x12, starting transfers between devices, to_expert(): lax.ppermute(value, 'expert', [(i, i ^ ke) for i in range(groups)])  16.5 us
    ppermute x8, starting transfers between devices, to_x(): lax.ppermute(value, 'fsdp', [(i, i ^ (k + 1) * CORES) for i in range(part...  12.7 us
    ppermute x12, waiting for transfers between devices, to_expert(): lax.ppermute(value, 'expert', [(i, i ^ ke) for i in range(groups)])  8.04 us
    ppermute x8, waiting for transfers between devices, to_x(): lax.ppermute(value, 'fsdp', [(i, i ^ (k + 1) * CORES) for i in range(part...  7.07 us
  transfers between devices with their start and end apart: 25, of which 7 were waited for; matrix products, arithmetic and copies ran while one was open for 0% of the time, Pallas kernels for 20%

profile of v3, /device:TPU:0, one launch (start us, length us, event | category | flops | bytes accessed | tf_op | source)
XLA Modules:
  0.0 65.0 jit_solution(5119766898736315741)
XLA Ops:
  0.6 0.1 pad_add_fusion.refs_0_
  0.7 2.8 %shard_map.94 = (bf16[64,1024]{1,0:T(8,128)(2,1)S(1)}, bf16[64,1024]{1,0:T(8,128)(2,1)S(1)}, bf16[64,256]{1,0:T(8,128)(2,1)S(1)}, bf16[256,64]{1,0:T(8,128)(2,1)...) custom-call(s32[2]{0:T(128)S(1)} %pad_add_fusion.refs_0_, s32[8,256]{1,0:T(8,128)} %bitcast.13, ...), custom_call_target="tpu_custom_call" | custom-call | flops 67108864 | bytes 2097152 | tf_op jit(solution)/shard_map/pallas_call | solution.py:37
  3.5 0.5 collective-permute-start.4
  4.0 0.1 collective-permute-start.7
  4.1 2.9 %collective-permute-start = (bf16[64,1024]{1,0:T(8,128)(2,1)S(1)}, bf16[64,1024]{1,0:T(8,128)(2,1)S(1)}, u32[]{:S(2)}, u32[]{:S(2)}) collective-permute-start(bf16[64,1024]{1,0:T(8,128)(2,1)S(1)} %get-tuple-element.53), channel_id=1, source_target_pairs={{0,2},{1,3},{2,0},{3,1},{4,6},{5,7},{6,4},{7,5},{8,10},{9,11},{10,... | collective-permute-start | bytes 393224 | tf_op jit(solution)/shard_map/ppermute | solution.py:258
  7.0 0.8 %shard_map.95 = (bf16[64,1024]{1,0:T(8,128)(2,1)S(1)}, bf16[64,1024]{1,0:T(8,128)(2,1)S(1)}, f32[8,128]{1,0:T(8,128)S(1)}) custom-call(s32[2]{0:T(128)S(1)} %pad_add_fusion.refs_0_, bf16[64,256]{1,0:T(8,128)(2,1)S(1)} %get-tuple-element.54.refs_1_, f32[64,128]{1,0:T(8,128)S(1)} %get-tuple-element.50.refs_2_, bf16[256,2048]{1,0:T(8,128)(2,1)S(1)} %get-tuple-element.55.refs_3_), custom_call_target="tpu_custom_call" | custom-call | flops 67108864 | bytes 2097152 | tf_op jit(solution)/shard_map/pallas_call | solution.py:37
  7.9 2.9 %collective-permute-done.refs_1_ = bf16[64,1024]{1,0:T(8,128)(2,1)S(1)} collective-permute-done((bf16[64,1024]{1,0:T(8,128)(2,1)S(1)}, bf16[64,1024]{1,0:T(8,128)(2,1)S(1)}, u32[]{:S(2)}, u32[]{:S(2)}) %collective-permute-start) | collective-permute-done | bytes 131104 | tf_op jit(solution)/shard_map/ppermute | solution.py:258
  10.8 0.6 shard_map.96
  11.4 1.8 %collective-permute-start.1 = (bf16[32,1024]{1,0:T(8,128)(2,1)S(1)}, bf16[32,1024]{1,0:T(8,128)(2,1)S(1)}, u32[]{:S(2)}, u32[]{:S(2)}) collective-permute-start(bf16[32,1024]{1,0:T(8,128)(2,1)S(1)} %get-tuple-element.58), channel_id=1, source_target_pairs={{0,4},{4,0},{8,12},{12,8},{1,5},{5,1},{9,13},{13,9},{2,6},{6,2},{1... | collective-permute-start | bytes 196616 | tf_op jit(solution)/shard_map/ppermute | solution.py:264
  13.2 2.6 %collective-permute-start.2 = (bf16[32,1024]{1,0:T(8,128)(2,1)S(1)}, bf16[32,1024]{1,0:T(8,128)(2,1)S(1)}, u32[]{:S(2)}, u32[]{:S(2)}) collective-permute-start(bf16[32,1024]{1,0:T(8,128)(2,1)S(1)} %get-tuple-element.59), channel_id=1, source_target_pairs={{0,8},{4,12},{8,0},{12,4},{1,9},{5,13},{9,1},{13,5},{2,10},{6,14},... | collective-permute-start | bytes 196616 | tf_op jit(solution)/shard_map/ppermute | solution.py:264
  15.8 0.0 collective-permute-start.3
  15.8 0.0 collective-permute-done.1.refs_1_
  15.8 2.2 %collective-permute-start.12 = (bf16[64,1024]{1,0:T(8,128)(2,1)S(1)}, bf16[64,1024]{1,0:T(8,128)(2,1)S(1)}, u32[]{:S(2)}, u32[]{:S(2)}) collective-permute-start(bf16[64,1024]{1,0:T(8,128)(2,1)S(1)} %get-tuple-element.73), channel_id=1, source_target_pairs={{0,2},{1,3},{2,0},{3,1},{4,6},{5,7},{6,4},{7,5},{8,10},{9,11},{10,... | collective-permute-start | bytes 393224 | tf_op jit(solution)/shard_map/ppermute | solution.py:258
  18.0 1.9 %collective-permute-done.2.refs_2_ = bf16[32,1024]{1,0:T(8,128)(2,1)S(1)} collective-permute-done((bf16[32,1024]{1,0:T(8,128)(2,1)S(1)}, bf16[32,1024]{1,0:T(8,128)(2,1)S(1)}, u32[]{:S(2)}, u32[]{:S(2)}) %collective-permute-start.2) | collective-permute-done | bytes 65568 | tf_op jit(solution)/shard_map/ppermute | solution.py:264
  19.9 2.0 %collective-permute-done.3.refs_3_ = bf16[32,1024]{1,0:T(8,128)(2,1)S(1)} collective-permute-done((bf16[32,1024]{1,0:T(8,128)(2,1)S(1)}, bf16[32,1024]{1,0:T(8,128)(2,1)S(1)}, u32[]{:S(2)}, u32[]{:S(2)}) %collective-permute-start.3) | collective-permute-done | bytes 65568 | tf_op jit(solution)/shard_map/ppermute | solution.py:264
  21.9 1.1 %shard_map.97 = (f32[64,1536]{1,0:T(8,128)S(1)}, bf16[64,1536]{1,0:T(8,128)(2,1)S(1)}, f32[8,128]{1,0:T(8,128)}) custom-call(bf16[32,1024]{1,0:T(8,128)(2,1)S(1)} %get-tuple-element.57.refs_0_, bf16[32,1024]{1,0:T(8,128)(2,1)S(1)} %collective-permute-done.1.refs_1_, bf16[32,1024]{1,0:T(8,128)(2,1)S(1)} %collective-permute-done.2.refs_2_, ...), custom_call_target="tpu_custom_call" | custom-call | flops 402653184 | bytes 3145728 | tf_op jit(solution)/shard_map/pallas_call | solution.py:37
  22.9 1.5 %collective-permute-start.5 = (bf16[64,1536]{1,0:T(8,128)(2,1)S(1)}, bf16[64,1536]{1,0:T(8,128)(2,1)S(1)}, u32[]{:S(2)}, u32[]{:S(2)}) collective-permute-start(bf16[64,1536]{1,0:T(8,128)(2,1)S(1)} %get-tuple-element.63), channel_id=1, source_target_pairs={{0,2},{1,3},{2,0},{3,1},{4,6},{5,7},{6,4},{7,5},{8,10},{9,11},{10,... | collective-permute-start | bytes 589832 | tf_op jit(solution)/shard_map/ppermute | solution.py:258
  24.4 0.0 collective-permute-done.12.refs_1_
  24.4 0.6 shard_map.102
  25.0 1.8 %collective-permute-start.14 = (bf16[32,1024]{1,0:T(8,128)(2,1)S(1)}, bf16[32,1024]{1,0:T(8,128)(2,1)S(1)}, u32[]{:S(2)}, u32[]{:S(2)}) collective-permute-start(bf16[32,1024]{1,0:T(8,128)(2,1)S(1)} %get-tuple-element.76), channel_id=1, source_target_pairs={{0,8},{4,12},{8,0},{12,4},{1,9},{5,13},{9,1},{13,5},{2,10},{6,14},... | collective-permute-start | bytes 196616 | tf_op jit(solution)/shard_map/ppermute | solution.py:264
  26.8 2.6 %collective-permute-start.15 = (bf16[32,1024]{1,0:T(8,128)(2,1)S(1)}, bf16[32,1024]{1,0:T(8,128)(2,1)S(1)}, u32[]{:S(2)}, u32[]{:S(2)}) collective-permute-start(bf16[32,1024]{1,0:T(8,128)(2,1)S(1)} %get-tuple-element.77), channel_id=1, source_target_pairs={{0,12},{4,8},{8,4},{12,0},{1,13},{5,9},{9,5},{13,1},{2,14},{6,10},... | collective-permute-start | bytes 196616 | tf_op jit(solution)/shard_map/ppermute | solution.py:264
  29.4 0.1 shard_map.98
  29.5 1.6 %collective-permute-start.6 = (bf16[64,768]{1,0:T(8,128)(2,1)S(1)}, bf16[64,768]{1,0:T(8,128)(2,1)S(1)}, u32[]{:S(2)}, u32[]{:S(2)}) collective-permute-start(bf16[64,768]{1,0:T(8,128)(2,1)S(1)} %get-tuple-element.64.refs_0_.refs_2_), channel_id=1, source_target_pairs={{0,2},{1,3},{2,0},{3,1},{4,6},{5,7},{6,4},{7,5},{8,10},{9,11},{10,... | collective-permute-start | bytes 294920 | tf_op jit(solution)/shard_map/ppermute | solution.py:258
  31.1 1.8 %collective-permute-done.15.refs_3_ = bf16[32,1024]{1,0:T(8,128)(2,1)S(1)} collective-permute-done((bf16[32,1024]{1,0:T(8,128)(2,1)S(1)}, bf16[32,1024]{1,0:T(8,128)(2,1)S(1)}, u32[]{:S(2)}, u32[]{:S(2)}) %collective-permute-start.15) | collective-permute-done | bytes 65568 | tf_op jit(solution)/shard_map/ppermute | solution.py:264
  32.9 0.9 %shard_map.103 = (bf16[128,512]{1,0:T(8,128)(2,1)S(1)}, bf16[128,512]{1,0:T(8,128)(2,1)S(1)}, f32[64,768]{1,0:T(8,128)S(1)}, bf16[64,768]{1,0:T(8,128)(2,1)S(1)}, f32[8,128]{1,0:T(8,128)}) custom-call(bf16[32,1024]{1,0:T(8,128)(2,1)S(1)} %get-tuple-element.74.refs_0_, bf16[32,1024]{1,0:T(8,128)(2,1)S(1)} %collective-permute-done.13.refs_1_, ...), custom_call_target="tpu_custom_call" | custom-call | flops 201326592 | bytes 1572864 | tf_op jit(solution)/shard_map/pallas_call | solution.py:37
  33.8 0.7 %collective-permute-start.16 = (bf16[64,768]{1,0:T(8,128)(2,1)S(1)}, bf16[64,768]{1,0:T(8,128)(2,1)S(1)}, u32[]{:S(2)}, u32[]{:S(2)}) collective-permute-start(bf16[64,768]{1,0:T(8,128)(2,1)S(1)} %get-tuple-element.80), channel_id=1, source_target_pairs={{0,2},{1,3},{2,0},{3,1},{4,6},{5,7},{6,4},{7,5},{8,10},{9,11},{10,... | collective-permute-start | bytes 294920 | tf_op jit(solution)/shard_map/ppermute | solution.py:258
  34.6 0.6 shard_map.99
  35.2 4.2 %collective-permute-done.16.refs_3_ = bf16[64,768]{1,0:T(8,128)(2,1)S(1)} collective-permute-done((bf16[64,768]{1,0:T(8,128)(2,1)S(1)}, bf16[64,768]{1,0:T(8,128)(2,1)S(1)}, u32[]{:S(2)}, u32[]{:S(2)}) %collective-permute-start.16) | collective-permute-done | bytes 98336 | tf_op jit(solution)/shard_map/ppermute | solution.py:258
  39.4 0.6 shard_map.104
  40.0 0.8 %collective-permute-start.17 = (bf16[64,1536]{1,0:T(8,128)(2,1)S(1)}, bf16[64,1536]{1,0:T(8,128)(2,1)S(1)}, u32[]{:S(2)}, u32[]{:S(2)}) collective-permute-start(bf16[64,1536]{1,0:T(8,128)(2,1)S(1)} %get-tuple-element.82.refs_0_), channel_id=1, source_target_pairs={{0,2},{1,3},{2,0},{3,1},{4,6},{5,7},{6,4},{7,5},{8,10},{9,11},{10,... | collective-permute-start | bytes 589832 | tf_op jit(solution)/shard_map/ppermute | solution.py:258
  40.8 0.5 collective-permute-start.21
  41.3 0.0 collective-permute-start.8
  41.3 2.7 %collective-permute-start.9 = (bf16[32,1024]{1,0:T(8,128)(2,1)S(1)}, bf16[32,1024]{1,0:T(8,128)(2,1)S(1)}, u32[]{:S(2)}, u32[]{:S(2)}) collective-permute-start(bf16[32,1024]{1,0:T(8,128)(2,1)S(1)} %get-tuple-element.68), channel_id=1, source_target_pairs={{0,8},{4,12},{8,0},{12,4},{1,9},{5,13},{9,1},{13,5},{2,10},{6,14},... | collective-permute-start | bytes 196616 | tf_op jit(solution)/shard_map/ppermute | solution.py:264
  44.0 1.7 %collective-permute-start.10 = (bf16[32,1024]{1,0:T(8,128)(2,1)S(1)}, bf16[32,1024]{1,0:T(8,128)(2,1)S(1)}, u32[]{:S(2)}, u32[]{:S(2)}) collective-permute-start(bf16[32,1024]{1,0:T(8,128)(2,1)S(1)} %get-tuple-element.69), channel_id=1, source_target_pairs={{0,12},{4,8},{8,4},{12,0},{1,13},{5,9},{9,5},{13,1},{2,14},{6,10},... | collective-permute-start | bytes 196616 | tf_op jit(solution)/shard_map/ppermute | solution.py:264
  45.7 1.5 %shard_map.105 = (bf16[32,1024]{1,0:T(8,128)(2,1)S(1)}, bf16[32,1024]{1,0:T(8,128)(2,1)S(1)}, bf16[32,1024]{1,0:T(8,128)(2,1)S(1)}, bf16[32,1024]{1,0:T(8,128)(2,1)S(1)}, f32[8,128]{1,0:T(8,128)}) custom-call(bf16[64,1536]{1,0:T(8,128)(2,1)S(1)} %get-tuple-element.82.refs_0_, bf16[64,1536]{1,0:T(8,128)(2,1)S(1)} %collective-permute-done.17.refs_1_, ...), custom_call_target="tpu_custom_call" | custom-call | flops 402653184 | bytes 3145728 | tf_op jit(solution)/shard_map/pallas_call | solution.py:37
  47.3 0.7 %collective-permute-start.18 = (bf16[32,1024]{1,0:T(8,128)(2,1)S(1)}, bf16[32,1024]{1,0:T(8,128)(2,1)S(1)}, u32[]{:S(2)}, u32[]{:S(2)}) collective-permute-start(bf16[32,1024]{1,0:T(8,128)(2,1)S(1)} %get-tuple-element.84), channel_id=1, source_target_pairs={{0,4},{4,0},{8,12},{12,8},{1,5},{5,1},{9,13},{13,9},{2,6},{6,2},{1... | collective-permute-start | bytes 196616 | tf_op jit(solution)/shard_map/ppermute | solution.py:264
  48.0 1.3 %collective-permute-done.9.refs_2_.refs_5_ = bf16[32,1024]{1,0:T(8,128)(2,1)S(1)} collective-permute-done((bf16[32,1024]{1,0:T(8,128)(2,1)S(1)}, bf16[32,1024]{1,0:T(8,128)(2,1)S(1)}, u32[]{:S(2)}, u32[]{:S(2)}) %collective-permute-start.9) | collective-permute-done | bytes 65568 | tf_op jit(solution)/shard_map/ppermute | solution.py:264
  49.3 1.1 %collective-permute-start.19 = (bf16[32,1024]{1,0:T(8,128)(2,1)S(1)}, bf16[32,1024]{1,0:T(8,128)(2,1)S(1)}, u32[]{:S(2)}, u32[]{:S(2)}) collective-permute-start(bf16[32,1024]{1,0:T(8,128)(2,1)S(1)} %get-tuple-element.85), channel_id=1, source_target_pairs={{0,8},{4,12},{8,0},{12,4},{1,9},{5,13},{9,1},{13,5},{2,10},{6,14},... | collective-permute-start | bytes 196616 | tf_op jit(solution)/shard_map/ppermute | solution.py:264
  50.4 1.5 %collective-permute-start.20 = (bf16[32,1024]{1,0:T(8,128)(2,1)S(1)}, bf16[32,1024]{1,0:T(8,128)(2,1)S(1)}, u32[]{:S(2)}, u32[]{:S(2)}) collective-permute-start(bf16[32,1024]{1,0:T(8,128)(2,1)S(1)} %get-tuple-element.86), channel_id=1, source_target_pairs={{0,12},{4,8},{8,4},{12,0},{1,13},{5,9},{9,5},{13,1},{2,14},{6,10},... | collective-permute-start | bytes 196616 | tf_op jit(solution)/shard_map/ppermute | solution.py:264
  51.9 0.6 shard_map.100
  52.5 1.7 %collective-permute-start.11 = (bf16[64,1024]{1,0:T(8,128)(2,1)S(1)}, bf16[64,1024]{1,0:T(8,128)(2,1)S(1)}, u32[]{:S(2)}, u32[]{:S(2)}) collective-permute-start(bf16[64,1024]{1,0:T(8,128)(2,1)S(1)} %get-tuple-element.70), channel_id=1, source_target_pairs={{0,2},{1,3},{2,0},{3,1},{4,6},{5,7},{6,4},{7,5},{8,10},{9,11},{10,... | collective-permute-start | bytes 393224 | tf_op jit(solution)/shard_map/ppermute | solution.py:258
  54.2 1.6 %shard_map.106 = (f32[512,768]{1,0:T(8,128)}, f32[8,128]{1,0:T(8,128)S(1)}) custom-call(bf16[128,512]{1,0:T(8,128)(2,1)S(1)} %get-tuple-element.87.refs_0_, bf16[128,512]{1,0:T(8,128)(2,1)S(1)} %collective-permute-done.21.refs_1_, bf16[64,768]{1,0:T(8,128)(2,1)S(1)} %get-tuple-element.64.refs_0_.refs_2_, ...), custom_call_target="tpu_custom_call" | custom-call | flops 201326592 | bytes 1572864 | tf_op jit(solution)/shard_map/pallas_call | solution.py:37
  55.7 1.1 %collective-permute-done.19.refs_2_.refs_4_ = bf16[32,1024]{1,0:T(8,128)(2,1)S(1)} collective-permute-done((bf16[32,1024]{1,0:T(8,128)(2,1)S(1)}, bf16[32,1024]{1,0:T(8,128)(2,1)S(1)}, u32[]{:S(2)}, u32[]{:S(2)}) %collective-permute-start.19) | collective-permute-done | bytes 65568 | tf_op jit(solution)/shard_map/ppermute | solution.py:264
  56.8 0.6 shard_map.107
  57.4 1.3 %collective-permute-start.24 = (bf16[64,1024]{1,0:T(8,128)(2,1)S(1)}, bf16[64,1024]{1,0:T(8,128)(2,1)S(1)}, u32[]{:S(2)}, u32[]{:S(2)}) collective-permute-start(bf16[64,1024]{1,0:T(8,128)(2,1)S(1)} %get-tuple-element.90), channel_id=1, source_target_pairs={{0,2},{1,3},{2,0},{3,1},{4,6},{5,7},{6,4},{7,5},{8,10},{9,11},{10,... | collective-permute-start | bytes 393224 | tf_op jit(solution)/shard_map/ppermute | solution.py:258
  58.7 2.0 %shard_map.101 = (bf16[256,2048]{1,0:T(8,128)(2,1)}, f32[8,128]{1,0:T(8,128)S(1)}) custom-call(s32[2]{0:T(128)S(1)} %pad_add_fusion.refs_0_, bf16[256,64]{1,0:T(8,128)(2,1)S(1)} %get-tuple-element.49.refs_1_, f32[64,128]{1,0:T(8,128)S(1)} %get-tuple-element.50.refs_2_, bf16[32,1024]{1,0:T(8,128)(2,1)S(1)} %get-tuple-element.66.refs_0_.refs_3_, ...), custom_call_target="tpu_custom_call" | custom-call | flops 134217728 | bytes 2097152 | tf_op jit(solution)/shard_map/pallas_call | solution.py:37
  60.7 2.1 %shard_map.108 = (bf16[256,2048]{1,0:T(8,128)(2,1)}, f32[8,128]{1,0:T(8,128)}) custom-call(s32[2]{0:T(128)S(1)} %pad_add_fusion.refs_0_, bf16[256,64]{1,0:T(8,128)(2,1)S(1)} %get-tuple-element.49.refs_1_, bf16[32,1024]{1,0:T(8,128)(2,1)S(1)} %get-tuple-element.83.refs_0_.refs_2_, bf16[32,1024]{1,0:T(8,128)(2,1)S(1)} %collective-permute-done.18.refs_1_.refs_3_, ...), custom_call_target="tpu_custom_call" | custom-call | flops 33554432 | bytes 524288 | tf_op jit(solution)/shard_map/pallas_call | solution.py:37
  62.9 2.2 %shard_map.109 = (bf16[256,2048]{1,0:T(8,128)(2,1)}, f32[8,128]{1,0:T(8,128)}) custom-call(s32[2]{0:T(128)S(1)} %pad_add_fusion.refs_0_, bf16[256,64]{1,0:T(8,128)(2,1)S(1)} %get-tuple-element.49.refs_1_, bf16[32,1024]{1,0:T(8,128)(2,1)S(1)} %get-tuple-element.83.refs_0_.refs_2_, ...), custom_call_target="tpu_custom_call", output_to_operand_aliasing={{0}: (7, {})} | custom-call | flops 33554432 | bytes 524288 | tf_op jit(solution)/shard_map/pallas_call | solution.py:37
  (23 shorter events, 0.1 us)
Async XLA Ops:
  0.6 2.9 %copy-start = (bf16[1,512,1536]{2,1,0:T(8,128)(2,1)S(1)}, bf16[1,512,1536]{2,1,0:T(8,128)(2,1)}, u32[]{:S(2)}) copy-start(bf16[1,512,1536]{2,1,0:T(8,128)(2,1)} %param.12) | copy-start | bytes 4718596
  3.5 18.3 %collective-permute-start.4 = (bf16[512,1536]{1,0:T(8,128)(2,1)S(1)}, bf16[512,1536]{1,0:T(8,128)(2,1)S(1)}, u32[]{:S(2)}, u32[]{:S(2)}) collective-permute-start(bf16[512,1536]{1,0:T(8,128)(2,1)S(1)} %bitcast.7), channel_id=1, source_target_pairs={{0,1},{1,0},{2,3},{3,2},{4,5},{5,4},{6,7},{7,6},{8,9},{9,8},{10,11... | collective-permute-start | bytes 4718600 | tf_op jit(solution)/shard_map/ppermute | solution.py:254
  4.0 28.9 %collective-permute-start.7 = (bf16[512,768]{1,0:T(8,128)(2,1)}, bf16[512,768]{1,0:T(8,128)(2,1)S(1)}, u32[]{:S(2)}, u32[]{:S(2)}) collective-permute-start(bf16[512,768]{1,0:T(8,128)(2,1)} %bitcast.10), channel_id=1, source_target_pairs={{0,1},{1,0},{2,3},{3,2},{4,5},{5,4},{6,7},{7,6},{8,9},{9,8},{10,11... | collective-permute-start | bytes 2359304 | tf_op jit(solution)/shard_map/ppermute | solution.py:254
  4.1 6.7 %collective-permute-start = (bf16[64,1024]{1,0:T(8,128)(2,1)S(1)}, bf16[64,1024]{1,0:T(8,128)(2,1)S(1)}, u32[]{:S(2)}, u32[]{:S(2)}) collective-permute-start(bf16[64,1024]{1,0:T(8,128)(2,1)S(1)} %get-tuple-element.53), channel_id=1, source_target_pairs={{0,2},{1,3},{2,0},{3,1},{4,6},{5,7},{6,4},{7,5},{8,10},{9,11},{10,... | collective-permute-start | bytes 393224 | tf_op jit(solution)/shard_map/ppermute | solution.py:258
  11.4 4.4 %collective-permute-start.1 = (bf16[32,1024]{1,0:T(8,128)(2,1)S(1)}, bf16[32,1024]{1,0:T(8,128)(2,1)S(1)}, u32[]{:S(2)}, u32[]{:S(2)}) collective-permute-start(bf16[32,1024]{1,0:T(8,128)(2,1)S(1)} %get-tuple-element.58), channel_id=1, source_target_pairs={{0,4},{4,0},{8,12},{12,8},{1,5},{5,1},{9,13},{13,9},{2,6},{6,2},{1... | collective-permute-start | bytes 196616 | tf_op jit(solution)/shard_map/ppermute | solution.py:264
  13.2 6.7 %collective-permute-start.2 = (bf16[32,1024]{1,0:T(8,128)(2,1)S(1)}, bf16[32,1024]{1,0:T(8,128)(2,1)S(1)}, u32[]{:S(2)}, u32[]{:S(2)}) collective-permute-start(bf16[32,1024]{1,0:T(8,128)(2,1)S(1)} %get-tuple-element.59), channel_id=1, source_target_pairs={{0,8},{4,12},{8,0},{12,4},{1,9},{5,13},{9,1},{13,5},{2,10},{6,14},... | collective-permute-start | bytes 196616 | tf_op jit(solution)/shard_map/ppermute | solution.py:264
  15.8 6.1 %collective-permute-start.3 = (bf16[32,1024]{1,0:T(8,128)(2,1)S(1)}, bf16[32,1024]{1,0:T(8,128)(2,1)S(1)}, u32[]{:S(2)}, u32[]{:S(2)}) collective-permute-start(bf16[32,1024]{1,0:T(8,128)(2,1)S(1)} %get-tuple-element.60), channel_id=1, source_target_pairs={{0,12},{4,8},{8,4},{12,0},{1,13},{5,9},{9,5},{13,1},{2,14},{6,10},... | collective-permute-start | bytes 196616 | tf_op jit(solution)/shard_map/ppermute | solution.py:264
  15.8 8.6 %collective-permute-start.12 = (bf16[64,1024]{1,0:T(8,128)(2,1)S(1)}, bf16[64,1024]{1,0:T(8,128)(2,1)S(1)}, u32[]{:S(2)}, u32[]{:S(2)}) collective-permute-start(bf16[64,1024]{1,0:T(8,128)(2,1)S(1)} %get-tuple-element.73), channel_id=1, source_target_pairs={{0,2},{1,3},{2,0},{3,1},{4,6},{5,7},{6,4},{7,5},{8,10},{9,11},{10,... | collective-permute-start | bytes 393224 | tf_op jit(solution)/shard_map/ppermute | solution.py:258
  21.9 11.1 %copy-start.1 = (bf16[1,512,768]{2,1,0:T(8,128)(2,1)S(1)}, bf16[1,512,768]{2,1,0:T(8,128)(2,1)}, u32[]{:S(2)}) copy-start(bf16[1,512,768]{2,1,0:T(8,128)(2,1)} %param.13) | copy-start | bytes 2359300
  22.9 6.5 %collective-permute-start.5 = (bf16[64,1536]{1,0:T(8,128)(2,1)S(1)}, bf16[64,1536]{1,0:T(8,128)(2,1)S(1)}, u32[]{:S(2)}, u32[]{:S(2)}) collective-permute-start(bf16[64,1536]{1,0:T(8,128)(2,1)S(1)} %get-tuple-element.63), channel_id=1, source_target_pairs={{0,2},{1,3},{2,0},{3,1},{4,6},{5,7},{6,4},{7,5},{8,10},{9,11},{10,... | collective-permute-start | bytes 589832 | tf_op jit(solution)/shard_map/ppermute | solution.py:258
  25.0 6.1 %collective-permute-start.13 = (bf16[32,1024]{1,0:T(8,128)(2,1)S(1)}, bf16[32,1024]{1,0:T(8,128)(2,1)S(1)}, u32[]{:S(2)}, u32[]{:S(2)}) collective-permute-start(bf16[32,1024]{1,0:T(8,128)(2,1)S(1)} %get-tuple-element.75), channel_id=1, source_target_pairs={{0,4},{4,0},{8,12},{12,8},{1,5},{5,1},{9,13},{13,9},{2,6},{6,2},{1... | collective-permute-start | bytes 196616 | tf_op jit(solution)/shard_map/ppermute | solution.py:264
  25.0 6.1 %collective-permute-start.14 = (bf16[32,1024]{1,0:T(8,128)(2,1)S(1)}, bf16[32,1024]{1,0:T(8,128)(2,1)S(1)}, u32[]{:S(2)}, u32[]{:S(2)}) collective-permute-start(bf16[32,1024]{1,0:T(8,128)(2,1)S(1)} %get-tuple-element.76), channel_id=1, source_target_pairs={{0,8},{4,12},{8,0},{12,4},{1,9},{5,13},{9,1},{13,5},{2,10},{6,14},... | collective-permute-start | bytes 196616 | tf_op jit(solution)/shard_map/ppermute | solution.py:264
  26.8 6.1 %collective-permute-start.15 = (bf16[32,1024]{1,0:T(8,128)(2,1)S(1)}, bf16[32,1024]{1,0:T(8,128)(2,1)S(1)}, u32[]{:S(2)}, u32[]{:S(2)}) collective-permute-start(bf16[32,1024]{1,0:T(8,128)(2,1)S(1)} %get-tuple-element.77), channel_id=1, source_target_pairs={{0,12},{4,8},{8,4},{12,0},{1,13},{5,9},{9,5},{13,1},{2,14},{6,10},... | collective-permute-start | bytes 196616 | tf_op jit(solution)/shard_map/ppermute | solution.py:264
  29.5 5.0 %collective-permute-start.6 = (bf16[64,768]{1,0:T(8,128)(2,1)S(1)}, bf16[64,768]{1,0:T(8,128)(2,1)S(1)}, u32[]{:S(2)}, u32[]{:S(2)}) collective-permute-start(bf16[64,768]{1,0:T(8,128)(2,1)S(1)} %get-tuple-element.64.refs_0_.refs_2_), channel_id=1, source_target_pairs={{0,2},{1,3},{2,0},{3,1},{4,6},{5,7},{6,4},{7,5},{8,10},{9,11},{10,... | collective-permute-start | bytes 294920 | tf_op jit(solution)/shard_map/ppermute | solution.py:258
  33.8 5.6 %collective-permute-start.16 = (bf16[64,768]{1,0:T(8,128)(2,1)S(1)}, bf16[64,768]{1,0:T(8,128)(2,1)S(1)}, u32[]{:S(2)}, u32[]{:S(2)}) collective-permute-start(bf16[64,768]{1,0:T(8,128)(2,1)S(1)} %get-tuple-element.80), channel_id=1, source_target_pairs={{0,2},{1,3},{2,0},{3,1},{4,6},{5,7},{6,4},{7,5},{8,10},{9,11},{10,... | collective-permute-start | bytes 294920 | tf_op jit(solution)/shard_map/ppermute | solution.py:258
  40.0 5.7 %collective-permute-start.17 = (bf16[64,1536]{1,0:T(8,128)(2,1)S(1)}, bf16[64,1536]{1,0:T(8,128)(2,1)S(1)}, u32[]{:S(2)}, u32[]{:S(2)}) collective-permute-start(bf16[64,1536]{1,0:T(8,128)(2,1)S(1)} %get-tuple-element.82.refs_0_), channel_id=1, source_target_pairs={{0,2},{1,3},{2,0},{3,1},{4,6},{5,7},{6,4},{7,5},{8,10},{9,11},{10,... | collective-permute-start | bytes 589832 | tf_op jit(solution)/shard_map/ppermute | solution.py:258
  40.8 3.2 %collective-permute-start.22 = (bf16[64,768]{1,0:T(8,128)(2,1)S(1)}, bf16[64,768]{1,0:T(8,128)(2,1)S(1)}, u32[]{:S(2)}, u32[]{:S(2)}) collective-permute-start(bf16[64,768]{1,0:T(8,128)(2,1)S(1)} %get-tuple-element.64.refs_0_.refs_2_), channel_id=1, source_target_pairs={{0,1},{1,0},{2,3},{3,2},{4,5},{5,4},{6,7},{7,6},{8,9},{9,8},{10,11... | collective-permute-start | bytes 294920 | tf_op jit(solution)/shard_map/ppermute | solution.py:254
  40.8 11.6 %collective-permute-start.21 = (bf16[128,512]{1,0:T(8,128)(2,1)S(1)}, bf16[128,512]{1,0:T(8,128)(2,1)S(1)}, u32[]{:S(2)}, u32[]{:S(2)}) collective-permute-start(bf16[128,512]{1,0:T(8,128)(2,1)S(1)} %get-tuple-element.88), channel_id=1, source_target_pairs={{0,1},{1,0},{2,3},{3,2},{4,5},{5,4},{6,7},{7,6},{8,9},{9,8},{10,11... | collective-permute-start | bytes 393224 | tf_op jit(solution)/shard_map/ppermute | solution.py:254
  41.3 5.9 %collective-permute-start.8 = (bf16[32,1024]{1,0:T(8,128)(2,1)S(1)}, bf16[32,1024]{1,0:T(8,128)(2,1)S(1)}, u32[]{:S(2)}, u32[]{:S(2)}) collective-permute-start(bf16[32,1024]{1,0:T(8,128)(2,1)S(1)} %get-tuple-element.67), channel_id=1, source_target_pairs={{0,4},{4,0},{8,12},{12,8},{1,5},{5,1},{9,13},{13,9},{2,6},{6,2},{1... | collective-permute-start | bytes 196616 | tf_op jit(solution)/shard_map/ppermute | solution.py:264
  41.3 7.9 %collective-permute-start.9 = (bf16[32,1024]{1,0:T(8,128)(2,1)S(1)}, bf16[32,1024]{1,0:T(8,128)(2,1)S(1)}, u32[]{:S(2)}, u32[]{:S(2)}) collective-permute-start(bf16[32,1024]{1,0:T(8,128)(2,1)S(1)} %get-tuple-element.68), channel_id=1, source_target_pairs={{0,8},{4,12},{8,0},{12,4},{1,9},{5,13},{9,1},{13,5},{2,10},{6,14},... | collective-permute-start | bytes 196616 | tf_op jit(solution)/shard_map/ppermute | solution.py:264
  44.0 6.4 %collective-permute-start.10 = (bf16[32,1024]{1,0:T(8,128)(2,1)S(1)}, bf16[32,1024]{1,0:T(8,128)(2,1)S(1)}, u32[]{:S(2)}, u32[]{:S(2)}) collective-permute-start(bf16[32,1024]{1,0:T(8,128)(2,1)S(1)} %get-tuple-element.69), channel_id=1, source_target_pairs={{0,12},{4,8},{8,4},{12,0},{1,13},{5,9},{9,5},{13,1},{2,14},{6,10},... | collective-permute-start | bytes 196616 | tf_op jit(solution)/shard_map/ppermute | solution.py:264
  45.7 8.4 %collective-permute-start.23 = (bf16[64,768]{1,0:T(8,128)(2,1)S(1)}, bf16[64,768]{1,0:T(8,128)(2,1)S(1)}, u32[]{:S(2)}, u32[]{:S(2)}) collective-permute-start(bf16[64,768]{1,0:T(8,128)(2,1)S(1)} %collective-permute-done.6.refs_1_.refs_3_), channel_id=1, source_target_pairs={{0,1},{1,0},{2,3},{3,2},{4,5},{5,4},{6,7},{7,6},{8,9},{9,8},{10,11... | collective-permute-start | bytes 294920 | tf_op jit(solution)/shard_map/ppermute | solution.py:254
  47.3 8.5 %collective-permute-start.18 = (bf16[32,1024]{1,0:T(8,128)(2,1)S(1)}, bf16[32,1024]{1,0:T(8,128)(2,1)S(1)}, u32[]{:S(2)}, u32[]{:S(2)}) collective-permute-start(bf16[32,1024]{1,0:T(8,128)(2,1)S(1)} %get-tuple-element.84), channel_id=1, source_target_pairs={{0,4},{4,0},{8,12},{12,8},{1,5},{5,1},{9,13},{13,9},{2,6},{6,2},{1... | collective-permute-start | bytes 196616 | tf_op jit(solution)/shard_map/ppermute | solution.py:264
  49.3 7.5 %collective-permute-start.19 = (bf16[32,1024]{1,0:T(8,128)(2,1)S(1)}, bf16[32,1024]{1,0:T(8,128)(2,1)S(1)}, u32[]{:S(2)}, u32[]{:S(2)}) collective-permute-start(bf16[32,1024]{1,0:T(8,128)(2,1)S(1)} %get-tuple-element.85), channel_id=1, source_target_pairs={{0,8},{4,12},{8,0},{12,4},{1,9},{5,13},{9,1},{13,5},{2,10},{6,14},... | collective-permute-start | bytes 196616 | tf_op jit(solution)/shard_map/ppermute | solution.py:264
  50.4 6.4 %collective-permute-start.20 = (bf16[32,1024]{1,0:T(8,128)(2,1)S(1)}, bf16[32,1024]{1,0:T(8,128)(2,1)S(1)}, u32[]{:S(2)}, u32[]{:S(2)}) collective-permute-start(bf16[32,1024]{1,0:T(8,128)(2,1)S(1)} %get-tuple-element.86), channel_id=1, source_target_pairs={{0,12},{4,8},{8,4},{12,0},{1,13},{5,9},{9,5},{13,1},{2,14},{6,10},... | collective-permute-start | bytes 196616 | tf_op jit(solution)/shard_map/ppermute | solution.py:264
  52.5 6.2 %collective-permute-start.11 = (bf16[64,1024]{1,0:T(8,128)(2,1)S(1)}, bf16[64,1024]{1,0:T(8,128)(2,1)S(1)}, u32[]{:S(2)}, u32[]{:S(2)}) collective-permute-start(bf16[64,1024]{1,0:T(8,128)(2,1)S(1)} %get-tuple-element.70), channel_id=1, source_target_pairs={{0,2},{1,3},{2,0},{3,1},{4,6},{5,7},{6,4},{7,5},{8,10},{9,11},{10,... | collective-permute-start | bytes 393224 | tf_op jit(solution)/shard_map/ppermute | solution.py:258
  57.4 5.5 %collective-permute-start.24 = (bf16[64,1024]{1,0:T(8,128)(2,1)S(1)}, bf16[64,1024]{1,0:T(8,128)(2,1)S(1)}, u32[]{:S(2)}, u32[]{:S(2)}) collective-permute-start(bf16[64,1024]{1,0:T(8,128)(2,1)S(1)} %get-tuple-element.90), channel_id=1, source_target_pairs={{0,2},{1,3},{2,0},{3,1},{4,6},{5,7},{6,4},{7,5},{8,10},{9,11},{10,... | collective-permute-start | bytes 393224 | tf_op jit(solution)/shard_map/ppermute | solution.py:258

commit v4 on v3

v4 whole, which is shorter than its diff:
```python
import jax
import jax.numpy as jnp
from jax import lax
from jax.experimental import pallas as pl
from jax.experimental.pallas import tpu as pltpu
from jax.sharding import PartitionSpec as P

EXPERTS = 128
CORES = 2
VMEM = 40 * 1024 * 1024
F32 = jnp.float32
BF16 = jnp.bfloat16


def product(left, right, left_dim, right_dim, **kw):
    return lax.dot_general(
        left, right, (((left_dim,), (right_dim,)), ((), ())), preferred_element_type=F32, **kw
    )


def call(body, out_shape, args, flops=0, nbytes=0, far=0, after=(), token=False, **kw):
    out_shape = [*out_shape] + [shape((8, 128), F32)] * token
    specs = [pl.BlockSpec(memory_space=pltpu.VMEM)] * (len(args) - far)
    specs += [pl.BlockSpec(memory_space=pltpu.HBM)] * far
    specs += [pl.BlockSpec(memory_space=pl.ANY)] * len(after)
    kw.setdefault("out_specs", [pl.BlockSpec(memory_space=pltpu.VMEM)] * len(out_shape))
    args = [
        pltpu.with_memory_space_constraint(arg, pltpu.HBM) if i >= len(args) - far else arg
        for i, arg in enumerate(args)
    ]
    count, first, last = len(args), len(args) + len(after), len(args) + len(after) + len(out_shape)

    def kernel(*refs):
        if token:
            refs[last - 1][...] = jnp.zeros(refs[last - 1].shape, F32)
        body(*refs[:count], *refs[first : last - token], *refs[last:])

    return pl.pallas_call(
        kernel,
        out_shape=out_shape,
        in_specs=specs,
        compiler_params=pltpu.CompilerParams(vmem_limit_bytes=VMEM),
        cost_estimate=pl.CostEstimate(flops=0, bytes_accessed=0, transcendentals=0),
        **kw,
    )(*args, *after)


def shape(dims, kind=BF16):
    return jax.ShapeDtypeStruct(dims, kind)


def columns(k, part):
    return pl.ds(pl.multiple_of((lax.axis_index("fsdp") ^ k) * part, part), part)


def piece_columns(n, width, replicas):
    return pl.ds(pl.multiple_of((lax.axis_index("replica") ^ n) * width, width), width)


def rows_kernel(groups, parts, capacity, replicas, *refs):
    sources, chunks, refs = refs[:6], refs[6 : 6 + groups], refs[6 + groups :]
    pick_out, turned_out, gate_out, cot, piece, ids, gates, order, tok, sems = refs
    sources = (*sources[:5], sources[5].at[:, piece_columns(0, piece.shape[1], replicas)])
    copies = [
        pltpu.make_async_copy(source, target, sems.at[i])
        for i, (source, target) in enumerate(zip(sources, (ids, gates, order, tok, cot, piece)))
    ]
    for copy in copies:
        copy.start()
    for copy in copies[:3]:
        copy.wait()
    choices, count = ids.shape
    slots = groups * capacity
    part = tok.shape[1] // parts
    slot = lax.broadcasted_iota(jnp.int32, (slots, count), 0)
    wanted = ((slot // capacity) ^ lax.axis_index("expert")) * (EXPERTS // groups)
    routed = jnp.zeros((slots, count), F32)
    gate = jnp.zeros((slots, count), F32)
    for k in range(choices):
        hit = ids[k : k + 1, :] == wanted
        routed = jnp.where(hit, 1.0, routed)
        gate = jnp.where(hit, gates[k : k + 1, :], gate)
    row = lax.broadcasted_iota(jnp.int32, (count, count), 0)
    col = lax.broadcasted_iota(jnp.int32, (count, count), 1)
    served = jnp.where(order[...] == row, 1.0, 0.0).astype(BF16)
    earlier = jnp.where(row < col, 1.0, 0.0).astype(BF16)
    by_rank = product(routed.astype(BF16), served, 1, 0)
    before = product(by_rank.astype(BF16), earlier, 1, 0)
    taken = jnp.where(before.astype(jnp.int32) == slot % capacity, by_rank, 0.0).astype(BF16)
    pick = product(taken, served, 1, 1)
    turned_out[...] = product(served, taken, 1, 1).astype(BF16)
    slot_gate = jnp.sum(pick * gate, axis=1, keepdims=True)
    gate_out[...] = jnp.broadcast_to(slot_gate, gate_out.shape)
    pick = pick.astype(BF16)
    pick_out[...] = pick
    copies[3].wait()
    for k in range(parts):
        rows = product(pick, tok[:, columns(k, part)], 1, 0).astype(BF16)
        for ke in range(groups):
            chunks[ke][:, k * part : (k + 1) * part] = rows[ke * capacity : (ke + 1) * capacity]
    copies[4].wait()
    copies[5].wait()


def grads_kernel(groups, parts, capacity, pick, gate, cot, *chunks):
    part = cot.shape[1] // parts
    for k in range(parts):
        value = product(pick[...], cot[:, columns(k, part)], 1, 0)
        value = (gate[:, :1] * value).astype(BF16)
        for ke in range(groups):
            chunks[ke][:, k * part : (k + 1) * part] = value[ke * capacity : (ke + 1) * capacity]


def split_kernel(groups, spread, capacity, *refs):
    chunks, by_x = refs[:groups], refs[groups:]
    half = by_x[0].shape[1]
    for kx in range(spread):
        for ke in range(groups):
            by_x[kx][ke * capacity : (ke + 1) * capacity] = chunks[ke][
                :, kx * half : (kx + 1) * half
            ]


def far_kernel(groups, spread, capacity, *refs):
    by_e, by_x = refs[:groups], refs[groups:]
    for ke in range(groups):
        for kx in range(1, spread):
            by_x[kx - 1][ke * capacity : (ke + 1) * capacity] = by_e[ke][
                kx * capacity : (kx + 1) * capacity
            ]


def pre_kernel(spread, *refs):
    left, (own, sib, *outs) = refs[:spread], refs[spread:]
    part = own.shape[0]
    rows = jnp.concatenate([r[...] for r in left], axis=0)
    total = product(rows[:, :part], own[...], 1, 0) + product(rows[:, part:], sib[...], 1, 0)
    count = left[0].shape[0]
    for kx in range(spread):
        outs[kx][...] = total[kx * count : (kx + 1) * count].astype(outs[kx].dtype)


def back_kernel(groups, replicas, *refs):
    chunks, weights, (grads, back) = refs[:groups], refs[groups:-2], refs[-2:]
    part, feed = weights[0].shape
    grads[...] = jnp.concatenate([c[...] for c in chunks], axis=0)
    total = product(grads[:, :part], weights[0][...], 1, 0)
    back[...] = total + product(grads[:, part : 2 * part], weights[1][...], 1, 0)
    add_pieces(grads, weights[CORES:], back, 0, replicas)


def add_pieces(grads, pieces, back, n, replicas):
    part, width = pieces[0].shape
    total = 0.0
    for k, piece in enumerate(pieces, CORES):
        total += product(grads[:, k * part : (k + 1) * part], piece[...], 1, 0)
    back[:, piece_columns(n, width, replicas)] += total


def act_kernel(spread, replicas, *refs):
    pre_refs, grads, back_in, pieces = refs[:spread], refs[spread], refs[spread + 1], refs[spread + 2 : -3]
    hidden, d_pre, back = refs[-3:]
    back[...] = back_in[...]
    for n in range(1, replicas):
        add_pieces(grads, pieces[n - 1 :: replicas - 1], back, n, replicas)
    pre = pre_refs[0][...]
    for ref in pre_refs[1:]:
        pre += ref[...].astype(F32)
    feed = back.shape[1]
    gate_act, up_act = pre[:, :feed], pre[:, feed:]
    sig = 1.0 / (1.0 + jnp.exp(-gate_act))
    silu = gate_act * sig
    hidden[...] = (silu * up_act).astype(BF16)
    d_pre[:, :feed] = (back[...] * up_act * (sig * (1.0 + gate_act * (1.0 - sig)))).astype(BF16)
    d_pre[:, feed:] = (back[...] * silu).astype(BF16)


def expert_out_kernel(groups, capacity, replicas, hidden, *refs):
    weights, chunks = refs[:-groups], refs[-groups:]
    part, feed = weights[0].shape
    width = feed // replicas

    def store(k, value):
        value = value.astype(BF16)
        for ke in range(groups):
            chunks[ke][:, k * part : (k + 1) * part] = value[ke * capacity : (ke + 1) * capacity]

    for k in range(CORES):
        store(k, product(hidden[...], weights[k][...], 1, 1))
    for k in range(CORES, chunks[0].shape[1] // part):
        pieces = weights[CORES + (k - CORES) * replicas :][:replicas]
        total = product(hidden[:, piece_columns(0, width, replicas)], pieces[0][...], 1, 1)
        for n in range(1, replicas):
            total += product(hidden[:, piece_columns(n, width, replicas)], pieces[n][...], 1, 1)
        store(k, total)


def d_rows_kernel(groups, spread, capacity, *refs):
    left, (own, sib, *chunks) = refs[:spread], refs[spread:]
    part = own.shape[0]
    rows = jnp.concatenate([r[...] for r in left], axis=0)
    for kc, weight in enumerate((own, sib)):
        value = product(rows, weight[...], 1, 1).astype(BF16)
        for ke in range(groups):
            for kx in range(spread):
                at = (kx * groups + ke) * capacity
                chunks[ke][kx * capacity : (kx + 1) * capacity, kc * part : (kc + 1) * part] = value[
                    at : at + capacity
                ]


def pack_kernel(spread, grads, hidden, *outs):
    half = grads.shape[1] // spread
    for kx in range(1, spread):
        outs[kx - 1][:, :half] = grads[:, kx * half : (kx + 1) * half]
        outs[kx - 1][:, half:] = hidden[...]


def gather_kernel(spread, grads, hidden, *refs):
    far, (own, sib, all_hidden) = refs[: spread - 1], refs[spread - 1 :]
    part = own.shape[1]
    count = grads.shape[0]
    for kx in range(spread):
        source = far[kx - 1] if kx else grads
        at = pl.ds(kx * count, count)
        own[at] = source[:, :part]
        sib[at] = source[:, part : 2 * part]
        all_hidden[at] = source[:, 2 * part :] if kx else hidden[...]


def weight_kernel(own, hidden, sib, sib_hidden, out):
    left = jnp.concatenate([own[...], sib[...]], axis=0)
    right = jnp.concatenate([hidden[...], sib_hidden[...]], axis=0)
    out[...] = product(left, right, 0, 0)


def combine_kernel(groups, parts, turned, gate, *refs):
    chunks, (out, held, sems) = refs[:groups], refs[groups:]
    part = out.shape[1] // parts
    twice = jnp.concatenate([turned[...], turned[...]], axis=1)
    copies = []
    for k in range(parts):
        rows = jnp.concatenate([c[:, k * part : (k + 1) * part] for c in chunks], axis=0)
        weighted = rows.astype(F32) * gate[:, :1]
        high = weighted.astype(BF16)
        low = (weighted - high.astype(F32)).astype(BF16)
        both = jnp.concatenate([high, low], axis=0)
        held[k] = product(twice, both, 1, 0).astype(BF16)
        copies.append(pltpu.make_async_copy(held.at[k], out.at[:, columns(k, part)], sems.at[k]))
        copies[-1].start()
    for copy in copies:
        copy.wait()


def d_tokens_kernel(groups, parts, capacity, span, turned, *refs):
    *refs, out, held, sems = refs
    part = out.shape[1] // parts
    copies = []
    for n, kx in enumerate(span):
        for kc in range(CORES):
            cols = slice(kc * part, (kc + 1) * part)
            if kx:
                rows = refs[n][:, cols]
            else:
                rows = jnp.concatenate([refs[ke][:capacity, cols] for ke in range(groups)], axis=0)
            i = len(copies)
            held[i] = product(turned[...], rows, 1, 0).astype(BF16)
            target = out.at[:, columns(kx * CORES + kc, part)]
            copies.append(pltpu.make_async_copy(held.at[i], target, sems.at[i]))
            copies[-1].start()
    for copy in copies:
        copy.wait()


def per_device(tokens, cotangent, route_ids, route_gates, served_order, w_in, w_out):
    replicas = lax.axis_size("replica")
    groups = lax.axis_size("expert")
    parts = lax.axis_size("fsdp")
    spread = parts // CORES
    count, width = tokens.shape
    capacity = count * route_ids.shape[1] // EXPERTS
    feed = w_out.shape[2]
    slots = groups * capacity
    half = width // spread
    part = width // parts

    def bound(kernel, *sizes):
        return lambda *refs: kernel(*sizes, *refs)

    def to_core(value):
        return lax.ppermute(value, "fsdp", [(i, i ^ 1) for i in range(parts)])

    def to_x(values):
        return [
            lax.ppermute(value, "fsdp", [(i, i ^ ((k + 1) * CORES)) for i in range(parts)])
            for k, value in enumerate(values)
        ]

    def to_replica(value, n):
        return lax.ppermute(value, "replica", [(i, i ^ n) for i in range(replicas)])

    def to_expert(chunks):
        return [
            lax.ppermute(value, "expert", [(i, i ^ ke) for i in range(groups)]) if ke else value
            for ke, value in enumerate(chunks)
        ]

    chunk = [shape((capacity, width))] * groups
    in_own, out_own = w_in[0], w_out[0]
    *rows, pick, turned, gate, cotangent, piece = call(
        bound(rows_kernel, groups, parts, capacity, replicas),
        chunk
        + [shape((slots, count)), shape((count, slots)), shape((slots, 128), F32)]
        + [shape(cotangent.shape), shape((part, feed // replicas))],
        (route_ids.T, route_gates.T, served_order, tokens, cotangent, out_own),
        flops=2 * slots * count * width,
        nbytes=4 * count * width,
        far=6,
        scratch_shapes=[
            pltpu.VMEM(route_ids.shape[::-1], jnp.int32),
            pltpu.VMEM(route_gates.shape[::-1], F32),
            pltpu.VMEM(served_order.shape, jnp.int32),
            pltpu.VMEM(tokens.shape, BF16),
            pltpu.SemaphoreType.DMA((6,)),
        ],
    )
    rows = to_expert(rows)
    grads = call(
        bound(grads_kernel, groups, parts, capacity),
        chunk,
        (pick, gate, cotangent),
        flops=2 * slots * count * width,
        nbytes=4 * count * width,
    )
    grads = list(grads)
    pieces = to_x([piece] * (spread - 1))
    near, *far = call(
        bound(split_kernel, groups, spread, capacity),
        [shape((slots, half))] * spread,
        rows,
        nbytes=4 * slots * width,
        after=pieces,
    )
    in_own, out_own, near, pieces = lax.optimization_barrier((in_own, out_own, near, pieces))
    in_sib, out_sib = to_core(in_own), to_core(out_own)
    pieces = [[value] + [to_replica(value, n) for n in range(1, replicas)] for value in pieces]
    pre, *pre_far = call(
        bound(pre_kernel, spread),
        [shape((slots, 2 * feed), F32)] + [shape((slots, 2 * feed))] * (spread - 1),
        (near, *to_x(far), in_own, in_sib),
        flops=4 * spread * slots * half * feed,
        nbytes=4 * half * feed,
    )
    *grads, pre = lax.optimization_barrier((*grads, pre))
    grads = to_expert(grads)
    first = [value for values in pieces for value in (values[0], to_core(values[0]))]
    grads, back = call(
        bound(back_kernel, groups, replicas),
        [shape((slots, width)), shape((slots, feed), F32)],
        (*grads, out_own, out_sib, *first),
    )
    pre_far = to_x(pre_far)
    rest = [values[1:] for values in pieces]
    rest, *_ = lax.optimization_barrier((rest, pre_far, back))
    rest = [(values, [to_core(value) for value in values]) for values in rest]
    w_outs = [out_own, out_sib]
    for i, pair in enumerate(rest):
        for core in range(CORES):
            w_outs += [first[i * CORES + core], *pair[core]]
    hidden, d_pre = call(
        bound(act_kernel, spread, replicas),
        [shape((slots, feed)), shape((slots, 2 * feed))],
        (pre, *pre_far, grads, back, *[value for pair in rest for values in pair for value in values]),
        scratch_shapes=[pltpu.VMEM((slots, feed), F32)],
    )
    d_pre = [d_pre, *to_x([d_pre] * (spread - 1))]
    expert_out = call(
        bound(expert_out_kernel, groups, capacity, replicas),
        chunk,
        (hidden, *w_outs),
        flops=2 * slots * width * feed,
        nbytes=2 * width * feed,
    )
    expert_out = to_expert(expert_out)
    d_rows = call(
        bound(d_rows_kernel, groups, spread, capacity),
        [shape((spread * capacity, half))] * groups,
        (*d_pre, in_own, in_sib),
        flops=4 * spread * slots * half * feed,
        nbytes=4 * half * feed,
        after=expert_out[1:],
    )
    d_rows = to_expert(d_rows)
    packed = call(
        bound(pack_kernel, spread),
        [shape((slots, half + feed))] * (spread - 1),
        (grads, hidden),
        after=(d_rows[0],),
    )
    own, sib, all_hidden = call(
        bound(gather_kernel, spread),
        [shape((spread * slots, part))] * 2 + [shape((spread * slots, feed))],
        (grads, hidden, *to_x(packed)),
    )
    (d_w_out,) = call(
        weight_kernel,
        [shape((part, feed), F32)],
        (own, all_hidden, to_core(sib), to_core(all_hidden)),
        flops=4 * spread * slots * part * feed,
        nbytes=4 * part * feed,
    )
    combined, combined_token = call(
        bound(combine_kernel, groups, parts),
        [shape((count, width))],
        (turned, gate, *expert_out),
        flops=4 * slots * count * width,
        nbytes=4 * count * width,
        token=True,
        out_specs=[pl.BlockSpec(memory_space=pltpu.HBM), pl.BlockSpec(memory_space=pltpu.VMEM)],
        scratch_shapes=[
            pltpu.VMEM((parts, count, part), BF16),
            pltpu.SemaphoreType.DMA((parts,)),
        ],
    )

    def d_tokens_columns(span, *operands, **kw):
        pieces = len(span) * CORES
        return call(
            bound(d_tokens_kernel, groups, parts, capacity, span),
            [shape((count, width))],
            (turned, *operands),
            flops=2 * slots * half * count,
            nbytes=2 * count * half,
            out_specs=[pl.BlockSpec(memory_space=pltpu.HBM)],
            scratch_shapes=[
                pltpu.VMEM((pieces, count, part), BF16),
                pltpu.SemaphoreType.DMA((pieces,)),
            ],
            **kw,
        )[0]

    far = call(
        bound(far_kernel, groups, spread, capacity),
        [shape((slots, half))] * (spread - 1),
        d_rows,
        nbytes=4 * slots * width,
    )
    far = to_x(far)
    d_tokens = d_tokens_columns([0], *d_rows, after=(combined_token,))
    d_tokens = d_tokens_columns(
        range(1, spread), *far, d_tokens, far=1, input_output_aliases={1 + len(far): 0}
    )
    return combined, d_tokens, d_w_out[None]


def solution(mesh):
    rows = P(("replica", "expert", "fsdp"), None)
    weights = P("expert", "fsdp", None)
    return jax.shard_map(
        per_device,
        mesh=mesh,
        in_specs=(rows,) * 5 + (weights,) * 2,
        out_specs=(rows, rows, P(("replica", "expert"), "fsdp", None)),
        check_vma=False,
    )
```

time: 65.2 us -> 67.6 us (1.037)
  waiting for transfers between devices: 15.1 us -> 28.8 us
  Pallas kernels: 18.7 us -> 10.8 us
  starting transfers between devices: 30.3 us -> 27 us
    ppermute x12, waiting for transfers between devices: 8.04 us -> 19.8 us  [to_expert(): lax.ppermute(value, 'expert', [(i, i ^ ke) for i in range(groups)])]
    pallas_call x16 -> x15, Pallas kernels: 18.7 us -> 10.8 us  [call(): pl.pallas_call(kernel, out_shape=out_shape, in_specs=specs, compiler_para...]
    ppermute x8 -> x6, starting transfers between devices: 12.7 us -> 7.06 us  [to_x(): lax.ppermute(value, 'fsdp', [(i, i ^ (k + 1) * CORES) for i in range(part...]
    ppermute x5 -> x6, waiting for transfers between devices: 0.01 us -> 1.72 us  [to_core(): return lax.ppermute(value, 'fsdp', [(i, i ^ 1) for i in range(parts)])]
    ppermute x0 -> x1, starting transfers between devices: none -> 1.52 us  [to_replica(): return lax.ppermute(value, 'replica', [(i, i ^ n) for i in range(replicas)])]
    ppermute x12, starting transfers between devices: 16.5 us -> 17.7 us  [to_expert(): lax.ppermute(value, 'expert', [(i, i ^ ke) for i in range(groups)])]
    ppermute x8 -> x6, waiting for transfers between devices: 7.07 us -> 7.2 us  [to_x(): lax.ppermute(value, 'fsdp', [(i, i ^ (k + 1) * CORES) for i in range(part...]
  transfers between devices with their start and end apart: 25 -> 25, of which waited for: 7 -> 14; matrix products, arithmetic and copies ran while one was open for 0% -> 0% of each run, Pallas kernels for 20% -> 9%
where the time goes in v4:
time: 67.6 us; the launch traced here: 67.5 us
  waiting for transfers between devices  28.8 us (43%)
  starting transfers between devices  27 us (40%)
  Pallas kernels  10.8 us (16%)
  between operations  0.84 us (1%)
    ppermute x12, waiting for transfers between devices, to_expert(): lax.ppermute(value, 'expert', [(i, i ^ ke) for i in range(groups)])  19.8 us
    ppermute x12, starting transfers between devices, to_expert(): lax.ppermute(value, 'expert', [(i, i ^ ke) for i in range(groups)])  17.7 us
    pallas_call x15, Pallas kernels, call(): pl.pallas_call(kernel, out_shape=out_shape, in_specs=specs, compiler_para...  10.8 us
    ppermute x6, waiting for transfers between devices, to_x(): lax.ppermute(value, 'fsdp', [(i, i ^ (k + 1) * CORES) for i in range(part...  7.2 us
    ppermute x6, starting transfers between devices, to_x(): lax.ppermute(value, 'fsdp', [(i, i ^ (k + 1) * CORES) for i in range(part...  7.06 us
    ppermute x6, waiting for transfers between devices, to_core(): return lax.ppermute(value, 'fsdp', [(i, i ^ 1) for i in range(parts)])  1.72 us
    ppermute x1, starting transfers between devices, to_replica(): return lax.ppermute(value, 'replica', [(i, i ^ n) for i in range(replicas)])  1.52 us
  transfers between devices with their start and end apart: 25, of which 14 were waited for; matrix products, arithmetic and copies ran while one was open for 0% of the time, Pallas kernels for 9%

profile of v4, /device:TPU:0, one launch (start us, length us, event | category | flops | bytes accessed | tf_op | source)
XLA Modules:
  0.0 67.5 jit_solution(3852543634988549481)
XLA Ops:
  0.7 1.9 %shard_map.94 = (bf16[16,2048]{1,0:T(8,128)(2,1)S(1)}, bf16[16,2048]{1,0:T(8,128)(2,1)S(1)}, bf16[16,2048]{1,0:T(8,128)(2,1)S(1)}, bf16[16,2048]{1,0:T(8,128)(2,...) custom-call(s32[8,256]{1,0:T(8,128)} %bitcast.13, ...), custom_call_target="tpu_custom_call" | custom-call | tf_op jit(solution)/shard_map/pallas_call | solution.py:38
  2.5 3.0 %collective-permute-start.3 = (bf16[512,384]{1,0:T(8,128)(2,1)S(1)}, bf16[512,384]{1,0:T(8,128)(2,1)S(1)}, u32[]{:S(2)}, u32[]{:S(2)}) collective-permute-start(bf16[512,384]{1,0:T(8,128)(2,1)S(1)} %get-tuple-element.59), channel_id=1, source_target_pairs={{0,2},{1,3},{2,0},{3,1},{4,6},{5,7},{6,4},{7,5},{8,10},{9,11},{10,... | collective-permute-start | bytes 1179656 | tf_op jit(solution)/shard_map/ppermute | solution.py:295
  5.5 1.6 %collective-permute-start = (bf16[16,2048]{1,0:T(8,128)(2,1)S(1)}, bf16[16,2048]{1,0:T(8,128)(2,1)S(1)}, u32[]{:S(2)}, u32[]{:S(2)}) collective-permute-start(bf16[16,2048]{1,0:T(8,128)(2,1)S(1)} %get-tuple-element.56), channel_id=1, source_target_pairs={{0,4},{4,0},{8,12},{12,8},{1,5},{5,1},{9,13},{13,9},{2,6},{6,2},{1... | collective-permute-start | bytes 196616 | tf_op jit(solution)/shard_map/ppermute | solution.py:304
  7.1 2.6 %collective-permute-start.1 = (bf16[16,2048]{1,0:T(8,128)(2,1)S(1)}, bf16[16,2048]{1,0:T(8,128)(2,1)S(1)}, u32[]{:S(2)}, u32[]{:S(2)}) collective-permute-start(bf16[16,2048]{1,0:T(8,128)(2,1)S(1)} %get-tuple-element.57), channel_id=1, source_target_pairs={{0,8},{4,12},{8,0},{12,4},{1,9},{5,13},{9,1},{13,5},{2,10},{6,14},... | collective-permute-start | bytes 196616 | tf_op jit(solution)/shard_map/ppermute | solution.py:304
  9.7 0.2 collective-permute-start.2
  9.9 4.2 %collective-permute-done.1.refs_2_ = bf16[16,2048]{1,0:T(8,128)(2,1)S(1)} collective-permute-done((bf16[16,2048]{1,0:T(8,128)(2,1)S(1)}, bf16[16,2048]{1,0:T(8,128)(2,1)S(1)}, u32[]{:S(2)}, u32[]{:S(2)}) %collective-permute-start.1) | collective-permute-done | bytes 65568 | tf_op jit(solution)/shard_map/ppermute | solution.py:304
  14.1 1.7 %collective-permute-done.2.refs_3_ = bf16[16,2048]{1,0:T(8,128)(2,1)S(1)} collective-permute-done((bf16[16,2048]{1,0:T(8,128)(2,1)S(1)}, bf16[16,2048]{1,0:T(8,128)(2,1)S(1)}, u32[]{:S(2)}, u32[]{:S(2)}) %collective-permute-start.2) | collective-permute-done | bytes 65568 | tf_op jit(solution)/shard_map/ppermute | solution.py:304
  15.8 0.1 collective-permute-start.5
  15.9 0.5 collective-permute-start.10
  16.4 0.1 collective-permute-start.11
  16.5 1.5 %collective-permute-start.12 = (bf16[512,384]{1,0:T(8,128)(2,1)S(1)}, bf16[512,384]{1,0:T(8,128)(2,1)S(1)}, u32[]{:S(2)}, u32[]{:S(2)}) collective-permute-start(bf16[512,384]{1,0:T(8,128)(2,1)S(1)} %collective-permute-done.3.refs_4_.refs_6_.refs_3_), channel_id=1, source_target_pairs={{0,16},{16,0},{1,17},{17,1},{2,18},{18,2},{3,19},{19,3},{4,20},{20... | collective-permute-start | bytes 1179656 | tf_op jit(solution)/shard_map/ppermute | solution.py:300
  18.0 0.6 collective-permute-start.4
  18.6 4.9 %collective-permute-done.4.refs_1_ = bf16[64,1024]{1,0:T(8,128)(2,1)S(1)} collective-permute-done((bf16[64,1024]{1,0:T(8,128)(2,1)S(1)}, bf16[64,1024]{1,0:T(8,128)(2,1)S(1)}, u32[]{:S(2)}, u32[]{:S(2)}) %collective-permute-start.4) | collective-permute-done | bytes 131104 | tf_op jit(solution)/shard_map/ppermute | solution.py:295
  23.6 0.6 shard_map.97
  24.2 0.7 %collective-permute-start.6 = (bf16[64,1536]{1,0:T(8,128)(2,1)S(1)}, bf16[64,1536]{1,0:T(8,128)(2,1)S(1)}, u32[]{:S(2)}, u32[]{:S(2)}) collective-permute-start(bf16[64,1536]{1,0:T(8,128)(2,1)S(1)} %get-tuple-element.66), channel_id=1, source_target_pairs={{0,2},{1,3},{2,0},{3,1},{4,6},{5,7},{6,4},{7,5},{8,10},{9,11},{10,... | collective-permute-start | bytes 589832 | tf_op jit(solution)/shard_map/ppermute | solution.py:295
  24.8 0.3 shard_map.95
  25.1 1.6 %collective-permute-start.7 = (bf16[16,2048]{1,0:T(8,128)(2,1)S(1)}, bf16[16,2048]{1,0:T(8,128)(2,1)S(1)}, u32[]{:S(2)}, u32[]{:S(2)}) collective-permute-start(bf16[16,2048]{1,0:T(8,128)(2,1)S(1)} %get-tuple-element.68), channel_id=1, source_target_pairs={{0,4},{4,0},{8,12},{12,8},{1,5},{5,1},{9,13},{13,9},{2,6},{6,2},{1... | collective-permute-start | bytes 196616 | tf_op jit(solution)/shard_map/ppermute | solution.py:304
  26.8 2.6 %collective-permute-start.8 = (bf16[16,2048]{1,0:T(8,128)(2,1)S(1)}, bf16[16,2048]{1,0:T(8,128)(2,1)S(1)}, u32[]{:S(2)}, u32[]{:S(2)}) collective-permute-start(bf16[16,2048]{1,0:T(8,128)(2,1)S(1)} %get-tuple-element.69), channel_id=1, source_target_pairs={{0,8},{4,12},{8,0},{12,4},{1,9},{5,13},{9,1},{13,5},{2,10},{6,14},... | collective-permute-start | bytes 196616 | tf_op jit(solution)/shard_map/ppermute | solution.py:304
  29.4 0.2 collective-permute-start.9
  29.6 0.5 collective-permute-done.7.refs_1_
  30.1 3.3 %collective-permute-done.8.refs_2_ = bf16[16,2048]{1,0:T(8,128)(2,1)S(1)} collective-permute-done((bf16[16,2048]{1,0:T(8,128)(2,1)S(1)}, bf16[16,2048]{1,0:T(8,128)(2,1)S(1)}, u32[]{:S(2)}, u32[]{:S(2)}) %collective-permute-start.8) | collective-permute-done | bytes 65568 | tf_op jit(solution)/shard_map/ppermute | solution.py:304
  33.3 2.1 %collective-permute-done.9.refs_3_ = bf16[16,2048]{1,0:T(8,128)(2,1)S(1)} collective-permute-done((bf16[16,2048]{1,0:T(8,128)(2,1)S(1)}, bf16[16,2048]{1,0:T(8,128)(2,1)S(1)}, u32[]{:S(2)}, u32[]{:S(2)}) %collective-permute-start.9) | collective-permute-done | bytes 65568 | tf_op jit(solution)/shard_map/ppermute | solution.py:304
  35.4 0.5 shard_map.98
  36.0 0.1 collective-permute-start.13
  36.1 1.7 %collective-permute-done.13.refs_5_.refs_6_ = bf16[512,384]{1,0:T(8,128)(2,1)S(1)} collective-permute-done((bf16[512,384]{1,0:T(8,128)(2,1)S(1)}, bf16[512,384]{1,0:T(8,128)(2,1)S(1)}, u32[]{:S(2)}, u32[]{:S(2)}) %collective-permute-start.13) | collective-permute-done | bytes 393248 | tf_op jit(solution)/shard_map/ppermute | solution.py:291
  37.8 0.4 shard_map.99
  38.2 0.6 collective-permute-start.17
  38.8 1.1 %shard_map.100 = (bf16[16,2048]{1,0:T(8,128)(2,1)S(1)}, bf16[16,2048]{1,0:T(8,128)(2,1)S(1)}, bf16[16,2048]{1,0:T(8,128)(2,1)S(1)}, bf16[16,2048]{1,0:T(8,128)(2,1)S(1)}) custom-call(bf16[64,768]{1,0:T(8,128)(2,1)S(1)} %get-tuple-element.76.refs_0_.refs_1_, bf16[512,768]{1,0:T(8,128)(2,1)S(1)} %bitcast.8, ...), custom_call_target="tpu_custom_call" | custom-call | tf_op jit(solution)/shard_map/pallas_call | solution.py:38
  39.9 1.7 %collective-permute-start.15 = (bf16[16,2048]{1,0:T(8,128)(2,1)S(1)}, bf16[16,2048]{1,0:T(8,128)(2,1)S(1)}, u32[]{:S(2)}, u32[]{:S(2)}) collective-permute-start(bf16[16,2048]{1,0:T(8,128)(2,1)S(1)} %get-tuple-element.79), channel_id=1, source_target_pairs={{0,8},{4,12},{8,0},{12,4},{1,9},{5,13},{9,1},{13,5},{2,10},{6,14},... | collective-permute-start | bytes 196616 | tf_op jit(solution)/shard_map/ppermute | solution.py:304
  41.6 2.7 %collective-permute-start.16 = (bf16[16,2048]{1,0:T(8,128)(2,1)S(1)}, bf16[16,2048]{1,0:T(8,128)(2,1)S(1)}, u32[]{:S(2)}, u32[]{:S(2)}) collective-permute-start(bf16[16,2048]{1,0:T(8,128)(2,1)S(1)} %get-tuple-element.80), channel_id=1, source_target_pairs={{0,12},{4,8},{8,4},{12,0},{1,13},{5,9},{9,5},{13,1},{2,14},{6,10},... | collective-permute-start | bytes 196616 | tf_op jit(solution)/shard_map/ppermute | solution.py:304
  44.3 0.5 collective-permute-done.14.refs_3_.refs_4_
  44.8 3.4 %collective-permute-done.15.refs_4_.refs_5_ = bf16[16,2048]{1,0:T(8,128)(2,1)S(1)} collective-permute-done((bf16[16,2048]{1,0:T(8,128)(2,1)S(1)}, bf16[16,2048]{1,0:T(8,128)(2,1)S(1)}, u32[]{:S(2)}, u32[]{:S(2)}) %collective-permute-start.15) | collective-permute-done | bytes 65568 | tf_op jit(solution)/shard_map/ppermute | solution.py:304
  48.3 1.1 %shard_map.102 = (bf16[32,1024]{1,0:T(8,128)(2,1)S(1)}, bf16[32,1024]{1,0:T(8,128)(2,1)S(1)}, bf16[32,1024]{1,0:T(8,128)(2,1)S(1)}, bf16[32,1024]{1,0:T(8,128)(2,1)S(1)}) custom-call(bf16[64,1536]{1,0:T(8,128)(2,1)S(1)} %get-tuple-element.82.refs_0_, bf16[64,1536]{1,0:T(8,128)(2,1)S(1)} %collective-permute-done.17.refs_1_, bf16[512,1536]{1,0:T(8,128)(2,1)S(1)} %bitcast.11, ...), custom_call_target="tpu_custom_call" | custom-call | tf_op jit(solution)/shard_map/pallas_call | solution.py:38
  49.4 1.6 %collective-permute-start.22 = (bf16[64,1792]{1,0:T(8,128)(2,1)S(1)}, bf16[64,1792]{1,0:T(8,128)(2,1)S(1)}, u32[]{:S(2)}, u32[]{:S(2)}) collective-permute-start(bf16[64,1792]{1,0:T(8,128)(2,1)S(1)} %shard_map.106), channel_id=1, source_target_pairs={{0,2},{1,3},{2,0},{3,1},{4,6},{5,7},{6,4},{7,5},{8,10},{9,11},{10,... | collective-permute-start | bytes 688136 | tf_op jit(solution)/shard_map/ppermute | solution.py:295
  51.0 1.3 %collective-permute-start.18 = (bf16[32,1024]{1,0:T(8,128)(2,1)S(1)}, bf16[32,1024]{1,0:T(8,128)(2,1)S(1)}, u32[]{:S(2)}, u32[]{:S(2)}) collective-permute-start(bf16[32,1024]{1,0:T(8,128)(2,1)S(1)} %get-tuple-element.84), channel_id=1, source_target_pairs={{0,4},{4,0},{8,12},{12,8},{1,5},{5,1},{9,13},{13,9},{2,6},{6,2},{1... | collective-permute-start | bytes 196616 | tf_op jit(solution)/shard_map/ppermute | solution.py:304
  52.3 1.5 %collective-permute-start.19 = (bf16[32,1024]{1,0:T(8,128)(2,1)S(1)}, bf16[32,1024]{1,0:T(8,128)(2,1)S(1)}, u32[]{:S(2)}, u32[]{:S(2)}) collective-permute-start(bf16[32,1024]{1,0:T(8,128)(2,1)S(1)} %get-tuple-element.85), channel_id=1, source_target_pairs={{0,8},{4,12},{8,0},{12,4},{1,9},{5,13},{9,1},{13,5},{2,10},{6,14},... | collective-permute-start | bytes 196616 | tf_op jit(solution)/shard_map/ppermute | solution.py:304
  53.8 1.6 %collective-permute-start.20 = (bf16[32,1024]{1,0:T(8,128)(2,1)S(1)}, bf16[32,1024]{1,0:T(8,128)(2,1)S(1)}, u32[]{:S(2)}, u32[]{:S(2)}) collective-permute-start(bf16[32,1024]{1,0:T(8,128)(2,1)S(1)} %get-tuple-element.86), channel_id=1, source_target_pairs={{0,12},{4,8},{8,4},{12,0},{1,13},{5,9},{9,5},{13,1},{2,14},{6,10},... | collective-permute-start | bytes 196616 | tf_op jit(solution)/shard_map/ppermute | solution.py:304
  55.4 0.1 collective-permute-done.22.refs_2_
  55.6 0.1 collective-permute-start.24
  55.6 0.8 %collective-permute-done.18.refs_1_.refs_2_ = bf16[32,1024]{1,0:T(8,128)(2,1)S(1)} collective-permute-done((bf16[32,1024]{1,0:T(8,128)(2,1)S(1)}, bf16[32,1024]{1,0:T(8,128)(2,1)S(1)}, u32[]{:S(2)}, u32[]{:S(2)}) %collective-permute-start.18) | collective-permute-done | bytes 65568 | tf_op jit(solution)/shard_map/ppermute | solution.py:304
  56.5 1.7 %collective-permute-done.19.refs_2_.refs_3_ = bf16[32,1024]{1,0:T(8,128)(2,1)S(1)} collective-permute-done((bf16[32,1024]{1,0:T(8,128)(2,1)S(1)}, bf16[32,1024]{1,0:T(8,128)(2,1)S(1)}, u32[]{:S(2)}, u32[]{:S(2)}) %collective-permute-start.19) | collective-permute-done | bytes 65568 | tf_op jit(solution)/shard_map/ppermute | solution.py:304
  58.1 1.7 %collective-permute-done.20.refs_3_.refs_4_ = bf16[32,1024]{1,0:T(8,128)(2,1)S(1)} collective-permute-done((bf16[32,1024]{1,0:T(8,128)(2,1)S(1)}, bf16[32,1024]{1,0:T(8,128)(2,1)S(1)}, u32[]{:S(2)}, u32[]{:S(2)}) %collective-permute-start.20) | collective-permute-done | bytes 65568 | tf_op jit(solution)/shard_map/ppermute | solution.py:304
  59.8 0.6 collective-permute-start.21
  60.4 1.3 %shard_map.101 = (bf16[256,2048]{1,0:T(8,128)(2,1)}, f32[8,128]{1,0:T(8,128)S(1)}) custom-call(bf16[256,64]{1,0:T(8,128)(2,1)S(1)} %get-tuple-element.47.refs_0_, f32[64,128]{1,0:T(8,128)S(1)} %get-tuple-element.48.refs_1_, bf16[16,2048]{1,0:T(8,128)(2,1)S(1)} %get-tuple-element.77.refs_2_, bf16[16,2048]{1,0:T(8,128)(2,1)S(1)} %collective-permute-done.14.refs_3_.refs_4_, ...), custom_call_target="tpu_custom_call" | custom-call | tf_op jit(solution)/shard_map/pallas_call | solution.py:38
  61.7 1.0 %shard_map.104.refs_2_ = bf16[256,2048]{1,0:T(8,128)(2,1)} custom-call(bf16[256,64]{1,0:T(8,128)(2,1)S(1)} %get-tuple-element.47.refs_0_, bf16[32,1024]{1,0:T(8,128)(2,1)S(1)} %get-tuple-element.83.refs_0_.refs_1_.refs_2_, bf16[32,1024]{1,0:T(8,128)(2,1)S(1)} %collective-permute-done.18.refs_1_.refs_2_, ...), custom_call_target="tpu_custom_call" | custom-call | tf_op jit(solution)/shard_map/pallas_call | solution.py:38
  62.8 2.1 %collective-permute-done.21.refs_1_ = bf16[64,1024]{1,0:T(8,128)(2,1)S(1)} collective-permute-done((bf16[64,1024]{1,0:T(8,128)(2,1)S(1)}, bf16[64,1024]{1,0:T(8,128)(2,1)S(1)}, u32[]{:S(2)}, u32[]{:S(2)}) %collective-permute-start.21) | collective-permute-done | bytes 131104 | tf_op jit(solution)/shard_map/ppermute | solution.py:295
  64.9 1.0 %shard_map.105 = bf16[256,2048]{1,0:T(8,128)(2,1)} custom-call(bf16[256,64]{1,0:T(8,128)(2,1)S(1)} %get-tuple-element.47.refs_0_, bf16[64,1024]{1,0:T(8,128)(2,1)S(1)} %collective-permute-done.21.refs_1_, bf16[256,2048]{1,0:T(8,128)(2,1)} %shard_map.104.refs_2_), custom_call_target="tpu_custom_call", output_to_operand_aliasing={{}: (2, {})} | custom-call | tf_op jit(solution)/shard_map/pallas_call | solution.py:38
  65.9 1.6 %shard_map.108 = f32[512,768]{1,0:T(8,128)} custom-call(bf16[128,512]{1,0:T(8,128)(2,1)S(1)} %get-tuple-element.88.refs_0_, bf16[128,768]{1,0:T(8,128)(2,1)S(1)} %get-tuple-element.89.refs_1_, bf16[128,512]{1,0:T(8,128)(2,1)S(1)} %collective-permute-done.23.refs_2_, bf16[128,768]{1,0:T(8,128)(2,1)S(1)} %collective-permute-done.24.refs_3_), custom_call_target="tpu_custom_call" | custom-call | tf_op jit(solution)/shard_map/pallas_call | solution.py:38
  (21 shorter events, 0.2 us)
Async XLA Ops:
  0.6 15.2 %copy-start.1 = (bf16[1,512,1536]{2,1,0:T(8,128)(2,1)S(1)}, bf16[1,512,1536]{2,1,0:T(8,128)(2,1)}, u32[]{:S(2)}) copy-start(bf16[1,512,1536]{2,1,0:T(8,128)(2,1)} %param.12) | copy-start | bytes 4718596
  0.6 15.3 %copy-start = (bf16[1,512,768]{2,1,0:T(8,128)(2,1)S(1)}, bf16[1,512,768]{2,1,0:T(8,128)(2,1)}, u32[]{:S(2)}) copy-start(bf16[1,512,768]{2,1,0:T(8,128)(2,1)} %param.13) | copy-start | bytes 2359300
  2.5 13.2 %collective-permute-start.3 = (bf16[512,384]{1,0:T(8,128)(2,1)S(1)}, bf16[512,384]{1,0:T(8,128)(2,1)S(1)}, u32[]{:S(2)}, u32[]{:S(2)}) collective-permute-start(bf16[512,384]{1,0:T(8,128)(2,1)S(1)} %get-tuple-element.59), channel_id=1, source_target_pairs={{0,2},{1,3},{2,0},{3,1},{4,6},{5,7},{6,4},{7,5},{8,10},{9,11},{10,... | collective-permute-start | bytes 1179656 | tf_op jit(solution)/shard_map/ppermute | solution.py:295
  5.5 4.4 %collective-permute-start = (bf16[16,2048]{1,0:T(8,128)(2,1)S(1)}, bf16[16,2048]{1,0:T(8,128)(2,1)S(1)}, u32[]{:S(2)}, u32[]{:S(2)}) collective-permute-start(bf16[16,2048]{1,0:T(8,128)(2,1)S(1)} %get-tuple-element.56), channel_id=1, source_target_pairs={{0,4},{4,0},{8,12},{12,8},{1,5},{5,1},{9,13},{13,9},{2,6},{6,2},{1... | collective-permute-start | bytes 196616 | tf_op jit(solution)/shard_map/ppermute | solution.py:304
  7.1 7.0 %collective-permute-start.1 = (bf16[16,2048]{1,0:T(8,128)(2,1)S(1)}, bf16[16,2048]{1,0:T(8,128)(2,1)S(1)}, u32[]{:S(2)}, u32[]{:S(2)}) collective-permute-start(bf16[16,2048]{1,0:T(8,128)(2,1)S(1)} %get-tuple-element.57), channel_id=1, source_target_pairs={{0,8},{4,12},{8,0},{12,4},{1,9},{5,13},{9,1},{13,5},{2,10},{6,14},... | collective-permute-start | bytes 196616 | tf_op jit(solution)/shard_map/ppermute | solution.py:304
  9.7 6.1 %collective-permute-start.2 = (bf16[16,2048]{1,0:T(8,128)(2,1)S(1)}, bf16[16,2048]{1,0:T(8,128)(2,1)S(1)}, u32[]{:S(2)}, u32[]{:S(2)}) collective-permute-start(bf16[16,2048]{1,0:T(8,128)(2,1)S(1)} %get-tuple-element.58), channel_id=1, source_target_pairs={{0,12},{4,8},{8,4},{12,0},{1,13},{5,9},{9,5},{13,1},{2,14},{6,10},... | collective-permute-start | bytes 196616 | tf_op jit(solution)/shard_map/ppermute | solution.py:304
  15.8 7.7 %collective-permute-start.5 = (bf16[512,1536]{1,0:T(8,128)(2,1)S(1)}, bf16[512,1536]{1,0:T(8,128)(2,1)S(1)}, u32[]{:S(2)}, u32[]{:S(2)}) collective-permute-start(bf16[512,1536]{1,0:T(8,128)(2,1)S(1)} %bitcast.9), channel_id=1, source_target_pairs={{0,1},{1,0},{2,3},{3,2},{4,5},{5,4},{6,7},{7,6},{8,9},{9,8},{10,11... | collective-permute-start | bytes 4718600 | tf_op jit(solution)/shard_map/ppermute | solution.py:291
  15.9 13.5 %collective-permute-start.10 = (bf16[512,768]{1,0:T(8,128)(2,1)S(1)}, bf16[512,768]{1,0:T(8,128)(2,1)S(1)}, u32[]{:S(2)}, u32[]{:S(2)}) collective-permute-start(bf16[512,768]{1,0:T(8,128)(2,1)S(1)} %bitcast.6), channel_id=1, source_target_pairs={{0,1},{1,0},{2,3},{3,2},{4,5},{5,4},{6,7},{7,6},{8,9},{9,8},{10,11... | collective-permute-start | bytes 2359304 | tf_op jit(solution)/shard_map/ppermute | solution.py:291
  16.4 10.4 %collective-permute-start.11 = (bf16[512,384]{1,0:T(8,128)(2,1)S(1)}, bf16[512,384]{1,0:T(8,128)(2,1)S(1)}, u32[]{:S(2)}, u32[]{:S(2)}) collective-permute-start(bf16[512,384]{1,0:T(8,128)(2,1)S(1)} %collective-permute-done.3.refs_4_.refs_6_.refs_3_), channel_id=1, source_target_pairs={{0,1},{1,0},{2,3},{3,2},{4,5},{5,4},{6,7},{7,6},{8,9},{9,8},{10,11... | collective-permute-start | bytes 1179656 | tf_op jit(solution)/shard_map/ppermute | solution.py:291
  16.5 19.5 %collective-permute-start.12 = (bf16[512,384]{1,0:T(8,128)(2,1)S(1)}, bf16[512,384]{1,0:T(8,128)(2,1)S(1)}, u32[]{:S(2)}, u32[]{:S(2)}) collective-permute-start(bf16[512,384]{1,0:T(8,128)(2,1)S(1)} %collective-permute-done.3.refs_4_.refs_6_.refs_3_), channel_id=1, source_target_pairs={{0,16},{16,0},{1,17},{17,1},{2,18},{18,2},{3,19},{19,3},{4,20},{20... | collective-permute-start | bytes 1179656 | tf_op jit(solution)/shard_map/ppermute | solution.py:300
  18.0 5.6 %collective-permute-start.4 = (bf16[64,1024]{1,0:T(8,128)(2,1)S(1)}, bf16[64,1024]{1,0:T(8,128)(2,1)S(1)}, u32[]{:S(2)}, u32[]{:S(2)}) collective-permute-start(bf16[64,1024]{1,0:T(8,128)(2,1)S(1)} %get-tuple-element.62), channel_id=1, source_target_pairs={{0,2},{1,3},{2,0},{3,1},{4,6},{5,7},{6,4},{7,5},{8,10},{9,11},{10,... | collective-permute-start | bytes 393224 | tf_op jit(solution)/shard_map/ppermute | solution.py:295
  24.2 11.8 %collective-permute-start.6 = (bf16[64,1536]{1,0:T(8,128)(2,1)S(1)}, bf16[64,1536]{1,0:T(8,128)(2,1)S(1)}, u32[]{:S(2)}, u32[]{:S(2)}) collective-permute-start(bf16[64,1536]{1,0:T(8,128)(2,1)S(1)} %get-tuple-element.66), channel_id=1, source_target_pairs={{0,2},{1,3},{2,0},{3,1},{4,6},{5,7},{6,4},{7,5},{8,10},{9,11},{10,... | collective-permute-start | bytes 589832 | tf_op jit(solution)/shard_map/ppermute | solution.py:295
  25.1 5.0 %collective-permute-start.7 = (bf16[16,2048]{1,0:T(8,128)(2,1)S(1)}, bf16[16,2048]{1,0:T(8,128)(2,1)S(1)}, u32[]{:S(2)}, u32[]{:S(2)}) collective-permute-start(bf16[16,2048]{1,0:T(8,128)(2,1)S(1)} %get-tuple-element.68), channel_id=1, source_target_pairs={{0,4},{4,0},{8,12},{12,8},{1,5},{5,1},{9,13},{13,9},{2,6},{6,2},{1... | collective-permute-start | bytes 196616 | tf_op jit(solution)/shard_map/ppermute | solution.py:304
  26.8 6.6 %collective-permute-start.8 = (bf16[16,2048]{1,0:T(8,128)(2,1)S(1)}, bf16[16,2048]{1,0:T(8,128)(2,1)S(1)}, u32[]{:S(2)}, u32[]{:S(2)}) collective-permute-start(bf16[16,2048]{1,0:T(8,128)(2,1)S(1)} %get-tuple-element.69), channel_id=1, source_target_pairs={{0,8},{4,12},{8,0},{12,4},{1,9},{5,13},{9,1},{13,5},{2,10},{6,14},... | collective-permute-start | bytes 196616 | tf_op jit(solution)/shard_map/ppermute | solution.py:304
  29.4 6.1 %collective-permute-start.9 = (bf16[16,2048]{1,0:T(8,128)(2,1)S(1)}, bf16[16,2048]{1,0:T(8,128)(2,1)S(1)}, u32[]{:S(2)}, u32[]{:S(2)}) collective-permute-start(bf16[16,2048]{1,0:T(8,128)(2,1)S(1)} %get-tuple-element.70), channel_id=1, source_target_pairs={{0,12},{4,8},{8,4},{12,0},{1,13},{5,9},{9,5},{13,1},{2,14},{6,10},... | collective-permute-start | bytes 196616 | tf_op jit(solution)/shard_map/ppermute | solution.py:304
  36.0 1.8 %collective-permute-start.13 = (bf16[512,384]{1,0:T(8,128)(2,1)S(1)}, bf16[512,384]{1,0:T(8,128)(2,1)S(1)}, u32[]{:S(2)}, u32[]{:S(2)}) collective-permute-start(bf16[512,384]{1,0:T(8,128)(2,1)S(1)} %collective-permute-done.12.refs_4_), channel_id=1, source_target_pairs={{0,1},{1,0},{2,3},{3,2},{4,5},{5,4},{6,7},{7,6},{8,9},{9,8},{10,11... | collective-permute-start | bytes 1179656 | tf_op jit(solution)/shard_map/ppermute | solution.py:291
  38.2 10.1 %collective-permute-start.17 = (bf16[64,1536]{1,0:T(8,128)(2,1)S(1)}, bf16[64,1536]{1,0:T(8,128)(2,1)S(1)}, u32[]{:S(2)}, u32[]{:S(2)}) collective-permute-start(bf16[64,1536]{1,0:T(8,128)(2,1)S(1)} %get-tuple-element.82.refs_0_), channel_id=1, source_target_pairs={{0,2},{1,3},{2,0},{3,1},{4,6},{5,7},{6,4},{7,5},{8,10},{9,11},{10,... | collective-permute-start | bytes 589832 | tf_op jit(solution)/shard_map/ppermute | solution.py:295
  39.8 5.0 %collective-permute-start.14 = (bf16[16,2048]{1,0:T(8,128)(2,1)S(1)}, bf16[16,2048]{1,0:T(8,128)(2,1)S(1)}, u32[]{:S(2)}, u32[]{:S(2)}) collective-permute-start(bf16[16,2048]{1,0:T(8,128)(2,1)S(1)} %get-tuple-element.78), channel_id=1, source_target_pairs={{0,4},{4,0},{8,12},{12,8},{1,5},{5,1},{9,13},{13,9},{2,6},{6,2},{1... | collective-permute-start | bytes 196616 | tf_op jit(solution)/shard_map/ppermute | solution.py:304
  39.9 8.4 %collective-permute-start.15 = (bf16[16,2048]{1,0:T(8,128)(2,1)S(1)}, bf16[16,2048]{1,0:T(8,128)(2,1)S(1)}, u32[]{:S(2)}, u32[]{:S(2)}) collective-permute-start(bf16[16,2048]{1,0:T(8,128)(2,1)S(1)} %get-tuple-element.79), channel_id=1, source_target_pairs={{0,8},{4,12},{8,0},{12,4},{1,9},{5,13},{9,1},{13,5},{2,10},{6,14},... | collective-permute-start | bytes 196616 | tf_op jit(solution)/shard_map/ppermute | solution.py:304
  41.6 6.6 %collective-permute-start.16 = (bf16[16,2048]{1,0:T(8,128)(2,1)S(1)}, bf16[16,2048]{1,0:T(8,128)(2,1)S(1)}, u32[]{:S(2)}, u32[]{:S(2)}) collective-permute-start(bf16[16,2048]{1,0:T(8,128)(2,1)S(1)} %get-tuple-element.80), channel_id=1, source_target_pairs={{0,12},{4,8},{8,4},{12,0},{1,13},{5,9},{9,5},{13,1},{2,14},{6,10},... | collective-permute-start | bytes 196616 | tf_op jit(solution)/shard_map/ppermute | solution.py:304
  49.4 6.1 %collective-permute-start.22 = (bf16[64,1792]{1,0:T(8,128)(2,1)S(1)}, bf16[64,1792]{1,0:T(8,128)(2,1)S(1)}, u32[]{:S(2)}, u32[]{:S(2)}) collective-permute-start(bf16[64,1792]{1,0:T(8,128)(2,1)S(1)} %shard_map.106), channel_id=1, source_target_pairs={{0,2},{1,3},{2,0},{3,1},{4,6},{5,7},{6,4},{7,5},{8,10},{9,11},{10,... | collective-permute-start | bytes 688136 | tf_op jit(solution)/shard_map/ppermute | solution.py:295
  51.0 5.5 %collective-permute-start.18 = (bf16[32,1024]{1,0:T(8,128)(2,1)S(1)}, bf16[32,1024]{1,0:T(8,128)(2,1)S(1)}, u32[]{:S(2)}, u32[]{:S(2)}) collective-permute-start(bf16[32,1024]{1,0:T(8,128)(2,1)S(1)} %get-tuple-element.84), channel_id=1, source_target_pairs={{0,4},{4,0},{8,12},{12,8},{1,5},{5,1},{9,13},{13,9},{2,6},{6,2},{1... | collective-permute-start | bytes 196616 | tf_op jit(solution)/shard_map/ppermute | solution.py:304
  52.3 5.9 %collective-permute-start.19 = (bf16[32,1024]{1,0:T(8,128)(2,1)S(1)}, bf16[32,1024]{1,0:T(8,128)(2,1)S(1)}, u32[]{:S(2)}, u32[]{:S(2)}) collective-permute-start(bf16[32,1024]{1,0:T(8,128)(2,1)S(1)} %get-tuple-element.85), channel_id=1, source_target_pairs={{0,8},{4,12},{8,0},{12,4},{1,9},{5,13},{9,1},{13,5},{2,10},{6,14},... | collective-permute-start | bytes 196616 | tf_op jit(solution)/shard_map/ppermute | solution.py:304
  53.8 6.1 %collective-permute-start.20 = (bf16[32,1024]{1,0:T(8,128)(2,1)S(1)}, bf16[32,1024]{1,0:T(8,128)(2,1)S(1)}, u32[]{:S(2)}, u32[]{:S(2)}) collective-permute-start(bf16[32,1024]{1,0:T(8,128)(2,1)S(1)} %get-tuple-element.86), channel_id=1, source_target_pairs={{0,12},{4,8},{8,4},{12,0},{1,13},{5,9},{9,5},{13,1},{2,14},{6,10},... | collective-permute-start | bytes 196616 | tf_op jit(solution)/shard_map/ppermute | solution.py:304
  55.6 10.3 %collective-permute-start.24 = (bf16[128,768]{1,0:T(8,128)(2,1)S(1)}, bf16[128,768]{1,0:T(8,128)(2,1)S(1)}, u32[]{:S(2)}, u32[]{:S(2)}) collective-permute-start(bf16[128,768]{1,0:T(8,128)(2,1)S(1)} %get-tuple-element.89.refs_1_), channel_id=1, source_target_pairs={{0,1},{1,0},{2,3},{3,2},{4,5},{5,4},{6,7},{7,6},{8,9},{9,8},{10,11... | collective-permute-start | bytes 589832 | tf_op jit(solution)/shard_map/ppermute | solution.py:291
  59.8 5.0 %collective-permute-start.21 = (bf16[64,1024]{1,0:T(8,128)(2,1)S(1)}, bf16[64,1024]{1,0:T(8,128)(2,1)S(1)}, u32[]{:S(2)}, u32[]{:S(2)}) collective-permute-start(bf16[64,1024]{1,0:T(8,128)(2,1)S(1)} %shard_map.103), channel_id=1, source_target_pairs={{0,2},{1,3},{2,0},{3,1},{4,6},{5,7},{6,4},{7,5},{8,10},{9,11},{10,... | collective-permute-start | bytes 393224 | tf_op jit(solution)/shard_map/ppermute | solution.py:295
  60.4 5.4 %collective-permute-start.23 = (bf16[128,512]{1,0:T(8,128)(2,1)S(1)}, bf16[128,512]{1,0:T(8,128)(2,1)S(1)}, u32[]{:S(2)}, u32[]{:S(2)}) collective-permute-start(bf16[128,512]{1,0:T(8,128)(2,1)S(1)} %get-tuple-element.90), channel_id=1, source_target_pairs={{0,1},{1,0},{2,3},{3,2},{4,5},{5,4},{6,7},{7,6},{8,9},{9,8},{10,11... | collective-permute-start | bytes 393224 | tf_op jit(solution)/shard_map/ppermute | solution.py:291

commit v5 on v4

v5 whole, which is shorter than its diff:
```python
import jax
import jax.numpy as jnp
from jax import lax
from jax.experimental import pallas as pl
from jax.experimental.pallas import tpu as pltpu
from jax.sharding import PartitionSpec as P

EXPERTS = 128
CORES = 2
VMEM = 40 * 1024 * 1024
F32 = jnp.float32
BF16 = jnp.bfloat16


def product(left, right, left_dim, right_dim, **kw):
    return lax.dot_general(
        left, right, (((left_dim,), (right_dim,)), ((), ())), preferred_element_type=F32, **kw
    )


def call(body, out_shape, args, far=0, after=(), token=False, **kw):
    out_shape = [*out_shape] + [shape((8, 128), F32)] * token
    specs = [pl.BlockSpec(memory_space=pltpu.VMEM)] * (len(args) - far)
    specs += [pl.BlockSpec(memory_space=pltpu.HBM)] * far
    specs += [pl.BlockSpec(memory_space=pl.ANY)] * len(after)
    kw.setdefault("out_specs", [pl.BlockSpec(memory_space=pltpu.VMEM)] * len(out_shape))
    args = [
        pltpu.with_memory_space_constraint(arg, pltpu.HBM) if i >= len(args) - far else arg
        for i, arg in enumerate(args)
    ]
    count, first, last = len(args), len(args) + len(after), len(args) + len(after) + len(out_shape)

    def kernel(*refs):
        if token:
            refs[last - 1][...] = jnp.zeros(refs[last - 1].shape, F32)
        body(*refs[:count], *refs[first : last - token], *refs[last:])

    return pl.pallas_call(
        kernel,
        out_shape=out_shape,
        in_specs=specs,
        compiler_params=pltpu.CompilerParams(vmem_limit_bytes=VMEM),
        cost_estimate=pl.CostEstimate(flops=0, bytes_accessed=0, transcendentals=0),
        **kw,
    )(*args, *after)


def shape(dims, kind=BF16):
    return jax.ShapeDtypeStruct(dims, kind)


def columns(k, part):
    return pl.ds(pl.multiple_of((lax.axis_index("fsdp") ^ k) * part, part), part)


def slot_kernel(groups, parts, capacity, *refs):
    sources, chunks, refs = refs[:5], refs[5 : 5 + groups], refs[5 + groups :]
    turned_out, gate_out, ids, gates, order, tok, cot, sems = refs
    copies = [
        pltpu.make_async_copy(source, target, sems.at[i])
        for i, (source, target) in enumerate(zip(sources, (ids, gates, order, tok, cot)))
    ]
    for copy in copies:
        copy.start()
    for copy in copies[:3]:
        copy.wait()
    choices, count = ids.shape
    slots = groups * capacity
    part = tok.shape[1] // parts
    slot = lax.broadcasted_iota(jnp.int32, (slots, count), 0)
    wanted = ((slot // capacity) ^ lax.axis_index("expert")) * (EXPERTS // groups)
    routed = jnp.zeros((slots, count), F32)
    gate = jnp.zeros((slots, count), F32)
    for k in range(choices):
        hit = ids[k : k + 1, :] == wanted
        routed = jnp.where(hit, 1.0, routed)
        gate = jnp.where(hit, gates[k : k + 1, :], gate)
    row = lax.broadcasted_iota(jnp.int32, (count, count), 0)
    col = lax.broadcasted_iota(jnp.int32, (count, count), 1)
    served = jnp.where(order[...] == row, 1.0, 0.0).astype(BF16)
    earlier = jnp.where(row < col, 1.0, 0.0).astype(BF16)
    by_rank = product(routed.astype(BF16), served, 1, 0)
    before = product(by_rank.astype(BF16), earlier, 1, 0)
    taken = jnp.where(before.astype(jnp.int32) == slot % capacity, by_rank, 0.0).astype(BF16)
    pick = product(taken, served, 1, 1)
    turned_out[...] = product(served, taken, 1, 1).astype(BF16)
    slot_gate = jnp.sum(pick * gate, axis=1, keepdims=True)
    gate_out[...] = jnp.broadcast_to(slot_gate, gate_out.shape)
    pick = pick.astype(BF16)
    for copy, source, scale, top in ((copies[3], tok, None, 0), (copies[4], cot, slot_gate, capacity)):
        copy.wait()
        for k in range(parts):
            rows = product(pick, source[:, columns(k, part)], 1, 0)
            rows = (rows if scale is None else scale * rows).astype(BF16)
            for ke in range(groups):
                chunks[ke][top : top + capacity, k * part : (k + 1) * part] = rows[
                    ke * capacity : (ke + 1) * capacity
                ]


def split_kernel(groups, spread, capacity, *refs):
    chunks, by_x = refs[:groups], refs[groups:]
    half = by_x[0].shape[1]
    for kx in range(spread):
        for ke in range(groups):
            by_x[kx][ke * capacity : (ke + 1) * capacity] = chunks[ke][
                :capacity, kx * half : (kx + 1) * half
            ]


def far_kernel(groups, spread, capacity, *refs):
    by_e, by_x = refs[:groups], refs[groups:]
    for ke in range(groups):
        for kx in range(1, spread):
            by_x[kx - 1][ke * capacity : (ke + 1) * capacity] = by_e[ke][
                kx * capacity : (kx + 1) * capacity
            ]


def pre_kernel(spread, *refs):
    left, (own, sib, *outs) = refs[:spread], refs[spread:]
    part = own.shape[0]
    rows = jnp.concatenate([r[...] for r in left], axis=0)
    total = product(rows[:, :part], own[...], 1, 0) + product(rows[:, part:], sib[...], 1, 0)
    count = left[0].shape[0]
    for kx in range(spread):
        outs[kx][...] = total[kx * count : (kx + 1) * count].astype(outs[kx].dtype)


def back_kernel(groups, capacity, *refs):
    chunks, weights, (grads, back) = refs[:groups], refs[groups:-2], refs[-2:]
    part = weights[0].shape[0]
    grads[...] = jnp.concatenate([c[capacity:] for c in chunks], axis=0)
    total = product(grads[:, :part], weights[0][...], 1, 0)
    for k, weight in enumerate(weights[1:], 1):
        total += product(grads[:, k * part : (k + 1) * part], weight[...], 1, 0)
    back[...] = total


def act_kernel(spread, *refs):
    back, hidden, d_pre = refs[spread:]
    pre = refs[0][...]
    for ref in refs[1:spread]:
        pre += ref[...].astype(F32)
    feed = back.shape[1]
    gate_act, up_act = pre[:, :feed], pre[:, feed:]
    sig = 1.0 / (1.0 + jnp.exp(-gate_act))
    silu = gate_act * sig
    hidden[...] = (silu * up_act).astype(BF16)
    d_pre[:, :feed] = (back[...] * up_act * (sig * (1.0 + gate_act * (1.0 - sig)))).astype(BF16)
    d_pre[:, feed:] = (back[...] * silu).astype(BF16)


def expert_out_kernel(groups, capacity, hidden, *refs):
    weights, chunks = refs[:-groups], refs[-groups:]
    part = weights[0].shape[0]
    for k, weight in enumerate(weights):
        value = product(hidden[...], weight[...], 1, 1).astype(BF16)
        for ke in range(groups):
            chunks[ke][:, k * part : (k + 1) * part] = value[ke * capacity : (ke + 1) * capacity]


def d_rows_kernel(groups, spread, capacity, *refs):
    left, (own, sib, *chunks) = refs[:spread], refs[spread:]
    part = own.shape[0]
    rows = jnp.concatenate([r[...] for r in left], axis=0)
    for kc, weight in enumerate((own, sib)):
        value = product(rows, weight[...], 1, 1).astype(BF16)
        for ke in range(groups):
            for kx in range(spread):
                at = (kx * groups + ke) * capacity
                chunks[ke][kx * capacity : (kx + 1) * capacity, kc * part : (kc + 1) * part] = value[
                    at : at + capacity
                ]


def pack_kernel(spread, grads, hidden, *outs):
    half = grads.shape[1] // spread
    for kx in range(1, spread):
        outs[kx - 1][:, :half] = grads[:, kx * half : (kx + 1) * half]
        outs[kx - 1][:, half:] = hidden[...]


def gather_kernel(spread, grads, hidden, *refs):
    far, (own, sib, all_hidden) = refs[: spread - 1], refs[spread - 1 :]
    part = own.shape[1]
    count = grads.shape[0]
    for kx in range(spread):
        source = far[kx - 1] if kx else grads
        at = pl.ds(kx * count, count)
        own[at] = source[:, :part]
        sib[at] = source[:, part : 2 * part]
        all_hidden[at] = source[:, 2 * part :] if kx else hidden[...]


def weight_kernel(own, hidden, sib, sib_hidden, out):
    left = jnp.concatenate([own[...], sib[...]], axis=0)
    right = jnp.concatenate([hidden[...], sib_hidden[...]], axis=0)
    out[...] = product(left, right, 0, 0)


def combine_kernel(groups, parts, turned, gate, *refs):
    chunks, (out, held, sems) = refs[:groups], refs[groups:]
    part = out.shape[1] // parts
    twice = jnp.concatenate([turned[...], turned[...]], axis=1)
    copies = []
    for k in range(parts):
        rows = jnp.concatenate([c[:, k * part : (k + 1) * part] for c in chunks], axis=0)
        weighted = rows.astype(F32) * gate[:, :1]
        high = weighted.astype(BF16)
        low = (weighted - high.astype(F32)).astype(BF16)
        both = jnp.concatenate([high, low], axis=0)
        held[k] = product(twice, both, 1, 0).astype(BF16)
        copies.append(pltpu.make_async_copy(held.at[k], out.at[:, columns(k, part)], sems.at[k]))
        copies[-1].start()
    for copy in copies:
        copy.wait()


def d_tokens_kernel(groups, parts, capacity, span, turned, *refs):
    *refs, out, held, sems = refs
    part = out.shape[1] // parts
    copies = []
    for n, kx in enumerate(span):
        for kc in range(CORES):
            cols = slice(kc * part, (kc + 1) * part)
            if kx:
                rows = refs[n][:, cols]
            else:
                rows = jnp.concatenate([refs[ke][:capacity, cols] for ke in range(groups)], axis=0)
            i = len(copies)
            held[i] = product(turned[...], rows, 1, 0).astype(BF16)
            target = out.at[:, columns(kx * CORES + kc, part)]
            copies.append(pltpu.make_async_copy(held.at[i], target, sems.at[i]))
            copies[-1].start()
    for copy in copies:
        copy.wait()


def per_device(tokens, cotangent, route_ids, route_gates, served_order, w_in, w_out):
    groups = lax.axis_size("expert")
    parts = lax.axis_size("fsdp")
    spread = parts // CORES
    count, width = tokens.shape
    capacity = count * route_ids.shape[1] // EXPERTS
    feed = w_out.shape[2]
    slots = groups * capacity
    half = width // spread
    part = width // parts

    def bound(kernel, *sizes):
        return lambda *refs: kernel(*sizes, *refs)

    def to_core(value):
        return lax.ppermute(value, "fsdp", [(i, i ^ 1) for i in range(parts)])

    def to_x(values):
        return [
            lax.ppermute(value, "fsdp", [(i, i ^ ((k + 1) * CORES)) for i in range(parts)])
            for k, value in enumerate(values)
        ]

    def to_expert(chunks):
        return [
            lax.ppermute(value, "expert", [(i, i ^ ke) for i in range(groups)]) if ke else value
            for ke, value in enumerate(chunks)
        ]

    chunk = [shape((capacity, width))] * groups
    in_own, out_own = w_in[0], w_out[0]
    *chunks, turned, gate = call(
        bound(slot_kernel, groups, parts, capacity),
        [shape((2 * capacity, width))] * groups
        + [shape((count, slots)), shape((slots, 128), F32)],
        (route_ids.T, route_gates.T, served_order, tokens, cotangent),
        far=5,
        scratch_shapes=[
            pltpu.VMEM(route_ids.shape[::-1], jnp.int32),
            pltpu.VMEM(route_gates.shape[::-1], F32),
            pltpu.VMEM(served_order.shape, jnp.int32),
            pltpu.VMEM(tokens.shape, BF16),
            pltpu.VMEM(cotangent.shape, BF16),
            pltpu.SemaphoreType.DMA((5,)),
        ],
    )
    in_own, out_own, chunks[0] = lax.optimization_barrier((in_own, out_own, chunks[0]))
    chunks = to_expert(chunks)
    out_far = to_x([out_own] * (spread - 1))
    in_sib, out_sib = to_core(in_own), to_core(out_own)
    near, *far = call(
        bound(split_kernel, groups, spread, capacity), [shape((slots, half))] * spread, chunks
    )
    pre, *pre_far = call(
        bound(pre_kernel, spread),
        [shape((slots, 2 * feed), F32)] + [shape((slots, 2 * feed))] * (spread - 1),
        (near, *to_x(far), in_own, in_sib),
    )
    out_far, pre = lax.optimization_barrier((out_far, pre))
    w_outs = [out_own, out_sib] + [w for value in out_far for w in (value, to_core(value))]
    grads, back = call(
        bound(back_kernel, groups, capacity),
        [shape((slots, width)), shape((slots, feed), F32)],
        (*chunks, *w_outs),
    )
    hidden, d_pre = call(
        bound(act_kernel, spread),
        [shape((slots, feed)), shape((slots, 2 * feed))],
        (pre, *to_x(pre_far), back),
    )
    expert_out = to_expert(
        call(bound(expert_out_kernel, groups, capacity), chunk, (hidden, *w_outs))
    )
    d_rows = call(
        bound(d_rows_kernel, groups, spread, capacity),
        [shape((spread * capacity, half))] * groups,
        (d_pre, *to_x([d_pre] * (spread - 1)), in_own, in_sib),
        after=expert_out[1:3],
    )
    packed = call(
        bound(pack_kernel, spread),
        [shape((slots, half + feed))] * (spread - 1),
        (grads, hidden),
        after=d_rows[:1],
    )
    d_rows = to_expert(d_rows)
    far = call(
        bound(far_kernel, groups, spread, capacity),
        [shape((slots, half))] * (spread - 1),
        d_rows,
        after=expert_out[3:],
    )
    own, sib, all_hidden = call(
        bound(gather_kernel, spread),
        [shape((spread * slots, part))] * 2 + [shape((spread * slots, feed))],
        (grads, hidden, *to_x(packed)),
        after=far[:1],
    )
    d_w_out, token = call(
        weight_kernel,
        [shape((part, feed), F32)],
        (own, all_hidden, to_core(sib), to_core(all_hidden)),
        token=True,
    )

    def scattered(kernel, pieces, operands, **kw):
        out, *token = call(
            kernel,
            [shape((count, width))],
            operands,
            out_specs=[pl.BlockSpec(memory_space=pltpu.HBM)]
            + [pl.BlockSpec(memory_space=pltpu.VMEM)] * kw.get("token", False),
            scratch_shapes=[
                pltpu.VMEM((pieces, count, part), BF16),
                pltpu.SemaphoreType.DMA((pieces,)),
            ],
            **kw,
        )
        return out, token

    combined, token = scattered(
        bound(combine_kernel, groups, parts),
        parts,
        (turned, gate, *expert_out),
        after=(token,),
        token=True,
    )
    d_tokens, _ = scattered(
        bound(d_tokens_kernel, groups, parts, capacity, [0]),
        CORES,
        (turned, *d_rows),
        after=token,
    )
    far = to_x(far)
    d_tokens, _ = scattered(
        bound(d_tokens_kernel, groups, parts, capacity, range(1, spread)),
        len(far) * CORES,
        (turned, *far, d_tokens),
        far=1,
        input_output_aliases={1 + len(far): 0},
    )
    return combined, d_tokens, d_w_out[None]


def solution(mesh):
    rows = P(("replica", "expert", "fsdp"), None)
    weights = P("expert", "fsdp", None)
    return jax.shard_map(
        per_device,
        mesh=mesh,
        in_specs=(rows,) * 5 + (weights,) * 2,
        out_specs=(rows, rows, P(("replica", "expert"), "fsdp", None)),
        check_vma=False,
    )
```

time: 67.6 us -> 65 us (0.962)
  starting transfers between devices: 27 us -> 24.8 us
    ppermute x6, waiting for transfers between devices: 7.2 us -> 10.5 us  [to_x(): lax.ppermute(value, 'fsdp', [(i, i ^ (k + 1) * CORES) for i in range(part...]
    ppermute x12 -> x9, starting transfers between devices: 17.7 us -> 14.8 us  [to_expert(): lax.ppermute(value, 'expert', [(i, i ^ ke) for i in range(groups)])]
    ppermute x12 -> x9, waiting for transfers between devices: 19.8 us -> 17.7 us  [to_expert(): lax.ppermute(value, 'expert', [(i, i ^ ke) for i in range(groups)])]
    ppermute x6, starting transfers between devices: 7.06 us -> 8.91 us  [to_x(): lax.ppermute(value, 'fsdp', [(i, i ^ (k + 1) * CORES) for i in range(part...]
    ppermute x1 -> x0, starting transfers between devices: 1.52 us -> none  [to_replica(): return lax.ppermute(value, 'replica', [(i, i ^ n) for i in range(replicas)])]
    ppermute x6 -> x5, waiting for transfers between devices: 1.72 us -> 0.45 us  [to_core(): return lax.ppermute(value, 'fsdp', [(i, i ^ 1) for i in range(parts)])]
    pallas_call x15 -> x14, Pallas kernels: 10.8 us -> 10.6 us  [call(): pl.pallas_call(kernel, out_shape=out_shape, in_specs=specs, compiler_para...]
  transfers between devices with their start and end apart: 25 -> 20, of which waited for: 14 -> 12; matrix products, arithmetic and copies ran while one was open for 0% -> 0% of each run, Pallas kernels for 9% -> 10%
where the time goes in v5:
time: 65 us; the launch traced here: 64.9 us
  waiting for transfers between devices  28.6 us (44%)
  starting transfers between devices  24.8 us (38%)
  Pallas kernels  10.6 us (16%)
  between operations  0.78 us (1%)
    ppermute x9, waiting for transfers between devices, to_expert(): lax.ppermute(value, 'expert', [(i, i ^ ke) for i in range(groups)])  17.7 us
    ppermute x9, starting transfers between devices, to_expert(): lax.ppermute(value, 'expert', [(i, i ^ ke) for i in range(groups)])  14.8 us
    pallas_call x14, Pallas kernels, call(): pl.pallas_call(kernel, out_shape=out_shape, in_specs=specs, compiler_para...  10.6 us
    ppermute x6, waiting for transfers between devices, to_x(): lax.ppermute(value, 'fsdp', [(i, i ^ (k + 1) * CORES) for i in range(part...  10.5 us
    ppermute x6, starting transfers between devices, to_x(): lax.ppermute(value, 'fsdp', [(i, i ^ (k + 1) * CORES) for i in range(part...  8.91 us
  transfers between devices with their start and end apart: 20, of which 12 were waited for; matrix products, arithmetic and copies ran while one was open for 0% of the time, Pallas kernels for 10%

profile of v5, /device:TPU:0, one launch (start us, length us, event | category | flops | bytes accessed | tf_op | source)
XLA Modules:
  0.0 64.9 jit_solution(3480168037879738814)
XLA Ops:
  0.6 0.0 copy-start.1
  0.7 2.1 %shard_map.94 = (bf16[32,2048]{1,0:T(8,128)(2,1)S(1)}, bf16[32,2048]{1,0:T(8,128)(2,1)S(1)}, bf16[32,2048]{1,0:T(8,128)(2,1)S(1)}, bf16[32,2048]{1,0:T(8,128)(2,...) custom-call(s32[8,256]{1,0:T(8,128)} %bitcast.12, f32[8,256]{1,0:T(8,128)} %bitcast.13, s32[1,256]{1,0:T(1,128)} %refs_2_.1, ...), custom_call_target="tpu_custom_call" | custom-call | tf_op jit(solution)/shard_map/pallas_call | solution.py:38
  2.8 0.5 collective-permute-start.5
  3.3 2.6 %collective-permute-start = (bf16[512,768]{1,0:T(8,128)(2,1)}, bf16[512,768]{1,0:T(8,128)(2,1)S(1)}, u32[]{:S(2)}, u32[]{:S(2)}) collective-permute-start(bf16[512,768]{1,0:T(8,128)(2,1)} %bitcast.8), channel_id=1, source_target_pairs={{0,2},{1,3},{2,0},{3,1},{4,6},{5,7},{6,4},{7,5},{8,10},{9,11},{10,... | collective-permute-start | bytes 2359304 | tf_op jit(solution)/shard_map/ppermute | solution.py:259
  5.8 1.6 %collective-permute-start.1 = (bf16[32,2048]{1,0:T(8,128)(2,1)S(1)}, bf16[32,2048]{1,0:T(8,128)(2,1)S(1)}, u32[]{:S(2)}, u32[]{:S(2)}) collective-permute-start(bf16[32,2048]{1,0:T(8,128)(2,1)S(1)} %get-tuple-element.42), channel_id=1, source_target_pairs={{0,4},{4,0},{8,12},{12,8},{1,5},{5,1},{9,13},{13,9},{2,6},{6,2},{1... | collective-permute-start | bytes 393224 | tf_op jit(solution)/shard_map/ppermute | solution.py:265
  7.4 2.6 %collective-permute-start.2 = (bf16[32,2048]{1,0:T(8,128)(2,1)S(1)}, bf16[32,2048]{1,0:T(8,128)(2,1)S(1)}, u32[]{:S(2)}, u32[]{:S(2)}) collective-permute-start(bf16[32,2048]{1,0:T(8,128)(2,1)S(1)} %get-tuple-element.43), channel_id=1, source_target_pairs={{0,8},{4,12},{8,0},{12,4},{1,9},{5,13},{9,1},{13,5},{2,10},{6,14},... | collective-permute-start | bytes 393224 | tf_op jit(solution)/shard_map/ppermute | solution.py:265
  10.0 0.2 collective-permute-start.3
  10.2 3.1 %collective-permute-done.1.refs_1_ = bf16[32,2048]{1,0:T(8,128)(2,1)S(1)} collective-permute-done((bf16[32,2048]{1,0:T(8,128)(2,1)S(1)}, bf16[32,2048]{1,0:T(8,128)(2,1)S(1)}, u32[]{:S(2)}, u32[]{:S(2)}) %collective-permute-start.1) | collective-permute-done | bytes 131104 | tf_op jit(solution)/shard_map/ppermute | solution.py:265
  13.4 6.9 %collective-permute-done.2.refs_2_ = bf16[32,2048]{1,0:T(8,128)(2,1)S(1)} collective-permute-done((bf16[32,2048]{1,0:T(8,128)(2,1)S(1)}, bf16[32,2048]{1,0:T(8,128)(2,1)S(1)}, u32[]{:S(2)}, u32[]{:S(2)}) %collective-permute-start.2) | collective-permute-done | bytes 131104 | tf_op jit(solution)/shard_map/ppermute | solution.py:265
  20.3 0.0 collective-permute-done.3.refs_3_
  20.3 0.6 collective-permute-start.4
  20.9 0.0 collective-permute-start.7
  20.9 6.0 %collective-permute-done.4.refs_1_ = bf16[64,1024]{1,0:T(8,128)(2,1)S(1)} collective-permute-done((bf16[64,1024]{1,0:T(8,128)(2,1)S(1)}, bf16[64,1024]{1,0:T(8,128)(2,1)S(1)}, u32[]{:S(2)}, u32[]{:S(2)}) %collective-permute-start.4) | collective-permute-done | bytes 131104 | tf_op jit(solution)/shard_map/ppermute | solution.py:259
  27.0 0.0 collective-permute-done.5.refs_3_
  27.0 0.6 shard_map.96
  27.6 0.0 collective-permute-done.refs_6_.refs_3_
  27.6 0.1 collective-permute-start.8
  27.7 1.8 %collective-permute-start.6 = (bf16[64,1536]{1,0:T(8,128)(2,1)S(1)}, bf16[64,1536]{1,0:T(8,128)(2,1)S(1)}, u32[]{:S(2)}, u32[]{:S(2)}) collective-permute-start(bf16[64,1536]{1,0:T(8,128)(2,1)S(1)} %get-tuple-element.50), channel_id=1, source_target_pairs={{0,2},{1,3},{2,0},{3,1},{4,6},{5,7},{6,4},{7,5},{8,10},{9,11},{10,... | collective-permute-start | bytes 589832 | tf_op jit(solution)/shard_map/ppermute | solution.py:259
  29.5 0.0 collective-permute-done.7.refs_5_.refs_2_
  29.5 0.4 collective-permute-done.8.refs_7_.refs_4_
  29.9 0.7 %shard_map.97 = (bf16[64,2048]{1,0:T(8,128)(2,1)S(1)}, f32[64,768]{1,0:T(8,128)S(1)}) custom-call(bf16[32,2048]{1,0:T(8,128)(2,1)S(1)} %get-tuple-element.41.refs_0_, bf16[32,2048]{1,0:T(8,128)(2,1)S(1)} %collective-permute-done.1.refs_1_, bf16[32,2048]{1,0:T(8,128)(2,1)S(1)} %collective-permute-done.2.refs_2_, ...), custom_call_target="tpu_custom_call" | custom-call | tf_op jit(solution)/shard_map/pallas_call | solution.py:38
  30.6 4.4 %collective-permute-done.6.refs_1_ = bf16[64,1536]{1,0:T(8,128)(2,1)S(1)} collective-permute-done((bf16[64,1536]{1,0:T(8,128)(2,1)S(1)}, bf16[64,1536]{1,0:T(8,128)(2,1)S(1)}, u32[]{:S(2)}, u32[]{:S(2)}) %collective-permute-start.6) | collective-permute-done | bytes 196640 | tf_op jit(solution)/shard_map/ppermute | solution.py:259
  35.0 0.1 shard_map.98
  35.1 1.8 %collective-permute-start.12 = (bf16[64,1536]{1,0:T(8,128)(2,1)S(1)}, bf16[64,1536]{1,0:T(8,128)(2,1)S(1)}, u32[]{:S(2)}, u32[]{:S(2)}) collective-permute-start(bf16[64,1536]{1,0:T(8,128)(2,1)S(1)} %get-tuple-element.59.refs_0_), channel_id=1, source_target_pairs={{0,2},{1,3},{2,0},{3,1},{4,6},{5,7},{6,4},{7,5},{8,10},{9,11},{10,... | collective-permute-start | bytes 589832 | tf_op jit(solution)/shard_map/ppermute | solution.py:259
  37.0 1.1 %shard_map.99 = (bf16[16,2048]{1,0:T(8,128)(2,1)S(1)}, bf16[16,2048]{1,0:T(8,128)(2,1)S(1)}, bf16[16,2048]{1,0:T(8,128)(2,1)S(1)}, bf16[16,2048]{1,0:T(8,128)(2,1)S(1)}) custom-call(bf16[64,768]{1,0:T(8,128)(2,1)S(1)} %get-tuple-element.53.refs_0_.refs_1_, bf16[512,768]{1,0:T(8,128)(2,1)S(1)} %bitcast.11, ...), custom_call_target="tpu_custom_call" | custom-call | tf_op jit(solution)/shard_map/pallas_call | solution.py:38
  38.0 1.6 %collective-permute-start.9 = (bf16[16,2048]{1,0:T(8,128)(2,1)S(1)}, bf16[16,2048]{1,0:T(8,128)(2,1)S(1)}, u32[]{:S(2)}, u32[]{:S(2)}) collective-permute-start(bf16[16,2048]{1,0:T(8,128)(2,1)S(1)} %get-tuple-element.55), channel_id=1, source_target_pairs={{0,4},{4,0},{8,12},{12,8},{1,5},{5,1},{9,13},{13,9},{2,6},{6,2},{1... | collective-permute-start | bytes 196616 | tf_op jit(solution)/shard_map/ppermute | solution.py:265
  39.6 2.6 %collective-permute-start.10 = (bf16[16,2048]{1,0:T(8,128)(2,1)S(1)}, bf16[16,2048]{1,0:T(8,128)(2,1)S(1)}, u32[]{:S(2)}, u32[]{:S(2)}) collective-permute-start(bf16[16,2048]{1,0:T(8,128)(2,1)S(1)} %get-tuple-element.56), channel_id=1, source_target_pairs={{0,8},{4,12},{8,0},{12,4},{1,9},{5,13},{9,1},{13,5},{2,10},{6,14},... | collective-permute-start | bytes 196616 | tf_op jit(solution)/shard_map/ppermute | solution.py:265
  42.2 0.7 %collective-permute-done.9.refs_4_.refs_3_ = bf16[16,2048]{1,0:T(8,128)(2,1)S(1)} collective-permute-done((bf16[16,2048]{1,0:T(8,128)(2,1)S(1)}, bf16[16,2048]{1,0:T(8,128)(2,1)S(1)}, u32[]{:S(2)}, u32[]{:S(2)}) %collective-permute-start.9) | collective-permute-done | bytes 65568 | tf_op jit(solution)/shard_map/ppermute | solution.py:265
  43.0 2.5 %collective-permute-done.10.refs_5_.refs_4_ = bf16[16,2048]{1,0:T(8,128)(2,1)S(1)} collective-permute-done((bf16[16,2048]{1,0:T(8,128)(2,1)S(1)}, bf16[16,2048]{1,0:T(8,128)(2,1)S(1)}, u32[]{:S(2)}, u32[]{:S(2)}) %collective-permute-start.10) | collective-permute-done | bytes 65568 | tf_op jit(solution)/shard_map/ppermute | solution.py:265
  45.5 0.0 collective-permute-done.12.refs_1_
  45.5 1.1 %shard_map.100 = (bf16[32,1024]{1,0:T(8,128)(2,1)S(1)}, bf16[32,1024]{1,0:T(8,128)(2,1)S(1)}, bf16[32,1024]{1,0:T(8,128)(2,1)S(1)}, bf16[32,1024]{1,0:T(8,128)(2,1)S(1)}) custom-call(bf16[64,1536]{1,0:T(8,128)(2,1)S(1)} %get-tuple-element.59.refs_0_, bf16[64,1536]{1,0:T(8,128)(2,1)S(1)} %collective-permute-done.12.refs_1_, bf16[512,1536]{1,0:T(8,128)(2,1)S(1)} %bitcast.7, ...), custom_call_target="tpu_custom_call" | custom-call | tf_op jit(solution)/shard_map/pallas_call | solution.py:38
  46.7 0.6 collective-permute-start.13
  47.3 1.8 %collective-permute-start.11 = (bf16[16,2048]{1,0:T(8,128)(2,1)S(1)}, bf16[16,2048]{1,0:T(8,128)(2,1)S(1)}, u32[]{:S(2)}, u32[]{:S(2)}) collective-permute-start(bf16[16,2048]{1,0:T(8,128)(2,1)S(1)} %get-tuple-element.57), channel_id=1, source_target_pairs={{0,12},{4,8},{8,4},{12,0},{1,13},{5,9},{9,5},{13,1},{2,14},{6,10},... | collective-permute-start | bytes 196616 | tf_op jit(solution)/shard_map/ppermute | solution.py:265
  49.1 0.7 %collective-permute-start.14 = (bf16[32,1024]{1,0:T(8,128)(2,1)S(1)}, bf16[32,1024]{1,0:T(8,128)(2,1)S(1)}, u32[]{:S(2)}, u32[]{:S(2)}) collective-permute-start(bf16[32,1024]{1,0:T(8,128)(2,1)S(1)} %get-tuple-element.61), channel_id=1, source_target_pairs={{0,4},{4,0},{8,12},{12,8},{1,5},{5,1},{9,13},{13,9},{2,6},{6,2},{1... | collective-permute-start | bytes 196616 | tf_op jit(solution)/shard_map/ppermute | solution.py:265
  49.7 1.9 %collective-permute-start.15 = (bf16[32,1024]{1,0:T(8,128)(2,1)S(1)}, bf16[32,1024]{1,0:T(8,128)(2,1)S(1)}, u32[]{:S(2)}, u32[]{:S(2)}) collective-permute-start(bf16[32,1024]{1,0:T(8,128)(2,1)S(1)} %get-tuple-element.62), channel_id=1, source_target_pairs={{0,8},{4,12},{8,0},{12,4},{1,9},{5,13},{9,1},{13,5},{2,10},{6,14},... | collective-permute-start | bytes 196616 | tf_op jit(solution)/shard_map/ppermute | solution.py:265
  51.7 1.8 %collective-permute-start.16 = (bf16[32,1024]{1,0:T(8,128)(2,1)S(1)}, bf16[32,1024]{1,0:T(8,128)(2,1)S(1)}, u32[]{:S(2)}, u32[]{:S(2)}) collective-permute-start(bf16[32,1024]{1,0:T(8,128)(2,1)S(1)} %get-tuple-element.63), channel_id=1, source_target_pairs={{0,12},{4,8},{8,4},{12,0},{1,13},{5,9},{9,5},{13,1},{2,14},{6,10},... | collective-permute-start | bytes 196616 | tf_op jit(solution)/shard_map/ppermute | solution.py:265
  53.4 0.5 collective-permute-done.11.refs_4_.refs_5_
  53.9 1.3 %collective-permute-done.14.refs_1_.refs_2_ = bf16[32,1024]{1,0:T(8,128)(2,1)S(1)} collective-permute-done((bf16[32,1024]{1,0:T(8,128)(2,1)S(1)}, bf16[32,1024]{1,0:T(8,128)(2,1)S(1)}, u32[]{:S(2)}, u32[]{:S(2)}) %collective-permute-start.14) | collective-permute-done | bytes 65568 | tf_op jit(solution)/shard_map/ppermute | solution.py:265
  55.3 0.7 %collective-permute-done.15.refs_2_.refs_3_ = bf16[32,1024]{1,0:T(8,128)(2,1)S(1)} collective-permute-done((bf16[32,1024]{1,0:T(8,128)(2,1)S(1)}, bf16[32,1024]{1,0:T(8,128)(2,1)S(1)}, u32[]{:S(2)}, u32[]{:S(2)}) %collective-permute-start.15) | collective-permute-done | bytes 65568 | tf_op jit(solution)/shard_map/ppermute | solution.py:265
  56.0 1.8 %collective-permute-done.16.refs_3_.refs_4_ = bf16[32,1024]{1,0:T(8,128)(2,1)S(1)} collective-permute-done((bf16[32,1024]{1,0:T(8,128)(2,1)S(1)}, bf16[32,1024]{1,0:T(8,128)(2,1)S(1)}, u32[]{:S(2)}, u32[]{:S(2)}) %collective-permute-start.16) | collective-permute-done | bytes 65568 | tf_op jit(solution)/shard_map/ppermute | solution.py:265
  57.8 0.1 collective-permute-start.18
  57.9 0.5 collective-permute-start.17
  58.4 1.5 %collective-permute-start.19 = (bf16[64,1024]{1,0:T(8,128)(2,1)S(1)}, bf16[64,1024]{1,0:T(8,128)(2,1)S(1)}, u32[]{:S(2)}, u32[]{:S(2)}) collective-permute-start(bf16[64,1024]{1,0:T(8,128)(2,1)S(1)} %shard_map.102.refs_3_), channel_id=1, source_target_pairs={{0,2},{1,3},{2,0},{3,1},{4,6},{5,7},{6,4},{7,5},{8,10},{9,11},{10,... | collective-permute-start | bytes 393224 | tf_op jit(solution)/shard_map/ppermute | solution.py:259
  59.9 1.6 %shard_map.104 = (f32[512,768]{1,0:T(8,128)}, f32[8,128]{1,0:T(8,128)S(1)}) custom-call(bf16[128,512]{1,0:T(8,128)(2,1)S(1)} %get-tuple-element.64.refs_0_, bf16[128,768]{1,0:T(8,128)(2,1)S(1)} %get-tuple-element.65.refs_1_, bf16[128,512]{1,0:T(8,128)(2,1)S(1)} %collective-permute-done.17.refs_2_, bf16[128,768]{1,0:T(8,128)(2,1)S(1)} %collective-permute-done.18.refs_3_), custom_call_target="tpu_custom_call" | custom-call | tf_op jit(solution)/shard_map/pallas_call | solution.py:38
  61.4 1.3 %shard_map.105 = (bf16[256,2048]{1,0:T(8,128)(2,1)}, f32[8,128]{1,0:T(8,128)S(1)}) custom-call(bf16[256,64]{1,0:T(8,128)(2,1)S(1)} %get-tuple-element.37.refs_0_, f32[64,128]{1,0:T(8,128)S(1)} %get-tuple-element.38.refs_1_, bf16[16,2048]{1,0:T(8,128)(2,1)S(1)} %get-tuple-element.54.refs_2_, bf16[16,2048]{1,0:T(8,128)(2,1)S(1)} %collective-permute-done.9.refs_4_.refs_3_, ...), custom_call_target="tpu_custom_call" | custom-call | tf_op jit(solution)/shard_map/pallas_call | solution.py:38
  62.7 1.0 %shard_map.106.refs_2_ = bf16[256,2048]{1,0:T(8,128)(2,1)} custom-call(bf16[256,64]{1,0:T(8,128)(2,1)S(1)} %get-tuple-element.37.refs_0_, bf16[32,1024]{1,0:T(8,128)(2,1)S(1)} %get-tuple-element.60.refs_2_.refs_0_.refs_1_, bf16[32,1024]{1,0:T(8,128)(2,1)S(1)} %collective-permute-done.14.refs_1_.refs_2_, ...), custom_call_target="tpu_custom_call" | custom-call | tf_op jit(solution)/shard_map/pallas_call | solution.py:38
  63.8 0.1 collective-permute-done.19.refs_1_
  63.9 1.0 %shard_map.107 = bf16[256,2048]{1,0:T(8,128)(2,1)} custom-call(bf16[256,64]{1,0:T(8,128)(2,1)S(1)} %get-tuple-element.37.refs_0_, bf16[64,1024]{1,0:T(8,128)(2,1)S(1)} %collective-permute-done.19.refs_1_, bf16[256,2048]{1,0:T(8,128)(2,1)} %shard_map.106.refs_2_), custom_call_target="tpu_custom_call", output_to_operand_aliasing={{}: (2, {})} | custom-call | tf_op jit(solution)/shard_map/pallas_call | solution.py:38
  (10 shorter events, 0.1 us)
Async XLA Ops:
  0.6 2.1 %copy-start = (bf16[1,512,1536]{2,1,0:T(8,128)(2,1)S(1)}, bf16[1,512,1536]{2,1,0:T(8,128)(2,1)}, u32[]{:S(2)}) copy-start(bf16[1,512,1536]{2,1,0:T(8,128)(2,1)} %param.12) | copy-start | bytes 4718596
  0.6 20.3 %copy-start.1 = (bf16[1,512,768]{2,1,0:T(8,128)(2,1)S(1)}, bf16[1,512,768]{2,1,0:T(8,128)(2,1)}, u32[]{:S(2)}) copy-start(bf16[1,512,768]{2,1,0:T(8,128)(2,1)} %param.13) | copy-start | bytes 2359300
  2.8 24.2 %collective-permute-start.5 = (bf16[512,1536]{1,0:T(8,128)(2,1)S(1)}, bf16[512,1536]{1,0:T(8,128)(2,1)S(1)}, u32[]{:S(2)}, u32[]{:S(2)}) collective-permute-start(bf16[512,1536]{1,0:T(8,128)(2,1)S(1)} %bitcast.5), channel_id=1, source_target_pairs={{0,1},{1,0},{2,3},{3,2},{4,5},{5,4},{6,7},{7,6},{8,9},{9,8},{10,11... | collective-permute-start | bytes 4718600 | tf_op jit(solution)/shard_map/ppermute | solution.py:255
  3.3 24.3 %collective-permute-start = (bf16[512,768]{1,0:T(8,128)(2,1)}, bf16[512,768]{1,0:T(8,128)(2,1)S(1)}, u32[]{:S(2)}, u32[]{:S(2)}) collective-permute-start(bf16[512,768]{1,0:T(8,128)(2,1)} %bitcast.8), channel_id=1, source_target_pairs={{0,2},{1,3},{2,0},{3,1},{4,6},{5,7},{6,4},{7,5},{8,10},{9,11},{10,... | collective-permute-start | bytes 2359304 | tf_op jit(solution)/shard_map/ppermute | solution.py:259
  5.8 7.5 %collective-permute-start.1 = (bf16[32,2048]{1,0:T(8,128)(2,1)S(1)}, bf16[32,2048]{1,0:T(8,128)(2,1)S(1)}, u32[]{:S(2)}, u32[]{:S(2)}) collective-permute-start(bf16[32,2048]{1,0:T(8,128)(2,1)S(1)} %get-tuple-element.42), channel_id=1, source_target_pairs={{0,4},{4,0},{8,12},{12,8},{1,5},{5,1},{9,13},{13,9},{2,6},{6,2},{1... | collective-permute-start | bytes 393224 | tf_op jit(solution)/shard_map/ppermute | solution.py:265
  7.4 12.9 %collective-permute-start.2 = (bf16[32,2048]{1,0:T(8,128)(2,1)S(1)}, bf16[32,2048]{1,0:T(8,128)(2,1)S(1)}, u32[]{:S(2)}, u32[]{:S(2)}) collective-permute-start(bf16[32,2048]{1,0:T(8,128)(2,1)S(1)} %get-tuple-element.43), channel_id=1, source_target_pairs={{0,8},{4,12},{8,0},{12,4},{1,9},{5,13},{9,1},{13,5},{2,10},{6,14},... | collective-permute-start | bytes 393224 | tf_op jit(solution)/shard_map/ppermute | solution.py:265
  10.0 10.3 %collective-permute-start.3 = (bf16[32,2048]{1,0:T(8,128)(2,1)S(1)}, bf16[32,2048]{1,0:T(8,128)(2,1)S(1)}, u32[]{:S(2)}, u32[]{:S(2)}) collective-permute-start(bf16[32,2048]{1,0:T(8,128)(2,1)S(1)} %get-tuple-element.44), channel_id=1, source_target_pairs={{0,12},{4,8},{8,4},{12,0},{1,13},{5,9},{9,5},{13,1},{2,14},{6,10},... | collective-permute-start | bytes 393224 | tf_op jit(solution)/shard_map/ppermute | solution.py:265
  20.3 6.7 %collective-permute-start.4 = (bf16[64,1024]{1,0:T(8,128)(2,1)S(1)}, bf16[64,1024]{1,0:T(8,128)(2,1)S(1)}, u32[]{:S(2)}, u32[]{:S(2)}) collective-permute-start(bf16[64,1024]{1,0:T(8,128)(2,1)S(1)} %get-tuple-element.46), channel_id=1, source_target_pairs={{0,2},{1,3},{2,0},{3,1},{4,6},{5,7},{6,4},{7,5},{8,10},{9,11},{10,... | collective-permute-start | bytes 393224 | tf_op jit(solution)/shard_map/ppermute | solution.py:259
  20.9 8.6 %collective-permute-start.7 = (bf16[512,768]{1,0:T(8,128)(2,1)S(1)}, bf16[512,768]{1,0:T(8,128)(2,1)S(1)}, u32[]{:S(2)}, u32[]{:S(2)}) collective-permute-start(bf16[512,768]{1,0:T(8,128)(2,1)S(1)} %bitcast.9), channel_id=1, source_target_pairs={{0,1},{1,0},{2,3},{3,2},{4,5},{5,4},{6,7},{7,6},{8,9},{9,8},{10,11... | collective-permute-start | bytes 2359304 | tf_op jit(solution)/shard_map/ppermute | solution.py:255
  27.6 2.4 %collective-permute-start.8 = (bf16[512,768]{1,0:T(8,128)(2,1)S(1)}, bf16[512,768]{1,0:T(8,128)(2,1)S(1)}, u32[]{:S(2)}, u32[]{:S(2)}) collective-permute-start(bf16[512,768]{1,0:T(8,128)(2,1)S(1)} %collective-permute-done.refs_6_.refs_3_), channel_id=1, source_target_pairs={{0,1},{1,0},{2,3},{3,2},{4,5},{5,4},{6,7},{7,6},{8,9},{9,8},{10,11... | collective-permute-start | bytes 2359304 | tf_op jit(solution)/shard_map/ppermute | solution.py:255
  27.7 7.3 %collective-permute-start.6 = (bf16[64,1536]{1,0:T(8,128)(2,1)S(1)}, bf16[64,1536]{1,0:T(8,128)(2,1)S(1)}, u32[]{:S(2)}, u32[]{:S(2)}) collective-permute-start(bf16[64,1536]{1,0:T(8,128)(2,1)S(1)} %get-tuple-element.50), channel_id=1, source_target_pairs={{0,2},{1,3},{2,0},{3,1},{4,6},{5,7},{6,4},{7,5},{8,10},{9,11},{10,... | collective-permute-start | bytes 589832 | tf_op jit(solution)/shard_map/ppermute | solution.py:259
  35.1 10.4 %collective-permute-start.12 = (bf16[64,1536]{1,0:T(8,128)(2,1)S(1)}, bf16[64,1536]{1,0:T(8,128)(2,1)S(1)}, u32[]{:S(2)}, u32[]{:S(2)}) collective-permute-start(bf16[64,1536]{1,0:T(8,128)(2,1)S(1)} %get-tuple-element.59.refs_0_), channel_id=1, source_target_pairs={{0,2},{1,3},{2,0},{3,1},{4,6},{5,7},{6,4},{7,5},{8,10},{9,11},{10,... | collective-permute-start | bytes 589832 | tf_op jit(solution)/shard_map/ppermute | solution.py:259
  38.0 5.0 %collective-permute-start.9 = (bf16[16,2048]{1,0:T(8,128)(2,1)S(1)}, bf16[16,2048]{1,0:T(8,128)(2,1)S(1)}, u32[]{:S(2)}, u32[]{:S(2)}) collective-permute-start(bf16[16,2048]{1,0:T(8,128)(2,1)S(1)} %get-tuple-element.55), channel_id=1, source_target_pairs={{0,4},{4,0},{8,12},{12,8},{1,5},{5,1},{9,13},{13,9},{2,6},{6,2},{1... | collective-permute-start | bytes 196616 | tf_op jit(solution)/shard_map/ppermute | solution.py:265
  39.6 5.9 %collective-permute-start.10 = (bf16[16,2048]{1,0:T(8,128)(2,1)S(1)}, bf16[16,2048]{1,0:T(8,128)(2,1)S(1)}, u32[]{:S(2)}, u32[]{:S(2)}) collective-permute-start(bf16[16,2048]{1,0:T(8,128)(2,1)S(1)} %get-tuple-element.56), channel_id=1, source_target_pairs={{0,8},{4,12},{8,0},{12,4},{1,9},{5,13},{9,1},{13,5},{2,10},{6,14},... | collective-permute-start | bytes 196616 | tf_op jit(solution)/shard_map/ppermute | solution.py:265
  46.7 11.1 %collective-permute-start.13 = (bf16[64,1792]{1,0:T(8,128)(2,1)S(1)}, bf16[64,1792]{1,0:T(8,128)(2,1)S(1)}, u32[]{:S(2)}, u32[]{:S(2)}) collective-permute-start(bf16[64,1792]{1,0:T(8,128)(2,1)S(1)} %shard_map.101), channel_id=1, source_target_pairs={{0,2},{1,3},{2,0},{3,1},{4,6},{5,7},{6,4},{7,5},{8,10},{9,11},{10,... | collective-permute-start | bytes 688136 | tf_op jit(solution)/shard_map/ppermute | solution.py:259
  47.3 6.7 %collective-permute-start.11 = (bf16[16,2048]{1,0:T(8,128)(2,1)S(1)}, bf16[16,2048]{1,0:T(8,128)(2,1)S(1)}, u32[]{:S(2)}, u32[]{:S(2)}) collective-permute-start(bf16[16,2048]{1,0:T(8,128)(2,1)S(1)} %get-tuple-element.57), channel_id=1, source_target_pairs={{0,12},{4,8},{8,4},{12,0},{1,13},{5,9},{9,5},{13,1},{2,14},{6,10},... | collective-permute-start | bytes 196616 | tf_op jit(solution)/shard_map/ppermute | solution.py:265
  49.1 6.2 %collective-permute-start.14 = (bf16[32,1024]{1,0:T(8,128)(2,1)S(1)}, bf16[32,1024]{1,0:T(8,128)(2,1)S(1)}, u32[]{:S(2)}, u32[]{:S(2)}) collective-permute-start(bf16[32,1024]{1,0:T(8,128)(2,1)S(1)} %get-tuple-element.61), channel_id=1, source_target_pairs={{0,4},{4,0},{8,12},{12,8},{1,5},{5,1},{9,13},{13,9},{2,6},{6,2},{1... | collective-permute-start | bytes 196616 | tf_op jit(solution)/shard_map/ppermute | solution.py:265
  49.7 6.2 %collective-permute-start.15 = (bf16[32,1024]{1,0:T(8,128)(2,1)S(1)}, bf16[32,1024]{1,0:T(8,128)(2,1)S(1)}, u32[]{:S(2)}, u32[]{:S(2)}) collective-permute-start(bf16[32,1024]{1,0:T(8,128)(2,1)S(1)} %get-tuple-element.62), channel_id=1, source_target_pairs={{0,8},{4,12},{8,0},{12,4},{1,9},{5,13},{9,1},{13,5},{2,10},{6,14},... | collective-permute-start | bytes 196616 | tf_op jit(solution)/shard_map/ppermute | solution.py:265
  51.7 6.1 %collective-permute-start.16 = (bf16[32,1024]{1,0:T(8,128)(2,1)S(1)}, bf16[32,1024]{1,0:T(8,128)(2,1)S(1)}, u32[]{:S(2)}, u32[]{:S(2)}) collective-permute-start(bf16[32,1024]{1,0:T(8,128)(2,1)S(1)} %get-tuple-element.63), channel_id=1, source_target_pairs={{0,12},{4,8},{8,4},{12,0},{1,13},{5,9},{9,5},{13,1},{2,14},{6,10},... | collective-permute-start | bytes 196616 | tf_op jit(solution)/shard_map/ppermute | solution.py:265
  57.8 2.1 %collective-permute-start.18 = (bf16[128,768]{1,0:T(8,128)(2,1)S(1)}, bf16[128,768]{1,0:T(8,128)(2,1)S(1)}, u32[]{:S(2)}, u32[]{:S(2)}) collective-permute-start(bf16[128,768]{1,0:T(8,128)(2,1)S(1)} %get-tuple-element.65.refs_1_), channel_id=1, source_target_pairs={{0,1},{1,0},{2,3},{3,2},{4,5},{5,4},{6,7},{7,6},{8,9},{9,8},{10,11... | collective-permute-start | bytes 589832 | tf_op jit(solution)/shard_map/ppermute | solution.py:255
  57.9 2.0 %collective-permute-start.17 = (bf16[128,512]{1,0:T(8,128)(2,1)S(1)}, bf16[128,512]{1,0:T(8,128)(2,1)S(1)}, u32[]{:S(2)}, u32[]{:S(2)}) collective-permute-start(bf16[128,512]{1,0:T(8,128)(2,1)S(1)} %get-tuple-element.66), channel_id=1, source_target_pairs={{0,1},{1,0},{2,3},{3,2},{4,5},{5,4},{6,7},{7,6},{8,9},{9,8},{10,11... | collective-permute-start | bytes 393224 | tf_op jit(solution)/shard_map/ppermute | solution.py:255
  58.4 5.5 %collective-permute-start.19 = (bf16[64,1024]{1,0:T(8,128)(2,1)S(1)}, bf16[64,1024]{1,0:T(8,128)(2,1)S(1)}, u32[]{:S(2)}, u32[]{:S(2)}) collective-permute-start(bf16[64,1024]{1,0:T(8,128)(2,1)S(1)} %shard_map.102.refs_3_), channel_id=1, source_target_pairs={{0,2},{1,3},{2,0},{3,1},{4,6},{5,7},{6,4},{7,5},{8,10},{9,11},{10,... | collective-permute-start | bytes 393224 | tf_op jit(solution)/shard_map/ppermute | solution.py:259

commit v6 on v5

--- a/solution.py
+++ b/solution.py
@@ -53,9 +53,10 @@
     return pl.ds(pl.multiple_of((lax.axis_index("fsdp") ^ k) * part, part), part)
 
 
-def slot_kernel(groups, parts, capacity, *refs):
-    sources, chunks, refs = refs[:5], refs[5 : 5 + groups], refs[5 + groups :]
-    turned_out, gate_out, ids, gates, order, tok, cot, sems = refs
+def slot_kernel(groups, spread, capacity, *refs):
+    sources, by_x, refs = refs[:5], refs[5 : 5 + spread], refs[5 + spread :]
+    chunks, (turned_out, gate_out, ids, gates, order, tok, cot, sems) = refs[:groups], refs[groups:]
+    parts = spread * CORES
     copies = [
         pltpu.make_async_copy(source, target, sems.at[i])
         for i, (source, target) in enumerate(zip(sources, (ids, gates, order, tok, cot)))
@@ -87,50 +88,47 @@
     slot_gate = jnp.sum(pick * gate, axis=1, keepdims=True)
     gate_out[...] = jnp.broadcast_to(slot_gate, gate_out.shape)
     pick = pick.astype(BF16)
-    for copy, source, scale, top in ((copies[3], tok, None, 0), (copies[4], cot, slot_gate, capacity)):
-        copy.wait()
-        for k in range(parts):
-            rows = product(pick, source[:, columns(k, part)], 1, 0)
-            rows = (rows if scale is None else scale * rows).astype(BF16)
-            for ke in range(groups):
-                chunks[ke][top : top + capacity, k * part : (k + 1) * part] = rows[
-                    ke * capacity : (ke + 1) * capacity
-                ]
-
-
-def split_kernel(groups, spread, capacity, *refs):
-    chunks, by_x = refs[:groups], refs[groups:]
+    copies[3].wait()
+    for k in range(parts):
+        rows = product(pick, tok[:, columns(k, part)], 1, 0).astype(BF16)
+        by_x[k // CORES][:, (k % CORES) * part : (k % CORES + 1) * part] = rows
+    copies[4].wait()
+    for k in range(parts):
+        grads = product(pick, cot[:, columns(k, part)], 1, 0)
+        grads = (slot_gate * grads).astype(BF16)
+        for ke in range(groups):
+            chunks[ke][:, k * part : (k + 1) * part] = grads[ke * capacity : (ke + 1) * capacity]
+
+
+def join_kernel(groups, spread, capacity, *refs):
+    by_x, riders, chunks = refs[:spread], refs[spread:-groups], refs[-groups:]
     half = by_x[0].shape[1]
+    for ke in range(groups):
+        for kx in range(spread):
+            chunks[ke][:capacity, kx * half : (kx + 1) * half] = by_x[kx][
+                ke * capacity : (ke + 1) * capacity
+            ]
+    for ke, rider in enumerate(riders, 1):
+        chunks[ke][capacity:] = rider[...]
+
+
+def pre_kernel(groups, spread, capacity, *refs):
+    chunks, (own, sib, *outs) = refs[:groups], refs[groups:]
+    part = own.shape[0]
+    half = CORES * part
+    slots = groups * capacity
+    rows = jnp.concatenate(
+        [c[:capacity, kx * half : (kx + 1) * half] for kx in range(spread) for c in chunks], axis=0
+    )
+    total = product(rows[:, :part], own[...], 1, 0) + product(rows[:, part:], sib[...], 1, 0)
     for kx in range(spread):
-        for ke in range(groups):
-            by_x[kx][ke * capacity : (ke + 1) * capacity] = chunks[ke][
-                :capacity, kx * half : (kx + 1) * half
-            ]
-
-
-def far_kernel(groups, spread, capacity, *refs):
-    by_e, by_x = refs[:groups], refs[groups:]
-    for ke in range(groups):
-        for kx in range(1, spread):
-            by_x[kx - 1][ke * capacity : (ke + 1) * capacity] = by_e[ke][
-                kx * capacity : (kx + 1) * capacity
-            ]
-
-
-def pre_kernel(spread, *refs):
-    left, (own, sib, *outs) = refs[:spread], refs[spread:]
-    part = own.shape[0]
-    rows = jnp.concatenate([r[...] for r in left], axis=0)
-    total = product(rows[:, :part], own[...], 1, 0) + product(rows[:, part:], sib[...], 1, 0)
-    count = left[0].shape[0]
-    for kx in range(spread):
-        outs[kx][...] = total[kx * count : (kx + 1) * count].astype(outs[kx].dtype)
+        outs[kx][...] = total[kx * slots : (kx + 1) * slots].astype(outs[kx].dtype)
 
 
 def back_kernel(groups, capacity, *refs):
     chunks, weights, (grads, back) = refs[:groups], refs[groups:-2], refs[-2:]
     part = weights[0].shape[0]
-    grads[...] = jnp.concatenate([c[capacity:] for c in chunks], axis=0)
+    grads[...] = jnp.concatenate([c[-capacity:] for c in chunks], axis=0)
     total = product(grads[:, :part], weights[0][...], 1, 0)
     for k, weight in enumerate(weights[1:], 1):
         total += product(grads[:, k * part : (k + 1) * part], weight[...], 1, 0)
@@ -160,18 +158,15 @@
             chunks[ke][:, k * part : (k + 1) * part] = value[ke * capacity : (ke + 1) * capacity]
 
 
-def d_rows_kernel(groups, spread, capacity, *refs):
-    left, (own, sib, *chunks) = refs[:spread], refs[spread:]
+def d_rows_kernel(spread, *refs):
+    left, (own, sib, *outs) = refs[:spread], refs[spread:]
     part = own.shape[0]
+    count = left[0].shape[0]
     rows = jnp.concatenate([r[...] for r in left], axis=0)
     for kc, weight in enumerate((own, sib)):
         value = product(rows, weight[...], 1, 1).astype(BF16)
-        for ke in range(groups):
-            for kx in range(spread):
-                at = (kx * groups + ke) * capacity
-                chunks[ke][kx * capacity : (kx + 1) * capacity, kc * part : (kc + 1) * part] = value[
-                    at : at + capacity
-                ]
+        for kx in range(spread):
+            outs[kx][:, kc * part : (kc + 1) * part] = value[kx * count : (kx + 1) * count]
 
 
 def pack_kernel(spread, grads, hidden, *outs):
@@ -206,33 +201,16 @@
     copies = []
     for k in range(parts):
         rows = jnp.concatenate([c[:, k * part : (k + 1) * part] for c in chunks], axis=0)
-        weighted = rows.astype(F32) * gate[:, :1]
-        high = weighted.astype(BF16)
-        low = (weighted - high.astype(F32)).astype(BF16)
-        both = jnp.concatenate([high, low], axis=0)
-        held[k] = product(twice, both, 1, 0).astype(BF16)
+        if gate is None:
+            held[k] = product(turned[...], rows, 1, 0).astype(BF16)
+        else:
+            weighted = rows.astype(F32) * gate[:, :1]
+            high = weighted.astype(BF16)
+            low = (weighted - high.astype(F32)).astype(BF16)
+            both = jnp.concatenate([high, low], axis=0)
+            held[k] = product(twice, both, 1, 0).astype(BF16)
         copies.append(pltpu.make_async_copy(held.at[k], out.at[:, columns(k, part)], sems.at[k]))
         copies[-1].start()
-    for copy in copies:
-        copy.wait()
-
-
-def d_tokens_kernel(groups, parts, capacity, span, turned, *refs):
-    *refs, out, held, sems = refs
-    part = out.shape[1] // parts
-    copies = []
-    for n, kx in enumerate(span):
-        for kc in range(CORES):
-            cols = slice(kc * part, (kc + 1) * part)
-            if kx:
-                rows = refs[n][:, cols]
-            else:
-                rows = jnp.concatenate([refs[ke][:capacity, cols] for ke in range(groups)], axis=0)
-            i = len(copies)
-            held[i] = product(turned[...], rows, 1, 0).astype(BF16)
-            target = out.at[:, columns(kx * CORES + kc, part)]
-            copies.append(pltpu.make_async_copy(held.at[i], target, sems.at[i]))
-            copies[-1].start()
     for copy in copies:
         copy.wait()
 
@@ -267,11 +245,11 @@
         ]
 
     chunk = [shape((capacity, width))] * groups
+    by_x = [shape((slots, half))] * spread
     in_own, out_own = w_in[0], w_out[0]
-    *chunks, turned, gate = call(
-        bound(slot_kernel, groups, parts, capacity),
-        [shape((2 * capacity, width))] * groups
-        + [shape((count, slots)), shape((slots, 128), F32)],
+    outs = call(
+        bound(slot_kernel, groups, spread, capacity),
+        by_x + chunk + [shape((count, slots)), shape((slots, 128), F32)],
         (route_ids.T, route_gates.T, served_order, tokens, cotangent),
         far=5,
         scratch_shapes=[
@@ -283,24 +261,29 @@
             pltpu.SemaphoreType.DMA((5,)),
         ],
     )
-    in_own, out_own, chunks[0] = lax.optimization_barrier((in_own, out_own, chunks[0]))
-    chunks = to_expert(chunks)
+    (near, *far), grads, (turned, gate) = outs[:spread], outs[spread:-2], outs[-2:]
+    in_own, out_own, near = lax.optimization_barrier((in_own, out_own, near))
+    in_sib, out_sib = to_core(in_own), to_core(out_own)
     out_far = to_x([out_own] * (spread - 1))
-    in_sib, out_sib = to_core(in_own), to_core(out_own)
-    near, *far = call(
-        bound(split_kernel, groups, spread, capacity), [shape((slots, half))] * spread, chunks
-    )
+    rows = call(
+        bound(join_kernel, groups, spread, capacity),
+        [shape(((1 + (ke == 1)) * capacity, width)) for ke in range(groups)],
+        (near, *to_x(far), grads[1]),
+    )
+    rows = to_expert(rows)
     pre, *pre_far = call(
-        bound(pre_kernel, spread),
+        bound(pre_kernel, groups, spread, capacity),
         [shape((slots, 2 * feed), F32)] + [shape((slots, 2 * feed))] * (spread - 1),
-        (near, *to_x(far), in_own, in_sib),
-    )
-    out_far, pre = lax.optimization_barrier((out_far, pre))
+        (*rows, in_own, in_sib),
+    )
+    out_far, pre, *grads = lax.optimization_barrier((out_far, pre, *grads))
     w_outs = [out_own, out_sib] + [w for value in out_far for w in (value, to_core(value))]
+    grads = to_expert(grads)
+    grads[1] = rows[1]
     grads, back = call(
         bound(back_kernel, groups, capacity),
         [shape((slots, width)), shape((slots, feed), F32)],
-        (*chunks, *w_outs),
+        (*grads, *w_outs),
     )
     hidden, d_pre = call(
         bound(act_kernel, spread),
@@ -310,11 +293,17 @@
     expert_out = to_expert(
         call(bound(expert_out_kernel, groups, capacity), chunk, (hidden, *w_outs))
     )
+    near, *far = call(
+        bound(d_rows_kernel, spread),
+        by_x,
+        (d_pre, *to_x([d_pre] * (spread - 1)), in_own, in_sib),
+        after=expert_out[2:3],
+    )
     d_rows = call(
-        bound(d_rows_kernel, groups, spread, capacity),
-        [shape((spread * capacity, half))] * groups,
-        (d_pre, *to_x([d_pre] * (spread - 1)), in_own, in_sib),
-        after=expert_out[1:3],
+        bound(join_kernel, groups, spread, capacity),
+        chunk,
+        (near, *to_x(far)),
+        after=(expert_out[1], *expert_out[3:]),
     )
     packed = call(
         bound(pack_kernel, spread),
@@ -323,60 +312,39 @@
         after=d_rows[:1],
     )
     d_rows = to_expert(d_rows)
-    far = call(
-        bound(far_kernel, groups, spread, capacity),
-        [shape((slots, half))] * (spread - 1),
-        d_rows,
-        after=expert_out[3:],
-    )
     own, sib, all_hidden = call(
         bound(gather_kernel, spread),
         [shape((spread * slots, part))] * 2 + [shape((spread * slots, feed))],
         (grads, hidden, *to_x(packed)),
-        after=far[:1],
-    )
-    d_w_out, token = call(
+        after=d_rows[1:],
+    )
+    (d_w_out,) = call(
         weight_kernel,
         [shape((part, feed), F32)],
         (own, all_hidden, to_core(sib), to_core(all_hidden)),
-        token=True,
-    )
-
-    def scattered(kernel, pieces, operands, **kw):
-        out, *token = call(
+    )
+
+    def scattered(kernel, operands, **kw):
+        return call(
             kernel,
             [shape((count, width))],
             operands,
             out_specs=[pl.BlockSpec(memory_space=pltpu.HBM)]
             + [pl.BlockSpec(memory_space=pltpu.VMEM)] * kw.get("token", False),
             scratch_shapes=[
-                pltpu.VMEM((pieces, count, part), BF16),
-                pltpu.SemaphoreType.DMA((pieces,)),
+                pltpu.VMEM((parts, count, part), BF16),
+                pltpu.SemaphoreType.DMA((parts,)),
             ],
             **kw,
         )
-        return out, token
 
     combined, token = scattered(
-        bound(combine_kernel, groups, parts),
-        parts,
-        (turned, gate, *expert_out),
+        bound(combine_kernel, groups, parts), (turned, gate, *expert_out), token=True
+    )
+    (d_tokens,) = scattered(
+        lambda turned, *refs: combine_kernel(groups, parts, turned, None, *refs),
+        (turned, *d_rows),
         after=(token,),
-        token=True,
-    )
-    d_tokens, _ = scattered(
-        bound(d_tokens_kernel, groups, parts, capacity, [0]),
-        CORES,
-        (turned, *d_rows),
-        after=token,
-    )
-    far = to_x(far)
-    d_tokens, _ = scattered(
-        bound(d_tokens_kernel, groups, parts, capacity, range(1, spread)),
-        len(far) * CORES,
-        (turned, *far, d_tokens),
-        far=1,
-        input_output_aliases={1 + len(far): 0},
     )
     return combined, d_tokens, d_w_out[None]
 

time: 65 us -> 80 us (1.23)
  waiting for transfers between devices: 28.6 us -> 44.2 us
  Pallas kernels: 10.6 us -> 9.78 us
    ppermute x6, waiting for transfers between devices: 10.5 us -> 21.1 us  [to_x(): lax.ppermute(value, 'fsdp', [(i, i ^ (k + 1) * CORES) for i in range(part...]
    ppermute x9 -> x11, waiting for transfers between devices: 17.7 us -> 23.1 us  [to_expert(): lax.ppermute(value, 'expert', [(i, i ^ ke) for i in range(groups)])]
    ppermute x9 -> x11, starting transfers between devices: 14.8 us -> 17 us  [to_expert(): lax.ppermute(value, 'expert', [(i, i ^ ke) for i in range(groups)])]
    ppermute x6, starting transfers between devices: 8.91 us -> 6.84 us  [to_x(): lax.ppermute(value, 'fsdp', [(i, i ^ (k + 1) * CORES) for i in range(part...]
    pallas_call x14 -> x13, Pallas kernels: 10.6 us -> 9.78 us  [call(): pl.pallas_call(kernel, out_shape=out_shape, in_specs=specs, compiler_para...]
  transfers between devices with their start and end apart: 20 -> 22, of which waited for: 12 -> 9; matrix products, arithmetic and copies ran while one was open for 0% -> 0% of each run, Pallas kernels for 10% -> 6%
where the time goes in v6:
time: 80 us; the launch traced here: 79.8 us
  waiting for transfers between devices  44.2 us (55%)
  starting transfers between devices  25 us (31%)
  Pallas kernels  9.78 us (12%)
  between operations  0.8 us (1%)
    ppermute x11, waiting for transfers between devices, to_expert(): lax.ppermute(value, 'expert', [(i, i ^ ke) for i in range(groups)])  23.1 us
    ppermute x6, waiting for transfers between devices, to_x(): lax.ppermute(value, 'fsdp', [(i, i ^ (k + 1) * CORES) for i in range(part...  21.1 us
    ppermute x11, starting transfers between devices, to_expert(): lax.ppermute(value, 'expert', [(i, i ^ ke) for i in range(groups)])  17 us
    pallas_call x13, Pallas kernels, call(): pl.pallas_call(kernel, out_shape=out_shape, in_specs=specs, compiler_para...  9.78 us
    ppermute x6, starting transfers between devices, to_x(): lax.ppermute(value, 'fsdp', [(i, i ^ (k + 1) * CORES) for i in range(part...  6.84 us
  transfers between devices with their start and end apart: 22, of which 9 were waited for; matrix products, arithmetic and copies ran while one was open for 0% of the time, Pallas kernels for 6%

profile of v6, /device:TPU:0, one launch (start us, length us, event | category | flops | bytes accessed | tf_op | source)
XLA Modules:
  0.0 79.8 jit_solution(4428227280917964504)
XLA Ops:
  0.6 0.0 copy-start.1
  0.7 2.1 %shard_map.94 = (bf16[64,1024]{1,0:T(8,128)(2,1)S(1)}, bf16[64,1024]{1,0:T(8,128)(2,1)S(1)}, bf16[16,2048]{1,0:T(8,128)(2,1)S(1)}, bf16[16,2048]{1,0:T(8,128)(2,...) custom-call(s32[8,256]{1,0:T(8,128)} %bitcast.13, ...), custom_call_target="tpu_custom_call" | custom-call | tf_op jit(solution)/shard_map/pallas_call | solution.py:38
  2.8 0.5 collective-permute-start.5
  3.3 2.6 %collective-permute-start = (bf16[512,768]{1,0:T(8,128)(2,1)}, bf16[512,768]{1,0:T(8,128)(2,1)S(1)}, u32[]{:S(2)}, u32[]{:S(2)}) collective-permute-start(bf16[512,768]{1,0:T(8,128)(2,1)} %bitcast.8), channel_id=1, source_target_pairs={{0,2},{1,3},{2,0},{3,1},{4,6},{5,7},{6,4},{7,5},{8,10},{9,11},{10,... | collective-permute-start | bytes 2359304 | tf_op jit(solution)/shard_map/ppermute | solution.py:237
  5.8 0.1 collective-permute-start.1
  5.9 21.1 %collective-permute-done.1.refs_1_ = bf16[64,1024]{1,0:T(8,128)(2,1)S(1)} collective-permute-done((bf16[64,1024]{1,0:T(8,128)(2,1)S(1)}, bf16[64,1024]{1,0:T(8,128)(2,1)S(1)}, u32[]{:S(2)}, u32[]{:S(2)}) %collective-permute-start.1) | collective-permute-done | bytes 131104 | tf_op jit(solution)/shard_map/ppermute | solution.py:237
  27.0 1.9 %collective-permute-start.2 = (bf16[32,2048]{1,0:T(8,128)(2,1)S(1)}, bf16[32,2048]{1,0:T(8,128)(2,1)S(1)}, u32[]{:S(2)}, u32[]{:S(2)}) collective-permute-start(bf16[32,2048]{1,0:T(8,128)(2,1)S(1)} %get-tuple-element.52), channel_id=1, source_target_pairs={{0,4},{4,0},{8,12},{12,8},{1,5},{5,1},{9,13},{13,9},{2,6},{6,2},{1... | collective-permute-start | bytes 393224 | tf_op jit(solution)/shard_map/ppermute | solution.py:243
  28.9 2.6 %collective-permute-start.3 = (bf16[16,2048]{1,0:T(8,128)(2,1)S(1)}, bf16[16,2048]{1,0:T(8,128)(2,1)S(1)}, u32[]{:S(2)}, u32[]{:S(2)}) collective-permute-start(bf16[16,2048]{1,0:T(8,128)(2,1)S(1)} %get-tuple-element.53), channel_id=1, source_target_pairs={{0,8},{4,12},{8,0},{12,4},{1,9},{5,13},{9,1},{13,5},{2,10},{6,14},... | collective-permute-start | bytes 196616 | tf_op jit(solution)/shard_map/ppermute | solution.py:243
  31.5 0.0 collective-permute-start.4
  31.5 3.8 %collective-permute-done.3.refs_2_ = bf16[16,2048]{1,0:T(8,128)(2,1)S(1)} collective-permute-done((bf16[16,2048]{1,0:T(8,128)(2,1)S(1)}, bf16[16,2048]{1,0:T(8,128)(2,1)S(1)}, u32[]{:S(2)}, u32[]{:S(2)}) %collective-permute-start.3) | collective-permute-done | bytes 65568 | tf_op jit(solution)/shard_map/ppermute | solution.py:243
  35.3 0.0 collective-permute-start.9
  35.3 2.4 %collective-permute-done.4.refs_3_ = bf16[16,2048]{1,0:T(8,128)(2,1)S(1)} collective-permute-done((bf16[16,2048]{1,0:T(8,128)(2,1)S(1)}, bf16[16,2048]{1,0:T(8,128)(2,1)S(1)}, u32[]{:S(2)}, u32[]{:S(2)}) %collective-permute-start.4) | collective-permute-done | bytes 65568 | tf_op jit(solution)/shard_map/ppermute | solution.py:243
  37.6 0.6 shard_map.96
  38.2 0.0 collective-permute-done.refs_6_.refs_3_
  38.2 0.1 collective-permute-start.10
  38.3 1.6 %collective-permute-start.6 = (bf16[64,1536]{1,0:T(8,128)(2,1)S(1)}, bf16[64,1536]{1,0:T(8,128)(2,1)S(1)}, u32[]{:S(2)}, u32[]{:S(2)}) collective-permute-start(bf16[64,1536]{1,0:T(8,128)(2,1)S(1)} %get-tuple-element.61), channel_id=1, source_target_pairs={{0,2},{1,3},{2,0},{3,1},{4,6},{5,7},{6,4},{7,5},{8,10},{9,11},{10,... | collective-permute-start | bytes 589832 | tf_op jit(solution)/shard_map/ppermute | solution.py:237
  39.9 1.4 %collective-permute-start.7 = (bf16[16,2048]{1,0:T(8,128)(2,1)S(1)}, bf16[16,2048]{1,0:T(8,128)(2,1)S(1)}, u32[]{:S(2)}, u32[]{:S(2)}) collective-permute-start(bf16[16,2048]{1,0:T(8,128)(2,1)S(1)} %get-tuple-element.63), channel_id=1, source_target_pairs={{0,8},{4,12},{8,0},{12,4},{1,9},{5,13},{9,1},{13,5},{2,10},{6,14},... | collective-permute-start | bytes 196616 | tf_op jit(solution)/shard_map/ppermute | solution.py:243
  41.2 1.9 %collective-permute-start.8 = (bf16[16,2048]{1,0:T(8,128)(2,1)S(1)}, bf16[16,2048]{1,0:T(8,128)(2,1)S(1)}, u32[]{:S(2)}, u32[]{:S(2)}) collective-permute-start(bf16[16,2048]{1,0:T(8,128)(2,1)S(1)} %get-tuple-element.64), channel_id=1, source_target_pairs={{0,12},{4,8},{8,4},{12,0},{1,13},{5,9},{9,5},{13,1},{2,14},{6,10},... | collective-permute-start | bytes 196616 | tf_op jit(solution)/shard_map/ppermute | solution.py:243
  43.2 0.0 collective-permute-done.9.refs_5_.refs_2_
  43.2 5.0 %collective-permute-done.7.refs_2_ = bf16[16,2048]{1,0:T(8,128)(2,1)S(1)} collective-permute-done((bf16[16,2048]{1,0:T(8,128)(2,1)S(1)}, bf16[16,2048]{1,0:T(8,128)(2,1)S(1)}, u32[]{:S(2)}, u32[]{:S(2)}) %collective-permute-start.7) | collective-permute-done | bytes 65568 | tf_op jit(solution)/shard_map/ppermute | solution.py:243
  48.2 0.0 collective-permute-done.8.refs_3_
  48.2 0.0 collective-permute-done.10.refs_7_.refs_4_
  48.2 0.7 shard_map.97
  48.9 0.0 collective-permute-done.6.refs_1_
  48.9 0.1 shard_map.98
  49.0 0.6 collective-permute-start.14
  49.6 1.1 %shard_map.99 = (bf16[16,2048]{1,0:T(8,128)(2,1)S(1)}, bf16[16,2048]{1,0:T(8,128)(2,1)S(1)}, bf16[16,2048]{1,0:T(8,128)(2,1)S(1)}, bf16[16,2048]{1,0:T(8,128)(2,1)S(1)}) custom-call(bf16[64,768]{1,0:T(8,128)(2,1)S(1)} %get-tuple-element.67.refs_0_.refs_1_, bf16[512,768]{1,0:T(8,128)(2,1)S(1)} %bitcast.11, ...), custom_call_target="tpu_custom_call" | custom-call | tf_op jit(solution)/shard_map/pallas_call | solution.py:38
  50.7 1.8 %collective-permute-start.12 = (bf16[16,2048]{1,0:T(8,128)(2,1)S(1)}, bf16[16,2048]{1,0:T(8,128)(2,1)S(1)}, u32[]{:S(2)}, u32[]{:S(2)}) collective-permute-start(bf16[16,2048]{1,0:T(8,128)(2,1)S(1)} %get-tuple-element.70), channel_id=1, source_target_pairs={{0,8},{4,12},{8,0},{12,4},{1,9},{5,13},{9,1},{13,5},{2,10},{6,14},... | collective-permute-start | bytes 196616 | tf_op jit(solution)/shard_map/ppermute | solution.py:243
  52.4 3.5 %collective-permute-done.12.refs_4_ = bf16[16,2048]{1,0:T(8,128)(2,1)S(1)} collective-permute-done((bf16[16,2048]{1,0:T(8,128)(2,1)S(1)}, bf16[16,2048]{1,0:T(8,128)(2,1)S(1)}, u32[]{:S(2)}, u32[]{:S(2)}) %collective-permute-start.12) | collective-permute-done | bytes 65568 | tf_op jit(solution)/shard_map/ppermute | solution.py:243
  56.0 0.0 collective-permute-done.14.refs_1_
  56.0 1.1 %shard_map.101 = (bf16[64,1024]{1,0:T(8,128)(2,1)S(1)}, bf16[64,1024]{1,0:T(8,128)(2,1)S(1)}) custom-call(bf16[64,1536]{1,0:T(8,128)(2,1)S(1)} %get-tuple-element.73.refs_0_, bf16[64,1536]{1,0:T(8,128)(2,1)S(1)} %collective-permute-done.14.refs_1_, bf16[512,1536]{1,0:T(8,128)(2,1)S(1)} %bitcast.7, ...), custom_call_target="tpu_custom_call" | custom-call | tf_op jit(solution)/shard_map/pallas_call | solution.py:38
  57.1 1.6 %collective-permute-start.15 = (bf16[64,1024]{1,0:T(8,128)(2,1)S(1)}, bf16[64,1024]{1,0:T(8,128)(2,1)S(1)}, u32[]{:S(2)}, u32[]{:S(2)}) collective-permute-start(bf16[64,1024]{1,0:T(8,128)(2,1)S(1)} %get-tuple-element.75), channel_id=1, source_target_pairs={{0,2},{1,3},{2,0},{3,1},{4,6},{5,7},{6,4},{7,5},{8,10},{9,11},{10,... | collective-permute-start | bytes 393224 | tf_op jit(solution)/shard_map/ppermute | solution.py:237
  58.7 1.4 %collective-permute-start.11 = (bf16[16,2048]{1,0:T(8,128)(2,1)S(1)}, bf16[16,2048]{1,0:T(8,128)(2,1)S(1)}, u32[]{:S(2)}, u32[]{:S(2)}) collective-permute-start(bf16[16,2048]{1,0:T(8,128)(2,1)S(1)} %get-tuple-element.69), channel_id=1, source_target_pairs={{0,4},{4,0},{8,12},{12,8},{1,5},{5,1},{9,13},{13,9},{2,6},{6,2},{1... | collective-permute-start | bytes 196616 | tf_op jit(solution)/shard_map/ppermute | solution.py:243
  60.1 1.6 %collective-permute-start.13 = (bf16[16,2048]{1,0:T(8,128)(2,1)S(1)}, bf16[16,2048]{1,0:T(8,128)(2,1)S(1)}, u32[]{:S(2)}, u32[]{:S(2)}) collective-permute-start(bf16[16,2048]{1,0:T(8,128)(2,1)S(1)} %get-tuple-element.71), channel_id=1, source_target_pairs={{0,12},{4,8},{8,4},{12,0},{1,13},{5,9},{9,5},{13,1},{2,14},{6,10},... | collective-permute-start | bytes 196616 | tf_op jit(solution)/shard_map/ppermute | solution.py:243
  61.8 1.8 %collective-permute-done.11.refs_3_.refs_2_ = bf16[16,2048]{1,0:T(8,128)(2,1)S(1)} collective-permute-done((bf16[16,2048]{1,0:T(8,128)(2,1)S(1)}, bf16[16,2048]{1,0:T(8,128)(2,1)S(1)}, u32[]{:S(2)}, u32[]{:S(2)}) %collective-permute-start.11) | collective-permute-done | bytes 65568 | tf_op jit(solution)/shard_map/ppermute | solution.py:243
  63.6 3.0 %collective-permute-done.13.refs_5_.refs_3_ = bf16[16,2048]{1,0:T(8,128)(2,1)S(1)} collective-permute-done((bf16[16,2048]{1,0:T(8,128)(2,1)S(1)}, bf16[16,2048]{1,0:T(8,128)(2,1)S(1)}, u32[]{:S(2)}, u32[]{:S(2)}) %collective-permute-start.13) | collective-permute-done | bytes 65568 | tf_op jit(solution)/shard_map/ppermute | solution.py:243
  66.7 0.5 collective-permute-start.19
  67.1 1.9 %collective-permute-start.17 = (bf16[16,2048]{1,0:T(8,128)(2,1)S(1)}, bf16[16,2048]{1,0:T(8,128)(2,1)S(1)}, u32[]{:S(2)}, u32[]{:S(2)}) collective-permute-start(bf16[16,2048]{1,0:T(8,128)(2,1)S(1)} %get-tuple-element.78), channel_id=1, source_target_pairs={{0,8},{4,12},{8,0},{12,4},{1,9},{5,13},{9,1},{13,5},{2,10},{6,14},... | collective-permute-start | bytes 196616 | tf_op jit(solution)/shard_map/ppermute | solution.py:243
  69.0 2.5 %collective-permute-start.18 = (bf16[16,2048]{1,0:T(8,128)(2,1)S(1)}, bf16[16,2048]{1,0:T(8,128)(2,1)S(1)}, u32[]{:S(2)}, u32[]{:S(2)}) collective-permute-start(bf16[16,2048]{1,0:T(8,128)(2,1)S(1)} %get-tuple-element.79), channel_id=1, source_target_pairs={{0,12},{4,8},{8,4},{12,0},{1,13},{5,9},{9,5},{13,1},{2,14},{6,10},... | collective-permute-start | bytes 196616 | tf_op jit(solution)/shard_map/ppermute | solution.py:243
  71.5 0.8 collective-permute-done.17.refs_3_.refs_4_
  72.3 2.8 %collective-permute-done.18.refs_4_.refs_5_ = bf16[16,2048]{1,0:T(8,128)(2,1)S(1)} collective-permute-done((bf16[16,2048]{1,0:T(8,128)(2,1)S(1)}, bf16[16,2048]{1,0:T(8,128)(2,1)S(1)}, u32[]{:S(2)}, u32[]{:S(2)}) %collective-permute-start.18) | collective-permute-done | bytes 65568 | tf_op jit(solution)/shard_map/ppermute | solution.py:243
  75.1 0.0 collective-permute-done.19.refs_2_
  75.1 0.1 collective-permute-start.21
  75.2 0.5 collective-permute-start.20
  75.7 1.3 %shard_map.100 = (bf16[256,2048]{1,0:T(8,128)(2,1)}, f32[8,128]{1,0:T(8,128)S(1)}) custom-call(bf16[256,64]{1,0:T(8,128)(2,1)S(1)} %get-tuple-element.44.refs_0_, f32[64,128]{1,0:T(8,128)S(1)} %get-tuple-element.45.refs_1_, bf16[16,2048]{1,0:T(8,128)(2,1)S(1)} %get-tuple-element.68.refs_2_, bf16[16,2048]{1,0:T(8,128)(2,1)S(1)} %collective-permute-done.11.refs_3_.refs_2_, ...), custom_call_target="tpu_custom_call" | custom-call | tf_op jit(solution)/shard_map/pallas_call | solution.py:38
  77.0 1.2 %shard_map.103 = bf16[256,2048]{1,0:T(8,128)(2,1)} custom-call(bf16[256,64]{1,0:T(8,128)(2,1)S(1)} %get-tuple-element.44.refs_0_, bf16[16,2048]{1,0:T(8,128)(2,1)S(1)} %get-tuple-element.76.refs_1_.refs_2_, bf16[16,2048]{1,0:T(8,128)(2,1)S(1)} %collective-permute-done.16.refs_2_.refs_3_, bf16[16,2048]{1,0:T(8,128)(2,1)S(1)} %collective-permute-done.17.refs_3_.refs_4_, ...), custom_call_target="tpu_custom_call" | custom-call | tf_op jit(solution)/shard_map/pallas_call | solution.py:38
  78.2 0.0 collective-permute-done.20.refs_2_
  78.3 1.6 %shard_map.106 = f32[512,768]{1,0:T(8,128)} custom-call(bf16[128,512]{1,0:T(8,128)(2,1)S(1)} %get-tuple-element.82.refs_0_, bf16[128,768]{1,0:T(8,128)(2,1)S(1)} %get-tuple-element.83.refs_1_, bf16[128,512]{1,0:T(8,128)(2,1)S(1)} %collective-permute-done.20.refs_2_, bf16[128,768]{1,0:T(8,128)(2,1)S(1)} %collective-permute-done.21.refs_3_), custom_call_target="tpu_custom_call" | custom-call | tf_op jit(solution)/shard_map/pallas_call | solution.py:38
  (13 shorter events, 0.1 us)
Async XLA Ops:
  0.6 2.1 %copy-start = (bf16[1,512,1536]{2,1,0:T(8,128)(2,1)S(1)}, bf16[1,512,1536]{2,1,0:T(8,128)(2,1)}, u32[]{:S(2)}) copy-start(bf16[1,512,1536]{2,1,0:T(8,128)(2,1)} %param.12) | copy-start | bytes 4718596
  0.6 34.6 %copy-start.1 = (bf16[1,512,768]{2,1,0:T(8,128)(2,1)S(1)}, bf16[1,512,768]{2,1,0:T(8,128)(2,1)}, u32[]{:S(2)}) copy-start(bf16[1,512,768]{2,1,0:T(8,128)(2,1)} %param.13) | copy-start | bytes 2359300
  2.8 34.9 %collective-permute-start.5 = (bf16[512,1536]{1,0:T(8,128)(2,1)S(1)}, bf16[512,1536]{1,0:T(8,128)(2,1)S(1)}, u32[]{:S(2)}, u32[]{:S(2)}) collective-permute-start(bf16[512,1536]{1,0:T(8,128)(2,1)S(1)} %bitcast.5), channel_id=1, source_target_pairs={{0,1},{1,0},{2,3},{3,2},{4,5},{5,4},{6,7},{7,6},{8,9},{9,8},{10,11... | collective-permute-start | bytes 4718600 | tf_op jit(solution)/shard_map/ppermute | solution.py:233
  3.3 35.0 %collective-permute-start = (bf16[512,768]{1,0:T(8,128)(2,1)}, bf16[512,768]{1,0:T(8,128)(2,1)S(1)}, u32[]{:S(2)}, u32[]{:S(2)}) collective-permute-start(bf16[512,768]{1,0:T(8,128)(2,1)} %bitcast.8), channel_id=1, source_target_pairs={{0,2},{1,3},{2,0},{3,1},{4,6},{5,7},{6,4},{7,5},{8,10},{9,11},{10,... | collective-permute-start | bytes 2359304 | tf_op jit(solution)/shard_map/ppermute | solution.py:237
  5.8 21.2 %collective-permute-start.1 = (bf16[64,1024]{1,0:T(8,128)(2,1)S(1)}, bf16[64,1024]{1,0:T(8,128)(2,1)S(1)}, u32[]{:S(2)}, u32[]{:S(2)}) collective-permute-start(bf16[64,1024]{1,0:T(8,128)(2,1)S(1)} %get-tuple-element.49), channel_id=1, source_target_pairs={{0,2},{1,3},{2,0},{3,1},{4,6},{5,7},{6,4},{7,5},{8,10},{9,11},{10,... | collective-permute-start | bytes 393224 | tf_op jit(solution)/shard_map/ppermute | solution.py:237
  27.0 10.6 %collective-permute-start.2 = (bf16[32,2048]{1,0:T(8,128)(2,1)S(1)}, bf16[32,2048]{1,0:T(8,128)(2,1)S(1)}, u32[]{:S(2)}, u32[]{:S(2)}) collective-permute-start(bf16[32,2048]{1,0:T(8,128)(2,1)S(1)} %get-tuple-element.52), channel_id=1, source_target_pairs={{0,4},{4,0},{8,12},{12,8},{1,5},{5,1},{9,13},{13,9},{2,6},{6,2},{1... | collective-permute-start | bytes 393224 | tf_op jit(solution)/shard_map/ppermute | solution.py:243
  28.9 6.3 %collective-permute-start.3 = (bf16[16,2048]{1,0:T(8,128)(2,1)S(1)}, bf16[16,2048]{1,0:T(8,128)(2,1)S(1)}, u32[]{:S(2)}, u32[]{:S(2)}) collective-permute-start(bf16[16,2048]{1,0:T(8,128)(2,1)S(1)} %get-tuple-element.53), channel_id=1, source_target_pairs={{0,8},{4,12},{8,0},{12,4},{1,9},{5,13},{9,1},{13,5},{2,10},{6,14},... | collective-permute-start | bytes 196616 | tf_op jit(solution)/shard_map/ppermute | solution.py:243
  31.5 6.1 %collective-permute-start.4 = (bf16[16,2048]{1,0:T(8,128)(2,1)S(1)}, bf16[16,2048]{1,0:T(8,128)(2,1)S(1)}, u32[]{:S(2)}, u32[]{:S(2)}) collective-permute-start(bf16[16,2048]{1,0:T(8,128)(2,1)S(1)} %get-tuple-element.54), channel_id=1, source_target_pairs={{0,12},{4,8},{8,4},{12,0},{1,13},{5,9},{9,5},{13,1},{2,14},{6,10},... | collective-permute-start | bytes 196616 | tf_op jit(solution)/shard_map/ppermute | solution.py:243
  35.3 7.9 %collective-permute-start.9 = (bf16[512,768]{1,0:T(8,128)(2,1)S(1)}, bf16[512,768]{1,0:T(8,128)(2,1)S(1)}, u32[]{:S(2)}, u32[]{:S(2)}) collective-permute-start(bf16[512,768]{1,0:T(8,128)(2,1)S(1)} %bitcast.9), channel_id=1, source_target_pairs={{0,1},{1,0},{2,3},{3,2},{4,5},{5,4},{6,7},{7,6},{8,9},{9,8},{10,11... | collective-permute-start | bytes 2359304 | tf_op jit(solution)/shard_map/ppermute | solution.py:233
  38.2 10.0 %collective-permute-start.10 = (bf16[512,768]{1,0:T(8,128)(2,1)S(1)}, bf16[512,768]{1,0:T(8,128)(2,1)S(1)}, u32[]{:S(2)}, u32[]{:S(2)}) collective-permute-start(bf16[512,768]{1,0:T(8,128)(2,1)S(1)} %collective-permute-done.refs_6_.refs_3_), channel_id=1, source_target_pairs={{0,1},{1,0},{2,3},{3,2},{4,5},{5,4},{6,7},{7,6},{8,9},{9,8},{10,11... | collective-permute-start | bytes 2359304 | tf_op jit(solution)/shard_map/ppermute | solution.py:233
  38.3 10.5 %collective-permute-start.6 = (bf16[64,1536]{1,0:T(8,128)(2,1)S(1)}, bf16[64,1536]{1,0:T(8,128)(2,1)S(1)}, u32[]{:S(2)}, u32[]{:S(2)}) collective-permute-start(bf16[64,1536]{1,0:T(8,128)(2,1)S(1)} %get-tuple-element.61), channel_id=1, source_target_pairs={{0,2},{1,3},{2,0},{3,1},{4,6},{5,7},{6,4},{7,5},{8,10},{9,11},{10,... | collective-permute-start | bytes 589832 | tf_op jit(solution)/shard_map/ppermute | solution.py:237
  39.9 8.3 %collective-permute-start.7 = (bf16[16,2048]{1,0:T(8,128)(2,1)S(1)}, bf16[16,2048]{1,0:T(8,128)(2,1)S(1)}, u32[]{:S(2)}, u32[]{:S(2)}) collective-permute-start(bf16[16,2048]{1,0:T(8,128)(2,1)S(1)} %get-tuple-element.63), channel_id=1, source_target_pairs={{0,8},{4,12},{8,0},{12,4},{1,9},{5,13},{9,1},{13,5},{2,10},{6,14},... | collective-permute-start | bytes 196616 | tf_op jit(solution)/shard_map/ppermute | solution.py:243
  41.2 7.0 %collective-permute-start.8 = (bf16[16,2048]{1,0:T(8,128)(2,1)S(1)}, bf16[16,2048]{1,0:T(8,128)(2,1)S(1)}, u32[]{:S(2)}, u32[]{:S(2)}) collective-permute-start(bf16[16,2048]{1,0:T(8,128)(2,1)S(1)} %get-tuple-element.64), channel_id=1, source_target_pairs={{0,12},{4,8},{8,4},{12,0},{1,13},{5,9},{9,5},{13,1},{2,14},{6,10},... | collective-permute-start | bytes 196616 | tf_op jit(solution)/shard_map/ppermute | solution.py:243
  49.0 7.0 %collective-permute-start.14 = (bf16[64,1536]{1,0:T(8,128)(2,1)S(1)}, bf16[64,1536]{1,0:T(8,128)(2,1)S(1)}, u32[]{:S(2)}, u32[]{:S(2)}) collective-permute-start(bf16[64,1536]{1,0:T(8,128)(2,1)S(1)} %get-tuple-element.73.refs_0_), channel_id=1, source_target_pairs={{0,2},{1,3},{2,0},{3,1},{4,6},{5,7},{6,4},{7,5},{8,10},{9,11},{10,... | collective-permute-start | bytes 589832 | tf_op jit(solution)/shard_map/ppermute | solution.py:237
  50.7 5.3 %collective-permute-start.12 = (bf16[16,2048]{1,0:T(8,128)(2,1)S(1)}, bf16[16,2048]{1,0:T(8,128)(2,1)S(1)}, u32[]{:S(2)}, u32[]{:S(2)}) collective-permute-start(bf16[16,2048]{1,0:T(8,128)(2,1)S(1)} %get-tuple-element.70), channel_id=1, source_target_pairs={{0,8},{4,12},{8,0},{12,4},{1,9},{5,13},{9,1},{13,5},{2,10},{6,14},... | collective-permute-start | bytes 196616 | tf_op jit(solution)/shard_map/ppermute | solution.py:243
  57.1 9.5 %collective-permute-start.15 = (bf16[64,1024]{1,0:T(8,128)(2,1)S(1)}, bf16[64,1024]{1,0:T(8,128)(2,1)S(1)}, u32[]{:S(2)}, u32[]{:S(2)}) collective-permute-start(bf16[64,1024]{1,0:T(8,128)(2,1)S(1)} %get-tuple-element.75), channel_id=1, source_target_pairs={{0,2},{1,3},{2,0},{3,1},{4,6},{5,7},{6,4},{7,5},{8,10},{9,11},{10,... | collective-permute-start | bytes 393224 | tf_op jit(solution)/shard_map/ppermute | solution.py:237
  58.7 4.9 %collective-permute-start.11 = (bf16[16,2048]{1,0:T(8,128)(2,1)S(1)}, bf16[16,2048]{1,0:T(8,128)(2,1)S(1)}, u32[]{:S(2)}, u32[]{:S(2)}) collective-permute-start(bf16[16,2048]{1,0:T(8,128)(2,1)S(1)} %get-tuple-element.69), channel_id=1, source_target_pairs={{0,4},{4,0},{8,12},{12,8},{1,5},{5,1},{9,13},{13,9},{2,6},{6,2},{1... | collective-permute-start | bytes 196616 | tf_op jit(solution)/shard_map/ppermute | solution.py:243
  60.1 6.5 %collective-permute-start.13 = (bf16[16,2048]{1,0:T(8,128)(2,1)S(1)}, bf16[16,2048]{1,0:T(8,128)(2,1)S(1)}, u32[]{:S(2)}, u32[]{:S(2)}) collective-permute-start(bf16[16,2048]{1,0:T(8,128)(2,1)S(1)} %get-tuple-element.71), channel_id=1, source_target_pairs={{0,12},{4,8},{8,4},{12,0},{1,13},{5,9},{9,5},{13,1},{2,14},{6,10},... | collective-permute-start | bytes 196616 | tf_op jit(solution)/shard_map/ppermute | solution.py:243
  66.7 8.4 %collective-permute-start.19 = (bf16[64,1792]{1,0:T(8,128)(2,1)S(1)}, bf16[64,1792]{1,0:T(8,128)(2,1)S(1)}, u32[]{:S(2)}, u32[]{:S(2)}) collective-permute-start(bf16[64,1792]{1,0:T(8,128)(2,1)S(1)} %shard_map.104), channel_id=1, source_target_pairs={{0,2},{1,3},{2,0},{3,1},{4,6},{5,7},{6,4},{7,5},{8,10},{9,11},{10,... | collective-permute-start | bytes 688136 | tf_op jit(solution)/shard_map/ppermute | solution.py:237
  67.1 4.4 %collective-permute-start.16 = (bf16[16,2048]{1,0:T(8,128)(2,1)S(1)}, bf16[16,2048]{1,0:T(8,128)(2,1)S(1)}, u32[]{:S(2)}, u32[]{:S(2)}) collective-permute-start(bf16[16,2048]{1,0:T(8,128)(2,1)S(1)} %get-tuple-element.77), channel_id=1, source_target_pairs={{0,4},{4,0},{8,12},{12,8},{1,5},{5,1},{9,13},{13,9},{2,6},{6,2},{1... | collective-permute-start | bytes 196616 | tf_op jit(solution)/shard_map/ppermute | solution.py:243
  67.1 5.2 %collective-permute-start.17 = (bf16[16,2048]{1,0:T(8,128)(2,1)S(1)}, bf16[16,2048]{1,0:T(8,128)(2,1)S(1)}, u32[]{:S(2)}, u32[]{:S(2)}) collective-permute-start(bf16[16,2048]{1,0:T(8,128)(2,1)S(1)} %get-tuple-element.78), channel_id=1, source_target_pairs={{0,8},{4,12},{8,0},{12,4},{1,9},{5,13},{9,1},{13,5},{2,10},{6,14},... | collective-permute-start | bytes 196616 | tf_op jit(solution)/shard_map/ppermute | solution.py:243
  69.0 6.1 %collective-permute-start.18 = (bf16[16,2048]{1,0:T(8,128)(2,1)S(1)}, bf16[16,2048]{1,0:T(8,128)(2,1)S(1)}, u32[]{:S(2)}, u32[]{:S(2)}) collective-permute-start(bf16[16,2048]{1,0:T(8,128)(2,1)S(1)} %get-tuple-element.79), channel_id=1, source_target_pairs={{0,12},{4,8},{8,4},{12,0},{1,13},{5,9},{9,5},{13,1},{2,14},{6,10},... | collective-permute-start | bytes 196616 | tf_op jit(solution)/shard_map/ppermute | solution.py:243
  75.1 3.1 %collective-permute-start.21 = (bf16[128,768]{1,0:T(8,128)(2,1)S(1)}, bf16[128,768]{1,0:T(8,128)(2,1)S(1)}, u32[]{:S(2)}, u32[]{:S(2)}) collective-permute-start(bf16[128,768]{1,0:T(8,128)(2,1)S(1)} %get-tuple-element.83.refs_1_), channel_id=1, source_target_pairs={{0,1},{1,0},{2,3},{3,2},{4,5},{5,4},{6,7},{7,6},{8,9},{9,8},{10,11... | collective-permute-start | bytes 589832 | tf_op jit(solution)/shard_map/ppermute | solution.py:233
  75.2 3.0 %collective-permute-start.20 = (bf16[128,512]{1,0:T(8,128)(2,1)S(1)}, bf16[128,512]{1,0:T(8,128)(2,1)S(1)}, u32[]{:S(2)}, u32[]{:S(2)}) collective-permute-start(bf16[128,512]{1,0:T(8,128)(2,1)S(1)} %get-tuple-element.84), channel_id=1, source_target_pairs={{0,1},{1,0},{2,3},{3,2},{4,5},{5,4},{6,7},{7,6},{8,9},{9,8},{10,11... | collective-permute-start | bytes 393224 | tf_op jit(solution)/shard_map/ppermute | solution.py:233

commit v7 on v6

v7 whole, which is shorter than its diff:
```python
import jax
import jax.numpy as jnp
from jax import lax
from jax.experimental import pallas as pl
from jax.experimental.pallas import tpu as pltpu
from jax.sharding import PartitionSpec as P

EXPERTS = 128
CORES = 2
PIECES = 3
VMEM = 40 * 1024 * 1024
F32 = jnp.float32
BF16 = jnp.bfloat16


def product(left, right, left_dim, right_dim, **kw):
    return lax.dot_general(
        left, right, (((left_dim,), (right_dim,)), ((), ())), preferred_element_type=F32, **kw
    )


def call(body, out_shape, args, far=0, cost=0, after=(), token=False, **kw):
    out_shape = [*out_shape] + [shape((8, 128), F32)] * token
    specs = [pl.BlockSpec(memory_space=pltpu.VMEM)] * (len(args) - far)
    specs += [pl.BlockSpec(memory_space=pltpu.HBM)] * far
    specs += [pl.BlockSpec(memory_space=pl.ANY)] * len(after)
    kw.setdefault("out_specs", [pl.BlockSpec(memory_space=pltpu.VMEM)] * len(out_shape))
    args = [
        pltpu.with_memory_space_constraint(arg, pltpu.HBM) if i >= len(args) - far else arg
        for i, arg in enumerate(args)
    ]
    count, first, last = len(args), len(args) + len(after), len(args) + len(after) + len(out_shape)

    def kernel(*refs):
        if token:
            refs[last - 1][...] = jnp.zeros(refs[last - 1].shape, F32)
        body(*refs[:count], *refs[first : last - token], *refs[last:])

    return pl.pallas_call(
        kernel,
        out_shape=out_shape,
        in_specs=specs,
        compiler_params=pltpu.CompilerParams(vmem_limit_bytes=VMEM),
        cost_estimate=pl.CostEstimate(flops=cost, bytes_accessed=0, transcendentals=0),
        **kw,
    )(*args, *after)


def shape(dims, kind=BF16):
    return jax.ShapeDtypeStruct(dims, kind)


def columns(k, part):
    return pl.ds(pl.multiple_of((lax.axis_index("fsdp") ^ k) * part, part), part)


def slot_kernel(groups, parts, capacity, *refs):
    sources, chunks, refs = refs[:5], refs[5 : 5 + groups], refs[5 + groups :]
    turned_out, gate_out, ids, gates, order, tok, cot, sems = refs
    copies = [
        pltpu.make_async_copy(source, target, sems.at[i])
        for i, (source, target) in enumerate(zip(sources, (ids, gates, order, tok, cot)))
    ]
    for copy in copies:
        copy.start()
    for copy in copies[:3]:
        copy.wait()
    choices, count = ids.shape
    slots = groups * capacity
    part = tok.shape[1] // parts
    slot = lax.broadcasted_iota(jnp.int32, (slots, count), 0)
    wanted = ((slot // capacity) ^ lax.axis_index("expert")) * (EXPERTS // groups)
    routed = jnp.zeros((slots, count), F32)
    gate = jnp.zeros((slots, count), F32)
    for k in range(choices):
        hit = ids[k : k + 1, :] == wanted
        routed = jnp.where(hit, 1.0, routed)
        gate = jnp.where(hit, gates[k : k + 1, :], gate)
    row = lax.broadcasted_iota(jnp.int32, (count, count), 0)
    col = lax.broadcasted_iota(jnp.int32, (count, count), 1)
    served = jnp.where(order[...] == row, 1.0, 0.0).astype(BF16)
    earlier = jnp.where(row < col, 1.0, 0.0).astype(BF16)
    by_rank = product(routed.astype(BF16), served, 1, 0)
    before = product(by_rank.astype(BF16), earlier, 1, 0)
    taken = jnp.where(before.astype(jnp.int32) == slot % capacity, by_rank, 0.0).astype(BF16)
    pick = product(taken, served, 1, 1)
    turned_out[...] = product(served, taken, 1, 1).astype(BF16)
    slot_gate = jnp.sum(pick * gate, axis=1, keepdims=True)
    gate_out[...] = jnp.broadcast_to(slot_gate, gate_out.shape)
    pick = pick.astype(BF16)
    for copy, source, scale, top in ((copies[3], tok, None, 0), (copies[4], cot, slot_gate, capacity)):
        copy.wait()
        for k in range(parts):
            rows = product(pick, source[:, columns(k, part)], 1, 0)
            rows = (rows if scale is None else scale * rows).astype(BF16)
            for ke in range(groups):
                chunks[ke][top : top + capacity, k * part : (k + 1) * part] = rows[
                    ke * capacity : (ke + 1) * capacity
                ]


def piece_columns(n, s, width, replicas):
    at = ((lax.axis_index("replica") ^ n) * PIECES + s) * width
    return pl.ds(pl.multiple_of(at, 128), width)


def piece_kernel(replicas, w_in, *refs):
    *outs, sems = refs
    copies = []
    for s, out in enumerate(outs):
        cols = piece_columns(0, s, out.shape[1], replicas)
        copies.append(pltpu.make_async_copy(w_in.at[:, cols], out, sems.at[s]))
        copies[-1].start()
    for copy in copies:
        copy.wait()


def near_kernel(groups, spread, capacity, *refs):
    chunks, (own, sib, rows, pre, *grads) = refs[:groups], refs[groups:]
    part = own.shape[0]
    half = CORES * part
    rows[...] = jnp.concatenate([c[:capacity] for c in chunks], axis=0)
    for kx in range(spread):
        cols = slice(kx * half, (kx + 1) * half)
        grads[kx][...] = jnp.concatenate([c[capacity:, cols] for c in chunks], axis=0)
    total = product(rows[:, :part], own[...], 1, 0)
    pre[...] = total + product(rows[:, part : 2 * part], sib[...], 1, 0)


def back_kernel(spread, *refs):
    left, (own, sib, *outs) = refs[:spread], refs[spread:]
    part = own.shape[0]
    count = left[0].shape[0]
    rows = jnp.concatenate([r[...] for r in left], axis=0)
    total = product(rows[:, :part], own[...], 1, 0) + product(rows[:, part:], sib[...], 1, 0)
    for kx in range(spread):
        outs[kx][...] = total[kx * count : (kx + 1) * count].astype(outs[kx].dtype)


def hidden_kernel(replicas, rows, pre_in, *refs):
    pieces, (hidden, pre) = refs[:-2], refs[-2:]
    part, width = pieces[0].shape
    feed = hidden.shape[1]
    each = PIECES * replicas
    pre[...] = pre_in[...]
    for i in range(each):
        total = 0.0
        for k, piece in enumerate(pieces[i::each], CORES):
            total += product(rows[:, k * part : (k + 1) * part], piece[...], 1, 0)
        pre[:, piece_columns(i // PIECES, i % PIECES, width, replicas)] += total
    gate_act, up_act = pre[:, :feed], pre[:, feed:]
    hidden[...] = (gate_act * (1.0 / (1.0 + jnp.exp(-gate_act))) * up_act).astype(BF16)


def d_rows_kernel(groups, spread, capacity, replicas, pre, *refs):
    backs, (own, sib), refs = refs[:spread], refs[spread : spread + 2], refs[spread + 2 :]
    pieces, chunks, d_pre = refs[: -groups - 1], refs[-groups - 1 : -1], refs[-1]
    part = own.shape[0]
    width = pieces[0].shape[1]
    each = PIECES * replicas
    back = backs[0][...]
    for ref in backs[1:]:
        back += ref[...].astype(F32)
    feed = back.shape[1]
    gate_act, up_act = pre[:, :feed], pre[:, feed:]
    sig = 1.0 / (1.0 + jnp.exp(-gate_act))
    d_pre[:, :feed] = (back * up_act * (sig * (1.0 + gate_act * (1.0 - sig)))).astype(BF16)
    d_pre[:, feed:] = (back * (gate_act * sig)).astype(BF16)

    def store(k, value):
        value = value.astype(BF16)
        for ke in range(groups):
            chunks[ke][:, k * part : (k + 1) * part] = value[ke * capacity : (ke + 1) * capacity]

    store(0, product(d_pre[...], own[...], 1, 1))
    store(1, product(d_pre[...], sib[...], 1, 1))
    for k in range(len(pieces) // each):
        total = 0.0
        for i, piece in enumerate(pieces[k * each : (k + 1) * each]):
            cols = piece_columns(i // PIECES, i % PIECES, width, replicas)
            total += product(d_pre[:, cols], piece[...], 1, 1)
        store(CORES + k, total)


def expert_out_kernel(spread, *refs):
    left, (own, sib, *outs) = refs[:spread], refs[spread:]
    part = own.shape[0]
    count = left[0].shape[0]
    rows = jnp.concatenate([r[...] for r in left], axis=0)
    for kc, weight in enumerate((own, sib)):
        value = product(rows, weight[...], 1, 1).astype(BF16)
        for kx in range(spread):
            outs[kx][:, kc * part : (kc + 1) * part] = value[kx * count : (kx + 1) * count]


def join_kernel(groups, spread, capacity, *refs):
    by_x, chunks = refs[:spread], refs[spread:]
    half = by_x[0].shape[1]
    for ke in range(groups):
        for kx in range(spread):
            chunks[ke][:, kx * half : (kx + 1) * half] = by_x[kx][
                ke * capacity : (ke + 1) * capacity
            ]


def gather_kernel(spread, *refs):
    grads, hidden, (own, sib, all_hidden) = refs[:spread], refs[spread : 2 * spread], refs[2 * spread :]
    part = own.shape[1]
    count = grads[0].shape[0]
    for kx in range(spread):
        at = pl.ds(kx * count, count)
        own[at] = grads[kx][:, :part]
        sib[at] = grads[kx][:, part:]
        all_hidden[at] = hidden[kx][...]


def weight_kernel(own, hidden, sib, sib_hidden, out):
    left = jnp.concatenate([own[...], sib[...]], axis=0)
    right = jnp.concatenate([hidden[...], sib_hidden[...]], axis=0)
    out[...] = product(left, right, 0, 0)


def combine_kernel(groups, parts, turned, gate, *refs):
    chunks, (out, held, sems) = refs[:groups], refs[groups:]
    part = out.shape[1] // parts
    twice = jnp.concatenate([turned[...], turned[...]], axis=1)
    copies = []
    for k in range(parts):
        rows = jnp.concatenate([c[:, k * part : (k + 1) * part] for c in chunks], axis=0)
        if gate is None:
            held[k] = product(turned[...], rows, 1, 0).astype(BF16)
        else:
            weighted = rows.astype(F32) * gate[:, :1]
            high = weighted.astype(BF16)
            low = (weighted - high.astype(F32)).astype(BF16)
            both = jnp.concatenate([high, low], axis=0)
            held[k] = product(twice, both, 1, 0).astype(BF16)
        copies.append(pltpu.make_async_copy(held.at[k], out.at[:, columns(k, part)], sems.at[k]))
        copies[-1].start()
    for copy in copies:
        copy.wait()


def per_device(tokens, cotangent, route_ids, route_gates, served_order, w_in, w_out):
    replicas = lax.axis_size("replica")
    groups = lax.axis_size("expert")
    parts = lax.axis_size("fsdp")
    spread = parts // CORES
    count, width = tokens.shape
    capacity = count * route_ids.shape[1] // EXPERTS
    feed = w_out.shape[2]
    slots = groups * capacity
    half = width // spread
    part = width // parts

    def bound(kernel, *sizes):
        return lambda *refs: kernel(*sizes, *refs)

    def to_core(value):
        return lax.ppermute(value, "fsdp", [(i, i ^ 1) for i in range(parts)])

    def to_x(values):
        return [
            lax.ppermute(value, "fsdp", [(i, i ^ ((k + 1) * CORES)) for i in range(parts)])
            for k, value in enumerate(values)
        ]

    def to_replica(value, n):
        return lax.ppermute(value, "replica", [(i, i ^ n) for i in range(replicas)])

    def to_expert(chunks):
        return [
            lax.ppermute(value, "expert", [(i, i ^ ke) for i in range(groups)]) if ke else value
            for ke, value in enumerate(chunks)
        ]

    chunk = [shape((capacity, width))] * groups
    by_x = [shape((slots, half))] * spread
    in_own, out_own = w_in[0], w_out[0]
    pieces = call(
        bound(piece_kernel, replicas),
        [shape((part, 2 * feed // (replicas * PIECES)))] * PIECES,
        (in_own,),
        far=1,
        scratch_shapes=[pltpu.SemaphoreType.DMA((PIECES,))],
    )
    *chunks, turned, gate = call(
        bound(slot_kernel, groups, parts, capacity),
        [shape((2 * capacity, width))] * groups
        + [shape((count, slots)), shape((slots, 128), F32)],
        (route_ids.T, route_gates.T, served_order, tokens, cotangent),
        far=5,
        after=pieces[:1],
        scratch_shapes=[
            pltpu.VMEM(route_ids.shape[::-1], jnp.int32),
            pltpu.VMEM(route_gates.shape[::-1], F32),
            pltpu.VMEM(served_order.shape, jnp.int32),
            pltpu.VMEM(tokens.shape, BF16),
            pltpu.VMEM(cotangent.shape, BF16),
            pltpu.SemaphoreType.DMA((5,)),
        ],
    )
    in_sib, out_sib = to_core(in_own), to_core(out_own)
    *chunks, in_sib, out_sib = lax.optimization_barrier((*chunks, in_sib, out_sib))
    chunks = to_expert(chunks)
    shares = [to_x([piece] * (spread - 1)) for piece in pieces]
    shares = [lax.optimization_barrier((vs, chunks[1 + i]))[0] for i, vs in enumerate(shares)]
    shares = [[[v] + [to_replica(v, n) for n in range(1, replicas)] for v in vs] for vs in shares]
    early = shares[0][0][1:]
    rows, pre, *grads = call(
        bound(near_kernel, groups, spread, capacity),
        [shape((slots, width)), shape((slots, 2 * feed), F32)] + by_x,
        (*chunks, in_own, in_sib),
        after=early,
    )
    grads[1:] = to_x(grads[1:])
    back, *back_far = call(
        bound(back_kernel, spread),
        [shape((slots, feed), F32)] + [shape((slots, feed))] * (spread - 1),
        (*grads, out_own, out_sib),
    )
    backs = (back, *to_x(back_far))
    shares[-1], back = lax.optimization_barrier((shares[-1], back))
    pieces = []
    for kx in range(spread - 1):
        here = [shares[s][kx][n] for n in range(replicas) for s in range(PIECES)]
        pieces += here + [to_core(value) for value in here]
    hidden, pre = call(
        bound(hidden_kernel, replicas),
        [shape((slots, feed)), shape((slots, 2 * feed), F32)],
        (rows, pre, *pieces),
    )
    hidden = (hidden, *to_x([hidden] * (spread - 1)))
    d_rows = call(
        bound(d_rows_kernel, groups, spread, capacity, replicas),
        chunk,
        (pre, *backs, in_own, in_sib, *pieces),
        scratch_shapes=[pltpu.VMEM((slots, 2 * feed), BF16)],
    )
    d_rows = to_expert(d_rows)
    near, *far = call(bound(expert_out_kernel, spread), by_x, (*hidden, out_own, out_sib))
    expert_out = call(
        bound(join_kernel, groups, spread, capacity), chunk, (near, *to_x(far))
    )
    expert_out = to_expert(expert_out)
    own, sib, all_hidden = call(
        bound(gather_kernel, spread),
        [shape((spread * slots, part))] * 2 + [shape((spread * slots, feed))],
        (*grads, *hidden),
    )
    d_w_out, token = call(
        weight_kernel,
        [shape((part, feed), F32)],
        (own, all_hidden, to_core(sib), to_core(all_hidden)),
        token=True,
    )

    def scattered(kernel, operands, **kw):
        return call(
            kernel,
            [shape((count, width))],
            operands,
            out_specs=[pl.BlockSpec(memory_space=pltpu.HBM)]
            + [pl.BlockSpec(memory_space=pltpu.VMEM)] * kw.get("token", False),
            scratch_shapes=[
                pltpu.VMEM((parts, count, part), BF16),
                pltpu.SemaphoreType.DMA((parts,)),
            ],
            **kw,
        )

    d_tokens, token = scattered(
        lambda turned, *refs: combine_kernel(groups, parts, turned, None, *refs),
        (turned, *d_rows),
        after=(token,),
        token=True,
    )
    (combined,) = scattered(
        bound(combine_kernel, groups, parts), (turned, gate, *expert_out), after=(token,)
    )
    return combined, d_tokens, d_w_out[None]


def solution(mesh):
    rows = P(("replica", "expert", "fsdp"), None)
    weights = P("expert", "fsdp", None)
    return jax.shard_map(
        per_device,
        mesh=mesh,
        in_specs=(rows,) * 5 + (weights,) * 2,
        out_specs=(rows, rows, P(("replica", "expert"), "fsdp", None)),
        check_vma=False,
    )
```

time: 80 us -> 65 us (0.81)
  waiting for transfers between devices: 44.2 us -> 19.8 us
  starting transfers between devices: 25 us -> 32.7 us
  Pallas kernels: 9.78 us -> 11.6 us
    ppermute x11 -> x9, waiting for transfers between devices: 23.1 us -> 7.05 us  [to_expert(): lax.ppermute(value, 'expert', [(i, i ^ ke) for i in range(groups)])]
    ppermute x6 -> x7, waiting for transfers between devices: 21.1 us -> 6.33 us  [to_x(): lax.ppermute(value, 'fsdp', [(i, i ^ (k + 1) * CORES) for i in range(part...]
    ppermute x0 -> x3, waiting for transfers between devices: none -> 5.03 us  [to_replica(): return lax.ppermute(value, 'replica', [(i, i ^ n) for i in range(replicas)])]
    ppermute x6 -> x7, starting transfers between devices: 6.84 us -> 11 us  [to_x(): lax.ppermute(value, 'fsdp', [(i, i ^ (k + 1) * CORES) for i in range(part...]
    ppermute x0 -> x3, starting transfers between devices: none -> 3.55 us  [to_replica(): return lax.ppermute(value, 'replica', [(i, i ^ n) for i in range(replicas)])]
    pallas_call x13 -> x12, Pallas kernels: 9.78 us -> 11.6 us  [call(): pl.pallas_call(kernel, out_shape=out_shape, in_specs=specs, compiler_para...]
    ppermute x5 -> x10, waiting for transfers between devices: 0.01 us -> 1.4 us  [to_core(): return lax.ppermute(value, 'fsdp', [(i, i ^ 1) for i in range(parts)])]
    ppermute x11 -> x9, starting transfers between devices: 17 us -> 16.7 us  [to_expert(): lax.ppermute(value, 'expert', [(i, i ^ ke) for i in range(groups)])]
  transfers between devices with their start and end apart: 22 -> 29, of which waited for: 9 -> 11; matrix products, arithmetic and copies ran while one was open for 0% -> 0% of each run, Pallas kernels for 6% -> 15%
where the time goes in v7:
time: 65 us; the launch traced here: 64.8 us
  starting transfers between devices  32.7 us (50%)
  waiting for transfers between devices  19.8 us (30%)
  Pallas kernels  11.6 us (18%)
  between operations  0.76 us (1%)
    ppermute x9, starting transfers between devices, to_expert(): lax.ppermute(value, 'expert', [(i, i ^ ke) for i in range(groups)])  16.7 us
    pallas_call x12, Pallas kernels, call(): pl.pallas_call(kernel, out_shape=out_shape, in_specs=specs, compiler_para...  11.6 us
    ppermute x7, starting transfers between devices, to_x(): lax.ppermute(value, 'fsdp', [(i, i ^ (k + 1) * CORES) for i in range(part...  11 us
    ppermute x9, waiting for transfers between devices, to_expert(): lax.ppermute(value, 'expert', [(i, i ^ ke) for i in range(groups)])  7.05 us
    ppermute x7, waiting for transfers between devices, to_x(): lax.ppermute(value, 'fsdp', [(i, i ^ (k + 1) * CORES) for i in range(part...  6.33 us
    ppermute x3, waiting for transfers between devices, to_replica(): return lax.ppermute(value, 'replica', [(i, i ^ n) for i in range(replicas)])  5.03 us
    ppermute x3, starting transfers between devices, to_replica(): return lax.ppermute(value, 'replica', [(i, i ^ n) for i in range(replicas)])  3.55 us
    ppermute x10, starting transfers between devices, to_core(): return lax.ppermute(value, 'fsdp', [(i, i ^ 1) for i in range(parts)])  1.41 us
  transfers between devices with their start and end apart: 29, of which 11 were waited for; matrix products, arithmetic and copies ran while one was open for 0% of the time, Pallas kernels for 15%

profile of v7, /device:TPU:0, one launch (start us, length us, event | category | flops | bytes accessed | tf_op | source)
XLA Modules:
  0.0 64.8 jit_solution(8750406004947506796)
XLA Ops:
  0.6 0.5 collective-permute-start
  1.1 0.1 collective-permute-start.1
  1.2 1.1 %shard_map.94 = (bf16[512,256]{1,0:T(8,128)(2,1)S(1)}, bf16[512,256]{1,0:T(8,128)(2,1)S(1)}, bf16[512,256]{1,0:T(8,128)(2,1)S(1)}) custom-call(bf16[512,1536]{1,0:T(8,128)(2,1)} %bitcast.6), custom_call_target="tpu_custom_call" | custom-call | tf_op jit(solution)/shard_map/pallas_call | solution.py:39
  2.4 0.0 copy-start
  2.4 3.0 %collective-permute-start.5 = (bf16[512,256]{1,0:T(8,128)(2,1)S(1)}, bf16[512,256]{1,0:T(8,128)(2,1)S(1)}, u32[]{:S(2)}, u32[]{:S(2)}) collective-permute-start(bf16[512,256]{1,0:T(8,128)(2,1)S(1)} %get-tuple-element.48.refs_5_), channel_id=1, source_target_pairs={{0,2},{1,3},{2,0},{3,1},{4,6},{5,7},{6,4},{7,5},{8,10},{9,11},{10,... | collective-permute-start | bytes 786440 | tf_op jit(solution)/shard_map/ppermute | solution.py:264
  5.4 1.9 %shard_map.95 = (bf16[32,2048]{1,0:T(8,128)(2,1)S(1)}, bf16[32,2048]{1,0:T(8,128)(2,1)S(1)}, bf16[32,2048]{1,0:T(8,128)(2,1)S(1)}, bf16[32,2048]{1,0:T(8,128)(2,...) custom-call(s32[8,256]{1,0:T(8,128)} %bitcast.12, f32[8,256]{1,0:T(8,128)} %bitcast.13, s32[1,256]{1,0:T(1,128)} %refs_2_.1, ...), custom_call_target="tpu_custom_call" | custom-call | tf_op jit(solution)/shard_map/pallas_call | solution.py:39
  7.3 1.6 %collective-permute-start.2 = (bf16[32,2048]{1,0:T(8,128)(2,1)S(1)}, bf16[32,2048]{1,0:T(8,128)(2,1)S(1)}, u32[]{:S(2)}, u32[]{:S(2)}) collective-permute-start(bf16[32,2048]{1,0:T(8,128)(2,1)S(1)} %get-tuple-element.56), channel_id=1, source_target_pairs={{0,4},{4,0},{8,12},{12,8},{1,5},{5,1},{9,13},{13,9},{2,6},{6,2},{1... | collective-permute-start | bytes 393224 | tf_op jit(solution)/shard_map/ppermute | solution.py:273
  9.0 1.0 %collective-permute-start.7 = (bf16[512,256]{1,0:T(8,128)(2,1)S(1)}, bf16[512,256]{1,0:T(8,128)(2,1)S(1)}, u32[]{:S(2)}, u32[]{:S(2)}) collective-permute-start(bf16[512,256]{1,0:T(8,128)(2,1)S(1)} %get-tuple-element.63), channel_id=1, source_target_pairs={{0,2},{1,3},{2,0},{3,1},{4,6},{5,7},{6,4},{7,5},{8,10},{9,11},{10,... | collective-permute-start | bytes 786440 | tf_op jit(solution)/shard_map/ppermute | solution.py:264
  10.0 1.0 %collective-permute-start.8 = (bf16[512,256]{1,0:T(8,128)(2,1)S(1)}, bf16[512,256]{1,0:T(8,128)(2,1)S(1)}, u32[]{:S(2)}, u32[]{:S(2)}) collective-permute-start(bf16[512,256]{1,0:T(8,128)(2,1)S(1)} %get-tuple-element.65), channel_id=1, source_target_pairs={{0,2},{1,3},{2,0},{3,1},{4,6},{5,7},{6,4},{7,5},{8,10},{9,11},{10,... | collective-permute-start | bytes 786440 | tf_op jit(solution)/shard_map/ppermute | solution.py:264
  11.0 2.6 %collective-permute-start.3 = (bf16[32,2048]{1,0:T(8,128)(2,1)S(1)}, bf16[32,2048]{1,0:T(8,128)(2,1)S(1)}, u32[]{:S(2)}, u32[]{:S(2)}) collective-permute-start(bf16[32,2048]{1,0:T(8,128)(2,1)S(1)} %get-tuple-element.57), channel_id=1, source_target_pairs={{0,8},{4,12},{8,0},{12,4},{1,9},{5,13},{9,1},{13,5},{2,10},{6,14},... | collective-permute-start | bytes 393224 | tf_op jit(solution)/shard_map/ppermute | solution.py:273
  13.6 1.5 %collective-permute-start.6 = (bf16[512,256]{1,0:T(8,128)(2,1)S(1)}, bf16[512,256]{1,0:T(8,128)(2,1)S(1)}, u32[]{:S(2)}, u32[]{:S(2)}) collective-permute-start(bf16[512,256]{1,0:T(8,128)(2,1)S(1)} %collective-permute-done.5.refs_2_.refs_5_), channel_id=1, source_target_pairs={{0,16},{16,0},{1,17},{17,1},{2,18},{18,2},{3,19},{19,3},{4,20},{20... | collective-permute-start | bytes 786440 | tf_op jit(solution)/shard_map/ppermute | solution.py:269
  15.1 3.7 %collective-permute-start.4 = (bf16[32,2048]{1,0:T(8,128)(2,1)S(1)}, bf16[32,2048]{1,0:T(8,128)(2,1)S(1)}, u32[]{:S(2)}, u32[]{:S(2)}) collective-permute-start(bf16[32,2048]{1,0:T(8,128)(2,1)S(1)} %get-tuple-element.58), channel_id=1, source_target_pairs={{0,12},{4,8},{8,4},{12,0},{1,13},{5,9},{9,5},{13,1},{2,14},{6,10},... | collective-permute-start | bytes 393224 | tf_op jit(solution)/shard_map/ppermute | solution.py:273
  18.8 4.1 %collective-permute-done.3.refs_2_ = bf16[32,2048]{1,0:T(8,128)(2,1)S(1)} collective-permute-done((bf16[32,2048]{1,0:T(8,128)(2,1)S(1)}, bf16[32,2048]{1,0:T(8,128)(2,1)S(1)}, u32[]{:S(2)}, u32[]{:S(2)}) %collective-permute-start.3) | collective-permute-done | bytes 131104 | tf_op jit(solution)/shard_map/ppermute | solution.py:273
  22.9 1.5 %collective-permute-start.11 = (bf16[512,256]{1,0:T(8,128)(2,1)S(1)}, bf16[512,256]{1,0:T(8,128)(2,1)S(1)}, u32[]{:S(2)}, u32[]{:S(2)}) collective-permute-start(bf16[512,256]{1,0:T(8,128)(2,1)S(1)} %collective-permute-done.7.refs_3_.refs_6_), channel_id=1, source_target_pairs={{0,16},{16,0},{1,17},{17,1},{2,18},{18,2},{3,19},{19,3},{4,20},{20... | collective-permute-start | bytes 786440 | tf_op jit(solution)/shard_map/ppermute | solution.py:269
  24.5 0.5 collective-permute-start.9
  25.0 0.0 collective-permute-start.13
  25.0 0.0 collective-permute-done.6.refs_6_.refs_5_.refs_8_
  25.0 0.7 %shard_map.96 = (bf16[64,2048]{1,0:T(8,128)(2,1)S(1)}, f32[64,1536]{1,0:T(8,128)S(1)}, bf16[64,1024]{1,0:T(8,128)(2,1)S(1)}, bf16[64,1024]{1,0:T(8,128)(2,1)S(1)}) custom-call(bf16[32,2048]{1,0:T(8,128)(2,1)S(1)} %get-tuple-element.55.refs_0_, bf16[32,2048]{1,0:T(8,128)(2,1)S(1)} %collective-permute-done.2.refs_1_, ...), custom_call_target="tpu_custom_call" | custom-call | tf_op jit(solution)/shard_map/pallas_call | solution.py:39
  25.6 1.5 %collective-permute-start.10 = (bf16[64,1024]{1,0:T(8,128)(2,1)S(1)}, bf16[64,1024]{1,0:T(8,128)(2,1)S(1)}, u32[]{:S(2)}, u32[]{:S(2)}) collective-permute-start(bf16[64,1024]{1,0:T(8,128)(2,1)S(1)} %get-tuple-element.68), channel_id=1, source_target_pairs={{0,2},{1,3},{2,0},{3,1},{4,6},{5,7},{6,4},{7,5},{8,10},{9,11},{10,... | collective-permute-start | bytes 393224 | tf_op jit(solution)/shard_map/ppermute | solution.py:264
  27.2 0.2 collective-permute-start.12
  27.4 3.4 %collective-permute-done.11.refs_6_.refs_9_ = bf16[512,256]{1,0:T(8,128)(2,1)S(1)} collective-permute-done((bf16[512,256]{1,0:T(8,128)(2,1)S(1)}, bf16[512,256]{1,0:T(8,128)(2,1)S(1)}, u32[]{:S(2)}, u32[]{:S(2)}) %collective-permute-start.11) | collective-permute-done | bytes 262176 | tf_op jit(solution)/shard_map/ppermute | solution.py:269
  30.8 0.0 collective-permute-start.15
  30.8 0.8 %collective-permute-done.10.refs_1_ = bf16[64,1024]{1,0:T(8,128)(2,1)S(1)} collective-permute-done((bf16[64,1024]{1,0:T(8,128)(2,1)S(1)}, bf16[64,1024]{1,0:T(8,128)(2,1)S(1)}, u32[]{:S(2)}, u32[]{:S(2)}) %collective-permute-start.10) | collective-permute-done | bytes 131104 | tf_op jit(solution)/shard_map/ppermute | solution.py:264
  31.6 0.4 shard_map.97
  32.0 1.6 %collective-permute-done.9.refs_7_.refs_10_ = bf16[512,256]{1,0:T(8,128)(2,1)S(1)} collective-permute-done((bf16[512,256]{1,0:T(8,128)(2,1)S(1)}, bf16[512,256]{1,0:T(8,128)(2,1)S(1)}, u32[]{:S(2)}, u32[]{:S(2)}) %collective-permute-start.9) | collective-permute-done | bytes 262176 | tf_op jit(solution)/shard_map/ppermute | solution.py:269
  33.6 0.5 collective-permute-start.17
  34.1 1.0 %collective-permute-done.14.refs_10_.refs_13_ = bf16[512,256]{1,0:T(8,128)(2,1)S(1)} collective-permute-done((bf16[512,256]{1,0:T(8,128)(2,1)S(1)}, bf16[512,256]{1,0:T(8,128)(2,1)S(1)}, u32[]{:S(2)}, u32[]{:S(2)}) %collective-permute-start.14) | collective-permute-done | bytes 262176 | tf_op jit(solution)/shard_map/ppermute | solution.py:260
  35.1 0.4 collective-permute-done.17.refs_13_.refs_16_
  35.5 0.7 %shard_map.98 = (bf16[64,768]{1,0:T(8,128)(2,1)S(1)}, f32[64,1536]{1,0:T(8,128)S(1)}) custom-call(bf16[64,2048]{1,0:T(8,128)(2,1)S(1)} %get-tuple-element.61.refs_0_, f32[64,1536]{1,0:T(8,128)S(1)} %get-tuple-element.62.refs_1_, bf16[512,256]{1,0:T(8,128)(2,1)S(1)} %collective-permute-done.5.refs_2_.refs_5_, ...), custom_call_target="tpu_custom_call" | custom-call | tf_op jit(solution)/shard_map/pallas_call | solution.py:39
  36.3 2.3 %collective-permute-start.18 = (bf16[64,768]{1,0:T(8,128)(2,1)S(1)}, bf16[64,768]{1,0:T(8,128)(2,1)S(1)}, u32[]{:S(2)}, u32[]{:S(2)}) collective-permute-start(bf16[64,768]{1,0:T(8,128)(2,1)S(1)} %get-tuple-element.73.refs_0_.refs_2_), channel_id=1, source_target_pairs={{0,2},{1,3},{2,0},{3,1},{4,6},{5,7},{6,4},{7,5},{8,10},{9,11},{10,... | collective-permute-start | bytes 294920 | tf_op jit(solution)/shard_map/ppermute | solution.py:264
  38.6 3.1 %collective-permute-done.18.refs_1_.refs_3_ = bf16[64,768]{1,0:T(8,128)(2,1)S(1)} collective-permute-done((bf16[64,768]{1,0:T(8,128)(2,1)S(1)}, bf16[64,768]{1,0:T(8,128)(2,1)S(1)}, u32[]{:S(2)}, u32[]{:S(2)}) %collective-permute-start.18) | collective-permute-done | bytes 98336 | tf_op jit(solution)/shard_map/ppermute | solution.py:264
  41.7 0.1 collective-permute-start.28
  41.8 1.8 %collective-permute-start.23 = (bf16[64,768]{1,0:T(8,128)(2,1)S(1)}, bf16[64,768]{1,0:T(8,128)(2,1)S(1)}, u32[]{:S(2)}, u32[]{:S(2)}) collective-permute-start(bf16[64,768]{1,0:T(8,128)(2,1)S(1)} %get-tuple-element.81), channel_id=1, source_target_pairs={{0,2},{1,3},{2,0},{3,1},{4,6},{5,7},{6,4},{7,5},{8,10},{9,11},{10,... | collective-permute-start | bytes 294920 | tf_op jit(solution)/shard_map/ppermute | solution.py:264
  43.6 0.6 shard_map.99
  44.2 0.3 collective-permute-start.19
  44.6 2.4 %collective-permute-done.23.refs_2_ = bf16[64,768]{1,0:T(8,128)(2,1)S(1)} collective-permute-done((bf16[64,768]{1,0:T(8,128)(2,1)S(1)}, bf16[64,768]{1,0:T(8,128)(2,1)S(1)}, u32[]{:S(2)}, u32[]{:S(2)}) %collective-permute-start.23) | collective-permute-done | bytes 98336 | tf_op jit(solution)/shard_map/ppermute | solution.py:264
  47.0 2.0 %shard_map.101 = (bf16[16,2048]{1,0:T(8,128)(2,1)S(1)}, bf16[16,2048]{1,0:T(8,128)(2,1)S(1)}, bf16[16,2048]{1,0:T(8,128)(2,1)S(1)}, bf16[16,2048]{1,0:T(8,128)(2,1)S(1)}) custom-call(f32[64,1536]{1,0:T(8,128)S(1)} %get-tuple-element.80.refs_0_, f32[64,768]{1,0:T(8,128)S(1)} %get-tuple-element.70.refs_1_, ...), custom_call_target="tpu_custom_call" | custom-call | tf_op jit(solution)/shard_map/pallas_call | solution.py:39
  49.0 0.5 collective-permute-start.24
  49.5 3.4 %collective-permute-start.25 = (bf16[16,2048]{1,0:T(8,128)(2,1)S(1)}, bf16[16,2048]{1,0:T(8,128)(2,1)S(1)}, u32[]{:S(2)}, u32[]{:S(2)}) collective-permute-start(bf16[16,2048]{1,0:T(8,128)(2,1)S(1)} %get-tuple-element.84), channel_id=1, source_target_pairs={{0,8},{4,12},{8,0},{12,4},{1,9},{5,13},{9,1},{13,5},{2,10},{6,14},... | collective-permute-start | bytes 196616 | tf_op jit(solution)/shard_map/ppermute | solution.py:273
  52.9 0.6 collective-permute-start.26
  53.5 0.6 collective-permute-done.24.refs_2_
  54.0 3.3 %collective-permute-start.21 = (bf16[16,2048]{1,0:T(8,128)(2,1)S(1)}, bf16[16,2048]{1,0:T(8,128)(2,1)S(1)}, u32[]{:S(2)}, u32[]{:S(2)}) collective-permute-start(bf16[16,2048]{1,0:T(8,128)(2,1)S(1)} %get-tuple-element.78), channel_id=1, source_target_pairs={{0,8},{4,12},{8,0},{12,4},{1,9},{5,13},{9,1},{13,5},{2,10},{6,14},... | collective-permute-start | bytes 196616 | tf_op jit(solution)/shard_map/ppermute | solution.py:273
  57.4 1.1 %collective-permute-start.22 = (bf16[16,2048]{1,0:T(8,128)(2,1)S(1)}, bf16[16,2048]{1,0:T(8,128)(2,1)S(1)}, u32[]{:S(2)}, u32[]{:S(2)}) collective-permute-start(bf16[16,2048]{1,0:T(8,128)(2,1)S(1)} %get-tuple-element.79), channel_id=1, source_target_pairs={{0,12},{4,8},{8,4},{12,0},{1,13},{5,9},{9,5},{13,1},{2,14},{6,10},... | collective-permute-start | bytes 196616 | tf_op jit(solution)/shard_map/ppermute | solution.py:273
  58.4 1.6 %shard_map.103 = (f32[512,768]{1,0:T(8,128)}, f32[8,128]{1,0:T(8,128)S(1)}) custom-call(bf16[128,512]{1,0:T(8,128)(2,1)S(1)} %get-tuple-element.86.refs_0_, bf16[128,768]{1,0:T(8,128)(2,1)S(1)} %get-tuple-element.87.refs_1_, bf16[128,512]{1,0:T(8,128)(2,1)S(1)} %collective-permute-done.27.refs_2_, bf16[128,768]{1,0:T(8,128)(2,1)S(1)} %collective-permute-done.28.refs_3_), custom_call_target="tpu_custom_call" | custom-call | tf_op jit(solution)/shard_map/pallas_call | solution.py:39
  60.0 1.2 %shard_map.104 = (bf16[256,2048]{1,0:T(8,128)(2,1)}, f32[8,128]{1,0:T(8,128)S(1)}) custom-call(bf16[256,64]{1,0:T(8,128)(2,1)S(1)} %get-tuple-element.49.refs_0_, bf16[16,2048]{1,0:T(8,128)(2,1)S(1)} %get-tuple-element.82.refs_1_, bf16[16,2048]{1,0:T(8,128)(2,1)S(1)} %collective-permute-done.24.refs_2_, ...), custom_call_target="tpu_custom_call" | custom-call | tf_op jit(solution)/shard_map/pallas_call | solution.py:39
  61.2 1.4 %collective-permute-done.21.refs_4_ = bf16[16,2048]{1,0:T(8,128)(2,1)S(1)} collective-permute-done((bf16[16,2048]{1,0:T(8,128)(2,1)S(1)}, bf16[16,2048]{1,0:T(8,128)(2,1)S(1)}, u32[]{:S(2)}, u32[]{:S(2)}) %collective-permute-start.21) | collective-permute-done | bytes 65568 | tf_op jit(solution)/shard_map/ppermute | solution.py:273
  62.6 0.9 %collective-permute-done.22.refs_5_ = bf16[16,2048]{1,0:T(8,128)(2,1)S(1)} collective-permute-done((bf16[16,2048]{1,0:T(8,128)(2,1)S(1)}, bf16[16,2048]{1,0:T(8,128)(2,1)S(1)}, u32[]{:S(2)}, u32[]{:S(2)}) %collective-permute-start.22) | collective-permute-done | bytes 65568 | tf_op jit(solution)/shard_map/ppermute | solution.py:273
  63.5 1.3 %shard_map.105 = bf16[256,2048]{1,0:T(8,128)(2,1)} custom-call(bf16[256,64]{1,0:T(8,128)(2,1)S(1)} %get-tuple-element.49.refs_0_, f32[64,128]{1,0:T(8,128)S(1)} %get-tuple-element.50.refs_1_, bf16[16,2048]{1,0:T(8,128)(2,1)S(1)} %get-tuple-element.76.refs_2_, bf16[16,2048]{1,0:T(8,128)(2,1)S(1)} %collective-permute-done.20.refs_3_, ...), custom_call_target="tpu_custom_call" | custom-call | tf_op jit(solution)/shard_map/pallas_call | solution.py:39
  (26 shorter events, 0.1 us)
Async XLA Ops:
  0.6 6.7 %collective-permute-start = (bf16[512,1536]{1,0:T(8,128)(2,1)}, bf16[512,1536]{1,0:T(8,128)(2,1)S(1)}, u32[]{:S(2)}, u32[]{:S(2)}) collective-permute-start(bf16[512,1536]{1,0:T(8,128)(2,1)} %bitcast.5), channel_id=1, source_target_pairs={{0,1},{1,0},{2,3},{3,2},{4,5},{5,4},{6,7},{7,6},{8,9},{9,8},{10,11... | collective-permute-start | bytes 4718600 | tf_op jit(solution)/shard_map/ppermute | solution.py:260
  1.1 6.2 %collective-permute-start.1 = (bf16[512,768]{1,0:T(8,128)(2,1)}, bf16[512,768]{1,0:T(8,128)(2,1)S(1)}, u32[]{:S(2)}, u32[]{:S(2)}) collective-permute-start(bf16[512,768]{1,0:T(8,128)(2,1)} %bitcast.9), channel_id=1, source_target_pairs={{0,1},{1,0},{2,3},{3,2},{4,5},{5,4},{6,7},{7,6},{8,9},{9,8},{10,11... | collective-permute-start | bytes 2359304 | tf_op jit(solution)/shard_map/ppermute | solution.py:260
  2.4 22.6 %copy-start = (bf16[1,512,1536]{2,1,0:T(8,128)(2,1)S(1)}, bf16[1,512,1536]{2,1,0:T(8,128)(2,1)}, u32[]{:S(2)}) copy-start(bf16[1,512,1536]{2,1,0:T(8,128)(2,1)} %param.12) | copy-start | bytes 4718596
  2.4 11.2 %collective-permute-start.5 = (bf16[512,256]{1,0:T(8,128)(2,1)S(1)}, bf16[512,256]{1,0:T(8,128)(2,1)S(1)}, u32[]{:S(2)}, u32[]{:S(2)}) collective-permute-start(bf16[512,256]{1,0:T(8,128)(2,1)S(1)} %get-tuple-element.48.refs_5_), channel_id=1, source_target_pairs={{0,2},{1,3},{2,0},{3,1},{4,6},{5,7},{6,4},{7,5},{8,10},{9,11},{10,... | collective-permute-start | bytes 786440 | tf_op jit(solution)/shard_map/ppermute | solution.py:264
  7.3 6.3 %collective-permute-start.2 = (bf16[32,2048]{1,0:T(8,128)(2,1)S(1)}, bf16[32,2048]{1,0:T(8,128)(2,1)S(1)}, u32[]{:S(2)}, u32[]{:S(2)}) collective-permute-start(bf16[32,2048]{1,0:T(8,128)(2,1)S(1)} %get-tuple-element.56), channel_id=1, source_target_pairs={{0,4},{4,0},{8,12},{12,8},{1,5},{5,1},{9,13},{13,9},{2,6},{6,2},{1... | collective-permute-start | bytes 393224 | tf_op jit(solution)/shard_map/ppermute | solution.py:273
  9.0 9.8 %collective-permute-start.7 = (bf16[512,256]{1,0:T(8,128)(2,1)S(1)}, bf16[512,256]{1,0:T(8,128)(2,1)S(1)}, u32[]{:S(2)}, u32[]{:S(2)}) collective-permute-start(bf16[512,256]{1,0:T(8,128)(2,1)S(1)} %get-tuple-element.63), channel_id=1, source_target_pairs={{0,2},{1,3},{2,0},{3,1},{4,6},{5,7},{6,4},{7,5},{8,10},{9,11},{10,... | collective-permute-start | bytes 786440 | tf_op jit(solution)/shard_map/ppermute | solution.py:264
  10.0 21.7 %copy-start.1 = (bf16[1,512,768]{2,1,0:T(8,128)(2,1)S(1)}, bf16[1,512,768]{2,1,0:T(8,128)(2,1)}, u32[]{:S(2)}) copy-start(bf16[1,512,768]{2,1,0:T(8,128)(2,1)} %param.13) | copy-start | bytes 2359300
  10.0 14.5 %collective-permute-start.8 = (bf16[512,256]{1,0:T(8,128)(2,1)S(1)}, bf16[512,256]{1,0:T(8,128)(2,1)S(1)}, u32[]{:S(2)}, u32[]{:S(2)}) collective-permute-start(bf16[512,256]{1,0:T(8,128)(2,1)S(1)} %get-tuple-element.65), channel_id=1, source_target_pairs={{0,2},{1,3},{2,0},{3,1},{4,6},{5,7},{6,4},{7,5},{8,10},{9,11},{10,... | collective-permute-start | bytes 786440 | tf_op jit(solution)/shard_map/ppermute | solution.py:264
  11.0 11.9 %collective-permute-start.3 = (bf16[32,2048]{1,0:T(8,128)(2,1)S(1)}, bf16[32,2048]{1,0:T(8,128)(2,1)S(1)}, u32[]{:S(2)}, u32[]{:S(2)}) collective-permute-start(bf16[32,2048]{1,0:T(8,128)(2,1)S(1)} %get-tuple-element.57), channel_id=1, source_target_pairs={{0,8},{4,12},{8,0},{12,4},{1,9},{5,13},{9,1},{13,5},{2,10},{6,14},... | collective-permute-start | bytes 393224 | tf_op jit(solution)/shard_map/ppermute | solution.py:273
  13.6 11.4 %collective-permute-start.6 = (bf16[512,256]{1,0:T(8,128)(2,1)S(1)}, bf16[512,256]{1,0:T(8,128)(2,1)S(1)}, u32[]{:S(2)}, u32[]{:S(2)}) collective-permute-start(bf16[512,256]{1,0:T(8,128)(2,1)S(1)} %collective-permute-done.5.refs_2_.refs_5_), channel_id=1, source_target_pairs={{0,16},{16,0},{1,17},{17,1},{2,18},{18,2},{3,19},{19,3},{4,20},{20... | collective-permute-start | bytes 786440 | tf_op jit(solution)/shard_map/ppermute | solution.py:269
  15.1 9.3 %collective-permute-start.4 = (bf16[32,2048]{1,0:T(8,128)(2,1)S(1)}, bf16[32,2048]{1,0:T(8,128)(2,1)S(1)}, u32[]{:S(2)}, u32[]{:S(2)}) collective-permute-start(bf16[32,2048]{1,0:T(8,128)(2,1)S(1)} %get-tuple-element.58), channel_id=1, source_target_pairs={{0,12},{4,8},{8,4},{12,0},{1,13},{5,9},{9,5},{13,1},{2,14},{6,10},... | collective-permute-start | bytes 393224 | tf_op jit(solution)/shard_map/ppermute | solution.py:273
  22.9 7.9 %collective-permute-start.11 = (bf16[512,256]{1,0:T(8,128)(2,1)S(1)}, bf16[512,256]{1,0:T(8,128)(2,1)S(1)}, u32[]{:S(2)}, u32[]{:S(2)}) collective-permute-start(bf16[512,256]{1,0:T(8,128)(2,1)S(1)} %collective-permute-done.7.refs_3_.refs_6_), channel_id=1, source_target_pairs={{0,16},{16,0},{1,17},{17,1},{2,18},{18,2},{3,19},{19,3},{4,20},{20... | collective-permute-start | bytes 786440 | tf_op jit(solution)/shard_map/ppermute | solution.py:269
  24.5 9.1 %collective-permute-start.9 = (bf16[512,256]{1,0:T(8,128)(2,1)S(1)}, bf16[512,256]{1,0:T(8,128)(2,1)S(1)}, u32[]{:S(2)}, u32[]{:S(2)}) collective-permute-start(bf16[512,256]{1,0:T(8,128)(2,1)S(1)} %collective-permute-done.8.refs_4_.refs_7_), channel_id=1, source_target_pairs={{0,16},{16,0},{1,17},{17,1},{2,18},{18,2},{3,19},{19,3},{4,20},{20... | collective-permute-start | bytes 786440 | tf_op jit(solution)/shard_map/ppermute | solution.py:269
  25.0 8.6 %collective-permute-start.13 = (bf16[512,256]{1,0:T(8,128)(2,1)S(1)}, bf16[512,256]{1,0:T(8,128)(2,1)S(1)}, u32[]{:S(2)}, u32[]{:S(2)}) collective-permute-start(bf16[512,256]{1,0:T(8,128)(2,1)S(1)} %collective-permute-done.7.refs_3_.refs_6_), channel_id=1, source_target_pairs={{0,1},{1,0},{2,3},{3,2},{4,5},{5,4},{6,7},{7,6},{8,9},{9,8},{10,11... | collective-permute-start | bytes 786440 | tf_op jit(solution)/shard_map/ppermute | solution.py:260
  25.6 6.0 %collective-permute-start.10 = (bf16[64,1024]{1,0:T(8,128)(2,1)S(1)}, bf16[64,1024]{1,0:T(8,128)(2,1)S(1)}, u32[]{:S(2)}, u32[]{:S(2)}) collective-permute-start(bf16[64,1024]{1,0:T(8,128)(2,1)S(1)} %get-tuple-element.68), channel_id=1, source_target_pairs={{0,2},{1,3},{2,0},{3,1},{4,6},{5,7},{6,4},{7,5},{8,10},{9,11},{10,... | collective-permute-start | bytes 393224 | tf_op jit(solution)/shard_map/ppermute | solution.py:264
  27.2 7.0 %collective-permute-start.12 = (bf16[512,256]{1,0:T(8,128)(2,1)S(1)}, bf16[512,256]{1,0:T(8,128)(2,1)S(1)}, u32[]{:S(2)}, u32[]{:S(2)}) collective-permute-start(bf16[512,256]{1,0:T(8,128)(2,1)S(1)} %collective-permute-done.5.refs_2_.refs_5_), channel_id=1, source_target_pairs={{0,1},{1,0},{2,3},{3,2},{4,5},{5,4},{6,7},{7,6},{8,9},{9,8},{10,11... | collective-permute-start | bytes 786440 | tf_op jit(solution)/shard_map/ppermute | solution.py:260
  30.8 3.3 %collective-permute-start.15 = (bf16[512,256]{1,0:T(8,128)(2,1)S(1)}, bf16[512,256]{1,0:T(8,128)(2,1)S(1)}, u32[]{:S(2)}, u32[]{:S(2)}) collective-permute-start(bf16[512,256]{1,0:T(8,128)(2,1)S(1)} %collective-permute-done.6.refs_6_.refs_5_.refs_8_), channel_id=1, source_target_pairs={{0,1},{1,0},{2,3},{3,2},{4,5},{5,4},{6,7},{7,6},{8,9},{9,8},{10,11... | collective-permute-start | bytes 786440 | tf_op jit(solution)/shard_map/ppermute | solution.py:260
  31.6 2.5 %collective-permute-start.16 = (bf16[512,256]{1,0:T(8,128)(2,1)S(1)}, bf16[512,256]{1,0:T(8,128)(2,1)S(1)}, u32[]{:S(2)}, u32[]{:S(2)}) collective-permute-start(bf16[512,256]{1,0:T(8,128)(2,1)S(1)} %collective-permute-done.11.refs_6_.refs_9_), channel_id=1, source_target_pairs={{0,1},{1,0},{2,3},{3,2},{4,5},{5,4},{6,7},{7,6},{8,9},{9,8},{10,11... | collective-permute-start | bytes 786440 | tf_op jit(solution)/shard_map/ppermute | solution.py:260
  33.6 1.5 %collective-permute-start.14 = (bf16[512,256]{1,0:T(8,128)(2,1)S(1)}, bf16[512,256]{1,0:T(8,128)(2,1)S(1)}, u32[]{:S(2)}, u32[]{:S(2)}) collective-permute-start(bf16[512,256]{1,0:T(8,128)(2,1)S(1)} %collective-permute-done.8.refs_4_.refs_7_), channel_id=1, source_target_pairs={{0,1},{1,0},{2,3},{3,2},{4,5},{5,4},{6,7},{7,6},{8,9},{9,8},{10,11... | collective-permute-start | bytes 786440 | tf_op jit(solution)/shard_map/ppermute | solution.py:260
  33.6 1.9 %collective-permute-start.17 = (bf16[512,256]{1,0:T(8,128)(2,1)S(1)}, bf16[512,256]{1,0:T(8,128)(2,1)S(1)}, u32[]{:S(2)}, u32[]{:S(2)}) collective-permute-start(bf16[512,256]{1,0:T(8,128)(2,1)S(1)} %collective-permute-done.9.refs_7_.refs_10_), channel_id=1, source_target_pairs={{0,1},{1,0},{2,3},{3,2},{4,5},{5,4},{6,7},{7,6},{8,9},{9,8},{10,11... | collective-permute-start | bytes 786440 | tf_op jit(solution)/shard_map/ppermute | solution.py:260
  36.3 5.4 %collective-permute-start.18 = (bf16[64,768]{1,0:T(8,128)(2,1)S(1)}, bf16[64,768]{1,0:T(8,128)(2,1)S(1)}, u32[]{:S(2)}, u32[]{:S(2)}) collective-permute-start(bf16[64,768]{1,0:T(8,128)(2,1)S(1)} %get-tuple-element.73.refs_0_.refs_2_), channel_id=1, source_target_pairs={{0,2},{1,3},{2,0},{3,1},{4,6},{5,7},{6,4},{7,5},{8,10},{9,11},{10,... | collective-permute-start | bytes 294920 | tf_op jit(solution)/shard_map/ppermute | solution.py:264
  41.7 15.7 %collective-permute-start.28 = (bf16[128,768]{1,0:T(8,128)(2,1)S(1)}, bf16[128,768]{1,0:T(8,128)(2,1)S(1)}, u32[]{:S(2)}, u32[]{:S(2)}) collective-permute-start(bf16[128,768]{1,0:T(8,128)(2,1)S(1)} %get-tuple-element.87.refs_1_), channel_id=1, source_target_pairs={{0,1},{1,0},{2,3},{3,2},{4,5},{5,4},{6,7},{7,6},{8,9},{9,8},{10,11... | collective-permute-start | bytes 589832 | tf_op jit(solution)/shard_map/ppermute | solution.py:260
  41.8 5.2 %collective-permute-start.23 = (bf16[64,768]{1,0:T(8,128)(2,1)S(1)}, bf16[64,768]{1,0:T(8,128)(2,1)S(1)}, u32[]{:S(2)}, u32[]{:S(2)}) collective-permute-start(bf16[64,768]{1,0:T(8,128)(2,1)S(1)} %get-tuple-element.81), channel_id=1, source_target_pairs={{0,2},{1,3},{2,0},{3,1},{4,6},{5,7},{6,4},{7,5},{8,10},{9,11},{10,... | collective-permute-start | bytes 294920 | tf_op jit(solution)/shard_map/ppermute | solution.py:264
  44.2 8.6 %collective-permute-start.19 = (bf16[64,1024]{1,0:T(8,128)(2,1)S(1)}, bf16[64,1024]{1,0:T(8,128)(2,1)S(1)}, u32[]{:S(2)}, u32[]{:S(2)}) collective-permute-start(bf16[64,1024]{1,0:T(8,128)(2,1)S(1)} %get-tuple-element.75), channel_id=1, source_target_pairs={{0,2},{1,3},{2,0},{3,1},{4,6},{5,7},{6,4},{7,5},{8,10},{9,11},{10,... | collective-permute-start | bytes 393224 | tf_op jit(solution)/shard_map/ppermute | solution.py:264
  44.6 9.5 %collective-permute-start.27 = (bf16[128,512]{1,0:T(8,128)(2,1)S(1)}, bf16[128,512]{1,0:T(8,128)(2,1)S(1)}, u32[]{:S(2)}, u32[]{:S(2)}) collective-permute-start(bf16[128,512]{1,0:T(8,128)(2,1)S(1)} %get-tuple-element.88), channel_id=1, source_target_pairs={{0,1},{1,0},{2,3},{3,2},{4,5},{5,4},{6,7},{7,6},{8,9},{9,8},{10,11... | collective-permute-start | bytes 393224 | tf_op jit(solution)/shard_map/ppermute | solution.py:260
  49.0 5.0 %collective-permute-start.24 = (bf16[16,2048]{1,0:T(8,128)(2,1)S(1)}, bf16[16,2048]{1,0:T(8,128)(2,1)S(1)}, u32[]{:S(2)}, u32[]{:S(2)}) collective-permute-start(bf16[16,2048]{1,0:T(8,128)(2,1)S(1)} %get-tuple-element.83), channel_id=1, source_target_pairs={{0,4},{4,0},{8,12},{12,8},{1,5},{5,1},{9,13},{13,9},{2,6},{6,2},{1... | collective-permute-start | bytes 196616 | tf_op jit(solution)/shard_map/ppermute | solution.py:273
  49.5 10.5 %collective-permute-start.25 = (bf16[16,2048]{1,0:T(8,128)(2,1)S(1)}, bf16[16,2048]{1,0:T(8,128)(2,1)S(1)}, u32[]{:S(2)}, u32[]{:S(2)}) collective-permute-start(bf16[16,2048]{1,0:T(8,128)(2,1)S(1)} %get-tuple-element.84), channel_id=1, source_target_pairs={{0,8},{4,12},{8,0},{12,4},{1,9},{5,13},{9,1},{13,5},{2,10},{6,14},... | collective-permute-start | bytes 196616 | tf_op jit(solution)/shard_map/ppermute | solution.py:273
  52.9 7.1 %collective-permute-start.26 = (bf16[16,2048]{1,0:T(8,128)(2,1)S(1)}, bf16[16,2048]{1,0:T(8,128)(2,1)S(1)}, u32[]{:S(2)}, u32[]{:S(2)}) collective-permute-start(bf16[16,2048]{1,0:T(8,128)(2,1)S(1)} %get-tuple-element.85), channel_id=1, source_target_pairs={{0,12},{4,8},{8,4},{12,0},{1,13},{5,9},{9,5},{13,1},{2,14},{6,10},... | collective-permute-start | bytes 196616 | tf_op jit(solution)/shard_map/ppermute | solution.py:273
  54.0 7.2 %collective-permute-start.20 = (bf16[16,2048]{1,0:T(8,128)(2,1)S(1)}, bf16[16,2048]{1,0:T(8,128)(2,1)S(1)}, u32[]{:S(2)}, u32[]{:S(2)}) collective-permute-start(bf16[16,2048]{1,0:T(8,128)(2,1)S(1)} %get-tuple-element.77), channel_id=1, source_target_pairs={{0,4},{4,0},{8,12},{12,8},{1,5},{5,1},{9,13},{13,9},{2,6},{6,2},{1... | collective-permute-start | bytes 196616 | tf_op jit(solution)/shard_map/ppermute | solution.py:273
  54.0 8.6 %collective-permute-start.21 = (bf16[16,2048]{1,0:T(8,128)(2,1)S(1)}, bf16[16,2048]{1,0:T(8,128)(2,1)S(1)}, u32[]{:S(2)}, u32[]{:S(2)}) collective-permute-start(bf16[16,2048]{1,0:T(8,128)(2,1)S(1)} %get-tuple-element.78), channel_id=1, source_target_pairs={{0,8},{4,12},{8,0},{12,4},{1,9},{5,13},{9,1},{13,5},{2,10},{6,14},... | collective-permute-start | bytes 196616 | tf_op jit(solution)/shard_map/ppermute | solution.py:273
  57.4 6.2 %collective-permute-start.22 = (bf16[16,2048]{1,0:T(8,128)(2,1)S(1)}, bf16[16,2048]{1,0:T(8,128)(2,1)S(1)}, u32[]{:S(2)}, u32[]{:S(2)}) collective-permute-start(bf16[16,2048]{1,0:T(8,128)(2,1)S(1)} %get-tuple-element.79), channel_id=1, source_target_pairs={{0,12},{4,8},{8,4},{12,0},{1,13},{5,9},{9,5},{13,1},{2,14},{6,10},... | collective-permute-start | bytes 196616 | tf_op jit(solution)/shard_map/ppermute | solution.py:273

commit v8 on v7

--- a/solution.py
+++ b/solution.py
@@ -304,7 +304,7 @@
     *chunks, in_sib, out_sib = lax.optimization_barrier((*chunks, in_sib, out_sib))
     chunks = to_expert(chunks)
     shares = [to_x([piece] * (spread - 1)) for piece in pieces]
-    shares = [lax.optimization_barrier((vs, chunks[1 + i]))[0] for i, vs in enumerate(shares)]
+    shares[0] = lax.optimization_barrier((shares[0], chunks[1]))[0]
     shares = [[[v] + [to_replica(v, n) for n in range(1, replicas)] for v in vs] for vs in shares]
     early = shares[0][0][1:]
     rows, pre, *grads = call(
@@ -320,7 +320,7 @@
         (*grads, out_own, out_sib),
     )
     backs = (back, *to_x(back_far))
-    shares[-1], back = lax.optimization_barrier((shares[-1], back))
+    shares[-1] = lax.optimization_barrier((shares[-1], *backs[1:]))[0]
     pieces = []
     for kx in range(spread - 1):
         here = [shares[s][kx][n] for n in range(replicas) for s in range(PIECES)]
@@ -338,7 +338,9 @@
         scratch_shapes=[pltpu.VMEM((slots, 2 * feed), BF16)],
     )
     d_rows = to_expert(d_rows)
-    near, *far = call(bound(expert_out_kernel, spread), by_x, (*hidden, out_own, out_sib))
+    near, *far = call(
+        bound(expert_out_kernel, spread), by_x, (*hidden, out_own, out_sib), after=d_rows[1:2]
+    )
     expert_out = call(
         bound(join_kernel, groups, spread, capacity), chunk, (near, *to_x(far))
     )

time: 65 us -> 65.9 us (1.014)
  starting transfers between devices: 32.7 us -> 34.1 us
    ppermute x7, waiting for transfers between devices: 6.33 us -> 11.9 us  [to_x(): lax.ppermute(value, 'fsdp', [(i, i ^ (k + 1) * CORES) for i in range(part...]
    ppermute x3, waiting for transfers between devices: 5.03 us -> 0.01 us  [to_replica(): return lax.ppermute(value, 'replica', [(i, i ^ n) for i in range(replicas)])]
    ppermute x3, starting transfers between devices: 3.55 us -> 5.41 us  [to_replica(): return lax.ppermute(value, 'replica', [(i, i ^ n) for i in range(replicas)])]
    ppermute x9, waiting for transfers between devices: 7.05 us -> 5.98 us  [to_expert(): lax.ppermute(value, 'expert', [(i, i ^ ke) for i in range(groups)])]
where the time goes in v8:
time: 65.9 us; the launch traced here: 65.7 us
  starting transfers between devices  34.1 us (52%)
  waiting for transfers between devices  19.3 us (29%)
  Pallas kernels  11.6 us (18%)
  between operations  0.77 us (1%)
    ppermute x9, starting transfers between devices, to_expert(): lax.ppermute(value, 'expert', [(i, i ^ ke) for i in range(groups)])  16.6 us
    ppermute x7, waiting for transfers between devices, to_x(): lax.ppermute(value, 'fsdp', [(i, i ^ (k + 1) * CORES) for i in range(part...  11.9 us
    pallas_call x12, Pallas kernels, call(): pl.pallas_call(kernel, out_shape=out_shape, in_specs=specs, compiler_para...  11.6 us
    ppermute x7, starting transfers between devices, to_x(): lax.ppermute(value, 'fsdp', [(i, i ^ (k + 1) * CORES) for i in range(part...  10.3 us
    ppermute x9, waiting for transfers between devices, to_expert(): lax.ppermute(value, 'expert', [(i, i ^ ke) for i in range(groups)])  5.98 us
    ppermute x3, starting transfers between devices, to_replica(): return lax.ppermute(value, 'replica', [(i, i ^ n) for i in range(replicas)])  5.41 us
    ppermute x10, starting transfers between devices, to_core(): return lax.ppermute(value, 'fsdp', [(i, i ^ 1) for i in range(parts)])  1.7 us
    ppermute x10, waiting for transfers between devices, to_core(): return lax.ppermute(value, 'fsdp', [(i, i ^ 1) for i in range(parts)])  1.4 us
  transfers between devices with their start and end apart: 29, of which 11 were waited for; matrix products, arithmetic and copies ran while one was open for 0% of the time, Pallas kernels for 15%

profile of v8, /device:TPU:0, one launch (start us, length us, event | category | flops | bytes accessed | tf_op | source)
XLA Modules:
  0.0 65.7 jit_solution(17350399976309541023)
XLA Ops:
  0.6 0.5 collective-permute-start
  1.1 0.1 collective-permute-start.1
  1.2 1.1 %shard_map.94 = (bf16[512,256]{1,0:T(8,128)(2,1)S(1)}, bf16[512,256]{1,0:T(8,128)(2,1)S(1)}, bf16[512,256]{1,0:T(8,128)(2,1)S(1)}) custom-call(bf16[512,1536]{1,0:T(8,128)(2,1)} %bitcast.6), custom_call_target="tpu_custom_call" | custom-call | tf_op jit(solution)/shard_map/pallas_call | solution.py:39
  2.4 0.0 copy-start
  2.4 3.0 %collective-permute-start.5 = (bf16[512,256]{1,0:T(8,128)(2,1)S(1)}, bf16[512,256]{1,0:T(8,128)(2,1)S(1)}, u32[]{:S(2)}, u32[]{:S(2)}) collective-permute-start(bf16[512,256]{1,0:T(8,128)(2,1)S(1)} %get-tuple-element.46.refs_5_), channel_id=1, source_target_pairs={{0,2},{1,3},{2,0},{3,1},{4,6},{5,7},{6,4},{7,5},{8,10},{9,11},{10,... | collective-permute-start | bytes 786440 | tf_op jit(solution)/shard_map/ppermute | solution.py:264
  5.4 1.9 %shard_map.95 = (bf16[32,2048]{1,0:T(8,128)(2,1)S(1)}, bf16[32,2048]{1,0:T(8,128)(2,1)S(1)}, bf16[32,2048]{1,0:T(8,128)(2,1)S(1)}, bf16[32,2048]{1,0:T(8,128)(2,...) custom-call(s32[8,256]{1,0:T(8,128)} %bitcast.12, f32[8,256]{1,0:T(8,128)} %bitcast.13, s32[1,256]{1,0:T(1,128)} %refs_2_.1, ...), custom_call_target="tpu_custom_call" | custom-call | tf_op jit(solution)/shard_map/pallas_call | solution.py:39
  7.3 0.0 collective-permute-done.refs_5_.refs_4_
  7.3 1.6 %collective-permute-start.2 = (bf16[32,2048]{1,0:T(8,128)(2,1)S(1)}, bf16[32,2048]{1,0:T(8,128)(2,1)S(1)}, u32[]{:S(2)}, u32[]{:S(2)}) collective-permute-start(bf16[32,2048]{1,0:T(8,128)(2,1)S(1)} %get-tuple-element.54), channel_id=1, source_target_pairs={{0,4},{4,0},{8,12},{12,8},{1,5},{5,1},{9,13},{13,9},{2,6},{6,2},{1... | collective-permute-start | bytes 393224 | tf_op jit(solution)/shard_map/ppermute | solution.py:273
  9.0 1.0 %collective-permute-start.7 = (bf16[512,256]{1,0:T(8,128)(2,1)S(1)}, bf16[512,256]{1,0:T(8,128)(2,1)S(1)}, u32[]{:S(2)}, u32[]{:S(2)}) collective-permute-start(bf16[512,256]{1,0:T(8,128)(2,1)S(1)} %get-tuple-element.61), channel_id=1, source_target_pairs={{0,2},{1,3},{2,0},{3,1},{4,6},{5,7},{6,4},{7,5},{8,10},{9,11},{10,... | collective-permute-start | bytes 786440 | tf_op jit(solution)/shard_map/ppermute | solution.py:264
  10.0 1.0 %collective-permute-start.8 = (bf16[512,256]{1,0:T(8,128)(2,1)S(1)}, bf16[512,256]{1,0:T(8,128)(2,1)S(1)}, u32[]{:S(2)}, u32[]{:S(2)}) collective-permute-start(bf16[512,256]{1,0:T(8,128)(2,1)S(1)} %get-tuple-element.62), channel_id=1, source_target_pairs={{0,2},{1,3},{2,0},{3,1},{4,6},{5,7},{6,4},{7,5},{8,10},{9,11},{10,... | collective-permute-start | bytes 786440 | tf_op jit(solution)/shard_map/ppermute | solution.py:264
  11.0 1.5 %collective-permute-done.5.refs_2_.refs_5_ = bf16[512,256]{1,0:T(8,128)(2,1)S(1)} collective-permute-done((bf16[512,256]{1,0:T(8,128)(2,1)S(1)}, bf16[512,256]{1,0:T(8,128)(2,1)S(1)}, u32[]{:S(2)}, u32[]{:S(2)}) %collective-permute-start.5) | collective-permute-done | bytes 262176 | tf_op jit(solution)/shard_map/ppermute | solution.py:264
  12.5 0.1 collective-permute-done.2.refs_1_
  12.6 2.0 %collective-permute-start.6 = (bf16[512,256]{1,0:T(8,128)(2,1)S(1)}, bf16[512,256]{1,0:T(8,128)(2,1)S(1)}, u32[]{:S(2)}, u32[]{:S(2)}) collective-permute-start(bf16[512,256]{1,0:T(8,128)(2,1)S(1)} %collective-permute-done.5.refs_2_.refs_5_), channel_id=1, source_target_pairs={{0,16},{16,0},{1,17},{17,1},{2,18},{18,2},{3,19},{19,3},{4,20},{20... | collective-permute-start | bytes 786440 | tf_op jit(solution)/shard_map/ppermute | solution.py:269
  14.6 2.6 %collective-permute-start.3 = (bf16[32,2048]{1,0:T(8,128)(2,1)S(1)}, bf16[32,2048]{1,0:T(8,128)(2,1)S(1)}, u32[]{:S(2)}, u32[]{:S(2)}) collective-permute-start(bf16[32,2048]{1,0:T(8,128)(2,1)S(1)} %get-tuple-element.55), channel_id=1, source_target_pairs={{0,8},{4,12},{8,0},{12,4},{1,9},{5,13},{9,1},{13,5},{2,10},{6,14},... | collective-permute-start | bytes 393224 | tf_op jit(solution)/shard_map/ppermute | solution.py:273
  17.2 1.3 %collective-permute-start.4 = (bf16[32,2048]{1,0:T(8,128)(2,1)S(1)}, bf16[32,2048]{1,0:T(8,128)(2,1)S(1)}, u32[]{:S(2)}, u32[]{:S(2)}) collective-permute-start(bf16[32,2048]{1,0:T(8,128)(2,1)S(1)} %get-tuple-element.56), channel_id=1, source_target_pairs={{0,12},{4,8},{8,4},{12,0},{1,13},{5,9},{9,5},{13,1},{2,14},{6,10},... | collective-permute-start | bytes 393224 | tf_op jit(solution)/shard_map/ppermute | solution.py:273
  18.5 1.7 %collective-permute-start.12 = (bf16[512,256]{1,0:T(8,128)(2,1)S(1)}, bf16[512,256]{1,0:T(8,128)(2,1)S(1)}, u32[]{:S(2)}, u32[]{:S(2)}) collective-permute-start(bf16[512,256]{1,0:T(8,128)(2,1)S(1)} %collective-permute-done.7.refs_3_.refs_6_), channel_id=1, source_target_pairs={{0,16},{16,0},{1,17},{17,1},{2,18},{18,2},{3,19},{19,3},{4,20},{20... | collective-permute-start | bytes 786440 | tf_op jit(solution)/shard_map/ppermute | solution.py:269
  20.2 3.0 %collective-permute-done.8.refs_4_.refs_7_ = bf16[512,256]{1,0:T(8,128)(2,1)S(1)} collective-permute-done((bf16[512,256]{1,0:T(8,128)(2,1)S(1)}, bf16[512,256]{1,0:T(8,128)(2,1)S(1)}, u32[]{:S(2)}, u32[]{:S(2)}) %collective-permute-start.8) | collective-permute-done | bytes 262176 | tf_op jit(solution)/shard_map/ppermute | solution.py:264
  23.2 1.8 %collective-permute-start.9 = (bf16[512,256]{1,0:T(8,128)(2,1)S(1)}, bf16[512,256]{1,0:T(8,128)(2,1)S(1)}, u32[]{:S(2)}, u32[]{:S(2)}) collective-permute-start(bf16[512,256]{1,0:T(8,128)(2,1)S(1)} %collective-permute-done.8.refs_4_.refs_7_), channel_id=1, source_target_pairs={{0,16},{16,0},{1,17},{17,1},{2,18},{18,2},{3,19},{19,3},{4,20},{20... | collective-permute-start | bytes 786440 | tf_op jit(solution)/shard_map/ppermute | solution.py:269
  24.9 1.2 %collective-permute-done.3.refs_2_ = bf16[32,2048]{1,0:T(8,128)(2,1)S(1)} collective-permute-done((bf16[32,2048]{1,0:T(8,128)(2,1)S(1)}, bf16[32,2048]{1,0:T(8,128)(2,1)S(1)}, u32[]{:S(2)}, u32[]{:S(2)}) %collective-permute-start.3) | collective-permute-done | bytes 131104 | tf_op jit(solution)/shard_map/ppermute | solution.py:273
  26.1 0.7 shard_map.96
  26.8 1.6 %collective-permute-start.10 = (bf16[64,1024]{1,0:T(8,128)(2,1)S(1)}, bf16[64,1024]{1,0:T(8,128)(2,1)S(1)}, u32[]{:S(2)}, u32[]{:S(2)}) collective-permute-start(bf16[64,1024]{1,0:T(8,128)(2,1)S(1)} %get-tuple-element.64), channel_id=1, source_target_pairs={{0,2},{1,3},{2,0},{3,1},{4,6},{5,7},{6,4},{7,5},{8,10},{9,11},{10,... | collective-permute-start | bytes 393224 | tf_op jit(solution)/shard_map/ppermute | solution.py:264
  28.4 4.4 %collective-permute-done.10.refs_1_ = bf16[64,1024]{1,0:T(8,128)(2,1)S(1)} collective-permute-done((bf16[64,1024]{1,0:T(8,128)(2,1)S(1)}, bf16[64,1024]{1,0:T(8,128)(2,1)S(1)}, u32[]{:S(2)}, u32[]{:S(2)}) %collective-permute-start.10) | collective-permute-done | bytes 131104 | tf_op jit(solution)/shard_map/ppermute | solution.py:264
  32.7 0.4 shard_map.97
  33.1 1.6 %collective-permute-start.11 = (bf16[64,768]{1,0:T(8,128)(2,1)S(1)}, bf16[64,768]{1,0:T(8,128)(2,1)S(1)}, u32[]{:S(2)}, u32[]{:S(2)}) collective-permute-start(bf16[64,768]{1,0:T(8,128)(2,1)S(1)} %get-tuple-element.66), channel_id=1, source_target_pairs={{0,2},{1,3},{2,0},{3,1},{4,6},{5,7},{6,4},{7,5},{8,10},{9,11},{10,... | collective-permute-start | bytes 294920 | tf_op jit(solution)/shard_map/ppermute | solution.py:264
  34.7 0.5 collective-permute-start.13
  35.2 0.0 collective-permute-start.16
  35.2 2.6 %collective-permute-done.11.refs_2_ = bf16[64,768]{1,0:T(8,128)(2,1)S(1)} collective-permute-done((bf16[64,768]{1,0:T(8,128)(2,1)S(1)}, bf16[64,768]{1,0:T(8,128)(2,1)S(1)}, u32[]{:S(2)}, u32[]{:S(2)}) %collective-permute-start.11) | collective-permute-done | bytes 98336 | tf_op jit(solution)/shard_map/ppermute | solution.py:264
  37.8 0.5 collective-permute-start.18
  38.3 1.0 %collective-permute-done.15.refs_10_.refs_13_ = bf16[512,256]{1,0:T(8,128)(2,1)S(1)} collective-permute-done((bf16[512,256]{1,0:T(8,128)(2,1)S(1)}, bf16[512,256]{1,0:T(8,128)(2,1)S(1)}, u32[]{:S(2)}, u32[]{:S(2)}) %collective-permute-start.15) | collective-permute-done | bytes 262176 | tf_op jit(solution)/shard_map/ppermute | solution.py:260
  39.3 0.4 collective-permute-done.18.refs_13_.refs_16_
  39.7 0.7 %shard_map.98 = (bf16[64,768]{1,0:T(8,128)(2,1)S(1)}, f32[64,1536]{1,0:T(8,128)S(1)}) custom-call(bf16[64,2048]{1,0:T(8,128)(2,1)S(1)} %get-tuple-element.59.refs_0_, f32[64,1536]{1,0:T(8,128)S(1)} %get-tuple-element.60.refs_1_, bf16[512,256]{1,0:T(8,128)(2,1)S(1)} %collective-permute-done.5.refs_2_.refs_5_, ...), custom_call_target="tpu_custom_call" | custom-call | tf_op jit(solution)/shard_map/pallas_call | solution.py:39
  40.5 1.6 %collective-permute-start.19 = (bf16[64,768]{1,0:T(8,128)(2,1)S(1)}, bf16[64,768]{1,0:T(8,128)(2,1)S(1)}, u32[]{:S(2)}, u32[]{:S(2)}) collective-permute-start(bf16[64,768]{1,0:T(8,128)(2,1)S(1)} %get-tuple-element.69.refs_0_.refs_2_), channel_id=1, source_target_pairs={{0,2},{1,3},{2,0},{3,1},{4,6},{5,7},{6,4},{7,5},{8,10},{9,11},{10,... | collective-permute-start | bytes 294920 | tf_op jit(solution)/shard_map/ppermute | solution.py:264
  42.0 2.0 %shard_map.99 = (bf16[16,2048]{1,0:T(8,128)(2,1)S(1)}, bf16[16,2048]{1,0:T(8,128)(2,1)S(1)}, bf16[16,2048]{1,0:T(8,128)(2,1)S(1)}, bf16[16,2048]{1,0:T(8,128)(2,1)S(1)}) custom-call(f32[64,1536]{1,0:T(8,128)S(1)} %get-tuple-element.70.refs_0_, f32[64,768]{1,0:T(8,128)S(1)} %get-tuple-element.71.refs_1_, bf16[64,768]{1,0:T(8,128)(2,1)S(1)} %collective-permute-done.11.refs_2_, ...), custom_call_target="tpu_custom_call" | custom-call | tf_op jit(solution)/shard_map/pallas_call | solution.py:39
  44.0 1.8 %collective-permute-start.20 = (bf16[16,2048]{1,0:T(8,128)(2,1)S(1)}, bf16[16,2048]{1,0:T(8,128)(2,1)S(1)}, u32[]{:S(2)}, u32[]{:S(2)}) collective-permute-start(bf16[16,2048]{1,0:T(8,128)(2,1)S(1)} %get-tuple-element.72), channel_id=1, source_target_pairs={{0,4},{4,0},{8,12},{12,8},{1,5},{5,1},{9,13},{13,9},{2,6},{6,2},{1... | collective-permute-start | bytes 196616 | tf_op jit(solution)/shard_map/ppermute | solution.py:273
  45.9 0.1 collective-permute-start.28
  46.0 2.4 %collective-permute-done.20.refs_4_.refs_2_ = bf16[16,2048]{1,0:T(8,128)(2,1)S(1)} collective-permute-done((bf16[16,2048]{1,0:T(8,128)(2,1)S(1)}, bf16[16,2048]{1,0:T(8,128)(2,1)S(1)}, u32[]{:S(2)}, u32[]{:S(2)}) %collective-permute-start.20) | collective-permute-done | bytes 65568 | tf_op jit(solution)/shard_map/ppermute | solution.py:273
  48.4 0.6 shard_map.100
  49.0 0.6 collective-permute-start.21
  49.6 3.5 %collective-permute-start.25 = (bf16[16,2048]{1,0:T(8,128)(2,1)S(1)}, bf16[16,2048]{1,0:T(8,128)(2,1)S(1)}, u32[]{:S(2)}, u32[]{:S(2)}) collective-permute-start(bf16[16,2048]{1,0:T(8,128)(2,1)S(1)} %get-tuple-element.80), channel_id=1, source_target_pairs={{0,8},{4,12},{8,0},{12,4},{1,9},{5,13},{9,1},{13,5},{2,10},{6,14},... | collective-permute-start | bytes 196616 | tf_op jit(solution)/shard_map/ppermute | solution.py:273
  53.1 0.4 collective-permute-start.26
  53.5 0.5 collective-permute-done.21.refs_1_
  54.1 1.8 %collective-permute-start.22 = (bf16[16,2048]{1,0:T(8,128)(2,1)S(1)}, bf16[16,2048]{1,0:T(8,128)(2,1)S(1)}, u32[]{:S(2)}, u32[]{:S(2)}) collective-permute-start(bf16[16,2048]{1,0:T(8,128)(2,1)S(1)} %get-tuple-element.76), channel_id=1, source_target_pairs={{0,4},{4,0},{8,12},{12,8},{1,5},{5,1},{9,13},{13,9},{2,6},{6,2},{1... | collective-permute-start | bytes 196616 | tf_op jit(solution)/shard_map/ppermute | solution.py:273
  55.9 2.0 %collective-permute-start.23 = (bf16[16,2048]{1,0:T(8,128)(2,1)S(1)}, bf16[16,2048]{1,0:T(8,128)(2,1)S(1)}, u32[]{:S(2)}, u32[]{:S(2)}) collective-permute-start(bf16[16,2048]{1,0:T(8,128)(2,1)S(1)} %get-tuple-element.77), channel_id=1, source_target_pairs={{0,8},{4,12},{8,0},{12,4},{1,9},{5,13},{9,1},{13,5},{2,10},{6,14},... | collective-permute-start | bytes 196616 | tf_op jit(solution)/shard_map/ppermute | solution.py:273
  57.9 1.4 %collective-permute-start.24 = (bf16[16,2048]{1,0:T(8,128)(2,1)S(1)}, bf16[16,2048]{1,0:T(8,128)(2,1)S(1)}, u32[]{:S(2)}, u32[]{:S(2)}) collective-permute-start(bf16[16,2048]{1,0:T(8,128)(2,1)S(1)} %get-tuple-element.78), channel_id=1, source_target_pairs={{0,12},{4,8},{8,4},{12,0},{1,13},{5,9},{9,5},{13,1},{2,14},{6,10},... | collective-permute-start | bytes 196616 | tf_op jit(solution)/shard_map/ppermute | solution.py:273
  59.4 1.5 %shard_map.103 = (f32[512,768]{1,0:T(8,128)}, f32[8,128]{1,0:T(8,128)S(1)}) custom-call(bf16[128,512]{1,0:T(8,128)(2,1)S(1)} %get-tuple-element.82.refs_0_, bf16[128,768]{1,0:T(8,128)(2,1)S(1)} %get-tuple-element.83.refs_1_, bf16[128,512]{1,0:T(8,128)(2,1)S(1)} %collective-permute-done.27.refs_2_, bf16[128,768]{1,0:T(8,128)(2,1)S(1)} %collective-permute-done.28.refs_3_), custom_call_target="tpu_custom_call" | custom-call | tf_op jit(solution)/shard_map/pallas_call | solution.py:39
  60.9 1.2 %shard_map.104 = (bf16[256,2048]{1,0:T(8,128)(2,1)}, f32[8,128]{1,0:T(8,128)S(1)}) custom-call(bf16[256,64]{1,0:T(8,128)(2,1)S(1)} %get-tuple-element.47.refs_0_, bf16[16,2048]{1,0:T(8,128)(2,1)S(1)} %get-tuple-element.79.refs_1_, bf16[16,2048]{1,0:T(8,128)(2,1)S(1)} %collective-permute-done.20.refs_4_.refs_2_, ...), custom_call_target="tpu_custom_call" | custom-call | tf_op jit(solution)/shard_map/pallas_call | solution.py:39
  62.1 2.3 %collective-permute-done.23.refs_4_ = bf16[16,2048]{1,0:T(8,128)(2,1)S(1)} collective-permute-done((bf16[16,2048]{1,0:T(8,128)(2,1)S(1)}, bf16[16,2048]{1,0:T(8,128)(2,1)S(1)}, u32[]{:S(2)}, u32[]{:S(2)}) %collective-permute-start.23) | collective-permute-done | bytes 65568 | tf_op jit(solution)/shard_map/ppermute | solution.py:273
  64.4 1.3 %shard_map.105 = bf16[256,2048]{1,0:T(8,128)(2,1)} custom-call(bf16[256,64]{1,0:T(8,128)(2,1)S(1)} %get-tuple-element.47.refs_0_, f32[64,128]{1,0:T(8,128)S(1)} %get-tuple-element.48.refs_1_, bf16[16,2048]{1,0:T(8,128)(2,1)S(1)} %get-tuple-element.75.refs_2_, bf16[16,2048]{1,0:T(8,128)(2,1)S(1)} %collective-permute-done.22.refs_3_, ...), custom_call_target="tpu_custom_call" | custom-call | tf_op jit(solution)/shard_map/pallas_call | solution.py:39
  (26 shorter events, 0.1 us)
Async XLA Ops:
  0.6 6.7 %collective-permute-start = (bf16[512,1536]{1,0:T(8,128)(2,1)}, bf16[512,1536]{1,0:T(8,128)(2,1)S(1)}, u32[]{:S(2)}, u32[]{:S(2)}) collective-permute-start(bf16[512,1536]{1,0:T(8,128)(2,1)} %bitcast.5), channel_id=1, source_target_pairs={{0,1},{1,0},{2,3},{3,2},{4,5},{5,4},{6,7},{7,6},{8,9},{9,8},{10,11... | collective-permute-start | bytes 4718600 | tf_op jit(solution)/shard_map/ppermute | solution.py:260
  1.1 6.2 %collective-permute-start.1 = (bf16[512,768]{1,0:T(8,128)(2,1)}, bf16[512,768]{1,0:T(8,128)(2,1)S(1)}, u32[]{:S(2)}, u32[]{:S(2)}) collective-permute-start(bf16[512,768]{1,0:T(8,128)(2,1)} %bitcast.9), channel_id=1, source_target_pairs={{0,1},{1,0},{2,3},{3,2},{4,5},{5,4},{6,7},{7,6},{8,9},{9,8},{10,11... | collective-permute-start | bytes 2359304 | tf_op jit(solution)/shard_map/ppermute | solution.py:260
  2.4 23.7 %copy-start = (bf16[1,512,1536]{2,1,0:T(8,128)(2,1)S(1)}, bf16[1,512,1536]{2,1,0:T(8,128)(2,1)}, u32[]{:S(2)}) copy-start(bf16[1,512,1536]{2,1,0:T(8,128)(2,1)} %param.12) | copy-start | bytes 4718596
  2.4 10.1 %collective-permute-start.5 = (bf16[512,256]{1,0:T(8,128)(2,1)S(1)}, bf16[512,256]{1,0:T(8,128)(2,1)S(1)}, u32[]{:S(2)}, u32[]{:S(2)}) collective-permute-start(bf16[512,256]{1,0:T(8,128)(2,1)S(1)} %get-tuple-element.46.refs_5_), channel_id=1, source_target_pairs={{0,2},{1,3},{2,0},{3,1},{4,6},{5,7},{6,4},{7,5},{8,10},{9,11},{10,... | collective-permute-start | bytes 786440 | tf_op jit(solution)/shard_map/ppermute | solution.py:264
  7.3 5.3 %collective-permute-start.2 = (bf16[32,2048]{1,0:T(8,128)(2,1)S(1)}, bf16[32,2048]{1,0:T(8,128)(2,1)S(1)}, u32[]{:S(2)}, u32[]{:S(2)}) collective-permute-start(bf16[32,2048]{1,0:T(8,128)(2,1)S(1)} %get-tuple-element.54), channel_id=1, source_target_pairs={{0,4},{4,0},{8,12},{12,8},{1,5},{5,1},{9,13},{13,9},{2,6},{6,2},{1... | collective-permute-start | bytes 393224 | tf_op jit(solution)/shard_map/ppermute | solution.py:273
  9.0 9.5 %collective-permute-start.7 = (bf16[512,256]{1,0:T(8,128)(2,1)S(1)}, bf16[512,256]{1,0:T(8,128)(2,1)S(1)}, u32[]{:S(2)}, u32[]{:S(2)}) collective-permute-start(bf16[512,256]{1,0:T(8,128)(2,1)S(1)} %get-tuple-element.61), channel_id=1, source_target_pairs={{0,2},{1,3},{2,0},{3,1},{4,6},{5,7},{6,4},{7,5},{8,10},{9,11},{10,... | collective-permute-start | bytes 786440 | tf_op jit(solution)/shard_map/ppermute | solution.py:264
  10.0 22.8 %copy-start.1 = (bf16[1,512,768]{2,1,0:T(8,128)(2,1)S(1)}, bf16[1,512,768]{2,1,0:T(8,128)(2,1)}, u32[]{:S(2)}) copy-start(bf16[1,512,768]{2,1,0:T(8,128)(2,1)} %param.13) | copy-start | bytes 2359300
  10.0 13.2 %collective-permute-start.8 = (bf16[512,256]{1,0:T(8,128)(2,1)S(1)}, bf16[512,256]{1,0:T(8,128)(2,1)S(1)}, u32[]{:S(2)}, u32[]{:S(2)}) collective-permute-start(bf16[512,256]{1,0:T(8,128)(2,1)S(1)} %get-tuple-element.62), channel_id=1, source_target_pairs={{0,2},{1,3},{2,0},{3,1},{4,6},{5,7},{6,4},{7,5},{8,10},{9,11},{10,... | collective-permute-start | bytes 786440 | tf_op jit(solution)/shard_map/ppermute | solution.py:264
  12.6 13.5 %collective-permute-start.6 = (bf16[512,256]{1,0:T(8,128)(2,1)S(1)}, bf16[512,256]{1,0:T(8,128)(2,1)S(1)}, u32[]{:S(2)}, u32[]{:S(2)}) collective-permute-start(bf16[512,256]{1,0:T(8,128)(2,1)S(1)} %collective-permute-done.5.refs_2_.refs_5_), channel_id=1, source_target_pairs={{0,16},{16,0},{1,17},{17,1},{2,18},{18,2},{3,19},{19,3},{4,20},{20... | collective-permute-start | bytes 786440 | tf_op jit(solution)/shard_map/ppermute | solution.py:269
  14.6 11.5 %collective-permute-start.3 = (bf16[32,2048]{1,0:T(8,128)(2,1)S(1)}, bf16[32,2048]{1,0:T(8,128)(2,1)S(1)}, u32[]{:S(2)}, u32[]{:S(2)}) collective-permute-start(bf16[32,2048]{1,0:T(8,128)(2,1)S(1)} %get-tuple-element.55), channel_id=1, source_target_pairs={{0,8},{4,12},{8,0},{12,4},{1,9},{5,13},{9,1},{13,5},{2,10},{6,14},... | collective-permute-start | bytes 393224 | tf_op jit(solution)/shard_map/ppermute | solution.py:273
  17.2 8.9 %collective-permute-start.4 = (bf16[32,2048]{1,0:T(8,128)(2,1)S(1)}, bf16[32,2048]{1,0:T(8,128)(2,1)S(1)}, u32[]{:S(2)}, u32[]{:S(2)}) collective-permute-start(bf16[32,2048]{1,0:T(8,128)(2,1)S(1)} %get-tuple-element.56), channel_id=1, source_target_pairs={{0,12},{4,8},{8,4},{12,0},{1,13},{5,9},{9,5},{13,1},{2,14},{6,10},... | collective-permute-start | bytes 393224 | tf_op jit(solution)/shard_map/ppermute | solution.py:273
  18.5 16.2 %collective-permute-start.12 = (bf16[512,256]{1,0:T(8,128)(2,1)S(1)}, bf16[512,256]{1,0:T(8,128)(2,1)S(1)}, u32[]{:S(2)}, u32[]{:S(2)}) collective-permute-start(bf16[512,256]{1,0:T(8,128)(2,1)S(1)} %collective-permute-done.7.refs_3_.refs_6_), channel_id=1, source_target_pairs={{0,16},{16,0},{1,17},{17,1},{2,18},{18,2},{3,19},{19,3},{4,20},{20... | collective-permute-start | bytes 786440 | tf_op jit(solution)/shard_map/ppermute | solution.py:269
  23.2 12.1 %collective-permute-start.9 = (bf16[512,256]{1,0:T(8,128)(2,1)S(1)}, bf16[512,256]{1,0:T(8,128)(2,1)S(1)}, u32[]{:S(2)}, u32[]{:S(2)}) collective-permute-start(bf16[512,256]{1,0:T(8,128)(2,1)S(1)} %collective-permute-done.8.refs_4_.refs_7_), channel_id=1, source_target_pairs={{0,16},{16,0},{1,17},{17,1},{2,18},{18,2},{3,19},{19,3},{4,20},{20... | collective-permute-start | bytes 786440 | tf_op jit(solution)/shard_map/ppermute | solution.py:269
  26.1 11.7 %collective-permute-start.14 = (bf16[512,256]{1,0:T(8,128)(2,1)S(1)}, bf16[512,256]{1,0:T(8,128)(2,1)S(1)}, u32[]{:S(2)}, u32[]{:S(2)}) collective-permute-start(bf16[512,256]{1,0:T(8,128)(2,1)S(1)} %collective-permute-done.7.refs_3_.refs_6_), channel_id=1, source_target_pairs={{0,1},{1,0},{2,3},{3,2},{4,5},{5,4},{6,7},{7,6},{8,9},{9,8},{10,11... | collective-permute-start | bytes 786440 | tf_op jit(solution)/shard_map/ppermute | solution.py:260
  26.8 6.0 %collective-permute-start.10 = (bf16[64,1024]{1,0:T(8,128)(2,1)S(1)}, bf16[64,1024]{1,0:T(8,128)(2,1)S(1)}, u32[]{:S(2)}, u32[]{:S(2)}) collective-permute-start(bf16[64,1024]{1,0:T(8,128)(2,1)S(1)} %get-tuple-element.64), channel_id=1, source_target_pairs={{0,2},{1,3},{2,0},{3,1},{4,6},{5,7},{6,4},{7,5},{8,10},{9,11},{10,... | collective-permute-start | bytes 393224 | tf_op jit(solution)/shard_map/ppermute | solution.py:264
  33.1 4.7 %collective-permute-start.11 = (bf16[64,768]{1,0:T(8,128)(2,1)S(1)}, bf16[64,768]{1,0:T(8,128)(2,1)S(1)}, u32[]{:S(2)}, u32[]{:S(2)}) collective-permute-start(bf16[64,768]{1,0:T(8,128)(2,1)S(1)} %get-tuple-element.66), channel_id=1, source_target_pairs={{0,2},{1,3},{2,0},{3,1},{4,6},{5,7},{6,4},{7,5},{8,10},{9,11},{10,... | collective-permute-start | bytes 294920 | tf_op jit(solution)/shard_map/ppermute | solution.py:264
  34.7 3.6 %collective-permute-start.17 = (bf16[512,256]{1,0:T(8,128)(2,1)S(1)}, bf16[512,256]{1,0:T(8,128)(2,1)S(1)}, u32[]{:S(2)}, u32[]{:S(2)}) collective-permute-start(bf16[512,256]{1,0:T(8,128)(2,1)S(1)} %collective-permute-done.12.refs_6_.refs_9_), channel_id=1, source_target_pairs={{0,1},{1,0},{2,3},{3,2},{4,5},{5,4},{6,7},{7,6},{8,9},{9,8},{10,11... | collective-permute-start | bytes 786440 | tf_op jit(solution)/shard_map/ppermute | solution.py:260
  34.7 3.6 %collective-permute-start.13 = (bf16[512,256]{1,0:T(8,128)(2,1)S(1)}, bf16[512,256]{1,0:T(8,128)(2,1)S(1)}, u32[]{:S(2)}, u32[]{:S(2)}) collective-permute-start(bf16[512,256]{1,0:T(8,128)(2,1)S(1)} %collective-permute-done.5.refs_2_.refs_5_), channel_id=1, source_target_pairs={{0,1},{1,0},{2,3},{3,2},{4,5},{5,4},{6,7},{7,6},{8,9},{9,8},{10,11... | collective-permute-start | bytes 786440 | tf_op jit(solution)/shard_map/ppermute | solution.py:260
  35.2 3.1 %collective-permute-start.16 = (bf16[512,256]{1,0:T(8,128)(2,1)S(1)}, bf16[512,256]{1,0:T(8,128)(2,1)S(1)}, u32[]{:S(2)}, u32[]{:S(2)}) collective-permute-start(bf16[512,256]{1,0:T(8,128)(2,1)S(1)} %collective-permute-done.6.refs_6_.refs_5_.refs_8_), channel_id=1, source_target_pairs={{0,1},{1,0},{2,3},{3,2},{4,5},{5,4},{6,7},{7,6},{8,9},{9,8},{10,11... | collective-permute-start | bytes 786440 | tf_op jit(solution)/shard_map/ppermute | solution.py:260
  37.8 1.5 %collective-permute-start.15 = (bf16[512,256]{1,0:T(8,128)(2,1)S(1)}, bf16[512,256]{1,0:T(8,128)(2,1)S(1)}, u32[]{:S(2)}, u32[]{:S(2)}) collective-permute-start(bf16[512,256]{1,0:T(8,128)(2,1)S(1)} %collective-permute-done.8.refs_4_.refs_7_), channel_id=1, source_target_pairs={{0,1},{1,0},{2,3},{3,2},{4,5},{5,4},{6,7},{7,6},{8,9},{9,8},{10,11... | collective-permute-start | bytes 786440 | tf_op jit(solution)/shard_map/ppermute | solution.py:260
  37.8 1.9 %collective-permute-start.18 = (bf16[512,256]{1,0:T(8,128)(2,1)S(1)}, bf16[512,256]{1,0:T(8,128)(2,1)S(1)}, u32[]{:S(2)}, u32[]{:S(2)}) collective-permute-start(bf16[512,256]{1,0:T(8,128)(2,1)S(1)} %collective-permute-done.9.refs_7_.refs_10_), channel_id=1, source_target_pairs={{0,1},{1,0},{2,3},{3,2},{4,5},{5,4},{6,7},{7,6},{8,9},{9,8},{10,11... | collective-permute-start | bytes 786440 | tf_op jit(solution)/shard_map/ppermute | solution.py:260
  40.5 5.4 %collective-permute-start.19 = (bf16[64,768]{1,0:T(8,128)(2,1)S(1)}, bf16[64,768]{1,0:T(8,128)(2,1)S(1)}, u32[]{:S(2)}, u32[]{:S(2)}) collective-permute-start(bf16[64,768]{1,0:T(8,128)(2,1)S(1)} %get-tuple-element.69.refs_0_.refs_2_), channel_id=1, source_target_pairs={{0,2},{1,3},{2,0},{3,1},{4,6},{5,7},{6,4},{7,5},{8,10},{9,11},{10,... | collective-permute-start | bytes 294920 | tf_op jit(solution)/shard_map/ppermute | solution.py:264
  44.0 4.3 %collective-permute-start.20 = (bf16[16,2048]{1,0:T(8,128)(2,1)S(1)}, bf16[16,2048]{1,0:T(8,128)(2,1)S(1)}, u32[]{:S(2)}, u32[]{:S(2)}) collective-permute-start(bf16[16,2048]{1,0:T(8,128)(2,1)S(1)} %get-tuple-element.72), channel_id=1, source_target_pairs={{0,4},{4,0},{8,12},{12,8},{1,5},{5,1},{9,13},{13,9},{2,6},{6,2},{1... | collective-permute-start | bytes 196616 | tf_op jit(solution)/shard_map/ppermute | solution.py:273
  45.9 12.0 %collective-permute-start.28 = (bf16[128,768]{1,0:T(8,128)(2,1)S(1)}, bf16[128,768]{1,0:T(8,128)(2,1)S(1)}, u32[]{:S(2)}, u32[]{:S(2)}) collective-permute-start(bf16[128,768]{1,0:T(8,128)(2,1)S(1)} %get-tuple-element.83.refs_1_), channel_id=1, source_target_pairs={{0,1},{1,0},{2,3},{3,2},{4,5},{5,4},{6,7},{7,6},{8,9},{9,8},{10,11... | collective-permute-start | bytes 589832 | tf_op jit(solution)/shard_map/ppermute | solution.py:260
  49.0 5.0 %collective-permute-start.21 = (bf16[64,1024]{1,0:T(8,128)(2,1)S(1)}, bf16[64,1024]{1,0:T(8,128)(2,1)S(1)}, u32[]{:S(2)}, u32[]{:S(2)}) collective-permute-start(bf16[64,1024]{1,0:T(8,128)(2,1)S(1)} %get-tuple-element.74), channel_id=1, source_target_pairs={{0,2},{1,3},{2,0},{3,1},{4,6},{5,7},{6,4},{7,5},{8,10},{9,11},{10,... | collective-permute-start | bytes 393224 | tf_op jit(solution)/shard_map/ppermute | solution.py:264
  49.6 6.3 %collective-permute-start.27 = (bf16[128,512]{1,0:T(8,128)(2,1)S(1)}, bf16[128,512]{1,0:T(8,128)(2,1)S(1)}, u32[]{:S(2)}, u32[]{:S(2)}) collective-permute-start(bf16[128,512]{1,0:T(8,128)(2,1)S(1)} %get-tuple-element.84), channel_id=1, source_target_pairs={{0,1},{1,0},{2,3},{3,2},{4,5},{5,4},{6,7},{7,6},{8,9},{9,8},{10,11... | collective-permute-start | bytes 393224 | tf_op jit(solution)/shard_map/ppermute | solution.py:260
  49.6 11.3 %collective-permute-start.25 = (bf16[16,2048]{1,0:T(8,128)(2,1)S(1)}, bf16[16,2048]{1,0:T(8,128)(2,1)S(1)}, u32[]{:S(2)}, u32[]{:S(2)}) collective-permute-start(bf16[16,2048]{1,0:T(8,128)(2,1)S(1)} %get-tuple-element.80), channel_id=1, source_target_pairs={{0,8},{4,12},{8,0},{12,4},{1,9},{5,13},{9,1},{13,5},{2,10},{6,14},... | collective-permute-start | bytes 196616 | tf_op jit(solution)/shard_map/ppermute | solution.py:273
  53.1 7.8 %collective-permute-start.26 = (bf16[16,2048]{1,0:T(8,128)(2,1)S(1)}, bf16[16,2048]{1,0:T(8,128)(2,1)S(1)}, u32[]{:S(2)}, u32[]{:S(2)}) collective-permute-start(bf16[16,2048]{1,0:T(8,128)(2,1)S(1)} %get-tuple-element.81), channel_id=1, source_target_pairs={{0,12},{4,8},{8,4},{12,0},{1,13},{5,9},{9,5},{13,1},{2,14},{6,10},... | collective-permute-start | bytes 196616 | tf_op jit(solution)/shard_map/ppermute | solution.py:273
  54.1 8.1 %collective-permute-start.22 = (bf16[16,2048]{1,0:T(8,128)(2,1)S(1)}, bf16[16,2048]{1,0:T(8,128)(2,1)S(1)}, u32[]{:S(2)}, u32[]{:S(2)}) collective-permute-start(bf16[16,2048]{1,0:T(8,128)(2,1)S(1)} %get-tuple-element.76), channel_id=1, source_target_pairs={{0,4},{4,0},{8,12},{12,8},{1,5},{5,1},{9,13},{13,9},{2,6},{6,2},{1... | collective-permute-start | bytes 196616 | tf_op jit(solution)/shard_map/ppermute | solution.py:273
  55.9 8.5 %collective-permute-start.23 = (bf16[16,2048]{1,0:T(8,128)(2,1)S(1)}, bf16[16,2048]{1,0:T(8,128)(2,1)S(1)}, u32[]{:S(2)}, u32[]{:S(2)}) collective-permute-start(bf16[16,2048]{1,0:T(8,128)(2,1)S(1)} %get-tuple-element.77), channel_id=1, source_target_pairs={{0,8},{4,12},{8,0},{12,4},{1,9},{5,13},{9,1},{13,5},{2,10},{6,14},... | collective-permute-start | bytes 196616 | tf_op jit(solution)/shard_map/ppermute | solution.py:273
  57.9 6.5 %collective-permute-start.24 = (bf16[16,2048]{1,0:T(8,128)(2,1)S(1)}, bf16[16,2048]{1,0:T(8,128)(2,1)S(1)}, u32[]{:S(2)}, u32[]{:S(2)}) collective-permute-start(bf16[16,2048]{1,0:T(8,128)(2,1)S(1)} %get-tuple-element.78), channel_id=1, source_target_pairs={{0,12},{4,8},{8,4},{12,0},{1,13},{5,9},{9,5},{13,1},{2,14},{6,10},... | collective-permute-start | bytes 196616 | tf_op jit(solution)/shard_map/ppermute | solution.py:273

commit v9 on v6

v9 whole, which is shorter than its diff:
```python
import jax
import jax.numpy as jnp
from jax import lax
from jax.experimental import pallas as pl
from jax.experimental.pallas import tpu as pltpu
from jax.sharding import PartitionSpec as P

EXPERTS = 128
CORES = 2
VMEM = 40 * 1024 * 1024
F32 = jnp.float32
BF16 = jnp.bfloat16


def product(left, right, left_dim, right_dim, **kw):
    return lax.dot_general(
        left, right, (((left_dim,), (right_dim,)), ((), ())), preferred_element_type=F32, **kw
    )


def call(body, out_shape, args, far=0, cost=0, after=(), token=False, **kw):
    out_shape = [*out_shape] + [shape((8, 128), F32)] * token
    specs = [pl.BlockSpec(memory_space=pltpu.VMEM)] * (len(args) - far)
    specs += [pl.BlockSpec(memory_space=pltpu.HBM)] * far
    specs += [pl.BlockSpec(memory_space=pl.ANY)] * len(after)
    kw.setdefault("out_specs", [pl.BlockSpec(memory_space=pltpu.VMEM)] * len(out_shape))
    args = [
        pltpu.with_memory_space_constraint(arg, pltpu.HBM) if i >= len(args) - far else arg
        for i, arg in enumerate(args)
    ]
    count, first, last = len(args), len(args) + len(after), len(args) + len(after) + len(out_shape)

    def kernel(*refs):
        if token:
            refs[last - 1][...] = jnp.zeros(refs[last - 1].shape, F32)
        body(*refs[:count], *refs[first : last - token], *refs[last:])

    return pl.pallas_call(
        kernel,
        out_shape=out_shape,
        in_specs=specs,
        compiler_params=pltpu.CompilerParams(vmem_limit_bytes=VMEM),
        cost_estimate=pl.CostEstimate(flops=cost, bytes_accessed=0, transcendentals=0),
        **kw,
    )(*args, *after)


def shape(dims, kind=BF16):
    return jax.ShapeDtypeStruct(dims, kind)


def columns(k, part):
    return pl.ds(pl.multiple_of((lax.axis_index("fsdp") ^ k) * part, part), part)


def slot_kernel(spread, *refs):
    sources, rows_out, grads_out, refs = refs[:5], refs[5 : 5 + spread], refs[5 + spread : 5 + 2 * spread], refs[5 + 2 * spread :]
    turned_out, gate_out, ids, gates, order, tok, cot, sems = refs
    parts = spread * CORES
    copies = [
        pltpu.make_async_copy(source, target, sems.at[i])
        for i, (source, target) in enumerate(zip(sources, (ids, gates, order, tok, cot)))
    ]
    for copy in copies:
        copy.start()
    for copy in copies[:3]:
        copy.wait()
    choices, count = ids.shape
    slots = gate_out.shape[0]
    groups = lax.axis_size("expert")
    capacity = slots // groups
    part = tok.shape[1] // parts
    slot = lax.broadcasted_iota(jnp.int32, (slots, count), 0)
    wanted = ((slot // capacity) ^ lax.axis_index("expert")) * (EXPERTS // groups)
    routed = jnp.zeros((slots, count), F32)
    gate = jnp.zeros((slots, count), F32)
    for k in range(choices):
        hit = ids[k : k + 1, :] == wanted
        routed = jnp.where(hit, 1.0, routed)
        gate = jnp.where(hit, gates[k : k + 1, :], gate)
    row = lax.broadcasted_iota(jnp.int32, (count, count), 0)
    col = lax.broadcasted_iota(jnp.int32, (count, count), 1)
    served = jnp.where(order[...] == row, 1.0, 0.0).astype(BF16)
    earlier = jnp.where(row < col, 1.0, 0.0).astype(BF16)
    by_rank = product(routed.astype(BF16), served, 1, 0)
    before = product(by_rank.astype(BF16), earlier, 1, 0)
    taken = jnp.where(before.astype(jnp.int32) == slot % capacity, by_rank, 0.0).astype(BF16)
    pick = product(taken, served, 1, 1)
    turned_out[...] = product(served, taken, 1, 1).astype(BF16)
    slot_gate = jnp.sum(pick * gate, axis=1, keepdims=True)
    gate_out[...] = jnp.broadcast_to(slot_gate, gate_out.shape)
    pick = pick.astype(BF16)
    for copy, source, scale, outs in (
        (copies[3], tok, None, rows_out),
        (copies[4], cot, slot_gate, grads_out),
    ):
        copy.wait()
        for k in reversed(range(parts)):
            value = product(pick, source[:, columns(k, part)], 1, 0)
            value = value if scale is None else scale * value
            to = pl.ds((k % CORES) * part, part)
            outs[k // CORES][:, to] = value.astype(BF16)


def join_kernel(groups, spread, capacity, *refs):
    by_x, chunks = refs[:spread], refs[spread:]
    half = by_x[0].shape[1]
    for ke in range(groups):
        for kx in range(spread):
            chunks[ke][:, kx * half : (kx + 1) * half] = by_x[kx][
                ke * capacity : (ke + 1) * capacity
            ]


def far_kernel(groups, spread, capacity, *refs):
    by_e, by_x = refs[:groups], refs[groups:]
    for ke in range(groups):
        for kx in range(1, spread):
            by_x[kx - 1][ke * capacity : (ke + 1) * capacity] = by_e[ke][
                kx * capacity : (kx + 1) * capacity
            ]


def partial(groups, spread, refs, outs):
    chunks, (own, sib) = refs[:groups], refs[groups:]
    part = own.shape[0]
    half = CORES * part
    rows = jnp.concatenate(
        [c[:, kx * half : (kx + 1) * half] for kx in range(spread) for c in chunks], axis=0
    )
    total = product(rows[:, :part], own[...], 1, 0) + product(rows[:, part:], sib[...], 1, 0)
    slots = rows.shape[0] // spread
    for kx in range(spread):
        outs[kx][...] = total[kx * slots : (kx + 1) * slots].astype(outs[kx].dtype)
    return rows


def pre_kernel(groups, spread, *refs):
    partial(groups, spread, refs[: groups + 2], refs[groups + 2 :])


def back_kernel(groups, spread, *refs):
    own, sib, *outs = refs[groups + 2 :]
    rows = partial(groups, spread, refs[: groups + 2], outs)
    part = own.shape[1]
    own[...] = rows[:, :part]
    sib[...] = rows[:, part:]


def summed(refs):
    total = refs[0][...]
    for ref in refs[1:]:
        total += ref[...].astype(F32)
    return total


def hidden_kernel(*refs):
    pre, out = summed(refs[:-1]), refs[-1]
    feed = out.shape[1]
    gate_act, up_act = pre[:, :feed], pre[:, feed:]
    out[...] = (gate_act * (1.0 / (1.0 + jnp.exp(-gate_act))) * up_act).astype(BF16)


def d_pre_kernel(*refs):
    spread = len(refs) // 2
    pre, back, out = summed(refs[:spread]), summed(refs[spread:-1]), refs[-1]
    feed = back.shape[1]
    gate_act, up_act = pre[:, :feed], pre[:, feed:]
    sig = 1.0 / (1.0 + jnp.exp(-gate_act))
    out[:, :feed] = (back * up_act * (sig * (1.0 + gate_act * (1.0 - sig)))).astype(BF16)
    out[:, feed:] = (back * (gate_act * sig)).astype(BF16)


def width_product(left, weights, store):
    rows = jnp.concatenate([r[...] for r in left], axis=0)
    for kc, weight in enumerate(weights):
        store(kc, product(rows, weight[...], 1, 1).astype(BF16))


def expert_out_kernel(groups, spread, capacity, *refs):
    chunks = refs[-groups:]
    part = refs[spread].shape[0]

    def store(kc, value):
        for ke in range(groups):
            for kx in range(spread):
                at = (kx * groups + ke) * capacity
                chunks[ke][kx * capacity : (kx + 1) * capacity, kc * part : (kc + 1) * part] = value[
                    at : at + capacity
                ]

    width_product(refs[:spread], refs[spread : spread + CORES], store)


def d_rows_kernel(spread, *refs):
    outs = refs[-spread:]
    part = refs[spread].shape[0]
    slots = outs[0].shape[0]

    def store(kc, value):
        for kx in range(spread):
            outs[kx][:, kc * part : (kc + 1) * part] = value[kx * slots : (kx + 1) * slots]

    width_product(refs[:spread], refs[spread : spread + CORES], store)


def weight_kernel(spread, own, sib, *refs):
    hidden, sib_hidden, out = refs[:spread], refs[spread:-1], refs[-1]
    left = jnp.concatenate([own[...], sib[...]], axis=0)
    right = jnp.concatenate([r[...] for r in (*hidden, *sib_hidden)], axis=0)
    out[...] = product(left, right, 0, 0)


def scatter(turned, groups_of_rows, out, held, sems):
    part = held.shape[2]
    copies = []
    for k, rows in enumerate(groups_of_rows):
        held[k] = product(turned, rows, 1, 0).astype(BF16)
        copies.append(pltpu.make_async_copy(held.at[k], out.at[:, columns(k, part)], sems.at[k]))
        copies[-1].start()
    for copy in copies:
        copy.wait()


def combine_kernel(groups, parts, capacity, turned, gate, *refs):
    chunks, far, (out, held, sems) = refs[:groups], refs[groups:-3], refs[-3:]
    part = held.shape[2]

    def weighted(k):
        cols = slice((k % CORES) * part, (k % CORES + 1) * part)
        if k < CORES:
            rows = jnp.concatenate([c[:capacity, cols] for c in chunks], axis=0)
        else:
            rows = far[k // CORES - 1][:, cols]
        rows = rows.astype(F32) * gate[:, :1]
        high = rows.astype(BF16)
        return jnp.concatenate([high, (rows - high.astype(F32)).astype(BF16)], axis=0)

    twice = jnp.concatenate([turned[...], turned[...]], axis=1)
    scatter(twice, map(weighted, range(parts)), out, held, sems)


def d_tokens_kernel(groups, parts, turned, *refs):
    chunks, (out, held, sems) = refs[:groups], refs[groups:]
    part = held.shape[2]
    rows = (
        jnp.concatenate([c[:, k * part : (k + 1) * part] for c in chunks], axis=0)
        for k in range(parts)
    )
    scatter(turned[...], rows, out, held, sems)


def per_device(tokens, cotangent, route_ids, route_gates, served_order, w_in, w_out):
    groups = lax.axis_size("expert")
    parts = lax.axis_size("fsdp")
    spread = parts // CORES
    count, width = tokens.shape
    capacity = count * route_ids.shape[1] // EXPERTS
    feed = w_out.shape[2]
    slots = groups * capacity
    half = width // spread
    part = width // parts

    def bound(kernel, *sizes):
        return lambda *refs: kernel(*sizes, *refs)

    def to_core(value):
        return lax.ppermute(value, "fsdp", [(i, i ^ 1) for i in range(parts)])

    def to_x(values):
        return [
            lax.ppermute(value, "fsdp", [(i, i ^ ((k + 1) * CORES)) for i in range(parts)])
            for k, value in enumerate(values)
        ]

    def to_expert(chunks):
        return [
            lax.ppermute(value, "expert", [(i, i ^ ke) for i in range(groups)]) if ke else value
            for ke, value in enumerate(chunks)
        ]

    chunk = [shape((capacity, width))] * groups
    by_x = [shape((slots, half))] * spread
    in_own, out_own = w_in[0], w_out[0]
    in_sib, out_sib = to_core(in_own), to_core(out_own)
    outs = call(
        bound(slot_kernel, spread),
        by_x * 2 + [shape((count, slots)), shape((slots, 128), F32)],
        (route_ids.T, route_gates.T, served_order, tokens, cotangent),
        far=5,
        scratch_shapes=[
            pltpu.VMEM(route_ids.shape[::-1], jnp.int32),
            pltpu.VMEM(route_gates.shape[::-1], F32),
            pltpu.VMEM(served_order.shape, jnp.int32),
            pltpu.VMEM(tokens.shape, BF16),
            pltpu.VMEM(cotangent.shape, BF16),
            pltpu.SemaphoreType.DMA((5,)),
        ],
    )
    turned, gate = outs[-2:]
    rows = [outs[0], *to_x(outs[1:spread])]
    grads = [outs[spread], *to_x(outs[spread + 1 : 2 * spread])]
    rows, in_sib, out_sib = lax.optimization_barrier((rows, in_sib, out_sib))
    join = bound(join_kernel, groups, spread, capacity)
    rows = to_expert(call(join, chunk, rows))
    grads = to_expert(call(join, chunk, grads))
    pre, *pre_far = call(
        bound(pre_kernel, groups, spread),
        [shape((slots, 2 * feed), F32)] + [shape((slots, 2 * feed))] * (spread - 1),
        (*rows, in_own, in_sib),
    )
    pre = (pre, *to_x(pre_far))
    (hidden,) = call(hidden_kernel, [shape((slots, feed))], pre)
    hidden = (hidden, *to_x([hidden] * (spread - 1)))
    own_grads, sib_grads, back, *back_far = call(
        bound(back_kernel, groups, spread),
        [shape((spread * slots, part))] * 2
        + [shape((slots, feed), F32)]
        + [shape((slots, feed))] * (spread - 1),
        (*grads, out_own, out_sib),
        after=hidden[:1],
    )
    back = (back, *to_x(back_far))
    expert_out = to_expert(
        call(
            bound(expert_out_kernel, groups, spread, capacity),
            [shape((spread * capacity, half))] * groups,
            (*hidden, out_own, out_sib),
        )
    )
    (d_pre,) = call(
        d_pre_kernel, [shape((slots, 2 * feed))], (*pre, *back), after=expert_out[:1]
    )
    d_pre = (d_pre, *to_x([d_pre] * (spread - 1)))
    near, *far = call(bound(d_rows_kernel, spread), by_x, (*d_pre, in_own, in_sib))
    d_rows = to_expert(call(join, chunk, (near, *to_x(far))))
    far = to_x(
        call(bound(far_kernel, groups, spread, capacity), by_x[1:], expert_out)
    )
    d_w_out, token = call(
        bound(weight_kernel, spread),
        [shape((part, feed), F32)],
        (own_grads, to_core(sib_grads), *hidden, *[to_core(value) for value in hidden]),
        token=True,
    )

    def scattered(kernel, operands, **kw):
        return call(
            kernel,
            [shape((count, width))],
            operands,
            out_specs=[pl.BlockSpec(memory_space=pltpu.HBM)]
            + [pl.BlockSpec(memory_space=pltpu.VMEM)] * kw.get("token", False),
            scratch_shapes=[
                pltpu.VMEM((parts, count, part), BF16),
                pltpu.SemaphoreType.DMA((parts,)),
            ],
            **kw,
        )

    combined, token = scattered(
        bound(combine_kernel, groups, parts, capacity),
        (turned, gate, *expert_out, *far),
        after=(token,),
        token=True,
    )
    (d_tokens,) = scattered(
        bound(d_tokens_kernel, groups, parts), (turned, *d_rows), after=(token,)
    )
    return combined, d_tokens, d_w_out[None]


def solution(mesh):
    rows = P(("replica", "expert", "fsdp"), None)
    weights = P("expert", "fsdp", None)
    return jax.shard_map(
        per_device,
        mesh=mesh,
        in_specs=(rows,) * 5 + (weights,) * 2,
        out_specs=(rows, rows, P(("replica", "expert"), "fsdp", None)),
        check_vma=False,
    )
```

time: 80 us -> 63 us (0.79)
  waiting for transfers between devices: 44.2 us -> 22 us
  starting transfers between devices: 25 us -> 31.1 us
    ppermute x6 -> x8, waiting for transfers between devices: 21.1 us -> 9.84 us  [to_x(): lax.ppermute(value, 'fsdp', [(i, i ^ (k + 1) * CORES) for i in range(part...]
    ppermute x11 -> x12, waiting for transfers between devices: 23.1 us -> 12.1 us  [to_expert(): lax.ppermute(value, 'expert', [(i, i ^ ke) for i in range(groups)])]
    ppermute x6 -> x8, starting transfers between devices: 6.84 us -> 13.5 us  [to_x(): lax.ppermute(value, 'fsdp', [(i, i ^ (k + 1) * CORES) for i in range(part...]
    pallas_call x13 -> x14, Pallas kernels: 9.78 us -> 9 us  [call(): pl.pallas_call(kernel, out_shape=out_shape, in_specs=specs, compiler_para...]
    ppermute x11 -> x12, starting transfers between devices: 17 us -> 16.6 us  [to_expert(): lax.ppermute(value, 'expert', [(i, i ^ ke) for i in range(groups)])]
  transfers between devices with their start and end apart: 22 -> 25, of which waited for: 9 -> 10; matrix products, arithmetic and copies ran while one was open for 0% -> 0% of each run, Pallas kernels for 6% -> 12%
where the time goes in v9:
time: 63 us; the launch traced here: 62.9 us
  starting transfers between devices  31.1 us (49%)
  waiting for transfers between devices  22 us (35%)
  Pallas kernels  9 us (14%)
  between operations  0.75 us (1%)
    ppermute x12, starting transfers between devices, to_expert(): lax.ppermute(value, 'expert', [(i, i ^ ke) for i in range(groups)])  16.6 us
    ppermute x8, starting transfers between devices, to_x(): lax.ppermute(value, 'fsdp', [(i, i ^ (k + 1) * CORES) for i in range(part...  13.5 us
    ppermute x12, waiting for transfers between devices, to_expert(): lax.ppermute(value, 'expert', [(i, i ^ ke) for i in range(groups)])  12.1 us
    ppermute x8, waiting for transfers between devices, to_x(): lax.ppermute(value, 'fsdp', [(i, i ^ (k + 1) * CORES) for i in range(part...  9.84 us
    pallas_call x14, Pallas kernels, call(): pl.pallas_call(kernel, out_shape=out_shape, in_specs=specs, compiler_para...  9 us
  transfers between devices with their start and end apart: 25, of which 10 were waited for; matrix products, arithmetic and copies ran while one was open for 0% of the time, Pallas kernels for 12%

profile of v9, /device:TPU:0, one launch (start us, length us, event | category | flops | bytes accessed | tf_op | source)
XLA Modules:
  0.0 62.9 jit_solution(384936081553333628)
XLA Ops:
  0.6 0.5 collective-permute-start.1
  1.2 0.1 collective-permute-start.2
  1.2 1.9 %shard_map.94 = (bf16[64,1024]{1,0:T(8,128)(2,1)S(1)}, bf16[64,1024]{1,0:T(8,128)(2,1)S(1)}, bf16[64,1024]{1,0:T(8,128)(2,1)S(1)}, bf16[64,1024]{1,0:T(8,128)(2,...) custom-call(s32[8,256]{1,0:T(8,128)} %bitcast.11, f32[8,256]{1,0:T(8,128)} %bitcast.12, s32[1,256]{1,0:T(1,128)} %refs_2_.1, ...), custom_call_target="tpu_custom_call" | custom-call | tf_op jit(solution)/shard_map/pallas_call | solution.py:38
  3.2 3.0 %collective-permute-start = (bf16[64,1024]{1,0:T(8,128)(2,1)S(1)}, bf16[64,1024]{1,0:T(8,128)(2,1)S(1)}, u32[]{:S(2)}, u32[]{:S(2)}) collective-permute-start(bf16[64,1024]{1,0:T(8,128)(2,1)S(1)} %get-tuple-element.44), channel_id=1, source_target_pairs={{0,2},{1,3},{2,0},{3,1},{4,6},{5,7},{6,4},{7,5},{8,10},{9,11},{10,... | collective-permute-start | bytes 393224 | tf_op jit(solution)/shard_map/ppermute | solution.py:272
  6.2 3.7 %collective-permute-done.refs_1_ = bf16[64,1024]{1,0:T(8,128)(2,1)S(1)} collective-permute-done((bf16[64,1024]{1,0:T(8,128)(2,1)S(1)}, bf16[64,1024]{1,0:T(8,128)(2,1)S(1)}, u32[]{:S(2)}, u32[]{:S(2)}) %collective-permute-start) | collective-permute-done | bytes 131104 | tf_op jit(solution)/shard_map/ppermute | solution.py:272
  9.9 1.9 %collective-permute-start.3 = (bf16[16,2048]{1,0:T(8,128)(2,1)S(1)}, bf16[16,2048]{1,0:T(8,128)(2,1)S(1)}, u32[]{:S(2)}, u32[]{:S(2)}) collective-permute-start(bf16[16,2048]{1,0:T(8,128)(2,1)S(1)} %get-tuple-element.48), channel_id=1, source_target_pairs={{0,4},{4,0},{8,12},{12,8},{1,5},{5,1},{9,13},{13,9},{2,6},{6,2},{1... | collective-permute-start | bytes 196616 | tf_op jit(solution)/shard_map/ppermute | solution.py:278
  11.8 2.6 %collective-permute-start.4 = (bf16[16,2048]{1,0:T(8,128)(2,1)S(1)}, bf16[16,2048]{1,0:T(8,128)(2,1)S(1)}, u32[]{:S(2)}, u32[]{:S(2)}) collective-permute-start(bf16[16,2048]{1,0:T(8,128)(2,1)S(1)} %get-tuple-element.49), channel_id=1, source_target_pairs={{0,8},{4,12},{8,0},{12,4},{1,9},{5,13},{9,1},{13,5},{2,10},{6,14},... | collective-permute-start | bytes 196616 | tf_op jit(solution)/shard_map/ppermute | solution.py:278
  14.4 0.0 collective-permute-start.5
  14.4 1.7 %collective-permute-start.12 = (bf16[64,1024]{1,0:T(8,128)(2,1)S(1)}, bf16[64,1024]{1,0:T(8,128)(2,1)S(1)}, u32[]{:S(2)}, u32[]{:S(2)}) collective-permute-start(bf16[64,1024]{1,0:T(8,128)(2,1)S(1)} %get-tuple-element.60), channel_id=1, source_target_pairs={{0,2},{1,3},{2,0},{3,1},{4,6},{5,7},{6,4},{7,5},{8,10},{9,11},{10,... | collective-permute-start | bytes 393224 | tf_op jit(solution)/shard_map/ppermute | solution.py:272
  16.1 0.0 collective-permute-done.3.refs_1_
  16.1 2.4 %collective-permute-done.4.refs_2_ = bf16[16,2048]{1,0:T(8,128)(2,1)S(1)} collective-permute-done((bf16[16,2048]{1,0:T(8,128)(2,1)S(1)}, bf16[16,2048]{1,0:T(8,128)(2,1)S(1)}, u32[]{:S(2)}, u32[]{:S(2)}) %collective-permute-start.4) | collective-permute-done | bytes 65568 | tf_op jit(solution)/shard_map/ppermute | solution.py:278
  18.5 2.0 %collective-permute-done.5.refs_3_ = bf16[16,2048]{1,0:T(8,128)(2,1)S(1)} collective-permute-done((bf16[16,2048]{1,0:T(8,128)(2,1)S(1)}, bf16[16,2048]{1,0:T(8,128)(2,1)S(1)}, u32[]{:S(2)}, u32[]{:S(2)}) %collective-permute-start.5) | collective-permute-done | bytes 65568 | tf_op jit(solution)/shard_map/ppermute | solution.py:278
  20.5 0.6 shard_map.96
  21.1 1.6 %collective-permute-start.6 = (bf16[64,1536]{1,0:T(8,128)(2,1)S(1)}, bf16[64,1536]{1,0:T(8,128)(2,1)S(1)}, u32[]{:S(2)}, u32[]{:S(2)}) collective-permute-start(bf16[64,1536]{1,0:T(8,128)(2,1)S(1)} %get-tuple-element.53), channel_id=1, source_target_pairs={{0,2},{1,3},{2,0},{3,1},{4,6},{5,7},{6,4},{7,5},{8,10},{9,11},{10,... | collective-permute-start | bytes 589832 | tf_op jit(solution)/shard_map/ppermute | solution.py:272
  22.6 0.0 collective-permute-done.12.refs_1_
  22.6 0.1 collective-permute-start.13
  22.7 2.0 %collective-permute-start.14 = (bf16[16,2048]{1,0:T(8,128)(2,1)S(1)}, bf16[16,2048]{1,0:T(8,128)(2,1)S(1)}, u32[]{:S(2)}, u32[]{:S(2)}) collective-permute-start(bf16[16,2048]{1,0:T(8,128)(2,1)S(1)} %get-tuple-element.63), channel_id=1, source_target_pairs={{0,8},{4,12},{8,0},{12,4},{1,9},{5,13},{9,1},{13,5},{2,10},{6,14},... | collective-permute-start | bytes 196616 | tf_op jit(solution)/shard_map/ppermute | solution.py:278
  24.7 2.4 %collective-permute-start.15 = (bf16[16,2048]{1,0:T(8,128)(2,1)S(1)}, bf16[16,2048]{1,0:T(8,128)(2,1)S(1)}, u32[]{:S(2)}, u32[]{:S(2)}) collective-permute-start(bf16[16,2048]{1,0:T(8,128)(2,1)S(1)} %get-tuple-element.64), channel_id=1, source_target_pairs={{0,12},{4,8},{8,4},{12,0},{1,13},{5,9},{9,5},{13,1},{2,14},{6,10},... | collective-permute-start | bytes 196616 | tf_op jit(solution)/shard_map/ppermute | solution.py:278
  27.1 0.2 collective-permute-done.6.refs_1_
  27.3 0.1 shard_map.97.refs_0_.refs_6_.refs_2_
  27.4 1.9 %collective-permute-start.7 = (bf16[64,768]{1,0:T(8,128)(2,1)S(1)}, bf16[64,768]{1,0:T(8,128)(2,1)S(1)}, u32[]{:S(2)}, u32[]{:S(2)}) collective-permute-start(bf16[64,768]{1,0:T(8,128)(2,1)S(1)} %shard_map.97.refs_0_.refs_6_.refs_2_), channel_id=1, source_target_pairs={{0,2},{1,3},{2,0},{3,1},{4,6},{5,7},{6,4},{7,5},{8,10},{9,11},{10,... | collective-permute-start | bytes 294920 | tf_op jit(solution)/shard_map/ppermute | solution.py:272
  29.3 0.0 collective-permute-done.13.refs_1_
  29.3 0.0 collective-permute-done.14.refs_2_
  29.3 1.5 %collective-permute-done.15.refs_3_ = bf16[16,2048]{1,0:T(8,128)(2,1)S(1)} collective-permute-done((bf16[16,2048]{1,0:T(8,128)(2,1)S(1)}, bf16[16,2048]{1,0:T(8,128)(2,1)S(1)}, u32[]{:S(2)}, u32[]{:S(2)}) %collective-permute-start.15) | collective-permute-done | bytes 65568 | tf_op jit(solution)/shard_map/ppermute | solution.py:278
  30.8 0.4 shard_map.101
  31.2 1.5 %collective-permute-start.19 = (bf16[64,768]{1,0:T(8,128)(2,1)S(1)}, bf16[64,768]{1,0:T(8,128)(2,1)S(1)}, u32[]{:S(2)}, u32[]{:S(2)}) collective-permute-start(bf16[64,768]{1,0:T(8,128)(2,1)S(1)} %get-tuple-element.70), channel_id=1, source_target_pairs={{0,2},{1,3},{2,0},{3,1},{4,6},{5,7},{6,4},{7,5},{8,10},{9,11},{10,... | collective-permute-start | bytes 294920 | tf_op jit(solution)/shard_map/ppermute | solution.py:272
  32.7 0.6 %shard_map.98 = (bf16[32,1024]{1,0:T(8,128)(2,1)S(1)}, bf16[32,1024]{1,0:T(8,128)(2,1)S(1)}, bf16[32,1024]{1,0:T(8,128)(2,1)S(1)}, bf16[32,1024]{1,0:T(8,128)(2,1)S(1)}) custom-call(bf16[64,768]{1,0:T(8,128)(2,1)S(1)} %shard_map.97.refs_0_.refs_6_.refs_2_, bf16[64,768]{1,0:T(8,128)(2,1)S(1)} %collective-permute-done.7.refs_1_.refs_3_, ...), custom_call_target="tpu_custom_call" | custom-call | tf_op jit(solution)/shard_map/pallas_call | solution.py:38
  33.4 2.9 %collective-permute-done.19.refs_3_ = bf16[64,768]{1,0:T(8,128)(2,1)S(1)} collective-permute-done((bf16[64,768]{1,0:T(8,128)(2,1)S(1)}, bf16[64,768]{1,0:T(8,128)(2,1)S(1)}, u32[]{:S(2)}, u32[]{:S(2)}) %collective-permute-start.19) | collective-permute-done | bytes 98336 | tf_op jit(solution)/shard_map/ppermute | solution.py:272
  36.3 0.1 shard_map.104.refs_0_
  36.4 1.5 %collective-permute-start.20 = (bf16[64,1536]{1,0:T(8,128)(2,1)S(1)}, bf16[64,1536]{1,0:T(8,128)(2,1)S(1)}, u32[]{:S(2)}, u32[]{:S(2)}) collective-permute-start(bf16[64,1536]{1,0:T(8,128)(2,1)S(1)} %shard_map.104.refs_0_), channel_id=1, source_target_pairs={{0,2},{1,3},{2,0},{3,1},{4,6},{5,7},{6,4},{7,5},{8,10},{9,11},{10,... | collective-permute-start | bytes 589832 | tf_op jit(solution)/shard_map/ppermute | solution.py:272
  37.9 2.2 %collective-permute-start.10 = (bf16[32,1024]{1,0:T(8,128)(2,1)S(1)}, bf16[32,1024]{1,0:T(8,128)(2,1)S(1)}, u32[]{:S(2)}, u32[]{:S(2)}) collective-permute-start(bf16[32,1024]{1,0:T(8,128)(2,1)S(1)} %get-tuple-element.58), channel_id=1, source_target_pairs={{0,12},{4,8},{8,4},{12,0},{1,13},{5,9},{9,5},{13,1},{2,14},{6,10},... | collective-permute-start | bytes 196616 | tf_op jit(solution)/shard_map/ppermute | solution.py:278
  40.0 0.0 collective-permute-start.8
  40.0 3.0 %collective-permute-done.20.refs_1_ = bf16[64,1536]{1,0:T(8,128)(2,1)S(1)} collective-permute-done((bf16[64,1536]{1,0:T(8,128)(2,1)S(1)}, bf16[64,1536]{1,0:T(8,128)(2,1)S(1)}, u32[]{:S(2)}, u32[]{:S(2)}) %collective-permute-start.20) | collective-permute-done | bytes 196640 | tf_op jit(solution)/shard_map/ppermute | solution.py:272
  43.0 1.1 %shard_map.105 = (bf16[64,1024]{1,0:T(8,128)(2,1)S(1)}, bf16[64,1024]{1,0:T(8,128)(2,1)S(1)}) custom-call(bf16[64,1536]{1,0:T(8,128)(2,1)S(1)} %shard_map.104.refs_0_, bf16[64,1536]{1,0:T(8,128)(2,1)S(1)} %collective-permute-done.20.refs_1_, bf16[512,1536]{1,0:T(8,128)(2,1)S(1)} %bitcast.7, bf16[512,1536]{1,0:T(8,128)(2,1)S(1)} %collective-permute-done.1.refs_5_.refs_3_), custom_call_target="tpu_custom_call" | custom-call | tf_op jit(solution)/shard_map/pallas_call | solution.py:38
  44.2 1.4 %collective-permute-start.21 = (bf16[64,1024]{1,0:T(8,128)(2,1)S(1)}, bf16[64,1024]{1,0:T(8,128)(2,1)S(1)}, u32[]{:S(2)}, u32[]{:S(2)}) collective-permute-start(bf16[64,1024]{1,0:T(8,128)(2,1)S(1)} %get-tuple-element.72), channel_id=1, source_target_pairs={{0,2},{1,3},{2,0},{3,1},{4,6},{5,7},{6,4},{7,5},{8,10},{9,11},{10,... | collective-permute-start | bytes 393224 | tf_op jit(solution)/shard_map/ppermute | solution.py:272
  45.5 1.0 %collective-permute-start.9 = (bf16[32,1024]{1,0:T(8,128)(2,1)S(1)}, bf16[32,1024]{1,0:T(8,128)(2,1)S(1)}, u32[]{:S(2)}, u32[]{:S(2)}) collective-permute-start(bf16[32,1024]{1,0:T(8,128)(2,1)S(1)} %get-tuple-element.57), channel_id=1, source_target_pairs={{0,8},{4,12},{8,0},{12,4},{1,9},{5,13},{9,1},{13,5},{2,10},{6,14},... | collective-permute-start | bytes 196616 | tf_op jit(solution)/shard_map/ppermute | solution.py:278
  46.5 0.0 collective-permute-start.16
  46.6 0.5 collective-permute-start.17
  47.1 4.2 %collective-permute-done.9.refs_2_.refs_4_ = bf16[32,1024]{1,0:T(8,128)(2,1)S(1)} collective-permute-done((bf16[32,1024]{1,0:T(8,128)(2,1)S(1)}, bf16[32,1024]{1,0:T(8,128)(2,1)S(1)}, u32[]{:S(2)}, u32[]{:S(2)}) %collective-permute-start.9) | collective-permute-done | bytes 65568 | tf_op jit(solution)/shard_map/ppermute | solution.py:278
  51.3 0.9 %collective-permute-start.11 = (bf16[64,1024]{1,0:T(8,128)(2,1)S(1)}, bf16[64,1024]{1,0:T(8,128)(2,1)S(1)}, u32[]{:S(2)}, u32[]{:S(2)}) collective-permute-start(bf16[64,1024]{1,0:T(8,128)(2,1)S(1)} %shard_map.99), channel_id=1, source_target_pairs={{0,2},{1,3},{2,0},{3,1},{4,6},{5,7},{6,4},{7,5},{8,10},{9,11},{10,... | collective-permute-start | bytes 393224 | tf_op jit(solution)/shard_map/ppermute | solution.py:272
  52.2 0.5 collective-permute-start.22
  52.7 2.8 %collective-permute-start.23 = (bf16[16,2048]{1,0:T(8,128)(2,1)S(1)}, bf16[16,2048]{1,0:T(8,128)(2,1)S(1)}, u32[]{:S(2)}, u32[]{:S(2)}) collective-permute-start(bf16[16,2048]{1,0:T(8,128)(2,1)S(1)} %get-tuple-element.75), channel_id=1, source_target_pairs={{0,8},{4,12},{8,0},{12,4},{1,9},{5,13},{9,1},{13,5},{2,10},{6,14},... | collective-permute-start | bytes 196616 | tf_op jit(solution)/shard_map/ppermute | solution.py:278
  55.5 1.2 %collective-permute-start.24 = (bf16[16,2048]{1,0:T(8,128)(2,1)S(1)}, bf16[16,2048]{1,0:T(8,128)(2,1)S(1)}, u32[]{:S(2)}, u32[]{:S(2)}) collective-permute-start(bf16[16,2048]{1,0:T(8,128)(2,1)S(1)} %get-tuple-element.76), channel_id=1, source_target_pairs={{0,12},{4,8},{8,4},{12,0},{1,13},{5,9},{9,5},{13,1},{2,14},{6,10},... | collective-permute-start | bytes 196616 | tf_op jit(solution)/shard_map/ppermute | solution.py:278
  56.7 1.6 %shard_map.102 = (f32[512,768]{1,0:T(8,128)}, f32[8,128]{1,0:T(8,128)S(1)}) custom-call(bf16[128,512]{1,0:T(8,128)(2,1)S(1)} %get-tuple-element.65.refs_0_, bf16[128,512]{1,0:T(8,128)(2,1)S(1)} %collective-permute-done.16.refs_1_, bf16[64,768]{1,0:T(8,128)(2,1)S(1)} %shard_map.97.refs_0_.refs_6_.refs_2_, ...), custom_call_target="tpu_custom_call" | custom-call | tf_op jit(solution)/shard_map/pallas_call | solution.py:38
  58.2 1.3 %shard_map.103 = (bf16[256,2048]{1,0:T(8,128)(2,1)}, f32[8,128]{1,0:T(8,128)S(1)}) custom-call(bf16[256,64]{1,0:T(8,128)(2,1)S(1)} %get-tuple-element.41.refs_0_, f32[64,128]{1,0:T(8,128)S(1)} %get-tuple-element.42.refs_1_, bf16[32,1024]{1,0:T(8,128)(2,1)S(1)} %get-tuple-element.55.refs_0_.refs_2_.refs_4_, ...), custom_call_target="tpu_custom_call" | custom-call | tf_op jit(solution)/shard_map/pallas_call | solution.py:38
  59.6 0.2 collective-permute-done.23.refs_3_
  59.8 1.9 %collective-permute-done.24.refs_4_ = bf16[16,2048]{1,0:T(8,128)(2,1)S(1)} collective-permute-done((bf16[16,2048]{1,0:T(8,128)(2,1)S(1)}, bf16[16,2048]{1,0:T(8,128)(2,1)S(1)}, u32[]{:S(2)}, u32[]{:S(2)}) %collective-permute-start.24) | collective-permute-done | bytes 65568 | tf_op jit(solution)/shard_map/ppermute | solution.py:278
  61.6 1.2 %shard_map.107 = bf16[256,2048]{1,0:T(8,128)(2,1)} custom-call(bf16[256,64]{1,0:T(8,128)(2,1)S(1)} %get-tuple-element.41.refs_0_, bf16[16,2048]{1,0:T(8,128)(2,1)S(1)} %get-tuple-element.73.refs_1_, bf16[16,2048]{1,0:T(8,128)(2,1)S(1)} %collective-permute-done.22.refs_2_, bf16[16,2048]{1,0:T(8,128)(2,1)S(1)} %collective-permute-done.23.refs_3_, ...), custom_call_target="tpu_custom_call" | custom-call | tf_op jit(solution)/shard_map/pallas_call | solution.py:38
  (20 shorter events, 0.1 us)
Async XLA Ops:
  0.6 19.8 %copy-start = (bf16[1,512,1536]{2,1,0:T(8,128)(2,1)S(1)}, bf16[1,512,1536]{2,1,0:T(8,128)(2,1)}, u32[]{:S(2)}) copy-start(bf16[1,512,1536]{2,1,0:T(8,128)(2,1)} %param.12) | copy-start | bytes 4718596
  0.6 9.3 %collective-permute-start.1 = (bf16[512,1536]{1,0:T(8,128)(2,1)}, bf16[512,1536]{1,0:T(8,128)(2,1)S(1)}, u32[]{:S(2)}, u32[]{:S(2)}) collective-permute-start(bf16[512,1536]{1,0:T(8,128)(2,1)} %bitcast.5), channel_id=1, source_target_pairs={{0,1},{1,0},{2,3},{3,2},{4,5},{5,4},{6,7},{7,6},{8,9},{9,8},{10,11... | collective-permute-start | bytes 4718600 | tf_op jit(solution)/shard_map/ppermute | solution.py:268
  1.2 8.7 %collective-permute-start.2 = (bf16[512,768]{1,0:T(8,128)(2,1)}, bf16[512,768]{1,0:T(8,128)(2,1)S(1)}, u32[]{:S(2)}, u32[]{:S(2)}) collective-permute-start(bf16[512,768]{1,0:T(8,128)(2,1)} %bitcast.8), channel_id=1, source_target_pairs={{0,1},{1,0},{2,3},{3,2},{4,5},{5,4},{6,7},{7,6},{8,9},{9,8},{10,11... | collective-permute-start | bytes 2359304 | tf_op jit(solution)/shard_map/ppermute | solution.py:268
  3.2 6.7 %collective-permute-start = (bf16[64,1024]{1,0:T(8,128)(2,1)S(1)}, bf16[64,1024]{1,0:T(8,128)(2,1)S(1)}, u32[]{:S(2)}, u32[]{:S(2)}) collective-permute-start(bf16[64,1024]{1,0:T(8,128)(2,1)S(1)} %get-tuple-element.44), channel_id=1, source_target_pairs={{0,2},{1,3},{2,0},{3,1},{4,6},{5,7},{6,4},{7,5},{8,10},{9,11},{10,... | collective-permute-start | bytes 393224 | tf_op jit(solution)/shard_map/ppermute | solution.py:272
  9.9 6.2 %collective-permute-start.3 = (bf16[16,2048]{1,0:T(8,128)(2,1)S(1)}, bf16[16,2048]{1,0:T(8,128)(2,1)S(1)}, u32[]{:S(2)}, u32[]{:S(2)}) collective-permute-start(bf16[16,2048]{1,0:T(8,128)(2,1)S(1)} %get-tuple-element.48), channel_id=1, source_target_pairs={{0,4},{4,0},{8,12},{12,8},{1,5},{5,1},{9,13},{13,9},{2,6},{6,2},{1... | collective-permute-start | bytes 196616 | tf_op jit(solution)/shard_map/ppermute | solution.py:278
  11.8 6.7 %collective-permute-start.4 = (bf16[16,2048]{1,0:T(8,128)(2,1)S(1)}, bf16[16,2048]{1,0:T(8,128)(2,1)S(1)}, u32[]{:S(2)}, u32[]{:S(2)}) collective-permute-start(bf16[16,2048]{1,0:T(8,128)(2,1)S(1)} %get-tuple-element.49), channel_id=1, source_target_pairs={{0,8},{4,12},{8,0},{12,4},{1,9},{5,13},{9,1},{13,5},{2,10},{6,14},... | collective-permute-start | bytes 196616 | tf_op jit(solution)/shard_map/ppermute | solution.py:278
  14.4 6.1 %collective-permute-start.5 = (bf16[16,2048]{1,0:T(8,128)(2,1)S(1)}, bf16[16,2048]{1,0:T(8,128)(2,1)S(1)}, u32[]{:S(2)}, u32[]{:S(2)}) collective-permute-start(bf16[16,2048]{1,0:T(8,128)(2,1)S(1)} %get-tuple-element.50), channel_id=1, source_target_pairs={{0,12},{4,8},{8,4},{12,0},{1,13},{5,9},{9,5},{13,1},{2,14},{6,10},... | collective-permute-start | bytes 196616 | tf_op jit(solution)/shard_map/ppermute | solution.py:278
  14.4 8.2 %collective-permute-start.12 = (bf16[64,1024]{1,0:T(8,128)(2,1)S(1)}, bf16[64,1024]{1,0:T(8,128)(2,1)S(1)}, u32[]{:S(2)}, u32[]{:S(2)}) collective-permute-start(bf16[64,1024]{1,0:T(8,128)(2,1)S(1)} %get-tuple-element.60), channel_id=1, source_target_pairs={{0,2},{1,3},{2,0},{3,1},{4,6},{5,7},{6,4},{7,5},{8,10},{9,11},{10,... | collective-permute-start | bytes 393224 | tf_op jit(solution)/shard_map/ppermute | solution.py:272
  20.5 10.3 %copy-start.1 = (bf16[1,512,768]{2,1,0:T(8,128)(2,1)S(1)}, bf16[1,512,768]{2,1,0:T(8,128)(2,1)}, u32[]{:S(2)}) copy-start(bf16[1,512,768]{2,1,0:T(8,128)(2,1)} %param.13) | copy-start | bytes 2359300
  21.1 6.2 %collective-permute-start.6 = (bf16[64,1536]{1,0:T(8,128)(2,1)S(1)}, bf16[64,1536]{1,0:T(8,128)(2,1)S(1)}, u32[]{:S(2)}, u32[]{:S(2)}) collective-permute-start(bf16[64,1536]{1,0:T(8,128)(2,1)S(1)} %get-tuple-element.53), channel_id=1, source_target_pairs={{0,2},{1,3},{2,0},{3,1},{4,6},{5,7},{6,4},{7,5},{8,10},{9,11},{10,... | collective-permute-start | bytes 589832 | tf_op jit(solution)/shard_map/ppermute | solution.py:272
  22.6 6.6 %collective-permute-start.13 = (bf16[16,2048]{1,0:T(8,128)(2,1)S(1)}, bf16[16,2048]{1,0:T(8,128)(2,1)S(1)}, u32[]{:S(2)}, u32[]{:S(2)}) collective-permute-start(bf16[16,2048]{1,0:T(8,128)(2,1)S(1)} %get-tuple-element.62), channel_id=1, source_target_pairs={{0,4},{4,0},{8,12},{12,8},{1,5},{5,1},{9,13},{13,9},{2,6},{6,2},{1... | collective-permute-start | bytes 196616 | tf_op jit(solution)/shard_map/ppermute | solution.py:278
  22.7 6.6 %collective-permute-start.14 = (bf16[16,2048]{1,0:T(8,128)(2,1)S(1)}, bf16[16,2048]{1,0:T(8,128)(2,1)S(1)}, u32[]{:S(2)}, u32[]{:S(2)}) collective-permute-start(bf16[16,2048]{1,0:T(8,128)(2,1)S(1)} %get-tuple-element.63), channel_id=1, source_target_pairs={{0,8},{4,12},{8,0},{12,4},{1,9},{5,13},{9,1},{13,5},{2,10},{6,14},... | collective-permute-start | bytes 196616 | tf_op jit(solution)/shard_map/ppermute | solution.py:278
  24.7 6.1 %collective-permute-start.15 = (bf16[16,2048]{1,0:T(8,128)(2,1)S(1)}, bf16[16,2048]{1,0:T(8,128)(2,1)S(1)}, u32[]{:S(2)}, u32[]{:S(2)}) collective-permute-start(bf16[16,2048]{1,0:T(8,128)(2,1)S(1)} %get-tuple-element.64), channel_id=1, source_target_pairs={{0,12},{4,8},{8,4},{12,0},{1,13},{5,9},{9,5},{13,1},{2,14},{6,10},... | collective-permute-start | bytes 196616 | tf_op jit(solution)/shard_map/ppermute | solution.py:278
  27.4 5.3 %collective-permute-start.7 = (bf16[64,768]{1,0:T(8,128)(2,1)S(1)}, bf16[64,768]{1,0:T(8,128)(2,1)S(1)}, u32[]{:S(2)}, u32[]{:S(2)}) collective-permute-start(bf16[64,768]{1,0:T(8,128)(2,1)S(1)} %shard_map.97.refs_0_.refs_6_.refs_2_), channel_id=1, source_target_pairs={{0,2},{1,3},{2,0},{3,1},{4,6},{5,7},{6,4},{7,5},{8,10},{9,11},{10,... | collective-permute-start | bytes 294920 | tf_op jit(solution)/shard_map/ppermute | solution.py:272
  31.2 5.1 %collective-permute-start.19 = (bf16[64,768]{1,0:T(8,128)(2,1)S(1)}, bf16[64,768]{1,0:T(8,128)(2,1)S(1)}, u32[]{:S(2)}, u32[]{:S(2)}) collective-permute-start(bf16[64,768]{1,0:T(8,128)(2,1)S(1)} %get-tuple-element.70), channel_id=1, source_target_pairs={{0,2},{1,3},{2,0},{3,1},{4,6},{5,7},{6,4},{7,5},{8,10},{9,11},{10,... | collective-permute-start | bytes 294920 | tf_op jit(solution)/shard_map/ppermute | solution.py:272
  36.4 6.6 %collective-permute-start.20 = (bf16[64,1536]{1,0:T(8,128)(2,1)S(1)}, bf16[64,1536]{1,0:T(8,128)(2,1)S(1)}, u32[]{:S(2)}, u32[]{:S(2)}) collective-permute-start(bf16[64,1536]{1,0:T(8,128)(2,1)S(1)} %shard_map.104.refs_0_), channel_id=1, source_target_pairs={{0,2},{1,3},{2,0},{3,1},{4,6},{5,7},{6,4},{7,5},{8,10},{9,11},{10,... | collective-permute-start | bytes 589832 | tf_op jit(solution)/shard_map/ppermute | solution.py:272
  37.9 8.7 %collective-permute-start.10 = (bf16[32,1024]{1,0:T(8,128)(2,1)S(1)}, bf16[32,1024]{1,0:T(8,128)(2,1)S(1)}, u32[]{:S(2)}, u32[]{:S(2)}) collective-permute-start(bf16[32,1024]{1,0:T(8,128)(2,1)S(1)} %get-tuple-element.58), channel_id=1, source_target_pairs={{0,12},{4,8},{8,4},{12,0},{1,13},{5,9},{9,5},{13,1},{2,14},{6,10},... | collective-permute-start | bytes 196616 | tf_op jit(solution)/shard_map/ppermute | solution.py:278
  40.0 7.0 %collective-permute-start.8 = (bf16[32,1024]{1,0:T(8,128)(2,1)S(1)}, bf16[32,1024]{1,0:T(8,128)(2,1)S(1)}, u32[]{:S(2)}, u32[]{:S(2)}) collective-permute-start(bf16[32,1024]{1,0:T(8,128)(2,1)S(1)} %get-tuple-element.56), channel_id=1, source_target_pairs={{0,4},{4,0},{8,12},{12,8},{1,5},{5,1},{9,13},{13,9},{2,6},{6,2},{1... | collective-permute-start | bytes 196616 | tf_op jit(solution)/shard_map/ppermute | solution.py:278
  44.2 8.0 %collective-permute-start.21 = (bf16[64,1024]{1,0:T(8,128)(2,1)S(1)}, bf16[64,1024]{1,0:T(8,128)(2,1)S(1)}, u32[]{:S(2)}, u32[]{:S(2)}) collective-permute-start(bf16[64,1024]{1,0:T(8,128)(2,1)S(1)} %get-tuple-element.72), channel_id=1, source_target_pairs={{0,2},{1,3},{2,0},{3,1},{4,6},{5,7},{6,4},{7,5},{8,10},{9,11},{10,... | collective-permute-start | bytes 393224 | tf_op jit(solution)/shard_map/ppermute | solution.py:272
  45.5 5.7 %collective-permute-start.9 = (bf16[32,1024]{1,0:T(8,128)(2,1)S(1)}, bf16[32,1024]{1,0:T(8,128)(2,1)S(1)}, u32[]{:S(2)}, u32[]{:S(2)}) collective-permute-start(bf16[32,1024]{1,0:T(8,128)(2,1)S(1)} %get-tuple-element.57), channel_id=1, source_target_pairs={{0,8},{4,12},{8,0},{12,4},{1,9},{5,13},{9,1},{13,5},{2,10},{6,14},... | collective-permute-start | bytes 196616 | tf_op jit(solution)/shard_map/ppermute | solution.py:278
  46.5 9.0 %collective-permute-start.16 = (bf16[128,512]{1,0:T(8,128)(2,1)S(1)}, bf16[128,512]{1,0:T(8,128)(2,1)S(1)}, u32[]{:S(2)}, u32[]{:S(2)}) collective-permute-start(bf16[128,512]{1,0:T(8,128)(2,1)S(1)} %get-tuple-element.66), channel_id=1, source_target_pairs={{0,1},{1,0},{2,3},{3,2},{4,5},{5,4},{6,7},{7,6},{8,9},{9,8},{10,11... | collective-permute-start | bytes 393224 | tf_op jit(solution)/shard_map/ppermute | solution.py:268
  46.6 6.1 %collective-permute-start.17 = (bf16[64,768]{1,0:T(8,128)(2,1)S(1)}, bf16[64,768]{1,0:T(8,128)(2,1)S(1)}, u32[]{:S(2)}, u32[]{:S(2)}) collective-permute-start(bf16[64,768]{1,0:T(8,128)(2,1)S(1)} %shard_map.97.refs_0_.refs_6_.refs_2_), channel_id=1, source_target_pairs={{0,1},{1,0},{2,3},{3,2},{4,5},{5,4},{6,7},{7,6},{8,9},{9,8},{10,11... | collective-permute-start | bytes 294920 | tf_op jit(solution)/shard_map/ppermute | solution.py:268
  51.3 7.0 %collective-permute-start.11 = (bf16[64,1024]{1,0:T(8,128)(2,1)S(1)}, bf16[64,1024]{1,0:T(8,128)(2,1)S(1)}, u32[]{:S(2)}, u32[]{:S(2)}) collective-permute-start(bf16[64,1024]{1,0:T(8,128)(2,1)S(1)} %shard_map.99), channel_id=1, source_target_pairs={{0,2},{1,3},{2,0},{3,1},{4,6},{5,7},{6,4},{7,5},{8,10},{9,11},{10,... | collective-permute-start | bytes 393224 | tf_op jit(solution)/shard_map/ppermute | solution.py:272
  52.2 4.5 %collective-permute-start.18 = (bf16[64,768]{1,0:T(8,128)(2,1)S(1)}, bf16[64,768]{1,0:T(8,128)(2,1)S(1)}, u32[]{:S(2)}, u32[]{:S(2)}) collective-permute-start(bf16[64,768]{1,0:T(8,128)(2,1)S(1)} %collective-permute-done.7.refs_1_.refs_3_), channel_id=1, source_target_pairs={{0,1},{1,0},{2,3},{3,2},{4,5},{5,4},{6,7},{7,6},{8,9},{9,8},{10,11... | collective-permute-start | bytes 294920 | tf_op jit(solution)/shard_map/ppermute | solution.py:268
  52.2 7.3 %collective-permute-start.22 = (bf16[16,2048]{1,0:T(8,128)(2,1)S(1)}, bf16[16,2048]{1,0:T(8,128)(2,1)S(1)}, u32[]{:S(2)}, u32[]{:S(2)}) collective-permute-start(bf16[16,2048]{1,0:T(8,128)(2,1)S(1)} %get-tuple-element.74), channel_id=1, source_target_pairs={{0,4},{4,0},{8,12},{12,8},{1,5},{5,1},{9,13},{13,9},{2,6},{6,2},{1... | collective-permute-start | bytes 196616 | tf_op jit(solution)/shard_map/ppermute | solution.py:278
  52.7 7.1 %collective-permute-start.23 = (bf16[16,2048]{1,0:T(8,128)(2,1)S(1)}, bf16[16,2048]{1,0:T(8,128)(2,1)S(1)}, u32[]{:S(2)}, u32[]{:S(2)}) collective-permute-start(bf16[16,2048]{1,0:T(8,128)(2,1)S(1)} %get-tuple-element.75), channel_id=1, source_target_pairs={{0,8},{4,12},{8,0},{12,4},{1,9},{5,13},{9,1},{13,5},{2,10},{6,14},... | collective-permute-start | bytes 196616 | tf_op jit(solution)/shard_map/ppermute | solution.py:278
  55.5 6.1 %collective-permute-start.24 = (bf16[16,2048]{1,0:T(8,128)(2,1)S(1)}, bf16[16,2048]{1,0:T(8,128)(2,1)S(1)}, u32[]{:S(2)}, u32[]{:S(2)}) collective-permute-start(bf16[16,2048]{1,0:T(8,128)(2,1)S(1)} %get-tuple-element.76), channel_id=1, source_target_pairs={{0,12},{4,8},{8,4},{12,0},{1,13},{5,9},{9,5},{13,1},{2,14},{6,10},... | collective-permute-start | bytes 196616 | tf_op jit(solution)/shard_map/ppermute | solution.py:278

commit v10 on v9

--- a/solution.py
+++ b/solution.py
@@ -7,6 +7,7 @@
 
 EXPERTS = 128
 CORES = 2
+BACK_COST = 12000000000
 VMEM = 40 * 1024 * 1024
 F32 = jnp.float32
 BF16 = jnp.bfloat16
@@ -318,7 +319,7 @@
         + [shape((slots, feed), F32)]
         + [shape((slots, feed))] * (spread - 1),
         (*grads, out_own, out_sib),
-        after=hidden[:1],
+        cost=BACK_COST,
     )
     back = (back, *to_x(back_far))
     expert_out = to_expert(
@@ -328,11 +329,11 @@
             (*hidden, out_own, out_sib),
         )
     )
-    (d_pre,) = call(
-        d_pre_kernel, [shape((slots, 2 * feed))], (*pre, *back), after=expert_out[:1]
-    )
+    (d_pre,) = call(d_pre_kernel, [shape((slots, 2 * feed))], (*pre, *back))
     d_pre = (d_pre, *to_x([d_pre] * (spread - 1)))
-    near, *far = call(bound(d_rows_kernel, spread), by_x, (*d_pre, in_own, in_sib))
+    near, *far = call(
+        bound(d_rows_kernel, spread), by_x, (*d_pre, in_own, in_sib), after=expert_out[1:2]
+    )
     d_rows = to_expert(call(join, chunk, (near, *to_x(far))))
     far = to_x(
         call(bound(far_kernel, groups, spread, capacity), by_x[1:], expert_out)

time: 63 us -> 61 us (0.968)
  starting transfers between devices: 31.1 us -> 29.8 us
  waiting for transfers between devices: 22 us -> 21.3 us
    ppermute x12, waiting for transfers between devices: 12.1 us -> 5.8 us  [to_expert(): lax.ppermute(value, 'expert', [(i, i ^ ke) for i in range(groups)])]
    ppermute x8, waiting for transfers between devices: 9.84 us -> 15.5 us  [to_x(): lax.ppermute(value, 'fsdp', [(i, i ^ (k + 1) * CORES) for i in range(part...]
    ppermute x8, starting transfers between devices: 13.5 us -> 10.6 us  [to_x(): lax.ppermute(value, 'fsdp', [(i, i ^ (k + 1) * CORES) for i in range(part...]
    ppermute x12, starting transfers between devices: 16.6 us -> 18.1 us  [to_expert(): lax.ppermute(value, 'expert', [(i, i ^ ke) for i in range(groups)])]
  transfers between devices with their start and end apart: 25 -> 25, of which waited for: 10 -> 9; matrix products, arithmetic and copies ran while one was open for 0% -> 0% of each run, Pallas kernels for 12% -> 13%
where the time goes in v10:
time: 61 us; the launch traced here: 60.9 us
  starting transfers between devices  29.8 us (49%)
  waiting for transfers between devices  21.3 us (35%)
  Pallas kernels  9 us (15%)
  between operations  0.77 us (1%)
    ppermute x12, starting transfers between devices, to_expert(): lax.ppermute(value, 'expert', [(i, i ^ ke) for i in range(groups)])  18.1 us
    ppermute x8, waiting for transfers between devices, to_x(): lax.ppermute(value, 'fsdp', [(i, i ^ (k + 1) * CORES) for i in range(part...  15.5 us
    ppermute x8, starting transfers between devices, to_x(): lax.ppermute(value, 'fsdp', [(i, i ^ (k + 1) * CORES) for i in range(part...  10.6 us
    pallas_call x14, Pallas kernels, call(): pl.pallas_call(kernel, out_shape=out_shape, in_specs=specs, compiler_para...  9 us
    ppermute x12, waiting for transfers between devices, to_expert(): lax.ppermute(value, 'expert', [(i, i ^ ke) for i in range(groups)])  5.8 us
  transfers between devices with their start and end apart: 25, of which 9 were waited for; matrix products, arithmetic and copies ran while one was open for 0% of the time, Pallas kernels for 13%

profile of v10, /device:TPU:0, one launch (start us, length us, event | category | flops | bytes accessed | tf_op | source)
XLA Modules:
  0.0 60.9 jit_solution(7774026536649104450)
XLA Ops:
  0.6 0.5 collective-permute-start.1
  1.2 0.1 collective-permute-start.2
  1.2 1.9 %shard_map.94 = (bf16[64,1024]{1,0:T(8,128)(2,1)S(1)}, bf16[64,1024]{1,0:T(8,128)(2,1)S(1)}, bf16[64,1024]{1,0:T(8,128)(2,1)S(1)}, bf16[64,1024]{1,0:T(8,128)(2,...) custom-call(s32[8,256]{1,0:T(8,128)} %bitcast.11, f32[8,256]{1,0:T(8,128)} %bitcast.12, s32[1,256]{1,0:T(1,128)} %refs_2_.1, ...), custom_call_target="tpu_custom_call" | custom-call | tf_op jit(solution)/shard_map/pallas_call | solution.py:39
  3.2 3.0 %collective-permute-start = (bf16[64,1024]{1,0:T(8,128)(2,1)S(1)}, bf16[64,1024]{1,0:T(8,128)(2,1)S(1)}, u32[]{:S(2)}, u32[]{:S(2)}) collective-permute-start(bf16[64,1024]{1,0:T(8,128)(2,1)S(1)} %get-tuple-element.44), channel_id=1, source_target_pairs={{0,2},{1,3},{2,0},{3,1},{4,6},{5,7},{6,4},{7,5},{8,10},{9,11},{10,... | collective-permute-start | bytes 393224 | tf_op jit(solution)/shard_map/ppermute | solution.py:273
  6.2 0.1 collective-permute-start.12
  6.2 4.2 %collective-permute-done.refs_1_ = bf16[64,1024]{1,0:T(8,128)(2,1)S(1)} collective-permute-done((bf16[64,1024]{1,0:T(8,128)(2,1)S(1)}, bf16[64,1024]{1,0:T(8,128)(2,1)S(1)}, u32[]{:S(2)}, u32[]{:S(2)}) %collective-permute-start) | collective-permute-done | bytes 131104 | tf_op jit(solution)/shard_map/ppermute | solution.py:273
  10.5 0.0 collective-permute-done.2.refs_3_.refs_5_
  10.5 0.0 collective-permute-done.1.refs_5_.refs_3_
  10.5 2.2 %collective-permute-start.3 = (bf16[16,2048]{1,0:T(8,128)(2,1)S(1)}, bf16[16,2048]{1,0:T(8,128)(2,1)S(1)}, u32[]{:S(2)}, u32[]{:S(2)}) collective-permute-start(bf16[16,2048]{1,0:T(8,128)(2,1)S(1)} %get-tuple-element.48), channel_id=1, source_target_pairs={{0,4},{4,0},{8,12},{12,8},{1,5},{5,1},{9,13},{13,9},{2,6},{6,2},{1... | collective-permute-start | bytes 196616 | tf_op jit(solution)/shard_map/ppermute | solution.py:279
  12.7 2.6 %collective-permute-start.4 = (bf16[16,2048]{1,0:T(8,128)(2,1)S(1)}, bf16[16,2048]{1,0:T(8,128)(2,1)S(1)}, u32[]{:S(2)}, u32[]{:S(2)}) collective-permute-start(bf16[16,2048]{1,0:T(8,128)(2,1)S(1)} %get-tuple-element.49), channel_id=1, source_target_pairs={{0,8},{4,12},{8,0},{12,4},{1,9},{5,13},{9,1},{13,5},{2,10},{6,14},... | collective-permute-start | bytes 196616 | tf_op jit(solution)/shard_map/ppermute | solution.py:279
  15.3 0.0 collective-permute-start.5
  15.3 0.0 collective-permute-done.12.refs_1_
  15.3 1.0 %collective-permute-start.13 = (bf16[16,2048]{1,0:T(8,128)(2,1)S(1)}, bf16[16,2048]{1,0:T(8,128)(2,1)S(1)}, u32[]{:S(2)}, u32[]{:S(2)}) collective-permute-start(bf16[16,2048]{1,0:T(8,128)(2,1)S(1)} %get-tuple-element.62), channel_id=1, source_target_pairs={{0,4},{4,0},{8,12},{12,8},{1,5},{5,1},{9,13},{13,9},{2,6},{6,2},{1... | collective-permute-start | bytes 196616 | tf_op jit(solution)/shard_map/ppermute | solution.py:279
  16.3 3.5 %collective-permute-start.14 = (bf16[16,2048]{1,0:T(8,128)(2,1)S(1)}, bf16[16,2048]{1,0:T(8,128)(2,1)S(1)}, u32[]{:S(2)}, u32[]{:S(2)}) collective-permute-start(bf16[16,2048]{1,0:T(8,128)(2,1)S(1)} %get-tuple-element.63), channel_id=1, source_target_pairs={{0,8},{4,12},{8,0},{12,4},{1,9},{5,13},{9,1},{13,5},{2,10},{6,14},... | collective-permute-start | bytes 196616 | tf_op jit(solution)/shard_map/ppermute | solution.py:279
  19.8 0.0 collective-permute-done.3.refs_1_
  19.8 0.0 collective-permute-start.15
  19.8 0.0 collective-permute-done.4.refs_2_
  19.8 1.9 %collective-permute-done.5.refs_3_ = bf16[16,2048]{1,0:T(8,128)(2,1)S(1)} collective-permute-done((bf16[16,2048]{1,0:T(8,128)(2,1)S(1)}, bf16[16,2048]{1,0:T(8,128)(2,1)S(1)}, u32[]{:S(2)}, u32[]{:S(2)}) %collective-permute-start.5) | collective-permute-done | bytes 65568 | tf_op jit(solution)/shard_map/ppermute | solution.py:279
  21.7 0.6 shard_map.96
  22.2 1.6 %collective-permute-start.6 = (bf16[64,1536]{1,0:T(8,128)(2,1)S(1)}, bf16[64,1536]{1,0:T(8,128)(2,1)S(1)}, u32[]{:S(2)}, u32[]{:S(2)}) collective-permute-start(bf16[64,1536]{1,0:T(8,128)(2,1)S(1)} %get-tuple-element.53), channel_id=1, source_target_pairs={{0,2},{1,3},{2,0},{3,1},{4,6},{5,7},{6,4},{7,5},{8,10},{9,11},{10,... | collective-permute-start | bytes 589832 | tf_op jit(solution)/shard_map/ppermute | solution.py:273
  23.8 1.1 %collective-permute-done.14.refs_2_ = bf16[16,2048]{1,0:T(8,128)(2,1)S(1)} collective-permute-done((bf16[16,2048]{1,0:T(8,128)(2,1)S(1)}, bf16[16,2048]{1,0:T(8,128)(2,1)S(1)}, u32[]{:S(2)}, u32[]{:S(2)}) %collective-permute-start.14) | collective-permute-done | bytes 65568 | tf_op jit(solution)/shard_map/ppermute | solution.py:279
  24.9 1.1 %collective-permute-done.15.refs_3_ = bf16[16,2048]{1,0:T(8,128)(2,1)S(1)} collective-permute-done((bf16[16,2048]{1,0:T(8,128)(2,1)S(1)}, bf16[16,2048]{1,0:T(8,128)(2,1)S(1)}, u32[]{:S(2)}, u32[]{:S(2)}) %collective-permute-start.15) | collective-permute-done | bytes 65568 | tf_op jit(solution)/shard_map/ppermute | solution.py:279
  25.9 0.4 shard_map.101
  26.3 1.6 %collective-permute-start.19 = (bf16[64,768]{1,0:T(8,128)(2,1)S(1)}, bf16[64,768]{1,0:T(8,128)(2,1)S(1)}, u32[]{:S(2)}, u32[]{:S(2)}) collective-permute-start(bf16[64,768]{1,0:T(8,128)(2,1)S(1)} %get-tuple-element.70), channel_id=1, source_target_pairs={{0,2},{1,3},{2,0},{3,1},{4,6},{5,7},{6,4},{7,5},{8,10},{9,11},{10,... | collective-permute-start | bytes 294920 | tf_op jit(solution)/shard_map/ppermute | solution.py:273
  27.9 4.2 %collective-permute-done.19.refs_3_ = bf16[64,768]{1,0:T(8,128)(2,1)S(1)} collective-permute-done((bf16[64,768]{1,0:T(8,128)(2,1)S(1)}, bf16[64,768]{1,0:T(8,128)(2,1)S(1)}, u32[]{:S(2)}, u32[]{:S(2)}) %collective-permute-start.19) | collective-permute-done | bytes 98336 | tf_op jit(solution)/shard_map/ppermute | solution.py:273
  32.1 0.0 collective-permute-done.6.refs_1_
  32.1 0.1 shard_map.104.refs_0_
  32.2 1.6 %collective-permute-start.20 = (bf16[64,1536]{1,0:T(8,128)(2,1)S(1)}, bf16[64,1536]{1,0:T(8,128)(2,1)S(1)}, u32[]{:S(2)}, u32[]{:S(2)}) collective-permute-start(bf16[64,1536]{1,0:T(8,128)(2,1)S(1)} %shard_map.104.refs_0_), channel_id=1, source_target_pairs={{0,2},{1,3},{2,0},{3,1},{4,6},{5,7},{6,4},{7,5},{8,10},{9,11},{10,... | collective-permute-start | bytes 589832 | tf_op jit(solution)/shard_map/ppermute | solution.py:273
  33.8 0.1 shard_map.97.refs_0_.refs_2_
  33.8 0.6 collective-permute-start.7
  34.4 4.5 %collective-permute-done.7.refs_1_.refs_3_ = bf16[64,768]{1,0:T(8,128)(2,1)S(1)} collective-permute-done((bf16[64,768]{1,0:T(8,128)(2,1)S(1)}, bf16[64,768]{1,0:T(8,128)(2,1)S(1)}, u32[]{:S(2)}, u32[]{:S(2)}) %collective-permute-start.7) | collective-permute-done | bytes 98336 | tf_op jit(solution)/shard_map/ppermute | solution.py:273
  39.0 0.6 %shard_map.98 = (bf16[32,1024]{1,0:T(8,128)(2,1)S(1)}, bf16[32,1024]{1,0:T(8,128)(2,1)S(1)}, bf16[32,1024]{1,0:T(8,128)(2,1)S(1)}, bf16[32,1024]{1,0:T(8,128)(2,1)S(1)}) custom-call(bf16[64,768]{1,0:T(8,128)(2,1)S(1)} %shard_map.97.refs_0_.refs_2_, bf16[64,768]{1,0:T(8,128)(2,1)S(1)} %collective-permute-done.7.refs_1_.refs_3_, ...), custom_call_target="tpu_custom_call" | custom-call | tf_op jit(solution)/shard_map/pallas_call | solution.py:39
  39.6 0.1 collective-permute-start.8
  39.8 1.9 %collective-permute-start.9 = (bf16[32,1024]{1,0:T(8,128)(2,1)S(1)}, bf16[32,1024]{1,0:T(8,128)(2,1)S(1)}, u32[]{:S(2)}, u32[]{:S(2)}) collective-permute-start(bf16[32,1024]{1,0:T(8,128)(2,1)S(1)} %get-tuple-element.57), channel_id=1, source_target_pairs={{0,8},{4,12},{8,0},{12,4},{1,9},{5,13},{9,1},{13,5},{2,10},{6,14},... | collective-permute-start | bytes 196616 | tf_op jit(solution)/shard_map/ppermute | solution.py:279
  41.7 2.4 %collective-permute-start.10 = (bf16[32,1024]{1,0:T(8,128)(2,1)S(1)}, bf16[32,1024]{1,0:T(8,128)(2,1)S(1)}, u32[]{:S(2)}, u32[]{:S(2)}) collective-permute-start(bf16[32,1024]{1,0:T(8,128)(2,1)S(1)} %get-tuple-element.58), channel_id=1, source_target_pairs={{0,12},{4,8},{8,4},{12,0},{1,13},{5,9},{9,5},{13,1},{2,14},{6,10},... | collective-permute-start | bytes 196616 | tf_op jit(solution)/shard_map/ppermute | solution.py:279
  44.1 1.3 %collective-permute-done.8.refs_1_.refs_3_.refs_4_ = bf16[32,1024]{1,0:T(8,128)(2,1)S(1)} collective-permute-done((bf16[32,1024]{1,0:T(8,128)(2,1)S(1)}, bf16[32,1024]{1,0:T(8,128)(2,1)S(1)}, u32[]{:S(2)}, u32[]{:S(2)}) %collective-permute-start.8) | collective-permute-done | bytes 65568 | tf_op jit(solution)/shard_map/ppermute | solution.py:279
  45.4 1.1 %shard_map.105 = (bf16[64,1024]{1,0:T(8,128)(2,1)S(1)}, bf16[64,1024]{1,0:T(8,128)(2,1)S(1)}) custom-call(bf16[64,1536]{1,0:T(8,128)(2,1)S(1)} %shard_map.104.refs_0_, bf16[64,1536]{1,0:T(8,128)(2,1)S(1)} %collective-permute-done.20.refs_1_, bf16[512,1536]{1,0:T(8,128)(2,1)S(1)} %bitcast.7, bf16[512,1536]{1,0:T(8,128)(2,1)S(1)} %collective-permute-done.1.refs_5_.refs_3_, ...), custom_call_target="tpu_custom_call" | custom-call | tf_op jit(solution)/shard_map/pallas_call | solution.py:39
  46.5 1.6 %collective-permute-start.21 = (bf16[64,1024]{1,0:T(8,128)(2,1)S(1)}, bf16[64,1024]{1,0:T(8,128)(2,1)S(1)}, u32[]{:S(2)}, u32[]{:S(2)}) collective-permute-start(bf16[64,1024]{1,0:T(8,128)(2,1)S(1)} %get-tuple-element.72), channel_id=1, source_target_pairs={{0,2},{1,3},{2,0},{3,1},{4,6},{5,7},{6,4},{7,5},{8,10},{9,11},{10,... | collective-permute-start | bytes 393224 | tf_op jit(solution)/shard_map/ppermute | solution.py:273
  48.1 0.5 collective-permute-start.17
  48.6 0.7 %collective-permute-start.11 = (bf16[64,1024]{1,0:T(8,128)(2,1)S(1)}, bf16[64,1024]{1,0:T(8,128)(2,1)S(1)}, u32[]{:S(2)}, u32[]{:S(2)}) collective-permute-start(bf16[64,1024]{1,0:T(8,128)(2,1)S(1)} %shard_map.99), channel_id=1, source_target_pairs={{0,2},{1,3},{2,0},{3,1},{4,6},{5,7},{6,4},{7,5},{8,10},{9,11},{10,... | collective-permute-start | bytes 393224 | tf_op jit(solution)/shard_map/ppermute | solution.py:273
  49.3 2.5 %collective-permute-done.21.refs_1_ = bf16[64,1024]{1,0:T(8,128)(2,1)S(1)} collective-permute-done((bf16[64,1024]{1,0:T(8,128)(2,1)S(1)}, bf16[64,1024]{1,0:T(8,128)(2,1)S(1)}, u32[]{:S(2)}, u32[]{:S(2)}) %collective-permute-start.21) | collective-permute-done | bytes 131104 | tf_op jit(solution)/shard_map/ppermute | solution.py:273
  51.8 0.1 collective-permute-start.22
  51.9 1.6 %collective-permute-start.23 = (bf16[16,2048]{1,0:T(8,128)(2,1)S(1)}, bf16[16,2048]{1,0:T(8,128)(2,1)S(1)}, u32[]{:S(2)}, u32[]{:S(2)}) collective-permute-start(bf16[16,2048]{1,0:T(8,128)(2,1)S(1)} %get-tuple-element.75), channel_id=1, source_target_pairs={{0,8},{4,12},{8,0},{12,4},{1,9},{5,13},{9,1},{13,5},{2,10},{6,14},... | collective-permute-start | bytes 196616 | tf_op jit(solution)/shard_map/ppermute | solution.py:279
  53.6 2.8 %collective-permute-start.24 = (bf16[16,2048]{1,0:T(8,128)(2,1)S(1)}, bf16[16,2048]{1,0:T(8,128)(2,1)S(1)}, u32[]{:S(2)}, u32[]{:S(2)}) collective-permute-start(bf16[16,2048]{1,0:T(8,128)(2,1)S(1)} %get-tuple-element.76), channel_id=1, source_target_pairs={{0,12},{4,8},{8,4},{12,0},{1,13},{5,9},{9,5},{13,1},{2,14},{6,10},... | collective-permute-start | bytes 196616 | tf_op jit(solution)/shard_map/ppermute | solution.py:279
  56.3 1.6 %shard_map.102 = (f32[512,768]{1,0:T(8,128)}, f32[8,128]{1,0:T(8,128)S(1)}) custom-call(bf16[128,512]{1,0:T(8,128)(2,1)S(1)} %get-tuple-element.65.refs_0_, bf16[128,512]{1,0:T(8,128)(2,1)S(1)} %collective-permute-done.16.refs_1_, bf16[64,768]{1,0:T(8,128)(2,1)S(1)} %shard_map.97.refs_0_.refs_2_, bf16[64,768]{1,0:T(8,128)(2,1)S(1)} %collective-permute-done.7.refs_1_.refs_3_, ...), custom_call_target="tpu_custom_call" | custom-call | tf_op jit(solution)/shard_map/pallas_call | solution.py:39
  57.9 1.3 %shard_map.103 = (bf16[256,2048]{1,0:T(8,128)(2,1)}, f32[8,128]{1,0:T(8,128)S(1)}) custom-call(bf16[256,64]{1,0:T(8,128)(2,1)S(1)} %get-tuple-element.41.refs_0_, f32[64,128]{1,0:T(8,128)S(1)} %get-tuple-element.42.refs_1_, bf16[32,1024]{1,0:T(8,128)(2,1)S(1)} %get-tuple-element.55.refs_0_.refs_2_, ...), custom_call_target="tpu_custom_call" | custom-call | tf_op jit(solution)/shard_map/pallas_call | solution.py:39
  59.2 0.5 collective-permute-done.24.refs_4_
  59.7 1.2 %shard_map.107 = bf16[256,2048]{1,0:T(8,128)(2,1)} custom-call(bf16[256,64]{1,0:T(8,128)(2,1)S(1)} %get-tuple-element.41.refs_0_, bf16[16,2048]{1,0:T(8,128)(2,1)S(1)} %get-tuple-element.73.refs_1_, bf16[16,2048]{1,0:T(8,128)(2,1)S(1)} %collective-permute-done.22.refs_2_, bf16[16,2048]{1,0:T(8,128)(2,1)S(1)} %collective-permute-done.23.refs_3_, ...), custom_call_target="tpu_custom_call" | custom-call | tf_op jit(solution)/shard_map/pallas_call | solution.py:39
  (20 shorter events, 0.1 us)
Async XLA Ops:
  0.6 21.0 %copy-start = (bf16[1,512,1536]{2,1,0:T(8,128)(2,1)S(1)}, bf16[1,512,1536]{2,1,0:T(8,128)(2,1)}, u32[]{:S(2)}) copy-start(bf16[1,512,1536]{2,1,0:T(8,128)(2,1)} %param.12) | copy-start | bytes 4718596
  0.6 9.8 %collective-permute-start.1 = (bf16[512,1536]{1,0:T(8,128)(2,1)}, bf16[512,1536]{1,0:T(8,128)(2,1)S(1)}, u32[]{:S(2)}, u32[]{:S(2)}) collective-permute-start(bf16[512,1536]{1,0:T(8,128)(2,1)} %bitcast.5), channel_id=1, source_target_pairs={{0,1},{1,0},{2,3},{3,2},{4,5},{5,4},{6,7},{7,6},{8,9},{9,8},{10,11... | collective-permute-start | bytes 4718600 | tf_op jit(solution)/shard_map/ppermute | solution.py:269
  1.2 9.3 %collective-permute-start.2 = (bf16[512,768]{1,0:T(8,128)(2,1)}, bf16[512,768]{1,0:T(8,128)(2,1)S(1)}, u32[]{:S(2)}, u32[]{:S(2)}) collective-permute-start(bf16[512,768]{1,0:T(8,128)(2,1)} %bitcast.8), channel_id=1, source_target_pairs={{0,1},{1,0},{2,3},{3,2},{4,5},{5,4},{6,7},{7,6},{8,9},{9,8},{10,11... | collective-permute-start | bytes 2359304 | tf_op jit(solution)/shard_map/ppermute | solution.py:269
  3.2 7.3 %collective-permute-start = (bf16[64,1024]{1,0:T(8,128)(2,1)S(1)}, bf16[64,1024]{1,0:T(8,128)(2,1)S(1)}, u32[]{:S(2)}, u32[]{:S(2)}) collective-permute-start(bf16[64,1024]{1,0:T(8,128)(2,1)S(1)} %get-tuple-element.44), channel_id=1, source_target_pairs={{0,2},{1,3},{2,0},{3,1},{4,6},{5,7},{6,4},{7,5},{8,10},{9,11},{10,... | collective-permute-start | bytes 393224 | tf_op jit(solution)/shard_map/ppermute | solution.py:273
  6.2 9.1 %collective-permute-start.12 = (bf16[64,1024]{1,0:T(8,128)(2,1)S(1)}, bf16[64,1024]{1,0:T(8,128)(2,1)S(1)}, u32[]{:S(2)}, u32[]{:S(2)}) collective-permute-start(bf16[64,1024]{1,0:T(8,128)(2,1)S(1)} %get-tuple-element.60), channel_id=1, source_target_pairs={{0,2},{1,3},{2,0},{3,1},{4,6},{5,7},{6,4},{7,5},{8,10},{9,11},{10,... | collective-permute-start | bytes 393224 | tf_op jit(solution)/shard_map/ppermute | solution.py:273
  10.5 9.3 %collective-permute-start.3 = (bf16[16,2048]{1,0:T(8,128)(2,1)S(1)}, bf16[16,2048]{1,0:T(8,128)(2,1)S(1)}, u32[]{:S(2)}, u32[]{:S(2)}) collective-permute-start(bf16[16,2048]{1,0:T(8,128)(2,1)S(1)} %get-tuple-element.48), channel_id=1, source_target_pairs={{0,4},{4,0},{8,12},{12,8},{1,5},{5,1},{9,13},{13,9},{2,6},{6,2},{1... | collective-permute-start | bytes 196616 | tf_op jit(solution)/shard_map/ppermute | solution.py:279
  12.7 7.1 %collective-permute-start.4 = (bf16[16,2048]{1,0:T(8,128)(2,1)S(1)}, bf16[16,2048]{1,0:T(8,128)(2,1)S(1)}, u32[]{:S(2)}, u32[]{:S(2)}) collective-permute-start(bf16[16,2048]{1,0:T(8,128)(2,1)S(1)} %get-tuple-element.49), channel_id=1, source_target_pairs={{0,8},{4,12},{8,0},{12,4},{1,9},{5,13},{9,1},{13,5},{2,10},{6,14},... | collective-permute-start | bytes 196616 | tf_op jit(solution)/shard_map/ppermute | solution.py:279
  15.3 6.4 %collective-permute-start.5 = (bf16[16,2048]{1,0:T(8,128)(2,1)S(1)}, bf16[16,2048]{1,0:T(8,128)(2,1)S(1)}, u32[]{:S(2)}, u32[]{:S(2)}) collective-permute-start(bf16[16,2048]{1,0:T(8,128)(2,1)S(1)} %get-tuple-element.50), channel_id=1, source_target_pairs={{0,12},{4,8},{8,4},{12,0},{1,13},{5,9},{9,5},{13,1},{2,14},{6,10},... | collective-permute-start | bytes 196616 | tf_op jit(solution)/shard_map/ppermute | solution.py:279
  15.3 8.5 %collective-permute-start.13 = (bf16[16,2048]{1,0:T(8,128)(2,1)S(1)}, bf16[16,2048]{1,0:T(8,128)(2,1)S(1)}, u32[]{:S(2)}, u32[]{:S(2)}) collective-permute-start(bf16[16,2048]{1,0:T(8,128)(2,1)S(1)} %get-tuple-element.62), channel_id=1, source_target_pairs={{0,4},{4,0},{8,12},{12,8},{1,5},{5,1},{9,13},{13,9},{2,6},{6,2},{1... | collective-permute-start | bytes 196616 | tf_op jit(solution)/shard_map/ppermute | solution.py:279
  16.3 8.6 %collective-permute-start.14 = (bf16[16,2048]{1,0:T(8,128)(2,1)S(1)}, bf16[16,2048]{1,0:T(8,128)(2,1)S(1)}, u32[]{:S(2)}, u32[]{:S(2)}) collective-permute-start(bf16[16,2048]{1,0:T(8,128)(2,1)S(1)} %get-tuple-element.63), channel_id=1, source_target_pairs={{0,8},{4,12},{8,0},{12,4},{1,9},{5,13},{9,1},{13,5},{2,10},{6,14},... | collective-permute-start | bytes 196616 | tf_op jit(solution)/shard_map/ppermute | solution.py:279
  19.8 6.2 %collective-permute-start.15 = (bf16[16,2048]{1,0:T(8,128)(2,1)S(1)}, bf16[16,2048]{1,0:T(8,128)(2,1)S(1)}, u32[]{:S(2)}, u32[]{:S(2)}) collective-permute-start(bf16[16,2048]{1,0:T(8,128)(2,1)S(1)} %get-tuple-element.64), channel_id=1, source_target_pairs={{0,12},{4,8},{8,4},{12,0},{1,13},{5,9},{9,5},{13,1},{2,14},{6,10},... | collective-permute-start | bytes 196616 | tf_op jit(solution)/shard_map/ppermute | solution.py:279
  21.6 4.3 %copy-start.1 = (bf16[1,512,768]{2,1,0:T(8,128)(2,1)S(1)}, bf16[1,512,768]{2,1,0:T(8,128)(2,1)}, u32[]{:S(2)}) copy-start(bf16[1,512,768]{2,1,0:T(8,128)(2,1)} %param.13) | copy-start | bytes 2359300
  22.2 9.8 %collective-permute-start.6 = (bf16[64,1536]{1,0:T(8,128)(2,1)S(1)}, bf16[64,1536]{1,0:T(8,128)(2,1)S(1)}, u32[]{:S(2)}, u32[]{:S(2)}) collective-permute-start(bf16[64,1536]{1,0:T(8,128)(2,1)S(1)} %get-tuple-element.53), channel_id=1, source_target_pairs={{0,2},{1,3},{2,0},{3,1},{4,6},{5,7},{6,4},{7,5},{8,10},{9,11},{10,... | collective-permute-start | bytes 589832 | tf_op jit(solution)/shard_map/ppermute | solution.py:273
  26.3 5.7 %collective-permute-start.19 = (bf16[64,768]{1,0:T(8,128)(2,1)S(1)}, bf16[64,768]{1,0:T(8,128)(2,1)S(1)}, u32[]{:S(2)}, u32[]{:S(2)}) collective-permute-start(bf16[64,768]{1,0:T(8,128)(2,1)S(1)} %get-tuple-element.70), channel_id=1, source_target_pairs={{0,2},{1,3},{2,0},{3,1},{4,6},{5,7},{6,4},{7,5},{8,10},{9,11},{10,... | collective-permute-start | bytes 294920 | tf_op jit(solution)/shard_map/ppermute | solution.py:273
  32.2 13.2 %collective-permute-start.20 = (bf16[64,1536]{1,0:T(8,128)(2,1)S(1)}, bf16[64,1536]{1,0:T(8,128)(2,1)S(1)}, u32[]{:S(2)}, u32[]{:S(2)}) collective-permute-start(bf16[64,1536]{1,0:T(8,128)(2,1)S(1)} %shard_map.104.refs_0_), channel_id=1, source_target_pairs={{0,2},{1,3},{2,0},{3,1},{4,6},{5,7},{6,4},{7,5},{8,10},{9,11},{10,... | collective-permute-start | bytes 589832 | tf_op jit(solution)/shard_map/ppermute | solution.py:273
  33.8 5.1 %collective-permute-start.7 = (bf16[64,768]{1,0:T(8,128)(2,1)S(1)}, bf16[64,768]{1,0:T(8,128)(2,1)S(1)}, u32[]{:S(2)}, u32[]{:S(2)}) collective-permute-start(bf16[64,768]{1,0:T(8,128)(2,1)S(1)} %shard_map.97.refs_0_.refs_2_), channel_id=1, source_target_pairs={{0,2},{1,3},{2,0},{3,1},{4,6},{5,7},{6,4},{7,5},{8,10},{9,11},{10,... | collective-permute-start | bytes 294920 | tf_op jit(solution)/shard_map/ppermute | solution.py:273
  39.6 5.7 %collective-permute-start.8 = (bf16[32,1024]{1,0:T(8,128)(2,1)S(1)}, bf16[32,1024]{1,0:T(8,128)(2,1)S(1)}, u32[]{:S(2)}, u32[]{:S(2)}) collective-permute-start(bf16[32,1024]{1,0:T(8,128)(2,1)S(1)} %get-tuple-element.56), channel_id=1, source_target_pairs={{0,4},{4,0},{8,12},{12,8},{1,5},{5,1},{9,13},{13,9},{2,6},{6,2},{1... | collective-permute-start | bytes 196616 | tf_op jit(solution)/shard_map/ppermute | solution.py:279
  39.8 8.8 %collective-permute-start.9 = (bf16[32,1024]{1,0:T(8,128)(2,1)S(1)}, bf16[32,1024]{1,0:T(8,128)(2,1)S(1)}, u32[]{:S(2)}, u32[]{:S(2)}) collective-permute-start(bf16[32,1024]{1,0:T(8,128)(2,1)S(1)} %get-tuple-element.57), channel_id=1, source_target_pairs={{0,8},{4,12},{8,0},{12,4},{1,9},{5,13},{9,1},{13,5},{2,10},{6,14},... | collective-permute-start | bytes 196616 | tf_op jit(solution)/shard_map/ppermute | solution.py:279
  41.7 6.9 %collective-permute-start.10 = (bf16[32,1024]{1,0:T(8,128)(2,1)S(1)}, bf16[32,1024]{1,0:T(8,128)(2,1)S(1)}, u32[]{:S(2)}, u32[]{:S(2)}) collective-permute-start(bf16[32,1024]{1,0:T(8,128)(2,1)S(1)} %get-tuple-element.58), channel_id=1, source_target_pairs={{0,12},{4,8},{8,4},{12,0},{1,13},{5,9},{9,5},{13,1},{2,14},{6,10},... | collective-permute-start | bytes 196616 | tf_op jit(solution)/shard_map/ppermute | solution.py:279
  46.5 5.3 %collective-permute-start.21 = (bf16[64,1024]{1,0:T(8,128)(2,1)S(1)}, bf16[64,1024]{1,0:T(8,128)(2,1)S(1)}, u32[]{:S(2)}, u32[]{:S(2)}) collective-permute-start(bf16[64,1024]{1,0:T(8,128)(2,1)S(1)} %get-tuple-element.72), channel_id=1, source_target_pairs={{0,2},{1,3},{2,0},{3,1},{4,6},{5,7},{6,4},{7,5},{8,10},{9,11},{10,... | collective-permute-start | bytes 393224 | tf_op jit(solution)/shard_map/ppermute | solution.py:273
  48.1 3.8 %collective-permute-start.16 = (bf16[128,512]{1,0:T(8,128)(2,1)S(1)}, bf16[128,512]{1,0:T(8,128)(2,1)S(1)}, u32[]{:S(2)}, u32[]{:S(2)}) collective-permute-start(bf16[128,512]{1,0:T(8,128)(2,1)S(1)} %get-tuple-element.66), channel_id=1, source_target_pairs={{0,1},{1,0},{2,3},{3,2},{4,5},{5,4},{6,7},{7,6},{8,9},{9,8},{10,11... | collective-permute-start | bytes 393224 | tf_op jit(solution)/shard_map/ppermute | solution.py:269
  48.1 5.5 %collective-permute-start.17 = (bf16[64,768]{1,0:T(8,128)(2,1)S(1)}, bf16[64,768]{1,0:T(8,128)(2,1)S(1)}, u32[]{:S(2)}, u32[]{:S(2)}) collective-permute-start(bf16[64,768]{1,0:T(8,128)(2,1)S(1)} %shard_map.97.refs_0_.refs_2_), channel_id=1, source_target_pairs={{0,1},{1,0},{2,3},{3,2},{4,5},{5,4},{6,7},{7,6},{8,9},{9,8},{10,11... | collective-permute-start | bytes 294920 | tf_op jit(solution)/shard_map/ppermute | solution.py:269
  48.6 9.2 %collective-permute-start.11 = (bf16[64,1024]{1,0:T(8,128)(2,1)S(1)}, bf16[64,1024]{1,0:T(8,128)(2,1)S(1)}, u32[]{:S(2)}, u32[]{:S(2)}) collective-permute-start(bf16[64,1024]{1,0:T(8,128)(2,1)S(1)} %shard_map.99), channel_id=1, source_target_pairs={{0,2},{1,3},{2,0},{3,1},{4,6},{5,7},{6,4},{7,5},{8,10},{9,11},{10,... | collective-permute-start | bytes 393224 | tf_op jit(solution)/shard_map/ppermute | solution.py:273
  49.3 7.0 %collective-permute-start.18 = (bf16[64,768]{1,0:T(8,128)(2,1)S(1)}, bf16[64,768]{1,0:T(8,128)(2,1)S(1)}, u32[]{:S(2)}, u32[]{:S(2)}) collective-permute-start(bf16[64,768]{1,0:T(8,128)(2,1)S(1)} %collective-permute-done.7.refs_1_.refs_3_), channel_id=1, source_target_pairs={{0,1},{1,0},{2,3},{3,2},{4,5},{5,4},{6,7},{7,6},{8,9},{9,8},{10,11... | collective-permute-start | bytes 294920 | tf_op jit(solution)/shard_map/ppermute | solution.py:269
  51.8 7.3 %collective-permute-start.22 = (bf16[16,2048]{1,0:T(8,128)(2,1)S(1)}, bf16[16,2048]{1,0:T(8,128)(2,1)S(1)}, u32[]{:S(2)}, u32[]{:S(2)}) collective-permute-start(bf16[16,2048]{1,0:T(8,128)(2,1)S(1)} %get-tuple-element.74), channel_id=1, source_target_pairs={{0,4},{4,0},{8,12},{12,8},{1,5},{5,1},{9,13},{13,9},{2,6},{6,2},{1... | collective-permute-start | bytes 196616 | tf_op jit(solution)/shard_map/ppermute | solution.py:279
  51.9 7.3 %collective-permute-start.23 = (bf16[16,2048]{1,0:T(8,128)(2,1)S(1)}, bf16[16,2048]{1,0:T(8,128)(2,1)S(1)}, u32[]{:S(2)}, u32[]{:S(2)}) collective-permute-start(bf16[16,2048]{1,0:T(8,128)(2,1)S(1)} %get-tuple-element.75), channel_id=1, source_target_pairs={{0,8},{4,12},{8,0},{12,4},{1,9},{5,13},{9,1},{13,5},{2,10},{6,14},... | collective-permute-start | bytes 196616 | tf_op jit(solution)/shard_map/ppermute | solution.py:279
  53.6 6.1 %collective-permute-start.24 = (bf16[16,2048]{1,0:T(8,128)(2,1)S(1)}, bf16[16,2048]{1,0:T(8,128)(2,1)S(1)}, u32[]{:S(2)}, u32[]{:S(2)}) collective-permute-start(bf16[16,2048]{1,0:T(8,128)(2,1)S(1)} %get-tuple-element.76), channel_id=1, source_target_pairs={{0,12},{4,8},{8,4},{12,0},{1,13},{5,9},{9,5},{13,1},{2,14},{6,10},... | collective-permute-start | bytes 196616 | tf_op jit(solution)/shard_map/ppermute | solution.py:279

commit v11 on v10

--- a/solution.py
+++ b/solution.py
@@ -329,7 +329,9 @@
             (*hidden, out_own, out_sib),
         )
     )
-    (d_pre,) = call(d_pre_kernel, [shape((slots, 2 * feed))], (*pre, *back))
+    (d_pre,) = call(
+        d_pre_kernel, [shape((slots, 2 * feed))], (*pre, *back), after=hidden[1:]
+    )
     d_pre = (d_pre, *to_x([d_pre] * (spread - 1)))
     near, *far = call(
         bound(d_rows_kernel, spread), by_x, (*d_pre, in_own, in_sib), after=expert_out[1:2]

time: 61 us -> 59.3 us (0.972)
  waiting for transfers between devices: 21.3 us -> 18.7 us
  starting transfers between devices: 29.8 us -> 30.7 us
    ppermute x8, waiting for transfers between devices: 15.5 us -> 10.8 us  [to_x(): lax.ppermute(value, 'fsdp', [(i, i ^ (k + 1) * CORES) for i in range(part...]
    ppermute x12, waiting for transfers between devices: 5.8 us -> 7.87 us  [to_expert(): lax.ppermute(value, 'expert', [(i, i ^ ke) for i in range(groups)])]
    ppermute x8, starting transfers between devices: 10.6 us -> 11.7 us  [to_x(): lax.ppermute(value, 'fsdp', [(i, i ^ (k + 1) * CORES) for i in range(part...]
  transfers between devices with their start and end apart: 25 -> 25, of which waited for: 9 -> 12; matrix products, arithmetic and copies ran while one was open for 0% -> 0% of each run, Pallas kernels for 13% -> 13%
where the time goes in v11:
time: 59.3 us; the launch traced here: 59.1 us
  starting transfers between devices  30.7 us (52%)
  waiting for transfers between devices  18.7 us (32%)
  Pallas kernels  8.99 us (15%)
  between operations  0.75 us (1%)
    ppermute x12, starting transfers between devices, to_expert(): lax.ppermute(value, 'expert', [(i, i ^ ke) for i in range(groups)])  17.9 us
    ppermute x8, starting transfers between devices, to_x(): lax.ppermute(value, 'fsdp', [(i, i ^ (k + 1) * CORES) for i in range(part...  11.7 us
    ppermute x8, waiting for transfers between devices, to_x(): lax.ppermute(value, 'fsdp', [(i, i ^ (k + 1) * CORES) for i in range(part...  10.8 us
    pallas_call x14, Pallas kernels, call(): pl.pallas_call(kernel, out_shape=out_shape, in_specs=specs, compiler_para...  8.99 us
    ppermute x12, waiting for transfers between devices, to_expert(): lax.ppermute(value, 'expert', [(i, i ^ ke) for i in range(groups)])  7.87 us
  transfers between devices with their start and end apart: 25, of which 12 were waited for; matrix products, arithmetic and copies ran while one was open for 0% of the time, Pallas kernels for 13%

profile of v11, /device:TPU:0, one launch (start us, length us, event | category | flops | bytes accessed | tf_op | source)
XLA Modules:
  0.0 59.1 jit_solution(8502263185478395239)
XLA Ops:
  0.6 0.5 collective-permute-start.1
  1.2 0.1 collective-permute-start.2
  1.2 1.9 %shard_map.94 = (bf16[64,1024]{1,0:T(8,128)(2,1)S(1)}, bf16[64,1024]{1,0:T(8,128)(2,1)S(1)}, bf16[64,1024]{1,0:T(8,128)(2,1)S(1)}, bf16[64,1024]{1,0:T(8,128)(2,...) custom-call(s32[8,256]{1,0:T(8,128)} %bitcast.11, f32[8,256]{1,0:T(8,128)} %bitcast.12, s32[1,256]{1,0:T(1,128)} %refs_2_.1, ...), custom_call_target="tpu_custom_call" | custom-call | tf_op jit(solution)/shard_map/pallas_call | solution.py:39
  3.2 3.0 %collective-permute-start = (bf16[64,1024]{1,0:T(8,128)(2,1)S(1)}, bf16[64,1024]{1,0:T(8,128)(2,1)S(1)}, u32[]{:S(2)}, u32[]{:S(2)}) collective-permute-start(bf16[64,1024]{1,0:T(8,128)(2,1)S(1)} %get-tuple-element.44), channel_id=1, source_target_pairs={{0,2},{1,3},{2,0},{3,1},{4,6},{5,7},{6,4},{7,5},{8,10},{9,11},{10,... | collective-permute-start | bytes 393224 | tf_op jit(solution)/shard_map/ppermute | solution.py:273
  6.2 0.1 collective-permute-start.12
  6.2 4.2 %collective-permute-done.refs_1_ = bf16[64,1024]{1,0:T(8,128)(2,1)S(1)} collective-permute-done((bf16[64,1024]{1,0:T(8,128)(2,1)S(1)}, bf16[64,1024]{1,0:T(8,128)(2,1)S(1)}, u32[]{:S(2)}, u32[]{:S(2)}) %collective-permute-start) | collective-permute-done | bytes 131104 | tf_op jit(solution)/shard_map/ppermute | solution.py:273
  10.5 0.0 collective-permute-done.1.refs_5_.refs_3_
  10.5 2.2 %collective-permute-start.3 = (bf16[16,2048]{1,0:T(8,128)(2,1)S(1)}, bf16[16,2048]{1,0:T(8,128)(2,1)S(1)}, u32[]{:S(2)}, u32[]{:S(2)}) collective-permute-start(bf16[16,2048]{1,0:T(8,128)(2,1)S(1)} %get-tuple-element.48), channel_id=1, source_target_pairs={{0,4},{4,0},{8,12},{12,8},{1,5},{5,1},{9,13},{13,9},{2,6},{6,2},{1... | collective-permute-start | bytes 196616 | tf_op jit(solution)/shard_map/ppermute | solution.py:279
  12.7 2.6 %collective-permute-start.4 = (bf16[16,2048]{1,0:T(8,128)(2,1)S(1)}, bf16[16,2048]{1,0:T(8,128)(2,1)S(1)}, u32[]{:S(2)}, u32[]{:S(2)}) collective-permute-start(bf16[16,2048]{1,0:T(8,128)(2,1)S(1)} %get-tuple-element.49), channel_id=1, source_target_pairs={{0,8},{4,12},{8,0},{12,4},{1,9},{5,13},{9,1},{13,5},{2,10},{6,14},... | collective-permute-start | bytes 196616 | tf_op jit(solution)/shard_map/ppermute | solution.py:279
  15.3 0.0 collective-permute-start.5
  15.3 1.0 %collective-permute-start.13 = (bf16[16,2048]{1,0:T(8,128)(2,1)S(1)}, bf16[16,2048]{1,0:T(8,128)(2,1)S(1)}, u32[]{:S(2)}, u32[]{:S(2)}) collective-permute-start(bf16[16,2048]{1,0:T(8,128)(2,1)S(1)} %get-tuple-element.62), channel_id=1, source_target_pairs={{0,4},{4,0},{8,12},{12,8},{1,5},{5,1},{9,13},{13,9},{2,6},{6,2},{1... | collective-permute-start | bytes 196616 | tf_op jit(solution)/shard_map/ppermute | solution.py:279
  16.3 3.5 %collective-permute-start.14 = (bf16[16,2048]{1,0:T(8,128)(2,1)S(1)}, bf16[16,2048]{1,0:T(8,128)(2,1)S(1)}, u32[]{:S(2)}, u32[]{:S(2)}) collective-permute-start(bf16[16,2048]{1,0:T(8,128)(2,1)S(1)} %get-tuple-element.63), channel_id=1, source_target_pairs={{0,8},{4,12},{8,0},{12,4},{1,9},{5,13},{9,1},{13,5},{2,10},{6,14},... | collective-permute-start | bytes 196616 | tf_op jit(solution)/shard_map/ppermute | solution.py:279
  19.8 0.0 collective-permute-start.15
  19.8 1.9 %collective-permute-done.5.refs_3_ = bf16[16,2048]{1,0:T(8,128)(2,1)S(1)} collective-permute-done((bf16[16,2048]{1,0:T(8,128)(2,1)S(1)}, bf16[16,2048]{1,0:T(8,128)(2,1)S(1)}, u32[]{:S(2)}, u32[]{:S(2)}) %collective-permute-start.5) | collective-permute-done | bytes 65568 | tf_op jit(solution)/shard_map/ppermute | solution.py:279
  21.7 0.6 shard_map.96
  22.2 1.6 %collective-permute-start.6 = (bf16[64,1536]{1,0:T(8,128)(2,1)S(1)}, bf16[64,1536]{1,0:T(8,128)(2,1)S(1)}, u32[]{:S(2)}, u32[]{:S(2)}) collective-permute-start(bf16[64,1536]{1,0:T(8,128)(2,1)S(1)} %get-tuple-element.53), channel_id=1, source_target_pairs={{0,2},{1,3},{2,0},{3,1},{4,6},{5,7},{6,4},{7,5},{8,10},{9,11},{10,... | collective-permute-start | bytes 589832 | tf_op jit(solution)/shard_map/ppermute | solution.py:273
  23.8 0.0 collective-permute-done.13.refs_1_
  23.8 1.1 %collective-permute-done.14.refs_2_ = bf16[16,2048]{1,0:T(8,128)(2,1)S(1)} collective-permute-done((bf16[16,2048]{1,0:T(8,128)(2,1)S(1)}, bf16[16,2048]{1,0:T(8,128)(2,1)S(1)}, u32[]{:S(2)}, u32[]{:S(2)}) %collective-permute-start.14) | collective-permute-done | bytes 65568 | tf_op jit(solution)/shard_map/ppermute | solution.py:279
  24.9 1.1 %collective-permute-done.15.refs_3_ = bf16[16,2048]{1,0:T(8,128)(2,1)S(1)} collective-permute-done((bf16[16,2048]{1,0:T(8,128)(2,1)S(1)}, bf16[16,2048]{1,0:T(8,128)(2,1)S(1)}, u32[]{:S(2)}, u32[]{:S(2)}) %collective-permute-start.15) | collective-permute-done | bytes 65568 | tf_op jit(solution)/shard_map/ppermute | solution.py:279
  25.9 0.4 shard_map.101
  26.3 1.6 %collective-permute-start.19 = (bf16[64,768]{1,0:T(8,128)(2,1)S(1)}, bf16[64,768]{1,0:T(8,128)(2,1)S(1)}, u32[]{:S(2)}, u32[]{:S(2)}) collective-permute-start(bf16[64,768]{1,0:T(8,128)(2,1)S(1)} %get-tuple-element.70), channel_id=1, source_target_pairs={{0,2},{1,3},{2,0},{3,1},{4,6},{5,7},{6,4},{7,5},{8,10},{9,11},{10,... | collective-permute-start | bytes 294920 | tf_op jit(solution)/shard_map/ppermute | solution.py:273
  27.9 1.7 %collective-permute-done.6.refs_1_ = bf16[64,1536]{1,0:T(8,128)(2,1)S(1)} collective-permute-done((bf16[64,1536]{1,0:T(8,128)(2,1)S(1)}, bf16[64,1536]{1,0:T(8,128)(2,1)S(1)}, u32[]{:S(2)}, u32[]{:S(2)}) %collective-permute-start.6) | collective-permute-done | bytes 196640 | tf_op jit(solution)/shard_map/ppermute | solution.py:273
  29.5 0.1 shard_map.97.refs_0_.refs_2_
  29.6 1.6 %collective-permute-start.7 = (bf16[64,768]{1,0:T(8,128)(2,1)S(1)}, bf16[64,768]{1,0:T(8,128)(2,1)S(1)}, u32[]{:S(2)}, u32[]{:S(2)}) collective-permute-start(bf16[64,768]{1,0:T(8,128)(2,1)S(1)} %shard_map.97.refs_0_.refs_2_), channel_id=1, source_target_pairs={{0,2},{1,3},{2,0},{3,1},{4,6},{5,7},{6,4},{7,5},{8,10},{9,11},{10,... | collective-permute-start | bytes 294920 | tf_op jit(solution)/shard_map/ppermute | solution.py:273
  31.2 0.0 collective-permute-done.19.refs_3_
  31.2 4.0 %collective-permute-done.7.refs_1_.refs_3_.refs_4_ = bf16[64,768]{1,0:T(8,128)(2,1)S(1)} collective-permute-done((bf16[64,768]{1,0:T(8,128)(2,1)S(1)}, bf16[64,768]{1,0:T(8,128)(2,1)S(1)}, u32[]{:S(2)}, u32[]{:S(2)}) %collective-permute-start.7) | collective-permute-done | bytes 98336 | tf_op jit(solution)/shard_map/ppermute | solution.py:273
  35.2 0.1 shard_map.104.refs_0_
  35.3 1.5 %collective-permute-start.20 = (bf16[64,1536]{1,0:T(8,128)(2,1)S(1)}, bf16[64,1536]{1,0:T(8,128)(2,1)S(1)}, u32[]{:S(2)}, u32[]{:S(2)}) collective-permute-start(bf16[64,1536]{1,0:T(8,128)(2,1)S(1)} %shard_map.104.refs_0_), channel_id=1, source_target_pairs={{0,2},{1,3},{2,0},{3,1},{4,6},{5,7},{6,4},{7,5},{8,10},{9,11},{10,... | collective-permute-start | bytes 589832 | tf_op jit(solution)/shard_map/ppermute | solution.py:273
  36.8 0.6 %shard_map.98 = (bf16[32,1024]{1,0:T(8,128)(2,1)S(1)}, bf16[32,1024]{1,0:T(8,128)(2,1)S(1)}, bf16[32,1024]{1,0:T(8,128)(2,1)S(1)}, bf16[32,1024]{1,0:T(8,128)(2,1)S(1)}) custom-call(bf16[64,768]{1,0:T(8,128)(2,1)S(1)} %shard_map.97.refs_0_.refs_2_, bf16[64,768]{1,0:T(8,128)(2,1)S(1)} %collective-permute-done.7.refs_1_.refs_3_.refs_4_, ...), custom_call_target="tpu_custom_call" | custom-call | tf_op jit(solution)/shard_map/pallas_call | solution.py:39
  37.5 2.4 %collective-permute-start.8 = (bf16[32,1024]{1,0:T(8,128)(2,1)S(1)}, bf16[32,1024]{1,0:T(8,128)(2,1)S(1)}, u32[]{:S(2)}, u32[]{:S(2)}) collective-permute-start(bf16[32,1024]{1,0:T(8,128)(2,1)S(1)} %get-tuple-element.56), channel_id=1, source_target_pairs={{0,4},{4,0},{8,12},{12,8},{1,5},{5,1},{9,13},{13,9},{2,6},{6,2},{1... | collective-permute-start | bytes 196616 | tf_op jit(solution)/shard_map/ppermute | solution.py:279
  39.9 1.0 %collective-permute-start.10 = (bf16[32,1024]{1,0:T(8,128)(2,1)S(1)}, bf16[32,1024]{1,0:T(8,128)(2,1)S(1)}, u32[]{:S(2)}, u32[]{:S(2)}) collective-permute-start(bf16[32,1024]{1,0:T(8,128)(2,1)S(1)} %get-tuple-element.58), channel_id=1, source_target_pairs={{0,12},{4,8},{8,4},{12,0},{1,13},{5,9},{9,5},{13,1},{2,14},{6,10},... | collective-permute-start | bytes 196616 | tf_op jit(solution)/shard_map/ppermute | solution.py:279
  40.9 0.6 collective-permute-start.9
  41.4 0.7 %collective-permute-done.8.refs_1_.refs_3_.refs_4_ = bf16[32,1024]{1,0:T(8,128)(2,1)S(1)} collective-permute-done((bf16[32,1024]{1,0:T(8,128)(2,1)S(1)}, bf16[32,1024]{1,0:T(8,128)(2,1)S(1)}, u32[]{:S(2)}, u32[]{:S(2)}) %collective-permute-start.8) | collective-permute-done | bytes 65568 | tf_op jit(solution)/shard_map/ppermute | solution.py:279
  42.1 1.1 %shard_map.105 = (bf16[64,1024]{1,0:T(8,128)(2,1)S(1)}, bf16[64,1024]{1,0:T(8,128)(2,1)S(1)}) custom-call(bf16[64,1536]{1,0:T(8,128)(2,1)S(1)} %shard_map.104.refs_0_, bf16[64,1536]{1,0:T(8,128)(2,1)S(1)} %collective-permute-done.20.refs_1_, bf16[512,1536]{1,0:T(8,128)(2,1)S(1)} %bitcast.7, bf16[512,1536]{1,0:T(8,128)(2,1)S(1)} %collective-permute-done.1.refs_5_.refs_3_, ...), custom_call_target="tpu_custom_call" | custom-call | tf_op jit(solution)/shard_map/pallas_call | solution.py:39
  43.3 1.8 %collective-permute-start.21 = (bf16[64,1024]{1,0:T(8,128)(2,1)S(1)}, bf16[64,1024]{1,0:T(8,128)(2,1)S(1)}, u32[]{:S(2)}, u32[]{:S(2)}) collective-permute-start(bf16[64,1024]{1,0:T(8,128)(2,1)S(1)} %get-tuple-element.72), channel_id=1, source_target_pairs={{0,2},{1,3},{2,0},{3,1},{4,6},{5,7},{6,4},{7,5},{8,10},{9,11},{10,... | collective-permute-start | bytes 393224 | tf_op jit(solution)/shard_map/ppermute | solution.py:273
  45.1 0.5 collective-permute-start.17
  45.6 0.4 collective-permute-done.10.refs_3_.refs_5_
  46.0 1.3 %collective-permute-done.9.refs_2_.refs_4_ = bf16[32,1024]{1,0:T(8,128)(2,1)S(1)} collective-permute-done((bf16[32,1024]{1,0:T(8,128)(2,1)S(1)}, bf16[32,1024]{1,0:T(8,128)(2,1)S(1)}, u32[]{:S(2)}, u32[]{:S(2)}) %collective-permute-start.9) | collective-permute-done | bytes 65568 | tf_op jit(solution)/shard_map/ppermute | solution.py:279
  47.4 0.6 %collective-permute-start.11 = (bf16[64,1024]{1,0:T(8,128)(2,1)S(1)}, bf16[64,1024]{1,0:T(8,128)(2,1)S(1)}, u32[]{:S(2)}, u32[]{:S(2)}) collective-permute-start(bf16[64,1024]{1,0:T(8,128)(2,1)S(1)} %shard_map.99), channel_id=1, source_target_pairs={{0,2},{1,3},{2,0},{3,1},{4,6},{5,7},{6,4},{7,5},{8,10},{9,11},{10,... | collective-permute-start | bytes 393224 | tf_op jit(solution)/shard_map/ppermute | solution.py:273
  48.0 1.0 %collective-permute-done.21.refs_1_ = bf16[64,1024]{1,0:T(8,128)(2,1)S(1)} collective-permute-done((bf16[64,1024]{1,0:T(8,128)(2,1)S(1)}, bf16[64,1024]{1,0:T(8,128)(2,1)S(1)}, u32[]{:S(2)}, u32[]{:S(2)}) %collective-permute-start.21) | collective-permute-done | bytes 131104 | tf_op jit(solution)/shard_map/ppermute | solution.py:273
  49.0 2.2 %collective-permute-start.22 = (bf16[16,2048]{1,0:T(8,128)(2,1)S(1)}, bf16[16,2048]{1,0:T(8,128)(2,1)S(1)}, u32[]{:S(2)}, u32[]{:S(2)}) collective-permute-start(bf16[16,2048]{1,0:T(8,128)(2,1)S(1)} %get-tuple-element.74), channel_id=1, source_target_pairs={{0,4},{4,0},{8,12},{12,8},{1,5},{5,1},{9,13},{13,9},{2,6},{6,2},{1... | collective-permute-start | bytes 196616 | tf_op jit(solution)/shard_map/ppermute | solution.py:279
  51.2 0.6 collective-permute-start.23
  51.8 1.9 %collective-permute-start.24 = (bf16[16,2048]{1,0:T(8,128)(2,1)S(1)}, bf16[16,2048]{1,0:T(8,128)(2,1)S(1)}, u32[]{:S(2)}, u32[]{:S(2)}) collective-permute-start(bf16[16,2048]{1,0:T(8,128)(2,1)S(1)} %get-tuple-element.76), channel_id=1, source_target_pairs={{0,12},{4,8},{8,4},{12,0},{1,13},{5,9},{9,5},{13,1},{2,14},{6,10},... | collective-permute-start | bytes 196616 | tf_op jit(solution)/shard_map/ppermute | solution.py:279
  53.6 1.6 %shard_map.102 = (f32[512,768]{1,0:T(8,128)}, f32[8,128]{1,0:T(8,128)S(1)}) custom-call(bf16[128,512]{1,0:T(8,128)(2,1)S(1)} %get-tuple-element.65.refs_0_, bf16[128,512]{1,0:T(8,128)(2,1)S(1)} %collective-permute-done.16.refs_1_, bf16[64,768]{1,0:T(8,128)(2,1)S(1)} %shard_map.97.refs_0_.refs_2_, ...), custom_call_target="tpu_custom_call" | custom-call | tf_op jit(solution)/shard_map/pallas_call | solution.py:39
  55.2 1.3 %shard_map.103 = (bf16[256,2048]{1,0:T(8,128)(2,1)}, f32[8,128]{1,0:T(8,128)S(1)}) custom-call(bf16[256,64]{1,0:T(8,128)(2,1)S(1)} %get-tuple-element.41.refs_0_, f32[64,128]{1,0:T(8,128)S(1)} %get-tuple-element.42.refs_1_, bf16[32,1024]{1,0:T(8,128)(2,1)S(1)} %get-tuple-element.55.refs_0_.refs_2_, ...), custom_call_target="tpu_custom_call" | custom-call | tf_op jit(solution)/shard_map/pallas_call | solution.py:39
  56.5 0.3 collective-permute-done.23.refs_3_
  56.8 1.2 %collective-permute-done.24.refs_4_ = bf16[16,2048]{1,0:T(8,128)(2,1)S(1)} collective-permute-done((bf16[16,2048]{1,0:T(8,128)(2,1)S(1)}, bf16[16,2048]{1,0:T(8,128)(2,1)S(1)}, u32[]{:S(2)}, u32[]{:S(2)}) %collective-permute-start.24) | collective-permute-done | bytes 65568 | tf_op jit(solution)/shard_map/ppermute | solution.py:279
  57.9 1.2 %shard_map.107 = bf16[256,2048]{1,0:T(8,128)(2,1)} custom-call(bf16[256,64]{1,0:T(8,128)(2,1)S(1)} %get-tuple-element.41.refs_0_, bf16[16,2048]{1,0:T(8,128)(2,1)S(1)} %get-tuple-element.73.refs_1_, bf16[16,2048]{1,0:T(8,128)(2,1)S(1)} %collective-permute-done.22.refs_2_, bf16[16,2048]{1,0:T(8,128)(2,1)S(1)} %collective-permute-done.23.refs_3_, ...), custom_call_target="tpu_custom_call" | custom-call | tf_op jit(solution)/shard_map/pallas_call | solution.py:39
  (20 shorter events, 0.1 us)
Async XLA Ops:
  0.6 21.0 %copy-start = (bf16[1,512,1536]{2,1,0:T(8,128)(2,1)S(1)}, bf16[1,512,1536]{2,1,0:T(8,128)(2,1)}, u32[]{:S(2)}) copy-start(bf16[1,512,1536]{2,1,0:T(8,128)(2,1)} %param.12) | copy-start | bytes 4718596
  0.6 9.8 %collective-permute-start.1 = (bf16[512,1536]{1,0:T(8,128)(2,1)}, bf16[512,1536]{1,0:T(8,128)(2,1)S(1)}, u32[]{:S(2)}, u32[]{:S(2)}) collective-permute-start(bf16[512,1536]{1,0:T(8,128)(2,1)} %bitcast.5), channel_id=1, source_target_pairs={{0,1},{1,0},{2,3},{3,2},{4,5},{5,4},{6,7},{7,6},{8,9},{9,8},{10,11... | collective-permute-start | bytes 4718600 | tf_op jit(solution)/shard_map/ppermute | solution.py:269
  1.2 9.3 %collective-permute-start.2 = (bf16[512,768]{1,0:T(8,128)(2,1)}, bf16[512,768]{1,0:T(8,128)(2,1)S(1)}, u32[]{:S(2)}, u32[]{:S(2)}) collective-permute-start(bf16[512,768]{1,0:T(8,128)(2,1)} %bitcast.8), channel_id=1, source_target_pairs={{0,1},{1,0},{2,3},{3,2},{4,5},{5,4},{6,7},{7,6},{8,9},{9,8},{10,11... | collective-permute-start | bytes 2359304 | tf_op jit(solution)/shard_map/ppermute | solution.py:269
  3.2 7.3 %collective-permute-start = (bf16[64,1024]{1,0:T(8,128)(2,1)S(1)}, bf16[64,1024]{1,0:T(8,128)(2,1)S(1)}, u32[]{:S(2)}, u32[]{:S(2)}) collective-permute-start(bf16[64,1024]{1,0:T(8,128)(2,1)S(1)} %get-tuple-element.44), channel_id=1, source_target_pairs={{0,2},{1,3},{2,0},{3,1},{4,6},{5,7},{6,4},{7,5},{8,10},{9,11},{10,... | collective-permute-start | bytes 393224 | tf_op jit(solution)/shard_map/ppermute | solution.py:273
  6.2 9.1 %collective-permute-start.12 = (bf16[64,1024]{1,0:T(8,128)(2,1)S(1)}, bf16[64,1024]{1,0:T(8,128)(2,1)S(1)}, u32[]{:S(2)}, u32[]{:S(2)}) collective-permute-start(bf16[64,1024]{1,0:T(8,128)(2,1)S(1)} %get-tuple-element.60), channel_id=1, source_target_pairs={{0,2},{1,3},{2,0},{3,1},{4,6},{5,7},{6,4},{7,5},{8,10},{9,11},{10,... | collective-permute-start | bytes 393224 | tf_op jit(solution)/shard_map/ppermute | solution.py:273
  10.5 9.3 %collective-permute-start.3 = (bf16[16,2048]{1,0:T(8,128)(2,1)S(1)}, bf16[16,2048]{1,0:T(8,128)(2,1)S(1)}, u32[]{:S(2)}, u32[]{:S(2)}) collective-permute-start(bf16[16,2048]{1,0:T(8,128)(2,1)S(1)} %get-tuple-element.48), channel_id=1, source_target_pairs={{0,4},{4,0},{8,12},{12,8},{1,5},{5,1},{9,13},{13,9},{2,6},{6,2},{1... | collective-permute-start | bytes 196616 | tf_op jit(solution)/shard_map/ppermute | solution.py:279
  12.7 7.1 %collective-permute-start.4 = (bf16[16,2048]{1,0:T(8,128)(2,1)S(1)}, bf16[16,2048]{1,0:T(8,128)(2,1)S(1)}, u32[]{:S(2)}, u32[]{:S(2)}) collective-permute-start(bf16[16,2048]{1,0:T(8,128)(2,1)S(1)} %get-tuple-element.49), channel_id=1, source_target_pairs={{0,8},{4,12},{8,0},{12,4},{1,9},{5,13},{9,1},{13,5},{2,10},{6,14},... | collective-permute-start | bytes 196616 | tf_op jit(solution)/shard_map/ppermute | solution.py:279
  15.3 6.4 %collective-permute-start.5 = (bf16[16,2048]{1,0:T(8,128)(2,1)S(1)}, bf16[16,2048]{1,0:T(8,128)(2,1)S(1)}, u32[]{:S(2)}, u32[]{:S(2)}) collective-permute-start(bf16[16,2048]{1,0:T(8,128)(2,1)S(1)} %get-tuple-element.50), channel_id=1, source_target_pairs={{0,12},{4,8},{8,4},{12,0},{1,13},{5,9},{9,5},{13,1},{2,14},{6,10},... | collective-permute-start | bytes 196616 | tf_op jit(solution)/shard_map/ppermute | solution.py:279
  15.3 8.5 %collective-permute-start.13 = (bf16[16,2048]{1,0:T(8,128)(2,1)S(1)}, bf16[16,2048]{1,0:T(8,128)(2,1)S(1)}, u32[]{:S(2)}, u32[]{:S(2)}) collective-permute-start(bf16[16,2048]{1,0:T(8,128)(2,1)S(1)} %get-tuple-element.62), channel_id=1, source_target_pairs={{0,4},{4,0},{8,12},{12,8},{1,5},{5,1},{9,13},{13,9},{2,6},{6,2},{1... | collective-permute-start | bytes 196616 | tf_op jit(solution)/shard_map/ppermute | solution.py:279
  16.3 8.6 %collective-permute-start.14 = (bf16[16,2048]{1,0:T(8,128)(2,1)S(1)}, bf16[16,2048]{1,0:T(8,128)(2,1)S(1)}, u32[]{:S(2)}, u32[]{:S(2)}) collective-permute-start(bf16[16,2048]{1,0:T(8,128)(2,1)S(1)} %get-tuple-element.63), channel_id=1, source_target_pairs={{0,8},{4,12},{8,0},{12,4},{1,9},{5,13},{9,1},{13,5},{2,10},{6,14},... | collective-permute-start | bytes 196616 | tf_op jit(solution)/shard_map/ppermute | solution.py:279
  19.8 6.2 %collective-permute-start.15 = (bf16[16,2048]{1,0:T(8,128)(2,1)S(1)}, bf16[16,2048]{1,0:T(8,128)(2,1)S(1)}, u32[]{:S(2)}, u32[]{:S(2)}) collective-permute-start(bf16[16,2048]{1,0:T(8,128)(2,1)S(1)} %get-tuple-element.64), channel_id=1, source_target_pairs={{0,12},{4,8},{8,4},{12,0},{1,13},{5,9},{9,5},{13,1},{2,14},{6,10},... | collective-permute-start | bytes 196616 | tf_op jit(solution)/shard_map/ppermute | solution.py:279
  21.6 4.3 %copy-start.1 = (bf16[1,512,768]{2,1,0:T(8,128)(2,1)S(1)}, bf16[1,512,768]{2,1,0:T(8,128)(2,1)}, u32[]{:S(2)}) copy-start(bf16[1,512,768]{2,1,0:T(8,128)(2,1)} %param.13) | copy-start | bytes 2359300
  22.2 7.3 %collective-permute-start.6 = (bf16[64,1536]{1,0:T(8,128)(2,1)S(1)}, bf16[64,1536]{1,0:T(8,128)(2,1)S(1)}, u32[]{:S(2)}, u32[]{:S(2)}) collective-permute-start(bf16[64,1536]{1,0:T(8,128)(2,1)S(1)} %get-tuple-element.53), channel_id=1, source_target_pairs={{0,2},{1,3},{2,0},{3,1},{4,6},{5,7},{6,4},{7,5},{8,10},{9,11},{10,... | collective-permute-start | bytes 589832 | tf_op jit(solution)/shard_map/ppermute | solution.py:273
  26.3 4.9 %collective-permute-start.19 = (bf16[64,768]{1,0:T(8,128)(2,1)S(1)}, bf16[64,768]{1,0:T(8,128)(2,1)S(1)}, u32[]{:S(2)}, u32[]{:S(2)}) collective-permute-start(bf16[64,768]{1,0:T(8,128)(2,1)S(1)} %get-tuple-element.70), channel_id=1, source_target_pairs={{0,2},{1,3},{2,0},{3,1},{4,6},{5,7},{6,4},{7,5},{8,10},{9,11},{10,... | collective-permute-start | bytes 294920 | tf_op jit(solution)/shard_map/ppermute | solution.py:273
  29.6 5.5 %collective-permute-start.7 = (bf16[64,768]{1,0:T(8,128)(2,1)S(1)}, bf16[64,768]{1,0:T(8,128)(2,1)S(1)}, u32[]{:S(2)}, u32[]{:S(2)}) collective-permute-start(bf16[64,768]{1,0:T(8,128)(2,1)S(1)} %shard_map.97.refs_0_.refs_2_), channel_id=1, source_target_pairs={{0,2},{1,3},{2,0},{3,1},{4,6},{5,7},{6,4},{7,5},{8,10},{9,11},{10,... | collective-permute-start | bytes 294920 | tf_op jit(solution)/shard_map/ppermute | solution.py:273
  35.3 6.8 %collective-permute-start.20 = (bf16[64,1536]{1,0:T(8,128)(2,1)S(1)}, bf16[64,1536]{1,0:T(8,128)(2,1)S(1)}, u32[]{:S(2)}, u32[]{:S(2)}) collective-permute-start(bf16[64,1536]{1,0:T(8,128)(2,1)S(1)} %shard_map.104.refs_0_), channel_id=1, source_target_pairs={{0,2},{1,3},{2,0},{3,1},{4,6},{5,7},{6,4},{7,5},{8,10},{9,11},{10,... | collective-permute-start | bytes 589832 | tf_op jit(solution)/shard_map/ppermute | solution.py:273
  37.5 4.6 %collective-permute-start.8 = (bf16[32,1024]{1,0:T(8,128)(2,1)S(1)}, bf16[32,1024]{1,0:T(8,128)(2,1)S(1)}, u32[]{:S(2)}, u32[]{:S(2)}) collective-permute-start(bf16[32,1024]{1,0:T(8,128)(2,1)S(1)} %get-tuple-element.56), channel_id=1, source_target_pairs={{0,4},{4,0},{8,12},{12,8},{1,5},{5,1},{9,13},{13,9},{2,6},{6,2},{1... | collective-permute-start | bytes 196616 | tf_op jit(solution)/shard_map/ppermute | solution.py:279
  39.9 6.1 %collective-permute-start.10 = (bf16[32,1024]{1,0:T(8,128)(2,1)S(1)}, bf16[32,1024]{1,0:T(8,128)(2,1)S(1)}, u32[]{:S(2)}, u32[]{:S(2)}) collective-permute-start(bf16[32,1024]{1,0:T(8,128)(2,1)S(1)} %get-tuple-element.58), channel_id=1, source_target_pairs={{0,12},{4,8},{8,4},{12,0},{1,13},{5,9},{9,5},{13,1},{2,14},{6,10},... | collective-permute-start | bytes 196616 | tf_op jit(solution)/shard_map/ppermute | solution.py:279
  40.9 6.5 %collective-permute-start.9 = (bf16[32,1024]{1,0:T(8,128)(2,1)S(1)}, bf16[32,1024]{1,0:T(8,128)(2,1)S(1)}, u32[]{:S(2)}, u32[]{:S(2)}) collective-permute-start(bf16[32,1024]{1,0:T(8,128)(2,1)S(1)} %get-tuple-element.57), channel_id=1, source_target_pairs={{0,8},{4,12},{8,0},{12,4},{1,9},{5,13},{9,1},{13,5},{2,10},{6,14},... | collective-permute-start | bytes 196616 | tf_op jit(solution)/shard_map/ppermute | solution.py:279
  43.3 5.7 %collective-permute-start.21 = (bf16[64,1024]{1,0:T(8,128)(2,1)S(1)}, bf16[64,1024]{1,0:T(8,128)(2,1)S(1)}, u32[]{:S(2)}, u32[]{:S(2)}) collective-permute-start(bf16[64,1024]{1,0:T(8,128)(2,1)S(1)} %get-tuple-element.72), channel_id=1, source_target_pairs={{0,2},{1,3},{2,0},{3,1},{4,6},{5,7},{6,4},{7,5},{8,10},{9,11},{10,... | collective-permute-start | bytes 393224 | tf_op jit(solution)/shard_map/ppermute | solution.py:273
  45.1 6.1 %collective-permute-start.16 = (bf16[128,512]{1,0:T(8,128)(2,1)S(1)}, bf16[128,512]{1,0:T(8,128)(2,1)S(1)}, u32[]{:S(2)}, u32[]{:S(2)}) collective-permute-start(bf16[128,512]{1,0:T(8,128)(2,1)S(1)} %get-tuple-element.66), channel_id=1, source_target_pairs={{0,1},{1,0},{2,3},{3,2},{4,5},{5,4},{6,7},{7,6},{8,9},{9,8},{10,11... | collective-permute-start | bytes 393224 | tf_op jit(solution)/shard_map/ppermute | solution.py:269
  45.1 6.6 %collective-permute-start.17 = (bf16[64,768]{1,0:T(8,128)(2,1)S(1)}, bf16[64,768]{1,0:T(8,128)(2,1)S(1)}, u32[]{:S(2)}, u32[]{:S(2)}) collective-permute-start(bf16[64,768]{1,0:T(8,128)(2,1)S(1)} %shard_map.97.refs_0_.refs_2_), channel_id=1, source_target_pairs={{0,1},{1,0},{2,3},{3,2},{4,5},{5,4},{6,7},{7,6},{8,9},{9,8},{10,11... | collective-permute-start | bytes 294920 | tf_op jit(solution)/shard_map/ppermute | solution.py:269
  47.4 7.8 %collective-permute-start.11 = (bf16[64,1024]{1,0:T(8,128)(2,1)S(1)}, bf16[64,1024]{1,0:T(8,128)(2,1)S(1)}, u32[]{:S(2)}, u32[]{:S(2)}) collective-permute-start(bf16[64,1024]{1,0:T(8,128)(2,1)S(1)} %shard_map.99), channel_id=1, source_target_pairs={{0,2},{1,3},{2,0},{3,1},{4,6},{5,7},{6,4},{7,5},{8,10},{9,11},{10,... | collective-permute-start | bytes 393224 | tf_op jit(solution)/shard_map/ppermute | solution.py:273
  48.0 5.7 %collective-permute-start.18 = (bf16[64,768]{1,0:T(8,128)(2,1)S(1)}, bf16[64,768]{1,0:T(8,128)(2,1)S(1)}, u32[]{:S(2)}, u32[]{:S(2)}) collective-permute-start(bf16[64,768]{1,0:T(8,128)(2,1)S(1)} %collective-permute-done.7.refs_1_.refs_3_.refs_4_), channel_id=1, source_target_pairs={{0,1},{1,0},{2,3},{3,2},{4,5},{5,4},{6,7},{7,6},{8,9},{9,8},{10,11... | collective-permute-start | bytes 294920 | tf_op jit(solution)/shard_map/ppermute | solution.py:269
  49.0 7.5 %collective-permute-start.22 = (bf16[16,2048]{1,0:T(8,128)(2,1)S(1)}, bf16[16,2048]{1,0:T(8,128)(2,1)S(1)}, u32[]{:S(2)}, u32[]{:S(2)}) collective-permute-start(bf16[16,2048]{1,0:T(8,128)(2,1)S(1)} %get-tuple-element.74), channel_id=1, source_target_pairs={{0,4},{4,0},{8,12},{12,8},{1,5},{5,1},{9,13},{13,9},{2,6},{6,2},{1... | collective-permute-start | bytes 196616 | tf_op jit(solution)/shard_map/ppermute | solution.py:279
  51.2 5.6 %collective-permute-start.23 = (bf16[16,2048]{1,0:T(8,128)(2,1)S(1)}, bf16[16,2048]{1,0:T(8,128)(2,1)S(1)}, u32[]{:S(2)}, u32[]{:S(2)}) collective-permute-start(bf16[16,2048]{1,0:T(8,128)(2,1)S(1)} %get-tuple-element.75), channel_id=1, source_target_pairs={{0,8},{4,12},{8,0},{12,4},{1,9},{5,13},{9,1},{13,5},{2,10},{6,14},... | collective-permute-start | bytes 196616 | tf_op jit(solution)/shard_map/ppermute | solution.py:279
  51.8 6.2 %collective-permute-start.24 = (bf16[16,2048]{1,0:T(8,128)(2,1)S(1)}, bf16[16,2048]{1,0:T(8,128)(2,1)S(1)}, u32[]{:S(2)}, u32[]{:S(2)}) collective-permute-start(bf16[16,2048]{1,0:T(8,128)(2,1)S(1)} %get-tuple-element.76), channel_id=1, source_target_pairs={{0,12},{4,8},{8,4},{12,0},{1,13},{5,9},{9,5},{13,1},{2,14},{6,10},... | collective-permute-start | bytes 196616 | tf_op jit(solution)/shard_map/ppermute | solution.py:279

commit v12 on v11

--- a/solution.py
+++ b/solution.py
@@ -7,7 +7,8 @@
 
 EXPERTS = 128
 CORES = 2
-BACK_COST = 12000000000
+PRE_COST = 4500000000
+BACK_COST = 3000000000
 VMEM = 40 * 1024 * 1024
 F32 = jnp.float32
 BF16 = jnp.bfloat16
@@ -54,8 +55,9 @@
     return pl.ds(pl.multiple_of((lax.axis_index("fsdp") ^ k) * part, part), part)
 
 
-def slot_kernel(spread, *refs):
-    sources, rows_out, grads_out, refs = refs[:5], refs[5 : 5 + spread], refs[5 + spread : 5 + 2 * spread], refs[5 + 2 * spread :]
+def slot_kernel(groups, spread, *refs):
+    sources, chunks, refs = refs[:5], refs[5 : 5 + groups], refs[5 + groups :]
+    rows_far, grads_out, refs = refs[: spread - 1], refs[spread - 1 : 2 * spread - 1], refs[2 * spread - 1 :]
     turned_out, gate_out, ids, gates, order, tok, cot, sems = refs
     parts = spread * CORES
     copies = [
@@ -68,7 +70,6 @@
         copy.wait()
     choices, count = ids.shape
     slots = gate_out.shape[0]
-    groups = lax.axis_size("expert")
     capacity = slots // groups
     part = tok.shape[1] // parts
     slot = lax.broadcasted_iota(jnp.int32, (slots, count), 0)
@@ -91,16 +92,28 @@
     slot_gate = jnp.sum(pick * gate, axis=1, keepdims=True)
     gate_out[...] = jnp.broadcast_to(slot_gate, gate_out.shape)
     pick = pick.astype(BF16)
-    for copy, source, scale, outs in (
-        (copies[3], tok, None, rows_out),
-        (copies[4], cot, slot_gate, grads_out),
-    ):
-        copy.wait()
-        for k in reversed(range(parts)):
-            value = product(pick, source[:, columns(k, part)], 1, 0)
-            value = value if scale is None else scale * value
-            to = pl.ds((k % CORES) * part, part)
-            outs[k // CORES][:, to] = value.astype(BF16)
+    copies[3].wait()
+    for k in reversed(range(parts)):
+        value = product(pick, tok[:, columns(k, part)], 1, 0).astype(BF16)
+        to = pl.ds((k % CORES) * part, part)
+        if k >= CORES:
+            rows_far[k // CORES - 1][:, to] = value
+        else:
+            for ke in range(groups):
+                chunks[ke][:, to] = value[ke * capacity : (ke + 1) * capacity]
+    copies[4].wait()
+    for k in reversed(range(parts)):
+        value = slot_gate * product(pick, cot[:, columns(k, part)], 1, 0)
+        grads_out[k // CORES][:, pl.ds((k % CORES) * part, part)] = value.astype(BF16)
+
+
+def split_kernel(groups, capacity, *refs):
+    by_x, by_e = refs[:-groups], refs[-groups:]
+    for ke in range(groups):
+        for i, source in enumerate(by_x):
+            by_e[ke][i * capacity : (i + 1) * capacity] = source[
+                ke * capacity : (ke + 1) * capacity
+            ]
 
 
 def join_kernel(groups, spread, capacity, *refs):
@@ -122,27 +135,37 @@
             ]
 
 
-def partial(groups, spread, refs, outs):
-    chunks, (own, sib) = refs[:groups], refs[groups:]
+def partial(rows, own, sib, outs):
     part = own.shape[0]
-    half = CORES * part
+    total = product(rows[:, :part], own[...], 1, 0) + product(rows[:, part:], sib[...], 1, 0)
+    slots = rows.shape[0] // len(outs)
+    for kx, out in enumerate(outs):
+        out[...] = total[kx * slots : (kx + 1) * slots].astype(out.dtype)
+
+
+def own_and_far(groups, spread, capacity, refs):
+    own, far = refs[:groups], refs[groups:]
+    yield jnp.concatenate([c[...] for c in own], axis=0)
+    for i in range(spread - 1):
+        at = slice(i * capacity, (i + 1) * capacity)
+        yield jnp.concatenate([c[at] for c in far], axis=0)
+
+
+def pre_kernel(groups, spread, capacity, *refs):
+    rows = jnp.concatenate(
+        list(own_and_far(groups, spread, capacity, refs[: 2 * groups])), axis=0
+    )
+    own, sib, *outs = refs[2 * groups :]
+    partial(rows, own, sib, outs)
+
+
+def back_kernel(groups, spread, *refs):
+    chunks, (out_own, out_sib, own, sib, *outs) = refs[:groups], refs[groups:]
+    half = CORES * out_own.shape[0]
     rows = jnp.concatenate(
         [c[:, kx * half : (kx + 1) * half] for kx in range(spread) for c in chunks], axis=0
     )
-    total = product(rows[:, :part], own[...], 1, 0) + product(rows[:, part:], sib[...], 1, 0)
-    slots = rows.shape[0] // spread
-    for kx in range(spread):
-        outs[kx][...] = total[kx * slots : (kx + 1) * slots].astype(outs[kx].dtype)
-    return rows
-
-
-def pre_kernel(groups, spread, *refs):
-    partial(groups, spread, refs[: groups + 2], refs[groups + 2 :])
-
-
-def back_kernel(groups, spread, *refs):
-    own, sib, *outs = refs[groups + 2 :]
-    rows = partial(groups, spread, refs[: groups + 2], outs)
+    partial(rows, out_own, out_sib, outs)
     part = own.shape[1]
     own[...] = rows[:, :part]
     sib[...] = rows[:, part:]
@@ -193,16 +216,20 @@
     width_product(refs[:spread], refs[spread : spread + CORES], store)
 
 
-def d_rows_kernel(spread, *refs):
-    outs = refs[-spread:]
-    part = refs[spread].shape[0]
-    slots = outs[0].shape[0]
+def d_rows_kernel(groups, spread, capacity, *refs):
+    left, weights, outs = refs[:spread], refs[spread : spread + CORES], refs[spread + CORES :]
+    chunks, far = outs[:groups], outs[groups:]
+    part = weights[0].shape[0]
+    slots = groups * capacity
 
     def store(kc, value):
-        for kx in range(spread):
-            outs[kx][:, kc * part : (kc + 1) * part] = value[kx * slots : (kx + 1) * slots]
-
-    width_product(refs[:spread], refs[spread : spread + CORES], store)
+        to = pl.ds(kc * part, part)
+        for kx in range(1, spread):
+            far[kx - 1][:, to] = value[kx * slots : (kx + 1) * slots]
+        for ke in range(groups):
+            chunks[ke][:, to] = value[ke * capacity : (ke + 1) * capacity]
+
+    width_product(left, weights, store)
 
 
 def weight_kernel(spread, own, sib, *refs):
@@ -241,13 +268,11 @@
     scatter(twice, map(weighted, range(parts)), out, held, sems)
 
 
-def d_tokens_kernel(groups, parts, turned, *refs):
-    chunks, (out, held, sems) = refs[:groups], refs[groups:]
+def d_tokens_kernel(groups, spread, capacity, turned, *refs):
+    chunks, (out, held, sems) = refs[: 2 * groups], refs[2 * groups :]
     part = held.shape[2]
-    rows = (
-        jnp.concatenate([c[:, k * part : (k + 1) * part] for c in chunks], axis=0)
-        for k in range(parts)
-    )
+    rows = own_and_far(groups, spread, capacity, chunks)
+    rows = (r[:, kc * part : (kc + 1) * part] for r in rows for kc in range(CORES))
     scatter(turned[...], rows, out, held, sems)
 
 
@@ -282,11 +307,13 @@
 
     chunk = [shape((capacity, width))] * groups
     by_x = [shape((slots, half))] * spread
+    own_chunk = [shape((capacity, half))] * groups
+    far_chunk = [shape(((spread - 1) * capacity, half))] * groups
     in_own, out_own = w_in[0], w_out[0]
     in_sib, out_sib = to_core(in_own), to_core(out_own)
     outs = call(
-        bound(slot_kernel, spread),
-        by_x * 2 + [shape((count, slots)), shape((slots, 128), F32)],
+        bound(slot_kernel, groups, spread),
+        own_chunk + by_x[1:] + by_x + [shape((count, slots)), shape((slots, 128), F32)],
         (route_ids.T, route_gates.T, served_order, tokens, cotangent),
         far=5,
         scratch_shapes=[
@@ -299,16 +326,24 @@
         ],
     )
     turned, gate = outs[-2:]
-    rows = [outs[0], *to_x(outs[1:spread])]
-    grads = [outs[spread], *to_x(outs[spread + 1 : 2 * spread])]
-    rows, in_sib, out_sib = lax.optimization_barrier((rows, in_sib, out_sib))
+    own, (*far, near), grads_far = (
+        outs[:groups],
+        outs[groups : groups + spread],
+        outs[groups + spread : -2],
+    )
+    far = to_x(far)
+    grads = [near, *to_x(grads_far)]
+    *own, in_sib, out_sib = lax.optimization_barrier((*own, in_sib, out_sib))
+    split = bound(split_kernel, groups, capacity)
+    own = to_expert(own)
+    far = to_expert(call(split, far_chunk, far, after=own[1:]))
     join = bound(join_kernel, groups, spread, capacity)
-    rows = to_expert(call(join, chunk, rows))
     grads = to_expert(call(join, chunk, grads))
     pre, *pre_far = call(
-        bound(pre_kernel, groups, spread),
+        bound(pre_kernel, groups, spread, capacity),
         [shape((slots, 2 * feed), F32)] + [shape((slots, 2 * feed))] * (spread - 1),
-        (*rows, in_own, in_sib),
+        (*own, *far, in_own, in_sib),
+        cost=PRE_COST,
     )
     pre = (pre, *to_x(pre_far))
     (hidden,) = call(hidden_kernel, [shape((slots, feed))], pre)
@@ -333,10 +368,14 @@
         d_pre_kernel, [shape((slots, 2 * feed))], (*pre, *back), after=hidden[1:]
     )
     d_pre = (d_pre, *to_x([d_pre] * (spread - 1)))
-    near, *far = call(
-        bound(d_rows_kernel, spread), by_x, (*d_pre, in_own, in_sib), after=expert_out[1:2]
-    )
-    d_rows = to_expert(call(join, chunk, (near, *to_x(far))))
+    outs = call(
+        bound(d_rows_kernel, groups, spread, capacity),
+        own_chunk + by_x[1:],
+        (*d_pre, in_own, in_sib),
+        after=expert_out[1:2],
+    )
+    own, d_far = to_expert(outs[:groups]), to_x(outs[groups:])
+    d_rows = (*own, *to_expert(call(split, far_chunk, d_far, after=own[1:])))
     far = to_x(
         call(bound(far_kernel, groups, spread, capacity), by_x[1:], expert_out)
     )
@@ -368,7 +407,7 @@
         token=True,
     )
     (d_tokens,) = scattered(
-        bound(d_tokens_kernel, groups, parts), (turned, *d_rows), after=(token,)
+        bound(d_tokens_kernel, groups, spread, capacity), (turned, *d_rows), after=(token,)
     )
     return combined, d_tokens, d_w_out[None]
 

time: 59.3 us -> 66.7 us (1.12)
  starting transfers between devices: 30.7 us -> 39 us
  waiting for transfers between devices: 18.7 us -> 17.7 us
    ppermute x12 -> x18, starting transfers between devices: 17.9 us -> 27 us  [to_expert(): lax.ppermute(value, 'expert', [(i, i ^ ke) for i in range(groups)])]
    ppermute x8, waiting for transfers between devices: 10.8 us -> 6.98 us  [to_x(): lax.ppermute(value, 'fsdp', [(i, i ^ (k + 1) * CORES) for i in range(part...]
    ppermute x12 -> x18, waiting for transfers between devices: 7.87 us -> 10.7 us  [to_expert(): lax.ppermute(value, 'expert', [(i, i ^ ke) for i in range(groups)])]
  transfers between devices with their start and end apart: 25 -> 31, of which waited for: 12 -> 8; matrix products, arithmetic and copies ran while one was open for 0% -> 0% of each run, Pallas kernels for 13% -> 12%
where the time goes in v12:
time: 66.7 us; the launch traced here: 66.5 us
  starting transfers between devices  39 us (58%)
  waiting for transfers between devices  17.7 us (27%)
  Pallas kernels  8.98 us (13%)
  between operations  0.82 us (1%)
    ppermute x18, starting transfers between devices, to_expert(): lax.ppermute(value, 'expert', [(i, i ^ ke) for i in range(groups)])  27 us
    ppermute x8, starting transfers between devices, to_x(): lax.ppermute(value, 'fsdp', [(i, i ^ (k + 1) * CORES) for i in range(part...  11.4 us
    ppermute x18, waiting for transfers between devices, to_expert(): lax.ppermute(value, 'expert', [(i, i ^ ke) for i in range(groups)])  10.7 us
    pallas_call x14, Pallas kernels, call(): pl.pallas_call(kernel, out_shape=out_shape, in_specs=specs, compiler_para...  8.98 us
    ppermute x8, waiting for transfers between devices, to_x(): lax.ppermute(value, 'fsdp', [(i, i ^ (k + 1) * CORES) for i in range(part...  6.98 us
  transfers between devices with their start and end apart: 31, of which 8 were waited for; matrix products, arithmetic and copies ran while one was open for 0% of the time, Pallas kernels for 12%

profile of v12, /device:TPU:0, one launch (start us, length us, event | category | flops | bytes accessed | tf_op | source)
XLA Modules:
  0.0 66.5 jit_solution(7145820425337140432)
XLA Ops:
  0.6 0.5 collective-permute-start
  1.2 0.1 collective-permute-start.1
  1.2 1.9 %shard_map.94 = (bf16[16,1024]{1,0:T(8,128)(2,1)S(1)}, bf16[16,1024]{1,0:T(8,128)(2,1)S(1)}, bf16[16,1024]{1,0:T(8,128)(2,1)S(1)}, bf16[16,1024]{1,0:T(8,128)(2,...) custom-call(s32[8,256]{1,0:T(8,128)} %bitcast.11, ...), custom_call_target="tpu_custom_call" | custom-call | tf_op jit(solution)/shard_map/pallas_call | solution.py:40
  3.2 3.0 %collective-permute-start.5 = (bf16[64,1024]{1,0:T(8,128)(2,1)S(1)}, bf16[64,1024]{1,0:T(8,128)(2,1)S(1)}, u32[]{:S(2)}, u32[]{:S(2)}) collective-permute-start(bf16[64,1024]{1,0:T(8,128)(2,1)S(1)} %get-tuple-element.59), channel_id=1, source_target_pairs={{0,2},{1,3},{2,0},{3,1},{4,6},{5,7},{6,4},{7,5},{8,10},{9,11},{10,... | collective-permute-start | bytes 393224 | tf_op jit(solution)/shard_map/ppermute | solution.py:298
  6.2 0.1 collective-permute-start.15
  6.2 0.0 collective-permute-done.1.refs_3_.refs_5_
  6.2 0.0 collective-permute-done.refs_9_.refs_3_
  6.2 2.2 %collective-permute-start.2 = (bf16[16,1024]{1,0:T(8,128)(2,1)S(1)}, bf16[16,1024]{1,0:T(8,128)(2,1)S(1)}, u32[]{:S(2)}, u32[]{:S(2)}) collective-permute-start(bf16[16,1024]{1,0:T(8,128)(2,1)S(1)} %get-tuple-element.56), channel_id=1, source_target_pairs={{0,4},{4,0},{8,12},{12,8},{1,5},{5,1},{9,13},{13,9},{2,6},{6,2},{1... | collective-permute-start | bytes 98312 | tf_op jit(solution)/shard_map/ppermute | solution.py:304
  8.5 2.6 %collective-permute-start.3 = (bf16[16,1024]{1,0:T(8,128)(2,1)S(1)}, bf16[16,1024]{1,0:T(8,128)(2,1)S(1)}, u32[]{:S(2)}, u32[]{:S(2)}) collective-permute-start(bf16[16,1024]{1,0:T(8,128)(2,1)S(1)} %get-tuple-element.57), channel_id=1, source_target_pairs={{0,8},{4,12},{8,0},{12,4},{1,9},{5,13},{9,1},{13,5},{2,10},{6,14},... | collective-permute-start | bytes 98312 | tf_op jit(solution)/shard_map/ppermute | solution.py:304
  11.1 0.0 collective-permute-done.5.refs_0_
  11.1 2.8 %collective-permute-done.3.refs_2_ = bf16[16,1024]{1,0:T(8,128)(2,1)S(1)} collective-permute-done((bf16[16,1024]{1,0:T(8,128)(2,1)S(1)}, bf16[16,1024]{1,0:T(8,128)(2,1)S(1)}, u32[]{:S(2)}, u32[]{:S(2)}) %collective-permute-start.3) | collective-permute-done | bytes 32800 | tf_op jit(solution)/shard_map/ppermute | solution.py:304
  13.9 2.9 %collective-permute-done.4.refs_3_ = bf16[16,1024]{1,0:T(8,128)(2,1)S(1)} collective-permute-done((bf16[16,1024]{1,0:T(8,128)(2,1)S(1)}, bf16[16,1024]{1,0:T(8,128)(2,1)S(1)}, u32[]{:S(2)}, u32[]{:S(2)}) %collective-permute-start.4) | collective-permute-done | bytes 32800 | tf_op jit(solution)/shard_map/ppermute | solution.py:304
  16.8 0.1 collective-permute-start.6
  16.9 1.0 %collective-permute-start.7 = (bf16[16,1024]{1,0:T(8,128)(2,1)S(1)}, bf16[16,1024]{1,0:T(8,128)(2,1)S(1)}, u32[]{:S(2)}, u32[]{:S(2)}) collective-permute-start(bf16[16,1024]{1,0:T(8,128)(2,1)S(1)} %get-tuple-element.62), channel_id=1, source_target_pairs={{0,8},{4,12},{8,0},{12,4},{1,9},{5,13},{9,1},{13,5},{2,10},{6,14},... | collective-permute-start | bytes 98312 | tf_op jit(solution)/shard_map/ppermute | solution.py:304
  17.8 3.4 %collective-permute-start.8 = (bf16[16,1024]{1,0:T(8,128)(2,1)S(1)}, bf16[16,1024]{1,0:T(8,128)(2,1)S(1)}, u32[]{:S(2)}, u32[]{:S(2)}) collective-permute-start(bf16[16,1024]{1,0:T(8,128)(2,1)S(1)} %get-tuple-element.63), channel_id=1, source_target_pairs={{0,12},{4,8},{8,4},{12,0},{1,13},{5,9},{9,5},{13,1},{2,14},{6,10},... | collective-permute-start | bytes 98312 | tf_op jit(solution)/shard_map/ppermute | solution.py:304
  21.3 0.1 collective-permute-start.16
  21.4 1.0 %collective-permute-start.17 = (bf16[16,2048]{1,0:T(8,128)(2,1)S(1)}, bf16[16,2048]{1,0:T(8,128)(2,1)S(1)}, u32[]{:S(2)}, u32[]{:S(2)}) collective-permute-start(bf16[16,2048]{1,0:T(8,128)(2,1)S(1)} %get-tuple-element.76), channel_id=1, source_target_pairs={{0,8},{4,12},{8,0},{12,4},{1,9},{5,13},{9,1},{13,5},{2,10},{6,14},... | collective-permute-start | bytes 196616 | tf_op jit(solution)/shard_map/ppermute | solution.py:304
  22.3 3.4 %collective-permute-start.18 = (bf16[16,2048]{1,0:T(8,128)(2,1)S(1)}, bf16[16,2048]{1,0:T(8,128)(2,1)S(1)}, u32[]{:S(2)}, u32[]{:S(2)}) collective-permute-start(bf16[16,2048]{1,0:T(8,128)(2,1)S(1)} %get-tuple-element.77), channel_id=1, source_target_pairs={{0,12},{4,8},{8,4},{12,0},{1,13},{5,9},{9,5},{13,1},{2,14},{6,10},... | collective-permute-start | bytes 196616 | tf_op jit(solution)/shard_map/ppermute | solution.py:304
  25.7 0.0 copy-start.1
  25.8 0.6 shard_map.96
  26.3 1.6 %collective-permute-start.9 = (bf16[64,1536]{1,0:T(8,128)(2,1)S(1)}, bf16[64,1536]{1,0:T(8,128)(2,1)S(1)}, u32[]{:S(2)}, u32[]{:S(2)}) collective-permute-start(bf16[64,1536]{1,0:T(8,128)(2,1)S(1)} %get-tuple-element.66), channel_id=1, source_target_pairs={{0,2},{1,3},{2,0},{3,1},{4,6},{5,7},{6,4},{7,5},{8,10},{9,11},{10,... | collective-permute-start | bytes 589832 | tf_op jit(solution)/shard_map/ppermute | solution.py:298
  27.9 0.9 %collective-permute-done.18.refs_3_ = bf16[16,2048]{1,0:T(8,128)(2,1)S(1)} collective-permute-done((bf16[16,2048]{1,0:T(8,128)(2,1)S(1)}, bf16[16,2048]{1,0:T(8,128)(2,1)S(1)}, u32[]{:S(2)}, u32[]{:S(2)}) %collective-permute-start.18) | collective-permute-done | bytes 65568 | tf_op jit(solution)/shard_map/ppermute | solution.py:304
  28.8 0.4 shard_map.101
  29.2 1.6 %collective-permute-start.22 = (bf16[64,768]{1,0:T(8,128)(2,1)S(1)}, bf16[64,768]{1,0:T(8,128)(2,1)S(1)}, u32[]{:S(2)}, u32[]{:S(2)}) collective-permute-start(bf16[64,768]{1,0:T(8,128)(2,1)S(1)} %get-tuple-element.83), channel_id=1, source_target_pairs={{0,2},{1,3},{2,0},{3,1},{4,6},{5,7},{6,4},{7,5},{8,10},{9,11},{10,... | collective-permute-start | bytes 294920 | tf_op jit(solution)/shard_map/ppermute | solution.py:298
  30.7 2.4 %collective-permute-done.9.refs_1_ = bf16[64,1536]{1,0:T(8,128)(2,1)S(1)} collective-permute-done((bf16[64,1536]{1,0:T(8,128)(2,1)S(1)}, bf16[64,1536]{1,0:T(8,128)(2,1)S(1)}, u32[]{:S(2)}, u32[]{:S(2)}) %collective-permute-start.9) | collective-permute-done | bytes 196640 | tf_op jit(solution)/shard_map/ppermute | solution.py:298
  33.1 0.1 shard_map.97.refs_0_.refs_2_
  33.2 1.6 %collective-permute-start.10 = (bf16[64,768]{1,0:T(8,128)(2,1)S(1)}, bf16[64,768]{1,0:T(8,128)(2,1)S(1)}, u32[]{:S(2)}, u32[]{:S(2)}) collective-permute-start(bf16[64,768]{1,0:T(8,128)(2,1)S(1)} %shard_map.97.refs_0_.refs_2_), channel_id=1, source_target_pairs={{0,2},{1,3},{2,0},{3,1},{4,6},{5,7},{6,4},{7,5},{8,10},{9,11},{10,... | collective-permute-start | bytes 294920 | tf_op jit(solution)/shard_map/ppermute | solution.py:298
  34.8 4.1 %collective-permute-done.10.refs_1_.refs_3_.refs_4_ = bf16[64,768]{1,0:T(8,128)(2,1)S(1)} collective-permute-done((bf16[64,768]{1,0:T(8,128)(2,1)S(1)}, bf16[64,768]{1,0:T(8,128)(2,1)S(1)}, u32[]{:S(2)}, u32[]{:S(2)}) %collective-permute-start.10) | collective-permute-done | bytes 98336 | tf_op jit(solution)/shard_map/ppermute | solution.py:298
  38.9 0.1 shard_map.104.refs_0_
  39.0 1.6 %collective-permute-start.23 = (bf16[64,1536]{1,0:T(8,128)(2,1)S(1)}, bf16[64,1536]{1,0:T(8,128)(2,1)S(1)}, u32[]{:S(2)}, u32[]{:S(2)}) collective-permute-start(bf16[64,1536]{1,0:T(8,128)(2,1)S(1)} %shard_map.104.refs_0_), channel_id=1, source_target_pairs={{0,2},{1,3},{2,0},{3,1},{4,6},{5,7},{6,4},{7,5},{8,10},{9,11},{10,... | collective-permute-start | bytes 589832 | tf_op jit(solution)/shard_map/ppermute | solution.py:298
  40.5 0.6 shard_map.98
  41.2 0.1 collective-permute-start.11
  41.3 2.6 %collective-permute-start.12 = (bf16[32,1024]{1,0:T(8,128)(2,1)S(1)}, bf16[32,1024]{1,0:T(8,128)(2,1)S(1)}, u32[]{:S(2)}, u32[]{:S(2)}) collective-permute-start(bf16[32,1024]{1,0:T(8,128)(2,1)S(1)} %get-tuple-element.70), channel_id=1, source_target_pairs={{0,8},{4,12},{8,0},{12,4},{1,9},{5,13},{9,1},{13,5},{2,10},{6,14},... | collective-permute-start | bytes 196616 | tf_op jit(solution)/shard_map/ppermute | solution.py:304
  43.9 1.8 %collective-permute-start.13 = (bf16[32,1024]{1,0:T(8,128)(2,1)S(1)}, bf16[32,1024]{1,0:T(8,128)(2,1)S(1)}, u32[]{:S(2)}, u32[]{:S(2)}) collective-permute-start(bf16[32,1024]{1,0:T(8,128)(2,1)S(1)} %get-tuple-element.71), channel_id=1, source_target_pairs={{0,12},{4,8},{8,4},{12,0},{1,13},{5,9},{9,5},{13,1},{2,14},{6,10},... | collective-permute-start | bytes 196616 | tf_op jit(solution)/shard_map/ppermute | solution.py:304
  45.6 0.5 collective-permute-done.23.refs_1_
  46.1 1.1 %shard_map.105 = (bf16[16,1024]{1,0:T(8,128)(2,1)S(1)}, bf16[16,1024]{1,0:T(8,128)(2,1)S(1)}, bf16[16,1024]{1,0:T(8,128)(2,1)S(1)}, bf16[16,1024]{1,0:T(8,128)(2,1)S(1)}, bf16[64,1024]{1,0:T(8,128)(2,1)S(1)}) custom-call(bf16[64,1536]{1,0:T(8,128)(2,1)S(1)} %shard_map.104.refs_0_, bf16[64,1536]{1,0:T(8,128)(2,1)S(1)} %collective-permute-done.23.refs_1_, ...), custom_call_target="tpu_custom_call" | custom-call | tf_op jit(solution)/shard_map/pallas_call | solution.py:40
  47.3 1.5 %collective-permute-start.27 = (bf16[64,1024]{1,0:T(8,128)(2,1)S(1)}, bf16[64,1024]{1,0:T(8,128)(2,1)S(1)}, u32[]{:S(2)}, u32[]{:S(2)}) collective-permute-start(bf16[64,1024]{1,0:T(8,128)(2,1)S(1)} %get-tuple-element.88), channel_id=1, source_target_pairs={{0,2},{1,3},{2,0},{3,1},{4,6},{5,7},{6,4},{7,5},{8,10},{9,11},{10,... | collective-permute-start | bytes 393224 | tf_op jit(solution)/shard_map/ppermute | solution.py:298
  48.8 2.6 %collective-permute-start.25 = (bf16[16,1024]{1,0:T(8,128)(2,1)S(1)}, bf16[16,1024]{1,0:T(8,128)(2,1)S(1)}, u32[]{:S(2)}, u32[]{:S(2)}) collective-permute-start(bf16[16,1024]{1,0:T(8,128)(2,1)S(1)} %get-tuple-element.86), channel_id=1, source_target_pairs={{0,8},{4,12},{8,0},{12,4},{1,9},{5,13},{9,1},{13,5},{2,10},{6,14},... | collective-permute-start | bytes 98312 | tf_op jit(solution)/shard_map/ppermute | solution.py:304
  51.5 1.8 %collective-permute-start.26 = (bf16[16,1024]{1,0:T(8,128)(2,1)S(1)}, bf16[16,1024]{1,0:T(8,128)(2,1)S(1)}, u32[]{:S(2)}, u32[]{:S(2)}) collective-permute-start(bf16[16,1024]{1,0:T(8,128)(2,1)S(1)} %get-tuple-element.87), channel_id=1, source_target_pairs={{0,12},{4,8},{8,4},{12,0},{1,13},{5,9},{9,5},{13,1},{2,14},{6,10},... | collective-permute-start | bytes 98312 | tf_op jit(solution)/shard_map/ppermute | solution.py:304
  53.2 0.6 collective-permute-start.14
  53.9 3.3 %collective-permute-done.26.refs_3_.refs_4_ = bf16[16,1024]{1,0:T(8,128)(2,1)S(1)} collective-permute-done((bf16[16,1024]{1,0:T(8,128)(2,1)S(1)}, bf16[16,1024]{1,0:T(8,128)(2,1)S(1)}, u32[]{:S(2)}, u32[]{:S(2)}) %collective-permute-start.26) | collective-permute-done | bytes 32800 | tf_op jit(solution)/shard_map/ppermute | solution.py:304
  57.2 0.1 collective-permute-start.28
  57.3 2.3 %collective-permute-start.29 = (bf16[16,1024]{1,0:T(8,128)(2,1)S(1)}, bf16[16,1024]{1,0:T(8,128)(2,1)S(1)}, u32[]{:S(2)}, u32[]{:S(2)}) collective-permute-start(bf16[16,1024]{1,0:T(8,128)(2,1)S(1)} %get-tuple-element.91), channel_id=1, source_target_pairs={{0,8},{4,12},{8,0},{12,4},{1,9},{5,13},{9,1},{13,5},{2,10},{6,14},... | collective-permute-start | bytes 98312 | tf_op jit(solution)/shard_map/ppermute | solution.py:304
  59.6 2.1 %collective-permute-start.30 = (bf16[16,1024]{1,0:T(8,128)(2,1)S(1)}, bf16[16,1024]{1,0:T(8,128)(2,1)S(1)}, u32[]{:S(2)}, u32[]{:S(2)}) collective-permute-start(bf16[16,1024]{1,0:T(8,128)(2,1)S(1)} %get-tuple-element.92), channel_id=1, source_target_pairs={{0,12},{4,8},{8,4},{12,0},{1,13},{5,9},{9,5},{13,1},{2,14},{6,10},... | collective-permute-start | bytes 98312 | tf_op jit(solution)/shard_map/ppermute | solution.py:304
  61.7 1.6 %shard_map.102 = (f32[512,768]{1,0:T(8,128)}, f32[8,128]{1,0:T(8,128)S(1)}) custom-call(bf16[128,512]{1,0:T(8,128)(2,1)S(1)} %get-tuple-element.78.refs_0_, bf16[128,512]{1,0:T(8,128)(2,1)S(1)} %collective-permute-done.19.refs_1_, bf16[64,768]{1,0:T(8,128)(2,1)S(1)} %shard_map.97.refs_0_.refs_2_, ...), custom_call_target="tpu_custom_call" | custom-call | tf_op jit(solution)/shard_map/pallas_call | solution.py:40
  63.2 1.3 %shard_map.103 = (bf16[256,2048]{1,0:T(8,128)(2,1)}, f32[8,128]{1,0:T(8,128)S(1)}) custom-call(bf16[256,64]{1,0:T(8,128)(2,1)S(1)} %get-tuple-element.49.refs_0_, f32[64,128]{1,0:T(8,128)S(1)} %get-tuple-element.50.refs_1_, bf16[32,1024]{1,0:T(8,128)(2,1)S(1)} %get-tuple-element.68.refs_0_.refs_2_, ...), custom_call_target="tpu_custom_call" | custom-call | tf_op jit(solution)/shard_map/pallas_call | solution.py:40
  64.5 0.8 %collective-permute-done.30.refs_8_ = bf16[16,1024]{1,0:T(8,128)(2,1)S(1)} collective-permute-done((bf16[16,1024]{1,0:T(8,128)(2,1)S(1)}, bf16[16,1024]{1,0:T(8,128)(2,1)S(1)}, u32[]{:S(2)}, u32[]{:S(2)}) %collective-permute-start.30) | collective-permute-done | bytes 32800 | tf_op jit(solution)/shard_map/ppermute | solution.py:304
  65.3 1.2 %shard_map.107 = bf16[256,2048]{1,0:T(8,128)(2,1)} custom-call(bf16[256,64]{1,0:T(8,128)(2,1)S(1)} %get-tuple-element.49.refs_0_, bf16[16,1024]{1,0:T(8,128)(2,1)S(1)} %get-tuple-element.84.refs_1_, bf16[16,1024]{1,0:T(8,128)(2,1)S(1)} %collective-permute-done.24.refs_1_.refs_2_, bf16[16,1024]{1,0:T(8,128)(2,1)S(1)} %collective-permute-done.25.refs_2_.refs_3_, ...), custom_call_target="tpu_custom_call" | custom-call | tf_op jit(solution)/shard_map/pallas_call | solution.py:40
  (32 shorter events, 0.1 us)
Async XLA Ops:
  0.6 25.1 %copy-start = (bf16[1,512,1536]{2,1,0:T(8,128)(2,1)S(1)}, bf16[1,512,1536]{2,1,0:T(8,128)(2,1)}, u32[]{:S(2)}) copy-start(bf16[1,512,1536]{2,1,0:T(8,128)(2,1)} %param.12) | copy-start | bytes 4718596
  0.6 5.6 %collective-permute-start = (bf16[512,1536]{1,0:T(8,128)(2,1)}, bf16[512,1536]{1,0:T(8,128)(2,1)S(1)}, u32[]{:S(2)}, u32[]{:S(2)}) collective-permute-start(bf16[512,1536]{1,0:T(8,128)(2,1)} %bitcast.5), channel_id=1, source_target_pairs={{0,1},{1,0},{2,3},{3,2},{4,5},{5,4},{6,7},{7,6},{8,9},{9,8},{10,11... | collective-permute-start | bytes 4718600 | tf_op jit(solution)/shard_map/ppermute | solution.py:294
  1.2 5.1 %collective-permute-start.1 = (bf16[512,768]{1,0:T(8,128)(2,1)}, bf16[512,768]{1,0:T(8,128)(2,1)S(1)}, u32[]{:S(2)}, u32[]{:S(2)}) collective-permute-start(bf16[512,768]{1,0:T(8,128)(2,1)} %bitcast.8), channel_id=1, source_target_pairs={{0,1},{1,0},{2,3},{3,2},{4,5},{5,4},{6,7},{7,6},{8,9},{9,8},{10,11... | collective-permute-start | bytes 2359304 | tf_op jit(solution)/shard_map/ppermute | solution.py:294
  3.2 7.9 %collective-permute-start.5 = (bf16[64,1024]{1,0:T(8,128)(2,1)S(1)}, bf16[64,1024]{1,0:T(8,128)(2,1)S(1)}, u32[]{:S(2)}, u32[]{:S(2)}) collective-permute-start(bf16[64,1024]{1,0:T(8,128)(2,1)S(1)} %get-tuple-element.59), channel_id=1, source_target_pairs={{0,2},{1,3},{2,0},{3,1},{4,6},{5,7},{6,4},{7,5},{8,10},{9,11},{10,... | collective-permute-start | bytes 393224 | tf_op jit(solution)/shard_map/ppermute | solution.py:298
  6.2 15.1 %collective-permute-start.15 = (bf16[64,1024]{1,0:T(8,128)(2,1)S(1)}, bf16[64,1024]{1,0:T(8,128)(2,1)S(1)}, u32[]{:S(2)}, u32[]{:S(2)}) collective-permute-start(bf16[64,1024]{1,0:T(8,128)(2,1)S(1)} %get-tuple-element.73), channel_id=1, source_target_pairs={{0,2},{1,3},{2,0},{3,1},{4,6},{5,7},{6,4},{7,5},{8,10},{9,11},{10,... | collective-permute-start | bytes 393224 | tf_op jit(solution)/shard_map/ppermute | solution.py:298
  6.2 4.8 %collective-permute-start.2 = (bf16[16,1024]{1,0:T(8,128)(2,1)S(1)}, bf16[16,1024]{1,0:T(8,128)(2,1)S(1)}, u32[]{:S(2)}, u32[]{:S(2)}) collective-permute-start(bf16[16,1024]{1,0:T(8,128)(2,1)S(1)} %get-tuple-element.56), channel_id=1, source_target_pairs={{0,4},{4,0},{8,12},{12,8},{1,5},{5,1},{9,13},{13,9},{2,6},{6,2},{1... | collective-permute-start | bytes 98312 | tf_op jit(solution)/shard_map/ppermute | solution.py:304
  8.5 5.4 %collective-permute-start.3 = (bf16[16,1024]{1,0:T(8,128)(2,1)S(1)}, bf16[16,1024]{1,0:T(8,128)(2,1)S(1)}, u32[]{:S(2)}, u32[]{:S(2)}) collective-permute-start(bf16[16,1024]{1,0:T(8,128)(2,1)S(1)} %get-tuple-element.57), channel_id=1, source_target_pairs={{0,8},{4,12},{8,0},{12,4},{1,9},{5,13},{9,1},{13,5},{2,10},{6,14},... | collective-permute-start | bytes 98312 | tf_op jit(solution)/shard_map/ppermute | solution.py:304
  11.1 5.7 %collective-permute-start.4 = (bf16[16,1024]{1,0:T(8,128)(2,1)S(1)}, bf16[16,1024]{1,0:T(8,128)(2,1)S(1)}, u32[]{:S(2)}, u32[]{:S(2)}) collective-permute-start(bf16[16,1024]{1,0:T(8,128)(2,1)S(1)} %get-tuple-element.58), channel_id=1, source_target_pairs={{0,12},{4,8},{8,4},{12,0},{1,13},{5,9},{9,5},{13,1},{2,14},{6,10},... | collective-permute-start | bytes 98312 | tf_op jit(solution)/shard_map/ppermute | solution.py:304
  16.8 5.5 %collective-permute-start.6 = (bf16[16,1024]{1,0:T(8,128)(2,1)S(1)}, bf16[16,1024]{1,0:T(8,128)(2,1)S(1)}, u32[]{:S(2)}, u32[]{:S(2)}) collective-permute-start(bf16[16,1024]{1,0:T(8,128)(2,1)S(1)} %get-tuple-element.61), channel_id=1, source_target_pairs={{0,4},{4,0},{8,12},{12,8},{1,5},{5,1},{9,13},{13,9},{2,6},{6,2},{1... | collective-permute-start | bytes 98312 | tf_op jit(solution)/shard_map/ppermute | solution.py:304
  16.9 8.9 %collective-permute-start.7 = (bf16[16,1024]{1,0:T(8,128)(2,1)S(1)}, bf16[16,1024]{1,0:T(8,128)(2,1)S(1)}, u32[]{:S(2)}, u32[]{:S(2)}) collective-permute-start(bf16[16,1024]{1,0:T(8,128)(2,1)S(1)} %get-tuple-element.62), channel_id=1, source_target_pairs={{0,8},{4,12},{8,0},{12,4},{1,9},{5,13},{9,1},{13,5},{2,10},{6,14},... | collective-permute-start | bytes 98312 | tf_op jit(solution)/shard_map/ppermute | solution.py:304
  17.8 7.9 %collective-permute-start.8 = (bf16[16,1024]{1,0:T(8,128)(2,1)S(1)}, bf16[16,1024]{1,0:T(8,128)(2,1)S(1)}, u32[]{:S(2)}, u32[]{:S(2)}) collective-permute-start(bf16[16,1024]{1,0:T(8,128)(2,1)S(1)} %get-tuple-element.63), channel_id=1, source_target_pairs={{0,12},{4,8},{8,4},{12,0},{1,13},{5,9},{9,5},{13,1},{2,14},{6,10},... | collective-permute-start | bytes 98312 | tf_op jit(solution)/shard_map/ppermute | solution.py:304
  21.3 6.6 %collective-permute-start.16 = (bf16[16,2048]{1,0:T(8,128)(2,1)S(1)}, bf16[16,2048]{1,0:T(8,128)(2,1)S(1)}, u32[]{:S(2)}, u32[]{:S(2)}) collective-permute-start(bf16[16,2048]{1,0:T(8,128)(2,1)S(1)} %get-tuple-element.75), channel_id=1, source_target_pairs={{0,4},{4,0},{8,12},{12,8},{1,5},{5,1},{9,13},{13,9},{2,6},{6,2},{1... | collective-permute-start | bytes 196616 | tf_op jit(solution)/shard_map/ppermute | solution.py:304
  21.4 6.6 %collective-permute-start.17 = (bf16[16,2048]{1,0:T(8,128)(2,1)S(1)}, bf16[16,2048]{1,0:T(8,128)(2,1)S(1)}, u32[]{:S(2)}, u32[]{:S(2)}) collective-permute-start(bf16[16,2048]{1,0:T(8,128)(2,1)S(1)} %get-tuple-element.76), channel_id=1, source_target_pairs={{0,8},{4,12},{8,0},{12,4},{1,9},{5,13},{9,1},{13,5},{2,10},{6,14},... | collective-permute-start | bytes 196616 | tf_op jit(solution)/shard_map/ppermute | solution.py:304
  22.3 6.5 %collective-permute-start.18 = (bf16[16,2048]{1,0:T(8,128)(2,1)S(1)}, bf16[16,2048]{1,0:T(8,128)(2,1)S(1)}, u32[]{:S(2)}, u32[]{:S(2)}) collective-permute-start(bf16[16,2048]{1,0:T(8,128)(2,1)S(1)} %get-tuple-element.77), channel_id=1, source_target_pairs={{0,12},{4,8},{8,4},{12,0},{1,13},{5,9},{9,5},{13,1},{2,14},{6,10},... | collective-permute-start | bytes 196616 | tf_op jit(solution)/shard_map/ppermute | solution.py:304
  25.7 3.0 %copy-start.1 = (bf16[1,512,768]{2,1,0:T(8,128)(2,1)S(1)}, bf16[1,512,768]{2,1,0:T(8,128)(2,1)}, u32[]{:S(2)}) copy-start(bf16[1,512,768]{2,1,0:T(8,128)(2,1)} %param.13) | copy-start | bytes 2359300
  26.3 6.8 %collective-permute-start.9 = (bf16[64,1536]{1,0:T(8,128)(2,1)S(1)}, bf16[64,1536]{1,0:T(8,128)(2,1)S(1)}, u32[]{:S(2)}, u32[]{:S(2)}) collective-permute-start(bf16[64,1536]{1,0:T(8,128)(2,1)S(1)} %get-tuple-element.66), channel_id=1, source_target_pairs={{0,2},{1,3},{2,0},{3,1},{4,6},{5,7},{6,4},{7,5},{8,10},{9,11},{10,... | collective-permute-start | bytes 589832 | tf_op jit(solution)/shard_map/ppermute | solution.py:298
  29.2 5.6 %collective-permute-start.22 = (bf16[64,768]{1,0:T(8,128)(2,1)S(1)}, bf16[64,768]{1,0:T(8,128)(2,1)S(1)}, u32[]{:S(2)}, u32[]{:S(2)}) collective-permute-start(bf16[64,768]{1,0:T(8,128)(2,1)S(1)} %get-tuple-element.83), channel_id=1, source_target_pairs={{0,2},{1,3},{2,0},{3,1},{4,6},{5,7},{6,4},{7,5},{8,10},{9,11},{10,... | collective-permute-start | bytes 294920 | tf_op jit(solution)/shard_map/ppermute | solution.py:298
  33.2 5.6 %collective-permute-start.10 = (bf16[64,768]{1,0:T(8,128)(2,1)S(1)}, bf16[64,768]{1,0:T(8,128)(2,1)S(1)}, u32[]{:S(2)}, u32[]{:S(2)}) collective-permute-start(bf16[64,768]{1,0:T(8,128)(2,1)S(1)} %shard_map.97.refs_0_.refs_2_), channel_id=1, source_target_pairs={{0,2},{1,3},{2,0},{3,1},{4,6},{5,7},{6,4},{7,5},{8,10},{9,11},{10,... | collective-permute-start | bytes 294920 | tf_op jit(solution)/shard_map/ppermute | solution.py:298
  39.0 7.1 %collective-permute-start.23 = (bf16[64,1536]{1,0:T(8,128)(2,1)S(1)}, bf16[64,1536]{1,0:T(8,128)(2,1)S(1)}, u32[]{:S(2)}, u32[]{:S(2)}) collective-permute-start(bf16[64,1536]{1,0:T(8,128)(2,1)S(1)} %shard_map.104.refs_0_), channel_id=1, source_target_pairs={{0,2},{1,3},{2,0},{3,1},{4,6},{5,7},{6,4},{7,5},{8,10},{9,11},{10,... | collective-permute-start | bytes 589832 | tf_op jit(solution)/shard_map/ppermute | solution.py:298
  41.2 4.5 %collective-permute-start.11 = (bf16[32,1024]{1,0:T(8,128)(2,1)S(1)}, bf16[32,1024]{1,0:T(8,128)(2,1)S(1)}, u32[]{:S(2)}, u32[]{:S(2)}) collective-permute-start(bf16[32,1024]{1,0:T(8,128)(2,1)S(1)} %get-tuple-element.69), channel_id=1, source_target_pairs={{0,4},{4,0},{8,12},{12,8},{1,5},{5,1},{9,13},{13,9},{2,6},{6,2},{1... | collective-permute-start | bytes 196616 | tf_op jit(solution)/shard_map/ppermute | solution.py:304
  41.3 7.6 %collective-permute-start.12 = (bf16[32,1024]{1,0:T(8,128)(2,1)S(1)}, bf16[32,1024]{1,0:T(8,128)(2,1)S(1)}, u32[]{:S(2)}, u32[]{:S(2)}) collective-permute-start(bf16[32,1024]{1,0:T(8,128)(2,1)S(1)} %get-tuple-element.70), channel_id=1, source_target_pairs={{0,8},{4,12},{8,0},{12,4},{1,9},{5,13},{9,1},{13,5},{2,10},{6,14},... | collective-permute-start | bytes 196616 | tf_op jit(solution)/shard_map/ppermute | solution.py:304
  43.9 7.6 %collective-permute-start.13 = (bf16[32,1024]{1,0:T(8,128)(2,1)S(1)}, bf16[32,1024]{1,0:T(8,128)(2,1)S(1)}, u32[]{:S(2)}, u32[]{:S(2)}) collective-permute-start(bf16[32,1024]{1,0:T(8,128)(2,1)S(1)} %get-tuple-element.71), channel_id=1, source_target_pairs={{0,12},{4,8},{8,4},{12,0},{1,13},{5,9},{9,5},{13,1},{2,14},{6,10},... | collective-permute-start | bytes 196616 | tf_op jit(solution)/shard_map/ppermute | solution.py:304
  47.3 9.9 %collective-permute-start.27 = (bf16[64,1024]{1,0:T(8,128)(2,1)S(1)}, bf16[64,1024]{1,0:T(8,128)(2,1)S(1)}, u32[]{:S(2)}, u32[]{:S(2)}) collective-permute-start(bf16[64,1024]{1,0:T(8,128)(2,1)S(1)} %get-tuple-element.88), channel_id=1, source_target_pairs={{0,2},{1,3},{2,0},{3,1},{4,6},{5,7},{6,4},{7,5},{8,10},{9,11},{10,... | collective-permute-start | bytes 393224 | tf_op jit(solution)/shard_map/ppermute | solution.py:298
  48.8 4.4 %collective-permute-start.24 = (bf16[16,1024]{1,0:T(8,128)(2,1)S(1)}, bf16[16,1024]{1,0:T(8,128)(2,1)S(1)}, u32[]{:S(2)}, u32[]{:S(2)}) collective-permute-start(bf16[16,1024]{1,0:T(8,128)(2,1)S(1)} %get-tuple-element.85), channel_id=1, source_target_pairs={{0,4},{4,0},{8,12},{12,8},{1,5},{5,1},{9,13},{13,9},{2,6},{6,2},{1... | collective-permute-start | bytes 98312 | tf_op jit(solution)/shard_map/ppermute | solution.py:304
  48.8 8.4 %collective-permute-start.19 = (bf16[128,512]{1,0:T(8,128)(2,1)S(1)}, bf16[128,512]{1,0:T(8,128)(2,1)S(1)}, u32[]{:S(2)}, u32[]{:S(2)}) collective-permute-start(bf16[128,512]{1,0:T(8,128)(2,1)S(1)} %get-tuple-element.79), channel_id=1, source_target_pairs={{0,1},{1,0},{2,3},{3,2},{4,5},{5,4},{6,7},{7,6},{8,9},{9,8},{10,11... | collective-permute-start | bytes 393224 | tf_op jit(solution)/shard_map/ppermute | solution.py:294
  48.8 5.0 %collective-permute-start.25 = (bf16[16,1024]{1,0:T(8,128)(2,1)S(1)}, bf16[16,1024]{1,0:T(8,128)(2,1)S(1)}, u32[]{:S(2)}, u32[]{:S(2)}) collective-permute-start(bf16[16,1024]{1,0:T(8,128)(2,1)S(1)} %get-tuple-element.86), channel_id=1, source_target_pairs={{0,8},{4,12},{8,0},{12,4},{1,9},{5,13},{9,1},{13,5},{2,10},{6,14},... | collective-permute-start | bytes 98312 | tf_op jit(solution)/shard_map/ppermute | solution.py:304
  51.5 5.7 %collective-permute-start.26 = (bf16[16,1024]{1,0:T(8,128)(2,1)S(1)}, bf16[16,1024]{1,0:T(8,128)(2,1)S(1)}, u32[]{:S(2)}, u32[]{:S(2)}) collective-permute-start(bf16[16,1024]{1,0:T(8,128)(2,1)S(1)} %get-tuple-element.87), channel_id=1, source_target_pairs={{0,12},{4,8},{8,4},{12,0},{1,13},{5,9},{9,5},{13,1},{2,14},{6,10},... | collective-permute-start | bytes 98312 | tf_op jit(solution)/shard_map/ppermute | solution.py:304
  53.2 10.0 %collective-permute-start.14 = (bf16[64,1024]{1,0:T(8,128)(2,1)S(1)}, bf16[64,1024]{1,0:T(8,128)(2,1)S(1)}, u32[]{:S(2)}, u32[]{:S(2)}) collective-permute-start(bf16[64,1024]{1,0:T(8,128)(2,1)S(1)} %shard_map.99), channel_id=1, source_target_pairs={{0,2},{1,3},{2,0},{3,1},{4,6},{5,7},{6,4},{7,5},{8,10},{9,11},{10,... | collective-permute-start | bytes 393224 | tf_op jit(solution)/shard_map/ppermute | solution.py:298
  53.9 5.7 %collective-permute-start.20 = (bf16[64,768]{1,0:T(8,128)(2,1)S(1)}, bf16[64,768]{1,0:T(8,128)(2,1)S(1)}, u32[]{:S(2)}, u32[]{:S(2)}) collective-permute-start(bf16[64,768]{1,0:T(8,128)(2,1)S(1)} %shard_map.97.refs_0_.refs_2_), channel_id=1, source_target_pairs={{0,1},{1,0},{2,3},{3,2},{4,5},{5,4},{6,7},{7,6},{8,9},{9,8},{10,11... | collective-permute-start | bytes 294920 | tf_op jit(solution)/shard_map/ppermute | solution.py:294
  57.2 4.5 %collective-permute-start.21 = (bf16[64,768]{1,0:T(8,128)(2,1)S(1)}, bf16[64,768]{1,0:T(8,128)(2,1)S(1)}, u32[]{:S(2)}, u32[]{:S(2)}) collective-permute-start(bf16[64,768]{1,0:T(8,128)(2,1)S(1)} %collective-permute-done.10.refs_1_.refs_3_.refs_4_), channel_id=1, source_target_pairs={{0,1},{1,0},{2,3},{3,2},{4,5},{5,4},{6,7},{7,6},{8,9},{9,8},{10,11... | collective-permute-start | bytes 294920 | tf_op jit(solution)/shard_map/ppermute | solution.py:294
  57.2 7.3 %collective-permute-start.28 = (bf16[16,1024]{1,0:T(8,128)(2,1)S(1)}, bf16[16,1024]{1,0:T(8,128)(2,1)S(1)}, u32[]{:S(2)}, u32[]{:S(2)}) collective-permute-start(bf16[16,1024]{1,0:T(8,128)(2,1)S(1)} %get-tuple-element.90), channel_id=1, source_target_pairs={{0,4},{4,0},{8,12},{12,8},{1,5},{5,1},{9,13},{13,9},{2,6},{6,2},{1... | collective-permute-start | bytes 98312 | tf_op jit(solution)/shard_map/ppermute | solution.py:304
  57.3 7.3 %collective-permute-start.29 = (bf16[16,1024]{1,0:T(8,128)(2,1)S(1)}, bf16[16,1024]{1,0:T(8,128)(2,1)S(1)}, u32[]{:S(2)}, u32[]{:S(2)}) collective-permute-start(bf16[16,1024]{1,0:T(8,128)(2,1)S(1)} %get-tuple-element.91), channel_id=1, source_target_pairs={{0,8},{4,12},{8,0},{12,4},{1,9},{5,13},{9,1},{13,5},{2,10},{6,14},... | collective-permute-start | bytes 98312 | tf_op jit(solution)/shard_map/ppermute | solution.py:304
  59.6 5.7 %collective-permute-start.30 = (bf16[16,1024]{1,0:T(8,128)(2,1)S(1)}, bf16[16,1024]{1,0:T(8,128)(2,1)S(1)}, u32[]{:S(2)}, u32[]{:S(2)}) collective-permute-start(bf16[16,1024]{1,0:T(8,128)(2,1)S(1)} %get-tuple-element.92), channel_id=1, source_target_pairs={{0,12},{4,8},{8,4},{12,0},{1,13},{5,9},{9,5},{13,1},{2,14},{6,10},... | collective-permute-start | bytes 98312 | tf_op jit(solution)/shard_map/ppermute | solution.py:304

commit v13 on v11

--- a/solution.py
+++ b/solution.py
@@ -103,6 +103,10 @@
             outs[k // CORES][:, to] = value.astype(BF16)
 
 
+def flip(chunks):
+    return [chunks[0], *chunks[:0:-1]]
+
+
 def join_kernel(groups, spread, capacity, *refs):
     by_x, chunks = refs[:spread], refs[spread:]
     half = by_x[0].shape[1]
@@ -114,7 +118,7 @@
 
 
 def far_kernel(groups, spread, capacity, *refs):
-    by_e, by_x = refs[:groups], refs[groups:]
+    by_e, by_x = flip(refs[:groups]), refs[groups:]
     for ke in range(groups):
         for kx in range(1, spread):
             by_x[kx - 1][ke * capacity : (ke + 1) * capacity] = by_e[ke][
@@ -123,7 +127,7 @@
 
 
 def partial(groups, spread, refs, outs):
-    chunks, (own, sib) = refs[:groups], refs[groups:]
+    chunks, (own, sib) = flip(refs[:groups]), refs[groups:]
     part = own.shape[0]
     half = CORES * part
     rows = jnp.concatenate(
@@ -224,7 +228,7 @@
 
 
 def combine_kernel(groups, parts, capacity, turned, gate, *refs):
-    chunks, far, (out, held, sems) = refs[:groups], refs[groups:-3], refs[-3:]
+    chunks, far, (out, held, sems) = flip(refs[:groups]), refs[groups:-3], refs[-3:]
     part = held.shape[2]
 
     def weighted(k):
@@ -242,7 +246,7 @@
 
 
 def d_tokens_kernel(groups, parts, turned, *refs):
-    chunks, (out, held, sems) = refs[:groups], refs[groups:]
+    chunks, (out, held, sems) = flip(refs[:groups]), refs[groups:]
     part = held.shape[2]
     rows = (
         jnp.concatenate([c[:, k * part : (k + 1) * part] for c in chunks], axis=0)
@@ -308,7 +312,7 @@
     pre, *pre_far = call(
         bound(pre_kernel, groups, spread),
         [shape((slots, 2 * feed), F32)] + [shape((slots, 2 * feed))] * (spread - 1),
-        (*rows, in_own, in_sib),
+        (*flip(rows), in_own, in_sib),
     )
     pre = (pre, *to_x(pre_far))
     (hidden,) = call(hidden_kernel, [shape((slots, feed))], pre)
@@ -318,7 +322,7 @@
         [shape((spread * slots, part))] * 2
         + [shape((slots, feed), F32)]
         + [shape((slots, feed))] * (spread - 1),
-        (*grads, out_own, out_sib),
+        (*flip(grads), out_own, out_sib),
         cost=BACK_COST,
     )
     back = (back, *to_x(back_far))
@@ -338,7 +342,7 @@
     )
     d_rows = to_expert(call(join, chunk, (near, *to_x(far))))
     far = to_x(
-        call(bound(far_kernel, groups, spread, capacity), by_x[1:], expert_out)
+        call(bound(far_kernel, groups, spread, capacity), by_x[1:], flip(expert_out))
     )
     d_w_out, token = call(
         bound(weight_kernel, spread),
@@ -363,12 +367,12 @@
 
     combined, token = scattered(
         bound(combine_kernel, groups, parts, capacity),
-        (turned, gate, *expert_out, *far),
+        (turned, gate, *flip(expert_out), *far),
         after=(token,),
         token=True,
     )
     (d_tokens,) = scattered(
-        bound(d_tokens_kernel, groups, parts), (turned, *d_rows), after=(token,)
+        bound(d_tokens_kernel, groups, parts), (turned, *flip(d_rows)), after=(token,)
     )
     return combined, d_tokens, d_w_out[None]
 

time: 59.3 us -> 58 us (0.978)
  starting transfers between devices: 30.7 us -> 29.6 us
    ppermute x12, waiting for transfers between devices: 7.87 us -> 6.15 us  [to_expert(): lax.ppermute(value, 'expert', [(i, i ^ ke) for i in range(groups)])]
    ppermute x8, waiting for transfers between devices: 10.8 us -> 12.3 us  [to_x(): lax.ppermute(value, 'fsdp', [(i, i ^ (k + 1) * CORES) for i in range(part...]
  transfers between devices with their start and end apart: 25 -> 25, of which waited for: 12 -> 10; matrix products, arithmetic and copies ran while one was open for 0% -> 0% of each run, Pallas kernels for 13% -> 13%
where the time goes in v13:
time: 58 us; the launch traced here: 57.8 us
  starting transfers between devices  29.6 us (51%)
  waiting for transfers between devices  18.4 us (32%)
  Pallas kernels  9 us (16%)
  between operations  0.75 us (1%)
    ppermute x12, starting transfers between devices, to_expert(): lax.ppermute(value, 'expert', [(i, i ^ ke) for i in range(groups)])  17.3 us
    ppermute x8, waiting for transfers between devices, to_x(): lax.ppermute(value, 'fsdp', [(i, i ^ (k + 1) * CORES) for i in range(part...  12.3 us
    ppermute x8, starting transfers between devices, to_x(): lax.ppermute(value, 'fsdp', [(i, i ^ (k + 1) * CORES) for i in range(part...  11.2 us
    pallas_call x14, Pallas kernels, call(): pl.pallas_call(kernel, out_shape=out_shape, in_specs=specs, compiler_para...  9 us
    ppermute x12, waiting for transfers between devices, to_expert(): lax.ppermute(value, 'expert', [(i, i ^ ke) for i in range(groups)])  6.15 us
  transfers between devices with their start and end apart: 25, of which 10 were waited for; matrix products, arithmetic and copies ran while one was open for 0% of the time, Pallas kernels for 13%

profile of v13, /device:TPU:0, one launch (start us, length us, event | category | flops | bytes accessed | tf_op | source)
XLA Modules:
  0.0 57.8 jit_solution(6492833943487182565)
XLA Ops:
  0.6 0.5 collective-permute-start.1
  1.2 0.1 collective-permute-start.2
  1.2 1.9 %shard_map.94 = (bf16[64,1024]{1,0:T(8,128)(2,1)S(1)}, bf16[64,1024]{1,0:T(8,128)(2,1)S(1)}, bf16[64,1024]{1,0:T(8,128)(2,1)S(1)}, bf16[64,1024]{1,0:T(8,128)(2,...) custom-call(s32[8,256]{1,0:T(8,128)} %bitcast.11, f32[8,256]{1,0:T(8,128)} %bitcast.12, s32[1,256]{1,0:T(1,128)} %refs_2_.1, ...), custom_call_target="tpu_custom_call" | custom-call | tf_op jit(solution)/shard_map/pallas_call | solution.py:39
  3.2 3.0 %collective-permute-start = (bf16[64,1024]{1,0:T(8,128)(2,1)S(1)}, bf16[64,1024]{1,0:T(8,128)(2,1)S(1)}, u32[]{:S(2)}, u32[]{:S(2)}) collective-permute-start(bf16[64,1024]{1,0:T(8,128)(2,1)S(1)} %get-tuple-element.44), channel_id=1, source_target_pairs={{0,2},{1,3},{2,0},{3,1},{4,6},{5,7},{6,4},{7,5},{8,10},{9,11},{10,... | collective-permute-start | bytes 393224 | tf_op jit(solution)/shard_map/ppermute | solution.py:277
  6.2 0.1 collective-permute-start.12
  6.2 4.2 %collective-permute-done.refs_1_ = bf16[64,1024]{1,0:T(8,128)(2,1)S(1)} collective-permute-done((bf16[64,1024]{1,0:T(8,128)(2,1)S(1)}, bf16[64,1024]{1,0:T(8,128)(2,1)S(1)}, u32[]{:S(2)}, u32[]{:S(2)}) %collective-permute-start) | collective-permute-done | bytes 131104 | tf_op jit(solution)/shard_map/ppermute | solution.py:277
  10.5 0.0 collective-permute-done.2.refs_3_.refs_5_
  10.5 0.0 collective-permute-done.1.refs_5_.refs_3_
  10.5 4.2 %collective-permute-start.3 = (bf16[16,2048]{1,0:T(8,128)(2,1)S(1)}, bf16[16,2048]{1,0:T(8,128)(2,1)S(1)}, u32[]{:S(2)}, u32[]{:S(2)}) collective-permute-start(bf16[16,2048]{1,0:T(8,128)(2,1)S(1)} %get-tuple-element.48), channel_id=1, source_target_pairs={{0,12},{4,8},{8,4},{12,0},{1,13},{5,9},{9,5},{13,1},{2,14},{6,10},... | collective-permute-start | bytes 196616 | tf_op jit(solution)/shard_map/ppermute | solution.py:283
  14.7 0.0 collective-permute-start.4
  14.7 0.6 %collective-permute-start.5 = (bf16[16,2048]{1,0:T(8,128)(2,1)S(1)}, bf16[16,2048]{1,0:T(8,128)(2,1)S(1)}, u32[]{:S(2)}, u32[]{:S(2)}) collective-permute-start(bf16[16,2048]{1,0:T(8,128)(2,1)S(1)} %get-tuple-element.50), channel_id=1, source_target_pairs={{0,4},{4,0},{8,12},{12,8},{1,5},{5,1},{9,13},{13,9},{2,6},{6,2},{1... | collective-permute-start | bytes 196616 | tf_op jit(solution)/shard_map/ppermute | solution.py:283
  15.4 0.0 collective-permute-done.12.refs_1_
  15.4 3.8 %collective-permute-start.13 = (bf16[16,2048]{1,0:T(8,128)(2,1)S(1)}, bf16[16,2048]{1,0:T(8,128)(2,1)S(1)}, u32[]{:S(2)}, u32[]{:S(2)}) collective-permute-start(bf16[16,2048]{1,0:T(8,128)(2,1)S(1)} %get-tuple-element.62), channel_id=1, source_target_pairs={{0,12},{4,8},{8,4},{12,0},{1,13},{5,9},{9,5},{13,1},{2,14},{6,10},... | collective-permute-start | bytes 196616 | tf_op jit(solution)/shard_map/ppermute | solution.py:283
  19.2 0.6 %collective-permute-start.15 = (bf16[16,2048]{1,0:T(8,128)(2,1)S(1)}, bf16[16,2048]{1,0:T(8,128)(2,1)S(1)}, u32[]{:S(2)}, u32[]{:S(2)}) collective-permute-start(bf16[16,2048]{1,0:T(8,128)(2,1)S(1)} %get-tuple-element.64), channel_id=1, source_target_pairs={{0,4},{4,0},{8,12},{12,8},{1,5},{5,1},{9,13},{13,9},{2,6},{6,2},{1... | collective-permute-start | bytes 196616 | tf_op jit(solution)/shard_map/ppermute | solution.py:283
  19.8 2.2 %collective-permute-done.4.refs_2_ = bf16[16,2048]{1,0:T(8,128)(2,1)S(1)} collective-permute-done((bf16[16,2048]{1,0:T(8,128)(2,1)S(1)}, bf16[16,2048]{1,0:T(8,128)(2,1)S(1)}, u32[]{:S(2)}, u32[]{:S(2)}) %collective-permute-start.4) | collective-permute-done | bytes 65568 | tf_op jit(solution)/shard_map/ppermute | solution.py:283
  22.1 0.6 shard_map.96
  22.6 1.6 %collective-permute-start.6 = (bf16[64,1536]{1,0:T(8,128)(2,1)S(1)}, bf16[64,1536]{1,0:T(8,128)(2,1)S(1)}, u32[]{:S(2)}, u32[]{:S(2)}) collective-permute-start(bf16[64,1536]{1,0:T(8,128)(2,1)S(1)} %get-tuple-element.53), channel_id=1, source_target_pairs={{0,2},{1,3},{2,0},{3,1},{4,6},{5,7},{6,4},{7,5},{8,10},{9,11},{10,... | collective-permute-start | bytes 589832 | tf_op jit(solution)/shard_map/ppermute | solution.py:277
  24.2 0.0 collective-permute-done.13.refs_1_
  24.2 0.9 %collective-permute-done.14.refs_2_ = bf16[16,2048]{1,0:T(8,128)(2,1)S(1)} collective-permute-done((bf16[16,2048]{1,0:T(8,128)(2,1)S(1)}, bf16[16,2048]{1,0:T(8,128)(2,1)S(1)}, u32[]{:S(2)}, u32[]{:S(2)}) %collective-permute-start.14) | collective-permute-done | bytes 65568 | tf_op jit(solution)/shard_map/ppermute | solution.py:283
  25.1 0.0 collective-permute-done.15.refs_3_
  25.1 0.4 shard_map.101
  25.5 1.6 %collective-permute-start.19 = (bf16[64,768]{1,0:T(8,128)(2,1)S(1)}, bf16[64,768]{1,0:T(8,128)(2,1)S(1)}, u32[]{:S(2)}, u32[]{:S(2)}) collective-permute-start(bf16[64,768]{1,0:T(8,128)(2,1)S(1)} %get-tuple-element.70), channel_id=1, source_target_pairs={{0,2},{1,3},{2,0},{3,1},{4,6},{5,7},{6,4},{7,5},{8,10},{9,11},{10,... | collective-permute-start | bytes 294920 | tf_op jit(solution)/shard_map/ppermute | solution.py:277
  27.1 2.7 %collective-permute-done.6.refs_1_ = bf16[64,1536]{1,0:T(8,128)(2,1)S(1)} collective-permute-done((bf16[64,1536]{1,0:T(8,128)(2,1)S(1)}, bf16[64,1536]{1,0:T(8,128)(2,1)S(1)}, u32[]{:S(2)}, u32[]{:S(2)}) %collective-permute-start.6) | collective-permute-done | bytes 196640 | tf_op jit(solution)/shard_map/ppermute | solution.py:277
  29.7 0.1 shard_map.97.refs_0_.refs_2_
  29.8 1.6 %collective-permute-start.7 = (bf16[64,768]{1,0:T(8,128)(2,1)S(1)}, bf16[64,768]{1,0:T(8,128)(2,1)S(1)}, u32[]{:S(2)}, u32[]{:S(2)}) collective-permute-start(bf16[64,768]{1,0:T(8,128)(2,1)S(1)} %shard_map.97.refs_0_.refs_2_), channel_id=1, source_target_pairs={{0,2},{1,3},{2,0},{3,1},{4,6},{5,7},{6,4},{7,5},{8,10},{9,11},{10,... | collective-permute-start | bytes 294920 | tf_op jit(solution)/shard_map/ppermute | solution.py:277
  31.4 0.2 collective-permute-done.19.refs_3_
  31.5 3.4 %collective-permute-done.7.refs_1_.refs_3_.refs_4_ = bf16[64,768]{1,0:T(8,128)(2,1)S(1)} collective-permute-done((bf16[64,768]{1,0:T(8,128)(2,1)S(1)}, bf16[64,768]{1,0:T(8,128)(2,1)S(1)}, u32[]{:S(2)}, u32[]{:S(2)}) %collective-permute-start.7) | collective-permute-done | bytes 98336 | tf_op jit(solution)/shard_map/ppermute | solution.py:277
  34.9 0.1 shard_map.104.refs_0_
  35.0 1.6 %collective-permute-start.20 = (bf16[64,1536]{1,0:T(8,128)(2,1)S(1)}, bf16[64,1536]{1,0:T(8,128)(2,1)S(1)}, u32[]{:S(2)}, u32[]{:S(2)}) collective-permute-start(bf16[64,1536]{1,0:T(8,128)(2,1)S(1)} %shard_map.104.refs_0_), channel_id=1, source_target_pairs={{0,2},{1,3},{2,0},{3,1},{4,6},{5,7},{6,4},{7,5},{8,10},{9,11},{10,... | collective-permute-start | bytes 589832 | tf_op jit(solution)/shard_map/ppermute | solution.py:277
  36.6 0.6 %shard_map.98 = (bf16[32,1024]{1,0:T(8,128)(2,1)S(1)}, bf16[32,1024]{1,0:T(8,128)(2,1)S(1)}, bf16[32,1024]{1,0:T(8,128)(2,1)S(1)}, bf16[32,1024]{1,0:T(8,128)(2,1)S(1)}) custom-call(bf16[64,768]{1,0:T(8,128)(2,1)S(1)} %shard_map.97.refs_0_.refs_2_, bf16[64,768]{1,0:T(8,128)(2,1)S(1)} %collective-permute-done.7.refs_1_.refs_3_.refs_4_, ...), custom_call_target="tpu_custom_call" | custom-call | tf_op jit(solution)/shard_map/pallas_call | solution.py:39
  37.3 0.6 collective-permute-start.10
  37.8 2.2 %collective-permute-start.8 = (bf16[32,1024]{1,0:T(8,128)(2,1)S(1)}, bf16[32,1024]{1,0:T(8,128)(2,1)S(1)}, u32[]{:S(2)}, u32[]{:S(2)}) collective-permute-start(bf16[32,1024]{1,0:T(8,128)(2,1)S(1)} %get-tuple-element.56), channel_id=1, source_target_pairs={{0,12},{4,8},{8,4},{12,0},{1,13},{5,9},{9,5},{13,1},{2,14},{6,10},... | collective-permute-start | bytes 196616 | tf_op jit(solution)/shard_map/ppermute | solution.py:283
  40.0 0.8 %collective-permute-start.9 = (bf16[32,1024]{1,0:T(8,128)(2,1)S(1)}, bf16[32,1024]{1,0:T(8,128)(2,1)S(1)}, u32[]{:S(2)}, u32[]{:S(2)}) collective-permute-start(bf16[32,1024]{1,0:T(8,128)(2,1)S(1)} %get-tuple-element.57), channel_id=1, source_target_pairs={{0,8},{4,12},{8,0},{12,4},{1,9},{5,13},{9,1},{13,5},{2,10},{6,14},... | collective-permute-start | bytes 196616 | tf_op jit(solution)/shard_map/ppermute | solution.py:283
  40.8 0.8 %collective-permute-done.10.refs_3_.refs_5_.refs_4_ = bf16[32,1024]{1,0:T(8,128)(2,1)S(1)} collective-permute-done((bf16[32,1024]{1,0:T(8,128)(2,1)S(1)}, bf16[32,1024]{1,0:T(8,128)(2,1)S(1)}, u32[]{:S(2)}, u32[]{:S(2)}) %collective-permute-start.10) | collective-permute-done | bytes 65568 | tf_op jit(solution)/shard_map/ppermute | solution.py:283
  41.6 1.1 %shard_map.105 = (bf16[64,1024]{1,0:T(8,128)(2,1)S(1)}, bf16[64,1024]{1,0:T(8,128)(2,1)S(1)}) custom-call(bf16[64,1536]{1,0:T(8,128)(2,1)S(1)} %shard_map.104.refs_0_, bf16[64,1536]{1,0:T(8,128)(2,1)S(1)} %collective-permute-done.20.refs_1_, bf16[512,1536]{1,0:T(8,128)(2,1)S(1)} %bitcast.7, bf16[512,1536]{1,0:T(8,128)(2,1)S(1)} %collective-permute-done.1.refs_5_.refs_3_, ...), custom_call_target="tpu_custom_call" | custom-call | tf_op jit(solution)/shard_map/pallas_call | solution.py:39
  42.7 1.3 %collective-permute-start.21 = (bf16[64,1024]{1,0:T(8,128)(2,1)S(1)}, bf16[64,1024]{1,0:T(8,128)(2,1)S(1)}, u32[]{:S(2)}, u32[]{:S(2)}) collective-permute-start(bf16[64,1024]{1,0:T(8,128)(2,1)S(1)} %get-tuple-element.72), channel_id=1, source_target_pairs={{0,2},{1,3},{2,0},{3,1},{4,6},{5,7},{6,4},{7,5},{8,10},{9,11},{10,... | collective-permute-start | bytes 393224 | tf_op jit(solution)/shard_map/ppermute | solution.py:277
  44.0 0.0 collective-permute-start.16
  44.0 0.5 collective-permute-start.17
  44.5 1.4 %collective-permute-done.9.refs_2_.refs_4_ = bf16[32,1024]{1,0:T(8,128)(2,1)S(1)} collective-permute-done((bf16[32,1024]{1,0:T(8,128)(2,1)S(1)}, bf16[32,1024]{1,0:T(8,128)(2,1)S(1)}, u32[]{:S(2)}, u32[]{:S(2)}) %collective-permute-start.9) | collective-permute-done | bytes 65568 | tf_op jit(solution)/shard_map/ppermute | solution.py:283
  45.9 0.6 %collective-permute-start.11 = (bf16[64,1024]{1,0:T(8,128)(2,1)S(1)}, bf16[64,1024]{1,0:T(8,128)(2,1)S(1)}, u32[]{:S(2)}, u32[]{:S(2)}) collective-permute-start(bf16[64,1024]{1,0:T(8,128)(2,1)S(1)} %shard_map.99), channel_id=1, source_target_pairs={{0,2},{1,3},{2,0},{3,1},{4,6},{5,7},{6,4},{7,5},{8,10},{9,11},{10,... | collective-permute-start | bytes 393224 | tf_op jit(solution)/shard_map/ppermute | solution.py:277
  46.5 0.0 collective-permute-start.18
  46.5 1.9 %collective-permute-done.21.refs_1_ = bf16[64,1024]{1,0:T(8,128)(2,1)S(1)} collective-permute-done((bf16[64,1024]{1,0:T(8,128)(2,1)S(1)}, bf16[64,1024]{1,0:T(8,128)(2,1)S(1)}, u32[]{:S(2)}, u32[]{:S(2)}) %collective-permute-start.21) | collective-permute-done | bytes 131104 | tf_op jit(solution)/shard_map/ppermute | solution.py:277
  48.4 3.0 %collective-permute-start.22 = (bf16[16,2048]{1,0:T(8,128)(2,1)S(1)}, bf16[16,2048]{1,0:T(8,128)(2,1)S(1)}, u32[]{:S(2)}, u32[]{:S(2)}) collective-permute-start(bf16[16,2048]{1,0:T(8,128)(2,1)S(1)} %get-tuple-element.74), channel_id=1, source_target_pairs={{0,12},{4,8},{8,4},{12,0},{1,13},{5,9},{9,5},{13,1},{2,14},{6,10},... | collective-permute-start | bytes 196616 | tf_op jit(solution)/shard_map/ppermute | solution.py:283
  51.4 1.4 %collective-permute-start.24 = (bf16[16,2048]{1,0:T(8,128)(2,1)S(1)}, bf16[16,2048]{1,0:T(8,128)(2,1)S(1)}, u32[]{:S(2)}, u32[]{:S(2)}) collective-permute-start(bf16[16,2048]{1,0:T(8,128)(2,1)S(1)} %get-tuple-element.76), channel_id=1, source_target_pairs={{0,4},{4,0},{8,12},{12,8},{1,5},{5,1},{9,13},{13,9},{2,6},{6,2},{1... | collective-permute-start | bytes 196616 | tf_op jit(solution)/shard_map/ppermute | solution.py:283
  52.9 1.6 %shard_map.102 = (f32[512,768]{1,0:T(8,128)}, f32[8,128]{1,0:T(8,128)S(1)}) custom-call(bf16[128,512]{1,0:T(8,128)(2,1)S(1)} %get-tuple-element.65.refs_0_, bf16[128,512]{1,0:T(8,128)(2,1)S(1)} %collective-permute-done.16.refs_1_, bf16[64,768]{1,0:T(8,128)(2,1)S(1)} %shard_map.97.refs_0_.refs_2_, ...), custom_call_target="tpu_custom_call" | custom-call | tf_op jit(solution)/shard_map/pallas_call | solution.py:39
  54.4 1.3 %shard_map.103 = (bf16[256,2048]{1,0:T(8,128)(2,1)}, f32[8,128]{1,0:T(8,128)S(1)}) custom-call(bf16[256,64]{1,0:T(8,128)(2,1)S(1)} %get-tuple-element.41.refs_0_, f32[64,128]{1,0:T(8,128)S(1)} %get-tuple-element.42.refs_1_, bf16[32,1024]{1,0:T(8,128)(2,1)S(1)} %get-tuple-element.55.refs_0_.refs_2_, ...), custom_call_target="tpu_custom_call" | custom-call | tf_op jit(solution)/shard_map/pallas_call | solution.py:39
  55.7 0.9 %collective-permute-done.23.refs_3_ = bf16[16,2048]{1,0:T(8,128)(2,1)S(1)} collective-permute-done((bf16[16,2048]{1,0:T(8,128)(2,1)S(1)}, bf16[16,2048]{1,0:T(8,128)(2,1)S(1)}, u32[]{:S(2)}, u32[]{:S(2)}) %collective-permute-start.23) | collective-permute-done | bytes 65568 | tf_op jit(solution)/shard_map/ppermute | solution.py:283
  56.6 1.2 %shard_map.107 = bf16[256,2048]{1,0:T(8,128)(2,1)} custom-call(bf16[256,64]{1,0:T(8,128)(2,1)S(1)} %get-tuple-element.41.refs_0_, bf16[16,2048]{1,0:T(8,128)(2,1)S(1)} %get-tuple-element.73.refs_1_, bf16[16,2048]{1,0:T(8,128)(2,1)S(1)} %collective-permute-done.22.refs_2_, bf16[16,2048]{1,0:T(8,128)(2,1)S(1)} %collective-permute-done.23.refs_3_, ...), custom_call_target="tpu_custom_call" | custom-call | tf_op jit(solution)/shard_map/pallas_call | solution.py:39
  (20 shorter events, 0.1 us)
Async XLA Ops:
  0.6 21.4 %copy-start = (bf16[1,512,1536]{2,1,0:T(8,128)(2,1)S(1)}, bf16[1,512,1536]{2,1,0:T(8,128)(2,1)}, u32[]{:S(2)}) copy-start(bf16[1,512,1536]{2,1,0:T(8,128)(2,1)} %param.12) | copy-start | bytes 4718596
  0.6 9.8 %collective-permute-start.1 = (bf16[512,1536]{1,0:T(8,128)(2,1)}, bf16[512,1536]{1,0:T(8,128)(2,1)S(1)}, u32[]{:S(2)}, u32[]{:S(2)}) collective-permute-start(bf16[512,1536]{1,0:T(8,128)(2,1)} %bitcast.5), channel_id=1, source_target_pairs={{0,1},{1,0},{2,3},{3,2},{4,5},{5,4},{6,7},{7,6},{8,9},{9,8},{10,11... | collective-permute-start | bytes 4718600 | tf_op jit(solution)/shard_map/ppermute | solution.py:273
  1.2 9.3 %collective-permute-start.2 = (bf16[512,768]{1,0:T(8,128)(2,1)}, bf16[512,768]{1,0:T(8,128)(2,1)S(1)}, u32[]{:S(2)}, u32[]{:S(2)}) collective-permute-start(bf16[512,768]{1,0:T(8,128)(2,1)} %bitcast.8), channel_id=1, source_target_pairs={{0,1},{1,0},{2,3},{3,2},{4,5},{5,4},{6,7},{7,6},{8,9},{9,8},{10,11... | collective-permute-start | bytes 2359304 | tf_op jit(solution)/shard_map/ppermute | solution.py:273
  3.2 7.3 %collective-permute-start = (bf16[64,1024]{1,0:T(8,128)(2,1)S(1)}, bf16[64,1024]{1,0:T(8,128)(2,1)S(1)}, u32[]{:S(2)}, u32[]{:S(2)}) collective-permute-start(bf16[64,1024]{1,0:T(8,128)(2,1)S(1)} %get-tuple-element.44), channel_id=1, source_target_pairs={{0,2},{1,3},{2,0},{3,1},{4,6},{5,7},{6,4},{7,5},{8,10},{9,11},{10,... | collective-permute-start | bytes 393224 | tf_op jit(solution)/shard_map/ppermute | solution.py:277
  6.2 9.2 %collective-permute-start.12 = (bf16[64,1024]{1,0:T(8,128)(2,1)S(1)}, bf16[64,1024]{1,0:T(8,128)(2,1)S(1)}, u32[]{:S(2)}, u32[]{:S(2)}) collective-permute-start(bf16[64,1024]{1,0:T(8,128)(2,1)S(1)} %get-tuple-element.60), channel_id=1, source_target_pairs={{0,2},{1,3},{2,0},{3,1},{4,6},{5,7},{6,4},{7,5},{8,10},{9,11},{10,... | collective-permute-start | bytes 393224 | tf_op jit(solution)/shard_map/ppermute | solution.py:277
  10.5 8.7 %collective-permute-start.3 = (bf16[16,2048]{1,0:T(8,128)(2,1)S(1)}, bf16[16,2048]{1,0:T(8,128)(2,1)S(1)}, u32[]{:S(2)}, u32[]{:S(2)}) collective-permute-start(bf16[16,2048]{1,0:T(8,128)(2,1)S(1)} %get-tuple-element.48), channel_id=1, source_target_pairs={{0,12},{4,8},{8,4},{12,0},{1,13},{5,9},{9,5},{13,1},{2,14},{6,10},... | collective-permute-start | bytes 196616 | tf_op jit(solution)/shard_map/ppermute | solution.py:283
  14.7 7.3 %collective-permute-start.4 = (bf16[16,2048]{1,0:T(8,128)(2,1)S(1)}, bf16[16,2048]{1,0:T(8,128)(2,1)S(1)}, u32[]{:S(2)}, u32[]{:S(2)}) collective-permute-start(bf16[16,2048]{1,0:T(8,128)(2,1)S(1)} %get-tuple-element.49), channel_id=1, source_target_pairs={{0,8},{4,12},{8,0},{12,4},{1,9},{5,13},{9,1},{13,5},{2,10},{6,14},... | collective-permute-start | bytes 196616 | tf_op jit(solution)/shard_map/ppermute | solution.py:283
  14.7 7.3 %collective-permute-start.5 = (bf16[16,2048]{1,0:T(8,128)(2,1)S(1)}, bf16[16,2048]{1,0:T(8,128)(2,1)S(1)}, u32[]{:S(2)}, u32[]{:S(2)}) collective-permute-start(bf16[16,2048]{1,0:T(8,128)(2,1)S(1)} %get-tuple-element.50), channel_id=1, source_target_pairs={{0,4},{4,0},{8,12},{12,8},{1,5},{5,1},{9,13},{13,9},{2,6},{6,2},{1... | collective-permute-start | bytes 196616 | tf_op jit(solution)/shard_map/ppermute | solution.py:283
  15.4 8.8 %collective-permute-start.13 = (bf16[16,2048]{1,0:T(8,128)(2,1)S(1)}, bf16[16,2048]{1,0:T(8,128)(2,1)S(1)}, u32[]{:S(2)}, u32[]{:S(2)}) collective-permute-start(bf16[16,2048]{1,0:T(8,128)(2,1)S(1)} %get-tuple-element.62), channel_id=1, source_target_pairs={{0,12},{4,8},{8,4},{12,0},{1,13},{5,9},{9,5},{13,1},{2,14},{6,10},... | collective-permute-start | bytes 196616 | tf_op jit(solution)/shard_map/ppermute | solution.py:283
  19.2 5.9 %collective-permute-start.14 = (bf16[16,2048]{1,0:T(8,128)(2,1)S(1)}, bf16[16,2048]{1,0:T(8,128)(2,1)S(1)}, u32[]{:S(2)}, u32[]{:S(2)}) collective-permute-start(bf16[16,2048]{1,0:T(8,128)(2,1)S(1)} %get-tuple-element.63), channel_id=1, source_target_pairs={{0,8},{4,12},{8,0},{12,4},{1,9},{5,13},{9,1},{13,5},{2,10},{6,14},... | collective-permute-start | bytes 196616 | tf_op jit(solution)/shard_map/ppermute | solution.py:283
  19.2 5.9 %collective-permute-start.15 = (bf16[16,2048]{1,0:T(8,128)(2,1)S(1)}, bf16[16,2048]{1,0:T(8,128)(2,1)S(1)}, u32[]{:S(2)}, u32[]{:S(2)}) collective-permute-start(bf16[16,2048]{1,0:T(8,128)(2,1)S(1)} %get-tuple-element.64), channel_id=1, source_target_pairs={{0,4},{4,0},{8,12},{12,8},{1,5},{5,1},{9,13},{13,9},{2,6},{6,2},{1... | collective-permute-start | bytes 196616 | tf_op jit(solution)/shard_map/ppermute | solution.py:283
  22.0 3.1 %copy-start.1 = (bf16[1,512,768]{2,1,0:T(8,128)(2,1)S(1)}, bf16[1,512,768]{2,1,0:T(8,128)(2,1)}, u32[]{:S(2)}) copy-start(bf16[1,512,768]{2,1,0:T(8,128)(2,1)} %param.13) | copy-start | bytes 2359300
  22.6 7.1 %collective-permute-start.6 = (bf16[64,1536]{1,0:T(8,128)(2,1)S(1)}, bf16[64,1536]{1,0:T(8,128)(2,1)S(1)}, u32[]{:S(2)}, u32[]{:S(2)}) collective-permute-start(bf16[64,1536]{1,0:T(8,128)(2,1)S(1)} %get-tuple-element.53), channel_id=1, source_target_pairs={{0,2},{1,3},{2,0},{3,1},{4,6},{5,7},{6,4},{7,5},{8,10},{9,11},{10,... | collective-permute-start | bytes 589832 | tf_op jit(solution)/shard_map/ppermute | solution.py:277
  25.5 6.0 %collective-permute-start.19 = (bf16[64,768]{1,0:T(8,128)(2,1)S(1)}, bf16[64,768]{1,0:T(8,128)(2,1)S(1)}, u32[]{:S(2)}, u32[]{:S(2)}) collective-permute-start(bf16[64,768]{1,0:T(8,128)(2,1)S(1)} %get-tuple-element.70), channel_id=1, source_target_pairs={{0,2},{1,3},{2,0},{3,1},{4,6},{5,7},{6,4},{7,5},{8,10},{9,11},{10,... | collective-permute-start | bytes 294920 | tf_op jit(solution)/shard_map/ppermute | solution.py:277
  29.8 5.1 %collective-permute-start.7 = (bf16[64,768]{1,0:T(8,128)(2,1)S(1)}, bf16[64,768]{1,0:T(8,128)(2,1)S(1)}, u32[]{:S(2)}, u32[]{:S(2)}) collective-permute-start(bf16[64,768]{1,0:T(8,128)(2,1)S(1)} %shard_map.97.refs_0_.refs_2_), channel_id=1, source_target_pairs={{0,2},{1,3},{2,0},{3,1},{4,6},{5,7},{6,4},{7,5},{8,10},{9,11},{10,... | collective-permute-start | bytes 294920 | tf_op jit(solution)/shard_map/ppermute | solution.py:277
  35.0 6.6 %collective-permute-start.20 = (bf16[64,1536]{1,0:T(8,128)(2,1)S(1)}, bf16[64,1536]{1,0:T(8,128)(2,1)S(1)}, u32[]{:S(2)}, u32[]{:S(2)}) collective-permute-start(bf16[64,1536]{1,0:T(8,128)(2,1)S(1)} %shard_map.104.refs_0_), channel_id=1, source_target_pairs={{0,2},{1,3},{2,0},{3,1},{4,6},{5,7},{6,4},{7,5},{8,10},{9,11},{10,... | collective-permute-start | bytes 589832 | tf_op jit(solution)/shard_map/ppermute | solution.py:277
  37.3 4.3 %collective-permute-start.10 = (bf16[32,1024]{1,0:T(8,128)(2,1)S(1)}, bf16[32,1024]{1,0:T(8,128)(2,1)S(1)}, u32[]{:S(2)}, u32[]{:S(2)}) collective-permute-start(bf16[32,1024]{1,0:T(8,128)(2,1)S(1)} %get-tuple-element.58), channel_id=1, source_target_pairs={{0,4},{4,0},{8,12},{12,8},{1,5},{5,1},{9,13},{13,9},{2,6},{6,2},{1... | collective-permute-start | bytes 196616 | tf_op jit(solution)/shard_map/ppermute | solution.py:283
  37.8 6.7 %collective-permute-start.8 = (bf16[32,1024]{1,0:T(8,128)(2,1)S(1)}, bf16[32,1024]{1,0:T(8,128)(2,1)S(1)}, u32[]{:S(2)}, u32[]{:S(2)}) collective-permute-start(bf16[32,1024]{1,0:T(8,128)(2,1)S(1)} %get-tuple-element.56), channel_id=1, source_target_pairs={{0,12},{4,8},{8,4},{12,0},{1,13},{5,9},{9,5},{13,1},{2,14},{6,10},... | collective-permute-start | bytes 196616 | tf_op jit(solution)/shard_map/ppermute | solution.py:283
  40.0 5.9 %collective-permute-start.9 = (bf16[32,1024]{1,0:T(8,128)(2,1)S(1)}, bf16[32,1024]{1,0:T(8,128)(2,1)S(1)}, u32[]{:S(2)}, u32[]{:S(2)}) collective-permute-start(bf16[32,1024]{1,0:T(8,128)(2,1)S(1)} %get-tuple-element.57), channel_id=1, source_target_pairs={{0,8},{4,12},{8,0},{12,4},{1,9},{5,13},{9,1},{13,5},{2,10},{6,14},... | collective-permute-start | bytes 196616 | tf_op jit(solution)/shard_map/ppermute | solution.py:283
  42.7 5.6 %collective-permute-start.21 = (bf16[64,1024]{1,0:T(8,128)(2,1)S(1)}, bf16[64,1024]{1,0:T(8,128)(2,1)S(1)}, u32[]{:S(2)}, u32[]{:S(2)}) collective-permute-start(bf16[64,1024]{1,0:T(8,128)(2,1)S(1)} %get-tuple-element.72), channel_id=1, source_target_pairs={{0,2},{1,3},{2,0},{3,1},{4,6},{5,7},{6,4},{7,5},{8,10},{9,11},{10,... | collective-permute-start | bytes 393224 | tf_op jit(solution)/shard_map/ppermute | solution.py:277
  44.0 7.4 %collective-permute-start.16 = (bf16[128,512]{1,0:T(8,128)(2,1)S(1)}, bf16[128,512]{1,0:T(8,128)(2,1)S(1)}, u32[]{:S(2)}, u32[]{:S(2)}) collective-permute-start(bf16[128,512]{1,0:T(8,128)(2,1)S(1)} %get-tuple-element.66), channel_id=1, source_target_pairs={{0,1},{1,0},{2,3},{3,2},{4,5},{5,4},{6,7},{7,6},{8,9},{9,8},{10,11... | collective-permute-start | bytes 393224 | tf_op jit(solution)/shard_map/ppermute | solution.py:273
  44.0 7.4 %collective-permute-start.17 = (bf16[64,768]{1,0:T(8,128)(2,1)S(1)}, bf16[64,768]{1,0:T(8,128)(2,1)S(1)}, u32[]{:S(2)}, u32[]{:S(2)}) collective-permute-start(bf16[64,768]{1,0:T(8,128)(2,1)S(1)} %shard_map.97.refs_0_.refs_2_), channel_id=1, source_target_pairs={{0,1},{1,0},{2,3},{3,2},{4,5},{5,4},{6,7},{7,6},{8,9},{9,8},{10,11... | collective-permute-start | bytes 294920 | tf_op jit(solution)/shard_map/ppermute | solution.py:273
  45.9 8.5 %collective-permute-start.11 = (bf16[64,1024]{1,0:T(8,128)(2,1)S(1)}, bf16[64,1024]{1,0:T(8,128)(2,1)S(1)}, u32[]{:S(2)}, u32[]{:S(2)}) collective-permute-start(bf16[64,1024]{1,0:T(8,128)(2,1)S(1)} %shard_map.99), channel_id=1, source_target_pairs={{0,2},{1,3},{2,0},{3,1},{4,6},{5,7},{6,4},{7,5},{8,10},{9,11},{10,... | collective-permute-start | bytes 393224 | tf_op jit(solution)/shard_map/ppermute | solution.py:277
  46.5 6.4 %collective-permute-start.18 = (bf16[64,768]{1,0:T(8,128)(2,1)S(1)}, bf16[64,768]{1,0:T(8,128)(2,1)S(1)}, u32[]{:S(2)}, u32[]{:S(2)}) collective-permute-start(bf16[64,768]{1,0:T(8,128)(2,1)S(1)} %collective-permute-done.7.refs_1_.refs_3_.refs_4_), channel_id=1, source_target_pairs={{0,1},{1,0},{2,3},{3,2},{4,5},{5,4},{6,7},{7,6},{8,9},{9,8},{10,11... | collective-permute-start | bytes 294920 | tf_op jit(solution)/shard_map/ppermute | solution.py:273
  48.4 7.3 %collective-permute-start.22 = (bf16[16,2048]{1,0:T(8,128)(2,1)S(1)}, bf16[16,2048]{1,0:T(8,128)(2,1)S(1)}, u32[]{:S(2)}, u32[]{:S(2)}) collective-permute-start(bf16[16,2048]{1,0:T(8,128)(2,1)S(1)} %get-tuple-element.74), channel_id=1, source_target_pairs={{0,12},{4,8},{8,4},{12,0},{1,13},{5,9},{9,5},{13,1},{2,14},{6,10},... | collective-permute-start | bytes 196616 | tf_op jit(solution)/shard_map/ppermute | solution.py:283
  51.4 5.2 %collective-permute-start.23 = (bf16[16,2048]{1,0:T(8,128)(2,1)S(1)}, bf16[16,2048]{1,0:T(8,128)(2,1)S(1)}, u32[]{:S(2)}, u32[]{:S(2)}) collective-permute-start(bf16[16,2048]{1,0:T(8,128)(2,1)S(1)} %get-tuple-element.75), channel_id=1, source_target_pairs={{0,8},{4,12},{8,0},{12,4},{1,9},{5,13},{9,1},{13,5},{2,10},{6,14},... | collective-permute-start | bytes 196616 | tf_op jit(solution)/shard_map/ppermute | solution.py:283
  51.4 5.2 %collective-permute-start.24 = (bf16[16,2048]{1,0:T(8,128)(2,1)S(1)}, bf16[16,2048]{1,0:T(8,128)(2,1)S(1)}, u32[]{:S(2)}, u32[]{:S(2)}) collective-permute-start(bf16[16,2048]{1,0:T(8,128)(2,1)S(1)} %get-tuple-element.76), channel_id=1, source_target_pairs={{0,4},{4,0},{8,12},{12,8},{1,5},{5,1},{9,13},{13,9},{2,6},{6,2},{1... | collective-permute-start | bytes 196616 | tf_op jit(solution)/shard_map/ppermute | solution.py:283

commit v14 on v13

--- a/solution.py
+++ b/solution.py
@@ -7,6 +7,7 @@
 
 EXPERTS = 128
 CORES = 2
+OUT_COST = 2000000000
 BACK_COST = 12000000000
 VMEM = 40 * 1024 * 1024
 F32 = jnp.float32
@@ -331,10 +332,11 @@
             bound(expert_out_kernel, groups, spread, capacity),
             [shape((spread * capacity, half))] * groups,
             (*hidden, out_own, out_sib),
+            cost=OUT_COST,
         )
     )
     (d_pre,) = call(
-        d_pre_kernel, [shape((slots, 2 * feed))], (*pre, *back), after=hidden[1:]
+        d_pre_kernel, [shape((slots, 2 * feed))], (*pre, *back), after=hidden[:1]
     )
     d_pre = (d_pre, *to_x([d_pre] * (spread - 1)))
     near, *far = call(

time: 58 us -> 56.2 us (0.969)
  waiting for transfers between devices: 18.4 us -> 15.5 us
  starting transfers between devices: 29.6 us -> 30.8 us
    ppermute x8, waiting for transfers between devices: 12.3 us -> 10.3 us  [to_x(): lax.ppermute(value, 'fsdp', [(i, i ^ (k + 1) * CORES) for i in range(part...]
    ppermute x8, starting transfers between devices: 11.2 us -> 12.4 us  [to_x(): lax.ppermute(value, 'fsdp', [(i, i ^ (k + 1) * CORES) for i in range(part...]
    ppermute x12, waiting for transfers between devices: 6.15 us -> 5.13 us  [to_expert(): lax.ppermute(value, 'expert', [(i, i ^ ke) for i in range(groups)])]
  transfers between devices with their start and end apart: 25 -> 25, of which waited for: 10 -> 10; matrix products, arithmetic and copies ran while one was open for 0% -> 0% of each run, Pallas kernels for 13% -> 14%
where the time goes in v14:
time: 56.2 us; the launch traced here: 56 us
  starting transfers between devices  30.8 us (55%)
  waiting for transfers between devices  15.5 us (28%)
  Pallas kernels  8.98 us (16%)
  between operations  0.76 us (1%)
    ppermute x12, starting transfers between devices, to_expert(): lax.ppermute(value, 'expert', [(i, i ^ ke) for i in range(groups)])  17.3 us
    ppermute x8, starting transfers between devices, to_x(): lax.ppermute(value, 'fsdp', [(i, i ^ (k + 1) * CORES) for i in range(part...  12.4 us
    ppermute x8, waiting for transfers between devices, to_x(): lax.ppermute(value, 'fsdp', [(i, i ^ (k + 1) * CORES) for i in range(part...  10.3 us
    pallas_call x14, Pallas kernels, call(): pl.pallas_call(kernel, out_shape=out_shape, in_specs=specs, compiler_para...  8.98 us
    ppermute x12, waiting for transfers between devices, to_expert(): lax.ppermute(value, 'expert', [(i, i ^ ke) for i in range(groups)])  5.13 us
  transfers between devices with their start and end apart: 25, of which 10 were waited for; matrix products, arithmetic and copies ran while one was open for 0% of the time, Pallas kernels for 14%

profile of v14, /device:TPU:0, one launch (start us, length us, event | category | flops | bytes accessed | tf_op | source)
XLA Modules:
  0.0 56.0 jit_solution(12956356003316787786)
XLA Ops:
  0.6 0.5 collective-permute-start.1
  1.2 0.1 collective-permute-start.2
  1.2 1.9 %shard_map.94 = (bf16[64,1024]{1,0:T(8,128)(2,1)S(1)}, bf16[64,1024]{1,0:T(8,128)(2,1)S(1)}, bf16[64,1024]{1,0:T(8,128)(2,1)S(1)}, bf16[64,1024]{1,0:T(8,128)(2,...) custom-call(s32[8,256]{1,0:T(8,128)} %bitcast.11, f32[8,256]{1,0:T(8,128)} %bitcast.12, s32[1,256]{1,0:T(1,128)} %refs_2_.1, ...), custom_call_target="tpu_custom_call" | custom-call | tf_op jit(solution)/shard_map/pallas_call | solution.py:40
  3.2 3.0 %collective-permute-start = (bf16[64,1024]{1,0:T(8,128)(2,1)S(1)}, bf16[64,1024]{1,0:T(8,128)(2,1)S(1)}, u32[]{:S(2)}, u32[]{:S(2)}) collective-permute-start(bf16[64,1024]{1,0:T(8,128)(2,1)S(1)} %get-tuple-element.44), channel_id=1, source_target_pairs={{0,2},{1,3},{2,0},{3,1},{4,6},{5,7},{6,4},{7,5},{8,10},{9,11},{10,... | collective-permute-start | bytes 393224 | tf_op jit(solution)/shard_map/ppermute | solution.py:278
  6.2 0.1 collective-permute-start.12
  6.2 4.2 %collective-permute-done.refs_1_ = bf16[64,1024]{1,0:T(8,128)(2,1)S(1)} collective-permute-done((bf16[64,1024]{1,0:T(8,128)(2,1)S(1)}, bf16[64,1024]{1,0:T(8,128)(2,1)S(1)}, u32[]{:S(2)}, u32[]{:S(2)}) %collective-permute-start) | collective-permute-done | bytes 131104 | tf_op jit(solution)/shard_map/ppermute | solution.py:278
  10.5 0.0 collective-permute-done.2.refs_3_.refs_5_
  10.5 0.0 collective-permute-done.1.refs_5_.refs_3_
  10.5 4.2 %collective-permute-start.3 = (bf16[16,2048]{1,0:T(8,128)(2,1)S(1)}, bf16[16,2048]{1,0:T(8,128)(2,1)S(1)}, u32[]{:S(2)}, u32[]{:S(2)}) collective-permute-start(bf16[16,2048]{1,0:T(8,128)(2,1)S(1)} %get-tuple-element.48), channel_id=1, source_target_pairs={{0,12},{4,8},{8,4},{12,0},{1,13},{5,9},{9,5},{13,1},{2,14},{6,10},... | collective-permute-start | bytes 196616 | tf_op jit(solution)/shard_map/ppermute | solution.py:284
  14.7 0.0 collective-permute-start.4
  14.7 0.6 %collective-permute-start.5 = (bf16[16,2048]{1,0:T(8,128)(2,1)S(1)}, bf16[16,2048]{1,0:T(8,128)(2,1)S(1)}, u32[]{:S(2)}, u32[]{:S(2)}) collective-permute-start(bf16[16,2048]{1,0:T(8,128)(2,1)S(1)} %get-tuple-element.50), channel_id=1, source_target_pairs={{0,4},{4,0},{8,12},{12,8},{1,5},{5,1},{9,13},{13,9},{2,6},{6,2},{1... | collective-permute-start | bytes 196616 | tf_op jit(solution)/shard_map/ppermute | solution.py:284
  15.4 0.0 collective-permute-done.12.refs_1_
  15.4 3.8 %collective-permute-start.13 = (bf16[16,2048]{1,0:T(8,128)(2,1)S(1)}, bf16[16,2048]{1,0:T(8,128)(2,1)S(1)}, u32[]{:S(2)}, u32[]{:S(2)}) collective-permute-start(bf16[16,2048]{1,0:T(8,128)(2,1)S(1)} %get-tuple-element.62), channel_id=1, source_target_pairs={{0,12},{4,8},{8,4},{12,0},{1,13},{5,9},{9,5},{13,1},{2,14},{6,10},... | collective-permute-start | bytes 196616 | tf_op jit(solution)/shard_map/ppermute | solution.py:284
  19.2 0.0 collective-permute-done.3.refs_1_
  19.2 0.6 %collective-permute-start.15 = (bf16[16,2048]{1,0:T(8,128)(2,1)S(1)}, bf16[16,2048]{1,0:T(8,128)(2,1)S(1)}, u32[]{:S(2)}, u32[]{:S(2)}) collective-permute-start(bf16[16,2048]{1,0:T(8,128)(2,1)S(1)} %get-tuple-element.64), channel_id=1, source_target_pairs={{0,4},{4,0},{8,12},{12,8},{1,5},{5,1},{9,13},{13,9},{2,6},{6,2},{1... | collective-permute-start | bytes 196616 | tf_op jit(solution)/shard_map/ppermute | solution.py:284
  19.8 2.2 %collective-permute-done.4.refs_2_ = bf16[16,2048]{1,0:T(8,128)(2,1)S(1)} collective-permute-done((bf16[16,2048]{1,0:T(8,128)(2,1)S(1)}, bf16[16,2048]{1,0:T(8,128)(2,1)S(1)}, u32[]{:S(2)}, u32[]{:S(2)}) %collective-permute-start.4) | collective-permute-done | bytes 65568 | tf_op jit(solution)/shard_map/ppermute | solution.py:284
  22.1 0.6 %shard_map.96 = (f32[64,1536]{1,0:T(8,128)S(1)}, bf16[64,1536]{1,0:T(8,128)(2,1)S(1)}) custom-call(bf16[16,2048]{1,0:T(8,128)(2,1)S(1)} %get-tuple-element.47.refs_0_, bf16[16,2048]{1,0:T(8,128)(2,1)S(1)} %collective-permute-done.3.refs_1_, bf16[16,2048]{1,0:T(8,128)(2,1)S(1)} %collective-permute-done.4.refs_2_, ...), custom_call_target="tpu_custom_call" | custom-call | tf_op jit(solution)/shard_map/pallas_call | solution.py:40
  22.6 1.6 %collective-permute-start.6 = (bf16[64,1536]{1,0:T(8,128)(2,1)S(1)}, bf16[64,1536]{1,0:T(8,128)(2,1)S(1)}, u32[]{:S(2)}, u32[]{:S(2)}) collective-permute-start(bf16[64,1536]{1,0:T(8,128)(2,1)S(1)} %get-tuple-element.53), channel_id=1, source_target_pairs={{0,2},{1,3},{2,0},{3,1},{4,6},{5,7},{6,4},{7,5},{8,10},{9,11},{10,... | collective-permute-start | bytes 589832 | tf_op jit(solution)/shard_map/ppermute | solution.py:278
  24.2 0.0 collective-permute-done.13.refs_1_
  24.2 0.9 %collective-permute-done.14.refs_2_ = bf16[16,2048]{1,0:T(8,128)(2,1)S(1)} collective-permute-done((bf16[16,2048]{1,0:T(8,128)(2,1)S(1)}, bf16[16,2048]{1,0:T(8,128)(2,1)S(1)}, u32[]{:S(2)}, u32[]{:S(2)}) %collective-permute-start.14) | collective-permute-done | bytes 65568 | tf_op jit(solution)/shard_map/ppermute | solution.py:284
  25.1 0.0 collective-permute-done.15.refs_3_
  25.1 0.4 shard_map.101
  25.5 1.6 %collective-permute-start.19 = (bf16[64,768]{1,0:T(8,128)(2,1)S(1)}, bf16[64,768]{1,0:T(8,128)(2,1)S(1)}, u32[]{:S(2)}, u32[]{:S(2)}) collective-permute-start(bf16[64,768]{1,0:T(8,128)(2,1)S(1)} %get-tuple-element.70), channel_id=1, source_target_pairs={{0,2},{1,3},{2,0},{3,1},{4,6},{5,7},{6,4},{7,5},{8,10},{9,11},{10,... | collective-permute-start | bytes 294920 | tf_op jit(solution)/shard_map/ppermute | solution.py:278
  27.1 2.7 %collective-permute-done.6.refs_1_ = bf16[64,1536]{1,0:T(8,128)(2,1)S(1)} collective-permute-done((bf16[64,1536]{1,0:T(8,128)(2,1)S(1)}, bf16[64,1536]{1,0:T(8,128)(2,1)S(1)}, u32[]{:S(2)}, u32[]{:S(2)}) %collective-permute-start.6) | collective-permute-done | bytes 196640 | tf_op jit(solution)/shard_map/ppermute | solution.py:278
  29.7 0.1 shard_map.97.refs_0_.refs_2_.refs_4_
  29.8 1.6 %collective-permute-start.7 = (bf16[64,768]{1,0:T(8,128)(2,1)S(1)}, bf16[64,768]{1,0:T(8,128)(2,1)S(1)}, u32[]{:S(2)}, u32[]{:S(2)}) collective-permute-start(bf16[64,768]{1,0:T(8,128)(2,1)S(1)} %shard_map.97.refs_0_.refs_2_.refs_4_), channel_id=1, source_target_pairs={{0,2},{1,3},{2,0},{3,1},{4,6},{5,7},{6,4},{7,5},{8,10},{9,11},{10,... | collective-permute-start | bytes 294920 | tf_op jit(solution)/shard_map/ppermute | solution.py:278
  31.4 0.2 collective-permute-done.19.refs_3_
  31.5 0.1 shard_map.104.refs_0_
  31.7 1.6 %collective-permute-start.20 = (bf16[64,1536]{1,0:T(8,128)(2,1)S(1)}, bf16[64,1536]{1,0:T(8,128)(2,1)S(1)}, u32[]{:S(2)}, u32[]{:S(2)}) collective-permute-start(bf16[64,1536]{1,0:T(8,128)(2,1)S(1)} %shard_map.104.refs_0_), channel_id=1, source_target_pairs={{0,2},{1,3},{2,0},{3,1},{4,6},{5,7},{6,4},{7,5},{8,10},{9,11},{10,... | collective-permute-start | bytes 589832 | tf_op jit(solution)/shard_map/ppermute | solution.py:278
  33.2 2.0 %collective-permute-done.7.refs_1_.refs_3_ = bf16[64,768]{1,0:T(8,128)(2,1)S(1)} collective-permute-done((bf16[64,768]{1,0:T(8,128)(2,1)S(1)}, bf16[64,768]{1,0:T(8,128)(2,1)S(1)}, u32[]{:S(2)}, u32[]{:S(2)}) %collective-permute-start.7) | collective-permute-done | bytes 98336 | tf_op jit(solution)/shard_map/ppermute | solution.py:278
  35.2 0.6 %shard_map.98 = (bf16[32,1024]{1,0:T(8,128)(2,1)S(1)}, bf16[32,1024]{1,0:T(8,128)(2,1)S(1)}, bf16[32,1024]{1,0:T(8,128)(2,1)S(1)}, bf16[32,1024]{1,0:T(8,128)(2,1)S(1)}) custom-call(bf16[64,768]{1,0:T(8,128)(2,1)S(1)} %shard_map.97.refs_0_.refs_2_.refs_4_, bf16[64,768]{1,0:T(8,128)(2,1)S(1)} %collective-permute-done.7.refs_1_.refs_3_, ...), custom_call_target="tpu_custom_call" | custom-call | flops 2000000000 | tf_op jit(solution)/shard_map/pallas_call | solution.py:40
  35.8 0.1 collective-permute-start.10
  35.9 1.7 %collective-permute-start.8 = (bf16[32,1024]{1,0:T(8,128)(2,1)S(1)}, bf16[32,1024]{1,0:T(8,128)(2,1)S(1)}, u32[]{:S(2)}, u32[]{:S(2)}) collective-permute-start(bf16[32,1024]{1,0:T(8,128)(2,1)S(1)} %get-tuple-element.56), channel_id=1, source_target_pairs={{0,12},{4,8},{8,4},{12,0},{1,13},{5,9},{9,5},{13,1},{2,14},{6,10},... | collective-permute-start | bytes 196616 | tf_op jit(solution)/shard_map/ppermute | solution.py:284
  37.6 1.8 %collective-permute-start.9 = (bf16[32,1024]{1,0:T(8,128)(2,1)S(1)}, bf16[32,1024]{1,0:T(8,128)(2,1)S(1)}, u32[]{:S(2)}, u32[]{:S(2)}) collective-permute-start(bf16[32,1024]{1,0:T(8,128)(2,1)S(1)} %get-tuple-element.57), channel_id=1, source_target_pairs={{0,8},{4,12},{8,0},{12,4},{1,9},{5,13},{9,1},{13,5},{2,10},{6,14},... | collective-permute-start | bytes 196616 | tf_op jit(solution)/shard_map/ppermute | solution.py:284
  39.4 0.8 %collective-permute-done.10.refs_3_.refs_5_.refs_4_ = bf16[32,1024]{1,0:T(8,128)(2,1)S(1)} collective-permute-done((bf16[32,1024]{1,0:T(8,128)(2,1)S(1)}, bf16[32,1024]{1,0:T(8,128)(2,1)S(1)}, u32[]{:S(2)}, u32[]{:S(2)}) %collective-permute-start.10) | collective-permute-done | bytes 65568 | tf_op jit(solution)/shard_map/ppermute | solution.py:284
  40.2 1.1 %shard_map.105 = (bf16[64,1024]{1,0:T(8,128)(2,1)S(1)}, bf16[64,1024]{1,0:T(8,128)(2,1)S(1)}) custom-call(bf16[64,1536]{1,0:T(8,128)(2,1)S(1)} %shard_map.104.refs_0_, bf16[64,1536]{1,0:T(8,128)(2,1)S(1)} %collective-permute-done.20.refs_1_, bf16[512,1536]{1,0:T(8,128)(2,1)S(1)} %bitcast.7, bf16[512,1536]{1,0:T(8,128)(2,1)S(1)} %collective-permute-done.1.refs_5_.refs_3_, ...), custom_call_target="tpu_custom_call" | custom-call | tf_op jit(solution)/shard_map/pallas_call | solution.py:40
  41.3 1.5 %collective-permute-start.21 = (bf16[64,1024]{1,0:T(8,128)(2,1)S(1)}, bf16[64,1024]{1,0:T(8,128)(2,1)S(1)}, u32[]{:S(2)}, u32[]{:S(2)}) collective-permute-start(bf16[64,1024]{1,0:T(8,128)(2,1)S(1)} %get-tuple-element.72), channel_id=1, source_target_pairs={{0,2},{1,3},{2,0},{3,1},{4,6},{5,7},{6,4},{7,5},{8,10},{9,11},{10,... | collective-permute-start | bytes 393224 | tf_op jit(solution)/shard_map/ppermute | solution.py:278
  42.8 0.5 collective-permute-start.17
  43.4 0.4 collective-permute-done.9.refs_2_.refs_4_
  43.7 1.5 %collective-permute-start.11 = (bf16[64,1024]{1,0:T(8,128)(2,1)S(1)}, bf16[64,1024]{1,0:T(8,128)(2,1)S(1)}, u32[]{:S(2)}, u32[]{:S(2)}) collective-permute-start(bf16[64,1024]{1,0:T(8,128)(2,1)S(1)} %shard_map.99), channel_id=1, source_target_pairs={{0,2},{1,3},{2,0},{3,1},{4,6},{5,7},{6,4},{7,5},{8,10},{9,11},{10,... | collective-permute-start | bytes 393224 | tf_op jit(solution)/shard_map/ppermute | solution.py:278
  45.3 1.3 %collective-permute-done.21.refs_1_ = bf16[64,1024]{1,0:T(8,128)(2,1)S(1)} collective-permute-done((bf16[64,1024]{1,0:T(8,128)(2,1)S(1)}, bf16[64,1024]{1,0:T(8,128)(2,1)S(1)}, u32[]{:S(2)}, u32[]{:S(2)}) %collective-permute-start.21) | collective-permute-done | bytes 131104 | tf_op jit(solution)/shard_map/ppermute | solution.py:278
  46.6 1.7 %collective-permute-start.22 = (bf16[16,2048]{1,0:T(8,128)(2,1)S(1)}, bf16[16,2048]{1,0:T(8,128)(2,1)S(1)}, u32[]{:S(2)}, u32[]{:S(2)}) collective-permute-start(bf16[16,2048]{1,0:T(8,128)(2,1)S(1)} %get-tuple-element.74), channel_id=1, source_target_pairs={{0,12},{4,8},{8,4},{12,0},{1,13},{5,9},{9,5},{13,1},{2,14},{6,10},... | collective-permute-start | bytes 196616 | tf_op jit(solution)/shard_map/ppermute | solution.py:284
  48.3 0.0 collective-permute-start.23
  48.4 2.7 %collective-permute-start.24 = (bf16[16,2048]{1,0:T(8,128)(2,1)S(1)}, bf16[16,2048]{1,0:T(8,128)(2,1)S(1)}, u32[]{:S(2)}, u32[]{:S(2)}) collective-permute-start(bf16[16,2048]{1,0:T(8,128)(2,1)S(1)} %get-tuple-element.76), channel_id=1, source_target_pairs={{0,4},{4,0},{8,12},{12,8},{1,5},{5,1},{9,13},{13,9},{2,6},{6,2},{1... | collective-permute-start | bytes 196616 | tf_op jit(solution)/shard_map/ppermute | solution.py:284
  51.1 1.6 %shard_map.102 = (f32[512,768]{1,0:T(8,128)}, f32[8,128]{1,0:T(8,128)S(1)}) custom-call(bf16[128,512]{1,0:T(8,128)(2,1)S(1)} %get-tuple-element.65.refs_0_, bf16[128,512]{1,0:T(8,128)(2,1)S(1)} %collective-permute-done.16.refs_1_, bf16[64,768]{1,0:T(8,128)(2,1)S(1)} %shard_map.97.refs_0_.refs_2_.refs_4_, ...), custom_call_target="tpu_custom_call" | custom-call | tf_op jit(solution)/shard_map/pallas_call | solution.py:40
  52.6 1.3 %shard_map.103 = (bf16[256,2048]{1,0:T(8,128)(2,1)}, f32[8,128]{1,0:T(8,128)S(1)}) custom-call(bf16[256,64]{1,0:T(8,128)(2,1)S(1)} %get-tuple-element.41.refs_0_, f32[64,128]{1,0:T(8,128)S(1)} %get-tuple-element.42.refs_1_, bf16[32,1024]{1,0:T(8,128)(2,1)S(1)} %get-tuple-element.55.refs_0_.refs_2_, ...), custom_call_target="tpu_custom_call" | custom-call | tf_op jit(solution)/shard_map/pallas_call | solution.py:40
  54.0 0.9 %collective-permute-done.23.refs_3_ = bf16[16,2048]{1,0:T(8,128)(2,1)S(1)} collective-permute-done((bf16[16,2048]{1,0:T(8,128)(2,1)S(1)}, bf16[16,2048]{1,0:T(8,128)(2,1)S(1)}, u32[]{:S(2)}, u32[]{:S(2)}) %collective-permute-start.23) | collective-permute-done | bytes 65568 | tf_op jit(solution)/shard_map/ppermute | solution.py:284
  54.8 1.2 %shard_map.107 = bf16[256,2048]{1,0:T(8,128)(2,1)} custom-call(bf16[256,64]{1,0:T(8,128)(2,1)S(1)} %get-tuple-element.41.refs_0_, bf16[16,2048]{1,0:T(8,128)(2,1)S(1)} %get-tuple-element.73.refs_1_, bf16[16,2048]{1,0:T(8,128)(2,1)S(1)} %collective-permute-done.22.refs_2_, bf16[16,2048]{1,0:T(8,128)(2,1)S(1)} %collective-permute-done.23.refs_3_, ...), custom_call_target="tpu_custom_call" | custom-call | tf_op jit(solution)/shard_map/pallas_call | solution.py:40
  (20 shorter events, 0.1 us)
Async XLA Ops:
  0.6 21.4 %copy-start = (bf16[1,512,1536]{2,1,0:T(8,128)(2,1)S(1)}, bf16[1,512,1536]{2,1,0:T(8,128)(2,1)}, u32[]{:S(2)}) copy-start(bf16[1,512,1536]{2,1,0:T(8,128)(2,1)} %param.12) | copy-start | bytes 4718596
  0.6 9.8 %collective-permute-start.1 = (bf16[512,1536]{1,0:T(8,128)(2,1)}, bf16[512,1536]{1,0:T(8,128)(2,1)S(1)}, u32[]{:S(2)}, u32[]{:S(2)}) collective-permute-start(bf16[512,1536]{1,0:T(8,128)(2,1)} %bitcast.5), channel_id=1, source_target_pairs={{0,1},{1,0},{2,3},{3,2},{4,5},{5,4},{6,7},{7,6},{8,9},{9,8},{10,11... | collective-permute-start | bytes 4718600 | tf_op jit(solution)/shard_map/ppermute | solution.py:274
  1.2 9.3 %collective-permute-start.2 = (bf16[512,768]{1,0:T(8,128)(2,1)}, bf16[512,768]{1,0:T(8,128)(2,1)S(1)}, u32[]{:S(2)}, u32[]{:S(2)}) collective-permute-start(bf16[512,768]{1,0:T(8,128)(2,1)} %bitcast.8), channel_id=1, source_target_pairs={{0,1},{1,0},{2,3},{3,2},{4,5},{5,4},{6,7},{7,6},{8,9},{9,8},{10,11... | collective-permute-start | bytes 2359304 | tf_op jit(solution)/shard_map/ppermute | solution.py:274
  3.2 7.3 %collective-permute-start = (bf16[64,1024]{1,0:T(8,128)(2,1)S(1)}, bf16[64,1024]{1,0:T(8,128)(2,1)S(1)}, u32[]{:S(2)}, u32[]{:S(2)}) collective-permute-start(bf16[64,1024]{1,0:T(8,128)(2,1)S(1)} %get-tuple-element.44), channel_id=1, source_target_pairs={{0,2},{1,3},{2,0},{3,1},{4,6},{5,7},{6,4},{7,5},{8,10},{9,11},{10,... | collective-permute-start | bytes 393224 | tf_op jit(solution)/shard_map/ppermute | solution.py:278
  6.2 9.2 %collective-permute-start.12 = (bf16[64,1024]{1,0:T(8,128)(2,1)S(1)}, bf16[64,1024]{1,0:T(8,128)(2,1)S(1)}, u32[]{:S(2)}, u32[]{:S(2)}) collective-permute-start(bf16[64,1024]{1,0:T(8,128)(2,1)S(1)} %get-tuple-element.60), channel_id=1, source_target_pairs={{0,2},{1,3},{2,0},{3,1},{4,6},{5,7},{6,4},{7,5},{8,10},{9,11},{10,... | collective-permute-start | bytes 393224 | tf_op jit(solution)/shard_map/ppermute | solution.py:278
  10.5 8.7 %collective-permute-start.3 = (bf16[16,2048]{1,0:T(8,128)(2,1)S(1)}, bf16[16,2048]{1,0:T(8,128)(2,1)S(1)}, u32[]{:S(2)}, u32[]{:S(2)}) collective-permute-start(bf16[16,2048]{1,0:T(8,128)(2,1)S(1)} %get-tuple-element.48), channel_id=1, source_target_pairs={{0,12},{4,8},{8,4},{12,0},{1,13},{5,9},{9,5},{13,1},{2,14},{6,10},... | collective-permute-start | bytes 196616 | tf_op jit(solution)/shard_map/ppermute | solution.py:284
  14.7 7.3 %collective-permute-start.4 = (bf16[16,2048]{1,0:T(8,128)(2,1)S(1)}, bf16[16,2048]{1,0:T(8,128)(2,1)S(1)}, u32[]{:S(2)}, u32[]{:S(2)}) collective-permute-start(bf16[16,2048]{1,0:T(8,128)(2,1)S(1)} %get-tuple-element.49), channel_id=1, source_target_pairs={{0,8},{4,12},{8,0},{12,4},{1,9},{5,13},{9,1},{13,5},{2,10},{6,14},... | collective-permute-start | bytes 196616 | tf_op jit(solution)/shard_map/ppermute | solution.py:284
  14.7 7.3 %collective-permute-start.5 = (bf16[16,2048]{1,0:T(8,128)(2,1)S(1)}, bf16[16,2048]{1,0:T(8,128)(2,1)S(1)}, u32[]{:S(2)}, u32[]{:S(2)}) collective-permute-start(bf16[16,2048]{1,0:T(8,128)(2,1)S(1)} %get-tuple-element.50), channel_id=1, source_target_pairs={{0,4},{4,0},{8,12},{12,8},{1,5},{5,1},{9,13},{13,9},{2,6},{6,2},{1... | collective-permute-start | bytes 196616 | tf_op jit(solution)/shard_map/ppermute | solution.py:284
  15.4 8.8 %collective-permute-start.13 = (bf16[16,2048]{1,0:T(8,128)(2,1)S(1)}, bf16[16,2048]{1,0:T(8,128)(2,1)S(1)}, u32[]{:S(2)}, u32[]{:S(2)}) collective-permute-start(bf16[16,2048]{1,0:T(8,128)(2,1)S(1)} %get-tuple-element.62), channel_id=1, source_target_pairs={{0,12},{4,8},{8,4},{12,0},{1,13},{5,9},{9,5},{13,1},{2,14},{6,10},... | collective-permute-start | bytes 196616 | tf_op jit(solution)/shard_map/ppermute | solution.py:284
  19.2 5.9 %collective-permute-start.14 = (bf16[16,2048]{1,0:T(8,128)(2,1)S(1)}, bf16[16,2048]{1,0:T(8,128)(2,1)S(1)}, u32[]{:S(2)}, u32[]{:S(2)}) collective-permute-start(bf16[16,2048]{1,0:T(8,128)(2,1)S(1)} %get-tuple-element.63), channel_id=1, source_target_pairs={{0,8},{4,12},{8,0},{12,4},{1,9},{5,13},{9,1},{13,5},{2,10},{6,14},... | collective-permute-start | bytes 196616 | tf_op jit(solution)/shard_map/ppermute | solution.py:284
  19.2 5.9 %collective-permute-start.15 = (bf16[16,2048]{1,0:T(8,128)(2,1)S(1)}, bf16[16,2048]{1,0:T(8,128)(2,1)S(1)}, u32[]{:S(2)}, u32[]{:S(2)}) collective-permute-start(bf16[16,2048]{1,0:T(8,128)(2,1)S(1)} %get-tuple-element.64), channel_id=1, source_target_pairs={{0,4},{4,0},{8,12},{12,8},{1,5},{5,1},{9,13},{13,9},{2,6},{6,2},{1... | collective-permute-start | bytes 196616 | tf_op jit(solution)/shard_map/ppermute | solution.py:284
  22.0 3.1 %copy-start.1 = (bf16[1,512,768]{2,1,0:T(8,128)(2,1)S(1)}, bf16[1,512,768]{2,1,0:T(8,128)(2,1)}, u32[]{:S(2)}) copy-start(bf16[1,512,768]{2,1,0:T(8,128)(2,1)} %param.13) | copy-start | bytes 2359300
  22.6 7.1 %collective-permute-start.6 = (bf16[64,1536]{1,0:T(8,128)(2,1)S(1)}, bf16[64,1536]{1,0:T(8,128)(2,1)S(1)}, u32[]{:S(2)}, u32[]{:S(2)}) collective-permute-start(bf16[64,1536]{1,0:T(8,128)(2,1)S(1)} %get-tuple-element.53), channel_id=1, source_target_pairs={{0,2},{1,3},{2,0},{3,1},{4,6},{5,7},{6,4},{7,5},{8,10},{9,11},{10,... | collective-permute-start | bytes 589832 | tf_op jit(solution)/shard_map/ppermute | solution.py:278
  25.5 6.0 %collective-permute-start.19 = (bf16[64,768]{1,0:T(8,128)(2,1)S(1)}, bf16[64,768]{1,0:T(8,128)(2,1)S(1)}, u32[]{:S(2)}, u32[]{:S(2)}) collective-permute-start(bf16[64,768]{1,0:T(8,128)(2,1)S(1)} %get-tuple-element.70), channel_id=1, source_target_pairs={{0,2},{1,3},{2,0},{3,1},{4,6},{5,7},{6,4},{7,5},{8,10},{9,11},{10,... | collective-permute-start | bytes 294920 | tf_op jit(solution)/shard_map/ppermute | solution.py:278
  29.8 5.4 %collective-permute-start.7 = (bf16[64,768]{1,0:T(8,128)(2,1)S(1)}, bf16[64,768]{1,0:T(8,128)(2,1)S(1)}, u32[]{:S(2)}, u32[]{:S(2)}) collective-permute-start(bf16[64,768]{1,0:T(8,128)(2,1)S(1)} %shard_map.97.refs_0_.refs_2_.refs_4_), channel_id=1, source_target_pairs={{0,2},{1,3},{2,0},{3,1},{4,6},{5,7},{6,4},{7,5},{8,10},{9,11},{10,... | collective-permute-start | bytes 294920 | tf_op jit(solution)/shard_map/ppermute | solution.py:278
  31.7 8.5 %collective-permute-start.20 = (bf16[64,1536]{1,0:T(8,128)(2,1)S(1)}, bf16[64,1536]{1,0:T(8,128)(2,1)S(1)}, u32[]{:S(2)}, u32[]{:S(2)}) collective-permute-start(bf16[64,1536]{1,0:T(8,128)(2,1)S(1)} %shard_map.104.refs_0_), channel_id=1, source_target_pairs={{0,2},{1,3},{2,0},{3,1},{4,6},{5,7},{6,4},{7,5},{8,10},{9,11},{10,... | collective-permute-start | bytes 589832 | tf_op jit(solution)/shard_map/ppermute | solution.py:278
  35.8 4.3 %collective-permute-start.10 = (bf16[32,1024]{1,0:T(8,128)(2,1)S(1)}, bf16[32,1024]{1,0:T(8,128)(2,1)S(1)}, u32[]{:S(2)}, u32[]{:S(2)}) collective-permute-start(bf16[32,1024]{1,0:T(8,128)(2,1)S(1)} %get-tuple-element.58), channel_id=1, source_target_pairs={{0,4},{4,0},{8,12},{12,8},{1,5},{5,1},{9,13},{13,9},{2,6},{6,2},{1... | collective-permute-start | bytes 196616 | tf_op jit(solution)/shard_map/ppermute | solution.py:284
  35.9 7.5 %collective-permute-start.8 = (bf16[32,1024]{1,0:T(8,128)(2,1)S(1)}, bf16[32,1024]{1,0:T(8,128)(2,1)S(1)}, u32[]{:S(2)}, u32[]{:S(2)}) collective-permute-start(bf16[32,1024]{1,0:T(8,128)(2,1)S(1)} %get-tuple-element.56), channel_id=1, source_target_pairs={{0,12},{4,8},{8,4},{12,0},{1,13},{5,9},{9,5},{13,1},{2,14},{6,10},... | collective-permute-start | bytes 196616 | tf_op jit(solution)/shard_map/ppermute | solution.py:284
  37.6 6.1 %collective-permute-start.9 = (bf16[32,1024]{1,0:T(8,128)(2,1)S(1)}, bf16[32,1024]{1,0:T(8,128)(2,1)S(1)}, u32[]{:S(2)}, u32[]{:S(2)}) collective-permute-start(bf16[32,1024]{1,0:T(8,128)(2,1)S(1)} %get-tuple-element.57), channel_id=1, source_target_pairs={{0,8},{4,12},{8,0},{12,4},{1,9},{5,13},{9,1},{13,5},{2,10},{6,14},... | collective-permute-start | bytes 196616 | tf_op jit(solution)/shard_map/ppermute | solution.py:284
  41.3 5.3 %collective-permute-start.21 = (bf16[64,1024]{1,0:T(8,128)(2,1)S(1)}, bf16[64,1024]{1,0:T(8,128)(2,1)S(1)}, u32[]{:S(2)}, u32[]{:S(2)}) collective-permute-start(bf16[64,1024]{1,0:T(8,128)(2,1)S(1)} %get-tuple-element.72), channel_id=1, source_target_pairs={{0,2},{1,3},{2,0},{3,1},{4,6},{5,7},{6,4},{7,5},{8,10},{9,11},{10,... | collective-permute-start | bytes 393224 | tf_op jit(solution)/shard_map/ppermute | solution.py:278
  42.8 5.5 %collective-permute-start.16 = (bf16[128,512]{1,0:T(8,128)(2,1)S(1)}, bf16[128,512]{1,0:T(8,128)(2,1)S(1)}, u32[]{:S(2)}, u32[]{:S(2)}) collective-permute-start(bf16[128,512]{1,0:T(8,128)(2,1)S(1)} %get-tuple-element.66), channel_id=1, source_target_pairs={{0,1},{1,0},{2,3},{3,2},{4,5},{5,4},{6,7},{7,6},{8,9},{9,8},{10,11... | collective-permute-start | bytes 393224 | tf_op jit(solution)/shard_map/ppermute | solution.py:274
  42.8 5.5 %collective-permute-start.17 = (bf16[64,768]{1,0:T(8,128)(2,1)S(1)}, bf16[64,768]{1,0:T(8,128)(2,1)S(1)}, u32[]{:S(2)}, u32[]{:S(2)}) collective-permute-start(bf16[64,768]{1,0:T(8,128)(2,1)S(1)} %shard_map.97.refs_0_.refs_2_.refs_4_), channel_id=1, source_target_pairs={{0,1},{1,0},{2,3},{3,2},{4,5},{5,4},{6,7},{7,6},{8,9},{9,8},{10,11... | collective-permute-start | bytes 294920 | tf_op jit(solution)/shard_map/ppermute | solution.py:274
  43.7 8.9 %collective-permute-start.11 = (bf16[64,1024]{1,0:T(8,128)(2,1)S(1)}, bf16[64,1024]{1,0:T(8,128)(2,1)S(1)}, u32[]{:S(2)}, u32[]{:S(2)}) collective-permute-start(bf16[64,1024]{1,0:T(8,128)(2,1)S(1)} %shard_map.99), channel_id=1, source_target_pairs={{0,2},{1,3},{2,0},{3,1},{4,6},{5,7},{6,4},{7,5},{8,10},{9,11},{10,... | collective-permute-start | bytes 393224 | tf_op jit(solution)/shard_map/ppermute | solution.py:278
  45.3 5.8 %collective-permute-start.18 = (bf16[64,768]{1,0:T(8,128)(2,1)S(1)}, bf16[64,768]{1,0:T(8,128)(2,1)S(1)}, u32[]{:S(2)}, u32[]{:S(2)}) collective-permute-start(bf16[64,768]{1,0:T(8,128)(2,1)S(1)} %collective-permute-done.7.refs_1_.refs_3_), channel_id=1, source_target_pairs={{0,1},{1,0},{2,3},{3,2},{4,5},{5,4},{6,7},{7,6},{8,9},{9,8},{10,11... | collective-permute-start | bytes 294920 | tf_op jit(solution)/shard_map/ppermute | solution.py:274
  46.6 7.3 %collective-permute-start.22 = (bf16[16,2048]{1,0:T(8,128)(2,1)S(1)}, bf16[16,2048]{1,0:T(8,128)(2,1)S(1)}, u32[]{:S(2)}, u32[]{:S(2)}) collective-permute-start(bf16[16,2048]{1,0:T(8,128)(2,1)S(1)} %get-tuple-element.74), channel_id=1, source_target_pairs={{0,12},{4,8},{8,4},{12,0},{1,13},{5,9},{9,5},{13,1},{2,14},{6,10},... | collective-permute-start | bytes 196616 | tf_op jit(solution)/shard_map/ppermute | solution.py:284
  48.3 6.5 %collective-permute-start.23 = (bf16[16,2048]{1,0:T(8,128)(2,1)S(1)}, bf16[16,2048]{1,0:T(8,128)(2,1)S(1)}, u32[]{:S(2)}, u32[]{:S(2)}) collective-permute-start(bf16[16,2048]{1,0:T(8,128)(2,1)S(1)} %get-tuple-element.75), channel_id=1, source_target_pairs={{0,8},{4,12},{8,0},{12,4},{1,9},{5,13},{9,1},{13,5},{2,10},{6,14},... | collective-permute-start | bytes 196616 | tf_op jit(solution)/shard_map/ppermute | solution.py:284
  48.4 6.4 %collective-permute-start.24 = (bf16[16,2048]{1,0:T(8,128)(2,1)S(1)}, bf16[16,2048]{1,0:T(8,128)(2,1)S(1)}, u32[]{:S(2)}, u32[]{:S(2)}) collective-permute-start(bf16[16,2048]{1,0:T(8,128)(2,1)S(1)} %get-tuple-element.76), channel_id=1, source_target_pairs={{0,4},{4,0},{8,12},{12,8},{1,5},{5,1},{9,13},{13,9},{2,6},{6,2},{1... | collective-permute-start | bytes 196616 | tf_op jit(solution)/shard_map/ppermute | solution.py:284

commit v15 on v14

--- a/solution.py
+++ b/solution.py
@@ -340,7 +340,7 @@
     )
     d_pre = (d_pre, *to_x([d_pre] * (spread - 1)))
     near, *far = call(
-        bound(d_rows_kernel, spread), by_x, (*d_pre, in_own, in_sib), after=expert_out[1:2]
+        bound(d_rows_kernel, spread), by_x, (*d_pre, in_own, in_sib)
     )
     d_rows = to_expert(call(join, chunk, (near, *to_x(far))))
     far = to_x(

time: 56.2 us -> 56.1 us (level)
  waiting for transfers between devices: 15.5 us -> 14.6 us
  starting transfers between devices: 30.8 us -> 31.6 us
    ppermute x12, waiting for transfers between devices: 5.13 us -> 3.82 us  [to_expert(): lax.ppermute(value, 'expert', [(i, i ^ ke) for i in range(groups)])]
    ppermute x12, starting transfers between devices: 17.3 us -> 18.2 us  [to_expert(): lax.ppermute(value, 'expert', [(i, i ^ ke) for i in range(groups)])]
  transfers between devices with their start and end apart: 25 -> 25, of which waited for: 10 -> 8; matrix products, arithmetic and copies ran while one was open for 0% -> 0% of each run, Pallas kernels for 14% -> 14%
where the time goes in v15:
time: 56.1 us; the launch traced here: 55.9 us
  starting transfers between devices  31.6 us (56%)
  waiting for transfers between devices  14.6 us (26%)
  Pallas kernels  8.98 us (16%)
  between operations  0.75 us (1%)
    ppermute x12, starting transfers between devices, to_expert(): lax.ppermute(value, 'expert', [(i, i ^ ke) for i in range(groups)])  18.2 us
    ppermute x8, starting transfers between devices, to_x(): lax.ppermute(value, 'fsdp', [(i, i ^ (k + 1) * CORES) for i in range(part...  12.3 us
    ppermute x8, waiting for transfers between devices, to_x(): lax.ppermute(value, 'fsdp', [(i, i ^ (k + 1) * CORES) for i in range(part...  10.8 us
    pallas_call x14, Pallas kernels, call(): pl.pallas_call(kernel, out_shape=out_shape, in_specs=specs, compiler_para...  8.98 us
    ppermute x12, waiting for transfers between devices, to_expert(): lax.ppermute(value, 'expert', [(i, i ^ ke) for i in range(groups)])  3.82 us
  transfers between devices with their start and end apart: 25, of which 8 were waited for; matrix products, arithmetic and copies ran while one was open for 0% of the time, Pallas kernels for 14%

profile of v15, /device:TPU:0, one launch (start us, length us, event | category | flops | bytes accessed | tf_op | source)
XLA Modules:
  0.0 55.9 jit_solution(4525484637153846878)
XLA Ops:
  0.6 0.5 collective-permute-start.1
  1.2 0.1 collective-permute-start.2
  1.2 1.9 %shard_map.94 = (bf16[64,1024]{1,0:T(8,128)(2,1)S(1)}, bf16[64,1024]{1,0:T(8,128)(2,1)S(1)}, bf16[64,1024]{1,0:T(8,128)(2,1)S(1)}, bf16[64,1024]{1,0:T(8,128)(2,...) custom-call(s32[8,256]{1,0:T(8,128)} %bitcast.11, f32[8,256]{1,0:T(8,128)} %bitcast.12, s32[1,256]{1,0:T(1,128)} %refs_2_.1, ...), custom_call_target="tpu_custom_call" | custom-call | tf_op jit(solution)/shard_map/pallas_call | solution.py:40
  3.2 3.0 %collective-permute-start = (bf16[64,1024]{1,0:T(8,128)(2,1)S(1)}, bf16[64,1024]{1,0:T(8,128)(2,1)S(1)}, u32[]{:S(2)}, u32[]{:S(2)}) collective-permute-start(bf16[64,1024]{1,0:T(8,128)(2,1)S(1)} %get-tuple-element.44), channel_id=1, source_target_pairs={{0,2},{1,3},{2,0},{3,1},{4,6},{5,7},{6,4},{7,5},{8,10},{9,11},{10,... | collective-permute-start | bytes 393224 | tf_op jit(solution)/shard_map/ppermute | solution.py:278
  6.2 0.1 collective-permute-start.12
  6.2 4.2 %collective-permute-done.refs_1_ = bf16[64,1024]{1,0:T(8,128)(2,1)S(1)} collective-permute-done((bf16[64,1024]{1,0:T(8,128)(2,1)S(1)}, bf16[64,1024]{1,0:T(8,128)(2,1)S(1)}, u32[]{:S(2)}, u32[]{:S(2)}) %collective-permute-start) | collective-permute-done | bytes 131104 | tf_op jit(solution)/shard_map/ppermute | solution.py:278
  10.5 0.0 collective-permute-done.2.refs_3_.refs_5_
  10.5 0.0 collective-permute-done.1.refs_5_.refs_3_
  10.5 4.2 %collective-permute-start.3 = (bf16[16,2048]{1,0:T(8,128)(2,1)S(1)}, bf16[16,2048]{1,0:T(8,128)(2,1)S(1)}, u32[]{:S(2)}, u32[]{:S(2)}) collective-permute-start(bf16[16,2048]{1,0:T(8,128)(2,1)S(1)} %get-tuple-element.48), channel_id=1, source_target_pairs={{0,12},{4,8},{8,4},{12,0},{1,13},{5,9},{9,5},{13,1},{2,14},{6,10},... | collective-permute-start | bytes 196616 | tf_op jit(solution)/shard_map/ppermute | solution.py:284
  14.7 0.6 %collective-permute-start.5 = (bf16[16,2048]{1,0:T(8,128)(2,1)S(1)}, bf16[16,2048]{1,0:T(8,128)(2,1)S(1)}, u32[]{:S(2)}, u32[]{:S(2)}) collective-permute-start(bf16[16,2048]{1,0:T(8,128)(2,1)S(1)} %get-tuple-element.50), channel_id=1, source_target_pairs={{0,4},{4,0},{8,12},{12,8},{1,5},{5,1},{9,13},{13,9},{2,6},{6,2},{1... | collective-permute-start | bytes 196616 | tf_op jit(solution)/shard_map/ppermute | solution.py:284
  15.4 3.8 %collective-permute-start.13 = (bf16[16,2048]{1,0:T(8,128)(2,1)S(1)}, bf16[16,2048]{1,0:T(8,128)(2,1)S(1)}, u32[]{:S(2)}, u32[]{:S(2)}) collective-permute-start(bf16[16,2048]{1,0:T(8,128)(2,1)S(1)} %get-tuple-element.62), channel_id=1, source_target_pairs={{0,12},{4,8},{8,4},{12,0},{1,13},{5,9},{9,5},{13,1},{2,14},{6,10},... | collective-permute-start | bytes 196616 | tf_op jit(solution)/shard_map/ppermute | solution.py:284
  19.2 0.0 collective-permute-start.14
  19.2 0.0 collective-permute-done.3.refs_1_
  19.2 0.6 %collective-permute-start.15 = (bf16[16,2048]{1,0:T(8,128)(2,1)S(1)}, bf16[16,2048]{1,0:T(8,128)(2,1)S(1)}, u32[]{:S(2)}, u32[]{:S(2)}) collective-permute-start(bf16[16,2048]{1,0:T(8,128)(2,1)S(1)} %get-tuple-element.64), channel_id=1, source_target_pairs={{0,4},{4,0},{8,12},{12,8},{1,5},{5,1},{9,13},{13,9},{2,6},{6,2},{1... | collective-permute-start | bytes 196616 | tf_op jit(solution)/shard_map/ppermute | solution.py:284
  19.8 2.2 %collective-permute-done.4.refs_2_ = bf16[16,2048]{1,0:T(8,128)(2,1)S(1)} collective-permute-done((bf16[16,2048]{1,0:T(8,128)(2,1)S(1)}, bf16[16,2048]{1,0:T(8,128)(2,1)S(1)}, u32[]{:S(2)}, u32[]{:S(2)}) %collective-permute-start.4) | collective-permute-done | bytes 65568 | tf_op jit(solution)/shard_map/ppermute | solution.py:284
  22.0 0.0 collective-permute-done.5.refs_3_
  22.1 0.6 %shard_map.96 = (f32[64,1536]{1,0:T(8,128)S(1)}, bf16[64,1536]{1,0:T(8,128)(2,1)S(1)}) custom-call(bf16[16,2048]{1,0:T(8,128)(2,1)S(1)} %get-tuple-element.47.refs_0_, bf16[16,2048]{1,0:T(8,128)(2,1)S(1)} %collective-permute-done.3.refs_1_, bf16[16,2048]{1,0:T(8,128)(2,1)S(1)} %collective-permute-done.4.refs_2_, ...), custom_call_target="tpu_custom_call" | custom-call | tf_op jit(solution)/shard_map/pallas_call | solution.py:40
  22.6 1.6 %collective-permute-start.6 = (bf16[64,1536]{1,0:T(8,128)(2,1)S(1)}, bf16[64,1536]{1,0:T(8,128)(2,1)S(1)}, u32[]{:S(2)}, u32[]{:S(2)}) collective-permute-start(bf16[64,1536]{1,0:T(8,128)(2,1)S(1)} %get-tuple-element.53), channel_id=1, source_target_pairs={{0,2},{1,3},{2,0},{3,1},{4,6},{5,7},{6,4},{7,5},{8,10},{9,11},{10,... | collective-permute-start | bytes 589832 | tf_op jit(solution)/shard_map/ppermute | solution.py:278
  24.2 0.0 collective-permute-done.13.refs_1_
  24.2 0.9 %collective-permute-done.14.refs_2_ = bf16[16,2048]{1,0:T(8,128)(2,1)S(1)} collective-permute-done((bf16[16,2048]{1,0:T(8,128)(2,1)S(1)}, bf16[16,2048]{1,0:T(8,128)(2,1)S(1)}, u32[]{:S(2)}, u32[]{:S(2)}) %collective-permute-start.14) | collective-permute-done | bytes 65568 | tf_op jit(solution)/shard_map/ppermute | solution.py:284
  25.1 0.4 shard_map.101
  25.5 1.6 %collective-permute-start.19 = (bf16[64,768]{1,0:T(8,128)(2,1)S(1)}, bf16[64,768]{1,0:T(8,128)(2,1)S(1)}, u32[]{:S(2)}, u32[]{:S(2)}) collective-permute-start(bf16[64,768]{1,0:T(8,128)(2,1)S(1)} %get-tuple-element.70), channel_id=1, source_target_pairs={{0,2},{1,3},{2,0},{3,1},{4,6},{5,7},{6,4},{7,5},{8,10},{9,11},{10,... | collective-permute-start | bytes 294920 | tf_op jit(solution)/shard_map/ppermute | solution.py:278
  27.1 2.7 %collective-permute-done.6.refs_1_ = bf16[64,1536]{1,0:T(8,128)(2,1)S(1)} collective-permute-done((bf16[64,1536]{1,0:T(8,128)(2,1)S(1)}, bf16[64,1536]{1,0:T(8,128)(2,1)S(1)}, u32[]{:S(2)}, u32[]{:S(2)}) %collective-permute-start.6) | collective-permute-done | bytes 196640 | tf_op jit(solution)/shard_map/ppermute | solution.py:278
  29.7 0.1 shard_map.97.refs_0_.refs_2_.refs_4_
  29.8 1.6 %collective-permute-start.7 = (bf16[64,768]{1,0:T(8,128)(2,1)S(1)}, bf16[64,768]{1,0:T(8,128)(2,1)S(1)}, u32[]{:S(2)}, u32[]{:S(2)}) collective-permute-start(bf16[64,768]{1,0:T(8,128)(2,1)S(1)} %shard_map.97.refs_0_.refs_2_.refs_4_), channel_id=1, source_target_pairs={{0,2},{1,3},{2,0},{3,1},{4,6},{5,7},{6,4},{7,5},{8,10},{9,11},{10,... | collective-permute-start | bytes 294920 | tf_op jit(solution)/shard_map/ppermute | solution.py:278
  31.4 0.2 collective-permute-done.19.refs_3_
  31.5 0.1 shard_map.104.refs_0_
  31.7 1.6 %collective-permute-start.20 = (bf16[64,1536]{1,0:T(8,128)(2,1)S(1)}, bf16[64,1536]{1,0:T(8,128)(2,1)S(1)}, u32[]{:S(2)}, u32[]{:S(2)}) collective-permute-start(bf16[64,1536]{1,0:T(8,128)(2,1)S(1)} %shard_map.104.refs_0_), channel_id=1, source_target_pairs={{0,2},{1,3},{2,0},{3,1},{4,6},{5,7},{6,4},{7,5},{8,10},{9,11},{10,... | collective-permute-start | bytes 589832 | tf_op jit(solution)/shard_map/ppermute | solution.py:278
  33.2 2.0 %collective-permute-done.7.refs_1_.refs_3_ = bf16[64,768]{1,0:T(8,128)(2,1)S(1)} collective-permute-done((bf16[64,768]{1,0:T(8,128)(2,1)S(1)}, bf16[64,768]{1,0:T(8,128)(2,1)S(1)}, u32[]{:S(2)}, u32[]{:S(2)}) %collective-permute-start.7) | collective-permute-done | bytes 98336 | tf_op jit(solution)/shard_map/ppermute | solution.py:278
  35.2 0.6 %shard_map.98 = (bf16[32,1024]{1,0:T(8,128)(2,1)S(1)}, bf16[32,1024]{1,0:T(8,128)(2,1)S(1)}, bf16[32,1024]{1,0:T(8,128)(2,1)S(1)}, bf16[32,1024]{1,0:T(8,128)(2,1)S(1)}) custom-call(bf16[64,768]{1,0:T(8,128)(2,1)S(1)} %shard_map.97.refs_0_.refs_2_.refs_4_, bf16[64,768]{1,0:T(8,128)(2,1)S(1)} %collective-permute-done.7.refs_1_.refs_3_, ...), custom_call_target="tpu_custom_call" | custom-call | flops 2000000000 | tf_op jit(solution)/shard_map/pallas_call | solution.py:40
  35.8 1.7 %collective-permute-start.8 = (bf16[32,1024]{1,0:T(8,128)(2,1)S(1)}, bf16[32,1024]{1,0:T(8,128)(2,1)S(1)}, u32[]{:S(2)}, u32[]{:S(2)}) collective-permute-start(bf16[32,1024]{1,0:T(8,128)(2,1)S(1)} %get-tuple-element.56), channel_id=1, source_target_pairs={{0,12},{4,8},{8,4},{12,0},{1,13},{5,9},{9,5},{13,1},{2,14},{6,10},... | collective-permute-start | bytes 196616 | tf_op jit(solution)/shard_map/ppermute | solution.py:284
  37.5 0.0 collective-permute-start.9
  37.5 2.7 %collective-permute-start.10 = (bf16[32,1024]{1,0:T(8,128)(2,1)S(1)}, bf16[32,1024]{1,0:T(8,128)(2,1)S(1)}, u32[]{:S(2)}, u32[]{:S(2)}) collective-permute-start(bf16[32,1024]{1,0:T(8,128)(2,1)S(1)} %get-tuple-element.58), channel_id=1, source_target_pairs={{0,4},{4,0},{8,12},{12,8},{1,5},{5,1},{9,13},{13,9},{2,6},{6,2},{1... | collective-permute-start | bytes 196616 | tf_op jit(solution)/shard_map/ppermute | solution.py:284
  40.3 0.0 collective-permute-done.20.refs_1_
  40.3 1.1 %shard_map.105 = (bf16[64,1024]{1,0:T(8,128)(2,1)S(1)}, bf16[64,1024]{1,0:T(8,128)(2,1)S(1)}) custom-call(bf16[64,1536]{1,0:T(8,128)(2,1)S(1)} %shard_map.104.refs_0_, bf16[64,1536]{1,0:T(8,128)(2,1)S(1)} %collective-permute-done.20.refs_1_, bf16[512,1536]{1,0:T(8,128)(2,1)S(1)} %bitcast.7, bf16[512,1536]{1,0:T(8,128)(2,1)S(1)} %collective-permute-done.1.refs_5_.refs_3_), custom_call_target="tpu_custom_call" | custom-call | tf_op jit(solution)/shard_map/pallas_call | solution.py:40
  41.4 1.6 %collective-permute-start.21 = (bf16[64,1024]{1,0:T(8,128)(2,1)S(1)}, bf16[64,1024]{1,0:T(8,128)(2,1)S(1)}, u32[]{:S(2)}, u32[]{:S(2)}) collective-permute-start(bf16[64,1024]{1,0:T(8,128)(2,1)S(1)} %get-tuple-element.72), channel_id=1, source_target_pairs={{0,2},{1,3},{2,0},{3,1},{4,6},{5,7},{6,4},{7,5},{8,10},{9,11},{10,... | collective-permute-start | bytes 393224 | tf_op jit(solution)/shard_map/ppermute | solution.py:278
  43.0 0.0 collective-permute-start.16
  43.0 0.0 collective-permute-done.8.refs_1_.refs_3_
  43.0 0.5 collective-permute-start.17
  43.5 1.4 %collective-permute-start.11 = (bf16[64,1024]{1,0:T(8,128)(2,1)S(1)}, bf16[64,1024]{1,0:T(8,128)(2,1)S(1)}, u32[]{:S(2)}, u32[]{:S(2)}) collective-permute-start(bf16[64,1024]{1,0:T(8,128)(2,1)S(1)} %shard_map.99), channel_id=1, source_target_pairs={{0,2},{1,3},{2,0},{3,1},{4,6},{5,7},{6,4},{7,5},{8,10},{9,11},{10,... | collective-permute-start | bytes 393224 | tf_op jit(solution)/shard_map/ppermute | solution.py:278
  44.9 1.8 %collective-permute-done.21.refs_1_ = bf16[64,1024]{1,0:T(8,128)(2,1)S(1)} collective-permute-done((bf16[64,1024]{1,0:T(8,128)(2,1)S(1)}, bf16[64,1024]{1,0:T(8,128)(2,1)S(1)}, u32[]{:S(2)}, u32[]{:S(2)}) %collective-permute-start.21) | collective-permute-done | bytes 131104 | tf_op jit(solution)/shard_map/ppermute | solution.py:278
  46.7 1.7 %collective-permute-start.22 = (bf16[16,2048]{1,0:T(8,128)(2,1)S(1)}, bf16[16,2048]{1,0:T(8,128)(2,1)S(1)}, u32[]{:S(2)}, u32[]{:S(2)}) collective-permute-start(bf16[16,2048]{1,0:T(8,128)(2,1)S(1)} %get-tuple-element.74), channel_id=1, source_target_pairs={{0,12},{4,8},{8,4},{12,0},{1,13},{5,9},{9,5},{13,1},{2,14},{6,10},... | collective-permute-start | bytes 196616 | tf_op jit(solution)/shard_map/ppermute | solution.py:284
  48.4 0.0 collective-permute-done.17.refs_4_
  48.4 2.7 %collective-permute-start.24 = (bf16[16,2048]{1,0:T(8,128)(2,1)S(1)}, bf16[16,2048]{1,0:T(8,128)(2,1)S(1)}, u32[]{:S(2)}, u32[]{:S(2)}) collective-permute-start(bf16[16,2048]{1,0:T(8,128)(2,1)S(1)} %get-tuple-element.76), channel_id=1, source_target_pairs={{0,4},{4,0},{8,12},{12,8},{1,5},{5,1},{9,13},{13,9},{2,6},{6,2},{1... | collective-permute-start | bytes 196616 | tf_op jit(solution)/shard_map/ppermute | solution.py:284
  51.2 1.6 %shard_map.102 = (f32[512,768]{1,0:T(8,128)}, f32[8,128]{1,0:T(8,128)S(1)}) custom-call(bf16[128,512]{1,0:T(8,128)(2,1)S(1)} %get-tuple-element.65.refs_0_, bf16[128,512]{1,0:T(8,128)(2,1)S(1)} %collective-permute-done.16.refs_1_, bf16[64,768]{1,0:T(8,128)(2,1)S(1)} %shard_map.97.refs_0_.refs_2_.refs_4_, ...), custom_call_target="tpu_custom_call" | custom-call | tf_op jit(solution)/shard_map/pallas_call | solution.py:40
  52.7 1.3 %shard_map.103 = (bf16[256,2048]{1,0:T(8,128)(2,1)}, f32[8,128]{1,0:T(8,128)S(1)}) custom-call(bf16[256,64]{1,0:T(8,128)(2,1)S(1)} %get-tuple-element.41.refs_0_, f32[64,128]{1,0:T(8,128)S(1)} %get-tuple-element.42.refs_1_, bf16[32,1024]{1,0:T(8,128)(2,1)S(1)} %get-tuple-element.55.refs_0_.refs_2_, ...), custom_call_target="tpu_custom_call" | custom-call | tf_op jit(solution)/shard_map/pallas_call | solution.py:40
  54.1 0.7 %collective-permute-done.23.refs_3_ = bf16[16,2048]{1,0:T(8,128)(2,1)S(1)} collective-permute-done((bf16[16,2048]{1,0:T(8,128)(2,1)S(1)}, bf16[16,2048]{1,0:T(8,128)(2,1)S(1)}, u32[]{:S(2)}, u32[]{:S(2)}) %collective-permute-start.23) | collective-permute-done | bytes 65568 | tf_op jit(solution)/shard_map/ppermute | solution.py:284
  54.7 1.2 %shard_map.107 = bf16[256,2048]{1,0:T(8,128)(2,1)} custom-call(bf16[256,64]{1,0:T(8,128)(2,1)S(1)} %get-tuple-element.41.refs_0_, bf16[16,2048]{1,0:T(8,128)(2,1)S(1)} %get-tuple-element.73.refs_1_, bf16[16,2048]{1,0:T(8,128)(2,1)S(1)} %collective-permute-done.22.refs_2_, bf16[16,2048]{1,0:T(8,128)(2,1)S(1)} %collective-permute-done.23.refs_3_, ...), custom_call_target="tpu_custom_call" | custom-call | tf_op jit(solution)/shard_map/pallas_call | solution.py:40
  (20 shorter events, 0.1 us)
Async XLA Ops:
  0.6 21.4 %copy-start = (bf16[1,512,1536]{2,1,0:T(8,128)(2,1)S(1)}, bf16[1,512,1536]{2,1,0:T(8,128)(2,1)}, u32[]{:S(2)}) copy-start(bf16[1,512,1536]{2,1,0:T(8,128)(2,1)} %param.12) | copy-start | bytes 4718596
  0.6 9.8 %collective-permute-start.1 = (bf16[512,1536]{1,0:T(8,128)(2,1)}, bf16[512,1536]{1,0:T(8,128)(2,1)S(1)}, u32[]{:S(2)}, u32[]{:S(2)}) collective-permute-start(bf16[512,1536]{1,0:T(8,128)(2,1)} %bitcast.5), channel_id=1, source_target_pairs={{0,1},{1,0},{2,3},{3,2},{4,5},{5,4},{6,7},{7,6},{8,9},{9,8},{10,11... | collective-permute-start | bytes 4718600 | tf_op jit(solution)/shard_map/ppermute | solution.py:274
  1.2 9.3 %collective-permute-start.2 = (bf16[512,768]{1,0:T(8,128)(2,1)}, bf16[512,768]{1,0:T(8,128)(2,1)S(1)}, u32[]{:S(2)}, u32[]{:S(2)}) collective-permute-start(bf16[512,768]{1,0:T(8,128)(2,1)} %bitcast.8), channel_id=1, source_target_pairs={{0,1},{1,0},{2,3},{3,2},{4,5},{5,4},{6,7},{7,6},{8,9},{9,8},{10,11... | collective-permute-start | bytes 2359304 | tf_op jit(solution)/shard_map/ppermute | solution.py:274
  3.2 7.3 %collective-permute-start = (bf16[64,1024]{1,0:T(8,128)(2,1)S(1)}, bf16[64,1024]{1,0:T(8,128)(2,1)S(1)}, u32[]{:S(2)}, u32[]{:S(2)}) collective-permute-start(bf16[64,1024]{1,0:T(8,128)(2,1)S(1)} %get-tuple-element.44), channel_id=1, source_target_pairs={{0,2},{1,3},{2,0},{3,1},{4,6},{5,7},{6,4},{7,5},{8,10},{9,11},{10,... | collective-permute-start | bytes 393224 | tf_op jit(solution)/shard_map/ppermute | solution.py:278
  6.2 9.2 %collective-permute-start.12 = (bf16[64,1024]{1,0:T(8,128)(2,1)S(1)}, bf16[64,1024]{1,0:T(8,128)(2,1)S(1)}, u32[]{:S(2)}, u32[]{:S(2)}) collective-permute-start(bf16[64,1024]{1,0:T(8,128)(2,1)S(1)} %get-tuple-element.60), channel_id=1, source_target_pairs={{0,2},{1,3},{2,0},{3,1},{4,6},{5,7},{6,4},{7,5},{8,10},{9,11},{10,... | collective-permute-start | bytes 393224 | tf_op jit(solution)/shard_map/ppermute | solution.py:278
  10.5 8.7 %collective-permute-start.3 = (bf16[16,2048]{1,0:T(8,128)(2,1)S(1)}, bf16[16,2048]{1,0:T(8,128)(2,1)S(1)}, u32[]{:S(2)}, u32[]{:S(2)}) collective-permute-start(bf16[16,2048]{1,0:T(8,128)(2,1)S(1)} %get-tuple-element.48), channel_id=1, source_target_pairs={{0,12},{4,8},{8,4},{12,0},{1,13},{5,9},{9,5},{13,1},{2,14},{6,10},... | collective-permute-start | bytes 196616 | tf_op jit(solution)/shard_map/ppermute | solution.py:284
  14.7 7.3 %collective-permute-start.4 = (bf16[16,2048]{1,0:T(8,128)(2,1)S(1)}, bf16[16,2048]{1,0:T(8,128)(2,1)S(1)}, u32[]{:S(2)}, u32[]{:S(2)}) collective-permute-start(bf16[16,2048]{1,0:T(8,128)(2,1)S(1)} %get-tuple-element.49), channel_id=1, source_target_pairs={{0,8},{4,12},{8,0},{12,4},{1,9},{5,13},{9,1},{13,5},{2,10},{6,14},... | collective-permute-start | bytes 196616 | tf_op jit(solution)/shard_map/ppermute | solution.py:284
  14.7 7.3 %collective-permute-start.5 = (bf16[16,2048]{1,0:T(8,128)(2,1)S(1)}, bf16[16,2048]{1,0:T(8,128)(2,1)S(1)}, u32[]{:S(2)}, u32[]{:S(2)}) collective-permute-start(bf16[16,2048]{1,0:T(8,128)(2,1)S(1)} %get-tuple-element.50), channel_id=1, source_target_pairs={{0,4},{4,0},{8,12},{12,8},{1,5},{5,1},{9,13},{13,9},{2,6},{6,2},{1... | collective-permute-start | bytes 196616 | tf_op jit(solution)/shard_map/ppermute | solution.py:284
  15.4 8.8 %collective-permute-start.13 = (bf16[16,2048]{1,0:T(8,128)(2,1)S(1)}, bf16[16,2048]{1,0:T(8,128)(2,1)S(1)}, u32[]{:S(2)}, u32[]{:S(2)}) collective-permute-start(bf16[16,2048]{1,0:T(8,128)(2,1)S(1)} %get-tuple-element.62), channel_id=1, source_target_pairs={{0,12},{4,8},{8,4},{12,0},{1,13},{5,9},{9,5},{13,1},{2,14},{6,10},... | collective-permute-start | bytes 196616 | tf_op jit(solution)/shard_map/ppermute | solution.py:284
  19.2 5.9 %collective-permute-start.14 = (bf16[16,2048]{1,0:T(8,128)(2,1)S(1)}, bf16[16,2048]{1,0:T(8,128)(2,1)S(1)}, u32[]{:S(2)}, u32[]{:S(2)}) collective-permute-start(bf16[16,2048]{1,0:T(8,128)(2,1)S(1)} %get-tuple-element.63), channel_id=1, source_target_pairs={{0,8},{4,12},{8,0},{12,4},{1,9},{5,13},{9,1},{13,5},{2,10},{6,14},... | collective-permute-start | bytes 196616 | tf_op jit(solution)/shard_map/ppermute | solution.py:284
  19.2 5.9 %collective-permute-start.15 = (bf16[16,2048]{1,0:T(8,128)(2,1)S(1)}, bf16[16,2048]{1,0:T(8,128)(2,1)S(1)}, u32[]{:S(2)}, u32[]{:S(2)}) collective-permute-start(bf16[16,2048]{1,0:T(8,128)(2,1)S(1)} %get-tuple-element.64), channel_id=1, source_target_pairs={{0,4},{4,0},{8,12},{12,8},{1,5},{5,1},{9,13},{13,9},{2,6},{6,2},{1... | collective-permute-start | bytes 196616 | tf_op jit(solution)/shard_map/ppermute | solution.py:284
  22.0 3.1 %copy-start.1 = (bf16[1,512,768]{2,1,0:T(8,128)(2,1)S(1)}, bf16[1,512,768]{2,1,0:T(8,128)(2,1)}, u32[]{:S(2)}) copy-start(bf16[1,512,768]{2,1,0:T(8,128)(2,1)} %param.13) | copy-start | bytes 2359300
  22.6 7.1 %collective-permute-start.6 = (bf16[64,1536]{1,0:T(8,128)(2,1)S(1)}, bf16[64,1536]{1,0:T(8,128)(2,1)S(1)}, u32[]{:S(2)}, u32[]{:S(2)}) collective-permute-start(bf16[64,1536]{1,0:T(8,128)(2,1)S(1)} %get-tuple-element.53), channel_id=1, source_target_pairs={{0,2},{1,3},{2,0},{3,1},{4,6},{5,7},{6,4},{7,5},{8,10},{9,11},{10,... | collective-permute-start | bytes 589832 | tf_op jit(solution)/shard_map/ppermute | solution.py:278
  25.5 6.0 %collective-permute-start.19 = (bf16[64,768]{1,0:T(8,128)(2,1)S(1)}, bf16[64,768]{1,0:T(8,128)(2,1)S(1)}, u32[]{:S(2)}, u32[]{:S(2)}) collective-permute-start(bf16[64,768]{1,0:T(8,128)(2,1)S(1)} %get-tuple-element.70), channel_id=1, source_target_pairs={{0,2},{1,3},{2,0},{3,1},{4,6},{5,7},{6,4},{7,5},{8,10},{9,11},{10,... | collective-permute-start | bytes 294920 | tf_op jit(solution)/shard_map/ppermute | solution.py:278
  29.8 5.4 %collective-permute-start.7 = (bf16[64,768]{1,0:T(8,128)(2,1)S(1)}, bf16[64,768]{1,0:T(8,128)(2,1)S(1)}, u32[]{:S(2)}, u32[]{:S(2)}) collective-permute-start(bf16[64,768]{1,0:T(8,128)(2,1)S(1)} %shard_map.97.refs_0_.refs_2_.refs_4_), channel_id=1, source_target_pairs={{0,2},{1,3},{2,0},{3,1},{4,6},{5,7},{6,4},{7,5},{8,10},{9,11},{10,... | collective-permute-start | bytes 294920 | tf_op jit(solution)/shard_map/ppermute | solution.py:278
  31.7 8.6 %collective-permute-start.20 = (bf16[64,1536]{1,0:T(8,128)(2,1)S(1)}, bf16[64,1536]{1,0:T(8,128)(2,1)S(1)}, u32[]{:S(2)}, u32[]{:S(2)}) collective-permute-start(bf16[64,1536]{1,0:T(8,128)(2,1)S(1)} %shard_map.104.refs_0_), channel_id=1, source_target_pairs={{0,2},{1,3},{2,0},{3,1},{4,6},{5,7},{6,4},{7,5},{8,10},{9,11},{10,... | collective-permute-start | bytes 589832 | tf_op jit(solution)/shard_map/ppermute | solution.py:278
  35.8 7.1 %collective-permute-start.8 = (bf16[32,1024]{1,0:T(8,128)(2,1)S(1)}, bf16[32,1024]{1,0:T(8,128)(2,1)S(1)}, u32[]{:S(2)}, u32[]{:S(2)}) collective-permute-start(bf16[32,1024]{1,0:T(8,128)(2,1)S(1)} %get-tuple-element.56), channel_id=1, source_target_pairs={{0,12},{4,8},{8,4},{12,0},{1,13},{5,9},{9,5},{13,1},{2,14},{6,10},... | collective-permute-start | bytes 196616 | tf_op jit(solution)/shard_map/ppermute | solution.py:284
  37.5 6.0 %collective-permute-start.9 = (bf16[32,1024]{1,0:T(8,128)(2,1)S(1)}, bf16[32,1024]{1,0:T(8,128)(2,1)S(1)}, u32[]{:S(2)}, u32[]{:S(2)}) collective-permute-start(bf16[32,1024]{1,0:T(8,128)(2,1)S(1)} %get-tuple-element.57), channel_id=1, source_target_pairs={{0,8},{4,12},{8,0},{12,4},{1,9},{5,13},{9,1},{13,5},{2,10},{6,14},... | collective-permute-start | bytes 196616 | tf_op jit(solution)/shard_map/ppermute | solution.py:284
  37.5 6.0 %collective-permute-start.10 = (bf16[32,1024]{1,0:T(8,128)(2,1)S(1)}, bf16[32,1024]{1,0:T(8,128)(2,1)S(1)}, u32[]{:S(2)}, u32[]{:S(2)}) collective-permute-start(bf16[32,1024]{1,0:T(8,128)(2,1)S(1)} %get-tuple-element.58), channel_id=1, source_target_pairs={{0,4},{4,0},{8,12},{12,8},{1,5},{5,1},{9,13},{13,9},{2,6},{6,2},{1... | collective-permute-start | bytes 196616 | tf_op jit(solution)/shard_map/ppermute | solution.py:284
  41.4 5.3 %collective-permute-start.21 = (bf16[64,1024]{1,0:T(8,128)(2,1)S(1)}, bf16[64,1024]{1,0:T(8,128)(2,1)S(1)}, u32[]{:S(2)}, u32[]{:S(2)}) collective-permute-start(bf16[64,1024]{1,0:T(8,128)(2,1)S(1)} %get-tuple-element.72), channel_id=1, source_target_pairs={{0,2},{1,3},{2,0},{3,1},{4,6},{5,7},{6,4},{7,5},{8,10},{9,11},{10,... | collective-permute-start | bytes 393224 | tf_op jit(solution)/shard_map/ppermute | solution.py:278
  43.0 5.5 %collective-permute-start.16 = (bf16[128,512]{1,0:T(8,128)(2,1)S(1)}, bf16[128,512]{1,0:T(8,128)(2,1)S(1)}, u32[]{:S(2)}, u32[]{:S(2)}) collective-permute-start(bf16[128,512]{1,0:T(8,128)(2,1)S(1)} %get-tuple-element.66), channel_id=1, source_target_pairs={{0,1},{1,0},{2,3},{3,2},{4,5},{5,4},{6,7},{7,6},{8,9},{9,8},{10,11... | collective-permute-start | bytes 393224 | tf_op jit(solution)/shard_map/ppermute | solution.py:274
  43.0 5.5 %collective-permute-start.17 = (bf16[64,768]{1,0:T(8,128)(2,1)S(1)}, bf16[64,768]{1,0:T(8,128)(2,1)S(1)}, u32[]{:S(2)}, u32[]{:S(2)}) collective-permute-start(bf16[64,768]{1,0:T(8,128)(2,1)S(1)} %shard_map.97.refs_0_.refs_2_.refs_4_), channel_id=1, source_target_pairs={{0,1},{1,0},{2,3},{3,2},{4,5},{5,4},{6,7},{7,6},{8,9},{9,8},{10,11... | collective-permute-start | bytes 294920 | tf_op jit(solution)/shard_map/ppermute | solution.py:274
  43.5 9.2 %collective-permute-start.11 = (bf16[64,1024]{1,0:T(8,128)(2,1)S(1)}, bf16[64,1024]{1,0:T(8,128)(2,1)S(1)}, u32[]{:S(2)}, u32[]{:S(2)}) collective-permute-start(bf16[64,1024]{1,0:T(8,128)(2,1)S(1)} %shard_map.99), channel_id=1, source_target_pairs={{0,2},{1,3},{2,0},{3,1},{4,6},{5,7},{6,4},{7,5},{8,10},{9,11},{10,... | collective-permute-start | bytes 393224 | tf_op jit(solution)/shard_map/ppermute | solution.py:278
  44.9 6.3 %collective-permute-start.18 = (bf16[64,768]{1,0:T(8,128)(2,1)S(1)}, bf16[64,768]{1,0:T(8,128)(2,1)S(1)}, u32[]{:S(2)}, u32[]{:S(2)}) collective-permute-start(bf16[64,768]{1,0:T(8,128)(2,1)S(1)} %collective-permute-done.7.refs_1_.refs_3_), channel_id=1, source_target_pairs={{0,1},{1,0},{2,3},{3,2},{4,5},{5,4},{6,7},{7,6},{8,9},{9,8},{10,11... | collective-permute-start | bytes 294920 | tf_op jit(solution)/shard_map/ppermute | solution.py:274
  46.7 7.3 %collective-permute-start.22 = (bf16[16,2048]{1,0:T(8,128)(2,1)S(1)}, bf16[16,2048]{1,0:T(8,128)(2,1)S(1)}, u32[]{:S(2)}, u32[]{:S(2)}) collective-permute-start(bf16[16,2048]{1,0:T(8,128)(2,1)S(1)} %get-tuple-element.74), channel_id=1, source_target_pairs={{0,12},{4,8},{8,4},{12,0},{1,13},{5,9},{9,5},{13,1},{2,14},{6,10},... | collective-permute-start | bytes 196616 | tf_op jit(solution)/shard_map/ppermute | solution.py:284
  48.4 6.3 %collective-permute-start.23 = (bf16[16,2048]{1,0:T(8,128)(2,1)S(1)}, bf16[16,2048]{1,0:T(8,128)(2,1)S(1)}, u32[]{:S(2)}, u32[]{:S(2)}) collective-permute-start(bf16[16,2048]{1,0:T(8,128)(2,1)S(1)} %get-tuple-element.75), channel_id=1, source_target_pairs={{0,8},{4,12},{8,0},{12,4},{1,9},{5,13},{9,1},{13,5},{2,10},{6,14},... | collective-permute-start | bytes 196616 | tf_op jit(solution)/shard_map/ppermute | solution.py:284
  48.4 6.3 %collective-permute-start.24 = (bf16[16,2048]{1,0:T(8,128)(2,1)S(1)}, bf16[16,2048]{1,0:T(8,128)(2,1)S(1)}, u32[]{:S(2)}, u32[]{:S(2)}) collective-permute-start(bf16[16,2048]{1,0:T(8,128)(2,1)S(1)} %get-tuple-element.76), channel_id=1, source_target_pairs={{0,4},{4,0},{8,12},{12,8},{1,5},{5,1},{9,13},{13,9},{2,6},{6,2},{1... | collective-permute-start | bytes 196616 | tf_op jit(solution)/shard_map/ppermute | solution.py:284

commit v16 on v15

--- a/solution.py
+++ b/solution.py
@@ -56,8 +56,8 @@
 
 
 def slot_kernel(spread, *refs):
-    sources, rows_out, grads_out, refs = refs[:5], refs[5 : 5 + spread], refs[5 + spread : 5 + 2 * spread], refs[5 + 2 * spread :]
-    turned_out, gate_out, ids, gates, order, tok, cot, sems = refs
+    sources, rows_out, refs = refs[:5], refs[5 : 5 + spread], refs[5 + spread :]
+    pick_out, turned_out, gate_out, cot, ids, gates, order, tok, sems = refs
     parts = spread * CORES
     copies = [
         pltpu.make_async_copy(source, target, sems.at[i])
@@ -92,16 +92,20 @@
     slot_gate = jnp.sum(pick * gate, axis=1, keepdims=True)
     gate_out[...] = jnp.broadcast_to(slot_gate, gate_out.shape)
     pick = pick.astype(BF16)
-    for copy, source, scale, outs in (
-        (copies[3], tok, None, rows_out),
-        (copies[4], cot, slot_gate, grads_out),
-    ):
-        copy.wait()
-        for k in reversed(range(parts)):
-            value = product(pick, source[:, columns(k, part)], 1, 0)
-            value = value if scale is None else scale * value
-            to = pl.ds((k % CORES) * part, part)
-            outs[k // CORES][:, to] = value.astype(BF16)
+    pick_out[...] = pick
+    copies[3].wait()
+    for k in reversed(range(parts)):
+        value = product(pick, tok[:, columns(k, part)], 1, 0)
+        rows_out[k // CORES][:, pl.ds((k % CORES) * part, part)] = value.astype(BF16)
+    copies[4].wait()
+
+
+def grads_kernel(spread, pick, gate, cot, *outs):
+    parts = spread * CORES
+    part = cot.shape[1] // parts
+    for k in reversed(range(parts)):
+        value = gate[:, :1] * product(pick[...], cot[:, columns(k, part)], 1, 0)
+        outs[k // CORES][:, pl.ds((k % CORES) * part, part)] = value.astype(BF16)
 
 
 def flip(chunks):
@@ -288,10 +292,11 @@
     chunk = [shape((capacity, width))] * groups
     by_x = [shape((slots, half))] * spread
     in_own, out_own = w_in[0], w_out[0]
-    in_sib, out_sib = to_core(in_own), to_core(out_own)
-    outs = call(
+    *rows, pick, turned, gate, cotangent = call(
         bound(slot_kernel, spread),
-        by_x * 2 + [shape((count, slots)), shape((slots, 128), F32)],
+        by_x
+        + [shape((slots, count)), shape((count, slots)), shape((slots, 128), F32)]
+        + [shape(cotangent.shape)],
         (route_ids.T, route_gates.T, served_order, tokens, cotangent),
         far=5,
         scratch_shapes=[
@@ -299,13 +304,14 @@
             pltpu.VMEM(route_gates.shape[::-1], F32),
             pltpu.VMEM(served_order.shape, jnp.int32),
             pltpu.VMEM(tokens.shape, BF16),
-            pltpu.VMEM(cotangent.shape, BF16),
             pltpu.SemaphoreType.DMA((5,)),
         ],
     )
-    turned, gate = outs[-2:]
-    rows = [outs[0], *to_x(outs[1:spread])]
-    grads = [outs[spread], *to_x(outs[spread + 1 : 2 * spread])]
+    rows[1:] = to_x(rows[1:])
+    grads = list(call(bound(grads_kernel, spread), by_x, (pick, gate, cotangent)))
+    grads[1:] = to_x(grads[1:])
+    in_own, out_own, _ = lax.optimization_barrier((in_own, out_own, turned))
+    in_sib, out_sib = to_core(in_own), to_core(out_own)
     rows, in_sib, out_sib = lax.optimization_barrier((rows, in_sib, out_sib))
     join = bound(join_kernel, groups, spread, capacity)
     rows = to_expert(call(join, chunk, rows))

time: 56.1 us -> 57.3 us (1.021)
  waiting for transfers between devices: 14.6 us -> 16.3 us
  starting transfers between devices: 31.6 us -> 30.7 us
    ppermute x12, waiting for transfers between devices: 3.82 us -> 7.59 us  [to_expert(): lax.ppermute(value, 'expert', [(i, i ^ ke) for i in range(groups)])]
    ppermute x8, waiting for transfers between devices: 10.8 us -> 8.66 us  [to_x(): lax.ppermute(value, 'fsdp', [(i, i ^ (k + 1) * CORES) for i in range(part...]
    ppermute x8, starting transfers between devices: 12.3 us -> 11.4 us  [to_x(): lax.ppermute(value, 'fsdp', [(i, i ^ (k + 1) * CORES) for i in range(part...]
    pallas_call x14 -> x15, Pallas kernels: 8.98 us -> 9.1 us  [call(): pl.pallas_call(kernel, out_shape=out_shape, in_specs=specs, compiler_para...]
  transfers between devices with their start and end apart: 25 -> 25, of which waited for: 8 -> 8; matrix products, arithmetic and copies ran while one was open for 0% -> 0% of each run, Pallas kernels for 14% -> 11%
where the time goes in v16:
time: 57.3 us; the launch traced here: 57.1 us
  starting transfers between devices  30.7 us (54%)
  waiting for transfers between devices  16.3 us (28%)
  Pallas kernels  9.1 us (16%)
  between operations  0.76 us (1%)
    ppermute x12, starting transfers between devices, to_expert(): lax.ppermute(value, 'expert', [(i, i ^ ke) for i in range(groups)])  18.3 us
    ppermute x8, starting transfers between devices, to_x(): lax.ppermute(value, 'fsdp', [(i, i ^ (k + 1) * CORES) for i in range(part...  11.4 us
    pallas_call x15, Pallas kernels, call(): pl.pallas_call(kernel, out_shape=out_shape, in_specs=specs, compiler_para...  9.1 us
    ppermute x8, waiting for transfers between devices, to_x(): lax.ppermute(value, 'fsdp', [(i, i ^ (k + 1) * CORES) for i in range(part...  8.66 us
    ppermute x12, waiting for transfers between devices, to_expert(): lax.ppermute(value, 'expert', [(i, i ^ ke) for i in range(groups)])  7.59 us
  transfers between devices with their start and end apart: 25, of which 8 were waited for; matrix products, arithmetic and copies ran while one was open for 0% of the time, Pallas kernels for 11%

profile of v16, /device:TPU:0, one launch (start us, length us, event | category | flops | bytes accessed | tf_op | source)
XLA Modules:
  0.0 57.1 jit_solution(2537552400752650667)
XLA Ops:
  0.6 1.8 %shard_map.94 = (bf16[64,1024]{1,0:T(8,128)(2,1)S(1)}, bf16[64,1024]{1,0:T(8,128)(2,1)S(1)}, bf16[64,256]{1,0:T(8,128)(2,1)S(1)}, bf16[256,64]{1,0:T(8,128)(2,1)...) custom-call(s32[8,256]{1,0:T(8,128)} %bitcast.11, f32[8,256]{1,0:T(8,128)} %bitcast.12, s32[1,256]{1,0:T(1,128)} %refs_2_.1, ...), custom_call_target="tpu_custom_call" | custom-call | tf_op jit(solution)/shard_map/pallas_call | solution.py:40
  2.4 0.3 copy-done
  2.7 0.5 collective-permute-start.1
  3.2 0.1 collective-permute-start.2
  3.2 3.0 %collective-permute-start = (bf16[64,1024]{1,0:T(8,128)(2,1)S(1)}, bf16[64,1024]{1,0:T(8,128)(2,1)S(1)}, u32[]{:S(2)}, u32[]{:S(2)}) collective-permute-start(bf16[64,1024]{1,0:T(8,128)(2,1)S(1)} %get-tuple-element.48), channel_id=1, source_target_pairs={{0,2},{1,3},{2,0},{3,1},{4,6},{5,7},{6,4},{7,5},{8,10},{9,11},{10,... | collective-permute-start | bytes 393224 | tf_op jit(solution)/shard_map/ppermute | solution.py:282
  6.2 0.3 shard_map.100
  6.5 0.1 collective-permute-start.12
  6.6 3.9 %collective-permute-done.refs_1_ = bf16[64,1024]{1,0:T(8,128)(2,1)S(1)} collective-permute-done((bf16[64,1024]{1,0:T(8,128)(2,1)S(1)}, bf16[64,1024]{1,0:T(8,128)(2,1)S(1)}, u32[]{:S(2)}, u32[]{:S(2)}) %collective-permute-start) | collective-permute-done | bytes 131104 | tf_op jit(solution)/shard_map/ppermute | solution.py:282
  10.5 0.0 collective-permute-done.1.refs_5_.refs_3_
  10.5 4.2 %collective-permute-start.3 = (bf16[16,2048]{1,0:T(8,128)(2,1)S(1)}, bf16[16,2048]{1,0:T(8,128)(2,1)S(1)}, u32[]{:S(2)}, u32[]{:S(2)}) collective-permute-start(bf16[16,2048]{1,0:T(8,128)(2,1)S(1)} %get-tuple-element.54), channel_id=1, source_target_pairs={{0,12},{4,8},{8,4},{12,0},{1,13},{5,9},{9,5},{13,1},{2,14},{6,10},... | collective-permute-start | bytes 196616 | tf_op jit(solution)/shard_map/ppermute | solution.py:288
  14.7 0.6 %collective-permute-start.5 = (bf16[16,2048]{1,0:T(8,128)(2,1)S(1)}, bf16[16,2048]{1,0:T(8,128)(2,1)S(1)}, u32[]{:S(2)}, u32[]{:S(2)}) collective-permute-start(bf16[16,2048]{1,0:T(8,128)(2,1)S(1)} %get-tuple-element.56), channel_id=1, source_target_pairs={{0,4},{4,0},{8,12},{12,8},{1,5},{5,1},{9,13},{13,9},{2,6},{6,2},{1... | collective-permute-start | bytes 196616 | tf_op jit(solution)/shard_map/ppermute | solution.py:288
  15.4 3.8 %collective-permute-start.13 = (bf16[16,2048]{1,0:T(8,128)(2,1)S(1)}, bf16[16,2048]{1,0:T(8,128)(2,1)S(1)}, u32[]{:S(2)}, u32[]{:S(2)}) collective-permute-start(bf16[16,2048]{1,0:T(8,128)(2,1)S(1)} %get-tuple-element.70), channel_id=1, source_target_pairs={{0,12},{4,8},{8,4},{12,0},{1,13},{5,9},{9,5},{13,1},{2,14},{6,10},... | collective-permute-start | bytes 196616 | tf_op jit(solution)/shard_map/ppermute | solution.py:288
  19.2 0.0 collective-permute-start.14
  19.2 0.6 %collective-permute-start.15 = (bf16[16,2048]{1,0:T(8,128)(2,1)S(1)}, bf16[16,2048]{1,0:T(8,128)(2,1)S(1)}, u32[]{:S(2)}, u32[]{:S(2)}) collective-permute-start(bf16[16,2048]{1,0:T(8,128)(2,1)S(1)} %get-tuple-element.72), channel_id=1, source_target_pairs={{0,4},{4,0},{8,12},{12,8},{1,5},{5,1},{9,13},{13,9},{2,6},{6,2},{1... | collective-permute-start | bytes 196616 | tf_op jit(solution)/shard_map/ppermute | solution.py:288
  19.9 1.8 %collective-permute-done.4.refs_2_ = bf16[16,2048]{1,0:T(8,128)(2,1)S(1)} collective-permute-done((bf16[16,2048]{1,0:T(8,128)(2,1)S(1)}, bf16[16,2048]{1,0:T(8,128)(2,1)S(1)}, u32[]{:S(2)}, u32[]{:S(2)}) %collective-permute-start.4) | collective-permute-done | bytes 65568 | tf_op jit(solution)/shard_map/ppermute | solution.py:288
  21.7 0.0 collective-permute-done.5.refs_3_
  21.7 0.6 %shard_map.96 = (f32[64,1536]{1,0:T(8,128)S(1)}, bf16[64,1536]{1,0:T(8,128)(2,1)S(1)}) custom-call(bf16[16,2048]{1,0:T(8,128)(2,1)S(1)} %get-tuple-element.53.refs_0_, bf16[16,2048]{1,0:T(8,128)(2,1)S(1)} %collective-permute-done.3.refs_1_, bf16[16,2048]{1,0:T(8,128)(2,1)S(1)} %collective-permute-done.4.refs_2_, ...), custom_call_target="tpu_custom_call" | custom-call | tf_op jit(solution)/shard_map/pallas_call | solution.py:40
  22.3 1.6 %collective-permute-start.6 = (bf16[64,1536]{1,0:T(8,128)(2,1)S(1)}, bf16[64,1536]{1,0:T(8,128)(2,1)S(1)}, u32[]{:S(2)}, u32[]{:S(2)}) collective-permute-start(bf16[64,1536]{1,0:T(8,128)(2,1)S(1)} %get-tuple-element.59), channel_id=1, source_target_pairs={{0,2},{1,3},{2,0},{3,1},{4,6},{5,7},{6,4},{7,5},{8,10},{9,11},{10,... | collective-permute-start | bytes 589832 | tf_op jit(solution)/shard_map/ppermute | solution.py:282
  23.9 1.1 %collective-permute-done.14.refs_2_ = bf16[16,2048]{1,0:T(8,128)(2,1)S(1)} collective-permute-done((bf16[16,2048]{1,0:T(8,128)(2,1)S(1)}, bf16[16,2048]{1,0:T(8,128)(2,1)S(1)}, u32[]{:S(2)}, u32[]{:S(2)}) %collective-permute-start.14) | collective-permute-done | bytes 65568 | tf_op jit(solution)/shard_map/ppermute | solution.py:288
  25.0 0.0 collective-permute-done.15.refs_3_
  25.0 0.4 shard_map.102
  25.4 1.6 %collective-permute-start.19 = (bf16[64,768]{1,0:T(8,128)(2,1)S(1)}, bf16[64,768]{1,0:T(8,128)(2,1)S(1)}, u32[]{:S(2)}, u32[]{:S(2)}) collective-permute-start(bf16[64,768]{1,0:T(8,128)(2,1)S(1)} %get-tuple-element.78), channel_id=1, source_target_pairs={{0,2},{1,3},{2,0},{3,1},{4,6},{5,7},{6,4},{7,5},{8,10},{9,11},{10,... | collective-permute-start | bytes 294920 | tf_op jit(solution)/shard_map/ppermute | solution.py:282
  26.9 2.3 %collective-permute-done.6.refs_1_ = bf16[64,1536]{1,0:T(8,128)(2,1)S(1)} collective-permute-done((bf16[64,1536]{1,0:T(8,128)(2,1)S(1)}, bf16[64,1536]{1,0:T(8,128)(2,1)S(1)}, u32[]{:S(2)}, u32[]{:S(2)}) %collective-permute-start.6) | collective-permute-done | bytes 196640 | tf_op jit(solution)/shard_map/ppermute | solution.py:282
  29.2 0.1 shard_map.97.refs_0_.refs_2_.refs_4_
  29.3 1.6 %collective-permute-start.7 = (bf16[64,768]{1,0:T(8,128)(2,1)S(1)}, bf16[64,768]{1,0:T(8,128)(2,1)S(1)}, u32[]{:S(2)}, u32[]{:S(2)}) collective-permute-start(bf16[64,768]{1,0:T(8,128)(2,1)S(1)} %shard_map.97.refs_0_.refs_2_.refs_4_), channel_id=1, source_target_pairs={{0,2},{1,3},{2,0},{3,1},{4,6},{5,7},{6,4},{7,5},{8,10},{9,11},{10,... | collective-permute-start | bytes 294920 | tf_op jit(solution)/shard_map/ppermute | solution.py:282
  30.8 0.3 collective-permute-done.19.refs_3_
  31.2 0.1 shard_map.105.refs_0_
  31.3 1.6 %collective-permute-start.20 = (bf16[64,1536]{1,0:T(8,128)(2,1)S(1)}, bf16[64,1536]{1,0:T(8,128)(2,1)S(1)}, u32[]{:S(2)}, u32[]{:S(2)}) collective-permute-start(bf16[64,1536]{1,0:T(8,128)(2,1)S(1)} %shard_map.105.refs_0_), channel_id=1, source_target_pairs={{0,2},{1,3},{2,0},{3,1},{4,6},{5,7},{6,4},{7,5},{8,10},{9,11},{10,... | collective-permute-start | bytes 589832 | tf_op jit(solution)/shard_map/ppermute | solution.py:282
  32.9 2.1 %collective-permute-done.7.refs_1_.refs_3_ = bf16[64,768]{1,0:T(8,128)(2,1)S(1)} collective-permute-done((bf16[64,768]{1,0:T(8,128)(2,1)S(1)}, bf16[64,768]{1,0:T(8,128)(2,1)S(1)}, u32[]{:S(2)}, u32[]{:S(2)}) %collective-permute-start.7) | collective-permute-done | bytes 98336 | tf_op jit(solution)/shard_map/ppermute | solution.py:282
  35.0 0.6 %shard_map.98 = (bf16[32,1024]{1,0:T(8,128)(2,1)S(1)}, bf16[32,1024]{1,0:T(8,128)(2,1)S(1)}, bf16[32,1024]{1,0:T(8,128)(2,1)S(1)}, bf16[32,1024]{1,0:T(8,128)(2,1)S(1)}) custom-call(bf16[64,768]{1,0:T(8,128)(2,1)S(1)} %shard_map.97.refs_0_.refs_2_.refs_4_, bf16[64,768]{1,0:T(8,128)(2,1)S(1)} %collective-permute-done.7.refs_1_.refs_3_, ...), custom_call_target="tpu_custom_call" | custom-call | flops 2000000000 | tf_op jit(solution)/shard_map/pallas_call | solution.py:40
  35.6 1.6 %collective-permute-start.8 = (bf16[32,1024]{1,0:T(8,128)(2,1)S(1)}, bf16[32,1024]{1,0:T(8,128)(2,1)S(1)}, u32[]{:S(2)}, u32[]{:S(2)}) collective-permute-start(bf16[32,1024]{1,0:T(8,128)(2,1)S(1)} %get-tuple-element.62), channel_id=1, source_target_pairs={{0,12},{4,8},{8,4},{12,0},{1,13},{5,9},{9,5},{13,1},{2,14},{6,10},... | collective-permute-start | bytes 196616 | tf_op jit(solution)/shard_map/ppermute | solution.py:288
  37.2 0.0 collective-permute-start.9
  37.2 0.0 collective-permute-done.20.refs_1_
  37.2 1.1 %shard_map.106 = (bf16[64,1024]{1,0:T(8,128)(2,1)S(1)}, bf16[64,1024]{1,0:T(8,128)(2,1)S(1)}) custom-call(bf16[64,1536]{1,0:T(8,128)(2,1)S(1)} %shard_map.105.refs_0_, bf16[64,1536]{1,0:T(8,128)(2,1)S(1)} %collective-permute-done.20.refs_1_, bf16[512,1536]{1,0:T(8,128)(2,1)S(1)} %bitcast.7, bf16[512,1536]{1,0:T(8,128)(2,1)S(1)} %collective-permute-done.1.refs_5_.refs_3_), custom_call_target="tpu_custom_call" | custom-call | tf_op jit(solution)/shard_map/pallas_call | solution.py:40
  38.4 1.6 %collective-permute-start.21 = (bf16[64,1024]{1,0:T(8,128)(2,1)S(1)}, bf16[64,1024]{1,0:T(8,128)(2,1)S(1)}, u32[]{:S(2)}, u32[]{:S(2)}) collective-permute-start(bf16[64,1024]{1,0:T(8,128)(2,1)S(1)} %get-tuple-element.80), channel_id=1, source_target_pairs={{0,2},{1,3},{2,0},{3,1},{4,6},{5,7},{6,4},{7,5},{8,10},{9,11},{10,... | collective-permute-start | bytes 393224 | tf_op jit(solution)/shard_map/ppermute | solution.py:282
  39.9 2.9 %collective-permute-start.10 = (bf16[32,1024]{1,0:T(8,128)(2,1)S(1)}, bf16[32,1024]{1,0:T(8,128)(2,1)S(1)}, u32[]{:S(2)}, u32[]{:S(2)}) collective-permute-start(bf16[32,1024]{1,0:T(8,128)(2,1)S(1)} %get-tuple-element.64), channel_id=1, source_target_pairs={{0,4},{4,0},{8,12},{12,8},{1,5},{5,1},{9,13},{13,9},{2,6},{6,2},{1... | collective-permute-start | bytes 196616 | tf_op jit(solution)/shard_map/ppermute | solution.py:288
  42.8 0.5 collective-permute-start.17
  43.3 1.7 %collective-permute-done.10.refs_3_.refs_5_ = bf16[32,1024]{1,0:T(8,128)(2,1)S(1)} collective-permute-done((bf16[32,1024]{1,0:T(8,128)(2,1)S(1)}, bf16[32,1024]{1,0:T(8,128)(2,1)S(1)}, u32[]{:S(2)}, u32[]{:S(2)}) %collective-permute-start.10) | collective-permute-done | bytes 65568 | tf_op jit(solution)/shard_map/ppermute | solution.py:288
  45.1 0.6 %collective-permute-start.11 = (bf16[64,1024]{1,0:T(8,128)(2,1)S(1)}, bf16[64,1024]{1,0:T(8,128)(2,1)S(1)}, u32[]{:S(2)}, u32[]{:S(2)}) collective-permute-start(bf16[64,1024]{1,0:T(8,128)(2,1)S(1)} %shard_map.99), channel_id=1, source_target_pairs={{0,2},{1,3},{2,0},{3,1},{4,6},{5,7},{6,4},{7,5},{8,10},{9,11},{10,... | collective-permute-start | bytes 393224 | tf_op jit(solution)/shard_map/ppermute | solution.py:282
  45.7 0.0 collective-permute-start.18
  45.7 0.0 collective-permute-done.21.refs_1_
  45.7 2.1 %collective-permute-start.22 = (bf16[16,2048]{1,0:T(8,128)(2,1)S(1)}, bf16[16,2048]{1,0:T(8,128)(2,1)S(1)}, u32[]{:S(2)}, u32[]{:S(2)}) collective-permute-start(bf16[16,2048]{1,0:T(8,128)(2,1)S(1)} %get-tuple-element.82), channel_id=1, source_target_pairs={{0,12},{4,8},{8,4},{12,0},{1,13},{5,9},{9,5},{13,1},{2,14},{6,10},... | collective-permute-start | bytes 196616 | tf_op jit(solution)/shard_map/ppermute | solution.py:288
  47.8 1.5 %collective-permute-start.23 = (bf16[16,2048]{1,0:T(8,128)(2,1)S(1)}, bf16[16,2048]{1,0:T(8,128)(2,1)S(1)}, u32[]{:S(2)}, u32[]{:S(2)}) collective-permute-start(bf16[16,2048]{1,0:T(8,128)(2,1)S(1)} %get-tuple-element.83), channel_id=1, source_target_pairs={{0,8},{4,12},{8,0},{12,4},{1,9},{5,13},{9,1},{13,5},{2,10},{6,14},... | collective-permute-start | bytes 196616 | tf_op jit(solution)/shard_map/ppermute | solution.py:288
  49.2 0.9 %collective-permute-start.24 = (bf16[16,2048]{1,0:T(8,128)(2,1)S(1)}, bf16[16,2048]{1,0:T(8,128)(2,1)S(1)}, u32[]{:S(2)}, u32[]{:S(2)}) collective-permute-start(bf16[16,2048]{1,0:T(8,128)(2,1)S(1)} %get-tuple-element.84), channel_id=1, source_target_pairs={{0,4},{4,0},{8,12},{12,8},{1,5},{5,1},{9,13},{13,9},{2,6},{6,2},{1... | collective-permute-start | bytes 196616 | tf_op jit(solution)/shard_map/ppermute | solution.py:288
  50.2 1.6 %shard_map.103 = (f32[512,768]{1,0:T(8,128)}, f32[8,128]{1,0:T(8,128)S(1)}) custom-call(bf16[128,512]{1,0:T(8,128)(2,1)S(1)} %get-tuple-element.73.refs_0_, bf16[128,512]{1,0:T(8,128)(2,1)S(1)} %collective-permute-done.16.refs_1_, bf16[64,768]{1,0:T(8,128)(2,1)S(1)} %shard_map.97.refs_0_.refs_2_.refs_4_, ...), custom_call_target="tpu_custom_call" | custom-call | tf_op jit(solution)/shard_map/pallas_call | solution.py:40
  51.7 1.3 %shard_map.104 = (bf16[256,2048]{1,0:T(8,128)(2,1)}, f32[8,128]{1,0:T(8,128)S(1)}) custom-call(bf16[256,64]{1,0:T(8,128)(2,1)S(1)} %get-tuple-element.45.refs_0_, f32[64,128]{1,0:T(8,128)S(1)} %get-tuple-element.46.refs_1_, bf16[32,1024]{1,0:T(8,128)(2,1)S(1)} %get-tuple-element.61.refs_0_.refs_2_, ...), custom_call_target="tpu_custom_call" | custom-call | tf_op jit(solution)/shard_map/pallas_call | solution.py:40
  53.0 2.9 %collective-permute-done.23.refs_3_ = bf16[16,2048]{1,0:T(8,128)(2,1)S(1)} collective-permute-done((bf16[16,2048]{1,0:T(8,128)(2,1)S(1)}, bf16[16,2048]{1,0:T(8,128)(2,1)S(1)}, u32[]{:S(2)}, u32[]{:S(2)}) %collective-permute-start.23) | collective-permute-done | bytes 65568 | tf_op jit(solution)/shard_map/ppermute | solution.py:288
  55.9 1.2 %shard_map.108 = bf16[256,2048]{1,0:T(8,128)(2,1)} custom-call(bf16[256,64]{1,0:T(8,128)(2,1)S(1)} %get-tuple-element.45.refs_0_, bf16[16,2048]{1,0:T(8,128)(2,1)S(1)} %get-tuple-element.81.refs_1_, bf16[16,2048]{1,0:T(8,128)(2,1)S(1)} %collective-permute-done.22.refs_2_, bf16[16,2048]{1,0:T(8,128)(2,1)S(1)} %collective-permute-done.23.refs_3_, ...), custom_call_target="tpu_custom_call" | custom-call | tf_op jit(solution)/shard_map/pallas_call | solution.py:40
  (21 shorter events, 0.1 us)
Async XLA Ops:
  0.6 2.1 %copy-start = (bf16[1,512,1536]{2,1,0:T(8,128)(2,1)S(1)}, bf16[1,512,1536]{2,1,0:T(8,128)(2,1)}, u32[]{:S(2)}) copy-start(bf16[1,512,1536]{2,1,0:T(8,128)(2,1)} %param.12) | copy-start | bytes 4718596
  2.7 7.8 %collective-permute-start.1 = (bf16[512,1536]{1,0:T(8,128)(2,1)S(1)}, bf16[512,1536]{1,0:T(8,128)(2,1)S(1)}, u32[]{:S(2)}, u32[]{:S(2)}) collective-permute-start(bf16[512,1536]{1,0:T(8,128)(2,1)S(1)} %bitcast.5), channel_id=1, source_target_pairs={{0,1},{1,0},{2,3},{3,2},{4,5},{5,4},{6,7},{7,6},{8,9},{9,8},{10,11... | collective-permute-start | bytes 4718600 | tf_op jit(solution)/shard_map/ppermute | solution.py:278
  3.2 7.3 %collective-permute-start.2 = (bf16[512,768]{1,0:T(8,128)(2,1)}, bf16[512,768]{1,0:T(8,128)(2,1)S(1)}, u32[]{:S(2)}, u32[]{:S(2)}) collective-permute-start(bf16[512,768]{1,0:T(8,128)(2,1)} %bitcast.8), channel_id=1, source_target_pairs={{0,1},{1,0},{2,3},{3,2},{4,5},{5,4},{6,7},{7,6},{8,9},{9,8},{10,11... | collective-permute-start | bytes 2359304 | tf_op jit(solution)/shard_map/ppermute | solution.py:278
  3.2 7.2 %collective-permute-start = (bf16[64,1024]{1,0:T(8,128)(2,1)S(1)}, bf16[64,1024]{1,0:T(8,128)(2,1)S(1)}, u32[]{:S(2)}, u32[]{:S(2)}) collective-permute-start(bf16[64,1024]{1,0:T(8,128)(2,1)S(1)} %get-tuple-element.48), channel_id=1, source_target_pairs={{0,2},{1,3},{2,0},{3,1},{4,6},{5,7},{6,4},{7,5},{8,10},{9,11},{10,... | collective-permute-start | bytes 393224 | tf_op jit(solution)/shard_map/ppermute | solution.py:282
  6.5 8.9 %collective-permute-start.12 = (bf16[64,1024]{1,0:T(8,128)(2,1)S(1)}, bf16[64,1024]{1,0:T(8,128)(2,1)S(1)}, u32[]{:S(2)}, u32[]{:S(2)}) collective-permute-start(bf16[64,1024]{1,0:T(8,128)(2,1)S(1)} %get-tuple-element.68), channel_id=1, source_target_pairs={{0,2},{1,3},{2,0},{3,1},{4,6},{5,7},{6,4},{7,5},{8,10},{9,11},{10,... | collective-permute-start | bytes 393224 | tf_op jit(solution)/shard_map/ppermute | solution.py:282
  10.5 8.7 %collective-permute-start.3 = (bf16[16,2048]{1,0:T(8,128)(2,1)S(1)}, bf16[16,2048]{1,0:T(8,128)(2,1)S(1)}, u32[]{:S(2)}, u32[]{:S(2)}) collective-permute-start(bf16[16,2048]{1,0:T(8,128)(2,1)S(1)} %get-tuple-element.54), channel_id=1, source_target_pairs={{0,12},{4,8},{8,4},{12,0},{1,13},{5,9},{9,5},{13,1},{2,14},{6,10},... | collective-permute-start | bytes 196616 | tf_op jit(solution)/shard_map/ppermute | solution.py:288
  14.7 7.0 %collective-permute-start.4 = (bf16[16,2048]{1,0:T(8,128)(2,1)S(1)}, bf16[16,2048]{1,0:T(8,128)(2,1)S(1)}, u32[]{:S(2)}, u32[]{:S(2)}) collective-permute-start(bf16[16,2048]{1,0:T(8,128)(2,1)S(1)} %get-tuple-element.55), channel_id=1, source_target_pairs={{0,8},{4,12},{8,0},{12,4},{1,9},{5,13},{9,1},{13,5},{2,10},{6,14},... | collective-permute-start | bytes 196616 | tf_op jit(solution)/shard_map/ppermute | solution.py:288
  14.7 7.0 %collective-permute-start.5 = (bf16[16,2048]{1,0:T(8,128)(2,1)S(1)}, bf16[16,2048]{1,0:T(8,128)(2,1)S(1)}, u32[]{:S(2)}, u32[]{:S(2)}) collective-permute-start(bf16[16,2048]{1,0:T(8,128)(2,1)S(1)} %get-tuple-element.56), channel_id=1, source_target_pairs={{0,4},{4,0},{8,12},{12,8},{1,5},{5,1},{9,13},{13,9},{2,6},{6,2},{1... | collective-permute-start | bytes 196616 | tf_op jit(solution)/shard_map/ppermute | solution.py:288
  15.4 8.4 %collective-permute-start.13 = (bf16[16,2048]{1,0:T(8,128)(2,1)S(1)}, bf16[16,2048]{1,0:T(8,128)(2,1)S(1)}, u32[]{:S(2)}, u32[]{:S(2)}) collective-permute-start(bf16[16,2048]{1,0:T(8,128)(2,1)S(1)} %get-tuple-element.70), channel_id=1, source_target_pairs={{0,12},{4,8},{8,4},{12,0},{1,13},{5,9},{9,5},{13,1},{2,14},{6,10},... | collective-permute-start | bytes 196616 | tf_op jit(solution)/shard_map/ppermute | solution.py:288
  19.2 5.7 %collective-permute-start.14 = (bf16[16,2048]{1,0:T(8,128)(2,1)S(1)}, bf16[16,2048]{1,0:T(8,128)(2,1)S(1)}, u32[]{:S(2)}, u32[]{:S(2)}) collective-permute-start(bf16[16,2048]{1,0:T(8,128)(2,1)S(1)} %get-tuple-element.71), channel_id=1, source_target_pairs={{0,8},{4,12},{8,0},{12,4},{1,9},{5,13},{9,1},{13,5},{2,10},{6,14},... | collective-permute-start | bytes 196616 | tf_op jit(solution)/shard_map/ppermute | solution.py:288
  19.2 5.7 %collective-permute-start.15 = (bf16[16,2048]{1,0:T(8,128)(2,1)S(1)}, bf16[16,2048]{1,0:T(8,128)(2,1)S(1)}, u32[]{:S(2)}, u32[]{:S(2)}) collective-permute-start(bf16[16,2048]{1,0:T(8,128)(2,1)S(1)} %get-tuple-element.72), channel_id=1, source_target_pairs={{0,4},{4,0},{8,12},{12,8},{1,5},{5,1},{9,13},{13,9},{2,6},{6,2},{1... | collective-permute-start | bytes 196616 | tf_op jit(solution)/shard_map/ppermute | solution.py:288
  21.7 3.3 %copy-start.1 = (bf16[1,512,768]{2,1,0:T(8,128)(2,1)S(1)}, bf16[1,512,768]{2,1,0:T(8,128)(2,1)}, u32[]{:S(2)}) copy-start(bf16[1,512,768]{2,1,0:T(8,128)(2,1)} %param.13) | copy-start | bytes 2359300
  22.3 6.9 %collective-permute-start.6 = (bf16[64,1536]{1,0:T(8,128)(2,1)S(1)}, bf16[64,1536]{1,0:T(8,128)(2,1)S(1)}, u32[]{:S(2)}, u32[]{:S(2)}) collective-permute-start(bf16[64,1536]{1,0:T(8,128)(2,1)S(1)} %get-tuple-element.59), channel_id=1, source_target_pairs={{0,2},{1,3},{2,0},{3,1},{4,6},{5,7},{6,4},{7,5},{8,10},{9,11},{10,... | collective-permute-start | bytes 589832 | tf_op jit(solution)/shard_map/ppermute | solution.py:282
  25.4 5.8 %collective-permute-start.19 = (bf16[64,768]{1,0:T(8,128)(2,1)S(1)}, bf16[64,768]{1,0:T(8,128)(2,1)S(1)}, u32[]{:S(2)}, u32[]{:S(2)}) collective-permute-start(bf16[64,768]{1,0:T(8,128)(2,1)S(1)} %get-tuple-element.78), channel_id=1, source_target_pairs={{0,2},{1,3},{2,0},{3,1},{4,6},{5,7},{6,4},{7,5},{8,10},{9,11},{10,... | collective-permute-start | bytes 294920 | tf_op jit(solution)/shard_map/ppermute | solution.py:282
  29.3 5.7 %collective-permute-start.7 = (bf16[64,768]{1,0:T(8,128)(2,1)S(1)}, bf16[64,768]{1,0:T(8,128)(2,1)S(1)}, u32[]{:S(2)}, u32[]{:S(2)}) collective-permute-start(bf16[64,768]{1,0:T(8,128)(2,1)S(1)} %shard_map.97.refs_0_.refs_2_.refs_4_), channel_id=1, source_target_pairs={{0,2},{1,3},{2,0},{3,1},{4,6},{5,7},{6,4},{7,5},{8,10},{9,11},{10,... | collective-permute-start | bytes 294920 | tf_op jit(solution)/shard_map/ppermute | solution.py:282
  31.3 5.9 %collective-permute-start.20 = (bf16[64,1536]{1,0:T(8,128)(2,1)S(1)}, bf16[64,1536]{1,0:T(8,128)(2,1)S(1)}, u32[]{:S(2)}, u32[]{:S(2)}) collective-permute-start(bf16[64,1536]{1,0:T(8,128)(2,1)S(1)} %shard_map.105.refs_0_), channel_id=1, source_target_pairs={{0,2},{1,3},{2,0},{3,1},{4,6},{5,7},{6,4},{7,5},{8,10},{9,11},{10,... | collective-permute-start | bytes 589832 | tf_op jit(solution)/shard_map/ppermute | solution.py:282
  35.6 7.2 %collective-permute-start.8 = (bf16[32,1024]{1,0:T(8,128)(2,1)S(1)}, bf16[32,1024]{1,0:T(8,128)(2,1)S(1)}, u32[]{:S(2)}, u32[]{:S(2)}) collective-permute-start(bf16[32,1024]{1,0:T(8,128)(2,1)S(1)} %get-tuple-element.62), channel_id=1, source_target_pairs={{0,12},{4,8},{8,4},{12,0},{1,13},{5,9},{9,5},{13,1},{2,14},{6,10},... | collective-permute-start | bytes 196616 | tf_op jit(solution)/shard_map/ppermute | solution.py:288
  37.2 6.1 %collective-permute-start.9 = (bf16[32,1024]{1,0:T(8,128)(2,1)S(1)}, bf16[32,1024]{1,0:T(8,128)(2,1)S(1)}, u32[]{:S(2)}, u32[]{:S(2)}) collective-permute-start(bf16[32,1024]{1,0:T(8,128)(2,1)S(1)} %get-tuple-element.63), channel_id=1, source_target_pairs={{0,8},{4,12},{8,0},{12,4},{1,9},{5,13},{9,1},{13,5},{2,10},{6,14},... | collective-permute-start | bytes 196616 | tf_op jit(solution)/shard_map/ppermute | solution.py:288
  38.4 7.3 %collective-permute-start.21 = (bf16[64,1024]{1,0:T(8,128)(2,1)S(1)}, bf16[64,1024]{1,0:T(8,128)(2,1)S(1)}, u32[]{:S(2)}, u32[]{:S(2)}) collective-permute-start(bf16[64,1024]{1,0:T(8,128)(2,1)S(1)} %get-tuple-element.80), channel_id=1, source_target_pairs={{0,2},{1,3},{2,0},{3,1},{4,6},{5,7},{6,4},{7,5},{8,10},{9,11},{10,... | collective-permute-start | bytes 393224 | tf_op jit(solution)/shard_map/ppermute | solution.py:282
  39.9 5.1 %collective-permute-start.10 = (bf16[32,1024]{1,0:T(8,128)(2,1)S(1)}, bf16[32,1024]{1,0:T(8,128)(2,1)S(1)}, u32[]{:S(2)}, u32[]{:S(2)}) collective-permute-start(bf16[32,1024]{1,0:T(8,128)(2,1)S(1)} %get-tuple-element.64), channel_id=1, source_target_pairs={{0,4},{4,0},{8,12},{12,8},{1,5},{5,1},{9,13},{13,9},{2,6},{6,2},{1... | collective-permute-start | bytes 196616 | tf_op jit(solution)/shard_map/ppermute | solution.py:288
  42.8 5.0 %collective-permute-start.16 = (bf16[128,512]{1,0:T(8,128)(2,1)S(1)}, bf16[128,512]{1,0:T(8,128)(2,1)S(1)}, u32[]{:S(2)}, u32[]{:S(2)}) collective-permute-start(bf16[128,512]{1,0:T(8,128)(2,1)S(1)} %get-tuple-element.74), channel_id=1, source_target_pairs={{0,1},{1,0},{2,3},{3,2},{4,5},{5,4},{6,7},{7,6},{8,9},{9,8},{10,11... | collective-permute-start | bytes 393224 | tf_op jit(solution)/shard_map/ppermute | solution.py:278
  42.8 6.4 %collective-permute-start.17 = (bf16[64,768]{1,0:T(8,128)(2,1)S(1)}, bf16[64,768]{1,0:T(8,128)(2,1)S(1)}, u32[]{:S(2)}, u32[]{:S(2)}) collective-permute-start(bf16[64,768]{1,0:T(8,128)(2,1)S(1)} %shard_map.97.refs_0_.refs_2_.refs_4_), channel_id=1, source_target_pairs={{0,1},{1,0},{2,3},{3,2},{4,5},{5,4},{6,7},{7,6},{8,9},{9,8},{10,11... | collective-permute-start | bytes 294920 | tf_op jit(solution)/shard_map/ppermute | solution.py:278
  45.1 6.6 %collective-permute-start.11 = (bf16[64,1024]{1,0:T(8,128)(2,1)S(1)}, bf16[64,1024]{1,0:T(8,128)(2,1)S(1)}, u32[]{:S(2)}, u32[]{:S(2)}) collective-permute-start(bf16[64,1024]{1,0:T(8,128)(2,1)S(1)} %shard_map.99), channel_id=1, source_target_pairs={{0,2},{1,3},{2,0},{3,1},{4,6},{5,7},{6,4},{7,5},{8,10},{9,11},{10,... | collective-permute-start | bytes 393224 | tf_op jit(solution)/shard_map/ppermute | solution.py:282
  45.7 4.5 %collective-permute-start.18 = (bf16[64,768]{1,0:T(8,128)(2,1)S(1)}, bf16[64,768]{1,0:T(8,128)(2,1)S(1)}, u32[]{:S(2)}, u32[]{:S(2)}) collective-permute-start(bf16[64,768]{1,0:T(8,128)(2,1)S(1)} %collective-permute-done.7.refs_1_.refs_3_), channel_id=1, source_target_pairs={{0,1},{1,0},{2,3},{3,2},{4,5},{5,4},{6,7},{7,6},{8,9},{9,8},{10,11... | collective-permute-start | bytes 294920 | tf_op jit(solution)/shard_map/ppermute | solution.py:278
  45.7 7.3 %collective-permute-start.22 = (bf16[16,2048]{1,0:T(8,128)(2,1)S(1)}, bf16[16,2048]{1,0:T(8,128)(2,1)S(1)}, u32[]{:S(2)}, u32[]{:S(2)}) collective-permute-start(bf16[16,2048]{1,0:T(8,128)(2,1)S(1)} %get-tuple-element.82), channel_id=1, source_target_pairs={{0,12},{4,8},{8,4},{12,0},{1,13},{5,9},{9,5},{13,1},{2,14},{6,10},... | collective-permute-start | bytes 196616 | tf_op jit(solution)/shard_map/ppermute | solution.py:288
  47.8 8.1 %collective-permute-start.23 = (bf16[16,2048]{1,0:T(8,128)(2,1)S(1)}, bf16[16,2048]{1,0:T(8,128)(2,1)S(1)}, u32[]{:S(2)}, u32[]{:S(2)}) collective-permute-start(bf16[16,2048]{1,0:T(8,128)(2,1)S(1)} %get-tuple-element.83), channel_id=1, source_target_pairs={{0,8},{4,12},{8,0},{12,4},{1,9},{5,13},{9,1},{13,5},{2,10},{6,14},... | collective-permute-start | bytes 196616 | tf_op jit(solution)/shard_map/ppermute | solution.py:288
  49.2 6.7 %collective-permute-start.24 = (bf16[16,2048]{1,0:T(8,128)(2,1)S(1)}, bf16[16,2048]{1,0:T(8,128)(2,1)S(1)}, u32[]{:S(2)}, u32[]{:S(2)}) collective-permute-start(bf16[16,2048]{1,0:T(8,128)(2,1)S(1)} %get-tuple-element.84), channel_id=1, source_target_pairs={{0,4},{4,0},{8,12},{12,8},{1,5},{5,1},{9,13},{13,9},{2,6},{6,2},{1... | collective-permute-start | bytes 196616 | tf_op jit(solution)/shard_map/ppermute | solution.py:288

commit v17 on v15

--- a/solution.py
+++ b/solution.py
@@ -8,7 +8,9 @@
 EXPERTS = 128
 CORES = 2
 OUT_COST = 2000000000
-BACK_COST = 12000000000
+PRE_COST = 4500000000
+JOIN_COST = 1000000000
+BACK_COST = 3000000000
 VMEM = 40 * 1024 * 1024
 F32 = jnp.float32
 BF16 = jnp.bfloat16
@@ -56,7 +58,9 @@
 
 
 def slot_kernel(spread, *refs):
-    sources, rows_out, grads_out, refs = refs[:5], refs[5 : 5 + spread], refs[5 + spread : 5 + 2 * spread], refs[5 + 2 * spread :]
+    sources, refs = refs[:5], refs[5:]
+    rows_out, refs = refs[: 2 * spread - 1], refs[2 * spread - 1 :]
+    grads_out, refs = refs[:spread], refs[spread:]
     turned_out, gate_out, ids, gates, order, tok, cot, sems = refs
     parts = spread * CORES
     copies = [
@@ -92,30 +96,36 @@
     slot_gate = jnp.sum(pick * gate, axis=1, keepdims=True)
     gate_out[...] = jnp.broadcast_to(slot_gate, gate_out.shape)
     pick = pick.astype(BF16)
-    for copy, source, scale, outs in (
-        (copies[3], tok, None, rows_out),
-        (copies[4], cot, slot_gate, grads_out),
-    ):
-        copy.wait()
-        for k in reversed(range(parts)):
-            value = product(pick, source[:, columns(k, part)], 1, 0)
-            value = value if scale is None else scale * value
-            to = pl.ds((k % CORES) * part, part)
-            outs[k // CORES][:, to] = value.astype(BF16)
+    copies[3].wait()
+    for k in reversed(range(parts)):
+        value = product(pick, tok[:, columns(k, part)], 1, 0).astype(BF16)
+        put_halves(rows_out, k // CORES, pl.ds((k % CORES) * part, part), value)
+    copies[4].wait()
+    for k in reversed(range(parts)):
+        value = slot_gate * product(pick, cot[:, columns(k, part)], 1, 0)
+        grads_out[k // CORES][:, pl.ds((k % CORES) * part, part)] = value.astype(BF16)
+
+
+def put_halves(outs, kx, cols, value):
+    half = value.shape[0] // 2
+    if kx:
+        outs[2 * kx - 1][:, cols] = value[half:]
+        outs[2 * kx][:, cols] = value[:half]
+    else:
+        outs[0][:, cols] = value
 
 
 def flip(chunks):
     return [chunks[0], *chunks[:0:-1]]
 
 
-def join_kernel(groups, spread, capacity, *refs):
+def join_kernel(groups, spread, capacity, first, *refs):
     by_x, chunks = refs[:spread], refs[spread:]
     half = by_x[0].shape[1]
-    for ke in range(groups):
+    for i, chunk in enumerate(chunks):
         for kx in range(spread):
-            chunks[ke][:, kx * half : (kx + 1) * half] = by_x[kx][
-                ke * capacity : (ke + 1) * capacity
-            ]
+            at = (i if kx else i + first) * capacity
+            chunk[:, kx * half : (kx + 1) * half] = by_x[kx][at : at + capacity]
 
 
 def far_kernel(groups, spread, capacity, *refs):
@@ -287,11 +297,12 @@
 
     chunk = [shape((capacity, width))] * groups
     by_x = [shape((slots, half))] * spread
+    by_halves = [shape((slots, half))] + [shape((slots // 2, half))] * (2 * spread - 2)
     in_own, out_own = w_in[0], w_out[0]
     in_sib, out_sib = to_core(in_own), to_core(out_own)
     outs = call(
         bound(slot_kernel, spread),
-        by_x * 2 + [shape((count, slots)), shape((slots, 128), F32)],
+        by_halves + by_x + [shape((count, slots)), shape((slots, 128), F32)],
         (route_ids.T, route_gates.T, served_order, tokens, cotangent),
         far=5,
         scratch_shapes=[
@@ -304,16 +315,28 @@
         ],
     )
     turned, gate = outs[-2:]
-    rows = [outs[0], *to_x(outs[1:spread])]
-    grads = [outs[spread], *to_x(outs[spread + 1 : 2 * spread])]
-    rows, in_sib, out_sib = lax.optimization_barrier((rows, in_sib, out_sib))
-    join = bound(join_kernel, groups, spread, capacity)
-    rows = to_expert(call(join, chunk, rows))
+    near, *far = outs[: 2 * spread - 1]
+    grads = outs[2 * spread - 1 : -2]
+
+    near, in_sib, out_sib = lax.optimization_barrier((near, in_sib, out_sib))
+    high, low = to_x(far[::2]), to_x(far[1::2])
+    middle = groups // 2
+    high = call(
+        bound(join_kernel, groups, spread, capacity, middle),
+        chunk[middle:],
+        (near, *high),
+        cost=JOIN_COST,
+    )
+    low = call(bound(join_kernel, groups, spread, capacity, 0), chunk[:middle], (near, *low))
+    rows = to_expert([*low, *high])
+    grads = [grads[0], *to_x(grads[1:])]
+    join = bound(join_kernel, groups, spread, capacity, 0)
     grads = to_expert(call(join, chunk, grads))
     pre, *pre_far = call(
         bound(pre_kernel, groups, spread),
         [shape((slots, 2 * feed), F32)] + [shape((slots, 2 * feed))] * (spread - 1),
         (*flip(rows), in_own, in_sib),
+        cost=PRE_COST,
     )
     pre = (pre, *to_x(pre_far))
     (hidden,) = call(hidden_kernel, [shape((slots, feed))], pre)

time: 56.1 us -> 55.1 us (0.982)
  waiting for transfers between devices: 14.6 us -> 13.3 us
    ppermute x8 -> x9, waiting for transfers between devices: 10.8 us -> 9.68 us  [to_x(): lax.ppermute(value, 'fsdp', [(i, i ^ (k + 1) * CORES) for i in range(part...]
    ppermute x8 -> x9, starting transfers between devices: 12.3 us -> 12.2 us  [to_x(): lax.ppermute(value, 'fsdp', [(i, i ^ (k + 1) * CORES) for i in range(part...]
    pallas_call x14 -> x15, Pallas kernels: 8.98 us -> 8.99 us  [call(): pl.pallas_call(kernel, out_shape=out_shape, in_specs=specs, compiler_para...]
  transfers between devices with their start and end apart: 25 -> 26, of which waited for: 8 -> 7; matrix products, arithmetic and copies ran while one was open for 0% -> 0% of each run, Pallas kernels for 14% -> 14%
where the time goes in v17:
time: 55.1 us; the launch traced here: 54.9 us
  starting transfers between devices  31.7 us (58%)
  waiting for transfers between devices  13.3 us (24%)
  Pallas kernels  8.99 us (16%)
  between operations  0.79 us (1%)
    ppermute x12, starting transfers between devices, to_expert(): lax.ppermute(value, 'expert', [(i, i ^ ke) for i in range(groups)])  18.4 us
    ppermute x9, starting transfers between devices, to_x(): lax.ppermute(value, 'fsdp', [(i, i ^ (k + 1) * CORES) for i in range(part...  12.2 us
    ppermute x9, waiting for transfers between devices, to_x(): lax.ppermute(value, 'fsdp', [(i, i ^ (k + 1) * CORES) for i in range(part...  9.68 us
    pallas_call x15, Pallas kernels, call(): pl.pallas_call(kernel, out_shape=out_shape, in_specs=specs, compiler_para...  8.99 us
    ppermute x12, waiting for transfers between devices, to_expert(): lax.ppermute(value, 'expert', [(i, i ^ ke) for i in range(groups)])  3.65 us
    ppermute x5, starting transfers between devices, to_core(): return lax.ppermute(value, 'fsdp', [(i, i ^ 1) for i in range(parts)])  1.11 us
  transfers between devices with their start and end apart: 26, of which 7 were waited for; matrix products, arithmetic and copies ran while one was open for 0% of the time, Pallas kernels for 14%

profile of v17, /device:TPU:0, one launch (start us, length us, event | category | flops | bytes accessed | tf_op | source)
XLA Modules:
  0.0 54.9 jit_solution(17730862757928137777)
XLA Ops:
  0.6 0.5 collective-permute-start
  1.1 0.1 collective-permute-start.1
  1.2 1.9 %shard_map.94 = (bf16[64,1024]{1,0:T(8,128)(2,1)S(1)}, bf16[32,1024]{1,0:T(8,128)(2,1)S(1)}, bf16[32,1024]{1,0:T(8,128)(2,1)S(1)}, bf16[64,1024]{1,0:T(8,128)(2,...) custom-call(s32[8,256]{1,0:T(8,128)} %bitcast.11, f32[8,256]{1,0:T(8,128)} %bitcast.12, ...), custom_call_target="tpu_custom_call" | custom-call | tf_op jit(solution)/shard_map/pallas_call | solution.py:42
  3.2 3.0 %collective-permute-start.3 = (bf16[32,1024]{1,0:T(8,128)(2,1)S(1)}, bf16[32,1024]{1,0:T(8,128)(2,1)S(1)}, u32[]{:S(2)}, u32[]{:S(2)}) collective-permute-start(bf16[32,1024]{1,0:T(8,128)(2,1)S(1)} %get-tuple-element.47), channel_id=1, source_target_pairs={{0,2},{1,3},{2,0},{3,1},{4,6},{5,7},{6,4},{7,5},{8,10},{9,11},{10,... | collective-permute-start | bytes 196616 | tf_op jit(solution)/shard_map/ppermute | solution.py:288
  6.2 0.1 collective-permute-start.2
  6.2 1.9 %collective-permute-start.13 = (bf16[64,1024]{1,0:T(8,128)(2,1)S(1)}, bf16[64,1024]{1,0:T(8,128)(2,1)S(1)}, u32[]{:S(2)}, u32[]{:S(2)}) collective-permute-start(bf16[64,1024]{1,0:T(8,128)(2,1)S(1)} %get-tuple-element.60), channel_id=1, source_target_pairs={{0,2},{1,3},{2,0},{3,1},{4,6},{5,7},{6,4},{7,5},{8,10},{9,11},{10,... | collective-permute-start | bytes 393224 | tf_op jit(solution)/shard_map/ppermute | solution.py:288
  8.2 0.0 collective-permute-done.1.refs_3_.refs_5_
  8.2 0.0 collective-permute-done.refs_5_.refs_3_
  8.2 0.4 collective-permute-done.3.refs_1_
  8.6 4.4 %collective-permute-start.4 = (bf16[16,2048]{1,0:T(8,128)(2,1)S(1)}, bf16[16,2048]{1,0:T(8,128)(2,1)S(1)}, u32[]{:S(2)}, u32[]{:S(2)}) collective-permute-start(bf16[16,2048]{1,0:T(8,128)(2,1)S(1)} %get-tuple-element.48), channel_id=1, source_target_pairs={{0,12},{4,8},{8,4},{12,0},{1,13},{5,9},{9,5},{13,1},{2,14},{6,10},... | collective-permute-start | bytes 196616 | tf_op jit(solution)/shard_map/ppermute | solution.py:294
  13.0 0.0 collective-permute-start.5
  13.0 0.0 collective-permute-done.2.refs_1_
  13.0 0.7 %collective-permute-start.6 = (bf16[16,2048]{1,0:T(8,128)(2,1)S(1)}, bf16[16,2048]{1,0:T(8,128)(2,1)S(1)}, u32[]{:S(2)}, u32[]{:S(2)}) collective-permute-start(bf16[16,2048]{1,0:T(8,128)(2,1)S(1)} %get-tuple-element.50), channel_id=1, source_target_pairs={{0,4},{4,0},{8,12},{12,8},{1,5},{5,1},{9,13},{13,9},{2,6},{6,2},{1... | collective-permute-start | bytes 196616 | tf_op jit(solution)/shard_map/ppermute | solution.py:294
  13.7 3.8 %collective-permute-start.14 = (bf16[16,2048]{1,0:T(8,128)(2,1)S(1)}, bf16[16,2048]{1,0:T(8,128)(2,1)S(1)}, u32[]{:S(2)}, u32[]{:S(2)}) collective-permute-start(bf16[16,2048]{1,0:T(8,128)(2,1)S(1)} %get-tuple-element.62), channel_id=1, source_target_pairs={{0,12},{4,8},{8,4},{12,0},{1,13},{5,9},{9,5},{13,1},{2,14},{6,10},... | collective-permute-start | bytes 196616 | tf_op jit(solution)/shard_map/ppermute | solution.py:294
  17.5 0.0 collective-permute-start.15
  17.6 0.6 %collective-permute-start.16 = (bf16[16,2048]{1,0:T(8,128)(2,1)S(1)}, bf16[16,2048]{1,0:T(8,128)(2,1)S(1)}, u32[]{:S(2)}, u32[]{:S(2)}) collective-permute-start(bf16[16,2048]{1,0:T(8,128)(2,1)S(1)} %get-tuple-element.64), channel_id=1, source_target_pairs={{0,4},{4,0},{8,12},{12,8},{1,5},{5,1},{9,13},{13,9},{2,6},{6,2},{1... | collective-permute-start | bytes 196616 | tf_op jit(solution)/shard_map/ppermute | solution.py:294
  18.2 3.3 %collective-permute-done.5.refs_2_ = bf16[16,2048]{1,0:T(8,128)(2,1)S(1)} collective-permute-done((bf16[16,2048]{1,0:T(8,128)(2,1)S(1)}, bf16[16,2048]{1,0:T(8,128)(2,1)S(1)}, u32[]{:S(2)}, u32[]{:S(2)}) %collective-permute-start.5) | collective-permute-done | bytes 65568 | tf_op jit(solution)/shard_map/ppermute | solution.py:294
  21.5 0.6 %shard_map.97 = (f32[64,1536]{1,0:T(8,128)S(1)}, bf16[64,1536]{1,0:T(8,128)(2,1)S(1)}) custom-call(bf16[16,2048]{1,0:T(8,128)(2,1)S(1)} %get-tuple-element.46.refs_0_, bf16[16,2048]{1,0:T(8,128)(2,1)S(1)} %collective-permute-done.4.refs_1_, bf16[16,2048]{1,0:T(8,128)(2,1)S(1)} %collective-permute-done.5.refs_2_, ...), custom_call_target="tpu_custom_call" | custom-call | flops 4499999744 | tf_op jit(solution)/shard_map/pallas_call | solution.py:42
  22.1 1.1 %collective-permute-start.7 = (bf16[64,1536]{1,0:T(8,128)(2,1)S(1)}, bf16[64,1536]{1,0:T(8,128)(2,1)S(1)}, u32[]{:S(2)}, u32[]{:S(2)}) collective-permute-start(bf16[64,1536]{1,0:T(8,128)(2,1)S(1)} %get-tuple-element.53), channel_id=1, source_target_pairs={{0,2},{1,3},{2,0},{3,1},{4,6},{5,7},{6,4},{7,5},{8,10},{9,11},{10,... | collective-permute-start | bytes 589832 | tf_op jit(solution)/shard_map/ppermute | solution.py:288
  23.2 0.0 collective-permute-done.14.refs_1_
  23.2 0.3 collective-permute-done.15.refs_2_
  23.6 0.0 collective-permute-done.16.refs_3_
  23.6 0.4 shard_map.102
  24.0 1.6 %collective-permute-start.20 = (bf16[64,768]{1,0:T(8,128)(2,1)S(1)}, bf16[64,768]{1,0:T(8,128)(2,1)S(1)}, u32[]{:S(2)}, u32[]{:S(2)}) collective-permute-start(bf16[64,768]{1,0:T(8,128)(2,1)S(1)} %get-tuple-element.70), channel_id=1, source_target_pairs={{0,2},{1,3},{2,0},{3,1},{4,6},{5,7},{6,4},{7,5},{8,10},{9,11},{10,... | collective-permute-start | bytes 294920 | tf_op jit(solution)/shard_map/ppermute | solution.py:288
  25.5 4.2 %collective-permute-done.7.refs_1_ = bf16[64,1536]{1,0:T(8,128)(2,1)S(1)} collective-permute-done((bf16[64,1536]{1,0:T(8,128)(2,1)S(1)}, bf16[64,1536]{1,0:T(8,128)(2,1)S(1)}, u32[]{:S(2)}, u32[]{:S(2)}) %collective-permute-start.7) | collective-permute-done | bytes 196640 | tf_op jit(solution)/shard_map/ppermute | solution.py:288
  29.7 0.1 shard_map.98.refs_0_.refs_2_.refs_4_
  29.8 1.3 %collective-permute-start.8 = (bf16[64,768]{1,0:T(8,128)(2,1)S(1)}, bf16[64,768]{1,0:T(8,128)(2,1)S(1)}, u32[]{:S(2)}, u32[]{:S(2)}) collective-permute-start(bf16[64,768]{1,0:T(8,128)(2,1)S(1)} %shard_map.98.refs_0_.refs_2_.refs_4_), channel_id=1, source_target_pairs={{0,2},{1,3},{2,0},{3,1},{4,6},{5,7},{6,4},{7,5},{8,10},{9,11},{10,... | collective-permute-start | bytes 294920 | tf_op jit(solution)/shard_map/ppermute | solution.py:288
  31.1 0.1 collective-permute-done.20.refs_3_
  31.2 0.1 shard_map.105.refs_0_
  31.3 1.1 %collective-permute-start.21 = (bf16[64,1536]{1,0:T(8,128)(2,1)S(1)}, bf16[64,1536]{1,0:T(8,128)(2,1)S(1)}, u32[]{:S(2)}, u32[]{:S(2)}) collective-permute-start(bf16[64,1536]{1,0:T(8,128)(2,1)S(1)} %shard_map.105.refs_0_), channel_id=1, source_target_pairs={{0,2},{1,3},{2,0},{3,1},{4,6},{5,7},{6,4},{7,5},{8,10},{9,11},{10,... | collective-permute-start | bytes 589832 | tf_op jit(solution)/shard_map/ppermute | solution.py:288
  32.3 2.1 %collective-permute-done.8.refs_1_.refs_3_ = bf16[64,768]{1,0:T(8,128)(2,1)S(1)} collective-permute-done((bf16[64,768]{1,0:T(8,128)(2,1)S(1)}, bf16[64,768]{1,0:T(8,128)(2,1)S(1)}, u32[]{:S(2)}, u32[]{:S(2)}) %collective-permute-start.8) | collective-permute-done | bytes 98336 | tf_op jit(solution)/shard_map/ppermute | solution.py:288
  34.4 0.6 %shard_map.99 = (bf16[32,1024]{1,0:T(8,128)(2,1)S(1)}, bf16[32,1024]{1,0:T(8,128)(2,1)S(1)}, bf16[32,1024]{1,0:T(8,128)(2,1)S(1)}, bf16[32,1024]{1,0:T(8,128)(2,1)S(1)}) custom-call(bf16[64,768]{1,0:T(8,128)(2,1)S(1)} %shard_map.98.refs_0_.refs_2_.refs_4_, bf16[64,768]{1,0:T(8,128)(2,1)S(1)} %collective-permute-done.8.refs_1_.refs_3_, ...), custom_call_target="tpu_custom_call" | custom-call | flops 2000000000 | tf_op jit(solution)/shard_map/pallas_call | solution.py:42
  35.1 0.1 collective-permute-start.9
  35.2 0.1 collective-permute-start.10
  35.3 4.3 %collective-permute-start.11 = (bf16[32,1024]{1,0:T(8,128)(2,1)S(1)}, bf16[32,1024]{1,0:T(8,128)(2,1)S(1)}, u32[]{:S(2)}, u32[]{:S(2)}) collective-permute-start(bf16[32,1024]{1,0:T(8,128)(2,1)S(1)} %get-tuple-element.58), channel_id=1, source_target_pairs={{0,4},{4,0},{8,12},{12,8},{1,5},{5,1},{9,13},{13,9},{2,6},{6,2},{1... | collective-permute-start | bytes 196616 | tf_op jit(solution)/shard_map/ppermute | solution.py:294
  39.6 0.0 collective-permute-done.21.refs_1_
  39.6 1.1 %shard_map.106 = (bf16[64,1024]{1,0:T(8,128)(2,1)S(1)}, bf16[64,1024]{1,0:T(8,128)(2,1)S(1)}) custom-call(bf16[64,1536]{1,0:T(8,128)(2,1)S(1)} %shard_map.105.refs_0_, bf16[64,1536]{1,0:T(8,128)(2,1)S(1)} %collective-permute-done.21.refs_1_, bf16[512,1536]{1,0:T(8,128)(2,1)S(1)} %bitcast.7, bf16[512,1536]{1,0:T(8,128)(2,1)S(1)} %collective-permute-done.refs_5_.refs_3_), custom_call_target="tpu_custom_call" | custom-call | tf_op jit(solution)/shard_map/pallas_call | solution.py:42
  40.7 1.3 %collective-permute-start.22 = (bf16[64,1024]{1,0:T(8,128)(2,1)S(1)}, bf16[64,1024]{1,0:T(8,128)(2,1)S(1)}, u32[]{:S(2)}, u32[]{:S(2)}) collective-permute-start(bf16[64,1024]{1,0:T(8,128)(2,1)S(1)} %get-tuple-element.72), channel_id=1, source_target_pairs={{0,2},{1,3},{2,0},{3,1},{4,6},{5,7},{6,4},{7,5},{8,10},{9,11},{10,... | collective-permute-start | bytes 393224 | tf_op jit(solution)/shard_map/ppermute | solution.py:288
  42.0 0.5 collective-permute-start.18
  42.5 0.9 %collective-permute-start.12 = (bf16[64,1024]{1,0:T(8,128)(2,1)S(1)}, bf16[64,1024]{1,0:T(8,128)(2,1)S(1)}, u32[]{:S(2)}, u32[]{:S(2)}) collective-permute-start(bf16[64,1024]{1,0:T(8,128)(2,1)S(1)} %shard_map.100), channel_id=1, source_target_pairs={{0,2},{1,3},{2,0},{3,1},{4,6},{5,7},{6,4},{7,5},{8,10},{9,11},{10,... | collective-permute-start | bytes 393224 | tf_op jit(solution)/shard_map/ppermute | solution.py:288
  43.4 0.0 collective-permute-start.19
  43.4 2.9 %collective-permute-done.22.refs_1_ = bf16[64,1024]{1,0:T(8,128)(2,1)S(1)} collective-permute-done((bf16[64,1024]{1,0:T(8,128)(2,1)S(1)}, bf16[64,1024]{1,0:T(8,128)(2,1)S(1)}, u32[]{:S(2)}, u32[]{:S(2)}) %collective-permute-start.22) | collective-permute-done | bytes 131104 | tf_op jit(solution)/shard_map/ppermute | solution.py:288
  46.3 0.1 collective-permute-start.23
  46.4 1.5 %collective-permute-start.24 = (bf16[16,2048]{1,0:T(8,128)(2,1)S(1)}, bf16[16,2048]{1,0:T(8,128)(2,1)S(1)}, u32[]{:S(2)}, u32[]{:S(2)}) collective-permute-start(bf16[16,2048]{1,0:T(8,128)(2,1)S(1)} %get-tuple-element.75), channel_id=1, source_target_pairs={{0,8},{4,12},{8,0},{12,4},{1,9},{5,13},{9,1},{13,5},{2,10},{6,14},... | collective-permute-start | bytes 196616 | tf_op jit(solution)/shard_map/ppermute | solution.py:294
  47.8 2.9 %collective-permute-start.25 = (bf16[16,2048]{1,0:T(8,128)(2,1)S(1)}, bf16[16,2048]{1,0:T(8,128)(2,1)S(1)}, u32[]{:S(2)}, u32[]{:S(2)}) collective-permute-start(bf16[16,2048]{1,0:T(8,128)(2,1)S(1)} %get-tuple-element.76), channel_id=1, source_target_pairs={{0,4},{4,0},{8,12},{12,8},{1,5},{5,1},{9,13},{13,9},{2,6},{6,2},{1... | collective-permute-start | bytes 196616 | tf_op jit(solution)/shard_map/ppermute | solution.py:294
  50.8 1.6 %shard_map.103 = (f32[512,768]{1,0:T(8,128)}, f32[8,128]{1,0:T(8,128)S(1)}) custom-call(bf16[128,512]{1,0:T(8,128)(2,1)S(1)} %get-tuple-element.65.refs_0_, bf16[128,512]{1,0:T(8,128)(2,1)S(1)} %collective-permute-done.17.refs_1_, bf16[64,768]{1,0:T(8,128)(2,1)S(1)} %shard_map.98.refs_0_.refs_2_.refs_4_, ...), custom_call_target="tpu_custom_call" | custom-call | tf_op jit(solution)/shard_map/pallas_call | solution.py:42
  52.3 1.3 %shard_map.104 = (bf16[256,2048]{1,0:T(8,128)(2,1)}, f32[8,128]{1,0:T(8,128)S(1)}) custom-call(bf16[256,64]{1,0:T(8,128)(2,1)S(1)} %get-tuple-element.41.refs_0_, f32[64,128]{1,0:T(8,128)S(1)} %get-tuple-element.42.refs_1_, bf16[32,1024]{1,0:T(8,128)(2,1)S(1)} %get-tuple-element.55.refs_0_.refs_2_, ...), custom_call_target="tpu_custom_call" | custom-call | tf_op jit(solution)/shard_map/pallas_call | solution.py:42
  53.6 1.2 %shard_map.108 = bf16[256,2048]{1,0:T(8,128)(2,1)} custom-call(bf16[256,64]{1,0:T(8,128)(2,1)S(1)} %get-tuple-element.41.refs_0_, bf16[16,2048]{1,0:T(8,128)(2,1)S(1)} %get-tuple-element.73.refs_1_, bf16[16,2048]{1,0:T(8,128)(2,1)S(1)} %collective-permute-done.23.refs_2_, bf16[16,2048]{1,0:T(8,128)(2,1)S(1)} %collective-permute-done.24.refs_3_, ...), custom_call_target="tpu_custom_call" | custom-call | tf_op jit(solution)/shard_map/pallas_call | solution.py:42
  (23 shorter events, 0.1 us)
Async XLA Ops:
  0.6 7.6 %collective-permute-start = (bf16[512,1536]{1,0:T(8,128)(2,1)}, bf16[512,1536]{1,0:T(8,128)(2,1)S(1)}, u32[]{:S(2)}, u32[]{:S(2)}) collective-permute-start(bf16[512,1536]{1,0:T(8,128)(2,1)} %bitcast.5), channel_id=1, source_target_pairs={{0,1},{1,0},{2,3},{3,2},{4,5},{5,4},{6,7},{7,6},{8,9},{9,8},{10,11... | collective-permute-start | bytes 4718600 | tf_op jit(solution)/shard_map/ppermute | solution.py:284
  1.1 7.0 %collective-permute-start.1 = (bf16[512,768]{1,0:T(8,128)(2,1)}, bf16[512,768]{1,0:T(8,128)(2,1)S(1)}, u32[]{:S(2)}, u32[]{:S(2)}) collective-permute-start(bf16[512,768]{1,0:T(8,128)(2,1)} %bitcast.8), channel_id=1, source_target_pairs={{0,1},{1,0},{2,3},{3,2},{4,5},{5,4},{6,7},{7,6},{8,9},{9,8},{10,11... | collective-permute-start | bytes 2359304 | tf_op jit(solution)/shard_map/ppermute | solution.py:284
  3.2 5.5 %collective-permute-start.3 = (bf16[32,1024]{1,0:T(8,128)(2,1)S(1)}, bf16[32,1024]{1,0:T(8,128)(2,1)S(1)}, u32[]{:S(2)}, u32[]{:S(2)}) collective-permute-start(bf16[32,1024]{1,0:T(8,128)(2,1)S(1)} %get-tuple-element.47), channel_id=1, source_target_pairs={{0,2},{1,3},{2,0},{3,1},{4,6},{5,7},{6,4},{7,5},{8,10},{9,11},{10,... | collective-permute-start | bytes 196616 | tf_op jit(solution)/shard_map/ppermute | solution.py:288
  6.2 6.8 %collective-permute-start.2 = (bf16[32,1024]{1,0:T(8,128)(2,1)S(1)}, bf16[32,1024]{1,0:T(8,128)(2,1)S(1)}, u32[]{:S(2)}, u32[]{:S(2)}) collective-permute-start(bf16[32,1024]{1,0:T(8,128)(2,1)S(1)} %get-tuple-element.45), channel_id=1, source_target_pairs={{0,2},{1,3},{2,0},{3,1},{4,6},{5,7},{6,4},{7,5},{8,10},{9,11},{10,... | collective-permute-start | bytes 196616 | tf_op jit(solution)/shard_map/ppermute | solution.py:288
  6.2 7.5 %collective-permute-start.13 = (bf16[64,1024]{1,0:T(8,128)(2,1)S(1)}, bf16[64,1024]{1,0:T(8,128)(2,1)S(1)}, u32[]{:S(2)}, u32[]{:S(2)}) collective-permute-start(bf16[64,1024]{1,0:T(8,128)(2,1)S(1)} %get-tuple-element.60), channel_id=1, source_target_pairs={{0,2},{1,3},{2,0},{3,1},{4,6},{5,7},{6,4},{7,5},{8,10},{9,11},{10,... | collective-permute-start | bytes 393224 | tf_op jit(solution)/shard_map/ppermute | solution.py:288
  8.2 13.3 %copy-start = (bf16[1,512,1536]{2,1,0:T(8,128)(2,1)S(1)}, bf16[1,512,1536]{2,1,0:T(8,128)(2,1)}, u32[]{:S(2)}) copy-start(bf16[1,512,1536]{2,1,0:T(8,128)(2,1)} %param.12) | copy-start | bytes 4718596
  8.6 8.9 %collective-permute-start.4 = (bf16[16,2048]{1,0:T(8,128)(2,1)S(1)}, bf16[16,2048]{1,0:T(8,128)(2,1)S(1)}, u32[]{:S(2)}, u32[]{:S(2)}) collective-permute-start(bf16[16,2048]{1,0:T(8,128)(2,1)S(1)} %get-tuple-element.48), channel_id=1, source_target_pairs={{0,12},{4,8},{8,4},{12,0},{1,13},{5,9},{9,5},{13,1},{2,14},{6,10},... | collective-permute-start | bytes 196616 | tf_op jit(solution)/shard_map/ppermute | solution.py:294
  13.0 8.5 %collective-permute-start.5 = (bf16[16,2048]{1,0:T(8,128)(2,1)S(1)}, bf16[16,2048]{1,0:T(8,128)(2,1)S(1)}, u32[]{:S(2)}, u32[]{:S(2)}) collective-permute-start(bf16[16,2048]{1,0:T(8,128)(2,1)S(1)} %get-tuple-element.49), channel_id=1, source_target_pairs={{0,8},{4,12},{8,0},{12,4},{1,9},{5,13},{9,1},{13,5},{2,10},{6,14},... | collective-permute-start | bytes 196616 | tf_op jit(solution)/shard_map/ppermute | solution.py:294
  13.0 8.5 %collective-permute-start.6 = (bf16[16,2048]{1,0:T(8,128)(2,1)S(1)}, bf16[16,2048]{1,0:T(8,128)(2,1)S(1)}, u32[]{:S(2)}, u32[]{:S(2)}) collective-permute-start(bf16[16,2048]{1,0:T(8,128)(2,1)S(1)} %get-tuple-element.50), channel_id=1, source_target_pairs={{0,4},{4,0},{8,12},{12,8},{1,5},{5,1},{9,13},{13,9},{2,6},{6,2},{1... | collective-permute-start | bytes 196616 | tf_op jit(solution)/shard_map/ppermute | solution.py:294
  13.7 9.5 %collective-permute-start.14 = (bf16[16,2048]{1,0:T(8,128)(2,1)S(1)}, bf16[16,2048]{1,0:T(8,128)(2,1)S(1)}, u32[]{:S(2)}, u32[]{:S(2)}) collective-permute-start(bf16[16,2048]{1,0:T(8,128)(2,1)S(1)} %get-tuple-element.62), channel_id=1, source_target_pairs={{0,12},{4,8},{8,4},{12,0},{1,13},{5,9},{9,5},{13,1},{2,14},{6,10},... | collective-permute-start | bytes 196616 | tf_op jit(solution)/shard_map/ppermute | solution.py:294
  17.5 6.0 %collective-permute-start.15 = (bf16[16,2048]{1,0:T(8,128)(2,1)S(1)}, bf16[16,2048]{1,0:T(8,128)(2,1)S(1)}, u32[]{:S(2)}, u32[]{:S(2)}) collective-permute-start(bf16[16,2048]{1,0:T(8,128)(2,1)S(1)} %get-tuple-element.63), channel_id=1, source_target_pairs={{0,8},{4,12},{8,0},{12,4},{1,9},{5,13},{9,1},{13,5},{2,10},{6,14},... | collective-permute-start | bytes 196616 | tf_op jit(solution)/shard_map/ppermute | solution.py:294
  17.6 6.0 %collective-permute-start.16 = (bf16[16,2048]{1,0:T(8,128)(2,1)S(1)}, bf16[16,2048]{1,0:T(8,128)(2,1)S(1)}, u32[]{:S(2)}, u32[]{:S(2)}) collective-permute-start(bf16[16,2048]{1,0:T(8,128)(2,1)S(1)} %get-tuple-element.64), channel_id=1, source_target_pairs={{0,4},{4,0},{8,12},{12,8},{1,5},{5,1},{9,13},{13,9},{2,6},{6,2},{1... | collective-permute-start | bytes 196616 | tf_op jit(solution)/shard_map/ppermute | solution.py:294
  21.5 2.1 %copy-start.1 = (bf16[1,512,768]{2,1,0:T(8,128)(2,1)S(1)}, bf16[1,512,768]{2,1,0:T(8,128)(2,1)}, u32[]{:S(2)}) copy-start(bf16[1,512,768]{2,1,0:T(8,128)(2,1)} %param.13) | copy-start | bytes 2359300
  22.1 7.6 %collective-permute-start.7 = (bf16[64,1536]{1,0:T(8,128)(2,1)S(1)}, bf16[64,1536]{1,0:T(8,128)(2,1)S(1)}, u32[]{:S(2)}, u32[]{:S(2)}) collective-permute-start(bf16[64,1536]{1,0:T(8,128)(2,1)S(1)} %get-tuple-element.53), channel_id=1, source_target_pairs={{0,2},{1,3},{2,0},{3,1},{4,6},{5,7},{6,4},{7,5},{8,10},{9,11},{10,... | collective-permute-start | bytes 589832 | tf_op jit(solution)/shard_map/ppermute | solution.py:288
  24.0 7.2 %collective-permute-start.20 = (bf16[64,768]{1,0:T(8,128)(2,1)S(1)}, bf16[64,768]{1,0:T(8,128)(2,1)S(1)}, u32[]{:S(2)}, u32[]{:S(2)}) collective-permute-start(bf16[64,768]{1,0:T(8,128)(2,1)S(1)} %get-tuple-element.70), channel_id=1, source_target_pairs={{0,2},{1,3},{2,0},{3,1},{4,6},{5,7},{6,4},{7,5},{8,10},{9,11},{10,... | collective-permute-start | bytes 294920 | tf_op jit(solution)/shard_map/ppermute | solution.py:288
  29.8 4.7 %collective-permute-start.8 = (bf16[64,768]{1,0:T(8,128)(2,1)S(1)}, bf16[64,768]{1,0:T(8,128)(2,1)S(1)}, u32[]{:S(2)}, u32[]{:S(2)}) collective-permute-start(bf16[64,768]{1,0:T(8,128)(2,1)S(1)} %shard_map.98.refs_0_.refs_2_.refs_4_), channel_id=1, source_target_pairs={{0,2},{1,3},{2,0},{3,1},{4,6},{5,7},{6,4},{7,5},{8,10},{9,11},{10,... | collective-permute-start | bytes 294920 | tf_op jit(solution)/shard_map/ppermute | solution.py:288
  31.3 8.3 %collective-permute-start.21 = (bf16[64,1536]{1,0:T(8,128)(2,1)S(1)}, bf16[64,1536]{1,0:T(8,128)(2,1)S(1)}, u32[]{:S(2)}, u32[]{:S(2)}) collective-permute-start(bf16[64,1536]{1,0:T(8,128)(2,1)S(1)} %shard_map.105.refs_0_), channel_id=1, source_target_pairs={{0,2},{1,3},{2,0},{3,1},{4,6},{5,7},{6,4},{7,5},{8,10},{9,11},{10,... | collective-permute-start | bytes 589832 | tf_op jit(solution)/shard_map/ppermute | solution.py:288
  35.1 6.9 %collective-permute-start.9 = (bf16[32,1024]{1,0:T(8,128)(2,1)S(1)}, bf16[32,1024]{1,0:T(8,128)(2,1)S(1)}, u32[]{:S(2)}, u32[]{:S(2)}) collective-permute-start(bf16[32,1024]{1,0:T(8,128)(2,1)S(1)} %get-tuple-element.56), channel_id=1, source_target_pairs={{0,12},{4,8},{8,4},{12,0},{1,13},{5,9},{9,5},{13,1},{2,14},{6,10},... | collective-permute-start | bytes 196616 | tf_op jit(solution)/shard_map/ppermute | solution.py:294
  35.2 7.3 %collective-permute-start.10 = (bf16[32,1024]{1,0:T(8,128)(2,1)S(1)}, bf16[32,1024]{1,0:T(8,128)(2,1)S(1)}, u32[]{:S(2)}, u32[]{:S(2)}) collective-permute-start(bf16[32,1024]{1,0:T(8,128)(2,1)S(1)} %get-tuple-element.57), channel_id=1, source_target_pairs={{0,8},{4,12},{8,0},{12,4},{1,9},{5,13},{9,1},{13,5},{2,10},{6,14},... | collective-permute-start | bytes 196616 | tf_op jit(solution)/shard_map/ppermute | solution.py:294
  35.3 7.2 %collective-permute-start.11 = (bf16[32,1024]{1,0:T(8,128)(2,1)S(1)}, bf16[32,1024]{1,0:T(8,128)(2,1)S(1)}, u32[]{:S(2)}, u32[]{:S(2)}) collective-permute-start(bf16[32,1024]{1,0:T(8,128)(2,1)S(1)} %get-tuple-element.58), channel_id=1, source_target_pairs={{0,4},{4,0},{8,12},{12,8},{1,5},{5,1},{9,13},{13,9},{2,6},{6,2},{1... | collective-permute-start | bytes 196616 | tf_op jit(solution)/shard_map/ppermute | solution.py:294
  40.7 5.6 %collective-permute-start.22 = (bf16[64,1024]{1,0:T(8,128)(2,1)S(1)}, bf16[64,1024]{1,0:T(8,128)(2,1)S(1)}, u32[]{:S(2)}, u32[]{:S(2)}) collective-permute-start(bf16[64,1024]{1,0:T(8,128)(2,1)S(1)} %get-tuple-element.72), channel_id=1, source_target_pairs={{0,2},{1,3},{2,0},{3,1},{4,6},{5,7},{6,4},{7,5},{8,10},{9,11},{10,... | collective-permute-start | bytes 393224 | tf_op jit(solution)/shard_map/ppermute | solution.py:288
  42.0 4.4 %collective-permute-start.17 = (bf16[128,512]{1,0:T(8,128)(2,1)S(1)}, bf16[128,512]{1,0:T(8,128)(2,1)S(1)}, u32[]{:S(2)}, u32[]{:S(2)}) collective-permute-start(bf16[128,512]{1,0:T(8,128)(2,1)S(1)} %get-tuple-element.66), channel_id=1, source_target_pairs={{0,1},{1,0},{2,3},{3,2},{4,5},{5,4},{6,7},{7,6},{8,9},{9,8},{10,11... | collective-permute-start | bytes 393224 | tf_op jit(solution)/shard_map/ppermute | solution.py:284
  42.0 5.9 %collective-permute-start.18 = (bf16[64,768]{1,0:T(8,128)(2,1)S(1)}, bf16[64,768]{1,0:T(8,128)(2,1)S(1)}, u32[]{:S(2)}, u32[]{:S(2)}) collective-permute-start(bf16[64,768]{1,0:T(8,128)(2,1)S(1)} %shard_map.98.refs_0_.refs_2_.refs_4_), channel_id=1, source_target_pairs={{0,1},{1,0},{2,3},{3,2},{4,5},{5,4},{6,7},{7,6},{8,9},{9,8},{10,11... | collective-permute-start | bytes 294920 | tf_op jit(solution)/shard_map/ppermute | solution.py:284
  42.5 9.8 %collective-permute-start.12 = (bf16[64,1024]{1,0:T(8,128)(2,1)S(1)}, bf16[64,1024]{1,0:T(8,128)(2,1)S(1)}, u32[]{:S(2)}, u32[]{:S(2)}) collective-permute-start(bf16[64,1024]{1,0:T(8,128)(2,1)S(1)} %shard_map.100), channel_id=1, source_target_pairs={{0,2},{1,3},{2,0},{3,1},{4,6},{5,7},{6,4},{7,5},{8,10},{9,11},{10,... | collective-permute-start | bytes 393224 | tf_op jit(solution)/shard_map/ppermute | solution.py:288
  43.4 7.4 %collective-permute-start.19 = (bf16[64,768]{1,0:T(8,128)(2,1)S(1)}, bf16[64,768]{1,0:T(8,128)(2,1)S(1)}, u32[]{:S(2)}, u32[]{:S(2)}) collective-permute-start(bf16[64,768]{1,0:T(8,128)(2,1)S(1)} %collective-permute-done.8.refs_1_.refs_3_), channel_id=1, source_target_pairs={{0,1},{1,0},{2,3},{3,2},{4,5},{5,4},{6,7},{7,6},{8,9},{9,8},{10,11... | collective-permute-start | bytes 294920 | tf_op jit(solution)/shard_map/ppermute | solution.py:284
  46.3 7.3 %collective-permute-start.23 = (bf16[16,2048]{1,0:T(8,128)(2,1)S(1)}, bf16[16,2048]{1,0:T(8,128)(2,1)S(1)}, u32[]{:S(2)}, u32[]{:S(2)}) collective-permute-start(bf16[16,2048]{1,0:T(8,128)(2,1)S(1)} %get-tuple-element.74), channel_id=1, source_target_pairs={{0,12},{4,8},{8,4},{12,0},{1,13},{5,9},{9,5},{13,1},{2,14},{6,10},... | collective-permute-start | bytes 196616 | tf_op jit(solution)/shard_map/ppermute | solution.py:294
  46.4 7.2 %collective-permute-start.24 = (bf16[16,2048]{1,0:T(8,128)(2,1)S(1)}, bf16[16,2048]{1,0:T(8,128)(2,1)S(1)}, u32[]{:S(2)}, u32[]{:S(2)}) collective-permute-start(bf16[16,2048]{1,0:T(8,128)(2,1)S(1)} %get-tuple-element.75), channel_id=1, source_target_pairs={{0,8},{4,12},{8,0},{12,4},{1,9},{5,13},{9,1},{13,5},{2,10},{6,14},... | collective-permute-start | bytes 196616 | tf_op jit(solution)/shard_map/ppermute | solution.py:294
  47.8 5.8 %collective-permute-start.25 = (bf16[16,2048]{1,0:T(8,128)(2,1)S(1)}, bf16[16,2048]{1,0:T(8,128)(2,1)S(1)}, u32[]{:S(2)}, u32[]{:S(2)}) collective-permute-start(bf16[16,2048]{1,0:T(8,128)(2,1)S(1)} %get-tuple-element.76), channel_id=1, source_target_pairs={{0,4},{4,0},{8,12},{12,8},{1,5},{5,1},{9,13},{13,9},{2,6},{6,2},{1... | collective-permute-start | bytes 196616 | tf_op jit(solution)/shard_map/ppermute | solution.py:294

commit v18 on v17

--- a/solution.py
+++ b/solution.py
@@ -365,10 +365,6 @@
     near, *far = call(
         bound(d_rows_kernel, spread), by_x, (*d_pre, in_own, in_sib)
     )
-    d_rows = to_expert(call(join, chunk, (near, *to_x(far))))
-    far = to_x(
-        call(bound(far_kernel, groups, spread, capacity), by_x[1:], flip(expert_out))
-    )
     d_w_out, token = call(
         bound(weight_kernel, spread),
         [shape((part, feed), F32)],
@@ -376,6 +372,10 @@
         token=True,
     )
 
+    d_rows = to_expert(call(join, chunk, (near, *to_x(far)), after=(token,)))
+    far = to_x(
+        call(bound(far_kernel, groups, spread, capacity), by_x[1:], flip(expert_out))
+    )
     def scattered(kernel, operands, **kw):
         return call(
             kernel,
@@ -393,7 +393,6 @@
     combined, token = scattered(
         bound(combine_kernel, groups, parts, capacity),
         (turned, gate, *flip(expert_out), *far),
-        after=(token,),
         token=True,
     )
     (d_tokens,) = scattered(

time: 55.1 us -> 56.4 us (1.024)
  waiting for transfers between devices: 13.3 us -> 14.2 us
    ppermute x12, waiting for transfers between devices: 3.65 us -> 5.94 us  [to_expert(): lax.ppermute(value, 'expert', [(i, i ^ ke) for i in range(groups)])]
    ppermute x9, waiting for transfers between devices: 9.68 us -> 8.25 us  [to_x(): lax.ppermute(value, 'fsdp', [(i, i ^ (k + 1) * CORES) for i in range(part...]
  transfers between devices with their start and end apart: 26 -> 26, of which waited for: 7 -> 10; matrix products, arithmetic and copies ran while one was open for 0% -> 0% of each run, Pallas kernels for 14% -> 14%
where the time goes in v18:
time: 56.4 us; the launch traced here: 56.2 us
  starting transfers between devices  32.2 us (57%)
  waiting for transfers between devices  14.2 us (25%)
  Pallas kernels  9 us (16%)
  between operations  0.77 us (1%)
    ppermute x12, starting transfers between devices, to_expert(): lax.ppermute(value, 'expert', [(i, i ^ ke) for i in range(groups)])  18.3 us
    ppermute x9, starting transfers between devices, to_x(): lax.ppermute(value, 'fsdp', [(i, i ^ (k + 1) * CORES) for i in range(part...  12.7 us
    pallas_call x15, Pallas kernels, call(): pl.pallas_call(kernel, out_shape=out_shape, in_specs=specs, compiler_para...  9 us
    ppermute x9, waiting for transfers between devices, to_x(): lax.ppermute(value, 'fsdp', [(i, i ^ (k + 1) * CORES) for i in range(part...  8.25 us
    ppermute x12, waiting for transfers between devices, to_expert(): lax.ppermute(value, 'expert', [(i, i ^ ke) for i in range(groups)])  5.94 us
    ppermute x5, starting transfers between devices, to_core(): return lax.ppermute(value, 'fsdp', [(i, i ^ 1) for i in range(parts)])  1.18 us
  transfers between devices with their start and end apart: 26, of which 10 were waited for; matrix products, arithmetic and copies ran while one was open for 0% of the time, Pallas kernels for 14%

profile of v18, /device:TPU:0, one launch (start us, length us, event | category | flops | bytes accessed | tf_op | source)
XLA Modules:
  0.0 56.2 jit_solution(11348523795877207264)
XLA Ops:
  0.6 0.5 collective-permute-start
  1.1 0.1 collective-permute-start.1
  1.2 1.9 %shard_map.94 = (bf16[64,1024]{1,0:T(8,128)(2,1)S(1)}, bf16[32,1024]{1,0:T(8,128)(2,1)S(1)}, bf16[32,1024]{1,0:T(8,128)(2,1)S(1)}, bf16[64,1024]{1,0:T(8,128)(2,...) custom-call(s32[8,256]{1,0:T(8,128)} %bitcast.11, f32[8,256]{1,0:T(8,128)} %bitcast.12, ...), custom_call_target="tpu_custom_call" | custom-call | tf_op jit(solution)/shard_map/pallas_call | solution.py:42
  3.2 3.0 %collective-permute-start.3 = (bf16[32,1024]{1,0:T(8,128)(2,1)S(1)}, bf16[32,1024]{1,0:T(8,128)(2,1)S(1)}, u32[]{:S(2)}, u32[]{:S(2)}) collective-permute-start(bf16[32,1024]{1,0:T(8,128)(2,1)S(1)} %get-tuple-element.47), channel_id=1, source_target_pairs={{0,2},{1,3},{2,0},{3,1},{4,6},{5,7},{6,4},{7,5},{8,10},{9,11},{10,... | collective-permute-start | bytes 196616 | tf_op jit(solution)/shard_map/ppermute | solution.py:288
  6.2 0.1 collective-permute-start.2
  6.2 1.9 %collective-permute-start.13 = (bf16[64,1024]{1,0:T(8,128)(2,1)S(1)}, bf16[64,1024]{1,0:T(8,128)(2,1)S(1)}, u32[]{:S(2)}, u32[]{:S(2)}) collective-permute-start(bf16[64,1024]{1,0:T(8,128)(2,1)S(1)} %get-tuple-element.61), channel_id=1, source_target_pairs={{0,2},{1,3},{2,0},{3,1},{4,6},{5,7},{6,4},{7,5},{8,10},{9,11},{10,... | collective-permute-start | bytes 393224 | tf_op jit(solution)/shard_map/ppermute | solution.py:288
  8.2 0.0 collective-permute-done.1.refs_3_.refs_5_
  8.2 0.0 collective-permute-done.refs_5_.refs_3_
  8.2 0.4 collective-permute-done.3.refs_1_
  8.6 4.4 %collective-permute-start.4 = (bf16[16,2048]{1,0:T(8,128)(2,1)S(1)}, bf16[16,2048]{1,0:T(8,128)(2,1)S(1)}, u32[]{:S(2)}, u32[]{:S(2)}) collective-permute-start(bf16[16,2048]{1,0:T(8,128)(2,1)S(1)} %get-tuple-element.48), channel_id=1, source_target_pairs={{0,12},{4,8},{8,4},{12,0},{1,13},{5,9},{9,5},{13,1},{2,14},{6,10},... | collective-permute-start | bytes 196616 | tf_op jit(solution)/shard_map/ppermute | solution.py:294
  13.0 0.0 collective-permute-start.5
  13.0 0.0 collective-permute-done.2.refs_1_
  13.0 0.7 %collective-permute-start.6 = (bf16[16,2048]{1,0:T(8,128)(2,1)S(1)}, bf16[16,2048]{1,0:T(8,128)(2,1)S(1)}, u32[]{:S(2)}, u32[]{:S(2)}) collective-permute-start(bf16[16,2048]{1,0:T(8,128)(2,1)S(1)} %get-tuple-element.50), channel_id=1, source_target_pairs={{0,4},{4,0},{8,12},{12,8},{1,5},{5,1},{9,13},{13,9},{2,6},{6,2},{1... | collective-permute-start | bytes 196616 | tf_op jit(solution)/shard_map/ppermute | solution.py:294
  13.7 0.0 collective-permute-done.13.refs_1_
  13.7 3.8 %collective-permute-start.14 = (bf16[16,2048]{1,0:T(8,128)(2,1)S(1)}, bf16[16,2048]{1,0:T(8,128)(2,1)S(1)}, u32[]{:S(2)}, u32[]{:S(2)}) collective-permute-start(bf16[16,2048]{1,0:T(8,128)(2,1)S(1)} %get-tuple-element.63), channel_id=1, source_target_pairs={{0,12},{4,8},{8,4},{12,0},{1,13},{5,9},{9,5},{13,1},{2,14},{6,10},... | collective-permute-start | bytes 196616 | tf_op jit(solution)/shard_map/ppermute | solution.py:294
  17.6 0.6 %collective-permute-start.16 = (bf16[16,2048]{1,0:T(8,128)(2,1)S(1)}, bf16[16,2048]{1,0:T(8,128)(2,1)S(1)}, u32[]{:S(2)}, u32[]{:S(2)}) collective-permute-start(bf16[16,2048]{1,0:T(8,128)(2,1)S(1)} %get-tuple-element.65), channel_id=1, source_target_pairs={{0,4},{4,0},{8,12},{12,8},{1,5},{5,1},{9,13},{13,9},{2,6},{6,2},{1... | collective-permute-start | bytes 196616 | tf_op jit(solution)/shard_map/ppermute | solution.py:294
  18.2 3.3 %collective-permute-done.5.refs_2_ = bf16[16,2048]{1,0:T(8,128)(2,1)S(1)} collective-permute-done((bf16[16,2048]{1,0:T(8,128)(2,1)S(1)}, bf16[16,2048]{1,0:T(8,128)(2,1)S(1)}, u32[]{:S(2)}, u32[]{:S(2)}) %collective-permute-start.5) | collective-permute-done | bytes 65568 | tf_op jit(solution)/shard_map/ppermute | solution.py:294
  21.5 0.6 %shard_map.97 = (f32[64,1536]{1,0:T(8,128)S(1)}, bf16[64,1536]{1,0:T(8,128)(2,1)S(1)}) custom-call(bf16[16,2048]{1,0:T(8,128)(2,1)S(1)} %get-tuple-element.46.refs_0_, bf16[16,2048]{1,0:T(8,128)(2,1)S(1)} %collective-permute-done.4.refs_1_, bf16[16,2048]{1,0:T(8,128)(2,1)S(1)} %collective-permute-done.5.refs_2_, ...), custom_call_target="tpu_custom_call" | custom-call | flops 4499999744 | tf_op jit(solution)/shard_map/pallas_call | solution.py:42
  22.1 1.1 %collective-permute-start.7 = (bf16[64,1536]{1,0:T(8,128)(2,1)S(1)}, bf16[64,1536]{1,0:T(8,128)(2,1)S(1)}, u32[]{:S(2)}, u32[]{:S(2)}) collective-permute-start(bf16[64,1536]{1,0:T(8,128)(2,1)S(1)} %get-tuple-element.53), channel_id=1, source_target_pairs={{0,2},{1,3},{2,0},{3,1},{4,6},{5,7},{6,4},{7,5},{8,10},{9,11},{10,... | collective-permute-start | bytes 589832 | tf_op jit(solution)/shard_map/ppermute | solution.py:288
  23.2 0.3 collective-permute-done.15.refs_2_
  23.6 0.4 shard_map.103
  24.0 1.6 %collective-permute-start.17 = (bf16[64,768]{1,0:T(8,128)(2,1)S(1)}, bf16[64,768]{1,0:T(8,128)(2,1)S(1)}, u32[]{:S(2)}, u32[]{:S(2)}) collective-permute-start(bf16[64,768]{1,0:T(8,128)(2,1)S(1)} %get-tuple-element.67), channel_id=1, source_target_pairs={{0,2},{1,3},{2,0},{3,1},{4,6},{5,7},{6,4},{7,5},{8,10},{9,11},{10,... | collective-permute-start | bytes 294920 | tf_op jit(solution)/shard_map/ppermute | solution.py:288
  25.5 4.2 %collective-permute-done.7.refs_1_ = bf16[64,1536]{1,0:T(8,128)(2,1)S(1)} collective-permute-done((bf16[64,1536]{1,0:T(8,128)(2,1)S(1)}, bf16[64,1536]{1,0:T(8,128)(2,1)S(1)}, u32[]{:S(2)}, u32[]{:S(2)}) %collective-permute-start.7) | collective-permute-done | bytes 196640 | tf_op jit(solution)/shard_map/ppermute | solution.py:288
  29.7 0.1 shard_map.98.refs_0_.refs_4_.refs_2_
  29.8 1.3 %collective-permute-start.8 = (bf16[64,768]{1,0:T(8,128)(2,1)S(1)}, bf16[64,768]{1,0:T(8,128)(2,1)S(1)}, u32[]{:S(2)}, u32[]{:S(2)}) collective-permute-start(bf16[64,768]{1,0:T(8,128)(2,1)S(1)} %shard_map.98.refs_0_.refs_4_.refs_2_), channel_id=1, source_target_pairs={{0,2},{1,3},{2,0},{3,1},{4,6},{5,7},{6,4},{7,5},{8,10},{9,11},{10,... | collective-permute-start | bytes 294920 | tf_op jit(solution)/shard_map/ppermute | solution.py:288
  31.1 0.1 collective-permute-done.17.refs_3_
  31.2 0.1 shard_map.104.refs_0_
  31.3 1.1 %collective-permute-start.18 = (bf16[64,1536]{1,0:T(8,128)(2,1)S(1)}, bf16[64,1536]{1,0:T(8,128)(2,1)S(1)}, u32[]{:S(2)}, u32[]{:S(2)}) collective-permute-start(bf16[64,1536]{1,0:T(8,128)(2,1)S(1)} %shard_map.104.refs_0_), channel_id=1, source_target_pairs={{0,2},{1,3},{2,0},{3,1},{4,6},{5,7},{6,4},{7,5},{8,10},{9,11},{10,... | collective-permute-start | bytes 589832 | tf_op jit(solution)/shard_map/ppermute | solution.py:288
  32.3 2.1 %collective-permute-done.8.refs_1_.refs_3_ = bf16[64,768]{1,0:T(8,128)(2,1)S(1)} collective-permute-done((bf16[64,768]{1,0:T(8,128)(2,1)S(1)}, bf16[64,768]{1,0:T(8,128)(2,1)S(1)}, u32[]{:S(2)}, u32[]{:S(2)}) %collective-permute-start.8) | collective-permute-done | bytes 98336 | tf_op jit(solution)/shard_map/ppermute | solution.py:288
  34.4 0.6 %shard_map.99 = (bf16[32,1024]{1,0:T(8,128)(2,1)S(1)}, bf16[32,1024]{1,0:T(8,128)(2,1)S(1)}, bf16[32,1024]{1,0:T(8,128)(2,1)S(1)}, bf16[32,1024]{1,0:T(8,128)(2,1)S(1)}) custom-call(bf16[64,768]{1,0:T(8,128)(2,1)S(1)} %shard_map.98.refs_0_.refs_4_.refs_2_, bf16[64,768]{1,0:T(8,128)(2,1)S(1)} %collective-permute-done.8.refs_1_.refs_3_, ...), custom_call_target="tpu_custom_call" | custom-call | flops 2000000000 | tf_op jit(solution)/shard_map/pallas_call | solution.py:42
  35.1 0.1 collective-permute-start.9
  35.2 0.1 collective-permute-start.10
  35.3 0.1 collective-permute-start.20
  35.3 4.2 %collective-permute-start.11 = (bf16[32,1024]{1,0:T(8,128)(2,1)S(1)}, bf16[32,1024]{1,0:T(8,128)(2,1)S(1)}, u32[]{:S(2)}, u32[]{:S(2)}) collective-permute-start(bf16[32,1024]{1,0:T(8,128)(2,1)S(1)} %get-tuple-element.58), channel_id=1, source_target_pairs={{0,4},{4,0},{8,12},{12,8},{1,5},{5,1},{9,13},{13,9},{2,6},{6,2},{1... | collective-permute-start | bytes 196616 | tf_op jit(solution)/shard_map/ppermute | solution.py:294
  39.6 1.1 %shard_map.105 = (bf16[64,1024]{1,0:T(8,128)(2,1)S(1)}, bf16[64,1024]{1,0:T(8,128)(2,1)S(1)}) custom-call(bf16[64,1536]{1,0:T(8,128)(2,1)S(1)} %shard_map.104.refs_0_, bf16[64,1536]{1,0:T(8,128)(2,1)S(1)} %collective-permute-done.18.refs_1_, bf16[512,1536]{1,0:T(8,128)(2,1)S(1)} %bitcast.7, bf16[512,1536]{1,0:T(8,128)(2,1)S(1)} %collective-permute-done.refs_5_.refs_3_), custom_call_target="tpu_custom_call" | custom-call | tf_op jit(solution)/shard_map/pallas_call | solution.py:42
  40.7 1.3 %collective-permute-start.19 = (bf16[64,1024]{1,0:T(8,128)(2,1)S(1)}, bf16[64,1024]{1,0:T(8,128)(2,1)S(1)}, u32[]{:S(2)}, u32[]{:S(2)}) collective-permute-start(bf16[64,1024]{1,0:T(8,128)(2,1)S(1)} %get-tuple-element.69), channel_id=1, source_target_pairs={{0,2},{1,3},{2,0},{3,1},{4,6},{5,7},{6,4},{7,5},{8,10},{9,11},{10,... | collective-permute-start | bytes 393224 | tf_op jit(solution)/shard_map/ppermute | solution.py:288
  42.0 0.5 collective-permute-start.22
  42.5 0.2 collective-permute-done.11.refs_3_.refs_5_
  42.8 1.3 %collective-permute-start.12 = (bf16[64,1024]{1,0:T(8,128)(2,1)S(1)}, bf16[64,1024]{1,0:T(8,128)(2,1)S(1)}, u32[]{:S(2)}, u32[]{:S(2)}) collective-permute-start(bf16[64,1024]{1,0:T(8,128)(2,1)S(1)} %shard_map.100), channel_id=1, source_target_pairs={{0,2},{1,3},{2,0},{3,1},{4,6},{5,7},{6,4},{7,5},{8,10},{9,11},{10,... | collective-permute-start | bytes 393224 | tf_op jit(solution)/shard_map/ppermute | solution.py:288
  44.1 1.6 %shard_map.106 = (f32[512,768]{1,0:T(8,128)}, f32[8,128]{1,0:T(8,128)S(1)}) custom-call(bf16[128,512]{1,0:T(8,128)(2,1)S(1)} %get-tuple-element.70.refs_0_, bf16[128,512]{1,0:T(8,128)(2,1)S(1)} %collective-permute-done.20.refs_1_, bf16[64,768]{1,0:T(8,128)(2,1)S(1)} %shard_map.98.refs_0_.refs_4_.refs_2_, ...), custom_call_target="tpu_custom_call" | custom-call | tf_op jit(solution)/shard_map/pallas_call | solution.py:42
  45.6 1.4 %collective-permute-done.19.refs_1_ = bf16[64,1024]{1,0:T(8,128)(2,1)S(1)} collective-permute-done((bf16[64,1024]{1,0:T(8,128)(2,1)S(1)}, bf16[64,1024]{1,0:T(8,128)(2,1)S(1)}, u32[]{:S(2)}, u32[]{:S(2)}) %collective-permute-start.19) | collective-permute-done | bytes 131104 | tf_op jit(solution)/shard_map/ppermute | solution.py:288
  47.1 0.1 collective-permute-start.23
  47.2 1.3 %collective-permute-start.24 = (bf16[16,2048]{1,0:T(8,128)(2,1)S(1)}, bf16[16,2048]{1,0:T(8,128)(2,1)S(1)}, u32[]{:S(2)}, u32[]{:S(2)}) collective-permute-start(bf16[16,2048]{1,0:T(8,128)(2,1)S(1)} %get-tuple-element.75), channel_id=1, source_target_pairs={{0,8},{4,12},{8,0},{12,4},{1,9},{5,13},{9,1},{13,5},{2,10},{6,14},... | collective-permute-start | bytes 196616 | tf_op jit(solution)/shard_map/ppermute | solution.py:294
  48.5 3.1 %collective-permute-start.25 = (bf16[16,2048]{1,0:T(8,128)(2,1)S(1)}, bf16[16,2048]{1,0:T(8,128)(2,1)S(1)}, u32[]{:S(2)}, u32[]{:S(2)}) collective-permute-start(bf16[16,2048]{1,0:T(8,128)(2,1)S(1)} %get-tuple-element.76), channel_id=1, source_target_pairs={{0,4},{4,0},{8,12},{12,8},{1,5},{5,1},{9,13},{13,9},{2,6},{6,2},{1... | collective-permute-start | bytes 196616 | tf_op jit(solution)/shard_map/ppermute | solution.py:294
  51.6 1.3 %shard_map.101 = (bf16[256,2048]{1,0:T(8,128)(2,1)}, f32[8,128]{1,0:T(8,128)S(1)}) custom-call(bf16[256,64]{1,0:T(8,128)(2,1)S(1)} %get-tuple-element.41.refs_0_, f32[64,128]{1,0:T(8,128)S(1)} %get-tuple-element.42.refs_1_, bf16[32,1024]{1,0:T(8,128)(2,1)S(1)} %get-tuple-element.55.refs_0_.refs_2_, ...), custom_call_target="tpu_custom_call" | custom-call | tf_op jit(solution)/shard_map/pallas_call | solution.py:42
  52.9 0.5 collective-permute-done.23.refs_2_
  53.4 1.6 %collective-permute-done.24.refs_3_ = bf16[16,2048]{1,0:T(8,128)(2,1)S(1)} collective-permute-done((bf16[16,2048]{1,0:T(8,128)(2,1)S(1)}, bf16[16,2048]{1,0:T(8,128)(2,1)S(1)}, u32[]{:S(2)}, u32[]{:S(2)}) %collective-permute-start.24) | collective-permute-done | bytes 65568 | tf_op jit(solution)/shard_map/ppermute | solution.py:294
  54.9 1.2 %shard_map.108 = bf16[256,2048]{1,0:T(8,128)(2,1)} custom-call(bf16[256,64]{1,0:T(8,128)(2,1)S(1)} %get-tuple-element.41.refs_0_, bf16[16,2048]{1,0:T(8,128)(2,1)S(1)} %get-tuple-element.73.refs_1_, bf16[16,2048]{1,0:T(8,128)(2,1)S(1)} %collective-permute-done.23.refs_2_, bf16[16,2048]{1,0:T(8,128)(2,1)S(1)} %collective-permute-done.24.refs_3_, ...), custom_call_target="tpu_custom_call" | custom-call | tf_op jit(solution)/shard_map/pallas_call | solution.py:42
  (23 shorter events, 0.1 us)
Async XLA Ops:
  0.6 7.6 %collective-permute-start = (bf16[512,1536]{1,0:T(8,128)(2,1)}, bf16[512,1536]{1,0:T(8,128)(2,1)S(1)}, u32[]{:S(2)}, u32[]{:S(2)}) collective-permute-start(bf16[512,1536]{1,0:T(8,128)(2,1)} %bitcast.5), channel_id=1, source_target_pairs={{0,1},{1,0},{2,3},{3,2},{4,5},{5,4},{6,7},{7,6},{8,9},{9,8},{10,11... | collective-permute-start | bytes 4718600 | tf_op jit(solution)/shard_map/ppermute | solution.py:284
  1.1 7.0 %collective-permute-start.1 = (bf16[512,768]{1,0:T(8,128)(2,1)}, bf16[512,768]{1,0:T(8,128)(2,1)S(1)}, u32[]{:S(2)}, u32[]{:S(2)}) collective-permute-start(bf16[512,768]{1,0:T(8,128)(2,1)} %bitcast.8), channel_id=1, source_target_pairs={{0,1},{1,0},{2,3},{3,2},{4,5},{5,4},{6,7},{7,6},{8,9},{9,8},{10,11... | collective-permute-start | bytes 2359304 | tf_op jit(solution)/shard_map/ppermute | solution.py:284
  3.2 5.5 %collective-permute-start.3 = (bf16[32,1024]{1,0:T(8,128)(2,1)S(1)}, bf16[32,1024]{1,0:T(8,128)(2,1)S(1)}, u32[]{:S(2)}, u32[]{:S(2)}) collective-permute-start(bf16[32,1024]{1,0:T(8,128)(2,1)S(1)} %get-tuple-element.47), channel_id=1, source_target_pairs={{0,2},{1,3},{2,0},{3,1},{4,6},{5,7},{6,4},{7,5},{8,10},{9,11},{10,... | collective-permute-start | bytes 196616 | tf_op jit(solution)/shard_map/ppermute | solution.py:288
  6.2 6.8 %collective-permute-start.2 = (bf16[32,1024]{1,0:T(8,128)(2,1)S(1)}, bf16[32,1024]{1,0:T(8,128)(2,1)S(1)}, u32[]{:S(2)}, u32[]{:S(2)}) collective-permute-start(bf16[32,1024]{1,0:T(8,128)(2,1)S(1)} %get-tuple-element.45), channel_id=1, source_target_pairs={{0,2},{1,3},{2,0},{3,1},{4,6},{5,7},{6,4},{7,5},{8,10},{9,11},{10,... | collective-permute-start | bytes 196616 | tf_op jit(solution)/shard_map/ppermute | solution.py:288
  6.2 7.5 %collective-permute-start.13 = (bf16[64,1024]{1,0:T(8,128)(2,1)S(1)}, bf16[64,1024]{1,0:T(8,128)(2,1)S(1)}, u32[]{:S(2)}, u32[]{:S(2)}) collective-permute-start(bf16[64,1024]{1,0:T(8,128)(2,1)S(1)} %get-tuple-element.61), channel_id=1, source_target_pairs={{0,2},{1,3},{2,0},{3,1},{4,6},{5,7},{6,4},{7,5},{8,10},{9,11},{10,... | collective-permute-start | bytes 393224 | tf_op jit(solution)/shard_map/ppermute | solution.py:288
  8.2 13.3 %copy-start = (bf16[1,512,1536]{2,1,0:T(8,128)(2,1)S(1)}, bf16[1,512,1536]{2,1,0:T(8,128)(2,1)}, u32[]{:S(2)}) copy-start(bf16[1,512,1536]{2,1,0:T(8,128)(2,1)} %param.12) | copy-start | bytes 4718596
  8.6 8.9 %collective-permute-start.4 = (bf16[16,2048]{1,0:T(8,128)(2,1)S(1)}, bf16[16,2048]{1,0:T(8,128)(2,1)S(1)}, u32[]{:S(2)}, u32[]{:S(2)}) collective-permute-start(bf16[16,2048]{1,0:T(8,128)(2,1)S(1)} %get-tuple-element.48), channel_id=1, source_target_pairs={{0,12},{4,8},{8,4},{12,0},{1,13},{5,9},{9,5},{13,1},{2,14},{6,10},... | collective-permute-start | bytes 196616 | tf_op jit(solution)/shard_map/ppermute | solution.py:294
  13.0 8.5 %collective-permute-start.5 = (bf16[16,2048]{1,0:T(8,128)(2,1)S(1)}, bf16[16,2048]{1,0:T(8,128)(2,1)S(1)}, u32[]{:S(2)}, u32[]{:S(2)}) collective-permute-start(bf16[16,2048]{1,0:T(8,128)(2,1)S(1)} %get-tuple-element.49), channel_id=1, source_target_pairs={{0,8},{4,12},{8,0},{12,4},{1,9},{5,13},{9,1},{13,5},{2,10},{6,14},... | collective-permute-start | bytes 196616 | tf_op jit(solution)/shard_map/ppermute | solution.py:294
  13.0 8.5 %collective-permute-start.6 = (bf16[16,2048]{1,0:T(8,128)(2,1)S(1)}, bf16[16,2048]{1,0:T(8,128)(2,1)S(1)}, u32[]{:S(2)}, u32[]{:S(2)}) collective-permute-start(bf16[16,2048]{1,0:T(8,128)(2,1)S(1)} %get-tuple-element.50), channel_id=1, source_target_pairs={{0,4},{4,0},{8,12},{12,8},{1,5},{5,1},{9,13},{13,9},{2,6},{6,2},{1... | collective-permute-start | bytes 196616 | tf_op jit(solution)/shard_map/ppermute | solution.py:294
  13.7 9.5 %collective-permute-start.14 = (bf16[16,2048]{1,0:T(8,128)(2,1)S(1)}, bf16[16,2048]{1,0:T(8,128)(2,1)S(1)}, u32[]{:S(2)}, u32[]{:S(2)}) collective-permute-start(bf16[16,2048]{1,0:T(8,128)(2,1)S(1)} %get-tuple-element.63), channel_id=1, source_target_pairs={{0,12},{4,8},{8,4},{12,0},{1,13},{5,9},{9,5},{13,1},{2,14},{6,10},... | collective-permute-start | bytes 196616 | tf_op jit(solution)/shard_map/ppermute | solution.py:294
  17.5 6.0 %collective-permute-start.15 = (bf16[16,2048]{1,0:T(8,128)(2,1)S(1)}, bf16[16,2048]{1,0:T(8,128)(2,1)S(1)}, u32[]{:S(2)}, u32[]{:S(2)}) collective-permute-start(bf16[16,2048]{1,0:T(8,128)(2,1)S(1)} %get-tuple-element.64), channel_id=1, source_target_pairs={{0,8},{4,12},{8,0},{12,4},{1,9},{5,13},{9,1},{13,5},{2,10},{6,14},... | collective-permute-start | bytes 196616 | tf_op jit(solution)/shard_map/ppermute | solution.py:294
  17.6 6.0 %collective-permute-start.16 = (bf16[16,2048]{1,0:T(8,128)(2,1)S(1)}, bf16[16,2048]{1,0:T(8,128)(2,1)S(1)}, u32[]{:S(2)}, u32[]{:S(2)}) collective-permute-start(bf16[16,2048]{1,0:T(8,128)(2,1)S(1)} %get-tuple-element.65), channel_id=1, source_target_pairs={{0,4},{4,0},{8,12},{12,8},{1,5},{5,1},{9,13},{13,9},{2,6},{6,2},{1... | collective-permute-start | bytes 196616 | tf_op jit(solution)/shard_map/ppermute | solution.py:294
  21.5 2.1 %copy-start.1 = (bf16[1,512,768]{2,1,0:T(8,128)(2,1)S(1)}, bf16[1,512,768]{2,1,0:T(8,128)(2,1)}, u32[]{:S(2)}) copy-start(bf16[1,512,768]{2,1,0:T(8,128)(2,1)} %param.13) | copy-start | bytes 2359300
  22.1 7.6 %collective-permute-start.7 = (bf16[64,1536]{1,0:T(8,128)(2,1)S(1)}, bf16[64,1536]{1,0:T(8,128)(2,1)S(1)}, u32[]{:S(2)}, u32[]{:S(2)}) collective-permute-start(bf16[64,1536]{1,0:T(8,128)(2,1)S(1)} %get-tuple-element.53), channel_id=1, source_target_pairs={{0,2},{1,3},{2,0},{3,1},{4,6},{5,7},{6,4},{7,5},{8,10},{9,11},{10,... | collective-permute-start | bytes 589832 | tf_op jit(solution)/shard_map/ppermute | solution.py:288
  24.0 7.2 %collective-permute-start.17 = (bf16[64,768]{1,0:T(8,128)(2,1)S(1)}, bf16[64,768]{1,0:T(8,128)(2,1)S(1)}, u32[]{:S(2)}, u32[]{:S(2)}) collective-permute-start(bf16[64,768]{1,0:T(8,128)(2,1)S(1)} %get-tuple-element.67), channel_id=1, source_target_pairs={{0,2},{1,3},{2,0},{3,1},{4,6},{5,7},{6,4},{7,5},{8,10},{9,11},{10,... | collective-permute-start | bytes 294920 | tf_op jit(solution)/shard_map/ppermute | solution.py:288
  29.8 4.7 %collective-permute-start.8 = (bf16[64,768]{1,0:T(8,128)(2,1)S(1)}, bf16[64,768]{1,0:T(8,128)(2,1)S(1)}, u32[]{:S(2)}, u32[]{:S(2)}) collective-permute-start(bf16[64,768]{1,0:T(8,128)(2,1)S(1)} %shard_map.98.refs_0_.refs_4_.refs_2_), channel_id=1, source_target_pairs={{0,2},{1,3},{2,0},{3,1},{4,6},{5,7},{6,4},{7,5},{8,10},{9,11},{10,... | collective-permute-start | bytes 294920 | tf_op jit(solution)/shard_map/ppermute | solution.py:288
  31.3 8.3 %collective-permute-start.18 = (bf16[64,1536]{1,0:T(8,128)(2,1)S(1)}, bf16[64,1536]{1,0:T(8,128)(2,1)S(1)}, u32[]{:S(2)}, u32[]{:S(2)}) collective-permute-start(bf16[64,1536]{1,0:T(8,128)(2,1)S(1)} %shard_map.104.refs_0_), channel_id=1, source_target_pairs={{0,2},{1,3},{2,0},{3,1},{4,6},{5,7},{6,4},{7,5},{8,10},{9,11},{10,... | collective-permute-start | bytes 589832 | tf_op jit(solution)/shard_map/ppermute | solution.py:288
  35.1 6.9 %collective-permute-start.9 = (bf16[32,1024]{1,0:T(8,128)(2,1)S(1)}, bf16[32,1024]{1,0:T(8,128)(2,1)S(1)}, u32[]{:S(2)}, u32[]{:S(2)}) collective-permute-start(bf16[32,1024]{1,0:T(8,128)(2,1)S(1)} %get-tuple-element.56), channel_id=1, source_target_pairs={{0,12},{4,8},{8,4},{12,0},{1,13},{5,9},{9,5},{13,1},{2,14},{6,10},... | collective-permute-start | bytes 196616 | tf_op jit(solution)/shard_map/ppermute | solution.py:294
  35.2 6.8 %collective-permute-start.10 = (bf16[32,1024]{1,0:T(8,128)(2,1)S(1)}, bf16[32,1024]{1,0:T(8,128)(2,1)S(1)}, u32[]{:S(2)}, u32[]{:S(2)}) collective-permute-start(bf16[32,1024]{1,0:T(8,128)(2,1)S(1)} %get-tuple-element.57), channel_id=1, source_target_pairs={{0,8},{4,12},{8,0},{12,4},{1,9},{5,13},{9,1},{13,5},{2,10},{6,14},... | collective-permute-start | bytes 196616 | tf_op jit(solution)/shard_map/ppermute | solution.py:294
  35.3 8.8 %collective-permute-start.20 = (bf16[128,512]{1,0:T(8,128)(2,1)S(1)}, bf16[128,512]{1,0:T(8,128)(2,1)S(1)}, u32[]{:S(2)}, u32[]{:S(2)}) collective-permute-start(bf16[128,512]{1,0:T(8,128)(2,1)S(1)} %get-tuple-element.71), channel_id=1, source_target_pairs={{0,1},{1,0},{2,3},{3,2},{4,5},{5,4},{6,7},{7,6},{8,9},{9,8},{10,11... | collective-permute-start | bytes 393224 | tf_op jit(solution)/shard_map/ppermute | solution.py:284
  35.3 7.4 %collective-permute-start.11 = (bf16[32,1024]{1,0:T(8,128)(2,1)S(1)}, bf16[32,1024]{1,0:T(8,128)(2,1)S(1)}, u32[]{:S(2)}, u32[]{:S(2)}) collective-permute-start(bf16[32,1024]{1,0:T(8,128)(2,1)S(1)} %get-tuple-element.58), channel_id=1, source_target_pairs={{0,4},{4,0},{8,12},{12,8},{1,5},{5,1},{9,13},{13,9},{2,6},{6,2},{1... | collective-permute-start | bytes 196616 | tf_op jit(solution)/shard_map/ppermute | solution.py:294
  40.7 6.4 %collective-permute-start.19 = (bf16[64,1024]{1,0:T(8,128)(2,1)S(1)}, bf16[64,1024]{1,0:T(8,128)(2,1)S(1)}, u32[]{:S(2)}, u32[]{:S(2)}) collective-permute-start(bf16[64,1024]{1,0:T(8,128)(2,1)S(1)} %get-tuple-element.69), channel_id=1, source_target_pairs={{0,2},{1,3},{2,0},{3,1},{4,6},{5,7},{6,4},{7,5},{8,10},{9,11},{10,... | collective-permute-start | bytes 393224 | tf_op jit(solution)/shard_map/ppermute | solution.py:288
  42.0 2.1 %collective-permute-start.21 = (bf16[64,768]{1,0:T(8,128)(2,1)S(1)}, bf16[64,768]{1,0:T(8,128)(2,1)S(1)}, u32[]{:S(2)}, u32[]{:S(2)}) collective-permute-start(bf16[64,768]{1,0:T(8,128)(2,1)S(1)} %shard_map.98.refs_0_.refs_4_.refs_2_), channel_id=1, source_target_pairs={{0,1},{1,0},{2,3},{3,2},{4,5},{5,4},{6,7},{7,6},{8,9},{9,8},{10,11... | collective-permute-start | bytes 294920 | tf_op jit(solution)/shard_map/ppermute | solution.py:284
  42.0 2.1 %collective-permute-start.22 = (bf16[64,768]{1,0:T(8,128)(2,1)S(1)}, bf16[64,768]{1,0:T(8,128)(2,1)S(1)}, u32[]{:S(2)}, u32[]{:S(2)}) collective-permute-start(bf16[64,768]{1,0:T(8,128)(2,1)S(1)} %collective-permute-done.8.refs_1_.refs_3_), channel_id=1, source_target_pairs={{0,1},{1,0},{2,3},{3,2},{4,5},{5,4},{6,7},{7,6},{8,9},{9,8},{10,11... | collective-permute-start | bytes 294920 | tf_op jit(solution)/shard_map/ppermute | solution.py:284
  42.8 8.8 %collective-permute-start.12 = (bf16[64,1024]{1,0:T(8,128)(2,1)S(1)}, bf16[64,1024]{1,0:T(8,128)(2,1)S(1)}, u32[]{:S(2)}, u32[]{:S(2)}) collective-permute-start(bf16[64,1024]{1,0:T(8,128)(2,1)S(1)} %shard_map.100), channel_id=1, source_target_pairs={{0,2},{1,3},{2,0},{3,1},{4,6},{5,7},{6,4},{7,5},{8,10},{9,11},{10,... | collective-permute-start | bytes 393224 | tf_op jit(solution)/shard_map/ppermute | solution.py:288
  47.1 6.2 %collective-permute-start.23 = (bf16[16,2048]{1,0:T(8,128)(2,1)S(1)}, bf16[16,2048]{1,0:T(8,128)(2,1)S(1)}, u32[]{:S(2)}, u32[]{:S(2)}) collective-permute-start(bf16[16,2048]{1,0:T(8,128)(2,1)S(1)} %get-tuple-element.74), channel_id=1, source_target_pairs={{0,12},{4,8},{8,4},{12,0},{1,13},{5,9},{9,5},{13,1},{2,14},{6,10},... | collective-permute-start | bytes 196616 | tf_op jit(solution)/shard_map/ppermute | solution.py:294
  47.2 7.7 %collective-permute-start.24 = (bf16[16,2048]{1,0:T(8,128)(2,1)S(1)}, bf16[16,2048]{1,0:T(8,128)(2,1)S(1)}, u32[]{:S(2)}, u32[]{:S(2)}) collective-permute-start(bf16[16,2048]{1,0:T(8,128)(2,1)S(1)} %get-tuple-element.75), channel_id=1, source_target_pairs={{0,8},{4,12},{8,0},{12,4},{1,9},{5,13},{9,1},{13,5},{2,10},{6,14},... | collective-permute-start | bytes 196616 | tf_op jit(solution)/shard_map/ppermute | solution.py:294
  48.5 6.5 %collective-permute-start.25 = (bf16[16,2048]{1,0:T(8,128)(2,1)S(1)}, bf16[16,2048]{1,0:T(8,128)(2,1)S(1)}, u32[]{:S(2)}, u32[]{:S(2)}) collective-permute-start(bf16[16,2048]{1,0:T(8,128)(2,1)S(1)} %get-tuple-element.76), channel_id=1, source_target_pairs={{0,4},{4,0},{8,12},{12,8},{1,5},{5,1},{9,13},{13,9},{2,6},{6,2},{1... | collective-permute-start | bytes 196616 | tf_op jit(solution)/shard_map/ppermute | solution.py:294

commit v19 on v17

--- a/solution.py
+++ b/solution.py
@@ -115,8 +115,23 @@
         outs[0][:, cols] = value
 
 
-def flip(chunks):
-    return [chunks[0], *chunks[:0:-1]]
+def farthest_first(groups):
+    return [groups - 1, *range(1, groups - 1)]
+
+
+def far_half_first(groups):
+    return [*range(groups // 2, groups), *range(1, groups // 2)]
+
+
+def arrange(chunks, order):
+    return [chunks[0], *[chunks[ke] for ke in order(len(chunks))]]
+
+
+def restore(chunks, order):
+    out = list(chunks)
+    for i, ke in enumerate(order(len(chunks))):
+        out[ke] = chunks[i + 1]
+    return out
 
 
 def join_kernel(groups, spread, capacity, first, *refs):
@@ -129,7 +144,7 @@
 
 
 def far_kernel(groups, spread, capacity, *refs):
-    by_e, by_x = flip(refs[:groups]), refs[groups:]
+    by_e, by_x = restore(refs[:groups], far_half_first), refs[groups:]
     for ke in range(groups):
         for kx in range(1, spread):
             by_x[kx - 1][ke * capacity : (ke + 1) * capacity] = by_e[ke][
@@ -138,7 +153,7 @@
 
 
 def partial(groups, spread, refs, outs):
-    chunks, (own, sib) = flip(refs[:groups]), refs[groups:]
+    chunks, (own, sib) = restore(refs[:groups], farthest_first), refs[groups:]
     part = own.shape[0]
     half = CORES * part
     rows = jnp.concatenate(
@@ -239,7 +254,8 @@
 
 
 def combine_kernel(groups, parts, capacity, turned, gate, *refs):
-    chunks, far, (out, held, sems) = flip(refs[:groups]), refs[groups:-3], refs[-3:]
+    chunks, far, (out, held, sems) = refs[:groups], refs[groups:-3], refs[-3:]
+    chunks = restore(chunks, far_half_first)
     part = held.shape[2]
 
     def weighted(k):
@@ -257,7 +273,7 @@
 
 
 def d_tokens_kernel(groups, parts, turned, *refs):
-    chunks, (out, held, sems) = flip(refs[:groups]), refs[groups:]
+    chunks, (out, held, sems) = restore(refs[:groups], far_half_first), refs[groups:]
     part = held.shape[2]
     rows = (
         jnp.concatenate([c[:, k * part : (k + 1) * part] for c in chunks], axis=0)
@@ -335,7 +351,7 @@
     pre, *pre_far = call(
         bound(pre_kernel, groups, spread),
         [shape((slots, 2 * feed), F32)] + [shape((slots, 2 * feed))] * (spread - 1),
-        (*flip(rows), in_own, in_sib),
+        (*arrange(rows, farthest_first), in_own, in_sib),
         cost=PRE_COST,
     )
     pre = (pre, *to_x(pre_far))
@@ -346,7 +362,7 @@
         [shape((spread * slots, part))] * 2
         + [shape((slots, feed), F32)]
         + [shape((slots, feed))] * (spread - 1),
-        (*flip(grads), out_own, out_sib),
+        (*arrange(grads, farthest_first), out_own, out_sib),
         cost=BACK_COST,
     )
     back = (back, *to_x(back_far))
@@ -367,7 +383,7 @@
     )
     d_rows = to_expert(call(join, chunk, (near, *to_x(far))))
     far = to_x(
-        call(bound(far_kernel, groups, spread, capacity), by_x[1:], flip(expert_out))
+        call(bound(far_kernel, groups, spread, capacity), by_x[1:], arrange(expert_out, far_half_first))
     )
     d_w_out, token = call(
         bound(weight_kernel, spread),
@@ -392,12 +408,12 @@
 
     combined, token = scattered(
         bound(combine_kernel, groups, parts, capacity),
-        (turned, gate, *flip(expert_out), *far),
+        (turned, gate, *arrange(expert_out, far_half_first), *far),
         after=(token,),
         token=True,
     )
     (d_tokens,) = scattered(
-        bound(d_tokens_kernel, groups, parts), (turned, *flip(d_rows)), after=(token,)
+        bound(d_tokens_kernel, groups, parts), (turned, *arrange(d_rows, far_half_first)), after=(token,)
     )
     return combined, d_tokens, d_w_out[None]
 

time: 55.1 us -> 53.8 us (0.976)
  waiting for transfers between devices: 13.3 us -> 8.71 us
  starting transfers between devices: 31.7 us -> 35.1 us
    ppermute x9, waiting for transfers between devices: 9.68 us -> 3.71 us  [to_x(): lax.ppermute(value, 'fsdp', [(i, i ^ (k + 1) * CORES) for i in range(part...]
    ppermute x9, starting transfers between devices: 12.2 us -> 16.9 us  [to_x(): lax.ppermute(value, 'fsdp', [(i, i ^ (k + 1) * CORES) for i in range(part...]
    ppermute x12, waiting for transfers between devices: 3.65 us -> 4.98 us  [to_expert(): lax.ppermute(value, 'expert', [(i, i ^ ke) for i in range(groups)])]
    ppermute x12, starting transfers between devices: 18.4 us -> 17.1 us  [to_expert(): lax.ppermute(value, 'expert', [(i, i ^ ke) for i in range(groups)])]
  transfers between devices with their start and end apart: 26 -> 26, of which waited for: 7 -> 13; matrix products, arithmetic and copies ran while one was open for 0% -> 0% of each run, Pallas kernels for 14% -> 15%
where the time goes in v19:
time: 53.8 us; the launch traced here: 53.5 us
  starting transfers between devices  35.1 us (65%)
  Pallas kernels  8.99 us (17%)
  waiting for transfers between devices  8.71 us (16%)
  between operations  0.74 us (1%)
    ppermute x12, starting transfers between devices, to_expert(): lax.ppermute(value, 'expert', [(i, i ^ ke) for i in range(groups)])  17.1 us
    ppermute x9, starting transfers between devices, to_x(): lax.ppermute(value, 'fsdp', [(i, i ^ (k + 1) * CORES) for i in range(part...  16.9 us
    pallas_call x15, Pallas kernels, call(): pl.pallas_call(kernel, out_shape=out_shape, in_specs=specs, compiler_para...  8.99 us
    ppermute x12, waiting for transfers between devices, to_expert(): lax.ppermute(value, 'expert', [(i, i ^ ke) for i in range(groups)])  4.98 us
    ppermute x9, waiting for transfers between devices, to_x(): lax.ppermute(value, 'fsdp', [(i, i ^ (k + 1) * CORES) for i in range(part...  3.71 us
    ppermute x5, starting transfers between devices, to_core(): return lax.ppermute(value, 'fsdp', [(i, i ^ 1) for i in range(parts)])  1.11 us
  transfers between devices with their start and end apart: 26, of which 13 were waited for; matrix products, arithmetic and copies ran while one was open for 0% of the time, Pallas kernels for 15%

profile of v19, /device:TPU:0, one launch (start us, length us, event | category | flops | bytes accessed | tf_op | source)
XLA Modules:
  0.0 53.5 jit_solution(4128353060161552583)
XLA Ops:
  0.6 0.5 collective-permute-start
  1.1 0.1 collective-permute-start.1
  1.2 1.9 %shard_map.94 = (bf16[64,1024]{1,0:T(8,128)(2,1)S(1)}, bf16[32,1024]{1,0:T(8,128)(2,1)S(1)}, bf16[32,1024]{1,0:T(8,128)(2,1)S(1)}, bf16[64,1024]{1,0:T(8,128)(2,...) custom-call(s32[8,256]{1,0:T(8,128)} %bitcast.11, f32[8,256]{1,0:T(8,128)} %bitcast.12, ...), custom_call_target="tpu_custom_call" | custom-call | tf_op jit(solution)/shard_map/pallas_call | solution.py:42
  3.2 3.0 %collective-permute-start.3 = (bf16[32,1024]{1,0:T(8,128)(2,1)S(1)}, bf16[32,1024]{1,0:T(8,128)(2,1)S(1)}, u32[]{:S(2)}, u32[]{:S(2)}) collective-permute-start(bf16[32,1024]{1,0:T(8,128)(2,1)S(1)} %get-tuple-element.47), channel_id=1, source_target_pairs={{0,2},{1,3},{2,0},{3,1},{4,6},{5,7},{6,4},{7,5},{8,10},{9,11},{10,... | collective-permute-start | bytes 196616 | tf_op jit(solution)/shard_map/ppermute | solution.py:304
  6.2 0.1 collective-permute-start.2
  6.2 1.9 %collective-permute-start.13 = (bf16[64,1024]{1,0:T(8,128)(2,1)S(1)}, bf16[64,1024]{1,0:T(8,128)(2,1)S(1)}, u32[]{:S(2)}, u32[]{:S(2)}) collective-permute-start(bf16[64,1024]{1,0:T(8,128)(2,1)S(1)} %get-tuple-element.60), channel_id=1, source_target_pairs={{0,2},{1,3},{2,0},{3,1},{4,6},{5,7},{6,4},{7,5},{8,10},{9,11},{10,... | collective-permute-start | bytes 393224 | tf_op jit(solution)/shard_map/ppermute | solution.py:304
  8.2 0.0 collective-permute-done.refs_5_.refs_3_
  8.2 0.4 collective-permute-done.3.refs_1_
  8.6 4.4 %collective-permute-start.4 = (bf16[16,2048]{1,0:T(8,128)(2,1)S(1)}, bf16[16,2048]{1,0:T(8,128)(2,1)S(1)}, u32[]{:S(2)}, u32[]{:S(2)}) collective-permute-start(bf16[16,2048]{1,0:T(8,128)(2,1)S(1)} %get-tuple-element.48), channel_id=1, source_target_pairs={{0,12},{4,8},{8,4},{12,0},{1,13},{5,9},{9,5},{13,1},{2,14},{6,10},... | collective-permute-start | bytes 196616 | tf_op jit(solution)/shard_map/ppermute | solution.py:310
  13.0 0.7 %collective-permute-start.5 = (bf16[16,2048]{1,0:T(8,128)(2,1)S(1)}, bf16[16,2048]{1,0:T(8,128)(2,1)S(1)}, u32[]{:S(2)}, u32[]{:S(2)}) collective-permute-start(bf16[16,2048]{1,0:T(8,128)(2,1)S(1)} %get-tuple-element.49), channel_id=1, source_target_pairs={{0,4},{4,0},{8,12},{12,8},{1,5},{5,1},{9,13},{13,9},{2,6},{6,2},{1... | collective-permute-start | bytes 196616 | tf_op jit(solution)/shard_map/ppermute | solution.py:310
  13.7 3.8 %collective-permute-start.14 = (bf16[16,2048]{1,0:T(8,128)(2,1)S(1)}, bf16[16,2048]{1,0:T(8,128)(2,1)S(1)}, u32[]{:S(2)}, u32[]{:S(2)}) collective-permute-start(bf16[16,2048]{1,0:T(8,128)(2,1)S(1)} %get-tuple-element.62), channel_id=1, source_target_pairs={{0,12},{4,8},{8,4},{12,0},{1,13},{5,9},{9,5},{13,1},{2,14},{6,10},... | collective-permute-start | bytes 196616 | tf_op jit(solution)/shard_map/ppermute | solution.py:310
  17.5 0.0 collective-permute-start.15
  17.6 0.0 collective-permute-done.4.refs_1_
  17.6 0.6 %collective-permute-start.16 = (bf16[16,2048]{1,0:T(8,128)(2,1)S(1)}, bf16[16,2048]{1,0:T(8,128)(2,1)S(1)}, u32[]{:S(2)}, u32[]{:S(2)}) collective-permute-start(bf16[16,2048]{1,0:T(8,128)(2,1)S(1)} %get-tuple-element.64), channel_id=1, source_target_pairs={{0,8},{4,12},{8,0},{12,4},{1,9},{5,13},{9,1},{13,5},{2,10},{6,14},... | collective-permute-start | bytes 196616 | tf_op jit(solution)/shard_map/ppermute | solution.py:310
  18.2 1.2 %collective-permute-done.6.refs_3_ = bf16[16,2048]{1,0:T(8,128)(2,1)S(1)} collective-permute-done((bf16[16,2048]{1,0:T(8,128)(2,1)S(1)}, bf16[16,2048]{1,0:T(8,128)(2,1)S(1)}, u32[]{:S(2)}, u32[]{:S(2)}) %collective-permute-start.6) | collective-permute-done | bytes 65568 | tf_op jit(solution)/shard_map/ppermute | solution.py:310
  19.4 0.0 collective-permute-done.5.refs_2_
  19.4 0.6 %shard_map.97 = (f32[64,1536]{1,0:T(8,128)S(1)}, bf16[64,1536]{1,0:T(8,128)(2,1)S(1)}) custom-call(bf16[16,2048]{1,0:T(8,128)(2,1)S(1)} %get-tuple-element.46.refs_0_, bf16[16,2048]{1,0:T(8,128)(2,1)S(1)} %collective-permute-done.4.refs_1_, bf16[16,2048]{1,0:T(8,128)(2,1)S(1)} %collective-permute-done.5.refs_2_, ...), custom_call_target="tpu_custom_call" | custom-call | flops 4499999744 | tf_op jit(solution)/shard_map/pallas_call | solution.py:42
  20.0 1.8 %collective-permute-start.7 = (bf16[64,1536]{1,0:T(8,128)(2,1)S(1)}, bf16[64,1536]{1,0:T(8,128)(2,1)S(1)}, u32[]{:S(2)}, u32[]{:S(2)}) collective-permute-start(bf16[64,1536]{1,0:T(8,128)(2,1)S(1)} %get-tuple-element.53), channel_id=1, source_target_pairs={{0,2},{1,3},{2,0},{3,1},{4,6},{5,7},{6,4},{7,5},{8,10},{9,11},{10,... | collective-permute-start | bytes 589832 | tf_op jit(solution)/shard_map/ppermute | solution.py:304
  21.8 0.2 collective-permute-done.15.refs_2_
  22.1 0.8 %collective-permute-done.16.refs_3_ = bf16[16,2048]{1,0:T(8,128)(2,1)S(1)} collective-permute-done((bf16[16,2048]{1,0:T(8,128)(2,1)S(1)}, bf16[16,2048]{1,0:T(8,128)(2,1)S(1)}, u32[]{:S(2)}, u32[]{:S(2)}) %collective-permute-start.16) | collective-permute-done | bytes 65568 | tf_op jit(solution)/shard_map/ppermute | solution.py:310
  22.9 0.4 shard_map.102
  23.3 1.7 %collective-permute-start.20 = (bf16[64,768]{1,0:T(8,128)(2,1)S(1)}, bf16[64,768]{1,0:T(8,128)(2,1)S(1)}, u32[]{:S(2)}, u32[]{:S(2)}) collective-permute-start(bf16[64,768]{1,0:T(8,128)(2,1)S(1)} %get-tuple-element.70), channel_id=1, source_target_pairs={{0,2},{1,3},{2,0},{3,1},{4,6},{5,7},{6,4},{7,5},{8,10},{9,11},{10,... | collective-permute-start | bytes 294920 | tf_op jit(solution)/shard_map/ppermute | solution.py:304
  25.0 1.2 %collective-permute-done.7.refs_1_ = bf16[64,1536]{1,0:T(8,128)(2,1)S(1)} collective-permute-done((bf16[64,1536]{1,0:T(8,128)(2,1)S(1)}, bf16[64,1536]{1,0:T(8,128)(2,1)S(1)}, u32[]{:S(2)}, u32[]{:S(2)}) %collective-permute-start.7) | collective-permute-done | bytes 196640 | tf_op jit(solution)/shard_map/ppermute | solution.py:304
  26.2 0.1 shard_map.98.refs_0_.refs_2_.refs_4_
  26.3 2.5 %collective-permute-start.8 = (bf16[64,768]{1,0:T(8,128)(2,1)S(1)}, bf16[64,768]{1,0:T(8,128)(2,1)S(1)}, u32[]{:S(2)}, u32[]{:S(2)}) collective-permute-start(bf16[64,768]{1,0:T(8,128)(2,1)S(1)} %shard_map.98.refs_0_.refs_2_.refs_4_), channel_id=1, source_target_pairs={{0,2},{1,3},{2,0},{3,1},{4,6},{5,7},{6,4},{7,5},{8,10},{9,11},{10,... | collective-permute-start | bytes 294920 | tf_op jit(solution)/shard_map/ppermute | solution.py:304
  28.8 0.1 collective-permute-done.20.refs_3_
  28.9 0.1 shard_map.105.refs_0_
  29.0 1.8 %collective-permute-start.21 = (bf16[64,1536]{1,0:T(8,128)(2,1)S(1)}, bf16[64,1536]{1,0:T(8,128)(2,1)S(1)}, u32[]{:S(2)}, u32[]{:S(2)}) collective-permute-start(bf16[64,1536]{1,0:T(8,128)(2,1)S(1)} %shard_map.105.refs_0_), channel_id=1, source_target_pairs={{0,2},{1,3},{2,0},{3,1},{4,6},{5,7},{6,4},{7,5},{8,10},{9,11},{10,... | collective-permute-start | bytes 589832 | tf_op jit(solution)/shard_map/ppermute | solution.py:304
  30.8 1.6 %collective-permute-done.8.refs_1_.refs_3_ = bf16[64,768]{1,0:T(8,128)(2,1)S(1)} collective-permute-done((bf16[64,768]{1,0:T(8,128)(2,1)S(1)}, bf16[64,768]{1,0:T(8,128)(2,1)S(1)}, u32[]{:S(2)}, u32[]{:S(2)}) %collective-permute-start.8) | collective-permute-done | bytes 98336 | tf_op jit(solution)/shard_map/ppermute | solution.py:304
  32.4 0.6 %shard_map.99 = (bf16[32,1024]{1,0:T(8,128)(2,1)S(1)}, bf16[32,1024]{1,0:T(8,128)(2,1)S(1)}, bf16[32,1024]{1,0:T(8,128)(2,1)S(1)}, bf16[32,1024]{1,0:T(8,128)(2,1)S(1)}) custom-call(bf16[64,768]{1,0:T(8,128)(2,1)S(1)} %shard_map.98.refs_0_.refs_2_.refs_4_, bf16[64,768]{1,0:T(8,128)(2,1)S(1)} %collective-permute-done.8.refs_1_.refs_3_, ...), custom_call_target="tpu_custom_call" | custom-call | flops 2000000000 | tf_op jit(solution)/shard_map/pallas_call | solution.py:42
  33.1 1.2 %collective-permute-start.9 = (bf16[32,1024]{1,0:T(8,128)(2,1)S(1)}, bf16[32,1024]{1,0:T(8,128)(2,1)S(1)}, u32[]{:S(2)}, u32[]{:S(2)}) collective-permute-start(bf16[32,1024]{1,0:T(8,128)(2,1)S(1)} %get-tuple-element.56), channel_id=1, source_target_pairs={{0,8},{4,12},{8,0},{12,4},{1,9},{5,13},{9,1},{13,5},{2,10},{6,14},... | collective-permute-start | bytes 196616 | tf_op jit(solution)/shard_map/ppermute | solution.py:310
  34.2 1.9 %collective-permute-start.10 = (bf16[32,1024]{1,0:T(8,128)(2,1)S(1)}, bf16[32,1024]{1,0:T(8,128)(2,1)S(1)}, u32[]{:S(2)}, u32[]{:S(2)}) collective-permute-start(bf16[32,1024]{1,0:T(8,128)(2,1)S(1)} %get-tuple-element.57), channel_id=1, source_target_pairs={{0,12},{4,8},{8,4},{12,0},{1,13},{5,9},{9,5},{13,1},{2,14},{6,10},... | collective-permute-start | bytes 196616 | tf_op jit(solution)/shard_map/ppermute | solution.py:310
  36.1 0.5 collective-permute-start.11
  36.6 1.1 %shard_map.106 = (bf16[64,1024]{1,0:T(8,128)(2,1)S(1)}, bf16[64,1024]{1,0:T(8,128)(2,1)S(1)}) custom-call(bf16[64,1536]{1,0:T(8,128)(2,1)S(1)} %shard_map.105.refs_0_, bf16[64,1536]{1,0:T(8,128)(2,1)S(1)} %collective-permute-done.21.refs_1_, bf16[512,1536]{1,0:T(8,128)(2,1)S(1)} %bitcast.7, bf16[512,1536]{1,0:T(8,128)(2,1)S(1)} %collective-permute-done.refs_5_.refs_3_), custom_call_target="tpu_custom_call" | custom-call | tf_op jit(solution)/shard_map/pallas_call | solution.py:42
  37.8 2.1 %collective-permute-start.22 = (bf16[64,1024]{1,0:T(8,128)(2,1)S(1)}, bf16[64,1024]{1,0:T(8,128)(2,1)S(1)}, u32[]{:S(2)}, u32[]{:S(2)}) collective-permute-start(bf16[64,1024]{1,0:T(8,128)(2,1)S(1)} %get-tuple-element.72), channel_id=1, source_target_pairs={{0,2},{1,3},{2,0},{3,1},{4,6},{5,7},{6,4},{7,5},{8,10},{9,11},{10,... | collective-permute-start | bytes 393224 | tf_op jit(solution)/shard_map/ppermute | solution.py:304
  39.9 0.5 collective-permute-start.18
  40.4 0.1 collective-permute-done.10.refs_2_.refs_4_
  40.5 0.5 %collective-permute-done.11.refs_3_.refs_5_ = bf16[32,1024]{1,0:T(8,128)(2,1)S(1)} collective-permute-done((bf16[32,1024]{1,0:T(8,128)(2,1)S(1)}, bf16[32,1024]{1,0:T(8,128)(2,1)S(1)}, u32[]{:S(2)}, u32[]{:S(2)}) %collective-permute-start.11) | collective-permute-done | bytes 65568 | tf_op jit(solution)/shard_map/ppermute | solution.py:310
  41.1 1.8 %collective-permute-start.12 = (bf16[64,1024]{1,0:T(8,128)(2,1)S(1)}, bf16[64,1024]{1,0:T(8,128)(2,1)S(1)}, u32[]{:S(2)}, u32[]{:S(2)}) collective-permute-start(bf16[64,1024]{1,0:T(8,128)(2,1)S(1)} %shard_map.100), channel_id=1, source_target_pairs={{0,2},{1,3},{2,0},{3,1},{4,6},{5,7},{6,4},{7,5},{8,10},{9,11},{10,... | collective-permute-start | bytes 393224 | tf_op jit(solution)/shard_map/ppermute | solution.py:304
  42.9 0.4 collective-permute-done.22.refs_1_
  43.3 2.3 %collective-permute-start.23 = (bf16[16,2048]{1,0:T(8,128)(2,1)S(1)}, bf16[16,2048]{1,0:T(8,128)(2,1)S(1)}, u32[]{:S(2)}, u32[]{:S(2)}) collective-permute-start(bf16[16,2048]{1,0:T(8,128)(2,1)S(1)} %get-tuple-element.74), channel_id=1, source_target_pairs={{0,8},{4,12},{8,0},{12,4},{1,9},{5,13},{9,1},{13,5},{2,10},{6,14},... | collective-permute-start | bytes 196616 | tf_op jit(solution)/shard_map/ppermute | solution.py:310
  45.7 1.7 %collective-permute-start.24 = (bf16[16,2048]{1,0:T(8,128)(2,1)S(1)}, bf16[16,2048]{1,0:T(8,128)(2,1)S(1)}, u32[]{:S(2)}, u32[]{:S(2)}) collective-permute-start(bf16[16,2048]{1,0:T(8,128)(2,1)S(1)} %get-tuple-element.75), channel_id=1, source_target_pairs={{0,12},{4,8},{8,4},{12,0},{1,13},{5,9},{9,5},{13,1},{2,14},{6,10},... | collective-permute-start | bytes 196616 | tf_op jit(solution)/shard_map/ppermute | solution.py:310
  47.4 1.6 %shard_map.103 = (f32[512,768]{1,0:T(8,128)}, f32[8,128]{1,0:T(8,128)S(1)}) custom-call(bf16[128,512]{1,0:T(8,128)(2,1)S(1)} %get-tuple-element.65.refs_0_, bf16[128,512]{1,0:T(8,128)(2,1)S(1)} %collective-permute-done.17.refs_1_, bf16[64,768]{1,0:T(8,128)(2,1)S(1)} %shard_map.98.refs_0_.refs_2_.refs_4_, ...), custom_call_target="tpu_custom_call" | custom-call | tf_op jit(solution)/shard_map/pallas_call | solution.py:42
  48.9 1.3 %shard_map.104 = (bf16[256,2048]{1,0:T(8,128)(2,1)}, f32[8,128]{1,0:T(8,128)S(1)}) custom-call(bf16[256,64]{1,0:T(8,128)(2,1)S(1)} %get-tuple-element.41.refs_0_, f32[64,128]{1,0:T(8,128)S(1)} %get-tuple-element.42.refs_1_, bf16[32,1024]{1,0:T(8,128)(2,1)S(1)} %get-tuple-element.55.refs_0_.refs_2_, ...), custom_call_target="tpu_custom_call" | custom-call | tf_op jit(solution)/shard_map/pallas_call | solution.py:42
  50.3 0.4 collective-permute-done.23.refs_2_
  50.7 1.3 %collective-permute-done.24.refs_3_ = bf16[16,2048]{1,0:T(8,128)(2,1)S(1)} collective-permute-done((bf16[16,2048]{1,0:T(8,128)(2,1)S(1)}, bf16[16,2048]{1,0:T(8,128)(2,1)S(1)}, u32[]{:S(2)}, u32[]{:S(2)}) %collective-permute-start.24) | collective-permute-done | bytes 65568 | tf_op jit(solution)/shard_map/ppermute | solution.py:310
  51.9 0.4 collective-permute-done.25.refs_4_
  52.3 1.2 %shard_map.108 = bf16[256,2048]{1,0:T(8,128)(2,1)} custom-call(bf16[256,64]{1,0:T(8,128)(2,1)S(1)} %get-tuple-element.41.refs_0_, bf16[16,2048]{1,0:T(8,128)(2,1)S(1)} %get-tuple-element.73.refs_1_, bf16[16,2048]{1,0:T(8,128)(2,1)S(1)} %collective-permute-done.23.refs_2_, bf16[16,2048]{1,0:T(8,128)(2,1)S(1)} %collective-permute-done.24.refs_3_, ...), custom_call_target="tpu_custom_call" | custom-call | tf_op jit(solution)/shard_map/pallas_call | solution.py:42
  (23 shorter events, 0.1 us)
Async XLA Ops:
  0.6 7.6 %collective-permute-start = (bf16[512,1536]{1,0:T(8,128)(2,1)}, bf16[512,1536]{1,0:T(8,128)(2,1)S(1)}, u32[]{:S(2)}, u32[]{:S(2)}) collective-permute-start(bf16[512,1536]{1,0:T(8,128)(2,1)} %bitcast.5), channel_id=1, source_target_pairs={{0,1},{1,0},{2,3},{3,2},{4,5},{5,4},{6,7},{7,6},{8,9},{9,8},{10,11... | collective-permute-start | bytes 4718600 | tf_op jit(solution)/shard_map/ppermute | solution.py:300
  1.1 7.0 %collective-permute-start.1 = (bf16[512,768]{1,0:T(8,128)(2,1)}, bf16[512,768]{1,0:T(8,128)(2,1)S(1)}, u32[]{:S(2)}, u32[]{:S(2)}) collective-permute-start(bf16[512,768]{1,0:T(8,128)(2,1)} %bitcast.8), channel_id=1, source_target_pairs={{0,1},{1,0},{2,3},{3,2},{4,5},{5,4},{6,7},{7,6},{8,9},{9,8},{10,11... | collective-permute-start | bytes 2359304 | tf_op jit(solution)/shard_map/ppermute | solution.py:300
  3.2 5.5 %collective-permute-start.3 = (bf16[32,1024]{1,0:T(8,128)(2,1)S(1)}, bf16[32,1024]{1,0:T(8,128)(2,1)S(1)}, u32[]{:S(2)}, u32[]{:S(2)}) collective-permute-start(bf16[32,1024]{1,0:T(8,128)(2,1)S(1)} %get-tuple-element.47), channel_id=1, source_target_pairs={{0,2},{1,3},{2,0},{3,1},{4,6},{5,7},{6,4},{7,5},{8,10},{9,11},{10,... | collective-permute-start | bytes 196616 | tf_op jit(solution)/shard_map/ppermute | solution.py:304
  6.2 6.8 %collective-permute-start.2 = (bf16[32,1024]{1,0:T(8,128)(2,1)S(1)}, bf16[32,1024]{1,0:T(8,128)(2,1)S(1)}, u32[]{:S(2)}, u32[]{:S(2)}) collective-permute-start(bf16[32,1024]{1,0:T(8,128)(2,1)S(1)} %get-tuple-element.45), channel_id=1, source_target_pairs={{0,2},{1,3},{2,0},{3,1},{4,6},{5,7},{6,4},{7,5},{8,10},{9,11},{10,... | collective-permute-start | bytes 196616 | tf_op jit(solution)/shard_map/ppermute | solution.py:304
  6.2 7.5 %collective-permute-start.13 = (bf16[64,1024]{1,0:T(8,128)(2,1)S(1)}, bf16[64,1024]{1,0:T(8,128)(2,1)S(1)}, u32[]{:S(2)}, u32[]{:S(2)}) collective-permute-start(bf16[64,1024]{1,0:T(8,128)(2,1)S(1)} %get-tuple-element.60), channel_id=1, source_target_pairs={{0,2},{1,3},{2,0},{3,1},{4,6},{5,7},{6,4},{7,5},{8,10},{9,11},{10,... | collective-permute-start | bytes 393224 | tf_op jit(solution)/shard_map/ppermute | solution.py:304
  8.2 11.2 %copy-start = (bf16[1,512,1536]{2,1,0:T(8,128)(2,1)S(1)}, bf16[1,512,1536]{2,1,0:T(8,128)(2,1)}, u32[]{:S(2)}) copy-start(bf16[1,512,1536]{2,1,0:T(8,128)(2,1)} %param.12) | copy-start | bytes 4718596
  8.6 8.9 %collective-permute-start.4 = (bf16[16,2048]{1,0:T(8,128)(2,1)S(1)}, bf16[16,2048]{1,0:T(8,128)(2,1)S(1)}, u32[]{:S(2)}, u32[]{:S(2)}) collective-permute-start(bf16[16,2048]{1,0:T(8,128)(2,1)S(1)} %get-tuple-element.48), channel_id=1, source_target_pairs={{0,12},{4,8},{8,4},{12,0},{1,13},{5,9},{9,5},{13,1},{2,14},{6,10},... | collective-permute-start | bytes 196616 | tf_op jit(solution)/shard_map/ppermute | solution.py:310
  13.0 6.4 %collective-permute-start.6 = (bf16[16,2048]{1,0:T(8,128)(2,1)S(1)}, bf16[16,2048]{1,0:T(8,128)(2,1)S(1)}, u32[]{:S(2)}, u32[]{:S(2)}) collective-permute-start(bf16[16,2048]{1,0:T(8,128)(2,1)S(1)} %get-tuple-element.50), channel_id=1, source_target_pairs={{0,8},{4,12},{8,0},{12,4},{1,9},{5,13},{9,1},{13,5},{2,10},{6,14},... | collective-permute-start | bytes 196616 | tf_op jit(solution)/shard_map/ppermute | solution.py:310
  13.0 6.4 %collective-permute-start.5 = (bf16[16,2048]{1,0:T(8,128)(2,1)S(1)}, bf16[16,2048]{1,0:T(8,128)(2,1)S(1)}, u32[]{:S(2)}, u32[]{:S(2)}) collective-permute-start(bf16[16,2048]{1,0:T(8,128)(2,1)S(1)} %get-tuple-element.49), channel_id=1, source_target_pairs={{0,4},{4,0},{8,12},{12,8},{1,5},{5,1},{9,13},{13,9},{2,6},{6,2},{1... | collective-permute-start | bytes 196616 | tf_op jit(solution)/shard_map/ppermute | solution.py:310
  13.7 8.1 %collective-permute-start.14 = (bf16[16,2048]{1,0:T(8,128)(2,1)S(1)}, bf16[16,2048]{1,0:T(8,128)(2,1)S(1)}, u32[]{:S(2)}, u32[]{:S(2)}) collective-permute-start(bf16[16,2048]{1,0:T(8,128)(2,1)S(1)} %get-tuple-element.62), channel_id=1, source_target_pairs={{0,12},{4,8},{8,4},{12,0},{1,13},{5,9},{9,5},{13,1},{2,14},{6,10},... | collective-permute-start | bytes 196616 | tf_op jit(solution)/shard_map/ppermute | solution.py:310
  17.5 4.5 %collective-permute-start.15 = (bf16[16,2048]{1,0:T(8,128)(2,1)S(1)}, bf16[16,2048]{1,0:T(8,128)(2,1)S(1)}, u32[]{:S(2)}, u32[]{:S(2)}) collective-permute-start(bf16[16,2048]{1,0:T(8,128)(2,1)S(1)} %get-tuple-element.63), channel_id=1, source_target_pairs={{0,4},{4,0},{8,12},{12,8},{1,5},{5,1},{9,13},{13,9},{2,6},{6,2},{1... | collective-permute-start | bytes 196616 | tf_op jit(solution)/shard_map/ppermute | solution.py:310
  17.6 5.3 %collective-permute-start.16 = (bf16[16,2048]{1,0:T(8,128)(2,1)S(1)}, bf16[16,2048]{1,0:T(8,128)(2,1)S(1)}, u32[]{:S(2)}, u32[]{:S(2)}) collective-permute-start(bf16[16,2048]{1,0:T(8,128)(2,1)S(1)} %get-tuple-element.64), channel_id=1, source_target_pairs={{0,8},{4,12},{8,0},{12,4},{1,9},{5,13},{9,1},{13,5},{2,10},{6,14},... | collective-permute-start | bytes 196616 | tf_op jit(solution)/shard_map/ppermute | solution.py:310
  19.4 3.5 %copy-start.1 = (bf16[1,512,768]{2,1,0:T(8,128)(2,1)S(1)}, bf16[1,512,768]{2,1,0:T(8,128)(2,1)}, u32[]{:S(2)}) copy-start(bf16[1,512,768]{2,1,0:T(8,128)(2,1)} %param.13) | copy-start | bytes 2359300
  20.0 6.2 %collective-permute-start.7 = (bf16[64,1536]{1,0:T(8,128)(2,1)S(1)}, bf16[64,1536]{1,0:T(8,128)(2,1)S(1)}, u32[]{:S(2)}, u32[]{:S(2)}) collective-permute-start(bf16[64,1536]{1,0:T(8,128)(2,1)S(1)} %get-tuple-element.53), channel_id=1, source_target_pairs={{0,2},{1,3},{2,0},{3,1},{4,6},{5,7},{6,4},{7,5},{8,10},{9,11},{10,... | collective-permute-start | bytes 589832 | tf_op jit(solution)/shard_map/ppermute | solution.py:304
  23.3 5.6 %collective-permute-start.20 = (bf16[64,768]{1,0:T(8,128)(2,1)S(1)}, bf16[64,768]{1,0:T(8,128)(2,1)S(1)}, u32[]{:S(2)}, u32[]{:S(2)}) collective-permute-start(bf16[64,768]{1,0:T(8,128)(2,1)S(1)} %get-tuple-element.70), channel_id=1, source_target_pairs={{0,2},{1,3},{2,0},{3,1},{4,6},{5,7},{6,4},{7,5},{8,10},{9,11},{10,... | collective-permute-start | bytes 294920 | tf_op jit(solution)/shard_map/ppermute | solution.py:304
  26.3 6.2 %collective-permute-start.8 = (bf16[64,768]{1,0:T(8,128)(2,1)S(1)}, bf16[64,768]{1,0:T(8,128)(2,1)S(1)}, u32[]{:S(2)}, u32[]{:S(2)}) collective-permute-start(bf16[64,768]{1,0:T(8,128)(2,1)S(1)} %shard_map.98.refs_0_.refs_2_.refs_4_), channel_id=1, source_target_pairs={{0,2},{1,3},{2,0},{3,1},{4,6},{5,7},{6,4},{7,5},{8,10},{9,11},{10,... | collective-permute-start | bytes 294920 | tf_op jit(solution)/shard_map/ppermute | solution.py:304
  29.0 7.6 %collective-permute-start.21 = (bf16[64,1536]{1,0:T(8,128)(2,1)S(1)}, bf16[64,1536]{1,0:T(8,128)(2,1)S(1)}, u32[]{:S(2)}, u32[]{:S(2)}) collective-permute-start(bf16[64,1536]{1,0:T(8,128)(2,1)S(1)} %shard_map.105.refs_0_), channel_id=1, source_target_pairs={{0,2},{1,3},{2,0},{3,1},{4,6},{5,7},{6,4},{7,5},{8,10},{9,11},{10,... | collective-permute-start | bytes 589832 | tf_op jit(solution)/shard_map/ppermute | solution.py:304
  33.1 6.8 %collective-permute-start.9 = (bf16[32,1024]{1,0:T(8,128)(2,1)S(1)}, bf16[32,1024]{1,0:T(8,128)(2,1)S(1)}, u32[]{:S(2)}, u32[]{:S(2)}) collective-permute-start(bf16[32,1024]{1,0:T(8,128)(2,1)S(1)} %get-tuple-element.56), channel_id=1, source_target_pairs={{0,8},{4,12},{8,0},{12,4},{1,9},{5,13},{9,1},{13,5},{2,10},{6,14},... | collective-permute-start | bytes 196616 | tf_op jit(solution)/shard_map/ppermute | solution.py:310
  34.2 6.3 %collective-permute-start.10 = (bf16[32,1024]{1,0:T(8,128)(2,1)S(1)}, bf16[32,1024]{1,0:T(8,128)(2,1)S(1)}, u32[]{:S(2)}, u32[]{:S(2)}) collective-permute-start(bf16[32,1024]{1,0:T(8,128)(2,1)S(1)} %get-tuple-element.57), channel_id=1, source_target_pairs={{0,12},{4,8},{8,4},{12,0},{1,13},{5,9},{9,5},{13,1},{2,14},{6,10},... | collective-permute-start | bytes 196616 | tf_op jit(solution)/shard_map/ppermute | solution.py:310
  36.1 5.0 %collective-permute-start.11 = (bf16[32,1024]{1,0:T(8,128)(2,1)S(1)}, bf16[32,1024]{1,0:T(8,128)(2,1)S(1)}, u32[]{:S(2)}, u32[]{:S(2)}) collective-permute-start(bf16[32,1024]{1,0:T(8,128)(2,1)S(1)} %get-tuple-element.58), channel_id=1, source_target_pairs={{0,4},{4,0},{8,12},{12,8},{1,5},{5,1},{9,13},{13,9},{2,6},{6,2},{1... | collective-permute-start | bytes 196616 | tf_op jit(solution)/shard_map/ppermute | solution.py:310
  37.8 5.5 %collective-permute-start.22 = (bf16[64,1024]{1,0:T(8,128)(2,1)S(1)}, bf16[64,1024]{1,0:T(8,128)(2,1)S(1)}, u32[]{:S(2)}, u32[]{:S(2)}) collective-permute-start(bf16[64,1024]{1,0:T(8,128)(2,1)S(1)} %get-tuple-element.72), channel_id=1, source_target_pairs={{0,2},{1,3},{2,0},{3,1},{4,6},{5,7},{6,4},{7,5},{8,10},{9,11},{10,... | collective-permute-start | bytes 393224 | tf_op jit(solution)/shard_map/ppermute | solution.py:304
  39.9 5.8 %collective-permute-start.17 = (bf16[128,512]{1,0:T(8,128)(2,1)S(1)}, bf16[128,512]{1,0:T(8,128)(2,1)S(1)}, u32[]{:S(2)}, u32[]{:S(2)}) collective-permute-start(bf16[128,512]{1,0:T(8,128)(2,1)S(1)} %get-tuple-element.66), channel_id=1, source_target_pairs={{0,1},{1,0},{2,3},{3,2},{4,5},{5,4},{6,7},{7,6},{8,9},{9,8},{10,11... | collective-permute-start | bytes 393224 | tf_op jit(solution)/shard_map/ppermute | solution.py:300
  39.9 7.5 %collective-permute-start.18 = (bf16[64,768]{1,0:T(8,128)(2,1)S(1)}, bf16[64,768]{1,0:T(8,128)(2,1)S(1)}, u32[]{:S(2)}, u32[]{:S(2)}) collective-permute-start(bf16[64,768]{1,0:T(8,128)(2,1)S(1)} %shard_map.98.refs_0_.refs_2_.refs_4_), channel_id=1, source_target_pairs={{0,1},{1,0},{2,3},{3,2},{4,5},{5,4},{6,7},{7,6},{8,9},{9,8},{10,11... | collective-permute-start | bytes 294920 | tf_op jit(solution)/shard_map/ppermute | solution.py:300
  41.1 7.9 %collective-permute-start.12 = (bf16[64,1024]{1,0:T(8,128)(2,1)S(1)}, bf16[64,1024]{1,0:T(8,128)(2,1)S(1)}, u32[]{:S(2)}, u32[]{:S(2)}) collective-permute-start(bf16[64,1024]{1,0:T(8,128)(2,1)S(1)} %shard_map.100), channel_id=1, source_target_pairs={{0,2},{1,3},{2,0},{3,1},{4,6},{5,7},{6,4},{7,5},{8,10},{9,11},{10,... | collective-permute-start | bytes 393224 | tf_op jit(solution)/shard_map/ppermute | solution.py:304
  42.9 4.5 %collective-permute-start.19 = (bf16[64,768]{1,0:T(8,128)(2,1)S(1)}, bf16[64,768]{1,0:T(8,128)(2,1)S(1)}, u32[]{:S(2)}, u32[]{:S(2)}) collective-permute-start(bf16[64,768]{1,0:T(8,128)(2,1)S(1)} %collective-permute-done.8.refs_1_.refs_3_), channel_id=1, source_target_pairs={{0,1},{1,0},{2,3},{3,2},{4,5},{5,4},{6,7},{7,6},{8,9},{9,8},{10,11... | collective-permute-start | bytes 294920 | tf_op jit(solution)/shard_map/ppermute | solution.py:300
  43.3 7.3 %collective-permute-start.23 = (bf16[16,2048]{1,0:T(8,128)(2,1)S(1)}, bf16[16,2048]{1,0:T(8,128)(2,1)S(1)}, u32[]{:S(2)}, u32[]{:S(2)}) collective-permute-start(bf16[16,2048]{1,0:T(8,128)(2,1)S(1)} %get-tuple-element.74), channel_id=1, source_target_pairs={{0,8},{4,12},{8,0},{12,4},{1,9},{5,13},{9,1},{13,5},{2,10},{6,14},... | collective-permute-start | bytes 196616 | tf_op jit(solution)/shard_map/ppermute | solution.py:310
  45.7 6.2 %collective-permute-start.24 = (bf16[16,2048]{1,0:T(8,128)(2,1)S(1)}, bf16[16,2048]{1,0:T(8,128)(2,1)S(1)}, u32[]{:S(2)}, u32[]{:S(2)}) collective-permute-start(bf16[16,2048]{1,0:T(8,128)(2,1)S(1)} %get-tuple-element.75), channel_id=1, source_target_pairs={{0,12},{4,8},{8,4},{12,0},{1,13},{5,9},{9,5},{13,1},{2,14},{6,10},... | collective-permute-start | bytes 196616 | tf_op jit(solution)/shard_map/ppermute | solution.py:310
  47.4 5.0 %collective-permute-start.25 = (bf16[16,2048]{1,0:T(8,128)(2,1)S(1)}, bf16[16,2048]{1,0:T(8,128)(2,1)S(1)}, u32[]{:S(2)}, u32[]{:S(2)}) collective-permute-start(bf16[16,2048]{1,0:T(8,128)(2,1)S(1)} %get-tuple-element.76), channel_id=1, source_target_pairs={{0,4},{4,0},{8,12},{12,8},{1,5},{5,1},{9,13},{13,9},{2,6},{6,2},{1... | collective-permute-start | bytes 196616 | tf_op jit(solution)/shard_map/ppermute | solution.py:310

commit v20 on v19

--- a/solution.py
+++ b/solution.py
@@ -116,7 +116,11 @@
 
 
 def farthest_first(groups):
-    return [groups - 1, *range(1, groups - 1)]
+    return [*range(groups - 1, 0, -1)]
+
+
+def nearest_first(groups):
+    return [*range(1, groups)]
 
 
 def far_half_first(groups):
@@ -152,8 +156,8 @@
             ]
 
 
-def partial(groups, spread, refs, outs):
-    chunks, (own, sib) = restore(refs[:groups], farthest_first), refs[groups:]
+def partial(groups, spread, refs, outs, order):
+    chunks, (own, sib) = restore(refs[:groups], order), refs[groups:]
     part = own.shape[0]
     half = CORES * part
     rows = jnp.concatenate(
@@ -167,12 +171,12 @@
 
 
 def pre_kernel(groups, spread, *refs):
-    partial(groups, spread, refs[: groups + 2], refs[groups + 2 :])
+    partial(groups, spread, refs[: groups + 2], refs[groups + 2 :], farthest_first)
 
 
 def back_kernel(groups, spread, *refs):
     own, sib, *outs = refs[groups + 2 :]
-    rows = partial(groups, spread, refs[: groups + 2], outs)
+    rows = partial(groups, spread, refs[: groups + 2], outs, nearest_first)
     part = own.shape[1]
     own[...] = rows[:, :part]
     sib[...] = rows[:, part:]
@@ -362,7 +366,7 @@
         [shape((spread * slots, part))] * 2
         + [shape((slots, feed), F32)]
         + [shape((slots, feed))] * (spread - 1),
-        (*arrange(grads, farthest_first), out_own, out_sib),
+        (*arrange(grads, nearest_first), out_own, out_sib),
         cost=BACK_COST,
     )
     back = (back, *to_x(back_far))

time: 53.8 us -> 53.5 us (level)
    ppermute x9, starting transfers between devices: 16.9 us -> 15.5 us  [to_x(): lax.ppermute(value, 'fsdp', [(i, i ^ (k + 1) * CORES) for i in range(part...]
    ppermute x12, starting transfers between devices: 17.1 us -> 18 us  [to_expert(): lax.ppermute(value, 'expert', [(i, i ^ ke) for i in range(groups)])]
  transfers between devices with their start and end apart: 26 -> 26, of which waited for: 13 -> 12; matrix products, arithmetic and copies ran while one was open for 0% -> 0% of each run, Pallas kernels for 15% -> 15%
where the time goes in v20:
time: 53.5 us; the launch traced here: 53.3 us
  starting transfers between devices  34.6 us (65%)
  Pallas kernels  9 us (17%)
  waiting for transfers between devices  8.92 us (17%)
  between operations  0.74 us (1%)
    ppermute x12, starting transfers between devices, to_expert(): lax.ppermute(value, 'expert', [(i, i ^ ke) for i in range(groups)])  18 us
    ppermute x9, starting transfers between devices, to_x(): lax.ppermute(value, 'fsdp', [(i, i ^ (k + 1) * CORES) for i in range(part...  15.5 us
    pallas_call x15, Pallas kernels, call(): pl.pallas_call(kernel, out_shape=out_shape, in_specs=specs, compiler_para...  9 us
    ppermute x12, waiting for transfers between devices, to_expert(): lax.ppermute(value, 'expert', [(i, i ^ ke) for i in range(groups)])  4.78 us
    ppermute x9, waiting for transfers between devices, to_x(): lax.ppermute(value, 'fsdp', [(i, i ^ (k + 1) * CORES) for i in range(part...  4.12 us
    ppermute x5, starting transfers between devices, to_core(): return lax.ppermute(value, 'fsdp', [(i, i ^ 1) for i in range(parts)])  1.11 us
  transfers between devices with their start and end apart: 26, of which 12 were waited for; matrix products, arithmetic and copies ran while one was open for 0% of the time, Pallas kernels for 15%

profile of v20, /device:TPU:0, one launch (start us, length us, event | category | flops | bytes accessed | tf_op | source)
XLA Modules:
  0.0 53.3 jit_solution(5559493303594835500)
XLA Ops:
  0.6 0.5 collective-permute-start
  1.1 0.1 collective-permute-start.1
  1.2 1.9 %shard_map.94 = (bf16[64,1024]{1,0:T(8,128)(2,1)S(1)}, bf16[32,1024]{1,0:T(8,128)(2,1)S(1)}, bf16[32,1024]{1,0:T(8,128)(2,1)S(1)}, bf16[64,1024]{1,0:T(8,128)(2,...) custom-call(s32[8,256]{1,0:T(8,128)} %bitcast.11, f32[8,256]{1,0:T(8,128)} %bitcast.12, ...), custom_call_target="tpu_custom_call" | custom-call | tf_op jit(solution)/shard_map/pallas_call | solution.py:42
  3.2 3.0 %collective-permute-start.3 = (bf16[32,1024]{1,0:T(8,128)(2,1)S(1)}, bf16[32,1024]{1,0:T(8,128)(2,1)S(1)}, u32[]{:S(2)}, u32[]{:S(2)}) collective-permute-start(bf16[32,1024]{1,0:T(8,128)(2,1)S(1)} %get-tuple-element.47), channel_id=1, source_target_pairs={{0,2},{1,3},{2,0},{3,1},{4,6},{5,7},{6,4},{7,5},{8,10},{9,11},{10,... | collective-permute-start | bytes 196616 | tf_op jit(solution)/shard_map/ppermute | solution.py:308
  6.2 0.1 collective-permute-start.2
  6.2 1.9 %collective-permute-start.13 = (bf16[64,1024]{1,0:T(8,128)(2,1)S(1)}, bf16[64,1024]{1,0:T(8,128)(2,1)S(1)}, u32[]{:S(2)}, u32[]{:S(2)}) collective-permute-start(bf16[64,1024]{1,0:T(8,128)(2,1)S(1)} %get-tuple-element.60), channel_id=1, source_target_pairs={{0,2},{1,3},{2,0},{3,1},{4,6},{5,7},{6,4},{7,5},{8,10},{9,11},{10,... | collective-permute-start | bytes 393224 | tf_op jit(solution)/shard_map/ppermute | solution.py:308
  8.2 0.4 collective-permute-done.3.refs_1_
  8.6 4.4 %collective-permute-start.4 = (bf16[16,2048]{1,0:T(8,128)(2,1)S(1)}, bf16[16,2048]{1,0:T(8,128)(2,1)S(1)}, u32[]{:S(2)}, u32[]{:S(2)}) collective-permute-start(bf16[16,2048]{1,0:T(8,128)(2,1)S(1)} %get-tuple-element.48), channel_id=1, source_target_pairs={{0,12},{4,8},{8,4},{12,0},{1,13},{5,9},{9,5},{13,1},{2,14},{6,10},... | collective-permute-start | bytes 196616 | tf_op jit(solution)/shard_map/ppermute | solution.py:314
  13.0 0.7 %collective-permute-start.6 = (bf16[16,2048]{1,0:T(8,128)(2,1)S(1)}, bf16[16,2048]{1,0:T(8,128)(2,1)S(1)}, u32[]{:S(2)}, u32[]{:S(2)}) collective-permute-start(bf16[16,2048]{1,0:T(8,128)(2,1)S(1)} %get-tuple-element.50), channel_id=1, source_target_pairs={{0,4},{4,0},{8,12},{12,8},{1,5},{5,1},{9,13},{13,9},{2,6},{6,2},{1... | collective-permute-start | bytes 196616 | tf_op jit(solution)/shard_map/ppermute | solution.py:314
  13.7 0.0 collective-permute-done.13.refs_1_
  13.7 1.5 %collective-permute-start.14 = (bf16[16,2048]{1,0:T(8,128)(2,1)S(1)}, bf16[16,2048]{1,0:T(8,128)(2,1)S(1)}, u32[]{:S(2)}, u32[]{:S(2)}) collective-permute-start(bf16[16,2048]{1,0:T(8,128)(2,1)S(1)} %get-tuple-element.62), channel_id=1, source_target_pairs={{0,4},{4,0},{8,12},{12,8},{1,5},{5,1},{9,13},{13,9},{2,6},{6,2},{1... | collective-permute-start | bytes 196616 | tf_op jit(solution)/shard_map/ppermute | solution.py:314
  15.2 2.9 %collective-permute-start.15 = (bf16[16,2048]{1,0:T(8,128)(2,1)S(1)}, bf16[16,2048]{1,0:T(8,128)(2,1)S(1)}, u32[]{:S(2)}, u32[]{:S(2)}) collective-permute-start(bf16[16,2048]{1,0:T(8,128)(2,1)S(1)} %get-tuple-element.63), channel_id=1, source_target_pairs={{0,8},{4,12},{8,0},{12,4},{1,9},{5,13},{9,1},{13,5},{2,10},{6,14},... | collective-permute-start | bytes 196616 | tf_op jit(solution)/shard_map/ppermute | solution.py:314
  18.1 0.0 collective-permute-done.4.refs_1_
  18.1 1.5 %collective-permute-start.16 = (bf16[16,2048]{1,0:T(8,128)(2,1)S(1)}, bf16[16,2048]{1,0:T(8,128)(2,1)S(1)}, u32[]{:S(2)}, u32[]{:S(2)}) collective-permute-start(bf16[16,2048]{1,0:T(8,128)(2,1)S(1)} %get-tuple-element.64), channel_id=1, source_target_pairs={{0,12},{4,8},{8,4},{12,0},{1,13},{5,9},{9,5},{13,1},{2,14},{6,10},... | collective-permute-start | bytes 196616 | tf_op jit(solution)/shard_map/ppermute | solution.py:314
  19.6 0.1 collective-permute-done.5.refs_2_
  19.7 0.0 collective-permute-done.6.refs_3_
  19.7 0.6 %shard_map.97 = (f32[64,1536]{1,0:T(8,128)S(1)}, bf16[64,1536]{1,0:T(8,128)(2,1)S(1)}) custom-call(bf16[16,2048]{1,0:T(8,128)(2,1)S(1)} %get-tuple-element.46.refs_0_, bf16[16,2048]{1,0:T(8,128)(2,1)S(1)} %collective-permute-done.4.refs_1_, bf16[16,2048]{1,0:T(8,128)(2,1)S(1)} %collective-permute-done.5.refs_2_, ...), custom_call_target="tpu_custom_call" | custom-call | flops 4499999744 | tf_op jit(solution)/shard_map/pallas_call | solution.py:42
  20.3 1.8 %collective-permute-start.7 = (bf16[64,1536]{1,0:T(8,128)(2,1)S(1)}, bf16[64,1536]{1,0:T(8,128)(2,1)S(1)}, u32[]{:S(2)}, u32[]{:S(2)}) collective-permute-start(bf16[64,1536]{1,0:T(8,128)(2,1)S(1)} %get-tuple-element.53), channel_id=1, source_target_pairs={{0,2},{1,3},{2,0},{3,1},{4,6},{5,7},{6,4},{7,5},{8,10},{9,11},{10,... | collective-permute-start | bytes 589832 | tf_op jit(solution)/shard_map/ppermute | solution.py:308
  22.1 0.3 collective-permute-done.15.refs_2_
  22.5 1.7 %collective-permute-done.16.refs_3_ = bf16[16,2048]{1,0:T(8,128)(2,1)S(1)} collective-permute-done((bf16[16,2048]{1,0:T(8,128)(2,1)S(1)}, bf16[16,2048]{1,0:T(8,128)(2,1)S(1)}, u32[]{:S(2)}, u32[]{:S(2)}) %collective-permute-start.16) | collective-permute-done | bytes 65568 | tf_op jit(solution)/shard_map/ppermute | solution.py:314
  24.2 0.4 shard_map.102
  24.6 1.9 %collective-permute-start.20 = (bf16[64,768]{1,0:T(8,128)(2,1)S(1)}, bf16[64,768]{1,0:T(8,128)(2,1)S(1)}, u32[]{:S(2)}, u32[]{:S(2)}) collective-permute-start(bf16[64,768]{1,0:T(8,128)(2,1)S(1)} %get-tuple-element.70), channel_id=1, source_target_pairs={{0,2},{1,3},{2,0},{3,1},{4,6},{5,7},{6,4},{7,5},{8,10},{9,11},{10,... | collective-permute-start | bytes 294920 | tf_op jit(solution)/shard_map/ppermute | solution.py:308
  26.4 0.9 %collective-permute-done.7.refs_1_ = bf16[64,1536]{1,0:T(8,128)(2,1)S(1)} collective-permute-done((bf16[64,1536]{1,0:T(8,128)(2,1)S(1)}, bf16[64,1536]{1,0:T(8,128)(2,1)S(1)}, u32[]{:S(2)}, u32[]{:S(2)}) %collective-permute-start.7) | collective-permute-done | bytes 196640 | tf_op jit(solution)/shard_map/ppermute | solution.py:308
  27.3 0.1 shard_map.98.refs_0_.refs_2_.refs_4_
  27.4 2.4 %collective-permute-start.8 = (bf16[64,768]{1,0:T(8,128)(2,1)S(1)}, bf16[64,768]{1,0:T(8,128)(2,1)S(1)}, u32[]{:S(2)}, u32[]{:S(2)}) collective-permute-start(bf16[64,768]{1,0:T(8,128)(2,1)S(1)} %shard_map.98.refs_0_.refs_2_.refs_4_), channel_id=1, source_target_pairs={{0,2},{1,3},{2,0},{3,1},{4,6},{5,7},{6,4},{7,5},{8,10},{9,11},{10,... | collective-permute-start | bytes 294920 | tf_op jit(solution)/shard_map/ppermute | solution.py:308
  29.8 0.1 shard_map.105.refs_0_
  29.9 1.4 %collective-permute-start.21 = (bf16[64,1536]{1,0:T(8,128)(2,1)S(1)}, bf16[64,1536]{1,0:T(8,128)(2,1)S(1)}, u32[]{:S(2)}, u32[]{:S(2)}) collective-permute-start(bf16[64,1536]{1,0:T(8,128)(2,1)S(1)} %shard_map.105.refs_0_), channel_id=1, source_target_pairs={{0,2},{1,3},{2,0},{3,1},{4,6},{5,7},{6,4},{7,5},{8,10},{9,11},{10,... | collective-permute-start | bytes 589832 | tf_op jit(solution)/shard_map/ppermute | solution.py:308
  31.3 1.6 %collective-permute-done.8.refs_1_.refs_3_ = bf16[64,768]{1,0:T(8,128)(2,1)S(1)} collective-permute-done((bf16[64,768]{1,0:T(8,128)(2,1)S(1)}, bf16[64,768]{1,0:T(8,128)(2,1)S(1)}, u32[]{:S(2)}, u32[]{:S(2)}) %collective-permute-start.8) | collective-permute-done | bytes 98336 | tf_op jit(solution)/shard_map/ppermute | solution.py:308
  32.9 0.6 %shard_map.99 = (bf16[32,1024]{1,0:T(8,128)(2,1)S(1)}, bf16[32,1024]{1,0:T(8,128)(2,1)S(1)}, bf16[32,1024]{1,0:T(8,128)(2,1)S(1)}, bf16[32,1024]{1,0:T(8,128)(2,1)S(1)}) custom-call(bf16[64,768]{1,0:T(8,128)(2,1)S(1)} %shard_map.98.refs_0_.refs_2_.refs_4_, bf16[64,768]{1,0:T(8,128)(2,1)S(1)} %collective-permute-done.8.refs_1_.refs_3_, ...), custom_call_target="tpu_custom_call" | custom-call | flops 2000000000 | tf_op jit(solution)/shard_map/pallas_call | solution.py:42
  33.6 0.7 %collective-permute-start.9 = (bf16[32,1024]{1,0:T(8,128)(2,1)S(1)}, bf16[32,1024]{1,0:T(8,128)(2,1)S(1)}, u32[]{:S(2)}, u32[]{:S(2)}) collective-permute-start(bf16[32,1024]{1,0:T(8,128)(2,1)S(1)} %get-tuple-element.56), channel_id=1, source_target_pairs={{0,8},{4,12},{8,0},{12,4},{1,9},{5,13},{9,1},{13,5},{2,10},{6,14},... | collective-permute-start | bytes 196616 | tf_op jit(solution)/shard_map/ppermute | solution.py:314
  34.3 1.6 %collective-permute-start.10 = (bf16[32,1024]{1,0:T(8,128)(2,1)S(1)}, bf16[32,1024]{1,0:T(8,128)(2,1)S(1)}, u32[]{:S(2)}, u32[]{:S(2)}) collective-permute-start(bf16[32,1024]{1,0:T(8,128)(2,1)S(1)} %get-tuple-element.57), channel_id=1, source_target_pairs={{0,12},{4,8},{8,4},{12,0},{1,13},{5,9},{9,5},{13,1},{2,14},{6,10},... | collective-permute-start | bytes 196616 | tf_op jit(solution)/shard_map/ppermute | solution.py:314
  35.9 1.2 %collective-permute-start.11 = (bf16[32,1024]{1,0:T(8,128)(2,1)S(1)}, bf16[32,1024]{1,0:T(8,128)(2,1)S(1)}, u32[]{:S(2)}, u32[]{:S(2)}) collective-permute-start(bf16[32,1024]{1,0:T(8,128)(2,1)S(1)} %get-tuple-element.58), channel_id=1, source_target_pairs={{0,4},{4,0},{8,12},{12,8},{1,5},{5,1},{9,13},{13,9},{2,6},{6,2},{1... | collective-permute-start | bytes 196616 | tf_op jit(solution)/shard_map/ppermute | solution.py:314
  37.1 1.1 %shard_map.106 = (bf16[64,1024]{1,0:T(8,128)(2,1)S(1)}, bf16[64,1024]{1,0:T(8,128)(2,1)S(1)}) custom-call(bf16[64,1536]{1,0:T(8,128)(2,1)S(1)} %shard_map.105.refs_0_, bf16[64,1536]{1,0:T(8,128)(2,1)S(1)} %collective-permute-done.21.refs_1_, bf16[512,1536]{1,0:T(8,128)(2,1)S(1)} %bitcast.7, bf16[512,1536]{1,0:T(8,128)(2,1)S(1)} %collective-permute-done.refs_5_.refs_3_), custom_call_target="tpu_custom_call" | custom-call | tf_op jit(solution)/shard_map/pallas_call | solution.py:42
  38.3 1.5 %collective-permute-start.22 = (bf16[64,1024]{1,0:T(8,128)(2,1)S(1)}, bf16[64,1024]{1,0:T(8,128)(2,1)S(1)}, u32[]{:S(2)}, u32[]{:S(2)}) collective-permute-start(bf16[64,1024]{1,0:T(8,128)(2,1)S(1)} %get-tuple-element.72), channel_id=1, source_target_pairs={{0,2},{1,3},{2,0},{3,1},{4,6},{5,7},{6,4},{7,5},{8,10},{9,11},{10,... | collective-permute-start | bytes 393224 | tf_op jit(solution)/shard_map/ppermute | solution.py:308
  39.8 0.5 collective-permute-start.18
  40.3 0.2 collective-permute-done.10.refs_2_.refs_4_
  40.5 0.4 collective-permute-done.11.refs_3_.refs_5_
  40.9 1.5 %collective-permute-start.12 = (bf16[64,1024]{1,0:T(8,128)(2,1)S(1)}, bf16[64,1024]{1,0:T(8,128)(2,1)S(1)}, u32[]{:S(2)}, u32[]{:S(2)}) collective-permute-start(bf16[64,1024]{1,0:T(8,128)(2,1)S(1)} %shard_map.100), channel_id=1, source_target_pairs={{0,2},{1,3},{2,0},{3,1},{4,6},{5,7},{6,4},{7,5},{8,10},{9,11},{10,... | collective-permute-start | bytes 393224 | tf_op jit(solution)/shard_map/ppermute | solution.py:308
  42.4 1.2 %collective-permute-done.22.refs_1_ = bf16[64,1024]{1,0:T(8,128)(2,1)S(1)} collective-permute-done((bf16[64,1024]{1,0:T(8,128)(2,1)S(1)}, bf16[64,1024]{1,0:T(8,128)(2,1)S(1)}, u32[]{:S(2)}, u32[]{:S(2)}) %collective-permute-start.22) | collective-permute-done | bytes 131104 | tf_op jit(solution)/shard_map/ppermute | solution.py:308
  43.6 1.7 %collective-permute-start.23 = (bf16[16,2048]{1,0:T(8,128)(2,1)S(1)}, bf16[16,2048]{1,0:T(8,128)(2,1)S(1)}, u32[]{:S(2)}, u32[]{:S(2)}) collective-permute-start(bf16[16,2048]{1,0:T(8,128)(2,1)S(1)} %get-tuple-element.74), channel_id=1, source_target_pairs={{0,8},{4,12},{8,0},{12,4},{1,9},{5,13},{9,1},{13,5},{2,10},{6,14},... | collective-permute-start | bytes 196616 | tf_op jit(solution)/shard_map/ppermute | solution.py:314
  45.3 1.6 %collective-permute-start.24 = (bf16[16,2048]{1,0:T(8,128)(2,1)S(1)}, bf16[16,2048]{1,0:T(8,128)(2,1)S(1)}, u32[]{:S(2)}, u32[]{:S(2)}) collective-permute-start(bf16[16,2048]{1,0:T(8,128)(2,1)S(1)} %get-tuple-element.75), channel_id=1, source_target_pairs={{0,12},{4,8},{8,4},{12,0},{1,13},{5,9},{9,5},{13,1},{2,14},{6,10},... | collective-permute-start | bytes 196616 | tf_op jit(solution)/shard_map/ppermute | solution.py:314
  46.9 0.3 collective-permute-start.25
  47.2 1.6 %shard_map.103 = (f32[512,768]{1,0:T(8,128)}, f32[8,128]{1,0:T(8,128)S(1)}) custom-call(bf16[128,512]{1,0:T(8,128)(2,1)S(1)} %get-tuple-element.65.refs_0_, bf16[128,512]{1,0:T(8,128)(2,1)S(1)} %collective-permute-done.17.refs_1_, bf16[64,768]{1,0:T(8,128)(2,1)S(1)} %shard_map.98.refs_0_.refs_2_.refs_4_, ...), custom_call_target="tpu_custom_call" | custom-call | tf_op jit(solution)/shard_map/pallas_call | solution.py:42
  48.7 1.3 %shard_map.104 = (bf16[256,2048]{1,0:T(8,128)(2,1)}, f32[8,128]{1,0:T(8,128)S(1)}) custom-call(bf16[256,64]{1,0:T(8,128)(2,1)S(1)} %get-tuple-element.41.refs_0_, f32[64,128]{1,0:T(8,128)S(1)} %get-tuple-element.42.refs_1_, bf16[32,1024]{1,0:T(8,128)(2,1)S(1)} %get-tuple-element.55.refs_0_.refs_2_, ...), custom_call_target="tpu_custom_call" | custom-call | tf_op jit(solution)/shard_map/pallas_call | solution.py:42
  50.1 0.7 %collective-permute-done.23.refs_2_ = bf16[16,2048]{1,0:T(8,128)(2,1)S(1)} collective-permute-done((bf16[16,2048]{1,0:T(8,128)(2,1)S(1)}, bf16[16,2048]{1,0:T(8,128)(2,1)S(1)}, u32[]{:S(2)}, u32[]{:S(2)}) %collective-permute-start.23) | collective-permute-done | bytes 65568 | tf_op jit(solution)/shard_map/ppermute | solution.py:314
  50.7 0.8 %collective-permute-done.24.refs_3_ = bf16[16,2048]{1,0:T(8,128)(2,1)S(1)} collective-permute-done((bf16[16,2048]{1,0:T(8,128)(2,1)S(1)}, bf16[16,2048]{1,0:T(8,128)(2,1)S(1)}, u32[]{:S(2)}, u32[]{:S(2)}) %collective-permute-start.24) | collective-permute-done | bytes 65568 | tf_op jit(solution)/shard_map/ppermute | solution.py:314
  51.6 0.5 %collective-permute-done.25.refs_4_ = bf16[16,2048]{1,0:T(8,128)(2,1)S(1)} collective-permute-done((bf16[16,2048]{1,0:T(8,128)(2,1)S(1)}, bf16[16,2048]{1,0:T(8,128)(2,1)S(1)}, u32[]{:S(2)}, u32[]{:S(2)}) %collective-permute-start.25) | collective-permute-done | bytes 65568 | tf_op jit(solution)/shard_map/ppermute | solution.py:314
  52.1 1.2 %shard_map.108 = bf16[256,2048]{1,0:T(8,128)(2,1)} custom-call(bf16[256,64]{1,0:T(8,128)(2,1)S(1)} %get-tuple-element.41.refs_0_, bf16[16,2048]{1,0:T(8,128)(2,1)S(1)} %get-tuple-element.73.refs_1_, bf16[16,2048]{1,0:T(8,128)(2,1)S(1)} %collective-permute-done.23.refs_2_, bf16[16,2048]{1,0:T(8,128)(2,1)S(1)} %collective-permute-done.24.refs_3_, ...), custom_call_target="tpu_custom_call" | custom-call | tf_op jit(solution)/shard_map/pallas_call | solution.py:42
  (23 shorter events, 0.1 us)
Async XLA Ops:
  0.6 7.6 %collective-permute-start = (bf16[512,1536]{1,0:T(8,128)(2,1)}, bf16[512,1536]{1,0:T(8,128)(2,1)S(1)}, u32[]{:S(2)}, u32[]{:S(2)}) collective-permute-start(bf16[512,1536]{1,0:T(8,128)(2,1)} %bitcast.5), channel_id=1, source_target_pairs={{0,1},{1,0},{2,3},{3,2},{4,5},{5,4},{6,7},{7,6},{8,9},{9,8},{10,11... | collective-permute-start | bytes 4718600 | tf_op jit(solution)/shard_map/ppermute | solution.py:304
  1.1 7.0 %collective-permute-start.1 = (bf16[512,768]{1,0:T(8,128)(2,1)}, bf16[512,768]{1,0:T(8,128)(2,1)S(1)}, u32[]{:S(2)}, u32[]{:S(2)}) collective-permute-start(bf16[512,768]{1,0:T(8,128)(2,1)} %bitcast.8), channel_id=1, source_target_pairs={{0,1},{1,0},{2,3},{3,2},{4,5},{5,4},{6,7},{7,6},{8,9},{9,8},{10,11... | collective-permute-start | bytes 2359304 | tf_op jit(solution)/shard_map/ppermute | solution.py:304
  3.2 5.5 %collective-permute-start.3 = (bf16[32,1024]{1,0:T(8,128)(2,1)S(1)}, bf16[32,1024]{1,0:T(8,128)(2,1)S(1)}, u32[]{:S(2)}, u32[]{:S(2)}) collective-permute-start(bf16[32,1024]{1,0:T(8,128)(2,1)S(1)} %get-tuple-element.47), channel_id=1, source_target_pairs={{0,2},{1,3},{2,0},{3,1},{4,6},{5,7},{6,4},{7,5},{8,10},{9,11},{10,... | collective-permute-start | bytes 196616 | tf_op jit(solution)/shard_map/ppermute | solution.py:308
  6.2 6.8 %collective-permute-start.2 = (bf16[32,1024]{1,0:T(8,128)(2,1)S(1)}, bf16[32,1024]{1,0:T(8,128)(2,1)S(1)}, u32[]{:S(2)}, u32[]{:S(2)}) collective-permute-start(bf16[32,1024]{1,0:T(8,128)(2,1)S(1)} %get-tuple-element.45), channel_id=1, source_target_pairs={{0,2},{1,3},{2,0},{3,1},{4,6},{5,7},{6,4},{7,5},{8,10},{9,11},{10,... | collective-permute-start | bytes 196616 | tf_op jit(solution)/shard_map/ppermute | solution.py:308
  6.2 7.5 %collective-permute-start.13 = (bf16[64,1024]{1,0:T(8,128)(2,1)S(1)}, bf16[64,1024]{1,0:T(8,128)(2,1)S(1)}, u32[]{:S(2)}, u32[]{:S(2)}) collective-permute-start(bf16[64,1024]{1,0:T(8,128)(2,1)S(1)} %get-tuple-element.60), channel_id=1, source_target_pairs={{0,2},{1,3},{2,0},{3,1},{4,6},{5,7},{6,4},{7,5},{8,10},{9,11},{10,... | collective-permute-start | bytes 393224 | tf_op jit(solution)/shard_map/ppermute | solution.py:308
  8.2 11.5 %copy-start = (bf16[1,512,1536]{2,1,0:T(8,128)(2,1)S(1)}, bf16[1,512,1536]{2,1,0:T(8,128)(2,1)}, u32[]{:S(2)}) copy-start(bf16[1,512,1536]{2,1,0:T(8,128)(2,1)} %param.12) | copy-start | bytes 4718596
  8.6 9.5 %collective-permute-start.4 = (bf16[16,2048]{1,0:T(8,128)(2,1)S(1)}, bf16[16,2048]{1,0:T(8,128)(2,1)S(1)}, u32[]{:S(2)}, u32[]{:S(2)}) collective-permute-start(bf16[16,2048]{1,0:T(8,128)(2,1)S(1)} %get-tuple-element.48), channel_id=1, source_target_pairs={{0,12},{4,8},{8,4},{12,0},{1,13},{5,9},{9,5},{13,1},{2,14},{6,10},... | collective-permute-start | bytes 196616 | tf_op jit(solution)/shard_map/ppermute | solution.py:314
  13.0 6.7 %collective-permute-start.5 = (bf16[16,2048]{1,0:T(8,128)(2,1)S(1)}, bf16[16,2048]{1,0:T(8,128)(2,1)S(1)}, u32[]{:S(2)}, u32[]{:S(2)}) collective-permute-start(bf16[16,2048]{1,0:T(8,128)(2,1)S(1)} %get-tuple-element.49), channel_id=1, source_target_pairs={{0,8},{4,12},{8,0},{12,4},{1,9},{5,13},{9,1},{13,5},{2,10},{6,14},... | collective-permute-start | bytes 196616 | tf_op jit(solution)/shard_map/ppermute | solution.py:314
  13.0 6.7 %collective-permute-start.6 = (bf16[16,2048]{1,0:T(8,128)(2,1)S(1)}, bf16[16,2048]{1,0:T(8,128)(2,1)S(1)}, u32[]{:S(2)}, u32[]{:S(2)}) collective-permute-start(bf16[16,2048]{1,0:T(8,128)(2,1)S(1)} %get-tuple-element.50), channel_id=1, source_target_pairs={{0,4},{4,0},{8,12},{12,8},{1,5},{5,1},{9,13},{13,9},{2,6},{6,2},{1... | collective-permute-start | bytes 196616 | tf_op jit(solution)/shard_map/ppermute | solution.py:314
  13.7 8.4 %collective-permute-start.14 = (bf16[16,2048]{1,0:T(8,128)(2,1)S(1)}, bf16[16,2048]{1,0:T(8,128)(2,1)S(1)}, u32[]{:S(2)}, u32[]{:S(2)}) collective-permute-start(bf16[16,2048]{1,0:T(8,128)(2,1)S(1)} %get-tuple-element.62), channel_id=1, source_target_pairs={{0,4},{4,0},{8,12},{12,8},{1,5},{5,1},{9,13},{13,9},{2,6},{6,2},{1... | collective-permute-start | bytes 196616 | tf_op jit(solution)/shard_map/ppermute | solution.py:314
  15.2 7.3 %collective-permute-start.15 = (bf16[16,2048]{1,0:T(8,128)(2,1)S(1)}, bf16[16,2048]{1,0:T(8,128)(2,1)S(1)}, u32[]{:S(2)}, u32[]{:S(2)}) collective-permute-start(bf16[16,2048]{1,0:T(8,128)(2,1)S(1)} %get-tuple-element.63), channel_id=1, source_target_pairs={{0,8},{4,12},{8,0},{12,4},{1,9},{5,13},{9,1},{13,5},{2,10},{6,14},... | collective-permute-start | bytes 196616 | tf_op jit(solution)/shard_map/ppermute | solution.py:314
  18.1 6.1 %collective-permute-start.16 = (bf16[16,2048]{1,0:T(8,128)(2,1)S(1)}, bf16[16,2048]{1,0:T(8,128)(2,1)S(1)}, u32[]{:S(2)}, u32[]{:S(2)}) collective-permute-start(bf16[16,2048]{1,0:T(8,128)(2,1)S(1)} %get-tuple-element.64), channel_id=1, source_target_pairs={{0,12},{4,8},{8,4},{12,0},{1,13},{5,9},{9,5},{13,1},{2,14},{6,10},... | collective-permute-start | bytes 196616 | tf_op jit(solution)/shard_map/ppermute | solution.py:314
  19.7 4.5 %copy-start.1 = (bf16[1,512,768]{2,1,0:T(8,128)(2,1)S(1)}, bf16[1,512,768]{2,1,0:T(8,128)(2,1)}, u32[]{:S(2)}) copy-start(bf16[1,512,768]{2,1,0:T(8,128)(2,1)} %param.13) | copy-start | bytes 2359300
  20.3 7.0 %collective-permute-start.7 = (bf16[64,1536]{1,0:T(8,128)(2,1)S(1)}, bf16[64,1536]{1,0:T(8,128)(2,1)S(1)}, u32[]{:S(2)}, u32[]{:S(2)}) collective-permute-start(bf16[64,1536]{1,0:T(8,128)(2,1)S(1)} %get-tuple-element.53), channel_id=1, source_target_pairs={{0,2},{1,3},{2,0},{3,1},{4,6},{5,7},{6,4},{7,5},{8,10},{9,11},{10,... | collective-permute-start | bytes 589832 | tf_op jit(solution)/shard_map/ppermute | solution.py:308
  24.6 5.2 %collective-permute-start.20 = (bf16[64,768]{1,0:T(8,128)(2,1)S(1)}, bf16[64,768]{1,0:T(8,128)(2,1)S(1)}, u32[]{:S(2)}, u32[]{:S(2)}) collective-permute-start(bf16[64,768]{1,0:T(8,128)(2,1)S(1)} %get-tuple-element.70), channel_id=1, source_target_pairs={{0,2},{1,3},{2,0},{3,1},{4,6},{5,7},{6,4},{7,5},{8,10},{9,11},{10,... | collective-permute-start | bytes 294920 | tf_op jit(solution)/shard_map/ppermute | solution.py:308
  27.4 5.5 %collective-permute-start.8 = (bf16[64,768]{1,0:T(8,128)(2,1)S(1)}, bf16[64,768]{1,0:T(8,128)(2,1)S(1)}, u32[]{:S(2)}, u32[]{:S(2)}) collective-permute-start(bf16[64,768]{1,0:T(8,128)(2,1)S(1)} %shard_map.98.refs_0_.refs_2_.refs_4_), channel_id=1, source_target_pairs={{0,2},{1,3},{2,0},{3,1},{4,6},{5,7},{6,4},{7,5},{8,10},{9,11},{10,... | collective-permute-start | bytes 294920 | tf_op jit(solution)/shard_map/ppermute | solution.py:308
  29.9 7.2 %collective-permute-start.21 = (bf16[64,1536]{1,0:T(8,128)(2,1)S(1)}, bf16[64,1536]{1,0:T(8,128)(2,1)S(1)}, u32[]{:S(2)}, u32[]{:S(2)}) collective-permute-start(bf16[64,1536]{1,0:T(8,128)(2,1)S(1)} %shard_map.105.refs_0_), channel_id=1, source_target_pairs={{0,2},{1,3},{2,0},{3,1},{4,6},{5,7},{6,4},{7,5},{8,10},{9,11},{10,... | collective-permute-start | bytes 589832 | tf_op jit(solution)/shard_map/ppermute | solution.py:308
  33.6 6.2 %collective-permute-start.9 = (bf16[32,1024]{1,0:T(8,128)(2,1)S(1)}, bf16[32,1024]{1,0:T(8,128)(2,1)S(1)}, u32[]{:S(2)}, u32[]{:S(2)}) collective-permute-start(bf16[32,1024]{1,0:T(8,128)(2,1)S(1)} %get-tuple-element.56), channel_id=1, source_target_pairs={{0,8},{4,12},{8,0},{12,4},{1,9},{5,13},{9,1},{13,5},{2,10},{6,14},... | collective-permute-start | bytes 196616 | tf_op jit(solution)/shard_map/ppermute | solution.py:314
  34.3 6.2 %collective-permute-start.10 = (bf16[32,1024]{1,0:T(8,128)(2,1)S(1)}, bf16[32,1024]{1,0:T(8,128)(2,1)S(1)}, u32[]{:S(2)}, u32[]{:S(2)}) collective-permute-start(bf16[32,1024]{1,0:T(8,128)(2,1)S(1)} %get-tuple-element.57), channel_id=1, source_target_pairs={{0,12},{4,8},{8,4},{12,0},{1,13},{5,9},{9,5},{13,1},{2,14},{6,10},... | collective-permute-start | bytes 196616 | tf_op jit(solution)/shard_map/ppermute | solution.py:314
  35.9 5.0 %collective-permute-start.11 = (bf16[32,1024]{1,0:T(8,128)(2,1)S(1)}, bf16[32,1024]{1,0:T(8,128)(2,1)S(1)}, u32[]{:S(2)}, u32[]{:S(2)}) collective-permute-start(bf16[32,1024]{1,0:T(8,128)(2,1)S(1)} %get-tuple-element.58), channel_id=1, source_target_pairs={{0,4},{4,0},{8,12},{12,8},{1,5},{5,1},{9,13},{13,9},{2,6},{6,2},{1... | collective-permute-start | bytes 196616 | tf_op jit(solution)/shard_map/ppermute | solution.py:314
  38.3 5.3 %collective-permute-start.22 = (bf16[64,1024]{1,0:T(8,128)(2,1)S(1)}, bf16[64,1024]{1,0:T(8,128)(2,1)S(1)}, u32[]{:S(2)}, u32[]{:S(2)}) collective-permute-start(bf16[64,1024]{1,0:T(8,128)(2,1)S(1)} %get-tuple-element.72), channel_id=1, source_target_pairs={{0,2},{1,3},{2,0},{3,1},{4,6},{5,7},{6,4},{7,5},{8,10},{9,11},{10,... | collective-permute-start | bytes 393224 | tf_op jit(solution)/shard_map/ppermute | solution.py:308
  39.8 5.5 %collective-permute-start.17 = (bf16[128,512]{1,0:T(8,128)(2,1)S(1)}, bf16[128,512]{1,0:T(8,128)(2,1)S(1)}, u32[]{:S(2)}, u32[]{:S(2)}) collective-permute-start(bf16[128,512]{1,0:T(8,128)(2,1)S(1)} %get-tuple-element.66), channel_id=1, source_target_pairs={{0,1},{1,0},{2,3},{3,2},{4,5},{5,4},{6,7},{7,6},{8,9},{9,8},{10,11... | collective-permute-start | bytes 393224 | tf_op jit(solution)/shard_map/ppermute | solution.py:304
  39.8 7.1 %collective-permute-start.18 = (bf16[64,768]{1,0:T(8,128)(2,1)S(1)}, bf16[64,768]{1,0:T(8,128)(2,1)S(1)}, u32[]{:S(2)}, u32[]{:S(2)}) collective-permute-start(bf16[64,768]{1,0:T(8,128)(2,1)S(1)} %shard_map.98.refs_0_.refs_2_.refs_4_), channel_id=1, source_target_pairs={{0,1},{1,0},{2,3},{3,2},{4,5},{5,4},{6,7},{7,6},{8,9},{9,8},{10,11... | collective-permute-start | bytes 294920 | tf_op jit(solution)/shard_map/ppermute | solution.py:304
  40.9 7.8 %collective-permute-start.12 = (bf16[64,1024]{1,0:T(8,128)(2,1)S(1)}, bf16[64,1024]{1,0:T(8,128)(2,1)S(1)}, u32[]{:S(2)}, u32[]{:S(2)}) collective-permute-start(bf16[64,1024]{1,0:T(8,128)(2,1)S(1)} %shard_map.100), channel_id=1, source_target_pairs={{0,2},{1,3},{2,0},{3,1},{4,6},{5,7},{6,4},{7,5},{8,10},{9,11},{10,... | collective-permute-start | bytes 393224 | tf_op jit(solution)/shard_map/ppermute | solution.py:308
  42.4 4.8 %collective-permute-start.19 = (bf16[64,768]{1,0:T(8,128)(2,1)S(1)}, bf16[64,768]{1,0:T(8,128)(2,1)S(1)}, u32[]{:S(2)}, u32[]{:S(2)}) collective-permute-start(bf16[64,768]{1,0:T(8,128)(2,1)S(1)} %collective-permute-done.8.refs_1_.refs_3_), channel_id=1, source_target_pairs={{0,1},{1,0},{2,3},{3,2},{4,5},{5,4},{6,7},{7,6},{8,9},{9,8},{10,11... | collective-permute-start | bytes 294920 | tf_op jit(solution)/shard_map/ppermute | solution.py:304
  43.6 7.1 %collective-permute-start.23 = (bf16[16,2048]{1,0:T(8,128)(2,1)S(1)}, bf16[16,2048]{1,0:T(8,128)(2,1)S(1)}, u32[]{:S(2)}, u32[]{:S(2)}) collective-permute-start(bf16[16,2048]{1,0:T(8,128)(2,1)S(1)} %get-tuple-element.74), channel_id=1, source_target_pairs={{0,8},{4,12},{8,0},{12,4},{1,9},{5,13},{9,1},{13,5},{2,10},{6,14},... | collective-permute-start | bytes 196616 | tf_op jit(solution)/shard_map/ppermute | solution.py:314
  45.3 6.2 %collective-permute-start.24 = (bf16[16,2048]{1,0:T(8,128)(2,1)S(1)}, bf16[16,2048]{1,0:T(8,128)(2,1)S(1)}, u32[]{:S(2)}, u32[]{:S(2)}) collective-permute-start(bf16[16,2048]{1,0:T(8,128)(2,1)S(1)} %get-tuple-element.75), channel_id=1, source_target_pairs={{0,12},{4,8},{8,4},{12,0},{1,13},{5,9},{9,5},{13,1},{2,14},{6,10},... | collective-permute-start | bytes 196616 | tf_op jit(solution)/shard_map/ppermute | solution.py:314
  46.9 5.2 %collective-permute-start.25 = (bf16[16,2048]{1,0:T(8,128)(2,1)S(1)}, bf16[16,2048]{1,0:T(8,128)(2,1)S(1)}, u32[]{:S(2)}, u32[]{:S(2)}) collective-permute-start(bf16[16,2048]{1,0:T(8,128)(2,1)S(1)} %get-tuple-element.76), channel_id=1, source_target_pairs={{0,4},{4,0},{8,12},{12,8},{1,5},{5,1},{9,13},{13,9},{2,6},{6,2},{1... | collective-permute-start | bytes 196616 | tf_op jit(solution)/shard_map/ppermute | solution.py:314
